TPU v7x, 32 devices: a whole 2x2x4 slice. The times are simulated.
32 devices in a mesh: ctx: 8 (over z, x), exp: 4 (over y, core).
Axes of the slice: x: 2, y: 2, z: 4, core: 2. Of those that a mesh axis runs over, the one named last changes fastest.
Arguments:
- grad_out: bfloat16 [4096, 2880], P(('ctx', 'exp')), may hold values from -6 to 6
- top_logits: float32 [4096, 4], P(('ctx', 'exp')), may hold values from -8 to 308
- expert_ids: int32 [4096, 4], P(('ctx', 'exp')), may hold values from 0 to 3, all different within a row; in each aligned block of 128 rows (0 to 127, 128 to 255, ...) at most 128 rows name the same one
- saved_hidden: bfloat16 [8, 4, 512, 1536], P('ctx', 'exp'), may hold values from -0.29882812 to 0.29882812
- w_down: bfloat16 [4, 1536, 2880], P('exp', 'ctx'), may hold values from -0.15625 to 0.15625
Outputs:
- logit_grad: float32 [4096, 4], P(('ctx', 'exp'))
- hidden_grad: bfloat16 [8, 4, 512, 1536], P('ctx', 'exp')
- down_grad: float32 [4, 1536, 2880], P('exp', 'ctx')
Inputs may be any that keep to these rules, and one draw needn't show every extreme that they name: `expert_ids`: each row names 4 different experts; among the rows of one device no expert is named by more than 128 rows, a bound that some blocks reach.
All inputs are finite; a program needn't handle non-finite values.
Results may differ from a plain program's by a relative error of at most 0.0048.
Values may be sent and summed in bfloat16 or wider, within the bound.
No kernel may reach another device: no remote copies, remote signals or barrier semaphores. Data moves between devices by JAX's collectives and lax.ppermute only.
A program may use at most 128 MiB of HBM per device.

v0:
```python
import jax
import jax.numpy as jnp
from jax import lax
from jax.sharding import PartitionSpec as P


def routing_tables(expert_ids, count_experts, capacity):
    columns = jnp.arange(count_experts, dtype=jnp.int32)
    matches = expert_ids[:, :, None] == columns[None, None, :]
    per_token = jnp.sum(matches.astype(jnp.int32), axis=1)
    rank_table = jnp.cumsum(per_token, axis=0) - per_token
    slot_iota = jnp.arange(capacity, dtype=jnp.int32)
    select = (per_token.T[:, None, :] == 1) & (rank_table.T[:, None, :] == slot_iota[None, :, None])
    return (matches.astype(jnp.float32), select)


def per_device(grad_out, top_logits, expert_ids, saved_hidden, w_down):
    count_experts = lax.axis_size("exp")
    slot_count = saved_hidden.shape[2]
    capacity = slot_count // count_experts
    model_width = grad_out.shape[1]
    onehot, select = routing_tables(expert_ids, count_experts, capacity)
    select_wide = select.astype(jnp.float32)
    gate_probs = jax.nn.softmax(top_logits, axis=-1)
    gate_sent = gate_probs.astype(jnp.bfloat16)
    gate_by_expert = jnp.sum(onehot * gate_sent.astype(jnp.float32)[:, :, None], axis=1)
    send_rows = jnp.einsum(
        "ect,td->ecd", select.astype(jnp.bfloat16), grad_out, preferred_element_type=jnp.float32
    ).astype(jnp.bfloat16)
    send_gate = jnp.sum(select_wide * gate_by_expert.T[:, None, :], axis=2).astype(jnp.bfloat16)
    hidden = saved_hidden[0, 0]
    rows_in, gate_in = (
        lax.all_to_all(send_rows, "exp", split_axis=0, concat_axis=0, tiled=True),
        lax.all_to_all(send_gate, "exp", split_axis=0, concat_axis=0, tiled=True),
    )
    flat_rows = rows_in.reshape(slot_count, model_width)
    backprop = lax.dot_general(
        flat_rows,
        lax.all_gather(w_down[0], "ctx", axis=0, tiled=True),
        (((1,), (1,)), ((), ())),
        preferred_element_type=jnp.float32,
    )
    flat_gate = gate_in.reshape(slot_count, 1).astype(jnp.float32)
    hidden_grad = (flat_gate * backprop).astype(jnp.bfloat16)
    slot_grad = jnp.sum(hidden.astype(jnp.float32) * backprop, axis=1)
    scaled = (flat_gate * flat_rows.astype(jnp.float32)).astype(jnp.bfloat16)
    partial_grad = lax.dot_general(
        hidden, scaled, (((0,), (0,)), ((), ())), preferred_element_type=jnp.float32
    )
    weight_grad = lax.psum_scatter(partial_grad, "ctx", scatter_dimension=0, tiled=True)
    returned = lax.all_to_all(
        slot_grad.reshape(count_experts, capacity), "exp", split_axis=0, concat_axis=0, tiled=True
    )
    grad_by_expert = jnp.sum(select_wide * returned[:, :, None], axis=1)
    gate_grad = jnp.sum(onehot * grad_by_expert.T[:, None, :], axis=2)
    logit_grad = gate_probs * (gate_grad - jnp.sum(gate_probs * gate_grad, axis=1, keepdims=True))
    return (logit_grad, hidden_grad.reshape(1, 1, slot_count, -1), weight_grad[None])


def solution(mesh):
    return jax.shard_map(
        per_device,
        mesh=mesh,
        in_specs=(
            P(("ctx", "exp"), None),
            P(("ctx", "exp"), None),
            P(("ctx", "exp"), None),
            P("ctx", "exp", None, None),
            P("exp", "ctx", None),
        ),
        out_specs=(P(("ctx", "exp"), None), P("ctx", "exp", None, None), P("exp", "ctx", None)),
        check_vma=False,
    )
```

profile of v0, /device:TPU:0, one launch (start us, length us, event | category | flops | bytes accessed | tf_op | source)
XLA Modules:
  0.0 516.8 jit_solution(3567888441870466610)
XLA Ops:
  7.2 0.7 all-gather.3.cloned.1.call-update
  7.9 0.7 convert_reduce_fusion
  8.6 0.1 copy.37
  8.7 0.2 reduce_window_sum.11
  9.0 2.6 convolution_convert_fusion
  11.6 4.4 all-to-all-start
  16.0 34.8 %all-to-all-done = bf16[4,128,2880]{1,2,0:T(8,128)(2,1)S(1)} async-done(((bf16[4,128,2880]{1,2,0:T(8,128)(2,1)}), bf16[4,128,2880]{1,2,0:T(8,128)(2,1)S(1)}, u32[]{:S(2)}, u32[]{:S(2)}) %all-to-all-start) | async-done | bytes 2949152 | tf_op jit(solution)/shard_map/all_to_all | solution.py:33
  50.8 2.8 copy.40
  53.6 92.6 %all-gather.3.cloned.1.call-done = bf16[1,1536,2880]{2,1,0:T(8,128)(2,1)} async-done(((bf16[1,192,2880]{2,1,0:T(8,128)(2,1)}), bf16[1,1536,2880]{2,1,0:T(8,128)(2,1)}) %all-gather.3.cloned.1.call-update) | async-done | bytes 8847376 | tf_op jit(solution)/shard_map/all_gather | solution.py:39
  146.2 10.6 %multiply_reduce_fusion = (f32[512]{0:T(512)}, f32[512,1536]{1,0:T(8,128)}) fusion(bf16[1,1,512,1536]{3,2,1,0:T(8,128)(2,1)} %param.8, bf16[512,2880]{1,0:T(8,128)(2,1)} %bitcast.36, bf16[1,1536,2880]{2,1,0:T(8,128)(2,1)} %all-gather.3.cloned.1.call-done), kind=kOutput, calls=%fused_computation.6 | convolution fusion | flops 4532207104 | bytes 16517120 | tf_op jit(solution)/shard_map/dot_general | solution.py:37
  156.8 3.2 all-to-all-start.1
  160.1 3.6 all-to-all-done.1
  163.7 0.2 select_reduce_fusion
  163.9 6.1 %all_to_all.20 = bf16[4,1,128]{2,1,0:T(2,128)(2,1)S(1)} all-to-all(bf16[4,1,128]{2,1,0:T(2,128)(2,1)S(1)} %copy.41), channel_id=1, replica_groups=mesh['ctx'=8,'exp'=4] {'exp'}, dimensions={0} | all-to-all | bytes 2048 | tf_op jit(solution)/shard_map/all_to_all | solution.py:34
  170.0 2.2 multiply_convert_fusion
  172.2 3.3 copy.42
  175.5 10.1 %convolution_bitcast_fusion = f32[1536,2880]{0,1:T(8,128)} fusion(bf16[512,2880]{1,0:T(8,128)(2,1)S(1)} %bitcast.37, bf16[1,1,512,1536]{3,2,1,0:T(8,128)(2,1)} %param.8), kind=kOutput, calls=%fused_computation | convolution fusion | flops 4529848320 | bytes 22216704 | tf_op jit(solution)/shard_map/dot_general | solution.py:47
  185.6 18.1 %copy.44 = f32[1536,2880]{1,0:T(8,128)} copy(f32[1536,2880]{0,1:T(8,128)} %convolution_bitcast_fusion) | data formatting | bytes 35389440
  203.8 0.6 subtract_multiply_fusion
  204.4 1.2 copy-done.2
  205.6 1.4 fusion.2
  207.0 296.3 %reduce-scatter.4.cloned.1.call-done = f32[192,2880]{1,0:T(8,128)} async-done(((f32[1536,2880]{1,0:T(8,128)}), f32[192,2880]{1,0:T(8,128)}) %reduce-scatter.4.cloned.1.call-update) | async-done | bytes 2211856
  503.3 3.4 copy.45
  506.7 3.3 copy.43
  (23 shorter events, 0.3 us)
Async XLA Ops:
  7.2 1.8 copy-start
  7.2 139.0 %all-gather.3.cloned.1.call-start = ((), (), s32[]{:S(2)}) async-start(), calls=%async_computation.4 | async-start | bytes 10174464 | tf_op jit(solution)/shard_map/all_gather | solution.py:39
  11.6 4.4 copy-start.3
  11.6 39.2 %all-to-all-start = ((bf16[4,128,2880]{1,2,0:T(8,128)(2,1)}), bf16[4,128,2880]{1,2,0:T(8,128)(2,1)S(1)}, u32[]{:S(2)}, u32[]{:S(2)}) async-start(bf16[4,128,2880]{1,2,0:T(8,128)(2,1)} %convolution_convert_fusion), calls=%async_computation | async-start | bytes 5898240 | tf_op jit(solution)/shard_map/all_to_all | solution.py:33
  146.2 13.9 %copy-start.4 = (s32[128,4]{0,1:T(4,128)S(1)}, s32[128,4]{0,1:T(4,128)}, u32[]{:S(2)}) copy-start(s32[128,4]{0,1:T(4,128)} %param.7) | copy-start | bytes 6148
  156.8 6.9 %all-to-all-start.1 = ((f32[4,1,128]{2,1,0:T(1,128)}), f32[4,1,128]{2,1,0:T(1,128)S(1)}, u32[]{:S(2)}, u32[]{:S(2)}) async-start(f32[4,1,128]{2,1,0:T(1,128)} %bitcast.6), calls=%async_computation.1 | async-start | bytes 4096 | tf_op jit(solution)/shard_map/all_to_all | solution.py:51
  160.0 343.3 %reduce-scatter.4.cloned.1.call-start = ((), (), s32[]{:S(2)}) async-start(), calls=%async_computation.5 | async-start | bytes 20348928
  203.7 1.9 copy-start.2
  503.3 6.7 %copy-start.1 = (bf16[128,2880]{0,1:T(8,128)(2,1)S(1)}, bf16[128,2880]{0,1:T(8,128)(2,1)}, u32[]{:S(2)}) copy-start(bf16[128,2880]{0,1:T(8,128)(2,1)} %param.5) | copy-start | bytes 2211844
Sparse Core Ops, SparseCore 0:
  10.2 135.9 all-gather.2
  203.9 299.3 reduce-scatter.3
where the time goes:
time: 518 us; the launch traced here: 517 us
  waiting for transfers between devices  428 us (83%)
  local copies, waits for them, and re-layouts  32.4 us (6%)
  matrix products  23.2 us (4%)
  between operations  14.1 us (3%)
  starting transfers between devices  7.67 us (1%)
  blocking collectives  6.09 us (1%)
  other arithmetic  5.37 us (1%)
    unnamed x3, waiting for transfers between devices  297 us
    all_gather x1, waiting for transfers between devices, per_device(): lax.all_gather(w_down[0], 'ctx', axis=0, tiled=True)  92.6 us
    all_to_all x1, waiting for transfers between devices, per_device(): lax.all_to_all(send_rows, 'exp', split_axis=0, concat_axis=0, tiled=True)  34.8 us
    unnamed x13, local copies, waits for them, and re-layouts  26.1 us
    dot_general x1, matrix products, per_device(): lax.dot_general(flat_rows, lax.all_gather(w_down[0], 'ctx', axis=0, tiled...  10.6 us
  transfers between devices with their start and end apart: 4, of which 4 were waited for; matrix products, arithmetic and copies ran while one was open for 2% of the time, Pallas kernels for 0%

commit v1 on v0

--- a/solution.py
+++ b/solution.py
@@ -1,7 +1,381 @@
+import functools
+
 import jax
 import jax.numpy as jnp
 from jax import lax
+from jax.experimental import pallas as pl
+from jax.experimental.pallas import tpu as pltpu
 from jax.sharding import PartitionSpec as P
+
+LANES = 128
+VMEM_BYTES = 56 * 1024 * 1024
+NT = (((1,), (1,)), ((), ()))
+NN = (((1,), (0,)), ((), ()))
+f32 = jnp.float32
+bf16 = jnp.bfloat16
+
+
+def dot(a, b, dims):
+    return lax.dot_general(a, b, dims, preferred_element_type=f32)
+
+
+def whole():
+    return pl.BlockSpec(memory_space=pltpu.VMEM)
+
+
+def scalars():
+    return pl.BlockSpec(memory_space=pltpu.SMEM)
+
+
+def params():
+    return pltpu.CompilerParams(vmem_limit_bytes=VMEM_BYTES)
+
+
+def cost(flops, size):
+    return pl.CostEstimate(flops=int(flops), bytes_accessed=int(size), transcendentals=0)
+
+
+def rows_kernel(width, grad_ref, logits_ref, ids_ref, rows_ref, gates_ref):
+    model, tokens = grad_ref.shape
+    count = logits_ref.shape[0]
+    logits = logits_ref[...]
+    powers = jnp.exp(logits - jnp.max(logits, axis=0, keepdims=True))
+    gates = powers / jnp.sum(powers, axis=0, keepdims=True)
+    gates_ref[...] = gates
+    sent = gates.astype(bf16).astype(f32)
+    ids = ids_ref[...]
+    tail = width - model
+    row = lax.broadcasted_iota(jnp.int32, (tail, tokens), 0)
+    extra = jnp.zeros((tail, tokens), f32)
+    for expert in range(count):
+        chosen = jnp.sum(jnp.where(ids == expert, sent, 0.0), axis=0, keepdims=True)
+        extra = extra + jnp.where(row == expert, chosen, 0.0)
+    for start in range(0, width, LANES):
+        stop = start + LANES
+        if stop <= model:
+            block = grad_ref[start:stop, :].astype(f32)
+        elif start >= model:
+            block = extra[start - model : stop - model, :]
+        else:
+            block = jnp.concatenate(
+                [grad_ref[start:model, :].astype(f32), extra[: stop - model, :]], axis=0
+            )
+        rows_ref[:, start:stop] = block.T.astype(bf16)
+
+
+def make_rows(grad_out, top_logits, expert_ids, width):
+    tokens, model = grad_out.shape
+    count = top_logits.shape[1]
+    return pl.pallas_call(
+        functools.partial(rows_kernel, width),
+        out_shape=(
+            jax.ShapeDtypeStruct((tokens, width), bf16),
+            jax.ShapeDtypeStruct((count, tokens), f32),
+        ),
+        in_specs=[whole()] * 3,
+        out_specs=(whole(), whole()),
+        compiler_params=params(),
+        cost_estimate=cost(0, 4 * tokens * width),
+        name="make_rows",
+    )(grad_out.T, top_logits.T, expert_ids.T)
+
+
+def split_kernel(where_ref, hidden_ref, own_ref, other_ref):
+    parts, units, _ = own_ref.shape
+    for part in range(parts):
+        turned = hidden_ref[:, part * 2 * units : (part + 1) * 2 * units].astype(f32).T.astype(bf16)
+
+        @pl.when(where_ref[1] == 0)
+        def _():
+            own_ref[part] = turned[:units]
+            other_ref[part] = turned[units:]
+
+        @pl.when(where_ref[1] != 0)
+        def _():
+            own_ref[part] = turned[units:]
+            other_ref[part] = turned[:units]
+
+
+def split_hidden(where, hidden, parts, units):
+    slots = hidden.shape[0]
+    half = jax.ShapeDtypeStruct((parts, units, slots), bf16)
+    return pl.pallas_call(
+        split_kernel,
+        out_shape=(half, half),
+        in_specs=[scalars(), whole()],
+        out_specs=(whole(), whole()),
+        compiler_params=params(),
+        cost_estimate=cost(0, 4 * hidden.size),
+        name="split_hidden",
+    )(where, hidden)
+
+
+def first_kernel(model, count, where_ref, *refs):
+    number = 2 * count
+    blocks, gate_tiles = refs[:number], refs[number : 2 * number]
+    own_ref, other_ref = refs[2 * number : 2 * number + 2]
+    sent_ref, rows_ref, scaled_ref, gate_rows_ref, column = refs[2 * number + 2 :]
+    tokens = blocks[0].shape[0]
+    me = where_ref[2]
+    shift = model % LANES
+
+    @pl.when(pl.program_id(0) == 0)
+    def _():
+        lane = lax.broadcasted_iota(jnp.int32, (tokens, LANES), 1)
+        eight = lax.broadcasted_iota(jnp.int32, (8, LANES), 1)
+        onehot = jnp.where(eight == shift + me, 1.0, 0.0).astype(bf16)
+        for place in range(number):
+            start = (place // count) * count * tokens + ((place % count) ^ me) * tokens
+            here = pl.ds(pl.multiple_of(start, tokens), tokens)
+            tile = gate_tiles[place][...]
+            picked = jnp.where(lane == shift + me, tile.astype(f32), 0.0)
+            total = jnp.sum(picked, axis=1, keepdims=True)
+            column[here, :] = jnp.broadcast_to(total, (tokens, LANES))
+            gate_rows_ref[:, here] = dot(onehot, tile, NT)
+
+    for place in range(number):
+        start = (place // count) * count * tokens + ((place % count) ^ me) * tokens
+        here = pl.ds(pl.multiple_of(start, tokens), tokens)
+        block = blocks[place][...]
+        rows_ref[here, :] = block
+        scaled_ref[here, :] = (block.astype(f32) * column[here, 0:1]).astype(bf16)
+    slots = count * tokens
+    index = where_ref[3]
+    total = dot(own_ref[index], scaled_ref[:slots, :], NN)
+    total = total + dot(other_ref[index], scaled_ref[slots:, :], NN)
+    sent_ref[...] = total.astype(bf16)
+
+
+def first_part(where, blocks, own, other, model, step):
+    tokens, width = blocks[0].shape
+    number = len(blocks)
+    units = own.shape[1]
+    grid = (pl.cdiv(width, step),)
+    tile_spec = pl.BlockSpec((tokens, LANES), lambda j, s: (0, model // LANES))
+    block_spec = pl.BlockSpec((tokens, step), lambda j, s: (0, j))
+    return pl.pallas_call(
+        functools.partial(first_kernel, model, number // 2),
+        out_shape=(
+            jax.ShapeDtypeStruct((units, model), bf16),
+            jax.ShapeDtypeStruct((number * tokens, width), bf16),
+            jax.ShapeDtypeStruct((number * tokens, width), bf16),
+            jax.ShapeDtypeStruct((8, number * tokens), f32),
+        ),
+        grid_spec=pltpu.PrefetchScalarGridSpec(
+            num_scalar_prefetch=1,
+            grid=grid,
+            in_specs=[block_spec] * number + [tile_spec] * number + [whole()] * 2,
+            out_specs=(
+                pl.BlockSpec((units, step), lambda j, s: (0, j)),
+                pl.BlockSpec((number * tokens, step), lambda j, s: (0, j)),
+                pl.BlockSpec((number * tokens, step), lambda j, s: (0, j)),
+                pl.BlockSpec((8, number * tokens), lambda j, s: (0, 0)),
+            ),
+            scratch_shapes=[pltpu.VMEM((number * tokens, LANES), f32)],
+        ),
+        compiler_params=params(),
+        cost_estimate=cost(2 * units * number * tokens * model, 6 * number * tokens * width),
+        name="first_part",
+    )(where, *blocks, *blocks, own, other)
+
+
+def rest_kernel(where_ref, scaled_ref, own_ref, other_ref, *outs):
+    slots = own_ref.shape[2]
+    for place, out_ref in enumerate(outs):
+        index = where_ref[4 + place]
+        total = dot(own_ref[index], scaled_ref[:slots, :], NN)
+        out_ref[...] = total + dot(other_ref[index], scaled_ref[slots:, :], NN)
+
+
+def rest_parts(where, scaled, own, other, model, count, step):
+    rows, width = scaled.shape
+    units = own.shape[1]
+    return pl.pallas_call(
+        rest_kernel,
+        out_shape=[jax.ShapeDtypeStruct((units, model), f32)] * count,
+        grid_spec=pltpu.PrefetchScalarGridSpec(
+            num_scalar_prefetch=1,
+            grid=(pl.cdiv(width, step),),
+            in_specs=[pl.BlockSpec((rows, step), lambda j, s: (0, j)), whole(), whole()],
+            out_specs=[pl.BlockSpec((units, step), lambda j, s: (0, j))] * count,
+        ),
+        compiler_params=params(),
+        cost_estimate=cost(2 * units * rows * model * count, 4 * count * units * model),
+        name="rest_parts",
+    )(where, scaled, own, other)
+
+
+def back_kernel(distance, where_ref, rows_ref, gate_ref, own_ref, other_ref, before_ref, *refs):
+    weights = refs[: len(refs) - 3]
+    mine_ref, theirs_ref, sums_ref = refs[len(refs) - 3 :]
+    model = weights[0].shape[1]
+    slots = own_ref.shape[2]
+    parts = own_ref.shape[0]
+    sums_ref[...] = before_ref[...]
+    for place, weight_ref in enumerate(weights):
+        index = where_ref[0] + (distance if place == 1 else -distance)
+
+        @pl.when(jnp.logical_and(index >= 0, index < parts))
+        def _():
+            for side, (hidden_ref, out_ref) in enumerate(((own_ref, mine_ref), (other_ref, theirs_ref))):
+                here = slice(side * slots, (side + 1) * slots)
+                product = dot(weight_ref[...], rows_ref[here, :model], NT)
+                out_ref[place] = (product * gate_ref[0:1, here]).astype(bf16)
+                sums_ref[0:1, here] += jnp.sum(
+                    hidden_ref[index].astype(f32) * product, axis=0, keepdims=True
+                )
+
+
+def back_part(where, rows, gate_rows, own, other, before, weights, distance):
+    units, slots = own.shape[1:]
+    model = weights[0].shape[1]
+    number = len(weights)
+    half = jax.ShapeDtypeStruct((number, units, slots), bf16)
+    return pl.pallas_call(
+        functools.partial(back_kernel, distance),
+        out_shape=(half, half, jax.ShapeDtypeStruct(before.shape, f32)),
+        in_specs=[scalars()] + [whole()] * (5 + number),
+        out_specs=(whole(),) * 3,
+        compiler_params=params(),
+        cost_estimate=cost(4 * units * slots * model, 2 * rows.size + 2 * number * units * model),
+        name="back_part",
+    )(where, rows, gate_rows, own, other, before, *weights)
+
+
+def join_kernel(where_ref, *refs):
+    out_ref = refs[-1]
+    pairs = refs[:-1]
+    units = pairs[0].shape[1]
+    parts = out_ref.shape[1] // (2 * units)
+    for distance in range(len(pairs) // 2):
+        mine_ref, theirs_ref = pairs[2 * distance], pairs[2 * distance + 1]
+        for place in range(mine_ref.shape[0]):
+            index = where_ref[0] + (distance if place == 1 else -distance)
+
+            @pl.when(jnp.logical_and(index >= 0, index < parts))
+            def _():
+                mine, theirs = mine_ref[place].astype(f32), theirs_ref[place].astype(f32)
+                low = jnp.where(where_ref[1] == 0, mine, theirs)
+                high = jnp.where(where_ref[1] == 0, theirs, mine)
+                both = jnp.concatenate([low, high], axis=0)
+                here = pl.ds(pl.multiple_of(index * 2 * units, LANES), 2 * units)
+                out_ref[:, here] = both.T.astype(bf16)
+
+
+def join_hidden(where, pairs, slots, hidden):
+    flat = [array for pair in pairs for array in pair]
+    return pl.pallas_call(
+        join_kernel,
+        out_shape=jax.ShapeDtypeStruct((slots, hidden), bf16),
+        in_specs=[scalars()] + [whole()] * len(flat),
+        out_specs=whole(),
+        compiler_params=params(),
+        cost_estimate=cost(0, 4 * slots * hidden),
+        name="join_hidden",
+    )(where, *flat)
+
+
+def logits_kernel(gates_ref, ids_ref, grads_ref, out_ref):
+    gates, ids, grads = gates_ref[...], ids_ref[...], grads_ref[...]
+    picked = jnp.zeros_like(gates)
+    for expert in range(grads.shape[0]):
+        picked = picked + jnp.where(ids == expert, grads[expert : expert + 1, :], 0.0)
+    out_ref[...] = gates * (picked - jnp.sum(gates * picked, axis=0, keepdims=True))
+
+
+def logits_grad(gates, ids, grads):
+    return pl.pallas_call(
+        logits_kernel,
+        out_shape=jax.ShapeDtypeStruct(gates.shape, f32),
+        in_specs=[whole()] * 3,
+        out_specs=whole(),
+        name="logits_grad",
+    )(gates, ids, grads)
+
+
+def per_device_full(grad_out, top_logits, expert_ids, saved_hidden, w_down):
+    experts = lax.axis_size("exp")
+    groups = lax.axis_size("ctx")
+    depth = groups // 2
+    tokens, model = grad_out.shape
+    slots, hidden = saved_hidden.shape[2:]
+    units = w_down.shape[1]
+    width = pl.cdiv(model + experts, LANES) * LANES
+    step = 4 * LANES
+
+    place = lax.axis_index("ctx")
+    z, x = place // 2, place % 2
+    me = lax.axis_index("exp")
+    first = jnp.where(z < (depth + 1) // 2, depth - 1, 0)
+
+    def swap_x(value):
+        return lax.ppermute(value, "ctx", [(i, i ^ 1) for i in range(groups)])
+
+    def swap_exp(value, bit):
+        return lax.ppermute(value, "exp", [(i, i ^ bit) for i in range(experts)])
+
+    def shift(value, way, sources):
+        pairs = [(2 * s + i, 2 * (s + way) + i) for s in sources for i in range(2) if 0 <= s + way < depth]
+        return lax.ppermute(value, "ctx", pairs)
+
+    roles = []
+    for turn in range(2, depth):
+        roles.append(("right", turn, jnp.clip(z + depth - turn, 0, depth - 1)))
+        roles.append(("left", turn, jnp.clip(z - depth + turn, 0, depth - 1)))
+    roles.append(("own", depth, z))
+    where = jnp.stack([z, x, me, first] + [role[2] for role in roles]).astype(jnp.int32)
+
+    rows, gates = make_rows(grad_out, top_logits, expert_ids, width)
+    own, other = split_hidden(where, saved_hidden[0, 0], depth, units)
+    near, far = [rows], [swap_x(rows)]
+    bit = experts // 2
+    while bit:
+        near = near + [swap_exp(block, bit) for block in near]
+        far = far + [swap_exp(block, bit) for block in far]
+        bit //= 2
+    order = [0]
+    bit = experts // 2
+    while bit:
+        order = order + [k ^ bit for k in order]
+        bit //= 2
+    near = [near[order.index(k)] for k in range(experts)]
+    far = [far[order.index(k)] for k in range(experts)]
+    other = swap_x(other)
+
+    weight = w_down[0]
+    gathered = [(weight,)]
+    right = left = weight
+    for turn in range(1, depth):
+        right = shift(right, 1, range(turn - 1, depth))
+        left = shift(left, -1, range(0, depth - turn + 1))
+        gathered.append((right, left))
+
+    sent, rows_all, scaled, gate_rows = first_part(where, near + far, own, other, model, step)
+    rest = rest_parts(where, scaled, own, other, model, len(roles), step)
+    parts = {role[:2]: part for role, part in zip(roles, rest)}
+    right = shift(sent, 1, range(0, 1))
+    left = shift(sent, -1, range(depth - 1, depth))
+    for turn in range(2, depth):
+        right = (parts["right", turn] + right.astype(f32)).astype(bf16)
+        left = (parts["left", turn] + left.astype(f32)).astype(bf16)
+        right = shift(right, 1, range(0, turn))
+        left = shift(left, -1, range(depth - turn, depth))
+    weight_grad = parts["own", depth] + right.astype(f32) + left.astype(f32)
+
+    sums = jnp.zeros((8, 2 * slots), f32)
+    pairs = []
+    for distance, weights in enumerate(gathered):
+        mine, theirs, sums = back_part(
+            where, rows_all, gate_rows, own, other, sums, weights, distance
+        )
+        pairs.append((mine, swap_x(theirs)))
+    hidden_grad = join_hidden(where, pairs, slots, hidden)
+    slot_grad = sums[0:1, :slots] + swap_x(sums[0:1, slots:])
+    grads = lax.all_to_all(
+        slot_grad.reshape(experts, tokens), "exp", split_axis=0, concat_axis=0, tiled=True
+    )
+    logit_grad = logits_grad(gates, expert_ids.T, grads).T
+    return (logit_grad, hidden_grad[None, None], weight_grad[None])
 
 
 def routing_tables(expert_ids, count_experts, capacity):
@@ -14,7 +388,7 @@
     return (matches.astype(jnp.float32), select)
 
 
-def per_device(grad_out, top_logits, expert_ids, saved_hidden, w_down):
+def per_device_routed(grad_out, top_logits, expert_ids, saved_hidden, w_down):
     count_experts = lax.axis_size("exp")
     slot_count = saved_hidden.shape[2]
     capacity = slot_count // count_experts
@@ -57,6 +431,15 @@
     return (logit_grad, hidden_grad.reshape(1, 1, slot_count, -1), weight_grad[None])
 
 
+def per_device(grad_out, top_logits, expert_ids, saved_hidden, w_down):
+    experts = lax.axis_size("exp")
+    groups = lax.axis_size("ctx")
+    everywhere = top_logits.shape[1] == experts and saved_hidden.shape[2] == experts * grad_out.shape[0]
+    plain = experts & (experts - 1) == 0 and groups % 2 == 0 and groups >= 4
+    body = per_device_full if everywhere and plain else per_device_routed
+    return body(grad_out, top_logits, expert_ids, saved_hidden, w_down)
+
+
 def solution(mesh):
     return jax.shard_map(
         per_device,

time: 518 us -> 200 us (0.39)
  waiting for transfers between devices: 428 us -> 80.5 us
  Pallas kernels: 0 us -> 62 us
  starting transfers between devices: 7.67 us -> 38 us
  local copies, waits for them, and re-layouts: 32.4 us -> 4.57 us
  matrix products: 23.2 us -> 0 us
  between operations: 14.1 us -> 0.98 us
    unnamed x3 -> x0, waiting for transfers between devices: 297 us -> none
    all_gather x1 -> x0, waiting for transfers between devices: 92.6 us -> none  [per_device(): lax.all_gather(w_down[0], 'ctx', axis=0, tiled=True)]
    ppermute x0 -> x25, waiting for transfers between devices: none -> 80.5 us  [the longest x12 38.5 us: shift(): return lax.ppermute(value, 'ctx', pairs)]
    pallas_call x0 -> x10, Pallas kernels: none -> 62 us  [the longest x4 27.4 us: back_part(): pl.pallas_call(functools.partial(back_kernel, distance), out_shape=(half,...]
    all_to_all x2 -> x0, waiting for transfers between devices: 38.4 us -> none  [the longest x1 34.8 us: per_device(): lax.all_to_all(send_rows, 'exp', split_axis=0, concat_axis=0, tiled=True)]
    ppermute x0 -> x25, starting transfers between devices: none -> 38 us  [the longest x12 25.2 us: shift(): return lax.ppermute(value, 'ctx', pairs)]
    unnamed x13 -> x36, local copies, waits for them, and re-layouts: 26.1 us -> 2.65 us
    dot_general x3 -> x0, matrix products: 23.2 us -> none  [the longest x1 10.6 us: per_device(): lax.dot_general(flat_rows, lax.all_gather(w_down[0], 'ctx', axis=0, tiled...]
  transfers between devices with their start and end apart: 4 -> 25, of which waited for: 4 -> 11; matrix products, arithmetic and copies ran while one was open for 2% -> 3% of each run, Pallas kernels for 0% -> 30%
where the time goes in v1:
time: 200 us; the launch traced here: 199 us
  waiting for transfers between devices  80.5 us (40%)
  Pallas kernels  62 us (31%)
  starting transfers between devices  38 us (19%)
  blocking collectives  6.6 us (3%)
  other arithmetic  6.04 us (3%)
  local copies, waits for them, and re-layouts  4.57 us (2%)
    ppermute x12, waiting for transfers between devices, shift(): return lax.ppermute(value, 'ctx', pairs)  38.5 us
    ppermute x7, waiting for transfers between devices, swap_x(): return lax.ppermute(value, 'ctx', [(i, i ^ 1) for i in range(groups)])  31.7 us
    pallas_call x4, Pallas kernels, back_part(): pl.pallas_call(functools.partial(back_kernel, distance), out_shape=(half,...  27.4 us
    ppermute x12, starting transfers between devices, shift(): return lax.ppermute(value, 'ctx', pairs)  25.2 us
    pallas_call x1, Pallas kernels, rest_parts(): pl.pallas_call(rest_kernel, out_shape=[jax.ShapeDtypeStruct((units, model...  12.3 us
    pallas_call x1, Pallas kernels, first_part(): pl.pallas_call(functools.partial(first_kernel, model, number // 2), out_s...  11.5 us
    ppermute x6, waiting for transfers between devices, swap_exp(): return lax.ppermute(value, 'exp', [(i, i ^ bit) for i in range(experts)])  10.3 us
    ppermute x7, starting transfers between devices, swap_x(): return lax.ppermute(value, 'ctx', [(i, i ^ 1) for i in range(groups)])  9.03 us
  transfers between devices with their start and end apart: 25, of which 11 were waited for; matrix products, arithmetic and copies ran while one was open for 3% of the time, Pallas kernels for 30%

profile of v1, /device:TPU:0, one launch (start us, length us, event | category | flops | bytes accessed | tf_op | source)
XLA Modules:
  0.0 198.7 jit_solution(14934627375683363873)
XLA Ops:
  0.6 2.3 %make_rows.1 = (bf16[128,2944]{1,0:T(8,128)(2,1)}, f32[4,128]{1,0:T(4,128)}) custom-call(bf16[2880,128]{1,0:T(8,128)(2,1)} %bitcast.27, f32[4,128]{1,0:T(4,128)} %bitcast.31, s32[4,128]{1,0:T(4,128)} %bitcast.28), custom_call_target="tpu_custom_call" | custom-call | bytes 1507328 | tf_op jit(solution)/shard_map/make_rows/pallas_call | solution.py:69
  2.9 2.9 %collective-permute-start.3 = (bf16[128,2944]{1,0:T(8,128)(2,1)}, bf16[128,2944]{1,0:T(8,128)(2,1)S(1)}, u32[]{:S(2)}, u32[]{:S(2)}) collective-permute-start(bf16[128,2944]{1,0:T(8,128)(2,1)} %get-tuple-element.29.refs_0_.refs_8_), channel_id=1, source_target_pairs={{0,4},{4,0},{8,12},{12,8},{16,20},{20,16},{24,28},{28,24},{1,5},{5... | collective-permute-start | bytes 2261000 | tf_op jit(solution)/shard_map/ppermute | solution.py:312
  7.4 15.6 %collective-permute-done.3.refs_4_.refs_12_ = bf16[128,2944]{1,0:T(8,128)(2,1)S(1)} collective-permute-done((bf16[128,2944]{1,0:T(8,128)(2,1)}, bf16[128,2944]{1,0:T(8,128)(2,1)S(1)}, u32[]{:S(2)}, u32[]{:S(2)}) %collective-permute-start.3) | collective-permute-done | bytes 753696 | tf_op jit(solution)/shard_map/ppermute | solution.py:312
  25.3 3.4 %split_hidden.1 = (bf16[4,192,512]{2,1,0:T(8,128)(2,1)}, bf16[4,192,512]{2,1,0:T(8,128)(2,1)}) custom-call(s32[9]{0:T(128)} %stack.36.where_ref, bf16[512,1536]{1,0:T(8,128)(2,1)} %bitcast.22), custom_call_target="tpu_custom_call" | custom-call | bytes 3145728 | tf_op jit(solution)/shard_map/split_hidden/pallas_call | solution.py:102
  30.8 10.2 %collective-permute-done.5.refs_6_.refs_14_ = bf16[128,2944]{1,0:T(8,128)(2,1)S(1)} collective-permute-done((bf16[128,2944]{1,0:T(8,128)(2,1)S(1)}, bf16[128,2944]{1,0:T(8,128)(2,1)S(1)}, u32[]{:S(2)}, u32[]{:S(2)}) %collective-permute-start.5) | collective-permute-done | bytes 753696 | tf_op jit(solution)/shard_map/ppermute | solution.py:315
  41.0 3.4 %collective-permute-start.8 = (bf16[192,2880]{1,0:T(8,128)(2,1)}, bf16[192,2880]{1,0:T(8,128)(2,1)S(1)}, u32[]{:S(2)}, u32[]{:S(2)}) collective-permute-start(bf16[192,2880]{1,0:T(8,128)(2,1)} %bitcast.24), channel_id=1, source_target_pairs={{0,8},{4,12},{8,16},{12,20},{16,24},{20,28},{1,9},{5,13},{9,17},{1... | collective-permute-start | bytes 3317768 | tf_op jit(solution)/shard_map/ppermute | solution.py:319
  44.5 2.6 %collective-permute-done.7.refs_17_.other_ref = bf16[4,192,512]{2,1,0:T(8,128)(2,1)S(1)} collective-permute-done((bf16[4,192,512]{2,1,0:T(8,128)(2,1)}, bf16[4,192,512]{2,1,0:T(8,128)(2,1)S(1)}, u32[]{:S(2)}, u32[]{:S(2)}) %collective-permute-start.7) | collective-permute-done | bytes 786464 | tf_op jit(solution)/shard_map/ppermute | solution.py:312
  49.7 11.5 %first_part.1 = (bf16[192,2880]{1,0:T(8,128)(2,1)}, bf16[1024,2944]{1,0:T(8,128)(2,1)}, bf16[1024,2944]{1,0:T(8,128)(2,1)}, f32[8,1024]{1,0:T(8,128)}) custom-call(s32[9]{0:T(128)} %stack.36.where_ref, bf16[128,2944]{1,0:T(8,128)(2,1)} %get-tuple-element.29.refs_0_.refs_8_, bf16[128,2944]{1,0:T(8,128)(2,1)} %copy-done.5, bf16[128,2944]{1,0:T(8,128)(2,1)} %copy-done.3, ...), custom_call_target="tpu_custom_call" | custom-call | flops 1132462080 | bytes 18087936 | tf_op jit(solution)/shard_map/first_part/pallas_call | solution.py:156
  61.9 7.6 %collective-permute-done.8.refs_0_ = bf16[192,2880]{1,0:T(8,128)(2,1)S(1)} collective-permute-done((bf16[192,2880]{1,0:T(8,128)(2,1)}, bf16[192,2880]{1,0:T(8,128)(2,1)S(1)}, u32[]{:S(2)}, u32[]{:S(2)}) %collective-permute-start.8) | collective-permute-done | bytes 1105952 | tf_op jit(solution)/shard_map/ppermute | solution.py:319
  70.2 3.6 %collective-permute-done.9.refs_1_ = bf16[192,2880]{1,0:T(8,128)(2,1)} collective-permute-done((bf16[192,2880]{1,0:T(8,128)(2,1)}, bf16[192,2880]{1,0:T(8,128)(2,1)}, u32[]{:S(2)}, u32[]{:S(2)}) %collective-permute-start.9) | collective-permute-done | bytes 1105952 | tf_op jit(solution)/shard_map/ppermute | solution.py:319
  75.1 4.6 %collective-permute-start.19 = (bf16[192,2880]{1,0:T(8,128)(2,1)}, bf16[192,2880]{1,0:T(8,128)(2,1)S(1)}, u32[]{:S(2)}, u32[]{:S(2)}) collective-permute-start(bf16[192,2880]{1,0:T(8,128)(2,1)} %get-tuple-element.50), channel_id=1, source_target_pairs={{0,8},{4,12},{1,9},{5,13},{2,10},{6,14},{3,11},{7,15}} | collective-permute-start | bytes 3317768 | tf_op jit(solution)/shard_map/ppermute | solution.py:319
  79.7 12.3 %rest_parts.1 = (f32[192,2880]{1,0:T(8,128)}, f32[192,2880]{1,0:T(8,128)}, f32[192,2880]{1,0:T(8,128)}, f32[192,2880]{1,0:T(8,128)}, f32[192,2880]{1,0:T(8,128)}) custom-call(s32[9]{0:T(128)} %stack.36.where_ref, bf16[1024,2944]{1,0:T(8,128)(2,1)} %get-tuple-element.46.scaled_ref, bf16[4,192,512]{2,1,0:T(8,128)(2,1)} %get-tuple-element.30.refs_16_.own_ref, ...), custom_call_target="tpu_custom_call" | custom-call | flops 5662310400 | bytes 11059200 | tf_op jit(solution)/shard_map/rest_parts/pallas_call | solution.py:193
  94.7 8.7 %collective-permute-done.19 = bf16[192,2880]{1,0:T(8,128)(2,1)S(1)} collective-permute-done((bf16[192,2880]{1,0:T(8,128)(2,1)}, bf16[192,2880]{1,0:T(8,128)(2,1)S(1)}, u32[]{:S(2)}, u32[]{:S(2)}) %collective-permute-start.19) | collective-permute-done | bytes 1105952 | tf_op jit(solution)/shard_map/ppermute | solution.py:319
  103.7 4.5 %collective-permute-start.20 = (bf16[192,2880]{1,0:T(8,128)(2,1)S(1)}, bf16[192,2880]{1,0:T(8,128)(2,1)S(1)}, u32[]{:S(2)}, u32[]{:S(2)}) collective-permute-start(bf16[192,2880]{1,0:T(8,128)(2,1)S(1)} %add_convert_fusion.3), channel_id=1, source_target_pairs={{0,8},{4,12},{8,16},{12,20},{1,9},{5,13},{9,17},{13,21},{2,10},{6,... | collective-permute-start | bytes 3317768 | tf_op jit(solution)/shard_map/ppermute | solution.py:319
  112.0 18.7 %collective-permute-done.20 = bf16[192,2880]{1,0:T(8,128)(2,1)S(1)} collective-permute-done((bf16[192,2880]{1,0:T(8,128)(2,1)S(1)}, bf16[192,2880]{1,0:T(8,128)(2,1)S(1)}, u32[]{:S(2)}, u32[]{:S(2)}) %collective-permute-start.20) | collective-permute-done | bytes 1105952 | tf_op jit(solution)/shard_map/ppermute | solution.py:319
  131.9 4.4 %collective-permute-start.21 = (bf16[192,2880]{1,0:T(8,128)(2,1)}, bf16[192,2880]{1,0:T(8,128)(2,1)S(1)}, u32[]{:S(2)}, u32[]{:S(2)}) collective-permute-start(bf16[192,2880]{1,0:T(8,128)(2,1)} %add_convert_fusion.2), channel_id=1, source_target_pairs={{0,8},{4,12},{8,16},{12,20},{16,24},{20,28},{1,9},{5,13},{9,17},{1... | collective-permute-start | bytes 3317768 | tf_op jit(solution)/shard_map/ppermute | solution.py:319
  136.9 6.4 %back_part.4 = (bf16[1,192,512]{2,1,0:T(8,128)(2,1)}, bf16[1,192,512]{2,1,0:T(8,128)(2,1)}, f32[8,1024]{1,0:T(8,128)}) custom-call(s32[9]{0:T(128)} %stack.36.where_ref, bf16[1024,2944]{1,0:T(8,128)(2,1)} %get-tuple-element.32.rows_ref, f32[8,1024]{1,0:T(8,128)} %get-tuple-element.33.gate_ref, bf16[4,192,512]{2,1,0:T(8,128)(2,1)} %get-tuple-element.30.refs_16_.own_ref, ...), custom_call_target="tpu_custom_call" | custom-call | flops 1132462080 | bytes 7135232 | tf_op jit(solution)/shard_map/back_part/pallas_call | solution.py:234
  144.8 7.0 %back_part.5 = (bf16[2,192,512]{2,1,0:T(8,128)(2,1)}, bf16[2,192,512]{2,1,0:T(8,128)(2,1)}, f32[8,1024]{1,0:T(8,128)}) custom-call(s32[9]{0:T(128)} %stack.36.where_ref, bf16[1024,2944]{1,0:T(8,128)(2,1)} %get-tuple-element.32.rows_ref, f32[8,1024]{1,0:T(8,128)} %get-tuple-element.33.gate_ref, bf16[4,192,512]{2,1,0:T(8,128)(2,1)} %get-tuple-element.30.refs_16_.own_ref, ...), custom_call_target="tpu_custom_call" | custom-call | flops 1132462080 | bytes 8241152 | tf_op jit(solution)/shard_map/back_part/pallas_call | solution.py:234
  151.8 7.1 %back_part.6 = (bf16[2,192,512]{2,1,0:T(8,128)(2,1)}, bf16[2,192,512]{2,1,0:T(8,128)(2,1)}, f32[8,1024]{1,0:T(8,128)}) custom-call(s32[9]{0:T(128)} %stack.36.where_ref, bf16[1024,2944]{1,0:T(8,128)(2,1)} %get-tuple-element.32.rows_ref, f32[8,1024]{1,0:T(8,128)} %get-tuple-element.33.gate_ref, bf16[4,192,512]{2,1,0:T(8,128)(2,1)} %get-tuple-element.30.refs_16_.own_ref, ...), custom_call_target="tpu_custom_call" | custom-call | flops 1132462080 | bytes 8241152 | tf_op jit(solution)/shard_map/back_part/pallas_call | solution.py:234
  160.2 6.9 %back_part.7 = (bf16[2,192,512]{2,1,0:T(8,128)(2,1)}, bf16[2,192,512]{2,1,0:T(8,128)(2,1)}, f32[8,1024]{1,0:T(8,128)}) custom-call(s32[9]{0:T(128)} %stack.36.where_ref, bf16[1024,2944]{1,0:T(8,128)(2,1)} %get-tuple-element.32.rows_ref, f32[8,1024]{1,0:T(8,128)} %get-tuple-element.33.gate_ref, bf16[4,192,512]{2,1,0:T(8,128)(2,1)} %get-tuple-element.30.refs_16_.own_ref, ...), custom_call_target="tpu_custom_call" | custom-call | flops 1132462080 | bytes 8241152 | tf_op jit(solution)/shard_map/back_part/pallas_call | solution.py:234
  172.8 6.6 %all_to_all.11 = f32[4,1,128]{2,1,0:T(1,128)} all-to-all(f32[4,1,128]{2,1,0:T(1,128)S(1)} %add_bitcast_fusion.1), channel_id=1, replica_groups=mesh['ctx'=8,'exp'=4] {'exp'}, dimensions={0} | all-to-all | bytes 4096 | tf_op jit(solution)/shard_map/all_to_all | solution.py:374
  180.8 8.1 %collective-permute-done.17.refs_5_ = bf16[2,192,512]{2,1,0:T(8,128)(2,1)} collective-permute-done((bf16[2,192,512]{2,1,0:T(8,128)(2,1)}, bf16[2,192,512]{2,1,0:T(8,128)(2,1)}, u32[]{:S(2)}, u32[]{:S(2)}) %collective-permute-start.17) | collective-permute-done | bytes 393248 | tf_op jit(solution)/shard_map/ppermute | solution.py:312
  188.9 4.2 %collective-permute-done.18.refs_7_ = bf16[2,192,512]{2,1,0:T(8,128)(2,1)} collective-permute-done((bf16[2,192,512]{2,1,0:T(8,128)(2,1)}, bf16[2,192,512]{2,1,0:T(8,128)(2,1)}, u32[]{:S(2)}, u32[]{:S(2)}) %collective-permute-start.18) | collective-permute-done | bytes 393248 | tf_op jit(solution)/shard_map/ppermute | solution.py:312
  193.1 3.9 %join_hidden.1 = bf16[512,1536]{1,0:T(8,128)(2,1)} custom-call(s32[9]{0:T(128)} %stack.36.where_ref, bf16[1,192,512]{2,1,0:T(8,128)(2,1)} %get-tuple-element.38.refs_0_, bf16[1,192,512]{2,1,0:T(8,128)(2,1)} %collective-permute-done.15.refs_1_, bf16[2,192,512]{2,1,0:T(8,128)(2,1)} %get-tuple-element.40.refs_2_, ...), custom_call_target="tpu_custom_call" | custom-call | bytes 3145728 | tf_op jit(solution)/shard_map/join_hidden/pallas_call | solution.py:267
  (82 shorter events, 31.2 us)
Async XLA Ops:
  2.9 20.1 %collective-permute-start.3 = (bf16[128,2944]{1,0:T(8,128)(2,1)}, bf16[128,2944]{1,0:T(8,128)(2,1)S(1)}, u32[]{:S(2)}, u32[]{:S(2)}) collective-permute-start(bf16[128,2944]{1,0:T(8,128)(2,1)} %get-tuple-element.29.refs_0_.refs_8_), channel_id=1, source_target_pairs={{0,4},{4,0},{8,12},{12,8},{16,20},{20,16},{24,28},{28,24},{1,5},{5... | collective-permute-start | bytes 2261000 | tf_op jit(solution)/shard_map/ppermute | solution.py:312
  5.9 24.8 %collective-permute-start.1 = (bf16[128,2944]{1,0:T(8,128)(2,1)}, bf16[128,2944]{1,0:T(8,128)(2,1)S(1)}, u32[]{:S(2)}, u32[]{:S(2)}) collective-permute-start(bf16[128,2944]{1,0:T(8,128)(2,1)} %get-tuple-element.29.refs_0_.refs_8_), channel_id=1, source_target_pairs={{0,2},{1,3},{2,0},{3,1},{4,6},{5,7},{6,4},{7,5},{8,10},{9,11},{10,... | collective-permute-start | bytes 2261000 | tf_op jit(solution)/shard_map/ppermute | solution.py:315
  23.0 18.0 %collective-permute-start.5 = (bf16[128,2944]{1,0:T(8,128)(2,1)S(1)}, bf16[128,2944]{1,0:T(8,128)(2,1)S(1)}, u32[]{:S(2)}, u32[]{:S(2)}) collective-permute-start(bf16[128,2944]{1,0:T(8,128)(2,1)S(1)} %collective-permute-done.3.refs_4_.refs_12_), channel_id=1, source_target_pairs={{0,2},{1,3},{2,0},{3,1},{4,6},{5,7},{6,4},{7,5},{8,10},{9,11},{10,... | collective-permute-start | bytes 2261000 | tf_op jit(solution)/shard_map/ppermute | solution.py:315
  28.7 18.3 %collective-permute-start.7 = (bf16[4,192,512]{2,1,0:T(8,128)(2,1)}, bf16[4,192,512]{2,1,0:T(8,128)(2,1)S(1)}, u32[]{:S(2)}, u32[]{:S(2)}) collective-permute-start(bf16[4,192,512]{2,1,0:T(8,128)(2,1)} %get-tuple-element.31), channel_id=1, source_target_pairs={{0,4},{4,0},{8,12},{12,8},{16,20},{20,16},{24,28},{28,24},{1,5},{5... | collective-permute-start | bytes 2359304 | tf_op jit(solution)/shard_map/ppermute | solution.py:312
  30.2 10.8 %collective-permute-start = (bf16[128,2944]{1,0:T(8,128)(2,1)S(1)}, bf16[128,2944]{1,0:T(8,128)(2,1)S(1)}, u32[]{:S(2)}, u32[]{:S(2)}) collective-permute-start(bf16[128,2944]{1,0:T(8,128)(2,1)S(1)} %copy-done.1), channel_id=1, source_target_pairs={{0,1},{1,0},{2,3},{3,2},{4,5},{5,4},{6,7},{7,6},{8,9},{9,8},{10,11... | collective-permute-start | bytes 2261000 | tf_op jit(solution)/shard_map/ppermute | solution.py:315
  30.2 18.2 %collective-permute-start.4 = (bf16[128,2944]{1,0:T(8,128)(2,1)S(1)}, bf16[128,2944]{1,0:T(8,128)(2,1)S(1)}, u32[]{:S(2)}, u32[]{:S(2)}) collective-permute-start(bf16[128,2944]{1,0:T(8,128)(2,1)S(1)} %collective-permute-done.3.refs_4_.refs_12_), channel_id=1, source_target_pairs={{0,1},{1,0},{2,3},{3,2},{4,5},{5,4},{6,7},{7,6},{8,9},{9,8},{10,11... | collective-permute-start | bytes 2261000 | tf_op jit(solution)/shard_map/ppermute | solution.py:315
  30.7 17.6 %collective-permute-start.2 = (bf16[128,2944]{1,0:T(8,128)(2,1)S(1)}, bf16[128,2944]{1,0:T(8,128)(2,1)S(1)}, u32[]{:S(2)}, u32[]{:S(2)}) collective-permute-start(bf16[128,2944]{1,0:T(8,128)(2,1)S(1)} %collective-permute-done.1.refs_2_.refs_10_), channel_id=1, source_target_pairs={{0,1},{1,0},{2,3},{3,2},{4,5},{5,4},{6,7},{7,6},{8,9},{9,8},{10,11... | collective-permute-start | bytes 2261000 | tf_op jit(solution)/shard_map/ppermute | solution.py:315
  41.0 7.3 %collective-permute-start.6 = (bf16[128,2944]{1,0:T(8,128)(2,1)S(1)}, bf16[128,2944]{1,0:T(8,128)(2,1)S(1)}, u32[]{:S(2)}, u32[]{:S(2)}) collective-permute-start(bf16[128,2944]{1,0:T(8,128)(2,1)S(1)} %collective-permute-done.5.refs_6_.refs_14_), channel_id=1, source_target_pairs={{0,1},{1,0},{2,3},{3,2},{4,5},{5,4},{6,7},{7,6},{8,9},{9,8},{10,11... | collective-permute-start | bytes 2261000 | tf_op jit(solution)/shard_map/ppermute | solution.py:315
  41.0 28.5 %collective-permute-start.8 = (bf16[192,2880]{1,0:T(8,128)(2,1)}, bf16[192,2880]{1,0:T(8,128)(2,1)S(1)}, u32[]{:S(2)}, u32[]{:S(2)}) collective-permute-start(bf16[192,2880]{1,0:T(8,128)(2,1)} %bitcast.24), channel_id=1, source_target_pairs={{0,8},{4,12},{8,16},{12,20},{16,24},{20,28},{1,9},{5,13},{9,17},{1... | collective-permute-start | bytes 3317768 | tf_op jit(solution)/shard_map/ppermute | solution.py:319
  47.0 26.8 %collective-permute-start.9 = (bf16[192,2880]{1,0:T(8,128)(2,1)}, bf16[192,2880]{1,0:T(8,128)(2,1)}, u32[]{:S(2)}, u32[]{:S(2)}) collective-permute-start(bf16[192,2880]{1,0:T(8,128)(2,1)} %bitcast.25), channel_id=1, source_target_pairs={{8,0},{12,4},{16,8},{20,12},{24,16},{28,20},{9,1},{13,5},{17,9},{2... | collective-permute-start | bytes 3317768 | tf_op jit(solution)/shard_map/ppermute | solution.py:319
  61.2 30.8 %collective-permute-start.22 = (bf16[192,2880]{1,0:T(8,128)(2,1)}, bf16[192,2880]{1,0:T(8,128)(2,1)S(1)}, u32[]{:S(2)}, u32[]{:S(2)}) collective-permute-start(bf16[192,2880]{1,0:T(8,128)(2,1)} %get-tuple-element.50), channel_id=1, source_target_pairs={{24,16},{28,20},{25,17},{29,21},{26,18},{30,22},{27,19},{31,23}} | collective-permute-start | bytes 3317768 | tf_op jit(solution)/shard_map/ppermute | solution.py:319
  69.5 38.7 %collective-permute-start.10 = (bf16[192,2880]{1,0:T(8,128)(2,1)S(1)}, bf16[192,2880]{1,0:T(8,128)(2,1)S(1)}, u32[]{:S(2)}, u32[]{:S(2)}) collective-permute-start(bf16[192,2880]{1,0:T(8,128)(2,1)S(1)} %collective-permute-done.8.refs_0_), channel_id=1, source_target_pairs={{8,16},{12,20},{16,24},{20,28},{9,17},{13,21},{17,25},{21,29},{10,... | collective-permute-start | bytes 3317768 | tf_op jit(solution)/shard_map/ppermute | solution.py:319
  73.8 35.2 %collective-permute-start.11 = (bf16[192,2880]{1,0:T(8,128)(2,1)}, bf16[192,2880]{1,0:T(8,128)(2,1)S(1)}, u32[]{:S(2)}, u32[]{:S(2)}) collective-permute-start(bf16[192,2880]{1,0:T(8,128)(2,1)} %collective-permute-done.9.refs_1_), channel_id=1, source_target_pairs={{8,0},{12,4},{16,8},{20,12},{9,1},{13,5},{17,9},{21,13},{10,2},{14... | collective-permute-start | bytes 3317768 | tf_op jit(solution)/shard_map/ppermute | solution.py:319
  75.1 28.4 %collective-permute-start.19 = (bf16[192,2880]{1,0:T(8,128)(2,1)}, bf16[192,2880]{1,0:T(8,128)(2,1)S(1)}, u32[]{:S(2)}, u32[]{:S(2)}) collective-permute-start(bf16[192,2880]{1,0:T(8,128)(2,1)} %get-tuple-element.50), channel_id=1, source_target_pairs={{0,8},{4,12},{1,9},{5,13},{2,10},{6,14},{3,11},{7,15}} | collective-permute-start | bytes 3317768 | tf_op jit(solution)/shard_map/ppermute | solution.py:319
  94.0 16.3 %collective-permute-start.23 = (bf16[192,2880]{1,0:T(8,128)(2,1)S(1)}, bf16[192,2880]{1,0:T(8,128)(2,1)S(1)}, u32[]{:S(2)}, u32[]{:S(2)}) collective-permute-start(bf16[192,2880]{1,0:T(8,128)(2,1)S(1)} %add_convert_fusion.1), channel_id=1, source_target_pairs={{16,8},{20,12},{24,16},{28,20},{17,9},{21,13},{25,17},{29,21},{18,... | collective-permute-start | bytes 3317768 | tf_op jit(solution)/shard_map/ppermute | solution.py:319
  103.7 27.0 %collective-permute-start.20 = (bf16[192,2880]{1,0:T(8,128)(2,1)S(1)}, bf16[192,2880]{1,0:T(8,128)(2,1)S(1)}, u32[]{:S(2)}, u32[]{:S(2)}) collective-permute-start(bf16[192,2880]{1,0:T(8,128)(2,1)S(1)} %add_convert_fusion.3), channel_id=1, source_target_pairs={{0,8},{4,12},{8,16},{12,20},{1,9},{5,13},{9,17},{13,21},{2,10},{6,... | collective-permute-start | bytes 3317768 | tf_op jit(solution)/shard_map/ppermute | solution.py:319
  108.2 50.7 %collective-permute-start.12 = (bf16[192,2880]{1,0:T(8,128)(2,1)S(1)}, bf16[192,2880]{1,0:T(8,128)(2,1)S(1)}, u32[]{:S(2)}, u32[]{:S(2)}) collective-permute-start(bf16[192,2880]{1,0:T(8,128)(2,1)S(1)} %collective-permute-done.10.refs_0_), channel_id=1, source_target_pairs={{16,24},{20,28},{17,25},{21,29},{18,26},{22,30},{19,27},{23,31}} | collective-permute-start | bytes 3317768 | tf_op jit(solution)/shard_map/ppermute | solution.py:319
  109.0 49.9 %collective-permute-start.13 = (bf16[192,2880]{1,0:T(8,128)(2,1)S(1)}, bf16[192,2880]{1,0:T(8,128)(2,1)S(1)}, u32[]{:S(2)}, u32[]{:S(2)}) collective-permute-start(bf16[192,2880]{1,0:T(8,128)(2,1)S(1)} %collective-permute-done.11.refs_1_), channel_id=1, source_target_pairs={{8,0},{12,4},{9,1},{13,5},{10,2},{14,6},{11,3},{15,7}} | collective-permute-start | bytes 3317768 | tf_op jit(solution)/shard_map/ppermute | solution.py:319
  110.6 86.4 %collective-permute-start.24 = (bf16[192,2880]{1,0:T(8,128)(2,1)S(1)}, bf16[192,2880]{1,0:T(8,128)(2,1)S(1)}, u32[]{:S(2)}, u32[]{:S(2)}) collective-permute-start(bf16[192,2880]{1,0:T(8,128)(2,1)S(1)} %add_convert_fusion), channel_id=1, source_target_pairs={{8,0},{12,4},{16,8},{20,12},{24,16},{28,20},{9,1},{13,5},{17,9},{2... | collective-permute-start | bytes 3317768 | tf_op jit(solution)/shard_map/ppermute | solution.py:319
  131.9 65.1 %collective-permute-start.21 = (bf16[192,2880]{1,0:T(8,128)(2,1)}, bf16[192,2880]{1,0:T(8,128)(2,1)S(1)}, u32[]{:S(2)}, u32[]{:S(2)}) collective-permute-start(bf16[192,2880]{1,0:T(8,128)(2,1)} %add_convert_fusion.2), channel_id=1, source_target_pairs={{0,8},{4,12},{8,16},{12,20},{16,24},{20,28},{1,9},{5,13},{9,17},{1... | collective-permute-start | bytes 3317768 | tf_op jit(solution)/shard_map/ppermute | solution.py:319
  143.3 26.6 %collective-permute-start.15 = (bf16[1,192,512]{2,1,0:T(8,128)(2,1)}, bf16[1,192,512]{2,1,0:T(8,128)(2,1)}, u32[]{:S(2)}, u32[]{:S(2)}) collective-permute-start(bf16[1,192,512]{2,1,0:T(8,128)(2,1)} %get-tuple-element.39), channel_id=1, source_target_pairs={{0,4},{4,0},{8,12},{12,8},{16,20},{20,16},{24,28},{28,24},{1,5},{5... | collective-permute-start | bytes 589832 | tf_op jit(solution)/shard_map/ppermute | solution.py:312
  168.4 12.4 %collective-permute-start.16 = (bf16[2,192,512]{2,1,0:T(8,128)(2,1)}, bf16[2,192,512]{2,1,0:T(8,128)(2,1)}, u32[]{:S(2)}, u32[]{:S(2)}) collective-permute-start(bf16[2,192,512]{2,1,0:T(8,128)(2,1)} %get-tuple-element.41), channel_id=1, source_target_pairs={{0,4},{4,0},{8,12},{12,8},{16,20},{20,16},{24,28},{28,24},{1,5},{5... | collective-permute-start | bytes 1179656 | tf_op jit(solution)/shard_map/ppermute | solution.py:312
  169.9 19.0 %collective-permute-start.17 = (bf16[2,192,512]{2,1,0:T(8,128)(2,1)}, bf16[2,192,512]{2,1,0:T(8,128)(2,1)}, u32[]{:S(2)}, u32[]{:S(2)}) collective-permute-start(bf16[2,192,512]{2,1,0:T(8,128)(2,1)} %get-tuple-element.43), channel_id=1, source_target_pairs={{0,4},{4,0},{8,12},{12,8},{16,20},{20,16},{24,28},{28,24},{1,5},{5... | collective-permute-start | bytes 1179656 | tf_op jit(solution)/shard_map/ppermute | solution.py:312
  171.5 21.6 %collective-permute-start.18 = (bf16[2,192,512]{2,1,0:T(8,128)(2,1)}, bf16[2,192,512]{2,1,0:T(8,128)(2,1)}, u32[]{:S(2)}, u32[]{:S(2)}) collective-permute-start(bf16[2,192,512]{2,1,0:T(8,128)(2,1)} %get-tuple-element.45), channel_id=1, source_target_pairs={{0,4},{4,0},{8,12},{12,8},{16,20},{20,16},{24,28},{28,24},{1,5},{5... | collective-permute-start | bytes 1179656 | tf_op jit(solution)/shard_map/ppermute | solution.py:312
  (19 other events, 164.8 us)

commit v2 on v0

--- a/solution.py
+++ b/solution.py
@@ -1,7 +1,601 @@
+import functools
+
 import jax
 import jax.numpy as jnp
+import numpy as np
 from jax import lax
+from jax.experimental import pallas as pl
+from jax.experimental.pallas import tpu as pltpu
 from jax.sharding import PartitionSpec as P
+
+LANES = 128
+NT = (((1,), (1,)), ((), ()))
+NN = (((1,), (0,)), ((), ()))
+f32 = jnp.float32
+bf16 = jnp.bfloat16
+
+
+def dot(a, b, dims):
+    return lax.dot_general(a, b, dims, preferred_element_type=f32)
+
+
+def anywhere():
+    return pl.BlockSpec(memory_space=pl.ANY)
+
+
+def whole():
+    return pl.BlockSpec(memory_space=pltpu.VMEM)
+
+
+def scalars():
+    return pl.BlockSpec(memory_space=pltpu.SMEM)
+
+
+def params(mib):
+    return pltpu.CompilerParams(vmem_limit_bytes=mib * 1024 * 1024)
+
+
+def small():
+    return pl.CostEstimate(flops=0, bytes_accessed=0, transcendentals=0)
+
+
+def rows_kernel(width, grad_ref, logits_ref, ids_ref, rows_ref, gates_ref):
+    model, tokens = grad_ref.shape
+    count = logits_ref.shape[0]
+    logits = logits_ref[...]
+    powers = jnp.exp(logits - jnp.max(logits, axis=0, keepdims=True))
+    gates = powers / jnp.sum(powers, axis=0, keepdims=True)
+    gates_ref[...] = gates
+    sent = gates.astype(bf16).astype(f32)
+    ids = ids_ref[...]
+    tail = width - model
+    row = lax.broadcasted_iota(jnp.int32, (tail, tokens), 0)
+    extra = jnp.zeros((tail, tokens), f32)
+    for expert in range(count):
+        chosen = jnp.sum(jnp.where(ids == expert, sent, 0.0), axis=0, keepdims=True)
+        extra = extra + jnp.where(row == expert, chosen, 0.0)
+    for start in range(0, width, LANES):
+        stop = start + LANES
+        if stop <= model:
+            block = grad_ref[start:stop, :].astype(f32)
+        elif start >= model:
+            block = extra[start - model : stop - model, :]
+        else:
+            block = jnp.concatenate(
+                [grad_ref[start:model, :].astype(f32), extra[: stop - model, :]], axis=0
+            )
+        rows_ref[:, start:stop] = block.T.astype(bf16)
+
+
+def make_rows(grad_out, top_logits, expert_ids, width):
+    tokens, model = grad_out.shape
+    count = top_logits.shape[1]
+    return pl.pallas_call(
+        functools.partial(rows_kernel, width),
+        out_shape=(
+            jax.ShapeDtypeStruct((tokens, width), bf16),
+            jax.ShapeDtypeStruct((count, tokens), f32),
+        ),
+        in_specs=[whole()] * 3,
+        out_specs=(whole(), whole()),
+        compiler_params=params(16),
+        cost_estimate=small(),
+        name="make_rows",
+    )(grad_out.T, top_logits.T, expert_ids.T)
+
+
+def chain_plan(depth):
+    products, weights = [], []
+    for z in range(depth):
+        uses = []
+        for turn in range(2, depth + 1):
+            if z < depth - 1 and turn >= z + 2:
+                uses.append((turn, "AB"[z % 2], depth + 1 + z - turn))
+            if z > 0 and turn >= depth - z + 1:
+                uses.append((turn, "BA"[z % 2], z + turn - depth - 1))
+        products.append(sorted(uses) + [(depth + 1, "own", z)])
+        brought = {}
+        for turn in range(1, depth):
+            for name in "AB":
+                index = z + turn if (name == "A") == (z % 2 == 0) else z - turn
+                brought[turn, name] = index if 0 <= index < depth else -1
+        weights.append(brought)
+    return products, weights
+
+
+class Scalars:
+    def __init__(self):
+        self.columns = []
+        self.names = {}
+
+    def add(self, name, values):
+        self.names[name] = len(self.columns)
+        self.columns.append(values)
+
+    def __getitem__(self, name):
+        return self.names[name]
+
+    def row(self, place, me):
+        return jnp.asarray(np.stack(self.columns, axis=-1).astype(np.int32))[place, me]
+
+
+def device_scalars(depth, experts):
+    products, weights = chain_plan(depth)
+    table = Scalars()
+    along = np.arange(2 * depth)[:, None] + np.zeros((1, experts), np.int32)
+
+    def by_z(values):
+        return np.asarray(values)[along // 2]
+
+    table.add("x", along % 2)
+    table.add("me", np.zeros_like(along) + np.arange(experts)[None, :])
+    table.add(("shard", 0, "own"), along // 2)
+    slot_of = [{use[2]: slot for slot, use in enumerate(products[z])} for z in range(depth)]
+    for part in range(depth):
+        table.add(("slot of", part), by_z([slot_of[z][part] for z in range(depth)]))
+    table.add(("slot", 0, "own"), by_z([slot_of[z][z] for z in range(depth)]))
+    for turn in range(1, depth):
+        for name in "AB":
+            shard = [weights[z][turn, name] for z in range(depth)]
+            table.add(("shard", turn, name), by_z(shard))
+            table.add(("slot", turn, name), by_z([slot_of[z].get(k, 0) for z, k in enumerate(shard)]))
+    uses = {}
+    for turn in range(2, depth + 1):
+        for name in "AB":
+            slots = [-1] * depth
+            for z in range(depth):
+                for slot, use in enumerate(products[z]):
+                    if use[:2] == (turn, name):
+                        slots[z] = slot
+            uses[turn, name] = slots
+            table.add(("use", turn, name), by_z(slots))
+            table.add(("block", turn, name), by_z([max(slot - 1, 0) for slot in slots]))
+    return table, weights, uses
+
+
+def hold_kernel(*refs):
+    del refs
+
+
+def hold(values, after):
+    return pl.pallas_call(
+        hold_kernel,
+        out_shape=tuple(jax.ShapeDtypeStruct(value.shape, value.dtype) for value in values),
+        in_specs=[anywhere()] * (len(values) + len(after)),
+        out_specs=(anywhere(),) * len(values),
+        input_output_aliases={place: place for place in range(len(values))},
+        cost_estimate=small(),
+        name="hold",
+    )(*values, *after)
+
+
+def split_kernel(table, where_ref, hidden_ref, *refs):
+    own_ref, first_ref, rest_ref = refs[-3:]
+    parts, units, _ = own_ref.shape
+    row = lax.broadcasted_iota(jnp.int32, (2 * units, 2 * units), 0)
+    column = lax.broadcasted_iota(jnp.int32, (2 * units, 2 * units), 1)
+    unit = jnp.where(row == column, 1.0, 0.0).astype(bf16)
+    low = where_ref[table["x"]] == 0
+    for part in range(parts):
+        block = hidden_ref[:, part * 2 * units : (part + 1) * 2 * units]
+        turned = dot(unit, block, NT).astype(bf16)
+        slot = where_ref[table["slot of", part]]
+        other = jnp.where(low, turned[units:], turned[:units])
+        own_ref[slot] = jnp.where(low, turned[:units], turned[units:])
+
+        @pl.when(slot == 0)
+        def _():
+            first_ref[0] = other
+
+        @pl.when(slot != 0)
+        def _():
+            rest_ref[slot - 1] = other
+
+
+def split_hidden(table, where, hidden, parts, units, after):
+    slots = hidden.shape[0]
+    return pl.pallas_call(
+        functools.partial(split_kernel, table),
+        out_shape=tuple(
+            jax.ShapeDtypeStruct((count, units, slots), bf16) for count in (parts, 1, parts - 1)
+        ),
+        in_specs=[scalars(), whole()] + [anywhere()] * len(after),
+        out_specs=(whole(),) * 3,
+        compiler_params=params(16),
+        cost_estimate=small(),
+        name="split_hidden",
+    )(where, hidden, *after)
+
+
+def place_of(place, count, me, tokens):
+    start = (place // count) * count * tokens + ((place % count) ^ me) * tokens
+    return pl.multiple_of(start, tokens)
+
+
+def products_kernel(table, model, count, number, first, where_ref, *refs):
+    blocks, gate_tiles = refs[:number], refs[number : 2 * number]
+    own_ref, other_ref = refs[2 * number : 2 * number + 2]
+    column, scaled, stacked = refs[-3:]
+    tokens, step = blocks[0].shape
+    slots = count * tokens
+    me = where_ref[table["me"]]
+    shift = model % LANES
+    shards = other_ref.shape[0]
+    units = other_ref.shape[1]
+    offset = own_ref.shape[0] - shards if not first else 0
+
+    @pl.when(pl.program_id(0) == 0)
+    def _():
+        lane = lax.broadcasted_iota(jnp.int32, (tokens, LANES), 1)
+        for place in range(number):
+            here = pl.ds(place_of(place, count, me, tokens), tokens)
+            picked = jnp.where(lane == shift + me, gate_tiles[place][...].astype(f32), 0.0)
+            total = jnp.sum(picked, axis=1, keepdims=True)
+            column[here, :] = jnp.broadcast_to(total, (tokens, LANES))
+        for shard in range(shards):
+            stacked[shard * units : (shard + 1) * units, :slots] = own_ref[offset + shard]
+            stacked[shard * units : (shard + 1) * units, slots:] = other_ref[shard]
+
+    for place in range(number):
+        here = pl.ds(place_of(place, count, me, tokens), tokens)
+        scaled[here, :] = (blocks[place][...].astype(f32) * column[here, 0:1]).astype(bf16)
+    total = dot(stacked[...], scaled[...], NN)
+    if first:
+        coming_ref = refs[2 * number + 2]
+        sent_ref, kept_ref = refs[-5:-3]
+        kept_ref[0] = total
+        flag = where_ref[table["use", 2, "A"]] == 0
+        sent_ref[...] = (coming_ref[...].astype(f32) + jnp.where(flag, total, 0.0)).astype(bf16)
+    else:
+        kept_ref = refs[-4]
+        for shard in range(shards):
+            kept_ref[shard] = total[shard * units : (shard + 1) * units]
+
+
+def products(table, where, blocks, own, other, model, step, coming, after, name):
+    tokens, width = blocks[0].shape
+    number = len(blocks)
+    shards, units, _ = other.shape
+    first = coming is not None
+    tile_spec = pl.BlockSpec((tokens, LANES), lambda j, s: (0, model // LANES))
+    block_spec = pl.BlockSpec((tokens, step), lambda j, s: (0, j))
+    flat_spec = pl.BlockSpec((units, step), lambda j, s: (0, j))
+    kept_spec = pl.BlockSpec((shards, units, step), lambda j, s: (0, 0, j))
+    kept = jax.ShapeDtypeStruct((shards, units, model), f32)
+    return pl.pallas_call(
+        functools.partial(products_kernel, table, model, number // 2, number, first),
+        out_shape=(jax.ShapeDtypeStruct((units, model), bf16), kept) if first else kept,
+        grid_spec=pltpu.PrefetchScalarGridSpec(
+            num_scalar_prefetch=1,
+            grid=(pl.cdiv(model, step),),
+            in_specs=[block_spec] * number
+            + [tile_spec] * number
+            + [whole()] * 2
+            + ([flat_spec] if first else [])
+            + [anywhere()] * len(after),
+            out_specs=(flat_spec, kept_spec) if first else kept_spec,
+            scratch_shapes=[
+                pltpu.VMEM((number * tokens, LANES), f32),
+                pltpu.VMEM((number * tokens, step), bf16),
+                pltpu.VMEM((shards * units, number * tokens), bf16),
+            ],
+        ),
+        compiler_params=params(24),
+        cost_estimate=small(),
+        name=name,
+    )(where, *blocks, *blocks, own, other, *([coming] if first else []), *after)
+
+
+def combine_kernel(table, key, sides, where_ref, coming_ref, *refs):
+    slot = where_ref[table[key]]
+    out_ref = refs[-1]
+    total = coming_ref[...].astype(f32)
+    for ref, side in zip(refs, sides):
+        flag = slot == 0 if side == "first" else slot > 0
+        total = total + jnp.where(flag, ref[0], 0.0)
+    out_ref[...] = total.astype(bf16)
+
+
+def combine(table, where, coming, first, rest, turn, name, used, after):
+    units, model = coming.shape
+    step = pl.cdiv(pl.cdiv(model, 2), LANES) * LANES
+    column = table["block", turn, name]
+    flat = pl.BlockSpec((units, step), lambda j, s: (0, j))
+    sides, operands, specs = [], [], []
+    if any(slot == 0 for slot in used):
+        sides, operands = ["first"], [first]
+        specs = [pl.BlockSpec((1, units, step), lambda j, s: (0, 0, j))]
+    if any(slot > 0 for slot in used):
+        sides, operands = sides + ["rest"], operands + [rest]
+        specs = specs + [pl.BlockSpec((1, units, step), lambda j, s: (s[column], 0, j))]
+    return pl.pallas_call(
+        functools.partial(combine_kernel, table, ("use", turn, name), sides),
+        out_shape=jax.ShapeDtypeStruct((units, model), bf16),
+        grid_spec=pltpu.PrefetchScalarGridSpec(
+            num_scalar_prefetch=1,
+            grid=(pl.cdiv(model, step),),
+            in_specs=[flat] + specs + [anywhere()] * len(after),
+            out_specs=flat,
+        ),
+        compiler_params=params(16),
+        cost_estimate=small(),
+        name="combine",
+    )(where, coming, *operands, *after)
+
+
+def total_kernel(a_ref, b_ref, kept_ref, out_ref):
+    out_ref[0] = kept_ref[0] + a_ref[...].astype(f32) + b_ref[...].astype(f32)
+
+
+def total_grad(a, b, rest):
+    units, model = a.shape
+    last = rest.shape[0] - 1
+    step = pl.cdiv(pl.cdiv(model, 2), LANES) * LANES
+    flat = pl.BlockSpec((units, step), lambda j: (0, j))
+    return pl.pallas_call(
+        total_kernel,
+        out_shape=jax.ShapeDtypeStruct((1, units, model), f32),
+        grid=(pl.cdiv(model, step),),
+        in_specs=[flat, flat, pl.BlockSpec((1, units, step), lambda j: (last, 0, j))],
+        out_specs=pl.BlockSpec((1, units, step), lambda j: (0, 0, j)),
+        compiler_params=params(16),
+        cost_estimate=small(),
+        name="total_grad",
+    )(a, b, rest)
+
+
+def back_kernel(table, model, count, choices, guard, summed, where_ref, *refs):
+    number = 2 * count
+    keys = [key for choice in choices for key in choice]
+    blocks = refs[:number]
+    own_ref, first_ref, rest_ref = refs[number : number + 3]
+    weight_refs = dict(zip(keys, refs[number + 3 : number + 3 + len(keys)]))
+    before_ref = refs[number + 3 + len(keys)] if summed else None
+    mine_ref, theirs_ref, sums_ref = refs[-3:]
+    tokens = blocks[0].shape[0]
+    units = own_ref.shape[1]
+    me = where_ref[table["me"]]
+    shift = model % LANES
+    start = (model // LANES) * LANES
+    eight = lax.broadcasted_iota(jnp.int32, (8, LANES), 1)
+    onehot = jnp.where(eight == shift + me, 1.0, 0.0).astype(bf16)
+    shards = {key: where_ref[table[("shard",) + key]] for key in keys}
+    slots = {key: where_ref[table[("slot",) + key]] for key in keys}
+    sums_ref[...] = before_ref[...] if summed else jnp.zeros(sums_ref.shape, f32)
+
+    def work():
+        stack, here_valid, here_slot = [], [], []
+        for choice in choices:
+            weight, valid, slot = weight_refs[choice[0]][...], shards[choice[0]] >= 0, slots[choice[0]]
+            for key in choice[1:]:
+                weight = jnp.where(valid, weight, weight_refs[key][...])
+                slot = jnp.where(valid, slot, slots[key])
+                valid = jnp.logical_or(valid, shards[key] >= 0)
+            stack.append(weight)
+            here_valid.append(valid)
+            here_slot.append(slot)
+        weight = jnp.concatenate(stack, axis=0) if len(stack) > 1 else stack[0]
+        for pair in range(0, number, 2):
+            both = jnp.concatenate([blocks[pair][:, :model], blocks[pair + 1][:, :model]], axis=0)
+            product = dot(weight, both, NT)
+            for half in range(2):
+                place = pair + half
+                block = product[:, half * tokens : (half + 1) * tokens]
+                gate = dot(onehot, blocks[place][:, start : start + LANES], NT)[0:1]
+                lanes = place_of(place % count, count, me, tokens)
+                wide = place_of(place, count, me, tokens)
+                out_ref = mine_ref if place < count else theirs_ref
+                gated = (block * gate).astype(bf16)
+                total = jnp.zeros((1, tokens), f32)
+                for index, (valid, slot) in enumerate(zip(here_valid, here_slot)):
+                    some = slice(index * units, (index + 1) * units)
+                    out_ref[index, :, pl.ds(lanes, tokens)] = gated[some]
+                    if place < count:
+                        hidden = own_ref[slot, :, pl.ds(lanes, tokens)].astype(f32)
+                    else:
+                        hidden = jnp.where(
+                            slot == 0,
+                            first_ref[0, :, pl.ds(lanes, tokens)].astype(f32),
+                            rest_ref[jnp.maximum(slot - 1, 0), :, pl.ds(lanes, tokens)].astype(f32),
+                        )
+                    part = jnp.sum(hidden * block[some], axis=0, keepdims=True)
+                    total = total + jnp.where(valid, part, 0.0)
+                sums_ref[0:1, pl.ds(wide, tokens)] += total
+
+    if guard:
+        some = functools.reduce(jnp.logical_or, [shards[key] >= 0 for key in keys])
+        pl.when(some)(work)
+    else:
+        work()
+
+
+def back_part(table, where, blocks, own, first, rest, choices, weights, before, guard, after, model):
+    units, slots = own.shape[1:]
+    keys = [key for choice in choices for key in choice]
+    count = len(blocks) // 2
+    half = jax.ShapeDtypeStruct((len(choices), units, slots), bf16)
+    summed = before is not None
+    operands = [*blocks, own, first, rest, *[weights[key] for key in keys]] + ([before] if summed else [])
+    return pl.pallas_call(
+        functools.partial(back_kernel, table, model, count, choices, guard, summed),
+        out_shape=(half, half, jax.ShapeDtypeStruct((8, 2 * slots), f32)),
+        in_specs=[scalars()] + [whole()] * len(operands) + [anywhere()] * len(after),
+        out_specs=(whole(),) * 3,
+        compiler_params=params(32),
+        cost_estimate=small(),
+        name="back_part",
+    )(where, *operands, *after)
+
+
+def join_kernel(table, groups, extends, where_ref, *refs):
+    out_ref, turned, sem = refs[-3:]
+    slots, _, width = turned.shape[1], turned.shape[0], turned.shape[2]
+    units = width // 2
+    row = lax.broadcasted_iota(jnp.int32, (slots, slots), 0)
+    column = lax.broadcasted_iota(jnp.int32, (slots, slots), 1)
+    unit = jnp.where(row == column, 1.0, 0.0).astype(bf16)
+    low = where_ref[table["x"]] == 0
+    copies = []
+    total = 0
+    for number, choices in enumerate(groups):
+        mine_ref, theirs_ref = refs[2 * number], refs[2 * number + 1]
+        for place, choice in enumerate(choices):
+            index = where_ref[table[("shard",) + choice[0]]]
+            for key in choice[1:]:
+                index = jnp.where(index >= 0, index, where_ref[table[("shard",) + key]])
+            mine, theirs = mine_ref[place], theirs_ref[place]
+            both = jnp.concatenate(
+                [jnp.where(low, mine, theirs), jnp.where(low, theirs, mine)], axis=0
+            )
+            turned[total] = dot(unit, both, NT).astype(bf16)
+            here = pl.ds(pl.multiple_of(jnp.maximum(index, 0) * width, LANES), width)
+            copy = pltpu.make_async_copy(turned.at[total], out_ref.at[:, here], sem.at[total])
+            copies.append((index, copy))
+
+            @pl.when(index >= 0)
+            def _():
+                copy.start()
+
+            total += 1
+    for index, copy in copies:
+        pl.when(index >= 0)(copy.wait)
+
+
+def join_hidden(table, where, groups, pairs, slots, hidden, before):
+    flat = [array for pair in pairs for array in pair]
+    units = flat[0].shape[1]
+    total = sum(len(choices) for choices in groups)
+    extends = before is not None
+    return pl.pallas_call(
+        functools.partial(join_kernel, table, groups, extends),
+        out_shape=jax.ShapeDtypeStruct((slots, hidden), bf16),
+        in_specs=[scalars()] + [whole()] * len(flat) + [anywhere()] * extends,
+        out_specs=anywhere(),
+        scratch_shapes=[
+            pltpu.VMEM((total, slots, 2 * units), bf16),
+            pltpu.SemaphoreType.DMA((total,)),
+        ],
+        input_output_aliases={1 + len(flat): 0} if extends else {},
+        compiler_params=params(24),
+        cost_estimate=small(),
+        name="join_hidden",
+    )(where, *flat, *([before] if extends else []))
+
+
+def logits_kernel(gates_ref, ids_ref, grads_ref, out_ref):
+    gates, ids, grads = gates_ref[...], ids_ref[...], grads_ref[...]
+    picked = jnp.zeros_like(gates)
+    for expert in range(grads.shape[0]):
+        picked = picked + jnp.where(ids == expert, grads[expert : expert + 1, :], 0.0)
+    out_ref[...] = gates * (picked - jnp.sum(gates * picked, axis=0, keepdims=True))
+
+
+def logits_grad(gates, ids, grads):
+    return pl.pallas_call(
+        logits_kernel,
+        out_shape=jax.ShapeDtypeStruct(gates.shape, f32),
+        in_specs=[whole()] * 3,
+        out_specs=whole(),
+        cost_estimate=small(),
+        name="logits_grad",
+    )(gates, ids, grads)
+
+
+def per_device_full(grad_out, top_logits, expert_ids, saved_hidden, w_down):
+    experts = lax.axis_size("exp")
+    groups = lax.axis_size("ctx")
+    depth = groups // 2
+    tokens, model = grad_out.shape
+    slots, hidden = saved_hidden.shape[2:]
+    units = w_down.shape[1]
+    width = pl.cdiv(model + experts, LANES) * LANES
+    step = 4 * LANES
+
+    table, brought, uses = device_scalars(depth, experts)
+    where = table.row(lax.axis_index("ctx"), lax.axis_index("exp"))
+
+    def swap_x(value):
+        return lax.ppermute(value, "ctx", [(i, i ^ 1) for i in range(groups)])
+
+    def swap_exp(value, bit):
+        return lax.ppermute(value, "exp", [(i, i ^ bit) for i in range(experts)])
+
+    def swap_z(value, name):
+        first = "AB".index(name)
+        pairs = []
+        for z in range(first, depth - 1, 2):
+            for x in range(2):
+                pairs += [(2 * z + x, 2 * z + 2 + x), (2 * z + 2 + x, 2 * z + x)]
+        return lax.ppermute(value, "ctx", pairs)
+
+    got = {(0, "own"): w_down[0]}
+    for name in "AB":
+        got[1, name] = swap_z(w_down[0], name)
+    got[2, "B"] = swap_z(got[1, "A"], "B")
+
+    rows, gates = make_rows(grad_out, top_logits, expert_ids, width)
+    own, other_first, other_rest = split_hidden(table, where, saved_hidden[0, 0], depth, units, [rows])
+    across, other_first, other_rest = hold((swap_x(rows), other_first, other_rest), [])
+    other_first, other_rest = swap_x(other_first), swap_x(other_rest)
+    near, far, order = [rows], [across], [0]
+    bit = experts // 2
+    while bit:
+        fresh = [swap_exp(block, bit) for block in near]
+        if len(near) == 1:
+            fresh = list(hold(fresh, [got[1, "A"], got[1, "B"]]))
+        near = near + fresh
+        distant = [swap_exp(block, bit) for block in far]
+        if len(far) == 1:
+            distant = list(hold(distant, [other_first, other_rest]))
+        far = far + distant
+        order = order + [k ^ bit for k in order]
+        bit //= 2
+    blocks = [near[order.index(k)] for k in range(experts)]
+    blocks += [far[order.index(k)] for k in range(experts)]
+
+    sent, kept_first = products(
+        table, where, blocks, own, other_first, model, step, got[1, "B"], [other_rest], "first_product"
+    )
+    got[2, "A"] = swap_z(sent, "A")
+    kept_rest = products(
+        table, where, blocks, own, other_rest, model, step, None, [sent], "other_products"
+    )
+
+    groups_of = [[[(0, "own")], [(1, "A")], [(1, "B")]]]
+    pairs = []
+
+    def backprop(choices, before, guard, after):
+        mine, theirs, sums = back_part(
+            table, where, blocks, own, other_first, other_rest, choices, got, before, guard, after, model
+        )
+        pairs.append((mine, swap_x(theirs)))
+        return sums
+
+    sums = backprop(groups_of[0], None, False, [kept_rest])
+    marker = sums
+    for turn in range(3, depth + 1):
+        for name, back in (("A", "B"), ("B", "A")):
+            used = uses[turn, name]
+            value = combine(
+                table, where, got[turn - 1, back], kept_first, kept_rest, turn, name, used, [marker]
+            )
+            marker = value
+            got[turn, name] = swap_z(value, name)
+        last = turn - 1
+        both = any(b[last, "A"] >= 0 and b[last, "B"] >= 0 for b in brought)
+        choices = [[(last, "A")], [(last, "B")]] if both else [[(last, "A"), (last, "B")]]
+        groups_of.append(choices)
+        sums = backprop(choices, sums, not both, [marker])
+        marker = sums
+    weight_grad = total_grad(got[depth, "A"], got[depth, "B"], kept_rest)
+
+    hidden_grad = join_hidden(table, where, groups_of, pairs, slots, hidden, None)
+    slot_grad = sums[0:1, :slots] + swap_x(sums[0:1, slots:])
+    grads = lax.all_to_all(
+        slot_grad.reshape(experts, tokens), "exp", split_axis=0, concat_axis=0, tiled=True
+    )
+    logit_grad = logits_grad(gates, expert_ids.T, grads).T
+    return (logit_grad, hidden_grad[None, None], weight_grad)
 
 
 def routing_tables(expert_ids, count_experts, capacity):
@@ -14,7 +608,7 @@
     return (matches.astype(jnp.float32), select)
 
 
-def per_device(grad_out, top_logits, expert_ids, saved_hidden, w_down):
+def per_device_routed(grad_out, top_logits, expert_ids, saved_hidden, w_down):
     count_experts = lax.axis_size("exp")
     slot_count = saved_hidden.shape[2]
     capacity = slot_count // count_experts
@@ -57,6 +651,15 @@
     return (logit_grad, hidden_grad.reshape(1, 1, slot_count, -1), weight_grad[None])
 
 
+def per_device(grad_out, top_logits, expert_ids, saved_hidden, w_down):
+    experts = lax.axis_size("exp")
+    groups = lax.axis_size("ctx")
+    everywhere = top_logits.shape[1] == experts and saved_hidden.shape[2] == experts * grad_out.shape[0]
+    plain = experts & (experts - 1) == 0 and groups % 4 == 0 and groups >= 8
+    body = per_device_full if everywhere and plain else per_device_routed
+    return body(grad_out, top_logits, expert_ids, saved_hidden, w_down)
+
+
 def solution(mesh):
     return jax.shard_map(
         per_device,

time: 518 us -> 163 us (0.31)
  waiting for transfers between devices: 428 us -> 34 us
  Pallas kernels: 0 us -> 53.6 us
  starting transfers between devices: 7.67 us -> 48.4 us
  matrix products: 23.2 us -> 0 us
  local copies, waits for them, and re-layouts: 32.4 us -> 18.5 us
  between operations: 14.1 us -> 0.92 us
  other arithmetic: 5.37 us -> 0.01 us
    unnamed x3 -> x0, waiting for transfers between devices: 297 us -> none
    all_gather x1 -> x0, waiting for transfers between devices: 92.6 us -> none  [per_device(): lax.all_gather(w_down[0], 'ctx', axis=0, tiled=True)]
    pallas_call x0 -> x17, Pallas kernels: none -> 53.6 us  [the longest x3 19.2 us: back_part(): pl.pallas_call(functools.partial(back_kernel, table, model, count, choice...]
    ppermute x0 -> x21, starting transfers between devices: none -> 48.4 us  [the longest x8 35.1 us: swap_z(): return lax.ppermute(value, 'ctx', pairs)]
    all_to_all x2 -> x0, waiting for transfers between devices: 38.4 us -> none  [the longest x1 34.8 us: per_device(): lax.all_to_all(send_rows, 'exp', split_axis=0, concat_axis=0, tiled=True)]
    ppermute x0 -> x21, waiting for transfers between devices: none -> 34 us  [the longest x7 19.4 us: swap_x(): return lax.ppermute(value, 'ctx', [(i, i ^ 1) for i in range(groups)])]
    dot_general x3 -> x0, matrix products: 23.2 us -> none  [the longest x1 10.6 us: per_device(): lax.dot_general(flat_rows, lax.all_gather(w_down[0], 'ctx', axis=0, tiled...]
    unnamed x13 -> x58, local copies, waits for them, and re-layouts: 26.1 us -> 17.8 us
  transfers between devices with their start and end apart: 4 -> 21, of which waited for: 4 -> 8; matrix products, arithmetic and copies ran while one was open for 2% -> 0% of each run, Pallas kernels for 0% -> 30%
where the time goes in v2:
time: 163 us; the launch traced here: 162 us
  Pallas kernels  53.6 us (33%)
  starting transfers between devices  48.4 us (30%)
  waiting for transfers between devices  34 us (21%)
  local copies, waits for them, and re-layouts  18.5 us (11%)
  blocking collectives  6.6 us (4%)
    ppermute x8, starting transfers between devices, swap_z(): return lax.ppermute(value, 'ctx', pairs)  35.1 us
    ppermute x7, waiting for transfers between devices, swap_x(): return lax.ppermute(value, 'ctx', [(i, i ^ 1) for i in range(groups)])  19.4 us
    pallas_call x3, Pallas kernels, back_part(): pl.pallas_call(functools.partial(back_kernel, table, model, count, choice...  19.2 us
    pallas_call x2, Pallas kernels, products(): pl.pallas_call(functools.partial(products_kernel, table, model, number //...  18.3 us
    unnamed x58, local copies, waits for them, and re-layouts  17.8 us
    ppermute x7, starting transfers between devices, swap_x(): return lax.ppermute(value, 'ctx', [(i, i ^ 1) for i in range(groups)])  10 us
    ppermute x8, waiting for transfers between devices, swap_z(): return lax.ppermute(value, 'ctx', pairs)  7.82 us
    ppermute x6, waiting for transfers between devices, swap_exp(): return lax.ppermute(value, 'exp', [(i, i ^ bit) for i in range(experts)])  6.7 us
  transfers between devices with their start and end apart: 21, of which 8 were waited for; matrix products, arithmetic and copies ran while one was open for 0% of the time, Pallas kernels for 30%

profile of v2, /device:TPU:0, one launch (start us, length us, event | category | flops | bytes accessed | tf_op | source)
XLA Modules:
  0.0 162.0 jit_solution(18374462264248549922)
XLA Ops:
  3.4 3.0 %collective-permute-start.5 = (bf16[128,2944]{1,0:T(8,128)(2,1)S(1)}, bf16[128,2944]{1,0:T(8,128)(2,1)S(1)}, u32[]{:S(2)}, u32[]{:S(2)}) collective-permute-start(bf16[128,2944]{1,0:T(8,128)(2,1)S(1)} %get-tuple-element.23.refs_0_.refs_8_), channel_id=1, source_target_pairs={{0,4},{4,0},{8,12},{12,8},{16,20},{20,16},{24,28},{28,24},{1,5},{5... | collective-permute-start | bytes 2261000 | tf_op jit(solution)/shard_map/ppermute | solution.py:518
  6.4 1.7 %collective-permute-start.3 = (bf16[192,2880]{1,0:T(8,128)(2,1)}, bf16[192,2880]{1,0:T(8,128)(2,1)}, u32[]{:S(2)}, u32[]{:S(2)}) collective-permute-start(bf16[192,2880]{1,0:T(8,128)(2,1)} %bitcast.15), channel_id=1, source_target_pairs={{8,16},{16,8},{12,20},{20,12},{9,17},{17,9},{13,21},{21,13},{10,18... | collective-permute-start | bytes 3317768 | tf_op jit(solution)/shard_map/ppermute | solution.py:529
  8.1 3.4 %collective-permute-start.2 = (bf16[192,2880]{1,0:T(8,128)(2,1)}, bf16[192,2880]{1,0:T(8,128)(2,1)}, u32[]{:S(2)}, u32[]{:S(2)}) collective-permute-start(bf16[192,2880]{1,0:T(8,128)(2,1)} %bitcast.16), channel_id=1, source_target_pairs={{0,8},{8,0},{4,12},{12,4},{16,24},{24,16},{20,28},{28,20},{1,9},{9... | collective-permute-start | bytes 3317768 | tf_op jit(solution)/shard_map/ppermute | solution.py:529
  15.2 2.2 %split_hidden.1 = (bf16[4,192,512]{2,1,0:T(8,128)(2,1)S(1)}, bf16[1,192,512]{2,1,0:T(8,128)(2,1)S(1)}, bf16[3,192,512]{2,1,0:T(8,128)(2,1)S(1)}) custom-call(s32[32]{0:T(128)S(1)} %dynamic-slice_bitcast_fusion.where_ref, bf16[512,1536]{1,0:T(8,128)(2,1)S(1)} %bitcast.14, bf16[128,2944]{1,0:T(8,128)(2,1)S(1)} %get-tuple-element.23.refs_0_.refs_8_), custom_call_target="tpu_custom_call" | custom-call | tf_op jit(solution)/shard_map/split_hidden/pallas_call | solution.py:197
  19.7 3.5 %collective-permute-done.5.refs_0_ = bf16[128,2944]{1,0:T(8,128)(2,1)S(1)} collective-permute-done((bf16[128,2944]{1,0:T(8,128)(2,1)S(1)}, bf16[128,2944]{1,0:T(8,128)(2,1)S(1)}, u32[]{:S(2)}, u32[]{:S(2)}) %collective-permute-start.5) | collective-permute-done | bytes 753696 | tf_op jit(solution)/shard_map/ppermute | solution.py:518
  24.1 1.8 %collective-permute-start.7 = (bf16[128,2944]{1,0:T(8,128)(2,1)}, bf16[128,2944]{1,0:T(8,128)(2,1)S(1)}, u32[]{:S(2)}, u32[]{:S(2)}) collective-permute-start(bf16[128,2944]{1,0:T(8,128)(2,1)} %get-tuple-element.26.refs_4_.refs_12_), channel_id=1, source_target_pairs={{0,2},{1,3},{2,0},{3,1},{4,6},{5,7},{6,4},{7,5},{8,10},{9,11},{10,... | collective-permute-start | bytes 2261000 | tf_op jit(solution)/shard_map/ppermute | solution.py:521
  27.4 3.9 %collective-permute-done.1.refs_0_ = bf16[128,2944]{1,0:T(8,128)(2,1)S(1)} collective-permute-done((bf16[128,2944]{1,0:T(8,128)(2,1)S(1)}, bf16[128,2944]{1,0:T(8,128)(2,1)S(1)}, u32[]{:S(2)}, u32[]{:S(2)}) %collective-permute-start.1) | collective-permute-done | bytes 753696 | tf_op jit(solution)/shard_map/ppermute | solution.py:521
  31.9 4.3 %collective-permute-done.2.refs_1_.refs_12_ = bf16[192,2880]{1,0:T(8,128)(2,1)} collective-permute-done((bf16[192,2880]{1,0:T(8,128)(2,1)}, bf16[192,2880]{1,0:T(8,128)(2,1)}, u32[]{:S(2)}, u32[]{:S(2)}) %collective-permute-start.2) | collective-permute-done | bytes 1105952 | tf_op jit(solution)/shard_map/ppermute | solution.py:529
  36.2 8.1 %collective-permute-done.8.refs_1_.refs_17_.refs_9_ = bf16[1,192,512]{2,1,0:T(8,128)(2,1)S(1)} collective-permute-done((bf16[1,192,512]{2,1,0:T(8,128)(2,1)}, bf16[1,192,512]{2,1,0:T(8,128)(2,1)S(1)}, u32[]{:S(2)}, u32[]{:S(2)}) %collective-permute-start.8) | collective-permute-done | bytes 196640 | tf_op jit(solution)/shard_map/ppermute | solution.py:518
  52.0 7.8 %first_product.1 = (bf16[192,2880]{1,0:T(8,128)(2,1)S(1)}, f32[1,192,2880]{2,1,0:T(8,128)S(1)}) custom-call(s32[32]{0:T(128)S(1)} %dynamic-slice_bitcast_fusion.where_ref, bf16[128,2944]{1,0:T(8,128)(2,1)S(1)} %get-tuple-element.23.refs_0_.refs_8_, bf16[128,2944]{1,0:T(8,128)(2,1)} %collective-permute-done.refs_1_.refs_9_, bf16[128,2944]{1,0:T(8,128)(2,1)S(1)} %copy-done.3, ...), custom_call_target="tpu_custom_call" | custom-call | tf_op jit(solution)/shard_map/first_product/pallas_call | solution.py:265
  59.8 2.3 %collective-permute-start.13 = (bf16[192,2880]{1,0:T(8,128)(2,1)S(1)}, bf16[192,2880]{1,0:T(8,128)(2,1)S(1)}, u32[]{:S(2)}, u32[]{:S(2)}) collective-permute-start(bf16[192,2880]{1,0:T(8,128)(2,1)S(1)} %get-tuple-element.30.refs_18_), channel_id=1, source_target_pairs={{0,8},{8,0},{4,12},{12,4},{16,24},{24,16},{20,28},{28,20},{1,9},{9... | collective-permute-start | bytes 3317768 | tf_op jit(solution)/shard_map/ppermute | solution.py:529
  62.2 10.5 %other_products.1.refs_14_.refs_0_.kept_ref = f32[3,192,2880]{2,1,0:T(8,128)S(1)} custom-call(s32[32]{0:T(128)S(1)} %dynamic-slice_bitcast_fusion.where_ref, bf16[128,2944]{1,0:T(8,128)(2,1)S(1)} %get-tuple-element.23.refs_0_.refs_8_, bf16[128,2944]{1,0:T(8,128)(2,1)} %collective-permute-done.refs_1_.refs_9_, bf16[128,2944]{1,0:T(8,128)(2,1)S(1)} %copy-done.3, ...), custom_call_target="tpu_custom_call" | custom-call | tf_op jit(solution)/shard_map/other_products/pallas_call | solution.py:265
  72.7 9.9 %back_part.3 = (bf16[3,192,512]{2,1,0:T(8,128)(2,1)S(1)}, bf16[3,192,512]{2,1,0:T(8,128)(2,1)}, f32[8,1024]{1,0:T(8,128)S(1)}) custom-call(s32[32]{0:T(128)S(1)} %dynamic-slice_bitcast_fusion.where_ref, bf16[128,2944]{1,0:T(8,128)(2,1)S(1)} %get-tuple-element.23.refs_0_.refs_8_, bf16[128,2944]{1,0:T(8,128)(2,1)} %collective-permute-done.refs_1_.refs_9_, ...), custom_call_target="tpu_custom_call" | custom-call | tf_op jit(solution)/shard_map/back_part/pallas_call | solution.py:419
  84.0 3.5 %collective-permute-done.13.coming_ref.refs_11_ = bf16[192,2880]{1,0:T(8,128)(2,1)S(1)} collective-permute-done((bf16[192,2880]{1,0:T(8,128)(2,1)S(1)}, bf16[192,2880]{1,0:T(8,128)(2,1)S(1)}, u32[]{:S(2)}, u32[]{:S(2)}) %collective-permute-start.13) | collective-permute-done | bytes 1105952 | tf_op jit(solution)/shard_map/ppermute | solution.py:529
  89.6 3.4 %collective-permute-start.12 = (bf16[192,2880]{1,0:T(8,128)(2,1)S(1)}, bf16[192,2880]{1,0:T(8,128)(2,1)S(1)}, u32[]{:S(2)}, u32[]{:S(2)}) collective-permute-start(bf16[192,2880]{1,0:T(8,128)(2,1)S(1)} %combine.4.refs_1_), channel_id=1, source_target_pairs={{0,8},{8,0},{4,12},{12,4},{16,24},{24,16},{20,28},{28,20},{1,9},{9... | collective-permute-start | bytes 3317768 | tf_op jit(solution)/shard_map/ppermute | solution.py:529
  93.0 4.7 %back_part.4 = (bf16[1,192,512]{2,1,0:T(8,128)(2,1)S(1)}, bf16[1,192,512]{2,1,0:T(8,128)(2,1)}, f32[8,1024]{1,0:T(8,128)S(1)}) custom-call(s32[32]{0:T(128)S(1)} %dynamic-slice_bitcast_fusion.where_ref, bf16[128,2944]{1,0:T(8,128)(2,1)S(1)} %get-tuple-element.23.refs_0_.refs_8_, bf16[128,2944]{1,0:T(8,128)(2,1)} %collective-permute-done.refs_1_.refs_9_, ...), custom_call_target="tpu_custom_call" | custom-call | tf_op jit(solution)/shard_map/back_part/pallas_call | solution.py:419
  99.1 21.0 %collective-permute-start.19 = (bf16[192,2880]{1,0:T(8,128)(2,1)S(1)}, bf16[192,2880]{1,0:T(8,128)(2,1)}, u32[]{:S(2)}, u32[]{:S(2)}) collective-permute-start(bf16[192,2880]{1,0:T(8,128)(2,1)S(1)} %combine.6.refs_1_), channel_id=1, source_target_pairs={{0,8},{8,0},{4,12},{12,4},{16,24},{24,16},{20,28},{28,20},{1,9},{9... | collective-permute-start | bytes 3317768 | tf_op jit(solution)/shard_map/ppermute | solution.py:529
  120.2 2.1 %combine.7.refs_14_ = bf16[192,2880]{1,0:T(8,128)(2,1)} custom-call(s32[32]{0:T(128)S(1)} %dynamic-slice_bitcast_fusion.where_ref, bf16[192,2880]{1,0:T(8,128)(2,1)S(1)} %collective-permute-done.12.coming_ref.refs_11_, f32[3,192,2880]{2,1,0:T(8,128)S(1)} %other_products.1.refs_14_.refs_0_.kept_ref, bf16[192,2880]{1,0:T(8,128)(2,1)S(1)} %combine.6.refs_1_), custom_call_target="tpu_custom_call" | custom-call | tf_op jit(solution)/shard_map/combine/pallas_call | solution.py:311
  125.4 4.6 %back_part.5 = (bf16[1,192,512]{2,1,0:T(8,128)(2,1)S(1)}, bf16[1,192,512]{2,1,0:T(8,128)(2,1)}, f32[8,1024]{1,0:T(8,128)S(1)}) custom-call(s32[32]{0:T(128)S(1)} %dynamic-slice_bitcast_fusion.where_ref, bf16[128,2944]{1,0:T(8,128)(2,1)S(1)} %get-tuple-element.23.refs_0_.refs_8_, bf16[128,2944]{1,0:T(8,128)(2,1)} %collective-permute-done.refs_1_.refs_9_, ...), custom_call_target="tpu_custom_call" | custom-call | tf_op jit(solution)/shard_map/back_part/pallas_call | solution.py:419
  132.7 7.8 %collective-permute-done.15 = f32[1,512]{1,0:T(1,128)S(1)} collective-permute-done((f32[1,512]{1,0:T(1,128)S(1)}, f32[1,512]{1,0:T(1,128)S(1)}, u32[]{:S(2)}, u32[]{:S(2)}) %collective-permute-start.15) | collective-permute-done | bytes 2080 | tf_op jit(solution)/shard_map/ppermute | solution.py:518
  142.0 6.6 %all_to_all.11 = f32[4,1,128]{2,1,0:T(1,128)} all-to-all(f32[4,1,128]{2,1,0:T(1,128)S(1)} %add_bitcast_fusion), channel_id=1, replica_groups=mesh['ctx'=8,'exp'=4] {'exp'}, dimensions={0} | all-to-all | bytes 4096 | tf_op jit(solution)/shard_map/all_to_all | solution.py:594
  152.8 3.4 %join_hidden.1 = bf16[512,1536]{1,0:T(8,128)(2,1)} custom-call(s32[32]{0:T(128)S(1)} %dynamic-slice_bitcast_fusion.where_ref, bf16[3,192,512]{2,1,0:T(8,128)(2,1)S(1)} %copy-done.20, bf16[3,192,512]{2,1,0:T(8,128)(2,1)} %collective-permute-done.16.refs_1_, bf16[1,192,512]{2,1,0:T(8,128)(2,1)S(1)} %copy-done.23, ...), custom_call_target="tpu_custom_call" | custom-call | tf_op jit(solution)/shard_map/join_hidden/pallas_call | solution.py:469
  156.3 2.9 %copy-done.1 = f32[3,192,2880]{2,1,0:T(8,128)S(1)} copy-done((f32[3,192,2880]{2,1,0:T(8,128)S(1)}, f32[3,192,2880]{2,1,0:T(8,128)}, u32[]{:S(2)}) %copy-start.1) | copy-done | bytes 6635544
  159.2 2.8 %total_grad.1 = f32[1,192,2880]{2,1,0:T(8,128)} custom-call(bf16[192,2880]{1,0:T(8,128)(2,1)} %collective-permute-done.19.a_ref, bf16[192,2880]{1,0:T(8,128)(2,1)} %collective-permute-done.20.b_ref, f32[3,192,2880]{2,1,0:T(8,128)S(1)} %copy-done.1), custom_call_target="tpu_custom_call" | custom-call | tf_op jit(solution)/shard_map/total_grad/pallas_call | solution.py:335
  (97 shorter events, 35.7 us)
Async XLA Ops:
  3.4 19.8 %collective-permute-start.5 = (bf16[128,2944]{1,0:T(8,128)(2,1)S(1)}, bf16[128,2944]{1,0:T(8,128)(2,1)S(1)}, u32[]{:S(2)}, u32[]{:S(2)}) collective-permute-start(bf16[128,2944]{1,0:T(8,128)(2,1)S(1)} %get-tuple-element.23.refs_0_.refs_8_), channel_id=1, source_target_pairs={{0,4},{4,0},{8,12},{12,8},{16,20},{20,16},{24,28},{28,24},{1,5},{5... | collective-permute-start | bytes 2261000 | tf_op jit(solution)/shard_map/ppermute | solution.py:518
  6.4 25.5 %collective-permute-start.3 = (bf16[192,2880]{1,0:T(8,128)(2,1)}, bf16[192,2880]{1,0:T(8,128)(2,1)}, u32[]{:S(2)}, u32[]{:S(2)}) collective-permute-start(bf16[192,2880]{1,0:T(8,128)(2,1)} %bitcast.15), channel_id=1, source_target_pairs={{8,16},{16,8},{12,20},{20,12},{9,17},{17,9},{13,21},{21,13},{10,18... | collective-permute-start | bytes 3317768 | tf_op jit(solution)/shard_map/ppermute | solution.py:529
  8.1 28.1 %collective-permute-start.2 = (bf16[192,2880]{1,0:T(8,128)(2,1)}, bf16[192,2880]{1,0:T(8,128)(2,1)}, u32[]{:S(2)}, u32[]{:S(2)}) collective-permute-start(bf16[192,2880]{1,0:T(8,128)(2,1)} %bitcast.16), channel_id=1, source_target_pairs={{0,8},{8,0},{4,12},{12,4},{16,24},{24,16},{20,28},{28,20},{1,9},{9... | collective-permute-start | bytes 3317768 | tf_op jit(solution)/shard_map/ppermute | solution.py:529
  11.5 19.8 %collective-permute-start.1 = (bf16[128,2944]{1,0:T(8,128)(2,1)S(1)}, bf16[128,2944]{1,0:T(8,128)(2,1)S(1)}, u32[]{:S(2)}, u32[]{:S(2)}) collective-permute-start(bf16[128,2944]{1,0:T(8,128)(2,1)S(1)} %get-tuple-element.23.refs_0_.refs_8_), channel_id=1, source_target_pairs={{0,2},{1,3},{2,0},{3,1},{4,6},{5,7},{6,4},{7,5},{8,10},{9,11},{10,... | collective-permute-start | bytes 2261000 | tf_op jit(solution)/shard_map/ppermute | solution.py:521
  24.1 21.3 %collective-permute-start.7 = (bf16[128,2944]{1,0:T(8,128)(2,1)}, bf16[128,2944]{1,0:T(8,128)(2,1)S(1)}, u32[]{:S(2)}, u32[]{:S(2)}) collective-permute-start(bf16[128,2944]{1,0:T(8,128)(2,1)} %get-tuple-element.26.refs_4_.refs_12_), channel_id=1, source_target_pairs={{0,2},{1,3},{2,0},{3,1},{4,6},{5,7},{6,4},{7,5},{8,10},{9,11},{10,... | collective-permute-start | bytes 2261000 | tf_op jit(solution)/shard_map/ppermute | solution.py:521
  25.9 18.5 %collective-permute-start.9 = (bf16[3,192,512]{2,1,0:T(8,128)(2,1)}, bf16[3,192,512]{2,1,0:T(8,128)(2,1)}, u32[]{:S(2)}, u32[]{:S(2)}) collective-permute-start(bf16[3,192,512]{2,1,0:T(8,128)(2,1)} %get-tuple-element.28), channel_id=1, source_target_pairs={{0,4},{4,0},{8,12},{12,8},{16,20},{20,16},{24,28},{28,24},{1,5},{5... | collective-permute-start | bytes 1769480 | tf_op jit(solution)/shard_map/ppermute | solution.py:518
  31.3 13.0 %collective-permute-start.8 = (bf16[1,192,512]{2,1,0:T(8,128)(2,1)}, bf16[1,192,512]{2,1,0:T(8,128)(2,1)S(1)}, u32[]{:S(2)}, u32[]{:S(2)}) collective-permute-start(bf16[1,192,512]{2,1,0:T(8,128)(2,1)} %get-tuple-element.27), channel_id=1, source_target_pairs={{0,4},{4,0},{8,12},{12,8},{16,20},{20,16},{24,28},{28,24},{1,5},{5... | collective-permute-start | bytes 589832 | tf_op jit(solution)/shard_map/ppermute | solution.py:518
  31.9 15.2 %collective-permute-start = (bf16[128,2944]{1,0:T(8,128)(2,1)S(1)}, bf16[128,2944]{1,0:T(8,128)(2,1)}, u32[]{:S(2)}, u32[]{:S(2)}) collective-permute-start(bf16[128,2944]{1,0:T(8,128)(2,1)S(1)} %get-tuple-element.23.refs_0_.refs_8_), channel_id=1, source_target_pairs={{0,1},{1,0},{2,3},{3,2},{4,5},{5,4},{6,7},{7,6},{8,9},{9,8},{10,11... | collective-permute-start | bytes 2261000 | tf_op jit(solution)/shard_map/ppermute | solution.py:521
  36.2 10.9 %collective-permute-start.6 = (bf16[128,2944]{1,0:T(8,128)(2,1)}, bf16[128,2944]{1,0:T(8,128)(2,1)}, u32[]{:S(2)}, u32[]{:S(2)}) collective-permute-start(bf16[128,2944]{1,0:T(8,128)(2,1)} %get-tuple-element.26.refs_4_.refs_12_), channel_id=1, source_target_pairs={{0,1},{1,0},{2,3},{3,2},{4,5},{5,4},{6,7},{7,6},{8,9},{9,8},{10,11... | collective-permute-start | bytes 2261000 | tf_op jit(solution)/shard_map/ppermute | solution.py:521
  44.4 2.7 %collective-permute-start.4 = (bf16[128,2944]{1,0:T(8,128)(2,1)}, bf16[128,2944]{1,0:T(8,128)(2,1)}, u32[]{:S(2)}, u32[]{:S(2)}) collective-permute-start(bf16[128,2944]{1,0:T(8,128)(2,1)} %hold.3.refs_2_.refs_10_), channel_id=1, source_target_pairs={{0,1},{1,0},{2,3},{3,2},{4,5},{5,4},{6,7},{7,6},{8,9},{9,8},{10,11... | collective-permute-start | bytes 2261000 | tf_op jit(solution)/shard_map/ppermute | solution.py:521
  46.3 2.4 %collective-permute-start.10 = (bf16[128,2944]{1,0:T(8,128)(2,1)}, bf16[128,2944]{1,0:T(8,128)(2,1)S(1)}, u32[]{:S(2)}, u32[]{:S(2)}) collective-permute-start(bf16[128,2944]{1,0:T(8,128)(2,1)} %hold.5.refs_6_.refs_14_), channel_id=1, source_target_pairs={{0,1},{1,0},{2,3},{3,2},{4,5},{5,4},{6,7},{7,6},{8,9},{9,8},{10,11... | collective-permute-start | bytes 2261000 | tf_op jit(solution)/shard_map/ppermute | solution.py:521
  46.3 36.3 %collective-permute-start.11 = (bf16[192,2880]{1,0:T(8,128)(2,1)}, bf16[192,2880]{1,0:T(8,128)(2,1)S(1)}, u32[]{:S(2)}, u32[]{:S(2)}) collective-permute-start(bf16[192,2880]{1,0:T(8,128)(2,1)} %collective-permute-done.2.refs_1_.refs_12_), channel_id=1, source_target_pairs={{8,16},{16,8},{12,20},{20,12},{9,17},{17,9},{13,21},{21,13},{10,18... | collective-permute-start | bytes 3317768 | tf_op jit(solution)/shard_map/ppermute | solution.py:529
  59.8 12.9 %copy-start.11 = (bf16[4,192,512]{2,1,0:T(8,128)(2,1)S(1)}, bf16[4,192,512]{2,1,0:T(8,128)(2,1)}, u32[]{:S(2)}) copy-start(bf16[4,192,512]{2,1,0:T(8,128)(2,1)} %copy-done.9) | copy-start | bytes 2359300
  59.8 12.9 %copy-start.14 = (bf16[1,192,512]{2,1,0:T(8,128)(2,1)S(1)}, bf16[1,192,512]{2,1,0:T(8,128)(2,1)}, u32[]{:S(2)}) copy-start(bf16[1,192,512]{2,1,0:T(8,128)(2,1)} %copy-done.12) | copy-start | bytes 589828
  59.8 27.6 %collective-permute-start.13 = (bf16[192,2880]{1,0:T(8,128)(2,1)S(1)}, bf16[192,2880]{1,0:T(8,128)(2,1)S(1)}, u32[]{:S(2)}, u32[]{:S(2)}) collective-permute-start(bf16[192,2880]{1,0:T(8,128)(2,1)S(1)} %get-tuple-element.30.refs_18_), channel_id=1, source_target_pairs={{0,8},{8,0},{4,12},{12,4},{16,24},{24,16},{20,28},{28,20},{1,9},{9... | collective-permute-start | bytes 3317768 | tf_op jit(solution)/shard_map/ppermute | solution.py:529
  72.7 47.4 %copy-start = (f32[3,192,2880]{2,1,0:T(8,128)}, f32[3,192,2880]{2,1,0:T(8,128)S(1)}, u32[]{:S(2)}) copy-start(f32[3,192,2880]{2,1,0:T(8,128)S(1)} %other_products.1.refs_14_.refs_0_.kept_ref) | copy-start | bytes 19906564
  88.8 8.9 %collective-permute-start.14 = (bf16[192,2880]{1,0:T(8,128)(2,1)S(1)}, bf16[192,2880]{1,0:T(8,128)(2,1)S(1)}, u32[]{:S(2)}, u32[]{:S(2)}) collective-permute-start(bf16[192,2880]{1,0:T(8,128)(2,1)S(1)} %combine.5.refs_14_), channel_id=1, source_target_pairs={{8,16},{16,8},{12,20},{20,12},{9,17},{17,9},{13,21},{21,13},{10,18... | collective-permute-start | bytes 3317768 | tf_op jit(solution)/shard_map/ppermute | solution.py:529
  89.6 30.6 %collective-permute-start.12 = (bf16[192,2880]{1,0:T(8,128)(2,1)S(1)}, bf16[192,2880]{1,0:T(8,128)(2,1)S(1)}, u32[]{:S(2)}, u32[]{:S(2)}) collective-permute-start(bf16[192,2880]{1,0:T(8,128)(2,1)S(1)} %combine.4.refs_1_), channel_id=1, source_target_pairs={{0,8},{8,0},{4,12},{12,4},{16,24},{24,16},{20,28},{28,20},{1,9},{9... | collective-permute-start | bytes 3317768 | tf_op jit(solution)/shard_map/ppermute | solution.py:529
  99.1 57.1 %collective-permute-start.19 = (bf16[192,2880]{1,0:T(8,128)(2,1)S(1)}, bf16[192,2880]{1,0:T(8,128)(2,1)}, u32[]{:S(2)}, u32[]{:S(2)}) collective-permute-start(bf16[192,2880]{1,0:T(8,128)(2,1)S(1)} %combine.6.refs_1_), channel_id=1, source_target_pairs={{0,8},{8,0},{4,12},{12,4},{16,24},{24,16},{20,28},{28,20},{1,9},{9... | collective-permute-start | bytes 3317768 | tf_op jit(solution)/shard_map/ppermute | solution.py:529
  122.2 34.0 %collective-permute-start.20 = (bf16[192,2880]{1,0:T(8,128)(2,1)}, bf16[192,2880]{1,0:T(8,128)(2,1)}, u32[]{:S(2)}, u32[]{:S(2)}) collective-permute-start(bf16[192,2880]{1,0:T(8,128)(2,1)} %combine.7.refs_14_), channel_id=1, source_target_pairs={{8,16},{16,8},{12,20},{20,12},{9,17},{17,9},{13,21},{21,13},{10,18... | collective-permute-start | bytes 3317768 | tf_op jit(solution)/shard_map/ppermute | solution.py:529
  123.9 25.9 %collective-permute-start.16 = (bf16[3,192,512]{2,1,0:T(8,128)(2,1)}, bf16[3,192,512]{2,1,0:T(8,128)(2,1)}, u32[]{:S(2)}, u32[]{:S(2)}) collective-permute-start(bf16[3,192,512]{2,1,0:T(8,128)(2,1)} %get-tuple-element.36), channel_id=1, source_target_pairs={{0,4},{4,0},{8,12},{12,8},{16,20},{20,16},{24,28},{28,24},{1,5},{5... | collective-permute-start | bytes 1769480 | tf_op jit(solution)/shard_map/ppermute | solution.py:518
  130.7 9.9 %collective-permute-start.15 = (f32[1,512]{1,0:T(1,128)S(1)}, f32[1,512]{1,0:T(1,128)S(1)}, u32[]{:S(2)}, u32[]{:S(2)}) collective-permute-start(f32[1,512]{1,0:T(1,128)S(1)} %slice.7), channel_id=1, source_target_pairs={{0,4},{4,0},{8,12},{12,8},{16,20},{20,16},{24,28},{28,24},{1,5},{5... | collective-permute-start | bytes 6152 | tf_op jit(solution)/shard_map/ppermute | solution.py:518
  131.2 18.7 %collective-permute-start.17 = (bf16[1,192,512]{2,1,0:T(8,128)(2,1)}, bf16[1,192,512]{2,1,0:T(8,128)(2,1)S(1)}, u32[]{:S(2)}, u32[]{:S(2)}) collective-permute-start(bf16[1,192,512]{2,1,0:T(8,128)(2,1)} %get-tuple-element.38), channel_id=1, source_target_pairs={{0,4},{4,0},{8,12},{12,8},{16,20},{20,16},{24,28},{28,24},{1,5},{5... | collective-permute-start | bytes 589832 | tf_op jit(solution)/shard_map/ppermute | solution.py:518
  140.5 9.4 %collective-permute-start.18 = (bf16[1,192,512]{2,1,0:T(8,128)(2,1)}, bf16[1,192,512]{2,1,0:T(8,128)(2,1)S(1)}, u32[]{:S(2)}, u32[]{:S(2)}) collective-permute-start(bf16[1,192,512]{2,1,0:T(8,128)(2,1)} %get-tuple-element.40), channel_id=1, source_target_pairs={{0,4},{4,0},{8,12},{12,8},{16,20},{20,16},{24,28},{28,24},{1,5},{5... | collective-permute-start | bytes 589832 | tf_op jit(solution)/shard_map/ppermute | solution.py:518
  (26 other events, 79.5 us)

commit v3 on v0

--- a/solution.py
+++ b/solution.py
@@ -1,7 +1,760 @@
+import functools
+
 import jax
 import jax.numpy as jnp
+import numpy as np
 from jax import lax
+from jax.experimental import pallas as pl
+from jax.experimental.pallas import tpu as pltpu
 from jax.sharding import PartitionSpec as P
+
+LANES = 128
+SCALE = 3_000_000
+NT = (((1,), (1,)), ((), ()))
+NN = (((1,), (0,)), ((), ()))
+f32 = jnp.float32
+bf16 = jnp.bfloat16
+
+
+def dot(a, b, dims):
+    return lax.dot_general(a, b, dims, preferred_element_type=f32)
+
+
+def anywhere():
+    return pl.BlockSpec(memory_space=pl.ANY)
+
+
+def whole():
+    return pl.BlockSpec(memory_space=pltpu.VMEM)
+
+
+def scalars():
+    return pl.BlockSpec(memory_space=pltpu.SMEM)
+
+
+def params():
+    return pltpu.CompilerParams(vmem_limit_bytes=24 * 1024 * 1024)
+
+
+def taking(microseconds):
+    return pl.CostEstimate(flops=0, bytes_accessed=int(microseconds * SCALE), transcendentals=0)
+
+
+def chain_plan(depth):
+    products, weights = [], []
+    for z in range(depth):
+        uses = []
+        for turn in range(2, depth + 1):
+            if z < depth - 1 and turn >= z + 2:
+                uses.append((turn, "AB"[z % 2], depth + 1 + z - turn))
+            if z > 0 and turn >= depth - z + 1:
+                uses.append((turn, "BA"[z % 2], z + turn - depth - 1))
+        products.append(sorted(uses) + [(depth + 1, "own", z)])
+        brought = {}
+        for turn in range(1, depth):
+            for name in "AB":
+                index = z + turn if (name == "A") == (z % 2 == 0) else z - turn
+                brought[turn, name] = index if 0 <= index < depth else -1
+        weights.append(brought)
+    return products, weights
+
+
+class Scalars:
+    def __init__(self):
+        self.columns = []
+        self.names = {}
+
+    def add(self, name, values):
+        self.names[name] = len(self.columns)
+        self.columns.append(values)
+
+    def __getitem__(self, name):
+        return self.names[name]
+
+    def row(self, place, me):
+        return jnp.asarray(np.stack(self.columns, axis=-1).astype(np.int32))[place, me]
+
+
+def device_scalars(depth, experts):
+    products, weights = chain_plan(depth)
+    table = Scalars()
+    along = np.arange(2 * depth)[:, None] + np.zeros((1, experts), np.int32)
+
+    def by_z(values):
+        return np.asarray(values)[along // 2]
+
+    table.add("x", along % 2)
+    table.add("me", np.zeros_like(along) + np.arange(experts)[None, :])
+    table.add(("shard", 0, "own"), along // 2)
+    slot_of = [{use[2]: slot for slot, use in enumerate(products[z])} for z in range(depth)]
+    for part in range(depth):
+        table.add(("slot of", part), by_z([slot_of[z][part] for z in range(depth)]))
+    table.add(("slot", 0, "own"), by_z([slot_of[z][z] for z in range(depth)]))
+    for turn in range(1, depth):
+        for name in "AB":
+            shard = [weights[z][turn, name] for z in range(depth)]
+            table.add(("shard", turn, name), by_z(shard))
+            table.add(("slot", turn, name), by_z([slot_of[z].get(k, 0) for z, k in enumerate(shard)]))
+    uses = {}
+    for turn in range(2, depth + 1):
+        for name in "AB":
+            slots = [-1] * depth
+            for z in range(depth):
+                for slot, use in enumerate(products[z]):
+                    if use[:2] == (turn, name):
+                        slots[z] = slot
+            uses[turn, name] = slots
+            table.add(("use", turn, name), by_z(slots))
+            limit = max(depth - 3, 0)
+            table.add(("block", turn, name), by_z([min(max(slot - 1, 0), limit) for slot in slots]))
+    return table, weights, uses
+
+
+def rows_kernel(cut, grad_ref, logits_ref, ids_ref, late_ref, early_ref, gates_ref):
+    model, tokens = grad_ref.shape
+    count = logits_ref.shape[0]
+    width = cut + late_ref.shape[1]
+    logits = logits_ref[...]
+    powers = jnp.exp(logits - jnp.max(logits, axis=0, keepdims=True))
+    gates = powers / jnp.sum(powers, axis=0, keepdims=True)
+    gates_ref[...] = gates
+    sent = gates.astype(bf16).astype(f32)
+    ids = ids_ref[...]
+    row = lax.broadcasted_iota(jnp.int32, (width - model, tokens), 0)
+    extra = jnp.zeros((width - model, tokens), f32)
+    for expert in range(count):
+        chosen = jnp.sum(jnp.where(ids == expert, sent, 0.0), axis=0, keepdims=True)
+        extra = extra + jnp.where(row == expert, chosen, 0.0)
+    for start in range(0, width, LANES):
+        stop = start + LANES
+        if stop <= model:
+            block = grad_ref[start:stop, :].astype(f32)
+        elif start >= model:
+            block = extra[start - model : stop - model, :]
+        else:
+            block = jnp.concatenate(
+                [grad_ref[start:model, :].astype(f32), extra[: stop - model, :]], axis=0
+            )
+        turned = block.T.astype(bf16)
+        if start < cut:
+            early_ref[:, start:stop] = turned
+        else:
+            late_ref[:, start - cut : stop - cut] = turned
+
+
+def make_rows(grad_out, top_logits, expert_ids, width, cut):
+    tokens, model = grad_out.shape
+    count = top_logits.shape[1]
+    return pl.pallas_call(
+        functools.partial(rows_kernel, cut),
+        out_shape=(
+            jax.ShapeDtypeStruct((tokens, width - cut), bf16),
+            jax.ShapeDtypeStruct((tokens, cut), bf16),
+            jax.ShapeDtypeStruct((count, tokens), f32),
+        ),
+        in_specs=[whole()] * 3,
+        out_specs=(whole(),) * 3,
+        compiler_params=params(),
+        cost_estimate=taking(2),
+        name="make_rows",
+    )(grad_out.T, top_logits.T, expert_ids.T)
+
+
+def pack_kernel(*refs):
+    out_ref, sems = refs[-2:]
+    copies = []
+    for place in range(out_ref.shape[0]):
+        copies.append(pltpu.make_async_copy(refs[place], out_ref.at[place], sems.at[place]))
+        copies[-1].start()
+    for copy in copies:
+        copy.wait()
+
+
+def pack(values, after):
+    number = len(values)
+    return pl.pallas_call(
+        pack_kernel,
+        out_shape=jax.ShapeDtypeStruct((number, *values[0].shape), values[0].dtype),
+        in_specs=[anywhere()] * (number + len(after)),
+        out_specs=anywhere(),
+        scratch_shapes=[pltpu.SemaphoreType.DMA((number,))],
+        compiler_params=params(),
+        cost_estimate=taking(1),
+        name="pack_rows",
+    )(*values, *after)
+
+
+def hold_kernel(*refs):
+    del refs
+
+
+def hold(values, after):
+    return pl.pallas_call(
+        hold_kernel,
+        out_shape=tuple(jax.ShapeDtypeStruct(value.shape, value.dtype) for value in values),
+        in_specs=[anywhere()] * (len(values) + len(after)),
+        out_specs=(anywhere(),) * len(values),
+        input_output_aliases={place: place for place in range(len(values))},
+        compiler_params=params(),
+        cost_estimate=taking(0),
+        name="hold",
+    )(*values, *after)
+
+
+def split_kernel(table, where_ref, hidden_ref, *refs):
+    own_ref, first_ref, rest_ref = refs[-3:]
+    parts, units, _ = own_ref.shape
+    row = lax.broadcasted_iota(jnp.int32, (2 * units, 2 * units), 0)
+    column = lax.broadcasted_iota(jnp.int32, (2 * units, 2 * units), 1)
+    unit = jnp.where(row == column, 1.0, 0.0).astype(bf16)
+    low = where_ref[table["x"]] == 0
+    for part in range(parts):
+        block = hidden_ref[:, part * 2 * units : (part + 1) * 2 * units]
+        turned = dot(unit, block, NT).astype(bf16)
+        slot = where_ref[table["slot of", part]]
+        other = jnp.where(low, turned[units:], turned[:units])
+        own_ref[slot] = jnp.where(low, turned[:units], turned[units:])
+
+        @pl.when(slot == 0)
+        def _():
+            first_ref[0] = other
+
+        @pl.when(slot != 0)
+        def _():
+            rest_ref[slot - 1] = other
+
+
+def split_hidden(table, where, hidden, parts, units, after):
+    slots = hidden.shape[0]
+    return pl.pallas_call(
+        functools.partial(split_kernel, table),
+        out_shape=tuple(
+            jax.ShapeDtypeStruct((count, units, slots), bf16) for count in (parts, 1, parts - 1)
+        ),
+        in_specs=[scalars(), whole()] + [anywhere()] * len(after),
+        out_specs=(whole(),) * 3,
+        compiler_params=params(),
+        cost_estimate=taking(2),
+        name="split_hidden",
+    )(where, hidden, *after)
+
+
+def pair_lanes(step, steps, me, tokens):
+    high = 2 * lax.rem(step, steps // 2)
+    return pl.multiple_of(lax.div(me ^ high, 2) * 2 * tokens, 2 * tokens)
+
+
+def half_of(me, tokens, other):
+    return pl.multiple_of((lax.rem(me, 2) ^ other) * tokens, tokens)
+
+
+def products_kernel(table, gate_lane, shards, cut, where_ref, *refs):
+    first = len(refs) == 10
+    rows = refs[:2]
+    gate_tiles = refs[2:4]
+    own_ref, other_ref = refs[4:6]
+    scaled = refs[-1]
+    kept_ref = refs[-2]
+    tokens = rows[0].shape[1]
+    slots = own_ref.shape[2]
+    me = where_ref[table["me"]]
+    step, steps = pl.program_id(0), pl.num_programs(0)
+    lane = lax.broadcasted_iota(jnp.int32, (tokens, LANES), 1)
+    for other in range(2):
+        here = pl.ds(half_of(me, tokens, other), tokens)
+        picked = jnp.where(lane == gate_lane + me, gate_tiles[other][0].astype(f32), 0.0)
+        gate = jnp.sum(picked, axis=1, keepdims=True)
+        scaled[here, :] = (rows[other][0].astype(f32) * gate).astype(bf16)
+    lanes = pl.ds(pair_lanes(step, steps, me, tokens), 2 * tokens)
+    skip = own_ref.shape[0] - len(shards)
+    width = kept_ref.shape[2]
+
+    def add(hidden):
+        total = dot(hidden, scaled[...], NN)[:, :width]
+        units = total.shape[0] // len(shards)
+
+        @pl.when(step == 0)
+        def _():
+            for place in range(len(shards)):
+                kept_ref[place] = total[place * units : (place + 1) * units]
+
+        @pl.when(step != 0)
+        def _():
+            for place in range(len(shards)):
+                kept_ref[place] += total[place * units : (place + 1) * units]
+
+    def stacked(ref, offset):
+        parts = [ref[offset + shard, :, lanes] for shard in range(len(shards))]
+        return jnp.concatenate(parts, axis=0) if len(parts) > 1 else parts[0]
+
+    @pl.when(step < steps // 2)
+    def _():
+        add(stacked(own_ref, skip))
+
+    @pl.when(step >= steps // 2)
+    def _():
+        add(stacked(other_ref, 0))
+
+
+def products(table, where, rows, gated, own, other, skip, model, cut, name, after):
+    number, tokens, width = rows[0].shape
+    shards, units, slots = other.shape
+    late = cut > 0
+    columns = model - cut if late else width
+    gate_tile = (gated[0].shape[2] - LANES) // LANES
+    row_spec = pl.BlockSpec((1, tokens, width), lambda j, s: (j, 0, 0))
+    tile_spec = pl.BlockSpec((1, tokens, LANES), lambda j, s: (j, 0, gate_tile))
+    own_shards = shards if skip == 0 else own.shape[0]
+    own_spec = pl.BlockSpec((own_shards, units, slots), lambda j, s: (0, 0, 0))
+    other_spec = pl.BlockSpec((shards, units, slots), lambda j, s: (0, 0, 0))
+    return pl.pallas_call(
+        functools.partial(products_kernel, table, model % LANES, list(range(shards)), cut),
+        out_shape=jax.ShapeDtypeStruct((shards, units, columns), f32),
+        grid_spec=pltpu.PrefetchScalarGridSpec(
+            num_scalar_prefetch=1,
+            grid=(number,),
+            in_specs=[row_spec] * 2
+            + [tile_spec] * 2
+            + [own_spec, other_spec]
+            + [anywhere()] * len(after),
+            out_specs=pl.BlockSpec((shards, units, columns), lambda j, s: (0, 0, 0)),
+            scratch_shapes=[pltpu.VMEM((2 * tokens, width), bf16)],
+        ),
+        compiler_params=params(),
+        cost_estimate=taking(4),
+        name=name,
+    )(where, *rows, *gated, own, other, *after)
+
+
+def rows_of(units):
+    return units // 4 if units % 64 == 0 else units
+
+
+def column_parts(arrays, cut):
+    return [(0, arrays[0])] if len(arrays) == 1 else [(cut, arrays[0]), (0, arrays[1])]
+
+
+def combine_kernel(table, key, cut, counts, sides, where_ref, *refs):
+    slot = where_ref[table[key]]
+    coming = refs[: counts[0]]
+    outs = refs[len(refs) - counts[2] :]
+    model = sum(ref.shape[1] for ref in coming)
+    spans = [(cut, model), (0, cut)] if cut else [(0, model)]
+    for chunk, (start, stop) in enumerate(spans):
+        if counts[0] == 1:
+            total = coming[0][:, start:stop]
+        else:
+            total = coming[chunk][...]
+        total = total.astype(f32)
+        for number, side in enumerate(sides):
+            flag = slot == 0 if side == "first" else slot > 0
+            total = total + jnp.where(flag, refs[counts[0] + len(spans) * number + chunk][0], 0.0)
+        total = total.astype(bf16)
+        if counts[2] == 1:
+            outs[0][:, start:stop] = total
+        else:
+            outs[chunk][...] = total
+
+
+def combine(table, where, coming, first, rest, turn, name, used, cut, after):
+    units = coming[0].shape[0]
+    model = sum(part.shape[1] for part in coming)
+    block = rows_of(units)
+    column = table["block", turn, name]
+    sides, operands, specs = [], [], []
+    if any(slot == 0 for slot in used):
+        sides.append("first")
+        operands += first
+        specs += [pl.BlockSpec((1, block, part.shape[2]), lambda j, s: (0, j, 0)) for part in first]
+    if any(slot > 0 for slot in used):
+        sides.append("rest")
+        operands += rest
+        specs += [pl.BlockSpec((1, block, part.shape[2]), lambda j, s: (s[column], j, 0)) for part in rest]
+    flat = pl.BlockSpec((block, model), lambda j, s: (j, 0))
+    return pl.pallas_call(
+        functools.partial(
+            combine_kernel, table, ("use", turn, name), cut, (len(coming), len(operands), 1), sides
+        ),
+        out_shape=jax.ShapeDtypeStruct((units, model), bf16),
+        grid_spec=pltpu.PrefetchScalarGridSpec(
+            num_scalar_prefetch=1,
+            grid=(units // block,),
+            in_specs=[pl.BlockSpec((block, part.shape[1]), lambda j, s: (j, 0)) for part in coming]
+            + specs
+            + [anywhere()] * len(after),
+            out_specs=flat,
+        ),
+        compiler_params=params(),
+        cost_estimate=taking(1.5),
+        name="combine",
+    )(where, *coming, *operands, *after)
+
+
+def begin_kernel(table, start, stop, where_ref, coming_ref, kept_ref, *refs):
+    out_ref = refs[-1]
+    flag = where_ref[table["use", 2, "A"]] == 0
+    total = coming_ref[:, start:stop].astype(f32) + jnp.where(flag, kept_ref[0], 0.0)
+    out_ref[...] = total.astype(bf16)
+
+
+def begin(table, where, coming, kept, start, after):
+    units, model = coming.shape
+    width = kept.shape[2]
+    block = rows_of(units)
+    return pl.pallas_call(
+        functools.partial(begin_kernel, table, start, start + width),
+        out_shape=jax.ShapeDtypeStruct((units, width), bf16),
+        grid_spec=pltpu.PrefetchScalarGridSpec(
+            num_scalar_prefetch=1,
+            grid=(units // block,),
+            in_specs=[
+                pl.BlockSpec((block, model), lambda j, s: (j, 0)),
+                pl.BlockSpec((1, block, width), lambda j, s: (0, j, 0)),
+            ]
+            + [anywhere()] * len(after),
+            out_specs=pl.BlockSpec((block, width), lambda j, s: (j, 0)),
+        ),
+        compiler_params=params(),
+        cost_estimate=taking(1),
+        name="begin",
+    )(where, coming, kept, *after)
+
+
+def total_kernel(cut, a_ref, b_ref, late_ref, early_ref, out_ref):
+    for start, kept_ref in ((cut, late_ref), (0, early_ref)):
+        here = slice(start, start + kept_ref.shape[2])
+        out_ref[0, :, here] = kept_ref[0] + a_ref[:, here].astype(f32) + b_ref[:, here].astype(f32)
+
+
+def total_grad(a, b, kept, cut):
+    units, model = a.shape
+    block = rows_of(units)
+    flat = pl.BlockSpec((block, model), lambda j: (j, 0))
+    return pl.pallas_call(
+        functools.partial(total_kernel, cut),
+        out_shape=jax.ShapeDtypeStruct((1, units, model), f32),
+        grid=(units // block,),
+        in_specs=[flat, flat]
+        + [
+            pl.BlockSpec((1, block, part.shape[2]), functools.partial(lambda last, j: (last, j, 0), part.shape[0] - 1))
+            for part in kept
+        ],
+        out_specs=pl.BlockSpec((1, block, model), lambda j: (0, j, 0)),
+        compiler_params=params(),
+        cost_estimate=taking(2),
+        name="total_grad",
+    )(a, b, *kept)
+
+
+def back_kernel(table, model, cut, choices, parts, guard, summed, where_ref, *refs):
+    keys = [key for choice in choices for key in choice]
+    late, early = refs[:2], refs[2:4]
+    own_ref, first_ref, rest_ref = refs[4:7]
+    weight_refs, used = {}, 7
+    for key, count in zip(keys, parts):
+        weight_refs[key] = refs[used : used + count]
+        used += count
+    before_ref = refs[used] if summed else None
+    mine_ref, theirs_ref, sums_ref = refs[-3:]
+    tokens = late[0].shape[1]
+    units = own_ref.shape[1]
+    slots_all = own_ref.shape[2]
+    me = where_ref[table["me"]]
+    step, steps = pl.program_id(0), pl.num_programs(0)
+    start = late[0].shape[2] - LANES
+    eight = lax.broadcasted_iota(jnp.int32, (8, LANES), 1)
+    onehot = jnp.where(eight == model % LANES + me, 1.0, 0.0).astype(bf16)
+    shards = {key: where_ref[table[("shard",) + key]] for key in keys}
+    slots = {key: where_ref[table[("slot",) + key]] for key in keys}
+
+    @pl.when(step == 0)
+    def _():
+        sums_ref[...] = before_ref[...] if summed else jnp.zeros(sums_ref.shape, f32)
+
+    def whole_weight(key):
+        got = weight_refs[key]
+        return got[0][...] if len(got) == 1 else jnp.concatenate([got[1][...], got[0][...]], axis=1)
+
+    def work(near):
+        stack, here_valid, here_slot = [], [], []
+        for choice in choices:
+            weight, valid, slot = whole_weight(choice[0]), shards[choice[0]] >= 0, slots[choice[0]]
+            for key in choice[1:]:
+                weight = jnp.where(valid, weight, whole_weight(key))
+                slot = jnp.where(valid, slot, slots[key])
+                valid = jnp.logical_or(valid, shards[key] >= 0)
+            stack.append(weight)
+            here_valid.append(valid)
+            here_slot.append(slot)
+        weight = jnp.concatenate(stack, axis=0) if len(stack) > 1 else stack[0]
+        both = jnp.concatenate(
+            [jnp.concatenate([early[k][0], late[k][0][:, : model - cut]], axis=1) for k in range(2)],
+            axis=0,
+        )
+        product = dot(weight, both, NT)
+        lanes = pair_lanes(step, steps, me, tokens)
+        out_ref = mine_ref if near else theirs_ref
+        for half in range(2):
+            block = product[:, half * tokens : (half + 1) * tokens]
+            gate = dot(onehot, late[half][0][:, start:], NT)[0:1]
+            here = pl.ds(pl.multiple_of(lanes + half_of(me, tokens, half), tokens), tokens)
+            offset = 0 if near else slots_all
+            wide = pl.ds(pl.multiple_of(offset + lanes + half_of(me, tokens, half), tokens), tokens)
+            gated = (block * gate).astype(bf16)
+            total = jnp.zeros((1, tokens), f32)
+            for index, (valid, slot) in enumerate(zip(here_valid, here_slot)):
+                some = slice(index * units, (index + 1) * units)
+                out_ref[index, :, here] = gated[some]
+                if near:
+                    hidden = own_ref[slot, :, here].astype(f32)
+                else:
+                    hidden = jnp.where(
+                        slot == 0,
+                        first_ref[0, :, here].astype(f32),
+                        rest_ref[jnp.maximum(slot - 1, 0), :, here].astype(f32),
+                    )
+                part = jnp.sum(hidden * block[some], axis=0, keepdims=True)
+                total = total + jnp.where(valid, part, 0.0)
+            sums_ref[0:1, wide] += total
+
+    some = functools.reduce(jnp.logical_or, [shards[key] >= 0 for key in keys]) if guard else True
+    pl.when(jnp.logical_and(some, step < steps // 2))(functools.partial(work, True))
+    pl.when(jnp.logical_and(some, step >= steps // 2))(functools.partial(work, False))
+
+
+def back_part(table, where, late, early, own, first, rest, choices, got, before, guard, after, model):
+    units, slots = own.shape[1:]
+    number, tokens, width = late[0].shape
+    cut = early[0].shape[2]
+    keys = [key for choice in choices for key in choice]
+    weights = [got[key] for key in keys]
+    flat = [part for weight in weights for part in weight]
+    half = jax.ShapeDtypeStruct((len(choices), units, slots), bf16)
+    summed = before is not None
+    fixed = [own, first, rest, *flat] + ([before] if summed else [])
+    sums = jax.ShapeDtypeStruct((8, 2 * slots), f32)
+
+    def still(shape):
+        zeros = (0,) * len(shape)
+        return pl.BlockSpec(shape, lambda j, s: zeros)
+
+    return pl.pallas_call(
+        functools.partial(
+            back_kernel, table, model, cut, choices, [len(weight) for weight in weights], guard, summed
+        ),
+        out_shape=(half, half, sums),
+        grid_spec=pltpu.PrefetchScalarGridSpec(
+            num_scalar_prefetch=1,
+            grid=(number,),
+            in_specs=[pl.BlockSpec((1, tokens, width), lambda j, s: (j, 0, 0))] * 2
+            + [pl.BlockSpec((1, tokens, cut), lambda j, s: (j, 0, 0))] * 2
+            + [still(value.shape) for value in fixed]
+            + [anywhere()] * len(after),
+            out_specs=(still(half.shape), still(half.shape), still(sums.shape)),
+        ),
+        compiler_params=params(),
+        cost_estimate=taking(6),
+        name="back_part",
+    )(where, *late, *early, *fixed, *after)
+
+
+def join_kernel(table, groups, where_ref, *refs):
+    out_ref, turned, sem = refs[-3:]
+    slots, width = turned.shape[1:]
+    row = lax.broadcasted_iota(jnp.int32, (slots, slots), 0)
+    column = lax.broadcasted_iota(jnp.int32, (slots, slots), 1)
+    unit = jnp.where(row == column, 1.0, 0.0).astype(bf16)
+    low = where_ref[table["x"]] == 0
+    copies = []
+    total = 0
+    for number, choices in enumerate(groups):
+        mine_ref, theirs_ref = refs[2 * number], refs[2 * number + 1]
+        for place, choice in enumerate(choices):
+            index = where_ref[table[("shard",) + choice[0]]]
+            for key in choice[1:]:
+                index = jnp.where(index >= 0, index, where_ref[table[("shard",) + key]])
+            mine, theirs = mine_ref[place], theirs_ref[place]
+            both = jnp.concatenate(
+                [jnp.where(low, mine, theirs), jnp.where(low, theirs, mine)], axis=0
+            )
+            turned[total] = dot(unit, both, NT).astype(bf16)
+            here = pl.ds(pl.multiple_of(jnp.maximum(index, 0) * width, LANES), width)
+            copy = pltpu.make_async_copy(turned.at[total], out_ref.at[:, here], sem.at[total])
+            copies.append((index, copy))
+            pl.when(index >= 0)(copy.start)
+            total += 1
+    for index, copy in copies:
+        pl.when(index >= 0)(copy.wait)
+
+
+def join_hidden(table, where, groups, pairs, slots, hidden, before, after):
+    flat = [array for pair in pairs for array in pair]
+    units = flat[0].shape[1]
+    total = sum(len(choices) for choices in groups)
+    extends = before is not None
+    return pl.pallas_call(
+        functools.partial(join_kernel, table, groups),
+        out_shape=jax.ShapeDtypeStruct((slots, hidden), bf16),
+        in_specs=[scalars()] + [whole()] * len(flat) + [anywhere()] * (extends + len(after)),
+        out_specs=anywhere(),
+        scratch_shapes=[
+            pltpu.VMEM((total, slots, 2 * units), bf16),
+            pltpu.SemaphoreType.DMA((total,)),
+        ],
+        input_output_aliases={1 + len(flat): 0} if extends else {},
+        compiler_params=params(),
+        cost_estimate=taking(2),
+        name="join_hidden",
+    )(where, *flat, *([before] if extends else []), *after)
+
+
+def logits_kernel(gates_ref, ids_ref, grads_ref, out_ref):
+    gates, ids, grads = gates_ref[...], ids_ref[...], grads_ref[...]
+    picked = jnp.zeros_like(gates)
+    for expert in range(grads.shape[0]):
+        picked = picked + jnp.where(ids == expert, grads[expert : expert + 1, :], 0.0)
+    out_ref[...] = gates * (picked - jnp.sum(gates * picked, axis=0, keepdims=True))
+
+
+def logits_grad(gates, ids, grads):
+    return pl.pallas_call(
+        logits_kernel,
+        out_shape=jax.ShapeDtypeStruct(gates.shape, f32),
+        in_specs=[whole()] * 3,
+        out_specs=whole(),
+        compiler_params=params(),
+        cost_estimate=taking(1),
+        name="logits_grad",
+    )(gates, ids, grads)
+
+
+def per_device_full(grad_out, top_logits, expert_ids, saved_hidden, w_down):
+    experts = lax.axis_size("exp")
+    groups = lax.axis_size("ctx")
+    depth = groups // 2
+    tokens, model = grad_out.shape
+    slots, hidden = saved_hidden.shape[2:]
+    width = pl.cdiv(model + experts, LANES) * LANES
+    cut = width // LANES // 2 * LANES
+
+    table, brought, uses = device_scalars(depth, experts)
+    where = table.row(lax.axis_index("ctx"), lax.axis_index("exp"))
+
+    def swap(value, x, exp):
+        if not exp:
+            return lax.ppermute(value, "ctx", [(i, i ^ x) for i in range(groups)])
+        if not x:
+            return lax.ppermute(value, "exp", [(i, i ^ exp) for i in range(experts)])
+        pairs = [(c * experts + e, (c ^ x) * experts + (e ^ exp)) for c in range(groups) for e in range(experts)]
+        return lax.ppermute(value, ("ctx", "exp"), pairs)
+
+    def swap_z(value, name):
+        first = "AB".index(name)
+        pairs = []
+        for z in range(first, depth - 1, 2):
+            for x in range(2):
+                pairs += [(2 * z + x, 2 * z + 2 + x), (2 * z + 2 + x, 2 * z + x)]
+        return lax.ppermute(value, "ctx", pairs)
+
+    got = {(0, "own"): [w_down[0]]}
+    for name in "AB":
+        got[1, name] = [swap_z(w_down[0], name)]
+
+    late, early, gates = make_rows(grad_out, top_logits, expert_ids, width, cut)
+    highs = list(range(2, experts, 2))
+    late_near = [late] + [swap(late, 0, high) for high in highs]
+    late_x = swap(late, 1, 0)
+    late_far = [late_x] + [swap(late_x, 0, high) for high in highs]
+    own, other_first, other_rest = split_hidden(
+        table, where, saved_hidden[0, 0], depth, w_down.shape[1], [late]
+    )
+    other_first = swap(other_first, 1, 0)
+    late_rows = pack(late_near + late_far, [other_first, got[1, "A"][0], got[1, "B"][0]])
+    late_rows = (late_rows, swap(late_rows, 0, 1))
+
+    (early,) = hold((early,), [late_rows[0]])
+    early_x = swap(early, 1, 0)
+    early_near = [early] + [swap(early, 0, high) for high in highs]
+    early_x, other_rest = hold((early_x, other_rest), [])
+    early_far = [early_x] + [swap(early_x, 0, high) for high in highs]
+    other_rest = swap(other_rest, 1, 0)
+    got[2, "B"] = [swap_z(got[1, "A"][0], "B")]
+
+    first = [
+        products(table, where, late_rows, late_rows, own, other_first, 0, model, cut, "first_late", [])
+    ]
+    sent = [begin(table, where, got[1, "B"][0], first[0], cut, [])]
+    got[2, "A"] = [swap_z(sent[0], "A")]
+    early_rows = pack(early_near + early_far, [sent[0]])
+    early_rows = (early_rows, swap(early_rows, 0, 1))
+    first.append(
+        products(table, where, early_rows, late_rows, own, other_first, 0, model, 0, "first_early", [other_rest])
+    )
+    sent.append(begin(table, where, got[1, "B"][0], first[1], 0, [got[2, "A"][0]]))
+    got[2, "A"].append(swap_z(sent[1], "A"))
+
+    rest = []
+    for rows, start, name in ((late_rows, cut, "rest_late"), (early_rows, 0, "rest_early")):
+        rest.append(
+            products(table, where, rows, late_rows, own, other_rest, 1, model, start, name, [sent[1]])
+        )
+
+    pairs, groups_of = [], []
+
+    def backprop(choices, before, guard, after):
+        mine, theirs, sums = back_part(
+            table, where, late_rows, early_rows, own, other_first, other_rest, choices, got, before, guard, after, model
+        )
+        pairs.append((mine, swap(theirs, 1, 0)))
+        groups_of.append(choices)
+        return sums
+
+    def pass_on(turn, name, after):
+        back = "B" if name == "A" else "A"
+        used = uses[turn, name]
+        coming = got[turn - 1, back]
+        if turn == 3 and name == "B":
+            values = []
+            for k in range(2):
+                value = combine(table, where, [coming[k]], [first[k]], [rest[k]], turn, name, used, 0, after)
+                values.append(value)
+                after = [value]
+        else:
+            values = [combine(table, where, coming, first, rest, turn, name, used, cut, after)]
+        got[turn, name] = [swap_z(value, name) for value in values]
+        return values[-1]
+
+    def choices_of(turn):
+        both = any(b[turn, "A"] >= 0 and b[turn, "B"] >= 0 for b in brought)
+        return [[(turn, "A")], [(turn, "B")]] if both else [[(turn, "A"), (turn, "B")]]
+
+    marker = pass_on(3, "A", [*rest, got[2, "A"][0]])
+    marker = pass_on(3, "B", [marker])
+    sums = backprop([[(0, "own")], [(1, "A")], [(1, "B")]], None, False, [marker])
+    marker = sums
+    hidden_grad = None
+    for turn in range(2, depth):
+        choices = choices_of(turn)
+        if turn > 2:
+            marker = pass_on(turn + 1, "A", [marker])
+            marker = pass_on(turn + 1, "B", [marker])
+        sums = backprop(choices, sums, len(choices) == 1, [marker])
+        marker = sums
+        if turn == 2:
+            hidden_grad = join_hidden(
+                table, where, groups_of[:1], pairs[:1], slots, hidden, None, [marker]
+            )
+            marker = hidden_grad
+    slot_grad = sums[0:1, :slots] + swap(sums[0:1, slots:], 1, 0)
+    grads = lax.all_to_all(
+        slot_grad.reshape(experts, tokens), "exp", split_axis=0, concat_axis=0, tiled=True
+    )
+    logit_grad = logits_grad(gates, expert_ids.T, grads).T
+    hidden_grad = join_hidden(
+        table, where, groups_of[1:], pairs[1:], slots, hidden, hidden_grad, [logit_grad]
+    )
+    weight_grad = total_grad(got[depth, "A"][0], got[depth, "B"][0], rest, cut)
+    return (logit_grad, hidden_grad[None, None], weight_grad)
 
 
 def routing_tables(expert_ids, count_experts, capacity):
@@ -14,7 +767,7 @@
     return (matches.astype(jnp.float32), select)
 
 
-def per_device(grad_out, top_logits, expert_ids, saved_hidden, w_down):
+def per_device_routed(grad_out, top_logits, expert_ids, saved_hidden, w_down):
     count_experts = lax.axis_size("exp")
     slot_count = saved_hidden.shape[2]
     capacity = slot_count // count_experts
@@ -57,6 +810,15 @@
     return (logit_grad, hidden_grad.reshape(1, 1, slot_count, -1), weight_grad[None])
 
 
+def per_device(grad_out, top_logits, expert_ids, saved_hidden, w_down):
+    experts = lax.axis_size("exp")
+    groups = lax.axis_size("ctx")
+    everywhere = top_logits.shape[1] == experts and saved_hidden.shape[2] == experts * grad_out.shape[0]
+    plain = experts & (experts - 1) == 0 and groups % 4 == 0 and groups >= 8
+    body = per_device_full if everywhere and plain else per_device_routed
+    return body(grad_out, top_logits, expert_ids, saved_hidden, w_down)
+
+
 def solution(mesh):
     return jax.shard_map(
         per_device,

time: 518 us -> 165 us (0.32)
  waiting for transfers between devices: 428 us -> 43 us
  Pallas kernels: 0 us -> 53 us
  starting transfers between devices: 7.67 us -> 48.1 us
  matrix products: 23.2 us -> 0 us
  local copies, waits for them, and re-layouts: 32.4 us -> 12.4 us
  between operations: 14.1 us -> 0.99 us
  other arithmetic: 5.37 us -> 0.01 us
    unnamed x3 -> x0, waiting for transfers between devices: 297 us -> none
    all_gather x1 -> x0, waiting for transfers between devices: 92.6 us -> none  [per_device(): lax.all_gather(w_down[0], 'ctx', axis=0, tiled=True)]
    pallas_call x0 -> x24, Pallas kernels: none -> 53 us  [the longest x4 17 us: products(): pl.pallas_call(functools.partial(products_kernel, table, model % LANES, l...]
    ppermute x0 -> x24, starting transfers between devices: none -> 48.1 us  [the longest x10 31.6 us: swap_z(): return lax.ppermute(value, 'ctx', pairs)]
    ppermute x0 -> x24, waiting for transfers between devices: none -> 43 us  [the longest x8 38.3 us: swap(): return lax.ppermute(value, 'ctx', [(i, i ^ x) for i in range(groups)])]
    all_to_all x2 -> x0, waiting for transfers between devices: 38.4 us -> none  [the longest x1 34.8 us: per_device(): lax.all_to_all(send_rows, 'exp', split_axis=0, concat_axis=0, tiled=True)]
    dot_general x3 -> x0, matrix products: 23.2 us -> none  [the longest x1 10.6 us: per_device(): lax.dot_general(flat_rows, lax.all_gather(w_down[0], 'ctx', axis=0, tiled...]
    unnamed x13 -> x33, local copies, waits for them, and re-layouts: 26.1 us -> 11 us
  transfers between devices with their start and end apart: 4 -> 24, of which waited for: 4 -> 8; matrix products, arithmetic and copies ran while one was open for 2% -> 2% of each run, Pallas kernels for 0% -> 29%
where the time goes in v3:
time: 165 us; the launch traced here: 164 us
  Pallas kernels  53 us (32%)
  starting transfers between devices  48.1 us (29%)
  waiting for transfers between devices  43 us (26%)
  local copies, waits for them, and re-layouts  12.4 us (8%)
  blocking collectives  6.34 us (4%)
    ppermute x8, waiting for transfers between devices, swap(): return lax.ppermute(value, 'ctx', [(i, i ^ x) for i in range(groups)])  38.3 us
    ppermute x10, starting transfers between devices, swap_z(): return lax.ppermute(value, 'ctx', pairs)  31.6 us
    pallas_call x4, Pallas kernels, products(): pl.pallas_call(functools.partial(products_kernel, table, model % LANES, l...  17 us
    pallas_call x3, Pallas kernels, back_part(): pl.pallas_call(functools.partial(back_kernel, table, model, cut, choices,...  15.1 us
    unnamed x33, local copies, waits for them, and re-layouts  11 us
    ppermute x8, starting transfers between devices, swap(): return lax.ppermute(value, 'ctx', [(i, i ^ x) for i in range(groups)])  10.4 us
    pallas_call x5, Pallas kernels, combine(): pl.pallas_call(functools.partial(combine_kernel, table, ('use', turn, nam...  6.83 us
    all_to_all x1, blocking collectives, per_device_full(): lax.all_to_all(slot_grad.reshape(experts, tokens), 'exp', split_axis=0, c...  6.34 us
  transfers between devices with their start and end apart: 24, of which 8 were waited for; matrix products, arithmetic and copies ran while one was open for 2% of the time, Pallas kernels for 29%

profile of v3, /device:TPU:0, one launch (start us, length us, event | category | flops | bytes accessed | tf_op | source)
XLA Modules:
  0.0 163.9 jit_solution(14038493513403480459)
XLA Ops:
  1.4 5.8 %collective-permute-start.4 = (bf16[192,2880]{1,0:T(8,128)(2,1)}, bf16[192,2880]{1,0:T(8,128)(2,1)}, u32[]{:S(2)}, u32[]{:S(2)}) collective-permute-start(bf16[192,2880]{1,0:T(8,128)(2,1)} %bitcast.17), channel_id=1, source_target_pairs={{0,8},{8,0},{4,12},{12,4},{16,24},{24,16},{20,28},{28,20},{1,9},{9... | collective-permute-start | bytes 3317768 | tf_op jit(solution)/shard_map/ppermute | solution.py:657
  13.1 7.3 %collective-permute-done.1.refs_2_ = bf16[128,1536]{1,0:T(8,128)(2,1)S(1)} collective-permute-done((bf16[128,1536]{1,0:T(8,128)(2,1)S(1)}, bf16[128,1536]{1,0:T(8,128)(2,1)S(1)}, u32[]{:S(2)}, u32[]{:S(2)}) %collective-permute-start.1) | collective-permute-done | bytes 393248 | tf_op jit(solution)/shard_map/ppermute | solution.py:645
  24.0 2.2 %split_hidden.1 = (bf16[4,192,512]{2,1,0:T(8,128)(2,1)S(1)}, bf16[1,192,512]{2,1,0:T(8,128)(2,1)S(1)}, bf16[3,192,512]{2,1,0:T(8,128)(2,1)S(1)}) custom-call(s32[32]{0:T(128)S(1)} %dynamic-slice_bitcast_fusion.where_ref, bf16[512,1536]{1,0:T(8,128)(2,1)S(1)} %bitcast.15, bf16[128,1536]{1,0:T(8,128)(2,1)S(1)} %get-tuple-element.21.refs_0_), custom_call_target="tpu_custom_call" | custom-call | bytes 6000000 | tf_op jit(solution)/shard_map/split_hidden/pallas_call | solution.py:229
  27.7 4.2 %collective-permute-done.3.refs_4_.refs_5_ = bf16[1,192,512]{2,1,0:T(8,128)(2,1)S(1)} collective-permute-done((bf16[1,192,512]{2,1,0:T(8,128)(2,1)S(1)}, bf16[1,192,512]{2,1,0:T(8,128)(2,1)S(1)}, u32[]{:S(2)}, u32[]{:S(2)}) %collective-permute-start.3) | collective-permute-done | bytes 196640 | tf_op jit(solution)/shard_map/ppermute | solution.py:645
  36.1 7.7 %collective-permute-done.8.refs_0_ = bf16[128,1408]{1,0:T(8,128)(2,1)S(1)} collective-permute-done((bf16[128,1408]{1,0:T(8,128)(2,1)S(1)}, bf16[128,1408]{1,0:T(8,128)(2,1)S(1)}, u32[]{:S(2)}, u32[]{:S(2)}) %collective-permute-start.8) | collective-permute-done | bytes 360480 | tf_op jit(solution)/shard_map/ppermute | solution.py:645
  45.4 3.3 %first_late.1.kept_ref.refs_1_ = f32[1,192,1472]{2,1,0:T(8,128)S(1)} custom-call(s32[32]{0:T(128)S(1)} %dynamic-slice_bitcast_fusion.where_ref, bf16[4,128,1536]{2,1,0:T(8,128)(2,1)S(1)} %pack_rows.2.refs_1_.refs_0_.refs_2_, bf16[4,128,1536]{2,1,0:T(8,128)(2,1)S(1)} %collective-permute-done.6.refs_1_.refs_3_, ...), custom_call_target="tpu_custom_call" | custom-call | bytes 12000000 | tf_op jit(solution)/shard_map/first_late/pallas_call | solution.py:310
  49.4 4.4 %collective-permute-done.9.refs_3_ = bf16[128,1408]{1,0:T(8,128)(2,1)S(1)} collective-permute-done((bf16[128,1408]{1,0:T(8,128)(2,1)S(1)}, bf16[128,1408]{1,0:T(8,128)(2,1)S(1)}, u32[]{:S(2)}, u32[]{:S(2)}) %collective-permute-start.9) | collective-permute-done | bytes 360480 | tf_op jit(solution)/shard_map/ppermute | solution.py:647
  56.8 3.4 %collective-permute-start.13 = (bf16[192,1472]{1,0:T(8,128)(2,1)S(1)}, bf16[192,1472]{1,0:T(8,128)(2,1)S(1)}, u32[]{:S(2)}, u32[]{:S(2)}) collective-permute-start(bf16[192,1472]{1,0:T(8,128)(2,1)S(1)} %begin.2.refs_4_), channel_id=1, source_target_pairs={{0,8},{8,0},{4,12},{12,4},{16,24},{24,16},{20,28},{28,20},{1,9},{9... | collective-permute-start | bytes 1695752 | tf_op jit(solution)/shard_map/ppermute | solution.py:657
  60.2 10.9 %collective-permute-done.11.refs_6_.refs_5_ = bf16[3,192,512]{2,1,0:T(8,128)(2,1)S(1)} collective-permute-done((bf16[3,192,512]{2,1,0:T(8,128)(2,1)S(1)}, bf16[3,192,512]{2,1,0:T(8,128)(2,1)S(1)}, u32[]{:S(2)}, u32[]{:S(2)}) %collective-permute-start.11) | collective-permute-done | bytes 589856 | tf_op jit(solution)/shard_map/ppermute | solution.py:645
  71.1 3.2 %first_early.1.kept_ref.refs_1_ = f32[1,192,1408]{2,1,0:T(8,128)S(1)} custom-call(s32[32]{0:T(128)S(1)} %dynamic-slice_bitcast_fusion.where_ref, bf16[4,128,1408]{2,1,0:T(8,128)(2,1)S(1)} %pack_rows.3.refs_0_.refs_2_, bf16[4,128,1408]{2,1,0:T(8,128)(2,1)S(1)} %collective-permute-done.10.refs_1_.refs_3_, ...), custom_call_target="tpu_custom_call" | custom-call | bytes 12000000 | tf_op jit(solution)/shard_map/first_early/pallas_call | solution.py:310
  75.1 3.1 %collective-permute-start.16 = (bf16[192,1408]{1,0:T(8,128)(2,1)S(1)}, bf16[192,1408]{1,0:T(8,128)(2,1)S(1)}, u32[]{:S(2)}, u32[]{:S(2)}) collective-permute-start(bf16[192,1408]{1,0:T(8,128)(2,1)S(1)} %begin.3.refs_6_), channel_id=1, source_target_pairs={{0,8},{8,0},{4,12},{12,4},{16,24},{24,16},{20,28},{28,20},{1,9},{9... | collective-permute-start | bytes 1622024 | tf_op jit(solution)/shard_map/ppermute | solution.py:657
  78.2 5.3 %rest_early.1.refs_2_.refs_4_.refs_3_.early_ref = f32[3,192,1408]{2,1,0:T(8,128)S(1)} custom-call(s32[32]{0:T(128)S(1)} %dynamic-slice_bitcast_fusion.where_ref, bf16[4,128,1408]{2,1,0:T(8,128)(2,1)S(1)} %pack_rows.3.refs_0_.refs_2_, bf16[4,128,1408]{2,1,0:T(8,128)(2,1)S(1)} %collective-permute-done.10.refs_1_.refs_3_, ...), custom_call_target="tpu_custom_call" | custom-call | bytes 12000000 | tf_op jit(solution)/shard_map/rest_early/pallas_call | solution.py:310
  83.5 5.2 %rest_late.1.refs_1_.refs_3_.refs_2_.late_ref = f32[3,192,1472]{2,1,0:T(8,128)S(1)} custom-call(s32[32]{0:T(128)S(1)} %dynamic-slice_bitcast_fusion.where_ref, bf16[4,128,1536]{2,1,0:T(8,128)(2,1)S(1)} %pack_rows.2.refs_1_.refs_0_.refs_2_, bf16[4,128,1536]{2,1,0:T(8,128)(2,1)S(1)} %collective-permute-done.6.refs_1_.refs_3_, ...), custom_call_target="tpu_custom_call" | custom-call | bytes 12000000 | tf_op jit(solution)/shard_map/rest_late/pallas_call | solution.py:310
  92.1 6.8 %back_part.3 = (bf16[3,192,512]{2,1,0:T(8,128)(2,1)S(1)}, bf16[3,192,512]{2,1,0:T(8,128)(2,1)S(1)}, f32[8,1024]{1,0:T(8,128)S(1)}) custom-call(s32[32]{0:T(128)S(1)} %dynamic-slice_bitcast_fusion.where_ref, bf16[4,128,1536]{2,1,0:T(8,128)(2,1)S(1)} %pack_rows.2.refs_1_.refs_0_.refs_2_, bf16[4,128,1536]{2,1,0:T(8,128)(2,1)S(1)} %collective-permute-done.6.refs_1_.refs_3_, ...), custom_call_target="tpu_custom_call" | custom-call | bytes 18000000 | tf_op jit(solution)/shard_map/back_part/pallas_call | solution.py:541
  102.0 4.2 %back_part.4 = (bf16[1,192,512]{2,1,0:T(8,128)(2,1)S(1)}, bf16[1,192,512]{2,1,0:T(8,128)(2,1)}, f32[8,1024]{1,0:T(8,128)S(1)}) custom-call(s32[32]{0:T(128)S(1)} %dynamic-slice_bitcast_fusion.where_ref, bf16[4,128,1536]{2,1,0:T(8,128)(2,1)S(1)} %pack_rows.2.refs_1_.refs_0_.refs_2_, bf16[4,128,1536]{2,1,0:T(8,128)(2,1)S(1)} %collective-permute-done.6.refs_1_.refs_3_, ...), custom_call_target="tpu_custom_call" | custom-call | bytes 18000000 | tf_op jit(solution)/shard_map/back_part/pallas_call | solution.py:541
  106.2 7.1 %collective-permute-done.18.refs_1_ = bf16[3,192,512]{2,1,0:T(8,128)(2,1)S(1)} collective-permute-done((bf16[3,192,512]{2,1,0:T(8,128)(2,1)S(1)}, bf16[3,192,512]{2,1,0:T(8,128)(2,1)S(1)}, u32[]{:S(2)}, u32[]{:S(2)}) %collective-permute-start.18) | collective-permute-done | bytes 589856 | tf_op jit(solution)/shard_map/ppermute | solution.py:645
  113.3 2.1 %join_hidden.2.refs_4_ = bf16[512,1536]{1,0:T(8,128)(2,1)} custom-call(s32[32]{0:T(128)S(1)} %dynamic-slice_bitcast_fusion.where_ref, bf16[3,192,512]{2,1,0:T(8,128)(2,1)S(1)} %get-tuple-element.30.refs_0_, bf16[3,192,512]{2,1,0:T(8,128)(2,1)S(1)} %collective-permute-done.18.refs_1_, f32[8,1024]{1,0:T(8,128)S(1)} %get-tuple-element.29.refs_2_.refs_10_), custom_call_target="tpu_custom_call" | custom-call | bytes 6000000 | tf_op jit(solution)/shard_map/join_hidden/pallas_call | solution.py:595
  116.8 2.2 %combine.8.refs_3_ = bf16[192,2880]{1,0:T(8,128)(2,1)} custom-call(s32[32]{0:T(128)S(1)} %dynamic-slice_bitcast_fusion.where_ref, bf16[192,1472]{1,0:T(8,128)(2,1)S(1)} %collective-permute-done.15.refs_0_.refs_8_, bf16[192,1408]{1,0:T(8,128)(2,1)S(1)} %collective-permute-done.17.refs_1_.refs_9_, ...), custom_call_target="tpu_custom_call" | custom-call | bytes 4500000 | tf_op jit(solution)/shard_map/combine/pallas_call | solution.py:374
  119.0 14.3 %collective-permute-start.22 = (bf16[192,2880]{1,0:T(8,128)(2,1)}, bf16[192,2880]{1,0:T(8,128)(2,1)}, u32[]{:S(2)}, u32[]{:S(2)}) collective-permute-start(bf16[192,2880]{1,0:T(8,128)(2,1)} %combine.8.refs_3_), channel_id=1, source_target_pairs={{0,8},{8,0},{4,12},{12,4},{16,24},{24,16},{20,28},{28,20},{1,9},{9... | collective-permute-start | bytes 3317768 | tf_op jit(solution)/shard_map/ppermute | solution.py:657
  133.3 2.2 %combine.9.refs_11_ = bf16[192,2880]{1,0:T(8,128)(2,1)} custom-call(s32[32]{0:T(128)S(1)} %dynamic-slice_bitcast_fusion.where_ref, bf16[192,2880]{1,0:T(8,128)(2,1)S(1)} %collective-permute-done.14.refs_0_.refs_7_, f32[3,192,1472]{2,1,0:T(8,128)S(1)} %rest_late.1.refs_1_.refs_3_.refs_2_.late_ref, ...), custom_call_target="tpu_custom_call" | custom-call | bytes 4500000 | tf_op jit(solution)/shard_map/combine/pallas_call | solution.py:374
  137.4 4.2 %back_part.5 = (bf16[1,192,512]{2,1,0:T(8,128)(2,1)S(1)}, bf16[1,192,512]{2,1,0:T(8,128)(2,1)}, f32[8,1024]{1,0:T(8,128)S(1)}) custom-call(s32[32]{0:T(128)S(1)} %dynamic-slice_bitcast_fusion.where_ref, bf16[4,128,1536]{2,1,0:T(8,128)(2,1)S(1)} %pack_rows.2.refs_1_.refs_0_.refs_2_, bf16[4,128,1536]{2,1,0:T(8,128)(2,1)S(1)} %collective-permute-done.6.refs_1_.refs_3_, ...), custom_call_target="tpu_custom_call" | custom-call | bytes 18000000 | tf_op jit(solution)/shard_map/back_part/pallas_call | solution.py:541
  145.9 6.3 %all_to_all.11 = f32[4,1,128]{2,1,0:T(1,128)S(1)} all-to-all(f32[4,1,128]{2,1,0:T(1,128)S(1)} %add_bitcast_fusion), channel_id=1, replica_groups=mesh['ctx'=8,'exp'=4] {'exp'}, dimensions={0} | all-to-all | bytes 4096 | tf_op jit(solution)/shard_map/all_to_all | solution.py:749
  157.2 2.7 %join_hidden.3 = bf16[512,1536]{1,0:T(8,128)(2,1)} custom-call(s32[32]{0:T(128)S(1)} %dynamic-slice_bitcast_fusion.where_ref, bf16[1,192,512]{2,1,0:T(8,128)(2,1)S(1)} %copy-done.10, bf16[1,192,512]{2,1,0:T(8,128)(2,1)} %collective-permute-done.20.refs_1_, bf16[1,192,512]{2,1,0:T(8,128)(2,1)S(1)} %copy-done.12, ...), custom_call_target="tpu_custom_call", output_to_operand_aliasing={{}: (5, {})} | custom-call | bytes 6000000 | tf_op jit(solution)/shard_map/join_hidden/pallas_call | solution.py:595
  159.9 3.9 %total_grad.1 = f32[1,192,2880]{2,1,0:T(8,128)} custom-call(bf16[192,2880]{1,0:T(8,128)(2,1)} %collective-permute-done.22.a_ref, bf16[192,2880]{1,0:T(8,128)(2,1)} %collective-permute-done.23.b_ref, f32[3,192,1472]{2,1,0:T(8,128)S(1)} %rest_late.1.refs_1_.refs_3_.refs_2_.late_ref, f32[3,192,1408]{2,1,0:T(8,128)S(1)} %copy-done.1), custom_call_target="tpu_custom_call" | custom-call | bytes 6000000 | tf_op jit(solution)/shard_map/total_grad/pallas_call | solution.py:433
  (86 shorter events, 40.9 us)
Async XLA Ops:
  0.6 31.3 %collective-permute-start.5 = (bf16[192,2880]{1,0:T(8,128)(2,1)}, bf16[192,2880]{1,0:T(8,128)(2,1)S(1)}, u32[]{:S(2)}, u32[]{:S(2)}) collective-permute-start(bf16[192,2880]{1,0:T(8,128)(2,1)} %bitcast.16), channel_id=1, source_target_pairs={{8,16},{16,8},{12,20},{20,12},{9,17},{17,9},{13,21},{21,13},{10,18... | collective-permute-start | bytes 3317768 | tf_op jit(solution)/shard_map/ppermute | solution.py:657
  1.4 30.8 %collective-permute-start.4 = (bf16[192,2880]{1,0:T(8,128)(2,1)}, bf16[192,2880]{1,0:T(8,128)(2,1)}, u32[]{:S(2)}, u32[]{:S(2)}) collective-permute-start(bf16[192,2880]{1,0:T(8,128)(2,1)} %bitcast.17), channel_id=1, source_target_pairs={{0,8},{8,0},{4,12},{12,4},{16,24},{24,16},{20,28},{28,20},{1,9},{9... | collective-permute-start | bytes 3317768 | tf_op jit(solution)/shard_map/ppermute | solution.py:657
  10.0 10.4 %collective-permute-start.1 = (bf16[128,1536]{1,0:T(8,128)(2,1)S(1)}, bf16[128,1536]{1,0:T(8,128)(2,1)S(1)}, u32[]{:S(2)}, u32[]{:S(2)}) collective-permute-start(bf16[128,1536]{1,0:T(8,128)(2,1)S(1)} %get-tuple-element.21.refs_0_), channel_id=1, source_target_pairs={{0,4},{4,0},{8,12},{12,8},{16,20},{20,16},{24,28},{28,24},{1,5},{5... | collective-permute-start | bytes 1179656 | tf_op jit(solution)/shard_map/ppermute | solution.py:645
  11.5 20.4 %collective-permute-start = (bf16[128,1536]{1,0:T(8,128)(2,1)S(1)}, bf16[128,1536]{1,0:T(8,128)(2,1)S(1)}, u32[]{:S(2)}, u32[]{:S(2)}) collective-permute-start(bf16[128,1536]{1,0:T(8,128)(2,1)S(1)} %get-tuple-element.21.refs_0_), channel_id=1, source_target_pairs={{0,2},{1,3},{2,0},{3,1},{4,6},{5,7},{6,4},{7,5},{8,10},{9,11},{10,... | collective-permute-start | bytes 1179656 | tf_op jit(solution)/shard_map/ppermute | solution.py:647
  20.3 11.6 %collective-permute-start.2 = (bf16[128,1536]{1,0:T(8,128)(2,1)S(1)}, bf16[128,1536]{1,0:T(8,128)(2,1)S(1)}, u32[]{:S(2)}, u32[]{:S(2)}) collective-permute-start(bf16[128,1536]{1,0:T(8,128)(2,1)S(1)} %collective-permute-done.1.refs_2_), channel_id=1, source_target_pairs={{0,2},{1,3},{2,0},{3,1},{4,6},{5,7},{6,4},{7,5},{8,10},{9,11},{10,... | collective-permute-start | bytes 1179656 | tf_op jit(solution)/shard_map/ppermute | solution.py:647
  26.2 5.7 %collective-permute-start.3 = (bf16[1,192,512]{2,1,0:T(8,128)(2,1)S(1)}, bf16[1,192,512]{2,1,0:T(8,128)(2,1)S(1)}, u32[]{:S(2)}, u32[]{:S(2)}) collective-permute-start(bf16[1,192,512]{2,1,0:T(8,128)(2,1)S(1)} %get-tuple-element.22), channel_id=1, source_target_pairs={{0,4},{4,0},{8,12},{12,8},{16,20},{20,16},{24,28},{28,24},{1,5},{5... | collective-permute-start | bytes 589832 | tf_op jit(solution)/shard_map/ppermute | solution.py:645
  33.0 12.4 %collective-permute-start.6 = (bf16[4,128,1536]{2,1,0:T(8,128)(2,1)S(1)}, bf16[4,128,1536]{2,1,0:T(8,128)(2,1)S(1)}, u32[]{:S(2)}, u32[]{:S(2)}) collective-permute-start(bf16[4,128,1536]{2,1,0:T(8,128)(2,1)S(1)} %pack_rows.2.refs_1_.refs_0_.refs_2_), channel_id=1, source_target_pairs={{0,1},{1,0},{2,3},{3,2},{4,5},{5,4},{6,7},{7,6},{8,9},{9,8},{10,11... | collective-permute-start | bytes 4718600 | tf_op jit(solution)/shard_map/ppermute | solution.py:647
  33.0 10.8 %collective-permute-start.8 = (bf16[128,1408]{1,0:T(8,128)(2,1)S(1)}, bf16[128,1408]{1,0:T(8,128)(2,1)S(1)}, u32[]{:S(2)}, u32[]{:S(2)}) collective-permute-start(bf16[128,1408]{1,0:T(8,128)(2,1)S(1)} %hold.2.refs_0_), channel_id=1, source_target_pairs={{0,4},{4,0},{8,12},{12,8},{16,20},{20,16},{24,28},{28,24},{1,5},{5... | collective-permute-start | bytes 1081352 | tf_op jit(solution)/shard_map/ppermute | solution.py:645
  34.6 14.8 %collective-permute-start.7 = (bf16[128,1408]{1,0:T(8,128)(2,1)S(1)}, bf16[128,1408]{1,0:T(8,128)(2,1)S(1)}, u32[]{:S(2)}, u32[]{:S(2)}) collective-permute-start(bf16[128,1408]{1,0:T(8,128)(2,1)S(1)} %hold.2.refs_0_), channel_id=1, source_target_pairs={{0,2},{1,3},{2,0},{3,1},{4,6},{5,7},{6,4},{7,5},{8,10},{9,11},{10,... | collective-permute-start | bytes 1081352 | tf_op jit(solution)/shard_map/ppermute | solution.py:647
  43.9 10.0 %collective-permute-start.9 = (bf16[128,1408]{1,0:T(8,128)(2,1)S(1)}, bf16[128,1408]{1,0:T(8,128)(2,1)S(1)}, u32[]{:S(2)}, u32[]{:S(2)}) collective-permute-start(bf16[128,1408]{1,0:T(8,128)(2,1)S(1)} %get-tuple-element.25.refs_2_), channel_id=1, source_target_pairs={{0,2},{1,3},{2,0},{3,1},{4,6},{5,7},{6,4},{7,5},{8,10},{9,11},{10,... | collective-permute-start | bytes 1081352 | tf_op jit(solution)/shard_map/ppermute | solution.py:647
  54.5 16.6 %collective-permute-start.10 = (bf16[4,128,1408]{2,1,0:T(8,128)(2,1)S(1)}, bf16[4,128,1408]{2,1,0:T(8,128)(2,1)S(1)}, u32[]{:S(2)}, u32[]{:S(2)}) collective-permute-start(bf16[4,128,1408]{2,1,0:T(8,128)(2,1)S(1)} %pack_rows.3.refs_0_.refs_2_), channel_id=1, source_target_pairs={{0,1},{1,0},{2,3},{3,2},{4,5},{5,4},{6,7},{7,6},{8,9},{9,8},{10,11... | collective-permute-start | bytes 4325384 | tf_op jit(solution)/shard_map/ppermute | solution.py:647
  54.5 34.2 %collective-permute-start.12 = (bf16[192,2880]{1,0:T(8,128)(2,1)}, bf16[192,2880]{1,0:T(8,128)(2,1)S(1)}, u32[]{:S(2)}, u32[]{:S(2)}) collective-permute-start(bf16[192,2880]{1,0:T(8,128)(2,1)} %collective-permute-done.4.refs_5_.refs_8_), channel_id=1, source_target_pairs={{8,16},{16,8},{12,20},{20,12},{9,17},{17,9},{13,21},{21,13},{10,18... | collective-permute-start | bytes 3317768 | tf_op jit(solution)/shard_map/ppermute | solution.py:657
  55.3 15.8 %collective-permute-start.11 = (bf16[3,192,512]{2,1,0:T(8,128)(2,1)S(1)}, bf16[3,192,512]{2,1,0:T(8,128)(2,1)S(1)}, u32[]{:S(2)}, u32[]{:S(2)}) collective-permute-start(bf16[3,192,512]{2,1,0:T(8,128)(2,1)S(1)} %get-tuple-element.27), channel_id=1, source_target_pairs={{0,4},{4,0},{8,12},{12,8},{16,20},{20,16},{24,28},{28,24},{1,5},{5... | collective-permute-start | bytes 1769480 | tf_op jit(solution)/shard_map/ppermute | solution.py:645
  56.8 17.4 %collective-permute-start.13 = (bf16[192,1472]{1,0:T(8,128)(2,1)S(1)}, bf16[192,1472]{1,0:T(8,128)(2,1)S(1)}, u32[]{:S(2)}, u32[]{:S(2)}) collective-permute-start(bf16[192,1472]{1,0:T(8,128)(2,1)S(1)} %begin.2.refs_4_), channel_id=1, source_target_pairs={{0,8},{8,0},{4,12},{12,4},{16,24},{24,16},{20,28},{28,20},{1,9},{9... | collective-permute-start | bytes 1695752 | tf_op jit(solution)/shard_map/ppermute | solution.py:657
  75.1 15.5 %collective-permute-start.16 = (bf16[192,1408]{1,0:T(8,128)(2,1)S(1)}, bf16[192,1408]{1,0:T(8,128)(2,1)S(1)}, u32[]{:S(2)}, u32[]{:S(2)}) collective-permute-start(bf16[192,1408]{1,0:T(8,128)(2,1)S(1)} %begin.3.refs_6_), channel_id=1, source_target_pairs={{0,8},{8,0},{4,12},{12,4},{16,24},{24,16},{20,28},{28,20},{1,9},{9... | collective-permute-start | bytes 1622024 | tf_op jit(solution)/shard_map/ppermute | solution.py:657
  89.7 43.7 %collective-permute-start.14 = (bf16[192,2880]{1,0:T(8,128)(2,1)S(1)}, bf16[192,2880]{1,0:T(8,128)(2,1)S(1)}, u32[]{:S(2)}, u32[]{:S(2)}) collective-permute-start(bf16[192,2880]{1,0:T(8,128)(2,1)S(1)} %combine.5.refs_2_), channel_id=1, source_target_pairs={{0,8},{8,0},{4,12},{12,4},{16,24},{24,16},{20,28},{28,20},{1,9},{9... | collective-permute-start | bytes 3317768 | tf_op jit(solution)/shard_map/ppermute | solution.py:657
  98.9 14.4 %collective-permute-start.18 = (bf16[3,192,512]{2,1,0:T(8,128)(2,1)S(1)}, bf16[3,192,512]{2,1,0:T(8,128)(2,1)S(1)}, u32[]{:S(2)}, u32[]{:S(2)}) collective-permute-start(bf16[3,192,512]{2,1,0:T(8,128)(2,1)S(1)} %get-tuple-element.31), channel_id=1, source_target_pairs={{0,4},{4,0},{8,12},{12,8},{16,20},{20,16},{24,28},{28,24},{1,5},{5... | collective-permute-start | bytes 1769480 | tf_op jit(solution)/shard_map/ppermute | solution.py:645
  100.4 14.9 %collective-permute-start.15 = (bf16[192,1472]{1,0:T(8,128)(2,1)S(1)}, bf16[192,1472]{1,0:T(8,128)(2,1)S(1)}, u32[]{:S(2)}, u32[]{:S(2)}) collective-permute-start(bf16[192,1472]{1,0:T(8,128)(2,1)S(1)} %combine.6.refs_2_), channel_id=1, source_target_pairs={{8,16},{16,8},{12,20},{20,12},{9,17},{17,9},{13,21},{21,13},{10,18... | collective-permute-start | bytes 1695752 | tf_op jit(solution)/shard_map/ppermute | solution.py:657
  101.1 14.2 %collective-permute-start.17 = (bf16[192,1408]{1,0:T(8,128)(2,1)S(1)}, bf16[192,1408]{1,0:T(8,128)(2,1)S(1)}, u32[]{:S(2)}, u32[]{:S(2)}) collective-permute-start(bf16[192,1408]{1,0:T(8,128)(2,1)S(1)} %combine.7.refs_10_), channel_id=1, source_target_pairs={{8,16},{16,8},{12,20},{20,12},{9,17},{17,9},{13,21},{21,13},{10,18... | collective-permute-start | bytes 1622024 | tf_op jit(solution)/shard_map/ppermute | solution.py:657
  119.0 40.9 %collective-permute-start.22 = (bf16[192,2880]{1,0:T(8,128)(2,1)}, bf16[192,2880]{1,0:T(8,128)(2,1)}, u32[]{:S(2)}, u32[]{:S(2)}) collective-permute-start(bf16[192,2880]{1,0:T(8,128)(2,1)} %combine.8.refs_3_), channel_id=1, source_target_pairs={{0,8},{8,0},{4,12},{12,4},{16,24},{24,16},{20,28},{28,20},{1,9},{9... | collective-permute-start | bytes 3317768 | tf_op jit(solution)/shard_map/ppermute | solution.py:657
  135.6 24.4 %collective-permute-start.23 = (bf16[192,2880]{1,0:T(8,128)(2,1)}, bf16[192,2880]{1,0:T(8,128)(2,1)}, u32[]{:S(2)}, u32[]{:S(2)}) collective-permute-start(bf16[192,2880]{1,0:T(8,128)(2,1)} %combine.9.refs_11_), channel_id=1, source_target_pairs={{8,16},{16,8},{12,20},{20,12},{9,17},{17,9},{13,21},{21,13},{10,18... | collective-permute-start | bytes 3317768 | tf_op jit(solution)/shard_map/ppermute | solution.py:657
  142.3 3.7 %collective-permute-start.19 = (f32[1,512]{1,0:T(1,128)S(1)}, f32[1,512]{1,0:T(1,128)S(1)}, u32[]{:S(2)}, u32[]{:S(2)}) collective-permute-start(f32[1,512]{1,0:T(1,128)S(1)} %slice.7), channel_id=1, source_target_pairs={{0,4},{4,0},{8,12},{12,8},{16,20},{20,16},{24,28},{28,24},{1,5},{5... | collective-permute-start | bytes 6152 | tf_op jit(solution)/shard_map/ppermute | solution.py:645
  142.8 11.7 %collective-permute-start.20 = (bf16[1,192,512]{2,1,0:T(8,128)(2,1)}, bf16[1,192,512]{2,1,0:T(8,128)(2,1)}, u32[]{:S(2)}, u32[]{:S(2)}) collective-permute-start(bf16[1,192,512]{2,1,0:T(8,128)(2,1)} %get-tuple-element.34), channel_id=1, source_target_pairs={{0,4},{4,0},{8,12},{12,8},{16,20},{20,16},{24,28},{28,24},{1,5},{5... | collective-permute-start | bytes 589832 | tf_op jit(solution)/shard_map/ppermute | solution.py:645
  144.3 10.2 %collective-permute-start.21 = (bf16[1,192,512]{2,1,0:T(8,128)(2,1)}, bf16[1,192,512]{2,1,0:T(8,128)(2,1)}, u32[]{:S(2)}, u32[]{:S(2)}) collective-permute-start(bf16[1,192,512]{2,1,0:T(8,128)(2,1)} %get-tuple-element.36), channel_id=1, source_target_pairs={{0,4},{4,0},{8,12},{12,8},{16,20},{20,16},{24,28},{28,24},{1,5},{5... | collective-permute-start | bytes 589832 | tf_op jit(solution)/shard_map/ppermute | solution.py:645
  (16 other events, 132.3 us)

commit v4 on v3

--- a/solution.py
+++ b/solution.py
@@ -9,7 +9,7 @@
 from jax.sharding import PartitionSpec as P
 
 LANES = 128
-SCALE = 3_000_000
+SCALE = 1_000_000
 NT = (((1,), (1,)), ((), ()))
 NN = (((1,), (0,)), ((), ()))
 f32 = jnp.float32
@@ -37,7 +37,7 @@
 
 
 def taking(microseconds):
-    return pl.CostEstimate(flops=0, bytes_accessed=int(microseconds * SCALE), transcendentals=0)
+    return pl.CostEstimate(flops=int(microseconds * SCALE), bytes_accessed=int(microseconds * 3e6), transcendentals=0)
 
 
 def chain_plan(depth):
@@ -110,8 +110,19 @@
     return table, weights, uses
 
 
-def rows_kernel(cut, grad_ref, logits_ref, ids_ref, late_ref, early_ref, gates_ref):
+def rows_kernel(cut, grad_hbm, logits_hbm, ids_hbm, late_ref, early_ref, gates_ref, *scratch):
+    grad_ref, logits_ref, ids_ref, sems = scratch
     model, tokens = grad_ref.shape
+    copies = [
+        pltpu.make_async_copy(source, target, sems.at[place])
+        for place, (source, target) in enumerate(
+            ((grad_hbm, grad_ref), (logits_hbm, logits_ref), (ids_hbm, ids_ref))
+        )
+    ]
+    for copy in copies:
+        copy.start()
+    for copy in copies:
+        copy.wait()
     count = logits_ref.shape[0]
     width = cut + late_ref.shape[1]
     logits = logits_ref[...]
@@ -152,8 +163,14 @@
             jax.ShapeDtypeStruct((tokens, cut), bf16),
             jax.ShapeDtypeStruct((count, tokens), f32),
         ),
-        in_specs=[whole()] * 3,
+        in_specs=[anywhere()] * 3,
         out_specs=(whole(),) * 3,
+        scratch_shapes=[
+            pltpu.VMEM((model, tokens), bf16),
+            pltpu.VMEM((count, tokens), f32),
+            pltpu.VMEM((count, tokens), jnp.int32),
+            pltpu.SemaphoreType.DMA((3,)),
+        ],
         compiler_params=params(),
         cost_estimate=taking(2),
         name="make_rows",
@@ -182,6 +199,10 @@
         cost_estimate=taking(1),
         name="pack_rows",
     )(*values, *after)
+
+
+def blocks_of(refs, places):
+    return [refs[array] if place is None else refs[array].at[place] for array, place in places]
 
 
 def hold_kernel(*refs):
@@ -239,95 +260,60 @@
     )(where, hidden, *after)
 
 
-def pair_lanes(step, steps, me, tokens):
-    high = 2 * lax.rem(step, steps // 2)
-    return pl.multiple_of(lax.div(me ^ high, 2) * 2 * tokens, 2 * tokens)
-
-
-def half_of(me, tokens, other):
-    return pl.multiple_of((lax.rem(me, 2) ^ other) * tokens, tokens)
-
-
-def products_kernel(table, gate_lane, shards, cut, where_ref, *refs):
-    first = len(refs) == 10
-    rows = refs[:2]
-    gate_tiles = refs[2:4]
-    own_ref, other_ref = refs[4:6]
-    scaled = refs[-1]
-    kept_ref = refs[-2]
-    tokens = rows[0].shape[1]
-    slots = own_ref.shape[2]
+def place_of(place, count, me, tokens):
+    start = (place // count) * count * tokens + ((place % count) ^ me) * tokens
+    return pl.multiple_of(start, tokens)
+
+
+def products_kernel(table, model, counts, places, shards, skip, where_ref, *refs):
+    used = sum(counts)
+    rows = blocks_of(refs[: counts[0]], places[0])
+    gated = blocks_of(refs[counts[0] : used], places[1])
+    number = len(rows)
+    own_ref, other_ref = refs[used : used + 2]
+    kept_ref, scaled = refs[-2:]
+    tokens = rows[0].shape[0]
+    units, slots = own_ref.shape[1:]
+    width = kept_ref.shape[2]
     me = where_ref[table["me"]]
-    step, steps = pl.program_id(0), pl.num_programs(0)
     lane = lax.broadcasted_iota(jnp.int32, (tokens, LANES), 1)
-    for other in range(2):
-        here = pl.ds(half_of(me, tokens, other), tokens)
-        picked = jnp.where(lane == gate_lane + me, gate_tiles[other][0].astype(f32), 0.0)
+    for place in range(number):
+        here = pl.ds(place_of(place, number // 2, me, tokens), tokens)
+        tile = gated[place][:, gated[place].shape[1] - LANES :]
+        picked = jnp.where(lane == model % LANES + me, tile.astype(f32), 0.0)
         gate = jnp.sum(picked, axis=1, keepdims=True)
-        scaled[here, :] = (rows[other][0].astype(f32) * gate).astype(bf16)
-    lanes = pl.ds(pair_lanes(step, steps, me, tokens), 2 * tokens)
-    skip = own_ref.shape[0] - len(shards)
-    width = kept_ref.shape[2]
-
-    def add(hidden):
-        total = dot(hidden, scaled[...], NN)[:, :width]
-        units = total.shape[0] // len(shards)
-
-        @pl.when(step == 0)
-        def _():
-            for place in range(len(shards)):
-                kept_ref[place] = total[place * units : (place + 1) * units]
-
-        @pl.when(step != 0)
-        def _():
-            for place in range(len(shards)):
-                kept_ref[place] += total[place * units : (place + 1) * units]
+        scaled[here, :] = (rows[place][:, :width].astype(f32) * gate).astype(bf16)
 
     def stacked(ref, offset):
-        parts = [ref[offset + shard, :, lanes] for shard in range(len(shards))]
+        parts = [ref[offset + shard] for shard in range(shards)]
         return jnp.concatenate(parts, axis=0) if len(parts) > 1 else parts[0]
 
-    @pl.when(step < steps // 2)
-    def _():
-        add(stacked(own_ref, skip))
-
-    @pl.when(step >= steps // 2)
-    def _():
-        add(stacked(other_ref, 0))
-
-
-def products(table, where, rows, gated, own, other, skip, model, cut, name, after):
-    number, tokens, width = rows[0].shape
+    total = dot(stacked(own_ref, skip), scaled[:slots, :], NN)
+    total = total + dot(stacked(other_ref, 0), scaled[slots:, :], NN)
+    for shard in range(shards):
+        kept_ref[shard] = total[shard * units : (shard + 1) * units]
+
+
+def products(table, where, rows, gated, own, other, skip, model, width, name, after):
+    arrays, places = zip(rows, gated)
+    tokens = arrays[0][0].shape[-2]
+    counts = [len(part) for part in arrays]
+    number = 2 * (own.shape[2] // tokens)
     shards, units, slots = other.shape
-    late = cut > 0
-    columns = model - cut if late else width
-    gate_tile = (gated[0].shape[2] - LANES) // LANES
-    row_spec = pl.BlockSpec((1, tokens, width), lambda j, s: (j, 0, 0))
-    tile_spec = pl.BlockSpec((1, tokens, LANES), lambda j, s: (j, 0, gate_tile))
-    own_shards = shards if skip == 0 else own.shape[0]
-    own_spec = pl.BlockSpec((own_shards, units, slots), lambda j, s: (0, 0, 0))
-    other_spec = pl.BlockSpec((shards, units, slots), lambda j, s: (0, 0, 0))
-    return pl.pallas_call(
-        functools.partial(products_kernel, table, model % LANES, list(range(shards)), cut),
-        out_shape=jax.ShapeDtypeStruct((shards, units, columns), f32),
-        grid_spec=pltpu.PrefetchScalarGridSpec(
-            num_scalar_prefetch=1,
-            grid=(number,),
-            in_specs=[row_spec] * 2
-            + [tile_spec] * 2
-            + [own_spec, other_spec]
-            + [anywhere()] * len(after),
-            out_specs=pl.BlockSpec((shards, units, columns), lambda j, s: (0, 0, 0)),
-            scratch_shapes=[pltpu.VMEM((2 * tokens, width), bf16)],
-        ),
+    return pl.pallas_call(
+        functools.partial(products_kernel, table, model, counts, places, shards, skip),
+        out_shape=jax.ShapeDtypeStruct((shards, units, width), f32),
+        in_specs=[scalars()] + [whole()] * (sum(counts) + 2) + [anywhere()] * len(after),
+        out_specs=whole(),
+        scratch_shapes=[pltpu.VMEM((number * tokens, width), bf16)],
         compiler_params=params(),
         cost_estimate=taking(4),
         name=name,
-    )(where, *rows, *gated, own, other, *after)
+    )(where, *arrays[0], *arrays[1], own, other, *after)
 
 
 def rows_of(units):
-    return units // 4 if units % 64 == 0 else units
+    return units // 2 if units % 32 == 0 else units
 
 
 def column_parts(arrays, cut):
@@ -356,7 +342,7 @@
             outs[chunk][...] = total
 
 
-def combine(table, where, coming, first, rest, turn, name, used, cut, after):
+def combine(table, where, coming, first, rest, turn, name, used, cut, after, chunked=False):
     units = coming[0].shape[0]
     model = sum(part.shape[1] for part in coming)
     block = rows_of(units)
@@ -370,19 +356,19 @@
         sides.append("rest")
         operands += rest
         specs += [pl.BlockSpec((1, block, part.shape[2]), lambda j, s: (s[column], j, 0)) for part in rest]
-    flat = pl.BlockSpec((block, model), lambda j, s: (j, 0))
+    widths = [model - cut, cut] if chunked else [model]
     return pl.pallas_call(
         functools.partial(
-            combine_kernel, table, ("use", turn, name), cut, (len(coming), len(operands), 1), sides
+            combine_kernel, table, ("use", turn, name), cut, (len(coming), len(operands), len(widths)), sides
         ),
-        out_shape=jax.ShapeDtypeStruct((units, model), bf16),
+        out_shape=[jax.ShapeDtypeStruct((units, count), bf16) for count in widths],
         grid_spec=pltpu.PrefetchScalarGridSpec(
             num_scalar_prefetch=1,
             grid=(units // block,),
             in_specs=[pl.BlockSpec((block, part.shape[1]), lambda j, s: (j, 0)) for part in coming]
             + specs
             + [anywhere()] * len(after),
-            out_specs=flat,
+            out_specs=[pl.BlockSpec((block, count), lambda j, s: (j, 0)) for count in widths],
         ),
         compiler_params=params(),
         cost_estimate=taking(1.5),
@@ -420,21 +406,27 @@
     )(where, coming, kept, *after)
 
 
-def total_kernel(cut, a_ref, b_ref, late_ref, early_ref, out_ref):
-    for start, kept_ref in ((cut, late_ref), (0, early_ref)):
+def total_kernel(cut, counts, *refs):
+    coming = [refs[: counts[0]], refs[counts[0] : sum(counts)]]
+    out_ref = refs[-1]
+    for chunk, start in enumerate((cut, 0)):
+        kept_ref = refs[sum(counts) + chunk]
         here = slice(start, start + kept_ref.shape[2])
-        out_ref[0, :, here] = kept_ref[0] + a_ref[:, here].astype(f32) + b_ref[:, here].astype(f32)
+        total = kept_ref[0]
+        for parts in coming:
+            total = total + (parts[0][:, here] if len(parts) == 1 else parts[chunk][...]).astype(f32)
+        out_ref[0, :, here] = total
 
 
 def total_grad(a, b, kept, cut):
-    units, model = a.shape
+    units = a[0].shape[0]
+    model = sum(part.shape[1] for part in a)
     block = rows_of(units)
-    flat = pl.BlockSpec((block, model), lambda j: (j, 0))
-    return pl.pallas_call(
-        functools.partial(total_kernel, cut),
+    return pl.pallas_call(
+        functools.partial(total_kernel, cut, (len(a), len(b))),
         out_shape=jax.ShapeDtypeStruct((1, units, model), f32),
         grid=(units // block,),
-        in_specs=[flat, flat]
+        in_specs=[pl.BlockSpec((block, part.shape[1]), lambda j: (j, 0)) for part in (*a, *b)]
         + [
             pl.BlockSpec((1, block, part.shape[2]), functools.partial(lambda last, j: (last, j, 0), part.shape[0] - 1))
             for part in kept
@@ -443,39 +435,38 @@
         compiler_params=params(),
         cost_estimate=taking(2),
         name="total_grad",
-    )(a, b, *kept)
-
-
-def back_kernel(table, model, cut, choices, parts, guard, summed, where_ref, *refs):
+    )(*a, *b, *kept)
+
+
+def back_kernel(table, model, cut, counts, places, choices, parts, guard, summed, where_ref, *refs):
     keys = [key for choice in choices for key in choice]
-    late, early = refs[:2], refs[2:4]
-    own_ref, first_ref, rest_ref = refs[4:7]
-    weight_refs, used = {}, 7
+    used = sum(counts)
+    late = blocks_of(refs[: counts[0]], places[0])
+    early = blocks_of(refs[counts[0] : used], places[1])
+    number = len(late)
+    own_ref, first_ref, rest_ref = refs[used : used + 3]
+    weight_refs, used = {}, used + 3
     for key, count in zip(keys, parts):
         weight_refs[key] = refs[used : used + count]
         used += count
     before_ref = refs[used] if summed else None
-    mine_ref, theirs_ref, sums_ref = refs[-3:]
-    tokens = late[0].shape[1]
+    outs = refs[len(refs) - 2 * len(choices) - 1 : -1]
+    sums_ref = refs[-1]
+    tokens = late[0].shape[0]
     units = own_ref.shape[1]
-    slots_all = own_ref.shape[2]
     me = where_ref[table["me"]]
-    step, steps = pl.program_id(0), pl.num_programs(0)
-    start = late[0].shape[2] - LANES
+    start = late[0].shape[1] - LANES
     eight = lax.broadcasted_iota(jnp.int32, (8, LANES), 1)
     onehot = jnp.where(eight == model % LANES + me, 1.0, 0.0).astype(bf16)
     shards = {key: where_ref[table[("shard",) + key]] for key in keys}
     slots = {key: where_ref[table[("slot",) + key]] for key in keys}
-
-    @pl.when(step == 0)
-    def _():
-        sums_ref[...] = before_ref[...] if summed else jnp.zeros(sums_ref.shape, f32)
+    sums_ref[...] = before_ref[...] if summed else jnp.zeros(sums_ref.shape, f32)
 
     def whole_weight(key):
         got = weight_refs[key]
         return got[0][...] if len(got) == 1 else jnp.concatenate([got[1][...], got[0][...]], axis=1)
 
-    def work(near):
+    def work():
         stack, here_valid, here_slot = [], [], []
         for choice in choices:
             weight, valid, slot = whole_weight(choice[0]), shards[choice[0]] >= 0, slots[choice[0]]
@@ -487,78 +478,71 @@
             here_valid.append(valid)
             here_slot.append(slot)
         weight = jnp.concatenate(stack, axis=0) if len(stack) > 1 else stack[0]
-        both = jnp.concatenate(
-            [jnp.concatenate([early[k][0], late[k][0][:, : model - cut]], axis=1) for k in range(2)],
-            axis=0,
-        )
-        product = dot(weight, both, NT)
-        lanes = pair_lanes(step, steps, me, tokens)
-        out_ref = mine_ref if near else theirs_ref
-        for half in range(2):
-            block = product[:, half * tokens : (half + 1) * tokens]
-            gate = dot(onehot, late[half][0][:, start:], NT)[0:1]
-            here = pl.ds(pl.multiple_of(lanes + half_of(me, tokens, half), tokens), tokens)
-            offset = 0 if near else slots_all
-            wide = pl.ds(pl.multiple_of(offset + lanes + half_of(me, tokens, half), tokens), tokens)
-            gated = (block * gate).astype(bf16)
-            total = jnp.zeros((1, tokens), f32)
-            for index, (valid, slot) in enumerate(zip(here_valid, here_slot)):
-                some = slice(index * units, (index + 1) * units)
-                out_ref[index, :, here] = gated[some]
-                if near:
-                    hidden = own_ref[slot, :, here].astype(f32)
-                else:
-                    hidden = jnp.where(
-                        slot == 0,
-                        first_ref[0, :, here].astype(f32),
-                        rest_ref[jnp.maximum(slot - 1, 0), :, here].astype(f32),
-                    )
-                part = jnp.sum(hidden * block[some], axis=0, keepdims=True)
-                total = total + jnp.where(valid, part, 0.0)
-            sums_ref[0:1, wide] += total
-
-    some = functools.reduce(jnp.logical_or, [shards[key] >= 0 for key in keys]) if guard else True
-    pl.when(jnp.logical_and(some, step < steps // 2))(functools.partial(work, True))
-    pl.when(jnp.logical_and(some, step >= steps // 2))(functools.partial(work, False))
+        for pair in range(0, number, 2):
+            both = jnp.concatenate(
+                [
+                    jnp.concatenate([early[k][...], late[k][:, : model - cut]], axis=1)
+                    for k in (pair, pair + 1)
+                ],
+                axis=0,
+            )
+            product = dot(weight, both, NT)
+            for place in (pair, pair + 1):
+                near = place < number // 2
+                block = product[:, (place - pair) * tokens : (place - pair + 1) * tokens]
+                gate = dot(onehot, late[place][:, start:], NT)[0:1]
+                here = pl.ds(place_of(place % (number // 2), number // 2, me, tokens), tokens)
+                wide = pl.ds(place_of(place, number // 2, me, tokens), tokens)
+                gated = (block * gate).astype(bf16)
+                total = jnp.zeros((1, tokens), f32)
+                for index, (valid, slot) in enumerate(zip(here_valid, here_slot)):
+                    some = slice(index * units, (index + 1) * units)
+                    outs[2 * index + (0 if near else 1)][:, here] = gated[some]
+                    if near:
+                        hidden = own_ref[slot, :, here].astype(f32)
+                    else:
+                        hidden = jnp.where(
+                            slot == 0,
+                            first_ref[0, :, here].astype(f32),
+                            rest_ref[jnp.maximum(slot - 1, 0), :, here].astype(f32),
+                        )
+                    part = jnp.sum(hidden * block[some], axis=0, keepdims=True)
+                    total = total + jnp.where(valid, part, 0.0)
+                sums_ref[0:1, wide] += total
+
+    if guard:
+        pl.when(functools.reduce(jnp.logical_or, [shards[key] >= 0 for key in keys]))(work)
+    else:
+        work()
 
 
 def back_part(table, where, late, early, own, first, rest, choices, got, before, guard, after, model):
     units, slots = own.shape[1:]
-    number, tokens, width = late[0].shape
-    cut = early[0].shape[2]
+    arrays, places = zip(late, early)
+    counts = [len(part) for part in arrays]
+    cut = arrays[1][0].shape[-1]
     keys = [key for choice in choices for key in choice]
     weights = [got[key] for key in keys]
     flat = [part for weight in weights for part in weight]
-    half = jax.ShapeDtypeStruct((len(choices), units, slots), bf16)
+    half = jax.ShapeDtypeStruct((units, slots), bf16)
     summed = before is not None
-    fixed = [own, first, rest, *flat] + ([before] if summed else [])
-    sums = jax.ShapeDtypeStruct((8, 2 * slots), f32)
-
-    def still(shape):
-        zeros = (0,) * len(shape)
-        return pl.BlockSpec(shape, lambda j, s: zeros)
-
+    operands = [*arrays[0], *arrays[1], own, first, rest, *flat] + ([before] if summed else [])
+    outs = [half] * (2 * len(choices)) + [jax.ShapeDtypeStruct((8, 2 * slots), f32)]
+    parts = [len(weight) for weight in weights]
     return pl.pallas_call(
         functools.partial(
-            back_kernel, table, model, cut, choices, [len(weight) for weight in weights], guard, summed
+            back_kernel, table, model, cut, counts, places, choices, parts, guard, summed
         ),
-        out_shape=(half, half, sums),
-        grid_spec=pltpu.PrefetchScalarGridSpec(
-            num_scalar_prefetch=1,
-            grid=(number,),
-            in_specs=[pl.BlockSpec((1, tokens, width), lambda j, s: (j, 0, 0))] * 2
-            + [pl.BlockSpec((1, tokens, cut), lambda j, s: (j, 0, 0))] * 2
-            + [still(value.shape) for value in fixed]
-            + [anywhere()] * len(after),
-            out_specs=(still(half.shape), still(half.shape), still(sums.shape)),
-        ),
+        out_shape=outs,
+        in_specs=[scalars()] + [whole()] * len(operands) + [anywhere()] * len(after),
+        out_specs=[whole()] * len(outs),
         compiler_params=params(),
         cost_estimate=taking(6),
         name="back_part",
-    )(where, *late, *early, *fixed, *after)
-
-
-def join_kernel(table, groups, where_ref, *refs):
+    )(where, *operands, *after)
+
+
+def join_kernel(table, choices, where_ref, *refs):
     out_ref, turned, sem = refs[-3:]
     slots, width = turned.shape[1:]
     row = lax.broadcasted_iota(jnp.int32, (slots, slots), 0)
@@ -566,46 +550,38 @@
     unit = jnp.where(row == column, 1.0, 0.0).astype(bf16)
     low = where_ref[table["x"]] == 0
     copies = []
-    total = 0
-    for number, choices in enumerate(groups):
-        mine_ref, theirs_ref = refs[2 * number], refs[2 * number + 1]
-        for place, choice in enumerate(choices):
-            index = where_ref[table[("shard",) + choice[0]]]
-            for key in choice[1:]:
-                index = jnp.where(index >= 0, index, where_ref[table[("shard",) + key]])
-            mine, theirs = mine_ref[place], theirs_ref[place]
-            both = jnp.concatenate(
-                [jnp.where(low, mine, theirs), jnp.where(low, theirs, mine)], axis=0
-            )
-            turned[total] = dot(unit, both, NT).astype(bf16)
-            here = pl.ds(pl.multiple_of(jnp.maximum(index, 0) * width, LANES), width)
-            copy = pltpu.make_async_copy(turned.at[total], out_ref.at[:, here], sem.at[total])
-            copies.append((index, copy))
-            pl.when(index >= 0)(copy.start)
-            total += 1
+    for place, choice in enumerate(choices):
+        mine, theirs = refs[2 * place][...], refs[2 * place + 1][...]
+        index = where_ref[table[("shard",) + choice[0]]]
+        for key in choice[1:]:
+            index = jnp.where(index >= 0, index, where_ref[table[("shard",) + key]])
+        both = jnp.concatenate([jnp.where(low, mine, theirs), jnp.where(low, theirs, mine)], axis=0)
+        turned[place] = dot(unit, both, NT).astype(bf16)
+        here = pl.ds(pl.multiple_of(jnp.maximum(index, 0) * width, LANES), width)
+        copy = pltpu.make_async_copy(turned.at[place], out_ref.at[:, here], sem.at[place])
+        copies.append((index, copy))
+        pl.when(index >= 0)(copy.start)
     for index, copy in copies:
         pl.when(index >= 0)(copy.wait)
 
 
-def join_hidden(table, where, groups, pairs, slots, hidden, before, after):
-    flat = [array for pair in pairs for array in pair]
-    units = flat[0].shape[1]
-    total = sum(len(choices) for choices in groups)
+def join_hidden(table, where, choices, halves, slots, hidden, before, after):
+    units = halves[0].shape[0]
     extends = before is not None
     return pl.pallas_call(
-        functools.partial(join_kernel, table, groups),
+        functools.partial(join_kernel, table, choices),
         out_shape=jax.ShapeDtypeStruct((slots, hidden), bf16),
-        in_specs=[scalars()] + [whole()] * len(flat) + [anywhere()] * (extends + len(after)),
+        in_specs=[scalars()] + [whole()] * len(halves) + [anywhere()] * (extends + len(after)),
         out_specs=anywhere(),
         scratch_shapes=[
-            pltpu.VMEM((total, slots, 2 * units), bf16),
-            pltpu.SemaphoreType.DMA((total,)),
+            pltpu.VMEM((len(choices), slots, 2 * units), bf16),
+            pltpu.SemaphoreType.DMA((len(choices),)),
         ],
-        input_output_aliases={1 + len(flat): 0} if extends else {},
+        input_output_aliases={1 + len(halves): 0} if extends else {},
         compiler_params=params(),
         cost_estimate=taking(2),
         name="join_hidden",
-    )(where, *flat, *([before] if extends else []), *after)
+    )(where, *halves, *([before] if extends else []), *after)
 
 
 def logits_kernel(gates_ref, ids_ref, grads_ref, out_ref):
@@ -662,99 +638,92 @@
 
     late, early, gates = make_rows(grad_out, top_logits, expert_ids, width, cut)
     highs = list(range(2, experts, 2))
-    late_near = [late] + [swap(late, 0, high) for high in highs]
+
+    def sides(mine):
+        return [mine, swap(mine, 0, 1)]
+
     late_x = swap(late, 1, 0)
-    late_far = [late_x] + [swap(late_x, 0, high) for high in highs]
+    late_mine = [late] + [swap(late, 0, high) for high in highs]
+    late_mine += [late_x] + [swap(late_x, 0, high) for high in highs]
+    (early,) = hold((early,), [late_x])
     own, other_first, other_rest = split_hidden(
-        table, where, saved_hidden[0, 0], depth, w_down.shape[1], [late]
+        table, where, saved_hidden[0, 0], depth, w_down.shape[1], [early]
     )
     other_first = swap(other_first, 1, 0)
-    late_rows = pack(late_near + late_far, [other_first, got[1, "A"][0], got[1, "B"][0]])
-    late_rows = (late_rows, swap(late_rows, 0, 1))
-
-    (early,) = hold((early,), [late_rows[0]])
     early_x = swap(early, 1, 0)
-    early_near = [early] + [swap(early, 0, high) for high in highs]
-    early_x, other_rest = hold((early_x, other_rest), [])
-    early_far = [early_x] + [swap(early_x, 0, high) for high in highs]
+    late_rows = sides(pack(late_mine, [other_first, got[1, "A"][0], got[1, "B"][0], early_x]))
+    late_rows = (late_rows, [(side, place) for place in range(experts) for side in range(2)])
+    early_rows = sides(pack([early, early_x], []))
+    places = [(0, 0), (1, 0)]
+    for block, base in ((early, 0), (early_x, 1)):
+        if base:
+            places += [(0, 1), (1, 1)]
+        for high in highs:
+            places += [(len(early_rows), None), (len(early_rows) + 1, None)]
+            early_rows += sides(swap(block, 0, high))
+    early_rows = (early_rows, places)
     other_rest = swap(other_rest, 1, 0)
+
+    first = [products(table, where, late_rows, late_rows, own, other_first, 0, model, model - cut, "first_late", [])]
+    sent = [begin(table, where, got[1, "B"][0], first[0], cut, [early_rows[0][1]])]
+    got[2, "A"] = [swap_z(sent[0], "A")]
     got[2, "B"] = [swap_z(got[1, "A"][0], "B")]
-
-    first = [
-        products(table, where, late_rows, late_rows, own, other_first, 0, model, cut, "first_late", [])
-    ]
-    sent = [begin(table, where, got[1, "B"][0], first[0], cut, [])]
-    got[2, "A"] = [swap_z(sent[0], "A")]
-    early_rows = pack(early_near + early_far, [sent[0]])
-    early_rows = (early_rows, swap(early_rows, 0, 1))
     first.append(
-        products(table, where, early_rows, late_rows, own, other_first, 0, model, 0, "first_early", [other_rest])
+        products(table, where, early_rows, late_rows, own, other_first, 0, model, cut, "first_early", [other_rest])
     )
     sent.append(begin(table, where, got[1, "B"][0], first[1], 0, [got[2, "A"][0]]))
     got[2, "A"].append(swap_z(sent[1], "A"))
 
-    rest = []
-    for rows, start, name in ((late_rows, cut, "rest_late"), (early_rows, 0, "rest_early")):
-        rest.append(
-            products(table, where, rows, late_rows, own, other_rest, 1, model, start, name, [sent[1]])
-        )
-
-    pairs, groups_of = [], []
+    halves, all_choices = [], []
+    only_first = max(uses[3, "B"]) <= 0
 
     def backprop(choices, before, guard, after):
-        mine, theirs, sums = back_part(
+        *outs, sums = back_part(
             table, where, late_rows, early_rows, own, other_first, other_rest, choices, got, before, guard, after, model
         )
-        pairs.append((mine, swap(theirs, 1, 0)))
-        groups_of.append(choices)
+        for mine, theirs in zip(outs[::2], outs[1::2]):
+            halves.extend([mine, swap(theirs, 1, 0)])
+        all_choices.extend(choices)
         return sums
 
-    def pass_on(turn, name, after):
-        back = "B" if name == "A" else "A"
-        used = uses[turn, name]
-        coming = got[turn - 1, back]
-        if turn == 3 and name == "B":
-            values = []
-            for k in range(2):
-                value = combine(table, where, [coming[k]], [first[k]], [rest[k]], turn, name, used, 0, after)
-                values.append(value)
-                after = [value]
-        else:
-            values = [combine(table, where, coming, first, rest, turn, name, used, cut, after)]
-        got[turn, name] = [swap_z(value, name) for value in values]
+    def pass_on(turn, name, after, chunk=None):
+        coming = got[turn - 1, "B" if name == "A" else "A"]
+        parts, start, chunked = (first, rest), cut, turn == depth and name == "B"
+        if chunk is not None:
+            coming, parts, start = [coming[chunk]], (first[chunk:][:1], rest[chunk:][:1]), 0
+        values = combine(table, where, coming, *parts, turn, name, uses[turn, name], start, after, chunked)
+        got.setdefault((turn, name), []).extend(swap_z(value, name) for value in values)
         return values[-1]
 
     def choices_of(turn):
         both = any(b[turn, "A"] >= 0 and b[turn, "B"] >= 0 for b in brought)
         return [[(turn, "A")], [(turn, "B")]] if both else [[(turn, "A"), (turn, "B")]]
 
-    marker = pass_on(3, "A", [*rest, got[2, "A"][0]])
-    marker = pass_on(3, "B", [marker])
+    rest = []
+    marker = pass_on(3, "B", [sent[1]], 0) if only_first else sent[1]
+    for rows, columns, name in ((late_rows, model - cut, "rest_late"), (early_rows, cut, "rest_early")):
+        rest.append(
+            products(table, where, rows, late_rows, own, other_rest, 1, model, columns, name, [marker])
+        )
+    marker = pass_on(3, "A", rest)
+    for chunk in range(2)[only_first:]:
+        marker = pass_on(3, "B", [marker], chunk)
     sums = backprop([[(0, "own")], [(1, "A")], [(1, "B")]], None, False, [marker])
-    marker = sums
-    hidden_grad = None
+    early_halves = halves[1::2]
     for turn in range(2, depth):
         choices = choices_of(turn)
         if turn > 2:
-            marker = pass_on(turn + 1, "A", [marker])
-            marker = pass_on(turn + 1, "B", [marker])
+            pass_on(turn + 1, "B", [sums, *early_halves])
+            marker = pass_on(turn + 1, "A", [sums, *early_halves])
         sums = backprop(choices, sums, len(choices) == 1, [marker])
-        marker = sums
-        if turn == 2:
-            hidden_grad = join_hidden(
-                table, where, groups_of[:1], pairs[:1], slots, hidden, None, [marker]
-            )
-            marker = hidden_grad
     slot_grad = sums[0:1, :slots] + swap(sums[0:1, slots:], 1, 0)
     grads = lax.all_to_all(
         slot_grad.reshape(experts, tokens), "exp", split_axis=0, concat_axis=0, tiled=True
     )
-    logit_grad = logits_grad(gates, expert_ids.T, grads).T
-    hidden_grad = join_hidden(
-        table, where, groups_of[1:], pairs[1:], slots, hidden, hidden_grad, [logit_grad]
-    )
-    weight_grad = total_grad(got[depth, "A"][0], got[depth, "B"][0], rest, cut)
-    return (logit_grad, hidden_grad[None, None], weight_grad)
+    logit_grad = logits_grad(gates, expert_ids.T, grads)
+    hidden_grad = join_hidden(table, where, all_choices, halves, slots, hidden, None, [])
+    weight_grad = total_grad(got[depth, "A"], got[depth, "B"], rest, cut)
+    return (logit_grad.T, hidden_grad[None, None], weight_grad)
 
 
 def routing_tables(expert_ids, count_experts, capacity):

time: 165 us -> 127 us (0.77)
  Pallas kernels: 53 us -> 36.6 us
  starting transfers between devices: 48.1 us -> 36.6 us
  local copies, waits for them, and re-layouts: 12.4 us -> 4.59 us
  waiting for transfers between devices: 43 us -> 40.3 us
    pallas_call x10 -> x9, Pallas kernels: 40.8 us -> 25.4 us  [the longest x4 11 us: products(): pl.pallas_call(functools.partial(products_kernel, table, model, counts, p...]
    ppermute x8 -> x10, waiting for transfers between devices: 38.3 us -> 23 us  [swap(): return lax.ppermute(value, 'ctx', [(i, i ^ x) for i in range(groups)])]
    ppermute x10 -> x11, starting transfers between devices: 31.6 us -> 18.8 us  [swap_z(): return lax.ppermute(value, 'ctx', pairs)]
    unnamed x33 -> x12, local copies, waits for them, and re-layouts: 11 us -> 3.9 us
    ppermute x10 -> x11, waiting for transfers between devices: 0.27 us -> 6.95 us  [swap_z(): return lax.ppermute(value, 'ctx', pairs)]
    ppermute x6 -> x8, waiting for transfers between devices: 4.41 us -> 10.4 us  [swap(): return lax.ppermute(value, 'exp', [(i, i ^ exp) for i in range(experts)])]
    pallas_call x5, Pallas kernels: 6.83 us -> 3.94 us  [combine(): pl.pallas_call(functools.partial(combine_kernel, table, ('use', turn, nam...]
    ppermute x8 -> x10, starting transfers between devices: 10.4 us -> 12.1 us  [swap(): return lax.ppermute(value, 'ctx', [(i, i ^ x) for i in range(groups)])]
  transfers between devices with their start and end apart: 24 -> 29, of which waited for: 8 -> 12; matrix products, arithmetic and copies ran while one was open for 2% -> 1% of each run, Pallas kernels for 29% -> 27%
where the time goes in v4:
time: 127 us; the launch traced here: 125 us
  waiting for transfers between devices  40.3 us (32%)
  starting transfers between devices  36.6 us (29%)
  Pallas kernels  36.6 us (29%)
  blocking collectives  6.08 us (5%)
  local copies, waits for them, and re-layouts  4.59 us (4%)
    ppermute x10, waiting for transfers between devices, swap(): return lax.ppermute(value, 'ctx', [(i, i ^ x) for i in range(groups)])  23 us
    ppermute x11, starting transfers between devices, swap_z(): return lax.ppermute(value, 'ctx', pairs)  18.8 us
    ppermute x10, starting transfers between devices, swap(): return lax.ppermute(value, 'ctx', [(i, i ^ x) for i in range(groups)])  12.1 us
    pallas_call x4, Pallas kernels, products(): pl.pallas_call(functools.partial(products_kernel, table, model, counts, p...  11 us
    ppermute x8, waiting for transfers between devices, swap(): return lax.ppermute(value, 'exp', [(i, i ^ exp) for i in range(experts)])  10.4 us
    pallas_call x3, Pallas kernels, back_part(): pl.pallas_call(functools.partial(back_kernel, table, model, cut, counts,...  9.97 us
    ppermute x11, waiting for transfers between devices, swap_z(): return lax.ppermute(value, 'ctx', pairs)  6.95 us
    all_to_all x1, blocking collectives, per_device_full(): lax.all_to_all(slot_grad.reshape(experts, tokens), 'exp', split_axis=0, c...  6.08 us
  transfers between devices with their start and end apart: 29, of which 12 were waited for; matrix products, arithmetic and copies ran while one was open for 1% of the time, Pallas kernels for 27%

profile of v4, /device:TPU:0, one launch (start us, length us, event | category | flops | bytes accessed | tf_op | source)
XLA Modules:
  0.0 125.2 jit_solution(14754930219052672449)
XLA Ops:
  1.4 5.8 %collective-permute-start.4 = (bf16[192,2880]{1,0:T(8,128)(2,1)}, bf16[192,2880]{1,0:T(8,128)(2,1)S(1)}, u32[]{:S(2)}, u32[]{:S(2)}) collective-permute-start(bf16[192,2880]{1,0:T(8,128)(2,1)} %bitcast.16), channel_id=1, source_target_pairs={{0,8},{8,0},{4,12},{12,4},{16,24},{24,16},{20,28},{28,20},{1,9},{9... | collective-permute-start | bytes 3317768 | tf_op jit(solution)/shard_map/ppermute | solution.py:633
  14.1 7.5 %collective-permute-done.1.refs_1_.refs_2_ = bf16[128,1536]{1,0:T(8,128)(2,1)S(1)} collective-permute-done((bf16[128,1536]{1,0:T(8,128)(2,1)}, bf16[128,1536]{1,0:T(8,128)(2,1)S(1)}, u32[]{:S(2)}, u32[]{:S(2)}) %collective-permute-start.1) | collective-permute-done | bytes 393248 | tf_op jit(solution)/shard_map/ppermute | solution.py:621
  26.7 2.2 %split_hidden.1 = (bf16[4,192,512]{2,1,0:T(8,128)(2,1)S(1)}, bf16[1,192,512]{2,1,0:T(8,128)(2,1)S(1)}, bf16[3,192,512]{2,1,0:T(8,128)(2,1)S(1)}) custom-call(s32[32]{0:T(128)S(1)} %dynamic-slice_bitcast_fusion.where_ref, bf16[512,1536]{1,0:T(8,128)(2,1)S(1)} %bitcast.14, bf16[128,1408]{1,0:T(8,128)(2,1)S(1)} %hold.1.refs_0_), custom_call_target="tpu_custom_call" | custom-call | flops 2000000 | bytes 6000000 | tf_op jit(solution)/shard_map/split_hidden/pallas_call | solution.py:250
  29.6 6.3 %collective-permute-done.3.refs_4_.refs_5_.refs_9_ = bf16[1,192,512]{2,1,0:T(8,128)(2,1)S(1)} collective-permute-done((bf16[1,192,512]{2,1,0:T(8,128)(2,1)S(1)}, bf16[1,192,512]{2,1,0:T(8,128)(2,1)S(1)}, u32[]{:S(2)}, u32[]{:S(2)}) %collective-permute-start.3) | collective-permute-done | bytes 196640 | tf_op jit(solution)/shard_map/ppermute | solution.py:621
  42.4 2.2 %first_late.1.kept_ref.refs_1_ = f32[1,192,1472]{2,1,0:T(8,128)S(1)} custom-call(s32[32]{0:T(128)S(1)} %dynamic-slice_bitcast_fusion.where_ref, bf16[4,128,1536]{2,1,0:T(8,128)(2,1)S(1)} %pack_rows.2.refs_0_.refs_2_.refs_6_, bf16[4,128,1536]{2,1,0:T(8,128)(2,1)S(1)} %collective-permute-done.7.refs_1_.refs_3_.refs_7_, ...), custom_call_target="tpu_custom_call" | custom-call | flops 4000000 | bytes 12000000 | tf_op jit(solution)/shard_map/first_late/pallas_call | solution.py:303
  45.4 2.3 %collective-permute-start.15 = (bf16[192,1472]{1,0:T(8,128)(2,1)S(1)}, bf16[192,1472]{1,0:T(8,128)(2,1)S(1)}, u32[]{:S(2)}, u32[]{:S(2)}) collective-permute-start(bf16[192,1472]{1,0:T(8,128)(2,1)S(1)} %begin.2), channel_id=1, source_target_pairs={{0,8},{8,0},{4,12},{12,4},{16,24},{24,16},{20,28},{28,20},{1,9},{9... | collective-permute-start | bytes 1695752 | tf_op jit(solution)/shard_map/ppermute | solution.py:633
  47.6 1.8 %collective-permute-done.9.refs_2_.refs_4_ = bf16[128,1408]{1,0:T(8,128)(2,1)S(1)} collective-permute-done((bf16[128,1408]{1,0:T(8,128)(2,1)S(1)}, bf16[128,1408]{1,0:T(8,128)(2,1)S(1)}, u32[]{:S(2)}, u32[]{:S(2)}) %collective-permute-start.9) | collective-permute-done | bytes 360480 | tf_op jit(solution)/shard_map/ppermute | solution.py:623
  49.4 6.8 %collective-permute-done.11.refs_4_.refs_6_ = bf16[128,1408]{1,0:T(8,128)(2,1)S(1)} collective-permute-done((bf16[128,1408]{1,0:T(8,128)(2,1)S(1)}, bf16[128,1408]{1,0:T(8,128)(2,1)S(1)}, u32[]{:S(2)}, u32[]{:S(2)}) %collective-permute-start.11) | collective-permute-done | bytes 360480 | tf_op jit(solution)/shard_map/ppermute | solution.py:623
  56.3 1.7 %collective-permute-done.12.refs_5_.refs_7_ = bf16[128,1408]{1,0:T(8,128)(2,1)S(1)} collective-permute-done((bf16[128,1408]{1,0:T(8,128)(2,1)S(1)}, bf16[128,1408]{1,0:T(8,128)(2,1)S(1)}, u32[]{:S(2)}, u32[]{:S(2)}) %collective-permute-start.12) | collective-permute-done | bytes 360480 | tf_op jit(solution)/shard_map/ppermute | solution.py:623
  58.0 2.1 %first_early.1.kept_ref.refs_1_ = f32[1,192,1408]{2,1,0:T(8,128)S(1)} custom-call(s32[32]{0:T(128)S(1)} %dynamic-slice_bitcast_fusion.where_ref, bf16[2,128,1408]{2,1,0:T(8,128)(2,1)S(1)} %pack_rows.3.refs_0_.refs_2_, bf16[2,128,1408]{2,1,0:T(8,128)(2,1)S(1)} %collective-permute-done.8.refs_0_.refs_1_.refs_3_, ...), custom_call_target="tpu_custom_call" | custom-call | flops 4000000 | bytes 12000000 | tf_op jit(solution)/shard_map/first_early/pallas_call | solution.py:303
  60.8 1.7 %collective-permute-start.18 = (bf16[192,1408]{1,0:T(8,128)(2,1)S(1)}, bf16[192,1408]{1,0:T(8,128)(2,1)S(1)}, u32[]{:S(2)}, u32[]{:S(2)}) collective-permute-start(bf16[192,1408]{1,0:T(8,128)(2,1)S(1)} %begin.3.refs_2_), channel_id=1, source_target_pairs={{0,8},{8,0},{4,12},{12,4},{16,24},{24,16},{20,28},{28,20},{1,9},{9... | collective-permute-start | bytes 1622024 | tf_op jit(solution)/shard_map/ppermute | solution.py:633
  64.0 3.4 %rest_early.1.refs_2_.refs_4_.refs_3_ = f32[3,192,1408]{2,1,0:T(8,128)S(1)} custom-call(s32[32]{0:T(128)S(1)} %dynamic-slice_bitcast_fusion.where_ref, bf16[2,128,1408]{2,1,0:T(8,128)(2,1)S(1)} %pack_rows.3.refs_0_.refs_2_, bf16[2,128,1408]{2,1,0:T(8,128)(2,1)S(1)} %collective-permute-done.8.refs_0_.refs_1_.refs_3_, ...), custom_call_target="tpu_custom_call" | custom-call | flops 4000000 | bytes 12000000 | tf_op jit(solution)/shard_map/rest_early/pallas_call | solution.py:303
  67.4 3.4 %rest_late.1.refs_1_.refs_3_.refs_2_ = f32[3,192,1472]{2,1,0:T(8,128)S(1)} custom-call(s32[32]{0:T(128)S(1)} %dynamic-slice_bitcast_fusion.where_ref, bf16[4,128,1536]{2,1,0:T(8,128)(2,1)S(1)} %pack_rows.2.refs_0_.refs_2_.refs_6_, bf16[4,128,1536]{2,1,0:T(8,128)(2,1)S(1)} %collective-permute-done.7.refs_1_.refs_3_.refs_7_, ...), custom_call_target="tpu_custom_call" | custom-call | flops 4000000 | bytes 12000000 | tf_op jit(solution)/shard_map/rest_late/pallas_call | solution.py:303
  71.7 3.1 %collective-permute-start.16 = (bf16[192,2880]{1,0:T(8,128)(2,1)S(1)}, bf16[192,2880]{1,0:T(8,128)(2,1)S(1)}, u32[]{:S(2)}, u32[]{:S(2)}) collective-permute-start(bf16[192,2880]{1,0:T(8,128)(2,1)S(1)} %combine.6.refs_2_), channel_id=1, source_target_pairs={{0,8},{8,0},{4,12},{12,4},{16,24},{24,16},{20,28},{28,20},{1,9},{9... | collective-permute-start | bytes 3317768 | tf_op jit(solution)/shard_map/ppermute | solution.py:633
  77.6 4.7 %back_part.3 = (bf16[192,512]{1,0:T(8,128)(2,1)S(1)}, bf16[192,512]{1,0:T(8,128)(2,1)S(1)}, bf16[192,512]{1,0:T(8,128)(2,1)S(1)}, bf16[192,512]{1,0:T(8,128)(2,1...) custom-call(s32[32]{0:T(128)S(1)} %dynamic-slice_bitcast_fusion.where_ref, ...), custom_call_target="tpu_custom_call" | custom-call | flops 6000000 | bytes 18000000 | tf_op jit(solution)/shard_map/back_part/pallas_call | solution.py:532
  85.9 2.6 %back_part.4 = (bf16[192,512]{1,0:T(8,128)(2,1)S(1)}, bf16[192,512]{1,0:T(8,128)(2,1)S(1)}, f32[8,1024]{1,0:T(8,128)S(1)}) custom-call(s32[32]{0:T(128)S(1)} %dynamic-slice_bitcast_fusion.where_ref, bf16[4,128,1536]{2,1,0:T(8,128)(2,1)S(1)} %pack_rows.2.refs_0_.refs_2_.refs_6_, bf16[4,128,1536]{2,1,0:T(8,128)(2,1)S(1)} %collective-permute-done.7.refs_1_.refs_3_.refs_7_, ...), custom_call_target="tpu_custom_call" | custom-call | flops 6000000 | bytes 18000000 | tf_op jit(solution)/shard_map/back_part/pallas_call | solution.py:532
  88.5 1.7 %collective-permute-done.20.refs_5_.refs_1_.refs_4_ = bf16[192,512]{1,0:T(8,128)(2,1)S(1)} collective-permute-done((bf16[192,512]{1,0:T(8,128)(2,1)S(1)}, bf16[192,512]{1,0:T(8,128)(2,1)S(1)}, u32[]{:S(2)}, u32[]{:S(2)}) %collective-permute-start.20) | collective-permute-done | bytes 196640 | tf_op jit(solution)/shard_map/ppermute | solution.py:621
  90.2 3.8 %collective-permute-done.21.refs_6_.refs_3_.refs_5_ = bf16[192,512]{1,0:T(8,128)(2,1)S(1)} collective-permute-done((bf16[192,512]{1,0:T(8,128)(2,1)S(1)}, bf16[192,512]{1,0:T(8,128)(2,1)S(1)}, u32[]{:S(2)}, u32[]{:S(2)}) %collective-permute-start.21) | collective-permute-done | bytes 196640 | tf_op jit(solution)/shard_map/ppermute | solution.py:621
  94.0 2.1 %collective-permute-done.22.refs_7_.refs_5_.refs_6_ = bf16[192,512]{1,0:T(8,128)(2,1)S(1)} collective-permute-done((bf16[192,512]{1,0:T(8,128)(2,1)S(1)}, bf16[192,512]{1,0:T(8,128)(2,1)S(1)}, u32[]{:S(2)}, u32[]{:S(2)}) %collective-permute-start.22) | collective-permute-done | bytes 196640 | tf_op jit(solution)/shard_map/ppermute | solution.py:621
  98.4 2.2 %collective-permute-done.16.refs_11_.refs_0_ = bf16[192,2880]{1,0:T(8,128)(2,1)S(1)} collective-permute-done((bf16[192,2880]{1,0:T(8,128)(2,1)S(1)}, bf16[192,2880]{1,0:T(8,128)(2,1)S(1)}, u32[]{:S(2)}, u32[]{:S(2)}) %collective-permute-start.16) | collective-permute-done | bytes 1105952 | tf_op jit(solution)/shard_map/ppermute | solution.py:633
  102.9 2.7 %back_part.5 = (bf16[192,512]{1,0:T(8,128)(2,1)S(1)}, bf16[192,512]{1,0:T(8,128)(2,1)S(1)}, f32[8,1024]{1,0:T(8,128)S(1)}) custom-call(s32[32]{0:T(128)S(1)} %dynamic-slice_bitcast_fusion.where_ref, bf16[4,128,1536]{2,1,0:T(8,128)(2,1)S(1)} %pack_rows.2.refs_0_.refs_2_.refs_6_, bf16[4,128,1536]{2,1,0:T(8,128)(2,1)S(1)} %collective-permute-done.7.refs_1_.refs_3_.refs_7_, ...), custom_call_target="tpu_custom_call" | custom-call | flops 6000000 | bytes 18000000 | tf_op jit(solution)/shard_map/back_part/pallas_call | solution.py:532
  110.6 6.1 %all_to_all.11 = f32[4,1,128]{2,1,0:T(1,128)S(1)} all-to-all(f32[4,1,128]{2,1,0:T(1,128)S(1)} %add_bitcast_fusion), channel_id=1, replica_groups=mesh['ctx'=8,'exp'=4] {'exp'}, dimensions={0} | all-to-all | bytes 4096 | tf_op jit(solution)/shard_map/all_to_all | solution.py:720
  117.3 2.9 %join_hidden.1 = bf16[512,1536]{1,0:T(8,128)(2,1)} custom-call(s32[32]{0:T(128)S(1)} %dynamic-slice_bitcast_fusion.where_ref, bf16[192,512]{1,0:T(8,128)(2,1)S(1)} %get-tuple-element.36.refs_0_, bf16[192,512]{1,0:T(8,128)(2,1)S(1)} %collective-permute-done.20.refs_5_.refs_1_.refs_4_, bf16[192,512]{1,0:T(8,128)(2,1)S(1)} %get-tuple-element.37.refs_2_, ...), custom_call_target="tpu_custom_call" | custom-call | flops 2000000 | bytes 6000000 | tf_op jit(solution)/shard_map/join_hidden/pallas_call | solution.py:571
  120.2 3.5 %collective-permute-done.26.refs_0_ = bf16[192,2880]{1,0:T(8,128)(2,1)S(1)} collective-permute-done((bf16[192,2880]{1,0:T(8,128)(2,1)S(1)}, bf16[192,2880]{1,0:T(8,128)(2,1)S(1)}, u32[]{:S(2)}, u32[]{:S(2)}) %collective-permute-start.26) | collective-permute-done | bytes 1105952 | tf_op jit(solution)/shard_map/ppermute | solution.py:633
  (72 shorter events, 41.7 us)
Async XLA Ops:
  0.6 35.2 %collective-permute-start.5 = (bf16[192,2880]{1,0:T(8,128)(2,1)}, bf16[192,2880]{1,0:T(8,128)(2,1)S(1)}, u32[]{:S(2)}, u32[]{:S(2)}) collective-permute-start(bf16[192,2880]{1,0:T(8,128)(2,1)} %bitcast.15), channel_id=1, source_target_pairs={{8,16},{16,8},{12,20},{20,12},{9,17},{17,9},{13,21},{21,13},{10,18... | collective-permute-start | bytes 3317768 | tf_op jit(solution)/shard_map/ppermute | solution.py:633
  1.4 34.5 %collective-permute-start.4 = (bf16[192,2880]{1,0:T(8,128)(2,1)}, bf16[192,2880]{1,0:T(8,128)(2,1)S(1)}, u32[]{:S(2)}, u32[]{:S(2)}) collective-permute-start(bf16[192,2880]{1,0:T(8,128)(2,1)} %bitcast.16), channel_id=1, source_target_pairs={{0,8},{8,0},{4,12},{12,4},{16,24},{24,16},{20,28},{28,20},{1,9},{9... | collective-permute-start | bytes 3317768 | tf_op jit(solution)/shard_map/ppermute | solution.py:633
  11.1 10.6 %collective-permute-start.1 = (bf16[128,1536]{1,0:T(8,128)(2,1)}, bf16[128,1536]{1,0:T(8,128)(2,1)S(1)}, u32[]{:S(2)}, u32[]{:S(2)}) collective-permute-start(bf16[128,1536]{1,0:T(8,128)(2,1)} %get-tuple-element.25.refs_0_), channel_id=1, source_target_pairs={{0,4},{4,0},{8,12},{12,8},{16,20},{20,16},{24,28},{28,24},{1,5},{5... | collective-permute-start | bytes 1179656 | tf_op jit(solution)/shard_map/ppermute | solution.py:621
  12.6 16.3 %collective-permute-start = (bf16[128,1536]{1,0:T(8,128)(2,1)}, bf16[128,1536]{1,0:T(8,128)(2,1)}, u32[]{:S(2)}, u32[]{:S(2)}) collective-permute-start(bf16[128,1536]{1,0:T(8,128)(2,1)} %get-tuple-element.25.refs_0_), channel_id=1, source_target_pairs={{0,2},{1,3},{2,0},{3,1},{4,6},{5,7},{6,4},{7,5},{8,10},{9,11},{10,... | collective-permute-start | bytes 1179656 | tf_op jit(solution)/shard_map/ppermute | solution.py:623
  21.6 14.2 %collective-permute-start.2 = (bf16[128,1536]{1,0:T(8,128)(2,1)S(1)}, bf16[128,1536]{1,0:T(8,128)(2,1)}, u32[]{:S(2)}, u32[]{:S(2)}) collective-permute-start(bf16[128,1536]{1,0:T(8,128)(2,1)S(1)} %collective-permute-done.1.refs_1_.refs_2_), channel_id=1, source_target_pairs={{0,2},{1,3},{2,0},{3,1},{4,6},{5,7},{6,4},{7,5},{8,10},{9,11},{10,... | collective-permute-start | bytes 1179656 | tf_op jit(solution)/shard_map/ppermute | solution.py:623
  23.2 12.7 %collective-permute-start.6 = (bf16[128,1408]{1,0:T(8,128)(2,1)S(1)}, bf16[128,1408]{1,0:T(8,128)(2,1)S(1)}, u32[]{:S(2)}, u32[]{:S(2)}) collective-permute-start(bf16[128,1408]{1,0:T(8,128)(2,1)S(1)} %hold.1.refs_0_), channel_id=1, source_target_pairs={{0,4},{4,0},{8,12},{12,8},{16,20},{20,16},{24,28},{28,24},{1,5},{5... | collective-permute-start | bytes 1081352 | tf_op jit(solution)/shard_map/ppermute | solution.py:621
  37.6 7.0 %collective-permute-start.8 = (bf16[2,128,1408]{2,1,0:T(8,128)(2,1)S(1)}, bf16[2,128,1408]{2,1,0:T(8,128)(2,1)S(1)}, u32[]{:S(2)}, u32[]{:S(2)}) collective-permute-start(bf16[2,128,1408]{2,1,0:T(8,128)(2,1)S(1)} %pack_rows.3.refs_0_.refs_2_), channel_id=1, source_target_pairs={{0,1},{1,0},{2,3},{3,2},{4,5},{5,4},{6,7},{7,6},{8,9},{9,8},{10,11... | collective-permute-start | bytes 2162696 | tf_op jit(solution)/shard_map/ppermute | solution.py:623
  38.2 11.3 %collective-permute-start.9 = (bf16[128,1408]{1,0:T(8,128)(2,1)S(1)}, bf16[128,1408]{1,0:T(8,128)(2,1)S(1)}, u32[]{:S(2)}, u32[]{:S(2)}) collective-permute-start(bf16[128,1408]{1,0:T(8,128)(2,1)S(1)} %hold.1.refs_0_), channel_id=1, source_target_pairs={{0,2},{1,3},{2,0},{3,1},{4,6},{5,7},{6,4},{7,5},{8,10},{9,11},{10,... | collective-permute-start | bytes 1081352 | tf_op jit(solution)/shard_map/ppermute | solution.py:623
  38.7 17.6 %collective-permute-start.11 = (bf16[128,1408]{1,0:T(8,128)(2,1)S(1)}, bf16[128,1408]{1,0:T(8,128)(2,1)S(1)}, u32[]{:S(2)}, u32[]{:S(2)}) collective-permute-start(bf16[128,1408]{1,0:T(8,128)(2,1)S(1)} %collective-permute-done.6.refs_7_.refs_1_), channel_id=1, source_target_pairs={{0,2},{1,3},{2,0},{3,1},{4,6},{5,7},{6,4},{7,5},{8,10},{9,11},{10,... | collective-permute-start | bytes 1081352 | tf_op jit(solution)/shard_map/ppermute | solution.py:623
  40.2 16.1 %collective-permute-start.13 = (bf16[3,192,512]{2,1,0:T(8,128)(2,1)S(1)}, bf16[3,192,512]{2,1,0:T(8,128)(2,1)S(1)}, u32[]{:S(2)}, u32[]{:S(2)}) collective-permute-start(bf16[3,192,512]{2,1,0:T(8,128)(2,1)S(1)} %get-tuple-element.29), channel_id=1, source_target_pairs={{0,4},{4,0},{8,12},{12,8},{16,20},{20,16},{24,28},{28,24},{1,5},{5... | collective-permute-start | bytes 1769480 | tf_op jit(solution)/shard_map/ppermute | solution.py:621
  41.7 29.1 %collective-permute-start.14 = (bf16[192,2880]{1,0:T(8,128)(2,1)S(1)}, bf16[192,2880]{1,0:T(8,128)(2,1)S(1)}, u32[]{:S(2)}, u32[]{:S(2)}) collective-permute-start(bf16[192,2880]{1,0:T(8,128)(2,1)S(1)} %collective-permute-done.4.refs_5_.refs_12_), channel_id=1, source_target_pairs={{8,16},{16,8},{12,20},{20,12},{9,17},{17,9},{13,21},{21,13},{10,18... | collective-permute-start | bytes 3317768 | tf_op jit(solution)/shard_map/ppermute | solution.py:633
  45.4 14.8 %collective-permute-start.15 = (bf16[192,1472]{1,0:T(8,128)(2,1)S(1)}, bf16[192,1472]{1,0:T(8,128)(2,1)S(1)}, u32[]{:S(2)}, u32[]{:S(2)}) collective-permute-start(bf16[192,1472]{1,0:T(8,128)(2,1)S(1)} %begin.2), channel_id=1, source_target_pairs={{0,8},{8,0},{4,12},{12,4},{16,24},{24,16},{20,28},{28,20},{1,9},{9... | collective-permute-start | bytes 1695752 | tf_op jit(solution)/shard_map/ppermute | solution.py:633
  60.8 15.2 %collective-permute-start.18 = (bf16[192,1408]{1,0:T(8,128)(2,1)S(1)}, bf16[192,1408]{1,0:T(8,128)(2,1)S(1)}, u32[]{:S(2)}, u32[]{:S(2)}) collective-permute-start(bf16[192,1408]{1,0:T(8,128)(2,1)S(1)} %begin.3.refs_2_), channel_id=1, source_target_pairs={{0,8},{8,0},{4,12},{12,4},{16,24},{24,16},{20,28},{28,20},{1,9},{9... | collective-permute-start | bytes 1622024 | tf_op jit(solution)/shard_map/ppermute | solution.py:633
  63.3 21.1 %collective-permute-start.17 = (bf16[192,1472]{1,0:T(8,128)(2,1)S(1)}, bf16[192,1472]{1,0:T(8,128)(2,1)S(1)}, u32[]{:S(2)}, u32[]{:S(2)}) collective-permute-start(bf16[192,1472]{1,0:T(8,128)(2,1)S(1)} %combine.5.refs_6_.refs_10_), channel_id=1, source_target_pairs={{8,16},{16,8},{12,20},{20,12},{9,17},{17,9},{13,21},{21,13},{10,18... | collective-permute-start | bytes 1695752 | tf_op jit(solution)/shard_map/ppermute | solution.py:633
  71.7 28.9 %collective-permute-start.16 = (bf16[192,2880]{1,0:T(8,128)(2,1)S(1)}, bf16[192,2880]{1,0:T(8,128)(2,1)S(1)}, u32[]{:S(2)}, u32[]{:S(2)}) collective-permute-start(bf16[192,2880]{1,0:T(8,128)(2,1)S(1)} %combine.6.refs_2_), channel_id=1, source_target_pairs={{0,8},{8,0},{4,12},{12,4},{16,24},{24,16},{20,28},{28,20},{1,9},{9... | collective-permute-start | bytes 3317768 | tf_op jit(solution)/shard_map/ppermute | solution.py:633
  76.7 19.4 %collective-permute-start.19 = (bf16[192,1408]{1,0:T(8,128)(2,1)S(1)}, bf16[192,1408]{1,0:T(8,128)(2,1)S(1)}, u32[]{:S(2)}, u32[]{:S(2)}) collective-permute-start(bf16[192,1408]{1,0:T(8,128)(2,1)S(1)} %combine.7.refs_14_.refs_15_), channel_id=1, source_target_pairs={{8,16},{16,8},{12,20},{20,12},{9,17},{17,9},{13,21},{21,13},{10,18... | collective-permute-start | bytes 1622024 | tf_op jit(solution)/shard_map/ppermute | solution.py:633
  82.3 7.9 %collective-permute-start.20 = (bf16[192,512]{1,0:T(8,128)(2,1)S(1)}, bf16[192,512]{1,0:T(8,128)(2,1)S(1)}, u32[]{:S(2)}, u32[]{:S(2)}) collective-permute-start(bf16[192,512]{1,0:T(8,128)(2,1)S(1)} %get-tuple-element.32), channel_id=1, source_target_pairs={{0,4},{4,0},{8,12},{12,8},{16,20},{20,16},{24,28},{28,24},{1,5},{5... | collective-permute-start | bytes 589832 | tf_op jit(solution)/shard_map/ppermute | solution.py:621
  83.9 10.1 %collective-permute-start.21 = (bf16[192,512]{1,0:T(8,128)(2,1)S(1)}, bf16[192,512]{1,0:T(8,128)(2,1)S(1)}, u32[]{:S(2)}, u32[]{:S(2)}) collective-permute-start(bf16[192,512]{1,0:T(8,128)(2,1)S(1)} %get-tuple-element.33), channel_id=1, source_target_pairs={{0,4},{4,0},{8,12},{12,8},{16,20},{20,16},{24,28},{28,24},{1,5},{5... | collective-permute-start | bytes 589832 | tf_op jit(solution)/shard_map/ppermute | solution.py:621
  84.4 11.7 %collective-permute-start.22 = (bf16[192,512]{1,0:T(8,128)(2,1)S(1)}, bf16[192,512]{1,0:T(8,128)(2,1)S(1)}, u32[]{:S(2)}, u32[]{:S(2)}) collective-permute-start(bf16[192,512]{1,0:T(8,128)(2,1)S(1)} %get-tuple-element.34), channel_id=1, source_target_pairs={{0,4},{4,0},{8,12},{12,8},{16,20},{20,16},{24,28},{28,24},{1,5},{5... | collective-permute-start | bytes 589832 | tf_op jit(solution)/shard_map/ppermute | solution.py:621
  97.0 26.7 %collective-permute-start.26 = (bf16[192,2880]{1,0:T(8,128)(2,1)S(1)}, bf16[192,2880]{1,0:T(8,128)(2,1)S(1)}, u32[]{:S(2)}, u32[]{:S(2)}) collective-permute-start(bf16[192,2880]{1,0:T(8,128)(2,1)S(1)} %combine.8.refs_15_), channel_id=1, source_target_pairs={{0,8},{8,0},{4,12},{12,4},{16,24},{24,16},{20,28},{28,20},{1,9},{9... | collective-permute-start | bytes 3317768 | tf_op jit(solution)/shard_map/ppermute | solution.py:633
  101.4 18.8 %collective-permute-start.27 = (bf16[192,1472]{1,0:T(8,128)(2,1)S(1)}, bf16[192,1472]{1,0:T(8,128)(2,1)S(1)}, u32[]{:S(2)}, u32[]{:S(2)}) collective-permute-start(bf16[192,1472]{1,0:T(8,128)(2,1)S(1)} %get-tuple-element.43), channel_id=1, source_target_pairs={{8,16},{16,8},{12,20},{20,12},{9,17},{17,9},{13,21},{21,13},{10,18... | collective-permute-start | bytes 1695752 | tf_op jit(solution)/shard_map/ppermute | solution.py:633
  102.2 18.0 %collective-permute-start.28 = (bf16[192,1408]{1,0:T(8,128)(2,1)S(1)}, bf16[192,1408]{1,0:T(8,128)(2,1)S(1)}, u32[]{:S(2)}, u32[]{:S(2)}) collective-permute-start(bf16[192,1408]{1,0:T(8,128)(2,1)S(1)} %get-tuple-element.44), channel_id=1, source_target_pairs={{8,16},{16,8},{12,20},{20,12},{9,17},{17,9},{13,21},{21,13},{10,18... | collective-permute-start | bytes 1622024 | tf_op jit(solution)/shard_map/ppermute | solution.py:633
  107.0 10.3 %collective-permute-start.24 = (bf16[192,512]{1,0:T(8,128)(2,1)S(1)}, bf16[192,512]{1,0:T(8,128)(2,1)S(1)}, u32[]{:S(2)}, u32[]{:S(2)}) collective-permute-start(bf16[192,512]{1,0:T(8,128)(2,1)S(1)} %get-tuple-element.40), channel_id=1, source_target_pairs={{0,4},{4,0},{8,12},{12,8},{16,20},{20,16},{24,28},{28,24},{1,5},{5... | collective-permute-start | bytes 589832 | tf_op jit(solution)/shard_map/ppermute | solution.py:621
  109.3 8.0 %collective-permute-start.25 = (bf16[192,512]{1,0:T(8,128)(2,1)S(1)}, bf16[192,512]{1,0:T(8,128)(2,1)S(1)}, u32[]{:S(2)}, u32[]{:S(2)}) collective-permute-start(bf16[192,512]{1,0:T(8,128)(2,1)S(1)} %get-tuple-element.42), channel_id=1, source_target_pairs={{0,4},{4,0},{8,12},{12,8},{16,20},{20,16},{24,28},{28,24},{1,5},{5... | collective-permute-start | bytes 589832 | tf_op jit(solution)/shard_map/ppermute | solution.py:621
  (11 other events, 48.0 us)

commit v5 on v4

--- a/solution.py
+++ b/solution.py
@@ -32,8 +32,8 @@
     return pl.BlockSpec(memory_space=pltpu.SMEM)
 
 
-def params():
-    return pltpu.CompilerParams(vmem_limit_bytes=24 * 1024 * 1024)
+def params(mib=24):
+    return pltpu.CompilerParams(vmem_limit_bytes=mib * 1024 * 1024)
 
 
 def taking(microseconds):
@@ -163,7 +163,7 @@
             jax.ShapeDtypeStruct((tokens, cut), bf16),
             jax.ShapeDtypeStruct((count, tokens), f32),
         ),
-        in_specs=[anywhere()] * 3,
+        in_specs=[pl.BlockSpec(memory_space=pltpu.HBM)] * 3,
         out_specs=(whole(),) * 3,
         scratch_shapes=[
             pltpu.VMEM((model, tokens), bf16),
@@ -171,7 +171,7 @@
             pltpu.VMEM((count, tokens), jnp.int32),
             pltpu.SemaphoreType.DMA((3,)),
         ],
-        compiler_params=params(),
+        compiler_params=params(58),
         cost_estimate=taking(2),
         name="make_rows",
     )(grad_out.T, top_logits.T, expert_ids.T)
@@ -633,7 +633,7 @@
         return lax.ppermute(value, "ctx", pairs)
 
     got = {(0, "own"): [w_down[0]]}
-    for name in "AB":
+    for name in "BA":
         got[1, name] = [swap_z(w_down[0], name)]
 
     late, early, gates = make_rows(grad_out, top_logits, expert_ids, width, cut)
@@ -645,13 +645,13 @@
     late_x = swap(late, 1, 0)
     late_mine = [late] + [swap(late, 0, high) for high in highs]
     late_mine += [late_x] + [swap(late_x, 0, high) for high in highs]
-    (early,) = hold((early,), [late_x])
     own, other_first, other_rest = split_hidden(
-        table, where, saved_hidden[0, 0], depth, w_down.shape[1], [early]
+        table, where, saved_hidden[0, 0], depth, w_down.shape[1], [late]
     )
+    (early,) = hold((early,), [late_x, own])
     other_first = swap(other_first, 1, 0)
     early_x = swap(early, 1, 0)
-    late_rows = sides(pack(late_mine, [other_first, got[1, "A"][0], got[1, "B"][0], early_x]))
+    late_rows = sides(pack(late_mine, [got[1, "B"][0], got[1, "A"][0], early_x]))
     late_rows = (late_rows, [(side, place) for place in range(experts) for side in range(2)])
     early_rows = sides(pack([early, early_x], []))
     places = [(0, 0), (1, 0)]
@@ -662,6 +662,7 @@
             places += [(len(early_rows), None), (len(early_rows) + 1, None)]
             early_rows += sides(swap(block, 0, high))
     early_rows = (early_rows, places)
+    (other_rest,) = hold((other_rest,), [other_first])
     other_rest = swap(other_rest, 1, 0)
 
     first = [products(table, where, late_rows, late_rows, own, other_first, 0, model, model - cut, "first_late", [])]
@@ -709,12 +710,11 @@
     for chunk in range(2)[only_first:]:
         marker = pass_on(3, "B", [marker], chunk)
     sums = backprop([[(0, "own")], [(1, "A")], [(1, "B")]], None, False, [marker])
-    early_halves = halves[1::2]
     for turn in range(2, depth):
         choices = choices_of(turn)
         if turn > 2:
-            pass_on(turn + 1, "B", [sums, *early_halves])
-            marker = pass_on(turn + 1, "A", [sums, *early_halves])
+            pass_on(turn + 1, "B", [sums])
+            marker = pass_on(turn + 1, "A", [sums])
         sums = backprop(choices, sums, len(choices) == 1, [marker])
     slot_grad = sums[0:1, :slots] + swap(sums[0:1, slots:], 1, 0)
     grads = lax.all_to_all(

time: 127 us -> 135 us (1.063)
  the two profiles are of different devices: /device:TPU:0 before, /device:TPU:16 now
where the time goes in v5:
time: 135 us; the launch traced here: 134 us
  waiting for transfers between devices  54.5 us (40%)
  starting transfers between devices  35.2 us (26%)
  Pallas kernels  34.5 us (26%)
  blocking collectives  6.08 us (5%)
  local copies, waits for them, and re-layouts  3.12 us (2%)
    ppermute x10, waiting for transfers between devices, swap(): return lax.ppermute(value, 'ctx', [(i, i ^ x) for i in range(groups)])  28.9 us
    ppermute x11, waiting for transfers between devices, swap_z(): return lax.ppermute(value, 'ctx', pairs)  21.1 us
    ppermute x11, starting transfers between devices, swap_z(): return lax.ppermute(value, 'ctx', pairs)  18.1 us
    ppermute x10, starting transfers between devices, swap(): return lax.ppermute(value, 'ctx', [(i, i ^ x) for i in range(groups)])  11.4 us
    pallas_call x4, Pallas kernels, products(): pl.pallas_call(functools.partial(products_kernel, table, model, counts, p...  11 us
    pallas_call x3, Pallas kernels, back_part(): pl.pallas_call(functools.partial(back_kernel, table, model, cut, counts,...  7.86 us
    all_to_all x1, blocking collectives, per_device_full(): lax.all_to_all(slot_grad.reshape(experts, tokens), 'exp', split_axis=0, c...  6.08 us
    ppermute x8, starting transfers between devices, swap(): return lax.ppermute(value, 'exp', [(i, i ^ exp) for i in range(experts)])  5.76 us
  transfers between devices with their start and end apart: 29, of which 11 were waited for; matrix products, arithmetic and copies ran while one was open for 1% of the time, Pallas kernels for 24%

profile of v5, /device:TPU:16, one launch (start us, length us, event | category | flops | bytes accessed | tf_op | source)
XLA Modules:
  0.0 134.5 jit_solution(2157778712105620213)
XLA Ops:
  4.2 2.2 %make_rows.1 = (bf16[128,1536]{1,0:T(8,128)(2,1)}, bf16[128,1408]{1,0:T(8,128)(2,1)}, f32[4,128]{1,0:T(4,128)}) custom-call(bf16[2880,128]{1,0:T(8,128)(2,1)} %bitcast.22, f32[4,128]{1,0:T(4,128)} %bitcast.23, s32[4,128]{1,0:T(4,128)} %bitcast.18), custom_call_target="tpu_custom_call" | custom-call | flops 2000000 | bytes 6000000 | tf_op jit(solution)/shard_map/make_rows/pallas_call | solution.py:159
  9.5 7.8 %collective-permute-done.1.refs_1_.refs_2_ = bf16[128,1536]{1,0:T(8,128)(2,1)S(1)} collective-permute-done((bf16[128,1536]{1,0:T(8,128)(2,1)}, bf16[128,1536]{1,0:T(8,128)(2,1)S(1)}, u32[]{:S(2)}, u32[]{:S(2)}) %collective-permute-start.1) | collective-permute-done | bytes 393248 | tf_op jit(solution)/shard_map/ppermute | solution.py:621
  21.9 2.2 %split_hidden.1 = (bf16[4,192,512]{2,1,0:T(8,128)(2,1)S(1)}, bf16[1,192,512]{2,1,0:T(8,128)(2,1)S(1)}, bf16[3,192,512]{2,1,0:T(8,128)(2,1)S(1)}) custom-call(s32[32]{0:T(128)S(1)} %dynamic-slice_bitcast_fusion.where_ref, bf16[512,1536]{1,0:T(8,128)(2,1)S(1)} %bitcast.14, bf16[128,1536]{1,0:T(8,128)(2,1)S(1)} %copy-done), custom_call_target="tpu_custom_call" | custom-call | flops 2000000 | bytes 6000000 | tf_op jit(solution)/shard_map/split_hidden/pallas_call | solution.py:250
  25.7 7.2 %collective-permute-done.5.refs_6_.refs_1_ = bf16[128,1408]{1,0:T(8,128)(2,1)S(1)} collective-permute-done((bf16[128,1408]{1,0:T(8,128)(2,1)S(1)}, bf16[128,1408]{1,0:T(8,128)(2,1)S(1)}, u32[]{:S(2)}, u32[]{:S(2)}) %collective-permute-start.5) | collective-permute-done | bytes 360480 | tf_op jit(solution)/shard_map/ppermute | solution.py:621
  38.2 3.4 %collective-permute-done.12.refs_1_.refs_5_.refs_9_ = bf16[1,192,512]{2,1,0:T(8,128)(2,1)S(1)} collective-permute-done((bf16[1,192,512]{2,1,0:T(8,128)(2,1)S(1)}, bf16[1,192,512]{2,1,0:T(8,128)(2,1)S(1)}, u32[]{:S(2)}, u32[]{:S(2)}) %collective-permute-start.12) | collective-permute-done | bytes 196640 | tf_op jit(solution)/shard_map/ppermute | solution.py:621
  43.0 3.3 %collective-permute-start.14 = (bf16[192,2880]{1,0:T(8,128)(2,1)S(1)}, bf16[192,2880]{1,0:T(8,128)(2,1)S(1)}, u32[]{:S(2)}, u32[]{:S(2)}) collective-permute-start(bf16[192,2880]{1,0:T(8,128)(2,1)S(1)} %collective-permute-done.4.refs_5_.refs_12_), channel_id=1, source_target_pairs={{8,16},{16,8},{12,20},{20,12},{9,17},{17,9},{13,21},{21,13},{10,18... | collective-permute-start | bytes 3317768 | tf_op jit(solution)/shard_map/ppermute | solution.py:633
  46.3 2.2 %first_late.1.kept_ref.refs_1_ = f32[1,192,1472]{2,1,0:T(8,128)S(1)} custom-call(s32[32]{0:T(128)S(1)} %dynamic-slice_bitcast_fusion.where_ref, bf16[4,128,1536]{2,1,0:T(8,128)(2,1)S(1)} %pack_rows.2.refs_0_.refs_2_.refs_6_, bf16[4,128,1536]{2,1,0:T(8,128)(2,1)S(1)} %collective-permute-done.6.refs_1_.refs_3_.refs_7_, ...), custom_call_target="tpu_custom_call" | custom-call | flops 4000000 | bytes 12000000 | tf_op jit(solution)/shard_map/first_late/pallas_call | solution.py:303
  49.4 4.5 %collective-permute-done.10.refs_4_.refs_6_ = bf16[128,1408]{1,0:T(8,128)(2,1)S(1)} collective-permute-done((bf16[128,1408]{1,0:T(8,128)(2,1)S(1)}, bf16[128,1408]{1,0:T(8,128)(2,1)S(1)}, u32[]{:S(2)}, u32[]{:S(2)}) %collective-permute-start.10) | collective-permute-done | bytes 360480 | tf_op jit(solution)/shard_map/ppermute | solution.py:623
  56.0 2.1 %first_early.1.kept_ref.refs_1_ = f32[1,192,1408]{2,1,0:T(8,128)S(1)} custom-call(s32[32]{0:T(128)S(1)} %dynamic-slice_bitcast_fusion.where_ref, bf16[2,128,1408]{2,1,0:T(8,128)(2,1)S(1)} %pack_rows.3.refs_0_.refs_2_, bf16[2,128,1408]{2,1,0:T(8,128)(2,1)S(1)} %collective-permute-done.7.refs_0_.refs_1_.refs_3_, ...), custom_call_target="tpu_custom_call" | custom-call | flops 4000000 | bytes 12000000 | tf_op jit(solution)/shard_map/first_early/pallas_call | solution.py:303
  58.1 5.1 %collective-permute-done.15.refs_0_.refs_11_ = bf16[192,1472]{1,0:T(8,128)(2,1)S(1)} collective-permute-done((bf16[192,1472]{1,0:T(8,128)(2,1)S(1)}, bf16[192,1472]{1,0:T(8,128)(2,1)S(1)}, u32[]{:S(2)}, u32[]{:S(2)}) %collective-permute-start.15) | collective-permute-done | bytes 565280 | tf_op jit(solution)/shard_map/ppermute | solution.py:633
  65.0 2.5 %collective-permute-start.17 = (bf16[192,1472]{1,0:T(8,128)(2,1)S(1)}, bf16[192,1472]{1,0:T(8,128)(2,1)S(1)}, u32[]{:S(2)}, u32[]{:S(2)}) collective-permute-start(bf16[192,1472]{1,0:T(8,128)(2,1)S(1)} %combine.5.refs_6_.refs_10_), channel_id=1, source_target_pairs={{8,16},{16,8},{12,20},{20,12},{9,17},{17,9},{13,21},{21,13},{10,18... | collective-permute-start | bytes 1695752 | tf_op jit(solution)/shard_map/ppermute | solution.py:633
  67.5 3.4 %rest_early.1.refs_2_.refs_4_.refs_3_ = f32[3,192,1408]{2,1,0:T(8,128)S(1)} custom-call(s32[32]{0:T(128)S(1)} %dynamic-slice_bitcast_fusion.where_ref, bf16[2,128,1408]{2,1,0:T(8,128)(2,1)S(1)} %pack_rows.3.refs_0_.refs_2_, bf16[2,128,1408]{2,1,0:T(8,128)(2,1)S(1)} %collective-permute-done.7.refs_0_.refs_1_.refs_3_, ...), custom_call_target="tpu_custom_call" | custom-call | flops 4000000 | bytes 12000000 | tf_op jit(solution)/shard_map/rest_early/pallas_call | solution.py:303
  70.9 3.4 %rest_late.1.refs_1_.refs_3_.refs_2_ = f32[3,192,1472]{2,1,0:T(8,128)S(1)} custom-call(s32[32]{0:T(128)S(1)} %dynamic-slice_bitcast_fusion.where_ref, bf16[4,128,1536]{2,1,0:T(8,128)(2,1)S(1)} %pack_rows.2.refs_0_.refs_2_.refs_6_, bf16[4,128,1536]{2,1,0:T(8,128)(2,1)S(1)} %collective-permute-done.6.refs_1_.refs_3_.refs_7_, ...), custom_call_target="tpu_custom_call" | custom-call | flops 4000000 | bytes 12000000 | tf_op jit(solution)/shard_map/rest_late/pallas_call | solution.py:303
  77.2 2.3 %collective-permute-start.19 = (bf16[192,1408]{1,0:T(8,128)(2,1)S(1)}, bf16[192,1408]{1,0:T(8,128)(2,1)S(1)}, u32[]{:S(2)}, u32[]{:S(2)}) collective-permute-start(bf16[192,1408]{1,0:T(8,128)(2,1)S(1)} %combine.7.refs_14_.refs_15_), channel_id=1, source_target_pairs={{8,16},{16,8},{12,20},{20,12},{9,17},{17,9},{13,21},{21,13},{10,18... | collective-permute-start | bytes 1622024 | tf_op jit(solution)/shard_map/ppermute | solution.py:633
  79.5 4.7 %back_part.3 = (bf16[192,512]{1,0:T(8,128)(2,1)S(1)}, bf16[192,512]{1,0:T(8,128)(2,1)S(1)}, bf16[192,512]{1,0:T(8,128)(2,1)S(1)}, bf16[192,512]{1,0:T(8,128)(2,1...) custom-call(s32[32]{0:T(128)S(1)} %dynamic-slice_bitcast_fusion.where_ref, ...), custom_call_target="tpu_custom_call" | custom-call | flops 6000000 | bytes 18000000 | tf_op jit(solution)/shard_map/back_part/pallas_call | solution.py:532
  84.2 2.6 %back_part.4 = (bf16[192,512]{1,0:T(8,128)(2,1)S(1)}, bf16[192,512]{1,0:T(8,128)(2,1)S(1)}, f32[8,1024]{1,0:T(8,128)S(1)}) custom-call(s32[32]{0:T(128)S(1)} %dynamic-slice_bitcast_fusion.where_ref, bf16[4,128,1536]{2,1,0:T(8,128)(2,1)S(1)} %pack_rows.2.refs_0_.refs_2_.refs_6_, bf16[4,128,1536]{2,1,0:T(8,128)(2,1)S(1)} %collective-permute-done.6.refs_1_.refs_3_.refs_7_, ...), custom_call_target="tpu_custom_call" | custom-call | flops 6000000 | bytes 18000000 | tf_op jit(solution)/shard_map/back_part/pallas_call | solution.py:532
  86.9 8.0 %collective-permute-done.19.refs_1_.refs_13_ = bf16[192,1408]{1,0:T(8,128)(2,1)S(1)} collective-permute-done((bf16[192,1408]{1,0:T(8,128)(2,1)S(1)}, bf16[192,1408]{1,0:T(8,128)(2,1)S(1)}, u32[]{:S(2)}, u32[]{:S(2)}) %collective-permute-start.19) | collective-permute-done | bytes 540704 | tf_op jit(solution)/shard_map/ppermute | solution.py:633
  96.4 6.7 %collective-permute-done.16.refs_11_.refs_0_ = bf16[192,2880]{1,0:T(8,128)(2,1)S(1)} collective-permute-done((bf16[192,2880]{1,0:T(8,128)(2,1)S(1)}, bf16[192,2880]{1,0:T(8,128)(2,1)S(1)}, u32[]{:S(2)}, u32[]{:S(2)}) %collective-permute-start.16) | collective-permute-done | bytes 1105952 | tf_op jit(solution)/shard_map/ppermute | solution.py:633
  104.0 2.8 %collective-permute-start.27 = (bf16[192,1472]{1,0:T(8,128)(2,1)S(1)}, bf16[192,1472]{1,0:T(8,128)(2,1)S(1)}, u32[]{:S(2)}, u32[]{:S(2)}) collective-permute-start(bf16[192,1472]{1,0:T(8,128)(2,1)S(1)} %get-tuple-element.43), channel_id=1, source_target_pairs={{8,16},{16,8},{12,20},{20,12},{9,17},{17,9},{13,21},{21,13},{10,18... | collective-permute-start | bytes 1695752 | tf_op jit(solution)/shard_map/ppermute | solution.py:633
  106.8 3.0 %collective-permute-start.28 = (bf16[192,1408]{1,0:T(8,128)(2,1)S(1)}, bf16[192,1408]{1,0:T(8,128)(2,1)S(1)}, u32[]{:S(2)}, u32[]{:S(2)}) collective-permute-start(bf16[192,1408]{1,0:T(8,128)(2,1)S(1)} %get-tuple-element.44), channel_id=1, source_target_pairs={{8,16},{16,8},{12,20},{20,12},{9,17},{17,9},{13,21},{21,13},{10,18... | collective-permute-start | bytes 1622024 | tf_op jit(solution)/shard_map/ppermute | solution.py:633
  112.5 5.2 %collective-permute-done.21.refs_1_ = bf16[192,512]{1,0:T(8,128)(2,1)S(1)} collective-permute-done((bf16[192,512]{1,0:T(8,128)(2,1)S(1)}, bf16[192,512]{1,0:T(8,128)(2,1)S(1)}, u32[]{:S(2)}, u32[]{:S(2)}) %collective-permute-start.21) | collective-permute-done | bytes 196640 | tf_op jit(solution)/shard_map/ppermute | solution.py:621
  118.2 3.3 %collective-permute-done.22.refs_3_ = bf16[192,512]{1,0:T(8,128)(2,1)S(1)} collective-permute-done((bf16[192,512]{1,0:T(8,128)(2,1)S(1)}, bf16[192,512]{1,0:T(8,128)(2,1)S(1)}, u32[]{:S(2)}, u32[]{:S(2)}) %collective-permute-start.22) | collective-permute-done | bytes 196640 | tf_op jit(solution)/shard_map/ppermute | solution.py:621
  123.6 6.1 %all_to_all.11 = f32[4,1,128]{2,1,0:T(1,128)S(1)} all-to-all(f32[4,1,128]{2,1,0:T(1,128)S(1)} %add_bitcast_fusion), channel_id=1, replica_groups=mesh['ctx'=8,'exp'=4] {'exp'}, dimensions={0} | all-to-all | bytes 4096 | tf_op jit(solution)/shard_map/all_to_all | solution.py:720
  130.3 2.6 %join_hidden.1 = bf16[512,1536]{1,0:T(8,128)(2,1)} custom-call(s32[32]{0:T(128)S(1)} %dynamic-slice_bitcast_fusion.where_ref, bf16[192,512]{1,0:T(8,128)(2,1)S(1)} %get-tuple-element.33.refs_0_, bf16[192,512]{1,0:T(8,128)(2,1)S(1)} %collective-permute-done.21.refs_1_, bf16[192,512]{1,0:T(8,128)(2,1)S(1)} %get-tuple-element.35.refs_2_, ...), custom_call_target="tpu_custom_call" | custom-call | flops 2000000 | bytes 6000000 | tf_op jit(solution)/shard_map/join_hidden/pallas_call | solution.py:571
  (75 shorter events, 36.9 us)
Async XLA Ops:
  0.6 32.2 %collective-permute-start.4 = (bf16[192,2880]{1,0:T(8,128)(2,1)}, bf16[192,2880]{1,0:T(8,128)(2,1)S(1)}, u32[]{:S(2)}, u32[]{:S(2)}) collective-permute-start(bf16[192,2880]{1,0:T(8,128)(2,1)} %bitcast.15), channel_id=1, source_target_pairs={{0,8},{8,0},{4,12},{12,4},{16,24},{24,16},{20,28},{28,20},{1,9},{9... | collective-permute-start | bytes 3317768 | tf_op jit(solution)/shard_map/ppermute | solution.py:633
  2.3 30.6 %collective-permute-start.3 = (bf16[192,2880]{1,0:T(8,128)(2,1)}, bf16[192,2880]{1,0:T(8,128)(2,1)S(1)}, u32[]{:S(2)}, u32[]{:S(2)}) collective-permute-start(bf16[192,2880]{1,0:T(8,128)(2,1)} %bitcast.16), channel_id=1, source_target_pairs={{8,16},{16,8},{12,20},{20,12},{9,17},{17,9},{13,21},{21,13},{10,18... | collective-permute-start | bytes 3317768 | tf_op jit(solution)/shard_map/ppermute | solution.py:633
  6.4 10.9 %collective-permute-start.1 = (bf16[128,1536]{1,0:T(8,128)(2,1)}, bf16[128,1536]{1,0:T(8,128)(2,1)S(1)}, u32[]{:S(2)}, u32[]{:S(2)}) collective-permute-start(bf16[128,1536]{1,0:T(8,128)(2,1)} %get-tuple-element.25.refs_0_), channel_id=1, source_target_pairs={{0,4},{4,0},{8,12},{12,8},{16,20},{20,16},{24,28},{28,24},{1,5},{5... | collective-permute-start | bytes 1179656 | tf_op jit(solution)/shard_map/ppermute | solution.py:621
  7.9 17.7 %collective-permute-start = (bf16[128,1536]{1,0:T(8,128)(2,1)}, bf16[128,1536]{1,0:T(8,128)(2,1)S(1)}, u32[]{:S(2)}, u32[]{:S(2)}) collective-permute-start(bf16[128,1536]{1,0:T(8,128)(2,1)} %get-tuple-element.25.refs_0_), channel_id=1, source_target_pairs={{0,2},{1,3},{2,0},{3,1},{4,6},{5,7},{6,4},{7,5},{8,10},{9,11},{10,... | collective-permute-start | bytes 1179656 | tf_op jit(solution)/shard_map/ppermute | solution.py:623
  17.2 15.6 %collective-permute-start.2 = (bf16[128,1536]{1,0:T(8,128)(2,1)S(1)}, bf16[128,1536]{1,0:T(8,128)(2,1)S(1)}, u32[]{:S(2)}, u32[]{:S(2)}) collective-permute-start(bf16[128,1536]{1,0:T(8,128)(2,1)S(1)} %collective-permute-done.1.refs_1_.refs_2_), channel_id=1, source_target_pairs={{0,2},{1,3},{2,0},{3,1},{4,6},{5,7},{6,4},{7,5},{8,10},{9,11},{10,... | collective-permute-start | bytes 1179656 | tf_op jit(solution)/shard_map/ppermute | solution.py:623
  24.1 8.8 %collective-permute-start.5 = (bf16[128,1408]{1,0:T(8,128)(2,1)S(1)}, bf16[128,1408]{1,0:T(8,128)(2,1)S(1)}, u32[]{:S(2)}, u32[]{:S(2)}) collective-permute-start(bf16[128,1408]{1,0:T(8,128)(2,1)S(1)} %hold.2.refs_0_), channel_id=1, source_target_pairs={{0,4},{4,0},{8,12},{12,8},{16,20},{20,16},{24,28},{28,24},{1,5},{5... | collective-permute-start | bytes 1081352 | tf_op jit(solution)/shard_map/ppermute | solution.py:621
  33.7 9.3 %collective-permute-start.6 = (bf16[4,128,1536]{2,1,0:T(8,128)(2,1)S(1)}, bf16[4,128,1536]{2,1,0:T(8,128)(2,1)S(1)}, u32[]{:S(2)}, u32[]{:S(2)}) collective-permute-start(bf16[4,128,1536]{2,1,0:T(8,128)(2,1)S(1)} %pack_rows.2.refs_0_.refs_2_.refs_6_), channel_id=1, source_target_pairs={{0,1},{1,0},{2,3},{3,2},{4,5},{5,4},{6,7},{7,6},{8,9},{9,8},{10,11... | collective-permute-start | bytes 4718600 | tf_op jit(solution)/shard_map/ppermute | solution.py:623
  34.1 14.4 %collective-permute-start.7 = (bf16[2,128,1408]{2,1,0:T(8,128)(2,1)S(1)}, bf16[2,128,1408]{2,1,0:T(8,128)(2,1)S(1)}, u32[]{:S(2)}, u32[]{:S(2)}) collective-permute-start(bf16[2,128,1408]{2,1,0:T(8,128)(2,1)S(1)} %pack_rows.3.refs_0_.refs_2_), channel_id=1, source_target_pairs={{0,1},{1,0},{2,3},{3,2},{4,5},{5,4},{6,7},{7,6},{8,9},{9,8},{10,11... | collective-permute-start | bytes 2162696 | tf_op jit(solution)/shard_map/ppermute | solution.py:623
  36.1 13.2 %collective-permute-start.8 = (bf16[128,1408]{1,0:T(8,128)(2,1)S(1)}, bf16[128,1408]{1,0:T(8,128)(2,1)S(1)}, u32[]{:S(2)}, u32[]{:S(2)}) collective-permute-start(bf16[128,1408]{1,0:T(8,128)(2,1)S(1)} %hold.2.refs_0_), channel_id=1, source_target_pairs={{0,2},{1,3},{2,0},{3,1},{4,6},{5,7},{6,4},{7,5},{8,10},{9,11},{10,... | collective-permute-start | bytes 1081352 | tf_op jit(solution)/shard_map/ppermute | solution.py:623
  36.6 17.3 %collective-permute-start.10 = (bf16[128,1408]{1,0:T(8,128)(2,1)S(1)}, bf16[128,1408]{1,0:T(8,128)(2,1)S(1)}, u32[]{:S(2)}, u32[]{:S(2)}) collective-permute-start(bf16[128,1408]{1,0:T(8,128)(2,1)S(1)} %collective-permute-done.5.refs_6_.refs_1_), channel_id=1, source_target_pairs={{0,2},{1,3},{2,0},{3,1},{4,6},{5,7},{6,4},{7,5},{8,10},{9,11},{10,... | collective-permute-start | bytes 1081352 | tf_op jit(solution)/shard_map/ppermute | solution.py:623
  41.5 14.5 %collective-permute-start.13 = (bf16[3,192,512]{2,1,0:T(8,128)(2,1)S(1)}, bf16[3,192,512]{2,1,0:T(8,128)(2,1)S(1)}, u32[]{:S(2)}, u32[]{:S(2)}) collective-permute-start(bf16[3,192,512]{2,1,0:T(8,128)(2,1)S(1)} %hold.3), channel_id=1, source_target_pairs={{0,4},{4,0},{8,12},{12,8},{16,20},{20,16},{24,28},{28,24},{1,5},{5... | collective-permute-start | bytes 1769480 | tf_op jit(solution)/shard_map/ppermute | solution.py:621
  43.0 31.3 %collective-permute-start.14 = (bf16[192,2880]{1,0:T(8,128)(2,1)S(1)}, bf16[192,2880]{1,0:T(8,128)(2,1)S(1)}, u32[]{:S(2)}, u32[]{:S(2)}) collective-permute-start(bf16[192,2880]{1,0:T(8,128)(2,1)S(1)} %collective-permute-done.4.refs_5_.refs_12_), channel_id=1, source_target_pairs={{8,16},{16,8},{12,20},{20,12},{9,17},{17,9},{13,21},{21,13},{10,18... | collective-permute-start | bytes 3317768 | tf_op jit(solution)/shard_map/ppermute | solution.py:633
  49.3 14.0 %collective-permute-start.15 = (bf16[192,1472]{1,0:T(8,128)(2,1)S(1)}, bf16[192,1472]{1,0:T(8,128)(2,1)S(1)}, u32[]{:S(2)}, u32[]{:S(2)}) collective-permute-start(bf16[192,1472]{1,0:T(8,128)(2,1)S(1)} %begin.2), channel_id=1, source_target_pairs={{0,8},{8,0},{4,12},{12,4},{16,24},{24,16},{20,28},{28,20},{1,9},{9... | collective-permute-start | bytes 1695752 | tf_op jit(solution)/shard_map/ppermute | solution.py:633
  63.9 12.6 %collective-permute-start.18 = (bf16[192,1408]{1,0:T(8,128)(2,1)S(1)}, bf16[192,1408]{1,0:T(8,128)(2,1)S(1)}, u32[]{:S(2)}, u32[]{:S(2)}) collective-permute-start(bf16[192,1408]{1,0:T(8,128)(2,1)S(1)} %begin.3.refs_2_), channel_id=1, source_target_pairs={{0,8},{8,0},{4,12},{12,4},{16,24},{24,16},{20,28},{28,20},{1,9},{9... | collective-permute-start | bytes 1622024 | tf_op jit(solution)/shard_map/ppermute | solution.py:633
  65.0 21.8 %collective-permute-start.17 = (bf16[192,1472]{1,0:T(8,128)(2,1)S(1)}, bf16[192,1472]{1,0:T(8,128)(2,1)S(1)}, u32[]{:S(2)}, u32[]{:S(2)}) collective-permute-start(bf16[192,1472]{1,0:T(8,128)(2,1)S(1)} %combine.5.refs_6_.refs_10_), channel_id=1, source_target_pairs={{8,16},{16,8},{12,20},{20,12},{9,17},{17,9},{13,21},{21,13},{10,18... | collective-permute-start | bytes 1695752 | tf_op jit(solution)/shard_map/ppermute | solution.py:633
  75.2 27.9 %collective-permute-start.16 = (bf16[192,2880]{1,0:T(8,128)(2,1)S(1)}, bf16[192,2880]{1,0:T(8,128)(2,1)S(1)}, u32[]{:S(2)}, u32[]{:S(2)}) collective-permute-start(bf16[192,2880]{1,0:T(8,128)(2,1)S(1)} %combine.6.refs_2_), channel_id=1, source_target_pairs={{0,8},{8,0},{4,12},{12,4},{16,24},{24,16},{20,28},{28,20},{1,9},{9... | collective-permute-start | bytes 3317768 | tf_op jit(solution)/shard_map/ppermute | solution.py:633
  77.2 17.7 %collective-permute-start.19 = (bf16[192,1408]{1,0:T(8,128)(2,1)S(1)}, bf16[192,1408]{1,0:T(8,128)(2,1)S(1)}, u32[]{:S(2)}, u32[]{:S(2)}) collective-permute-start(bf16[192,1408]{1,0:T(8,128)(2,1)S(1)} %combine.7.refs_14_.refs_15_), channel_id=1, source_target_pairs={{8,16},{16,8},{12,20},{20,12},{9,17},{17,9},{13,21},{21,13},{10,18... | collective-permute-start | bytes 1622024 | tf_op jit(solution)/shard_map/ppermute | solution.py:633
  95.8 37.2 %collective-permute-start.26 = (bf16[192,2880]{1,0:T(8,128)(2,1)S(1)}, bf16[192,2880]{1,0:T(8,128)(2,1)S(1)}, u32[]{:S(2)}, u32[]{:S(2)}) collective-permute-start(bf16[192,2880]{1,0:T(8,128)(2,1)S(1)} %combine.8.refs_15_), channel_id=1, source_target_pairs={{0,8},{8,0},{4,12},{12,4},{16,24},{24,16},{20,28},{28,20},{1,9},{9... | collective-permute-start | bytes 3317768 | tf_op jit(solution)/shard_map/ppermute | solution.py:633
  95.8 14.6 %collective-permute-start.24 = (bf16[192,512]{1,0:T(8,128)(2,1)S(1)}, bf16[192,512]{1,0:T(8,128)(2,1)S(1)}, u32[]{:S(2)}, u32[]{:S(2)}) collective-permute-start(bf16[192,512]{1,0:T(8,128)(2,1)S(1)} %get-tuple-element.40), channel_id=1, source_target_pairs={{0,4},{4,0},{8,12},{12,8},{16,20},{20,16},{24,28},{28,24},{1,5},{5... | collective-permute-start | bytes 589832 | tf_op jit(solution)/shard_map/ppermute | solution.py:621
  104.0 28.9 %collective-permute-start.27 = (bf16[192,1472]{1,0:T(8,128)(2,1)S(1)}, bf16[192,1472]{1,0:T(8,128)(2,1)S(1)}, u32[]{:S(2)}, u32[]{:S(2)}) collective-permute-start(bf16[192,1472]{1,0:T(8,128)(2,1)S(1)} %get-tuple-element.43), channel_id=1, source_target_pairs={{8,16},{16,8},{12,20},{20,12},{9,17},{17,9},{13,21},{21,13},{10,18... | collective-permute-start | bytes 1695752 | tf_op jit(solution)/shard_map/ppermute | solution.py:633
  106.8 26.1 %collective-permute-start.28 = (bf16[192,1408]{1,0:T(8,128)(2,1)S(1)}, bf16[192,1408]{1,0:T(8,128)(2,1)S(1)}, u32[]{:S(2)}, u32[]{:S(2)}) collective-permute-start(bf16[192,1408]{1,0:T(8,128)(2,1)S(1)} %get-tuple-element.44), channel_id=1, source_target_pairs={{8,16},{16,8},{12,20},{20,12},{9,17},{17,9},{13,21},{21,13},{10,18... | collective-permute-start | bytes 1622024 | tf_op jit(solution)/shard_map/ppermute | solution.py:633
  110.4 11.1 %collective-permute-start.22 = (bf16[192,512]{1,0:T(8,128)(2,1)S(1)}, bf16[192,512]{1,0:T(8,128)(2,1)S(1)}, u32[]{:S(2)}, u32[]{:S(2)}) collective-permute-start(bf16[192,512]{1,0:T(8,128)(2,1)S(1)} %get-tuple-element.36), channel_id=1, source_target_pairs={{0,4},{4,0},{8,12},{12,8},{16,20},{20,16},{24,28},{28,24},{1,5},{5... | collective-permute-start | bytes 589832 | tf_op jit(solution)/shard_map/ppermute | solution.py:621
  121.5 8.7 %collective-permute-start.23 = (bf16[192,512]{1,0:T(8,128)(2,1)S(1)}, bf16[192,512]{1,0:T(8,128)(2,1)S(1)}, u32[]{:S(2)}, u32[]{:S(2)}) collective-permute-start(bf16[192,512]{1,0:T(8,128)(2,1)S(1)} %get-tuple-element.38), channel_id=1, source_target_pairs={{0,4},{4,0},{8,12},{12,8},{16,20},{20,16},{24,28},{28,24},{1,5},{5... | collective-permute-start | bytes 589832 | tf_op jit(solution)/shard_map/ppermute | solution.py:621
  122.1 8.2 %collective-permute-start.25 = (bf16[192,512]{1,0:T(8,128)(2,1)S(1)}, bf16[192,512]{1,0:T(8,128)(2,1)S(1)}, u32[]{:S(2)}, u32[]{:S(2)}) collective-permute-start(bf16[192,512]{1,0:T(8,128)(2,1)S(1)} %get-tuple-element.42), channel_id=1, source_target_pairs={{0,4},{4,0},{8,12},{12,8},{16,20},{20,16},{24,28},{28,24},{1,5},{5... | collective-permute-start | bytes 589832 | tf_op jit(solution)/shard_map/ppermute | solution.py:621
  (12 other events, 84.1 us)

commit v6 on v5

--- a/solution.py
+++ b/solution.py
@@ -10,6 +10,7 @@
 
 LANES = 128
 SCALE = 1_000_000
+BEGIN_WEIGHT = 600
 NT = (((1,), (1,)), ((), ()))
 NN = (((1,), (0,)), ((), ()))
 f32 = jnp.float32
@@ -401,7 +402,7 @@
             out_specs=pl.BlockSpec((block, width), lambda j, s: (j, 0)),
         ),
         compiler_params=params(),
-        cost_estimate=taking(1),
+        cost_estimate=taking(BEGIN_WEIGHT),
         name="begin",
     )(where, coming, kept, *after)
 
@@ -643,13 +644,14 @@
         return [mine, swap(mine, 0, 1)]
 
     late_x = swap(late, 1, 0)
-    late_mine = [late] + [swap(late, 0, high) for high in highs]
-    late_mine += [late_x] + [swap(late_x, 0, high) for high in highs]
+    late_near = [late] + [swap(late, 0, high) for high in highs]
     own, other_first, other_rest = split_hidden(
         table, where, saved_hidden[0, 0], depth, w_down.shape[1], [late]
     )
-    (early,) = hold((early,), [late_x, own])
     other_first = swap(other_first, 1, 0)
+    (late_x,) = hold((late_x,), late_near[1:])
+    late_mine = late_near + [late_x] + [swap(late_x, 0, high) for high in highs]
+    (early,) = hold((early,), [late_x, other_first])
     early_x = swap(early, 1, 0)
     late_rows = sides(pack(late_mine, [got[1, "B"][0], got[1, "A"][0], early_x]))
     late_rows = (late_rows, [(side, place) for place in range(experts) for side in range(2)])
@@ -662,7 +664,6 @@
             places += [(len(early_rows), None), (len(early_rows) + 1, None)]
             early_rows += sides(swap(block, 0, high))
     early_rows = (early_rows, places)
-    (other_rest,) = hold((other_rest,), [other_first])
     other_rest = swap(other_rest, 1, 0)
 
     first = [products(table, where, late_rows, late_rows, own, other_first, 0, model, model - cut, "first_late", [])]
@@ -670,10 +671,10 @@
     got[2, "A"] = [swap_z(sent[0], "A")]
     got[2, "B"] = [swap_z(got[1, "A"][0], "B")]
     first.append(
-        products(table, where, early_rows, late_rows, own, other_first, 0, model, cut, "first_early", [other_rest])
+        products(table, where, early_rows, late_rows, own, other_first, 0, model, cut, "first_early", [])
     )
     sent.append(begin(table, where, got[1, "B"][0], first[1], 0, [got[2, "A"][0]]))
-    got[2, "A"].append(swap_z(sent[1], "A"))
+    got[2, "A"].append(swap_z(hold((sent[1],), [other_rest])[0], "A"))
 
     halves, all_choices = [], []
     only_first = max(uses[3, "B"]) <= 0
@@ -710,11 +711,12 @@
     for chunk in range(2)[only_first:]:
         marker = pass_on(3, "B", [marker], chunk)
     sums = backprop([[(0, "own")], [(1, "A")], [(1, "B")]], None, False, [marker])
+    sooner = halves[1::2]
     for turn in range(2, depth):
         choices = choices_of(turn)
         if turn > 2:
-            pass_on(turn + 1, "B", [sums])
-            marker = pass_on(turn + 1, "A", [sums])
+            pass_on(turn + 1, "B", [sums, *sooner])
+            marker = pass_on(turn + 1, "A", [sums, *sooner])
         sums = backprop(choices, sums, len(choices) == 1, [marker])
     slot_grad = sums[0:1, :slots] + swap(sums[0:1, slots:], 1, 0)
     grads = lax.all_to_all(

time: 135 us -> 125 us (0.926)
  the two profiles are of different devices: /device:TPU:16 before, /device:TPU:0 now
where the time goes in v6:
time: 125 us; the launch traced here: 123 us
  starting transfers between devices  40.3 us (32%)
  Pallas kernels  36.9 us (30%)
  waiting for transfers between devices  34.9 us (28%)
  blocking collectives  6.35 us (5%)
  local copies, waits for them, and re-layouts  3.12 us (2%)
    ppermute x11, starting transfers between devices, swap_z(): return lax.ppermute(value, 'ctx', pairs)  22.9 us
    ppermute x10, waiting for transfers between devices, swap(): return lax.ppermute(value, 'ctx', [(i, i ^ x) for i in range(groups)])  21.1 us
    ppermute x10, starting transfers between devices, swap(): return lax.ppermute(value, 'ctx', [(i, i ^ x) for i in range(groups)])  11.4 us
    pallas_call x4, Pallas kernels, products(): pl.pallas_call(functools.partial(products_kernel, table, model, counts, p...  11.1 us
    pallas_call x3, Pallas kernels, back_part(): pl.pallas_call(functools.partial(back_kernel, table, model, cut, counts,...  9.96 us
    ppermute x8, waiting for transfers between devices, swap(): return lax.ppermute(value, 'exp', [(i, i ^ exp) for i in range(experts)])  9.37 us
    all_to_all x1, blocking collectives, per_device_full(): lax.all_to_all(slot_grad.reshape(experts, tokens), 'exp', split_axis=0, c...  6.35 us
    ppermute x8, starting transfers between devices, swap(): return lax.ppermute(value, 'exp', [(i, i ^ exp) for i in range(experts)])  6.02 us
  transfers between devices with their start and end apart: 29, of which 13 were waited for; matrix products, arithmetic and copies ran while one was open for 1% of the time, Pallas kernels for 28%

profile of v6, /device:TPU:0, one launch (start us, length us, event | category | flops | bytes accessed | tf_op | source)
XLA Modules:
  0.0 122.6 jit_solution(14890504219243772125)
XLA Ops:
  0.6 3.1 %collective-permute-start.4 = (bf16[192,2880]{1,0:T(8,128)(2,1)}, bf16[192,2880]{1,0:T(8,128)(2,1)S(1)}, u32[]{:S(2)}, u32[]{:S(2)}) collective-permute-start(bf16[192,2880]{1,0:T(8,128)(2,1)} %bitcast.15), channel_id=1, source_target_pairs={{0,8},{8,0},{4,12},{12,4},{16,24},{24,16},{20,28},{28,20},{1,9},{9... | collective-permute-start | bytes 3317768 | tf_op jit(solution)/shard_map/ppermute | solution.py:634
  4.4 2.2 %make_rows.1 = (bf16[128,1536]{1,0:T(8,128)(2,1)}, bf16[128,1408]{1,0:T(8,128)(2,1)}, f32[4,128]{1,0:T(4,128)}) custom-call(bf16[2880,128]{1,0:T(8,128)(2,1)} %bitcast.22, f32[4,128]{1,0:T(4,128)} %bitcast.23, s32[4,128]{1,0:T(4,128)} %bitcast.18), custom_call_target="tpu_custom_call" | custom-call | flops 2000000 | bytes 6000000 | tf_op jit(solution)/shard_map/make_rows/pallas_call | solution.py:160
  12.8 2.2 %split_hidden.1 = (bf16[4,192,512]{2,1,0:T(8,128)(2,1)S(1)}, bf16[1,192,512]{2,1,0:T(8,128)(2,1)S(1)}, bf16[3,192,512]{2,1,0:T(8,128)(2,1)S(1)}) custom-call(s32[32]{0:T(128)S(1)} %dynamic-slice_bitcast_fusion.where_ref, bf16[512,1536]{1,0:T(8,128)(2,1)S(1)} %bitcast.14, bf16[128,1536]{1,0:T(8,128)(2,1)S(1)} %copy-done), custom_call_target="tpu_custom_call" | custom-call | flops 2000000 | bytes 6000000 | tf_op jit(solution)/shard_map/split_hidden/pallas_call | solution.py:251
  15.6 2.6 %collective-permute-done.1.refs_0_ = bf16[128,1536]{1,0:T(8,128)(2,1)S(1)} collective-permute-done((bf16[128,1536]{1,0:T(8,128)(2,1)}, bf16[128,1536]{1,0:T(8,128)(2,1)S(1)}, u32[]{:S(2)}, u32[]{:S(2)}) %collective-permute-start.1) | collective-permute-done | bytes 393248 | tf_op jit(solution)/shard_map/ppermute | solution.py:622
  18.7 1.8 %collective-permute-start.2 = (bf16[128,1536]{1,0:T(8,128)(2,1)S(1)}, bf16[128,1536]{1,0:T(8,128)(2,1)S(1)}, u32[]{:S(2)}, u32[]{:S(2)}) collective-permute-start(bf16[128,1536]{1,0:T(8,128)(2,1)S(1)} %hold.3.refs_1_.refs_2_), channel_id=1, source_target_pairs={{0,2},{1,3},{2,0},{3,1},{4,6},{5,7},{6,4},{7,5},{8,10},{9,11},{10,... | collective-permute-start | bytes 1179656 | tf_op jit(solution)/shard_map/ppermute | solution.py:624
  23.2 7.7 %collective-permute-done.6.refs_6_.refs_1_ = bf16[128,1408]{1,0:T(8,128)(2,1)S(1)} collective-permute-done((bf16[128,1408]{1,0:T(8,128)(2,1)S(1)}, bf16[128,1408]{1,0:T(8,128)(2,1)S(1)}, u32[]{:S(2)}, u32[]{:S(2)}) %collective-permute-start.6) | collective-permute-done | bytes 360480 | tf_op jit(solution)/shard_map/ppermute | solution.py:622
  35.2 2.2 %first_late.1.kept_ref.refs_1_ = f32[1,192,1472]{2,1,0:T(8,128)S(1)} custom-call(s32[32]{0:T(128)S(1)} %dynamic-slice_bitcast_fusion.where_ref, bf16[4,128,1536]{2,1,0:T(8,128)(2,1)S(1)} %pack_rows.2.refs_0_.refs_2_.refs_6_, bf16[4,128,1536]{2,1,0:T(8,128)(2,1)S(1)} %collective-permute-done.7.refs_1_.refs_3_.refs_7_, ...), custom_call_target="tpu_custom_call" | custom-call | flops 4000000 | bytes 12000000 | tf_op jit(solution)/shard_map/first_late/pallas_call | solution.py:304
  38.1 3.8 %collective-permute-start.15 = (bf16[192,1472]{1,0:T(8,128)(2,1)S(1)}, bf16[192,1472]{1,0:T(8,128)(2,1)S(1)}, u32[]{:S(2)}, u32[]{:S(2)}) collective-permute-start(bf16[192,1472]{1,0:T(8,128)(2,1)S(1)} %begin.2), channel_id=1, source_target_pairs={{0,8},{8,0},{4,12},{12,4},{16,24},{24,16},{20,28},{28,20},{1,9},{9... | collective-permute-start | bytes 1695752 | tf_op jit(solution)/shard_map/ppermute | solution.py:634
  44.1 6.7 %collective-permute-done.11.refs_4_.refs_6_ = bf16[128,1408]{1,0:T(8,128)(2,1)S(1)} collective-permute-done((bf16[128,1408]{1,0:T(8,128)(2,1)S(1)}, bf16[128,1408]{1,0:T(8,128)(2,1)S(1)}, u32[]{:S(2)}, u32[]{:S(2)}) %collective-permute-start.11) | collective-permute-done | bytes 360480 | tf_op jit(solution)/shard_map/ppermute | solution.py:624
  52.5 2.1 %first_early.1.kept_ref.refs_1_ = f32[1,192,1408]{2,1,0:T(8,128)S(1)} custom-call(s32[32]{0:T(128)S(1)} %dynamic-slice_bitcast_fusion.where_ref, bf16[2,128,1408]{2,1,0:T(8,128)(2,1)S(1)} %pack_rows.3.refs_0_.refs_2_, bf16[2,128,1408]{2,1,0:T(8,128)(2,1)S(1)} %collective-permute-done.8.refs_0_.refs_1_.refs_3_, ...), custom_call_target="tpu_custom_call" | custom-call | flops 4000000 | bytes 12000000 | tf_op jit(solution)/shard_map/first_early/pallas_call | solution.py:304
  57.1 2.9 %collective-permute-start.18 = (bf16[192,1408]{1,0:T(8,128)(2,1)S(1)}, bf16[192,1408]{1,0:T(8,128)(2,1)S(1)}, u32[]{:S(2)}, u32[]{:S(2)}) collective-permute-start(bf16[192,1408]{1,0:T(8,128)(2,1)S(1)} %hold.5), channel_id=1, source_target_pairs={{0,8},{8,0},{4,12},{12,4},{16,24},{24,16},{20,28},{28,20},{1,9},{9... | collective-permute-start | bytes 1622024 | tf_op jit(solution)/shard_map/ppermute | solution.py:634
  60.6 3.4 %rest_early.1.refs_2_.refs_4_.refs_3_ = f32[3,192,1408]{2,1,0:T(8,128)S(1)} custom-call(s32[32]{0:T(128)S(1)} %dynamic-slice_bitcast_fusion.where_ref, bf16[2,128,1408]{2,1,0:T(8,128)(2,1)S(1)} %pack_rows.3.refs_0_.refs_2_, bf16[2,128,1408]{2,1,0:T(8,128)(2,1)S(1)} %collective-permute-done.8.refs_0_.refs_1_.refs_3_, ...), custom_call_target="tpu_custom_call" | custom-call | flops 4000000 | bytes 12000000 | tf_op jit(solution)/shard_map/rest_early/pallas_call | solution.py:304
  64.0 3.4 %rest_late.1.refs_1_.refs_3_.refs_2_ = f32[3,192,1472]{2,1,0:T(8,128)S(1)} custom-call(s32[32]{0:T(128)S(1)} %dynamic-slice_bitcast_fusion.where_ref, bf16[4,128,1536]{2,1,0:T(8,128)(2,1)S(1)} %pack_rows.2.refs_0_.refs_2_.refs_6_, bf16[4,128,1536]{2,1,0:T(8,128)(2,1)S(1)} %collective-permute-done.7.refs_1_.refs_3_.refs_7_, ...), custom_call_target="tpu_custom_call" | custom-call | flops 4000000 | bytes 12000000 | tf_op jit(solution)/shard_map/rest_late/pallas_call | solution.py:304
  68.3 5.7 %collective-permute-start.16 = (bf16[192,2880]{1,0:T(8,128)(2,1)S(1)}, bf16[192,2880]{1,0:T(8,128)(2,1)S(1)}, u32[]{:S(2)}, u32[]{:S(2)}) collective-permute-start(bf16[192,2880]{1,0:T(8,128)(2,1)S(1)} %combine.6.refs_2_), channel_id=1, source_target_pairs={{0,8},{8,0},{4,12},{12,4},{16,24},{24,16},{20,28},{28,20},{1,9},{9... | collective-permute-start | bytes 3317768 | tf_op jit(solution)/shard_map/ppermute | solution.py:634
  75.5 4.7 %back_part.3 = (bf16[192,512]{1,0:T(8,128)(2,1)S(1)}, bf16[192,512]{1,0:T(8,128)(2,1)S(1)}, bf16[192,512]{1,0:T(8,128)(2,1)S(1)}, bf16[192,512]{1,0:T(8,128)(2,1...) custom-call(s32[32]{0:T(128)S(1)} %dynamic-slice_bitcast_fusion.where_ref, ...), custom_call_target="tpu_custom_call" | custom-call | flops 6000000 | bytes 18000000 | tf_op jit(solution)/shard_map/back_part/pallas_call | solution.py:533
  83.0 2.6 %back_part.4 = (bf16[192,512]{1,0:T(8,128)(2,1)S(1)}, bf16[192,512]{1,0:T(8,128)(2,1)S(1)}, f32[8,1024]{1,0:T(8,128)S(1)}) custom-call(s32[32]{0:T(128)S(1)} %dynamic-slice_bitcast_fusion.where_ref, bf16[4,128,1536]{2,1,0:T(8,128)(2,1)S(1)} %pack_rows.2.refs_0_.refs_2_.refs_6_, bf16[4,128,1536]{2,1,0:T(8,128)(2,1)S(1)} %collective-permute-done.7.refs_1_.refs_3_.refs_7_, ...), custom_call_target="tpu_custom_call" | custom-call | flops 6000000 | bytes 18000000 | tf_op jit(solution)/shard_map/back_part/pallas_call | solution.py:533
  85.7 2.5 %collective-permute-done.20.refs_5_.refs_1_.refs_4_ = bf16[192,512]{1,0:T(8,128)(2,1)S(1)} collective-permute-done((bf16[192,512]{1,0:T(8,128)(2,1)S(1)}, bf16[192,512]{1,0:T(8,128)(2,1)S(1)}, u32[]{:S(2)}, u32[]{:S(2)}) %collective-permute-start.20) | collective-permute-done | bytes 196640 | tf_op jit(solution)/shard_map/ppermute | solution.py:622
  88.1 3.5 %collective-permute-done.21.refs_6_.refs_3_.refs_5_ = bf16[192,512]{1,0:T(8,128)(2,1)S(1)} collective-permute-done((bf16[192,512]{1,0:T(8,128)(2,1)S(1)}, bf16[192,512]{1,0:T(8,128)(2,1)S(1)}, u32[]{:S(2)}, u32[]{:S(2)}) %collective-permute-start.21) | collective-permute-done | bytes 196640 | tf_op jit(solution)/shard_map/ppermute | solution.py:622
  91.6 2.1 %collective-permute-done.22.refs_7_.refs_5_.refs_6_ = bf16[192,512]{1,0:T(8,128)(2,1)S(1)} collective-permute-done((bf16[192,512]{1,0:T(8,128)(2,1)S(1)}, bf16[192,512]{1,0:T(8,128)(2,1)S(1)}, u32[]{:S(2)}, u32[]{:S(2)}) %collective-permute-start.22) | collective-permute-done | bytes 196640 | tf_op jit(solution)/shard_map/ppermute | solution.py:622
  94.6 3.1 %collective-permute-start.26 = (bf16[192,2880]{1,0:T(8,128)(2,1)S(1)}, bf16[192,2880]{1,0:T(8,128)(2,1)S(1)}, u32[]{:S(2)}, u32[]{:S(2)}) collective-permute-start(bf16[192,2880]{1,0:T(8,128)(2,1)S(1)} %combine.8.refs_15_), channel_id=1, source_target_pairs={{0,8},{8,0},{4,12},{12,4},{16,24},{24,16},{20,28},{28,20},{1,9},{9... | collective-permute-start | bytes 3317768 | tf_op jit(solution)/shard_map/ppermute | solution.py:634
  99.9 2.7 %back_part.5 = (bf16[192,512]{1,0:T(8,128)(2,1)S(1)}, bf16[192,512]{1,0:T(8,128)(2,1)S(1)}, f32[8,1024]{1,0:T(8,128)S(1)}) custom-call(s32[32]{0:T(128)S(1)} %dynamic-slice_bitcast_fusion.where_ref, bf16[4,128,1536]{2,1,0:T(8,128)(2,1)S(1)} %pack_rows.2.refs_0_.refs_2_.refs_6_, bf16[4,128,1536]{2,1,0:T(8,128)(2,1)S(1)} %collective-permute-done.7.refs_1_.refs_3_.refs_7_, ...), custom_call_target="tpu_custom_call" | custom-call | flops 6000000 | bytes 18000000 | tf_op jit(solution)/shard_map/back_part/pallas_call | solution.py:533
  107.8 6.3 %all_to_all.11 = f32[4,1,128]{2,1,0:T(1,128)S(1)} all-to-all(f32[4,1,128]{2,1,0:T(1,128)S(1)} %add_bitcast_fusion), channel_id=1, replica_groups=mesh['ctx'=8,'exp'=4] {'exp'}, dimensions={0} | all-to-all | bytes 4096 | tf_op jit(solution)/shard_map/all_to_all | solution.py:722
  114.8 2.9 %join_hidden.1 = bf16[512,1536]{1,0:T(8,128)(2,1)} custom-call(s32[32]{0:T(128)S(1)} %dynamic-slice_bitcast_fusion.where_ref, bf16[192,512]{1,0:T(8,128)(2,1)S(1)} %get-tuple-element.36.refs_0_, bf16[192,512]{1,0:T(8,128)(2,1)S(1)} %collective-permute-done.20.refs_5_.refs_1_.refs_4_, bf16[192,512]{1,0:T(8,128)(2,1)S(1)} %get-tuple-element.37.refs_2_, ...), custom_call_target="tpu_custom_call" | custom-call | flops 2000000 | bytes 6000000 | tf_op jit(solution)/shard_map/join_hidden/pallas_call | solution.py:572
  117.7 3.4 %collective-permute-done.26.refs_0_ = bf16[192,2880]{1,0:T(8,128)(2,1)S(1)} collective-permute-done((bf16[192,2880]{1,0:T(8,128)(2,1)S(1)}, bf16[192,2880]{1,0:T(8,128)(2,1)S(1)}, u32[]{:S(2)}, u32[]{:S(2)}) %collective-permute-start.26) | collective-permute-done | bytes 1105952 | tf_op jit(solution)/shard_map/ppermute | solution.py:634
  (76 shorter events, 38.3 us)
Async XLA Ops:
  0.6 30.3 %collective-permute-start.4 = (bf16[192,2880]{1,0:T(8,128)(2,1)}, bf16[192,2880]{1,0:T(8,128)(2,1)S(1)}, u32[]{:S(2)}, u32[]{:S(2)}) collective-permute-start(bf16[192,2880]{1,0:T(8,128)(2,1)} %bitcast.15), channel_id=1, source_target_pairs={{0,8},{8,0},{4,12},{12,4},{16,24},{24,16},{20,28},{28,20},{1,9},{9... | collective-permute-start | bytes 3317768 | tf_op jit(solution)/shard_map/ppermute | solution.py:634
  3.7 27.2 %collective-permute-start.3 = (bf16[192,2880]{1,0:T(8,128)(2,1)}, bf16[192,2880]{1,0:T(8,128)(2,1)S(1)}, u32[]{:S(2)}, u32[]{:S(2)}) collective-permute-start(bf16[192,2880]{1,0:T(8,128)(2,1)} %bitcast.16), channel_id=1, source_target_pairs={{8,16},{16,8},{12,20},{20,12},{9,17},{17,9},{13,21},{21,13},{10,18... | collective-permute-start | bytes 3317768 | tf_op jit(solution)/shard_map/ppermute | solution.py:634
  6.6 11.6 %collective-permute-start.1 = (bf16[128,1536]{1,0:T(8,128)(2,1)}, bf16[128,1536]{1,0:T(8,128)(2,1)S(1)}, u32[]{:S(2)}, u32[]{:S(2)}) collective-permute-start(bf16[128,1536]{1,0:T(8,128)(2,1)} %get-tuple-element.25.refs_0_), channel_id=1, source_target_pairs={{0,4},{4,0},{8,12},{12,8},{16,20},{20,16},{24,28},{28,24},{1,5},{5... | collective-permute-start | bytes 1179656 | tf_op jit(solution)/shard_map/ppermute | solution.py:622
  8.2 10.5 %collective-permute-start = (bf16[128,1536]{1,0:T(8,128)(2,1)}, bf16[128,1536]{1,0:T(8,128)(2,1)S(1)}, u32[]{:S(2)}, u32[]{:S(2)}) collective-permute-start(bf16[128,1536]{1,0:T(8,128)(2,1)} %get-tuple-element.25.refs_0_), channel_id=1, source_target_pairs={{0,2},{1,3},{2,0},{3,1},{4,6},{5,7},{6,4},{7,5},{8,10},{9,11},{10,... | collective-permute-start | bytes 1179656 | tf_op jit(solution)/shard_map/ppermute | solution.py:624
  18.7 12.2 %collective-permute-start.2 = (bf16[128,1536]{1,0:T(8,128)(2,1)S(1)}, bf16[128,1536]{1,0:T(8,128)(2,1)S(1)}, u32[]{:S(2)}, u32[]{:S(2)}) collective-permute-start(bf16[128,1536]{1,0:T(8,128)(2,1)S(1)} %hold.3.refs_1_.refs_2_), channel_id=1, source_target_pairs={{0,2},{1,3},{2,0},{3,1},{4,6},{5,7},{6,4},{7,5},{8,10},{9,11},{10,... | collective-permute-start | bytes 1179656 | tf_op jit(solution)/shard_map/ppermute | solution.py:624
  21.7 9.2 %collective-permute-start.6 = (bf16[128,1408]{1,0:T(8,128)(2,1)S(1)}, bf16[128,1408]{1,0:T(8,128)(2,1)S(1)}, u32[]{:S(2)}, u32[]{:S(2)}) collective-permute-start(bf16[128,1408]{1,0:T(8,128)(2,1)S(1)} %hold.4.refs_0_), channel_id=1, source_target_pairs={{0,4},{4,0},{8,12},{12,8},{16,20},{20,16},{24,28},{28,24},{1,5},{5... | collective-permute-start | bytes 1081352 | tf_op jit(solution)/shard_map/ppermute | solution.py:622
  32.7 11.3 %collective-permute-start.9 = (bf16[128,1408]{1,0:T(8,128)(2,1)S(1)}, bf16[128,1408]{1,0:T(8,128)(2,1)S(1)}, u32[]{:S(2)}, u32[]{:S(2)}) collective-permute-start(bf16[128,1408]{1,0:T(8,128)(2,1)S(1)} %hold.4.refs_0_), channel_id=1, source_target_pairs={{0,2},{1,3},{2,0},{3,1},{4,6},{5,7},{6,4},{7,5},{8,10},{9,11},{10,... | collective-permute-start | bytes 1081352 | tf_op jit(solution)/shard_map/ppermute | solution.py:624
  34.0 16.8 %collective-permute-start.11 = (bf16[128,1408]{1,0:T(8,128)(2,1)S(1)}, bf16[128,1408]{1,0:T(8,128)(2,1)S(1)}, u32[]{:S(2)}, u32[]{:S(2)}) collective-permute-start(bf16[128,1408]{1,0:T(8,128)(2,1)S(1)} %collective-permute-done.6.refs_6_.refs_1_), channel_id=1, source_target_pairs={{0,2},{1,3},{2,0},{3,1},{4,6},{5,7},{6,4},{7,5},{8,10},{9,11},{10,... | collective-permute-start | bytes 1081352 | tf_op jit(solution)/shard_map/ppermute | solution.py:624
  38.1 17.5 %collective-permute-start.15 = (bf16[192,1472]{1,0:T(8,128)(2,1)S(1)}, bf16[192,1472]{1,0:T(8,128)(2,1)S(1)}, u32[]{:S(2)}, u32[]{:S(2)}) collective-permute-start(bf16[192,1472]{1,0:T(8,128)(2,1)S(1)} %begin.2), channel_id=1, source_target_pairs={{0,8},{8,0},{4,12},{12,4},{16,24},{24,16},{20,28},{28,20},{1,9},{9... | collective-permute-start | bytes 1695752 | tf_op jit(solution)/shard_map/ppermute | solution.py:634
  41.9 15.1 %collective-permute-start.13 = (bf16[3,192,512]{2,1,0:T(8,128)(2,1)S(1)}, bf16[3,192,512]{2,1,0:T(8,128)(2,1)S(1)}, u32[]{:S(2)}, u32[]{:S(2)}) collective-permute-start(bf16[3,192,512]{2,1,0:T(8,128)(2,1)S(1)} %get-tuple-element.29), channel_id=1, source_target_pairs={{0,4},{4,0},{8,12},{12,8},{16,20},{20,16},{24,28},{28,24},{1,5},{5... | collective-permute-start | bytes 1769480 | tf_op jit(solution)/shard_map/ppermute | solution.py:622
  43.3 24.1 %collective-permute-start.14 = (bf16[192,2880]{1,0:T(8,128)(2,1)S(1)}, bf16[192,2880]{1,0:T(8,128)(2,1)S(1)}, u32[]{:S(2)}, u32[]{:S(2)}) collective-permute-start(bf16[192,2880]{1,0:T(8,128)(2,1)S(1)} %collective-permute-done.4.refs_5_.refs_12_), channel_id=1, source_target_pairs={{8,16},{16,8},{12,20},{20,12},{9,17},{17,9},{13,21},{21,13},{10,18... | collective-permute-start | bytes 3317768 | tf_op jit(solution)/shard_map/ppermute | solution.py:634
  44.0 6.8 %collective-permute-start.10 = (bf16[128,1408]{1,0:T(8,128)(2,1)S(1)}, bf16[128,1408]{1,0:T(8,128)(2,1)S(1)}, u32[]{:S(2)}, u32[]{:S(2)}) collective-permute-start(bf16[128,1408]{1,0:T(8,128)(2,1)S(1)} %collective-permute-done.9.refs_2_.refs_4_), channel_id=1, source_target_pairs={{0,1},{1,0},{2,3},{3,2},{4,5},{5,4},{6,7},{7,6},{8,9},{9,8},{10,11... | collective-permute-start | bytes 1081352 | tf_op jit(solution)/shard_map/ppermute | solution.py:624
  57.1 16.9 %collective-permute-start.18 = (bf16[192,1408]{1,0:T(8,128)(2,1)S(1)}, bf16[192,1408]{1,0:T(8,128)(2,1)S(1)}, u32[]{:S(2)}, u32[]{:S(2)}) collective-permute-start(bf16[192,1408]{1,0:T(8,128)(2,1)S(1)} %hold.5), channel_id=1, source_target_pairs={{0,8},{8,0},{4,12},{12,4},{16,24},{24,16},{20,28},{28,20},{1,9},{9... | collective-permute-start | bytes 1622024 | tf_op jit(solution)/shard_map/ppermute | solution.py:634
  59.9 22.4 %collective-permute-start.17 = (bf16[192,1472]{1,0:T(8,128)(2,1)S(1)}, bf16[192,1472]{1,0:T(8,128)(2,1)S(1)}, u32[]{:S(2)}, u32[]{:S(2)}) collective-permute-start(bf16[192,1472]{1,0:T(8,128)(2,1)S(1)} %combine.5.refs_6_.refs_10_), channel_id=1, source_target_pairs={{8,16},{16,8},{12,20},{20,12},{9,17},{17,9},{13,21},{21,13},{10,18... | collective-permute-start | bytes 1695752 | tf_op jit(solution)/shard_map/ppermute | solution.py:634
  68.3 29.4 %collective-permute-start.16 = (bf16[192,2880]{1,0:T(8,128)(2,1)S(1)}, bf16[192,2880]{1,0:T(8,128)(2,1)S(1)}, u32[]{:S(2)}, u32[]{:S(2)}) collective-permute-start(bf16[192,2880]{1,0:T(8,128)(2,1)S(1)} %combine.6.refs_2_), channel_id=1, source_target_pairs={{0,8},{8,0},{4,12},{12,4},{16,24},{24,16},{20,28},{28,20},{1,9},{9... | collective-permute-start | bytes 3317768 | tf_op jit(solution)/shard_map/ppermute | solution.py:634
  74.6 19.1 %collective-permute-start.19 = (bf16[192,1408]{1,0:T(8,128)(2,1)S(1)}, bf16[192,1408]{1,0:T(8,128)(2,1)S(1)}, u32[]{:S(2)}, u32[]{:S(2)}) collective-permute-start(bf16[192,1408]{1,0:T(8,128)(2,1)S(1)} %combine.7.refs_14_.refs_15_), channel_id=1, source_target_pairs={{8,16},{16,8},{12,20},{20,12},{9,17},{17,9},{13,21},{21,13},{10,18... | collective-permute-start | bytes 1622024 | tf_op jit(solution)/shard_map/ppermute | solution.py:634
  80.2 7.9 %collective-permute-start.20 = (bf16[192,512]{1,0:T(8,128)(2,1)S(1)}, bf16[192,512]{1,0:T(8,128)(2,1)S(1)}, u32[]{:S(2)}, u32[]{:S(2)}) collective-permute-start(bf16[192,512]{1,0:T(8,128)(2,1)S(1)} %get-tuple-element.32), channel_id=1, source_target_pairs={{0,4},{4,0},{8,12},{12,8},{16,20},{20,16},{24,28},{28,24},{1,5},{5... | collective-permute-start | bytes 589832 | tf_op jit(solution)/shard_map/ppermute | solution.py:622
  81.0 10.6 %collective-permute-start.21 = (bf16[192,512]{1,0:T(8,128)(2,1)S(1)}, bf16[192,512]{1,0:T(8,128)(2,1)S(1)}, u32[]{:S(2)}, u32[]{:S(2)}) collective-permute-start(bf16[192,512]{1,0:T(8,128)(2,1)S(1)} %get-tuple-element.33), channel_id=1, source_target_pairs={{0,4},{4,0},{8,12},{12,8},{16,20},{20,16},{24,28},{28,24},{1,5},{5... | collective-permute-start | bytes 589832 | tf_op jit(solution)/shard_map/ppermute | solution.py:622
  82.3 11.4 %collective-permute-start.22 = (bf16[192,512]{1,0:T(8,128)(2,1)S(1)}, bf16[192,512]{1,0:T(8,128)(2,1)S(1)}, u32[]{:S(2)}, u32[]{:S(2)}) collective-permute-start(bf16[192,512]{1,0:T(8,128)(2,1)S(1)} %get-tuple-element.34), channel_id=1, source_target_pairs={{0,4},{4,0},{8,12},{12,8},{16,20},{20,16},{24,28},{28,24},{1,5},{5... | collective-permute-start | bytes 589832 | tf_op jit(solution)/shard_map/ppermute | solution.py:622
  94.6 26.5 %collective-permute-start.26 = (bf16[192,2880]{1,0:T(8,128)(2,1)S(1)}, bf16[192,2880]{1,0:T(8,128)(2,1)S(1)}, u32[]{:S(2)}, u32[]{:S(2)}) collective-permute-start(bf16[192,2880]{1,0:T(8,128)(2,1)S(1)} %combine.8.refs_15_), channel_id=1, source_target_pairs={{0,8},{8,0},{4,12},{12,4},{16,24},{24,16},{20,28},{28,20},{1,9},{9... | collective-permute-start | bytes 3317768 | tf_op jit(solution)/shard_map/ppermute | solution.py:634
  98.5 19.2 %collective-permute-start.27 = (bf16[192,1472]{1,0:T(8,128)(2,1)S(1)}, bf16[192,1472]{1,0:T(8,128)(2,1)S(1)}, u32[]{:S(2)}, u32[]{:S(2)}) collective-permute-start(bf16[192,1472]{1,0:T(8,128)(2,1)S(1)} %get-tuple-element.43), channel_id=1, source_target_pairs={{8,16},{16,8},{12,20},{20,12},{9,17},{17,9},{13,21},{21,13},{10,18... | collective-permute-start | bytes 1695752 | tf_op jit(solution)/shard_map/ppermute | solution.py:634
  99.2 18.5 %collective-permute-start.28 = (bf16[192,1408]{1,0:T(8,128)(2,1)S(1)}, bf16[192,1408]{1,0:T(8,128)(2,1)S(1)}, u32[]{:S(2)}, u32[]{:S(2)}) collective-permute-start(bf16[192,1408]{1,0:T(8,128)(2,1)S(1)} %get-tuple-element.44), channel_id=1, source_target_pairs={{8,16},{16,8},{12,20},{20,12},{9,17},{17,9},{13,21},{21,13},{10,18... | collective-permute-start | bytes 1622024 | tf_op jit(solution)/shard_map/ppermute | solution.py:634
  104.1 10.6 %collective-permute-start.24 = (bf16[192,512]{1,0:T(8,128)(2,1)S(1)}, bf16[192,512]{1,0:T(8,128)(2,1)S(1)}, u32[]{:S(2)}, u32[]{:S(2)}) collective-permute-start(bf16[192,512]{1,0:T(8,128)(2,1)S(1)} %get-tuple-element.40), channel_id=1, source_target_pairs={{0,4},{4,0},{8,12},{12,8},{16,20},{20,16},{24,28},{28,24},{1,5},{5... | collective-permute-start | bytes 589832 | tf_op jit(solution)/shard_map/ppermute | solution.py:622
  106.2 8.5 %collective-permute-start.25 = (bf16[192,512]{1,0:T(8,128)(2,1)S(1)}, bf16[192,512]{1,0:T(8,128)(2,1)S(1)}, u32[]{:S(2)}, u32[]{:S(2)}) collective-permute-start(bf16[192,512]{1,0:T(8,128)(2,1)S(1)} %get-tuple-element.42), channel_id=1, source_target_pairs={{0,4},{4,0},{8,12},{12,8},{16,20},{20,16},{24,28},{28,24},{1,5},{5... | collective-permute-start | bytes 589832 | tf_op jit(solution)/shard_map/ppermute | solution.py:622
  (12 other events, 85.2 us)

commit v7 on v6

--- a/solution.py
+++ b/solution.py
@@ -325,14 +325,15 @@
     slot = where_ref[table[key]]
     coming = refs[: counts[0]]
     outs = refs[len(refs) - counts[2] :]
-    model = sum(ref.shape[1] for ref in coming)
+    model = sum(ref.shape[1] for ref in outs)
     spans = [(cut, model), (0, cut)] if cut else [(0, model)]
     for chunk, (start, stop) in enumerate(spans):
-        if counts[0] == 1:
-            total = coming[0][:, start:stop]
+        if counts[0] == 0:
+            total = jnp.zeros((outs[0].shape[0], stop - start), f32)
+        elif counts[0] == 1:
+            total = coming[0][:, start:stop].astype(f32)
         else:
-            total = coming[chunk][...]
-        total = total.astype(f32)
+            total = coming[chunk][...].astype(f32)
         for number, side in enumerate(sides):
             flag = slot == 0 if side == "first" else slot > 0
             total = total + jnp.where(flag, refs[counts[0] + len(spans) * number + chunk][0], 0.0)
@@ -344,8 +345,8 @@
 
 
 def combine(table, where, coming, first, rest, turn, name, used, cut, after, chunked=False):
-    units = coming[0].shape[0]
-    model = sum(part.shape[1] for part in coming)
+    units = first[0].shape[1]
+    model = sum(part.shape[2] for part in first)
     block = rows_of(units)
     column = table["block", turn, name]
     sides, operands, specs = [], [], []
@@ -625,12 +626,12 @@
         pairs = [(c * experts + e, (c ^ x) * experts + (e ^ exp)) for c in range(groups) for e in range(experts)]
         return lax.ppermute(value, ("ctx", "exp"), pairs)
 
-    def swap_z(value, name):
+    def swap_z(value, name, senders=range(depth)):
         first = "AB".index(name)
         pairs = []
-        for z in range(first, depth - 1, 2):
-            for x in range(2):
-                pairs += [(2 * z + x, 2 * z + 2 + x), (2 * z + 2 + x, 2 * z + x)]
+        for low in range(first, depth - 1, 2):
+            for z, other in ((low, low + 1), (low + 1, low)):
+                pairs += [(2 * z + x, 2 * other + x) for x in range(2) if z in senders]
         return lax.ppermute(value, "ctx", pairs)
 
     got = {(0, "own"): [w_down[0]]}
@@ -674,27 +675,38 @@
         products(table, where, early_rows, late_rows, own, other_first, 0, model, cut, "first_early", [])
     )
     sent.append(begin(table, where, got[1, "B"][0], first[1], 0, [got[2, "A"][0]]))
-    got[2, "A"].append(swap_z(hold((sent[1],), [other_rest])[0], "A"))
-
-    halves, all_choices = [], []
+    sent[1:] = hold((sent[1],), [other_rest])
+    got[2, "A"].append(swap_z(sent[1], "A"))
+
+    halves, all_choices, weights_of = [], [], {}
     only_first = max(uses[3, "B"]) <= 0
 
     def backprop(choices, before, guard, after):
         *outs, sums = back_part(
-            table, where, late_rows, early_rows, own, other_first, other_rest, choices, got, before, guard, after, model
+            table, where, late_rows, early_rows, own, other_first, other_rest, choices,
+            {**got, **weights_of}, before, guard, after, model,
         )
         for mine, theirs in zip(outs[::2], outs[1::2]):
             halves.extend([mine, swap(theirs, 1, 0)])
         all_choices.extend(choices)
         return sums
 
-    def pass_on(turn, name, after, chunk=None):
+    def pass_on(turn, name, after, chunk=None, waited=()):
         coming = got[turn - 1, "B" if name == "A" else "A"]
         parts, start, chunked = (first, rest), cut, turn == depth and name == "B"
+        used = uses[turn, name]
+        senders = [z for z in range(depth) if used[z] >= 0] if turn == depth - 1 else range(depth)
+        others = [z for z in range(depth) if z not in senders]
+        if others and chunk is None and len(coming) == 1:
+            weights_of[turn, name] = [swap_z(coming[0], name, others)]
+            ends = {0, depth - 1} if name == "A" else set()
+            coming = [] if set(senders) <= ends else coming
         if chunk is not None:
             coming, parts, start = [coming[chunk]], (first[chunk:][:1], rest[chunk:][:1]), 0
-        values = combine(table, where, coming, *parts, turn, name, uses[turn, name], start, after, chunked)
-        got.setdefault((turn, name), []).extend(swap_z(value, name) for value in values)
+        values = list(combine(table, where, coming, *parts, turn, name, used, start, after, chunked))
+        if waited:
+            values[1:] = hold(values[1:], list(waited))
+        got.setdefault((turn, name), []).extend(swap_z(value, name, senders) for value in values)
         return values[-1]
 
     def choices_of(turn):
@@ -715,7 +727,8 @@
     for turn in range(2, depth):
         choices = choices_of(turn)
         if turn > 2:
-            pass_on(turn + 1, "B", [sums, *sooner])
+            waited = [array for key in ((turn, "A"), (turn, "B")) for array in weights_of.get(key, [])]
+            pass_on(turn + 1, "B", [sums, *sooner], waited=waited)
             marker = pass_on(turn + 1, "A", [sums, *sooner])
         sums = backprop(choices, sums, len(choices) == 1, [marker])
     slot_grad = sums[0:1, :slots] + swap(sums[0:1, slots:], 1, 0)

time: 125 us -> 127 us (1.016); the launches traced: 123 us -> 126 us
  waiting for transfers between devices: 34.9 us -> 37.3 us
  starting transfers between devices: 40.3 us -> 41.6 us
    ppermute x10, waiting for transfers between devices: 21.1 us -> 22.5 us  [swap(): return lax.ppermute(value, 'ctx', [(i, i ^ x) for i in range(groups)])]
    ppermute x11 -> x12, waiting for transfers between devices: 4.43 us -> 5.35 us  [swap_z(): return lax.ppermute(value, 'ctx', pairs)]
    ppermute x11 -> x12, starting transfers between devices: 22.9 us -> 23.6 us  [swap_z(): return lax.ppermute(value, 'ctx', pairs)]
  transfers between devices with their start and end apart: 29 -> 30, of which waited for: 13 -> 14; matrix products, arithmetic and copies ran while one was open for 1% -> 1% of each run, Pallas kernels for 28% -> 27%
where the time goes in v7:
time: 127 us; the launch traced here: 126 us
  starting transfers between devices  41.6 us (33%)
  waiting for transfers between devices  37.3 us (29%)
  Pallas kernels  36.9 us (29%)
  blocking collectives  6.41 us (5%)
  local copies, waits for them, and re-layouts  3.12 us (2%)
    ppermute x12, starting transfers between devices, swap_z(): return lax.ppermute(value, 'ctx', pairs)  23.6 us
    ppermute x10, waiting for transfers between devices, swap(): return lax.ppermute(value, 'ctx', [(i, i ^ x) for i in range(groups)])  22.5 us
    ppermute x10, starting transfers between devices, swap(): return lax.ppermute(value, 'ctx', [(i, i ^ x) for i in range(groups)])  12 us
    pallas_call x4, Pallas kernels, products(): pl.pallas_call(functools.partial(products_kernel, table, model, counts, p...  11.1 us
    pallas_call x3, Pallas kernels, back_part(): pl.pallas_call(functools.partial(back_kernel, table, model, cut, counts,...  9.96 us
    ppermute x8, waiting for transfers between devices, swap(): return lax.ppermute(value, 'exp', [(i, i ^ exp) for i in range(experts)])  9.37 us
    all_to_all x1, blocking collectives, per_device_full(): lax.all_to_all(slot_grad.reshape(experts, tokens), 'exp', split_axis=0, c...  6.41 us
    ppermute x8, starting transfers between devices, swap(): return lax.ppermute(value, 'exp', [(i, i ^ exp) for i in range(experts)])  6.02 us
  transfers between devices with their start and end apart: 30, of which 14 were waited for; matrix products, arithmetic and copies ran while one was open for 1% of the time, Pallas kernels for 27%

profile of v7, /device:TPU:0, one launch (start us, length us, event | category | flops | bytes accessed | tf_op | source)
XLA Modules:
  0.0 126.2 jit_solution(17221172864033783353)
XLA Ops:
  0.6 3.1 %collective-permute-start.4 = (bf16[192,2880]{1,0:T(8,128)(2,1)}, bf16[192,2880]{1,0:T(8,128)(2,1)S(1)}, u32[]{:S(2)}, u32[]{:S(2)}) collective-permute-start(bf16[192,2880]{1,0:T(8,128)(2,1)} %bitcast.15), channel_id=1, source_target_pairs={{0,8},{4,12},{8,0},{12,4},{16,24},{20,28},{24,16},{28,20},{1,9},{5... | collective-permute-start | bytes 3317768 | tf_op jit(solution)/shard_map/ppermute | solution.py:635
  4.4 2.2 %make_rows.1 = (bf16[128,1536]{1,0:T(8,128)(2,1)}, bf16[128,1408]{1,0:T(8,128)(2,1)}, f32[4,128]{1,0:T(4,128)}) custom-call(bf16[2880,128]{1,0:T(8,128)(2,1)} %bitcast.22, f32[4,128]{1,0:T(4,128)} %bitcast.23, s32[4,128]{1,0:T(4,128)} %bitcast.18), custom_call_target="tpu_custom_call" | custom-call | flops 2000000 | bytes 6000000 | tf_op jit(solution)/shard_map/make_rows/pallas_call | solution.py:160
  12.8 2.2 %split_hidden.1 = (bf16[4,192,512]{2,1,0:T(8,128)(2,1)S(1)}, bf16[1,192,512]{2,1,0:T(8,128)(2,1)S(1)}, bf16[3,192,512]{2,1,0:T(8,128)(2,1)S(1)}) custom-call(s32[32]{0:T(128)S(1)} %dynamic-slice_bitcast_fusion.where_ref, bf16[512,1536]{1,0:T(8,128)(2,1)S(1)} %bitcast.14, bf16[128,1536]{1,0:T(8,128)(2,1)S(1)} %copy-done), custom_call_target="tpu_custom_call" | custom-call | flops 2000000 | bytes 6000000 | tf_op jit(solution)/shard_map/split_hidden/pallas_call | solution.py:251
  15.6 2.6 %collective-permute-done.1.refs_0_ = bf16[128,1536]{1,0:T(8,128)(2,1)S(1)} collective-permute-done((bf16[128,1536]{1,0:T(8,128)(2,1)}, bf16[128,1536]{1,0:T(8,128)(2,1)S(1)}, u32[]{:S(2)}, u32[]{:S(2)}) %collective-permute-start.1) | collective-permute-done | bytes 393248 | tf_op jit(solution)/shard_map/ppermute | solution.py:623
  18.7 1.8 %collective-permute-start.2 = (bf16[128,1536]{1,0:T(8,128)(2,1)S(1)}, bf16[128,1536]{1,0:T(8,128)(2,1)S(1)}, u32[]{:S(2)}, u32[]{:S(2)}) collective-permute-start(bf16[128,1536]{1,0:T(8,128)(2,1)S(1)} %hold.4.refs_1_.refs_2_), channel_id=1, source_target_pairs={{0,2},{1,3},{2,0},{3,1},{4,6},{5,7},{6,4},{7,5},{8,10},{9,11},{10,... | collective-permute-start | bytes 1179656 | tf_op jit(solution)/shard_map/ppermute | solution.py:625
  23.2 7.7 %collective-permute-done.6.refs_6_.refs_1_ = bf16[128,1408]{1,0:T(8,128)(2,1)S(1)} collective-permute-done((bf16[128,1408]{1,0:T(8,128)(2,1)S(1)}, bf16[128,1408]{1,0:T(8,128)(2,1)S(1)}, u32[]{:S(2)}, u32[]{:S(2)}) %collective-permute-start.6) | collective-permute-done | bytes 360480 | tf_op jit(solution)/shard_map/ppermute | solution.py:623
  35.2 2.2 %first_late.1.kept_ref.refs_1_ = f32[1,192,1472]{2,1,0:T(8,128)S(1)} custom-call(s32[32]{0:T(128)S(1)} %dynamic-slice_bitcast_fusion.where_ref, bf16[4,128,1536]{2,1,0:T(8,128)(2,1)S(1)} %pack_rows.2.refs_0_.refs_2_.refs_6_, bf16[4,128,1536]{2,1,0:T(8,128)(2,1)S(1)} %collective-permute-done.7.refs_1_.refs_3_.refs_7_, ...), custom_call_target="tpu_custom_call" | custom-call | flops 4000000 | bytes 12000000 | tf_op jit(solution)/shard_map/first_late/pallas_call | solution.py:304
  38.1 3.8 %collective-permute-start.16 = (bf16[192,1472]{1,0:T(8,128)(2,1)S(1)}, bf16[192,1472]{1,0:T(8,128)(2,1)S(1)}, u32[]{:S(2)}, u32[]{:S(2)}) collective-permute-start(bf16[192,1472]{1,0:T(8,128)(2,1)S(1)} %begin.2), channel_id=1, source_target_pairs={{0,8},{4,12},{8,0},{12,4},{16,24},{20,28},{24,16},{28,20},{1,9},{5... | collective-permute-start | bytes 1695752 | tf_op jit(solution)/shard_map/ppermute | solution.py:635
  44.1 6.7 %collective-permute-done.11.refs_4_.refs_6_ = bf16[128,1408]{1,0:T(8,128)(2,1)S(1)} collective-permute-done((bf16[128,1408]{1,0:T(8,128)(2,1)S(1)}, bf16[128,1408]{1,0:T(8,128)(2,1)S(1)}, u32[]{:S(2)}, u32[]{:S(2)}) %collective-permute-start.11) | collective-permute-done | bytes 360480 | tf_op jit(solution)/shard_map/ppermute | solution.py:625
  50.8 1.7 %collective-permute-done.12.refs_5_.refs_7_ = bf16[128,1408]{1,0:T(8,128)(2,1)S(1)} collective-permute-done((bf16[128,1408]{1,0:T(8,128)(2,1)S(1)}, bf16[128,1408]{1,0:T(8,128)(2,1)S(1)}, u32[]{:S(2)}, u32[]{:S(2)}) %collective-permute-start.12) | collective-permute-done | bytes 360480 | tf_op jit(solution)/shard_map/ppermute | solution.py:625
  52.5 2.1 %first_early.1.kept_ref.refs_1_ = f32[1,192,1408]{2,1,0:T(8,128)S(1)} custom-call(s32[32]{0:T(128)S(1)} %dynamic-slice_bitcast_fusion.where_ref, bf16[2,128,1408]{2,1,0:T(8,128)(2,1)S(1)} %pack_rows.3.refs_0_.refs_2_, bf16[2,128,1408]{2,1,0:T(8,128)(2,1)S(1)} %collective-permute-done.8.refs_0_.refs_1_.refs_3_, ...), custom_call_target="tpu_custom_call" | custom-call | flops 4000000 | bytes 12000000 | tf_op jit(solution)/shard_map/first_early/pallas_call | solution.py:304
  57.0 2.2 %collective-permute-start.18 = (bf16[192,1408]{1,0:T(8,128)(2,1)S(1)}, bf16[192,1408]{1,0:T(8,128)(2,1)S(1)}, u32[]{:S(2)}, u32[]{:S(2)}) collective-permute-start(bf16[192,1408]{1,0:T(8,128)(2,1)S(1)} %hold.6.refs_2_), channel_id=1, source_target_pairs={{0,8},{4,12},{8,0},{12,4},{16,24},{20,28},{24,16},{28,20},{1,9},{5... | collective-permute-start | bytes 1622024 | tf_op jit(solution)/shard_map/ppermute | solution.py:635
  60.6 3.4 %rest_early.1.refs_1_.refs_3_.refs_2_.refs_4_ = f32[3,192,1408]{2,1,0:T(8,128)S(1)} custom-call(s32[32]{0:T(128)S(1)} %dynamic-slice_bitcast_fusion.where_ref, bf16[2,128,1408]{2,1,0:T(8,128)(2,1)S(1)} %pack_rows.3.refs_0_.refs_2_, bf16[2,128,1408]{2,1,0:T(8,128)(2,1)S(1)} %collective-permute-done.8.refs_0_.refs_1_.refs_3_, ...), custom_call_target="tpu_custom_call" | custom-call | flops 4000000 | bytes 12000000 | tf_op jit(solution)/shard_map/rest_early/pallas_call | solution.py:304
  64.0 3.4 %rest_late.1.refs_0_.refs_2_.refs_1_.refs_3_ = f32[3,192,1472]{2,1,0:T(8,128)S(1)} custom-call(s32[32]{0:T(128)S(1)} %dynamic-slice_bitcast_fusion.where_ref, bf16[4,128,1536]{2,1,0:T(8,128)(2,1)S(1)} %pack_rows.2.refs_0_.refs_2_.refs_6_, bf16[4,128,1536]{2,1,0:T(8,128)(2,1)S(1)} %collective-permute-done.7.refs_1_.refs_3_.refs_7_, ...), custom_call_target="tpu_custom_call" | custom-call | flops 4000000 | bytes 12000000 | tf_op jit(solution)/shard_map/rest_late/pallas_call | solution.py:304
  68.2 4.0 %collective-permute-start.27 = (bf16[192,2880]{1,0:T(8,128)(2,1)S(1)}, bf16[192,2880]{1,0:T(8,128)(2,1)S(1)}, u32[]{:S(2)}, u32[]{:S(2)}) collective-permute-start(bf16[192,2880]{1,0:T(8,128)(2,1)S(1)} %combine.6.refs_2_), channel_id=1, source_target_pairs={{0,8},{4,12},{24,16},{28,20},{1,9},{5,13},{25,17},{29,21},{2,10},{... | collective-permute-start | bytes 3317768 | tf_op jit(solution)/shard_map/ppermute | solution.py:635
  75.1 4.7 %back_part.3 = (bf16[192,512]{1,0:T(8,128)(2,1)S(1)}, bf16[192,512]{1,0:T(8,128)(2,1)S(1)}, bf16[192,512]{1,0:T(8,128)(2,1)S(1)}, bf16[192,512]{1,0:T(8,128)(2,1...) custom-call(s32[32]{0:T(128)S(1)} %dynamic-slice_bitcast_fusion.where_ref, ...), custom_call_target="tpu_custom_call" | custom-call | flops 6000000 | bytes 18000000 | tf_op jit(solution)/shard_map/back_part/pallas_call | solution.py:534
  81.9 5.8 %collective-permute-done.20.refs_5_.refs_1_.refs_4_ = bf16[192,512]{1,0:T(8,128)(2,1)S(1)} collective-permute-done((bf16[192,512]{1,0:T(8,128)(2,1)S(1)}, bf16[192,512]{1,0:T(8,128)(2,1)S(1)}, u32[]{:S(2)}, u32[]{:S(2)}) %collective-permute-start.20) | collective-permute-done | bytes 196640 | tf_op jit(solution)/shard_map/ppermute | solution.py:623
  89.2 2.6 %back_part.4 = (bf16[192,512]{1,0:T(8,128)(2,1)S(1)}, bf16[192,512]{1,0:T(8,128)(2,1)S(1)}, f32[8,1024]{1,0:T(8,128)S(1)}) custom-call(s32[32]{0:T(128)S(1)} %dynamic-slice_bitcast_fusion.where_ref, bf16[4,128,1536]{2,1,0:T(8,128)(2,1)S(1)} %pack_rows.2.refs_0_.refs_2_.refs_6_, bf16[4,128,1536]{2,1,0:T(8,128)(2,1)S(1)} %collective-permute-done.7.refs_1_.refs_3_.refs_7_, ...), custom_call_target="tpu_custom_call" | custom-call | flops 6000000 | bytes 18000000 | tf_op jit(solution)/shard_map/back_part/pallas_call | solution.py:534
  91.9 2.8 %collective-permute-done.22.refs_7_.refs_5_.refs_6_ = bf16[192,512]{1,0:T(8,128)(2,1)S(1)} collective-permute-done((bf16[192,512]{1,0:T(8,128)(2,1)S(1)}, bf16[192,512]{1,0:T(8,128)(2,1)S(1)}, u32[]{:S(2)}, u32[]{:S(2)}) %collective-permute-start.22) | collective-permute-done | bytes 196640 | tf_op jit(solution)/shard_map/ppermute | solution.py:623
  95.5 4.8 %collective-permute-start.26 = (bf16[192,2880]{1,0:T(8,128)(2,1)S(1)}, bf16[192,2880]{1,0:T(8,128)(2,1)S(1)}, u32[]{:S(2)}, u32[]{:S(2)}) collective-permute-start(bf16[192,2880]{1,0:T(8,128)(2,1)S(1)} %combine.8.refs_15_), channel_id=1, source_target_pairs={{0,8},{4,12},{8,0},{12,4},{16,24},{20,28},{24,16},{28,20},{1,9},{5... | collective-permute-start | bytes 3317768 | tf_op jit(solution)/shard_map/ppermute | solution.py:635
  102.7 2.7 %back_part.5 = (bf16[192,512]{1,0:T(8,128)(2,1)S(1)}, bf16[192,512]{1,0:T(8,128)(2,1)S(1)}, f32[8,1024]{1,0:T(8,128)S(1)}) custom-call(s32[32]{0:T(128)S(1)} %dynamic-slice_bitcast_fusion.where_ref, bf16[4,128,1536]{2,1,0:T(8,128)(2,1)S(1)} %pack_rows.2.refs_0_.refs_2_.refs_6_, bf16[4,128,1536]{2,1,0:T(8,128)(2,1)S(1)} %collective-permute-done.7.refs_1_.refs_3_.refs_7_, ...), custom_call_target="tpu_custom_call" | custom-call | flops 6000000 | bytes 18000000 | tf_op jit(solution)/shard_map/back_part/pallas_call | solution.py:534
  110.4 6.4 %all_to_all.11 = f32[4,1,128]{2,1,0:T(1,128)S(1)} all-to-all(f32[4,1,128]{2,1,0:T(1,128)S(1)} %add_bitcast_fusion), channel_id=1, replica_groups=mesh['ctx'=8,'exp'=4] {'exp'}, dimensions={0} | all-to-all | bytes 4096 | tf_op jit(solution)/shard_map/all_to_all | solution.py:735
  117.5 2.9 %join_hidden.1 = bf16[512,1536]{1,0:T(8,128)(2,1)} custom-call(s32[32]{0:T(128)S(1)} %dynamic-slice_bitcast_fusion.where_ref, bf16[192,512]{1,0:T(8,128)(2,1)S(1)} %get-tuple-element.36.refs_0_, bf16[192,512]{1,0:T(8,128)(2,1)S(1)} %collective-permute-done.20.refs_5_.refs_1_.refs_4_, bf16[192,512]{1,0:T(8,128)(2,1)S(1)} %get-tuple-element.37.refs_2_, ...), custom_call_target="tpu_custom_call" | custom-call | flops 2000000 | bytes 6000000 | tf_op jit(solution)/shard_map/join_hidden/pallas_call | solution.py:573
  120.4 4.4 %collective-permute-done.26.refs_0_ = bf16[192,2880]{1,0:T(8,128)(2,1)S(1)} collective-permute-done((bf16[192,2880]{1,0:T(8,128)(2,1)S(1)}, bf16[192,2880]{1,0:T(8,128)(2,1)S(1)}, u32[]{:S(2)}, u32[]{:S(2)}) %collective-permute-start.26) | collective-permute-done | bytes 1105952 | tf_op jit(solution)/shard_map/ppermute | solution.py:635
  (79 shorter events, 39.3 us)
Async XLA Ops:
  0.6 30.3 %collective-permute-start.4 = (bf16[192,2880]{1,0:T(8,128)(2,1)}, bf16[192,2880]{1,0:T(8,128)(2,1)S(1)}, u32[]{:S(2)}, u32[]{:S(2)}) collective-permute-start(bf16[192,2880]{1,0:T(8,128)(2,1)} %bitcast.15), channel_id=1, source_target_pairs={{0,8},{4,12},{8,0},{12,4},{16,24},{20,28},{24,16},{28,20},{1,9},{5... | collective-permute-start | bytes 3317768 | tf_op jit(solution)/shard_map/ppermute | solution.py:635
  3.7 27.2 %collective-permute-start.3 = (bf16[192,2880]{1,0:T(8,128)(2,1)}, bf16[192,2880]{1,0:T(8,128)(2,1)S(1)}, u32[]{:S(2)}, u32[]{:S(2)}) collective-permute-start(bf16[192,2880]{1,0:T(8,128)(2,1)} %bitcast.16), channel_id=1, source_target_pairs={{8,16},{12,20},{16,8},{20,12},{9,17},{13,21},{17,9},{21,13},{10,18... | collective-permute-start | bytes 3317768 | tf_op jit(solution)/shard_map/ppermute | solution.py:635
  6.6 11.6 %collective-permute-start.1 = (bf16[128,1536]{1,0:T(8,128)(2,1)}, bf16[128,1536]{1,0:T(8,128)(2,1)S(1)}, u32[]{:S(2)}, u32[]{:S(2)}) collective-permute-start(bf16[128,1536]{1,0:T(8,128)(2,1)} %get-tuple-element.25.refs_0_), channel_id=1, source_target_pairs={{0,4},{4,0},{8,12},{12,8},{16,20},{20,16},{24,28},{28,24},{1,5},{5... | collective-permute-start | bytes 1179656 | tf_op jit(solution)/shard_map/ppermute | solution.py:623
  8.2 10.5 %collective-permute-start = (bf16[128,1536]{1,0:T(8,128)(2,1)}, bf16[128,1536]{1,0:T(8,128)(2,1)S(1)}, u32[]{:S(2)}, u32[]{:S(2)}) collective-permute-start(bf16[128,1536]{1,0:T(8,128)(2,1)} %get-tuple-element.25.refs_0_), channel_id=1, source_target_pairs={{0,2},{1,3},{2,0},{3,1},{4,6},{5,7},{6,4},{7,5},{8,10},{9,11},{10,... | collective-permute-start | bytes 1179656 | tf_op jit(solution)/shard_map/ppermute | solution.py:625
  18.7 12.2 %collective-permute-start.2 = (bf16[128,1536]{1,0:T(8,128)(2,1)S(1)}, bf16[128,1536]{1,0:T(8,128)(2,1)S(1)}, u32[]{:S(2)}, u32[]{:S(2)}) collective-permute-start(bf16[128,1536]{1,0:T(8,128)(2,1)S(1)} %hold.4.refs_1_.refs_2_), channel_id=1, source_target_pairs={{0,2},{1,3},{2,0},{3,1},{4,6},{5,7},{6,4},{7,5},{8,10},{9,11},{10,... | collective-permute-start | bytes 1179656 | tf_op jit(solution)/shard_map/ppermute | solution.py:625
  21.7 9.2 %collective-permute-start.6 = (bf16[128,1408]{1,0:T(8,128)(2,1)S(1)}, bf16[128,1408]{1,0:T(8,128)(2,1)S(1)}, u32[]{:S(2)}, u32[]{:S(2)}) collective-permute-start(bf16[128,1408]{1,0:T(8,128)(2,1)S(1)} %hold.5.refs_0_), channel_id=1, source_target_pairs={{0,4},{4,0},{8,12},{12,8},{16,20},{20,16},{24,28},{28,24},{1,5},{5... | collective-permute-start | bytes 1081352 | tf_op jit(solution)/shard_map/ppermute | solution.py:623
  32.7 11.3 %collective-permute-start.9 = (bf16[128,1408]{1,0:T(8,128)(2,1)S(1)}, bf16[128,1408]{1,0:T(8,128)(2,1)S(1)}, u32[]{:S(2)}, u32[]{:S(2)}) collective-permute-start(bf16[128,1408]{1,0:T(8,128)(2,1)S(1)} %hold.5.refs_0_), channel_id=1, source_target_pairs={{0,2},{1,3},{2,0},{3,1},{4,6},{5,7},{6,4},{7,5},{8,10},{9,11},{10,... | collective-permute-start | bytes 1081352 | tf_op jit(solution)/shard_map/ppermute | solution.py:625
  34.0 16.8 %collective-permute-start.11 = (bf16[128,1408]{1,0:T(8,128)(2,1)S(1)}, bf16[128,1408]{1,0:T(8,128)(2,1)S(1)}, u32[]{:S(2)}, u32[]{:S(2)}) collective-permute-start(bf16[128,1408]{1,0:T(8,128)(2,1)S(1)} %collective-permute-done.6.refs_6_.refs_1_), channel_id=1, source_target_pairs={{0,2},{1,3},{2,0},{3,1},{4,6},{5,7},{6,4},{7,5},{8,10},{9,11},{10,... | collective-permute-start | bytes 1081352 | tf_op jit(solution)/shard_map/ppermute | solution.py:625
  38.1 17.5 %collective-permute-start.16 = (bf16[192,1472]{1,0:T(8,128)(2,1)S(1)}, bf16[192,1472]{1,0:T(8,128)(2,1)S(1)}, u32[]{:S(2)}, u32[]{:S(2)}) collective-permute-start(bf16[192,1472]{1,0:T(8,128)(2,1)S(1)} %begin.2), channel_id=1, source_target_pairs={{0,8},{4,12},{8,0},{12,4},{16,24},{20,28},{24,16},{28,20},{1,9},{5... | collective-permute-start | bytes 1695752 | tf_op jit(solution)/shard_map/ppermute | solution.py:635
  41.9 15.1 %collective-permute-start.13 = (bf16[3,192,512]{2,1,0:T(8,128)(2,1)S(1)}, bf16[3,192,512]{2,1,0:T(8,128)(2,1)S(1)}, u32[]{:S(2)}, u32[]{:S(2)}) collective-permute-start(bf16[3,192,512]{2,1,0:T(8,128)(2,1)S(1)} %get-tuple-element.29), channel_id=1, source_target_pairs={{0,4},{4,0},{8,12},{12,8},{16,20},{20,16},{24,28},{28,24},{1,5},{5... | collective-permute-start | bytes 1769480 | tf_op jit(solution)/shard_map/ppermute | solution.py:623
  43.3 28.9 %collective-permute-start.14 = (bf16[192,2880]{1,0:T(8,128)(2,1)S(1)}, bf16[192,2880]{1,0:T(8,128)(2,1)S(1)}, u32[]{:S(2)}, u32[]{:S(2)}) collective-permute-start(bf16[192,2880]{1,0:T(8,128)(2,1)S(1)} %collective-permute-done.4.refs_5_.refs_12_), channel_id=1, source_target_pairs={{8,16},{12,20},{16,8},{20,12},{9,17},{13,21},{17,9},{21,13},{10,18... | collective-permute-start | bytes 3317768 | tf_op jit(solution)/shard_map/ppermute | solution.py:635
  57.0 16.5 %collective-permute-start.18 = (bf16[192,1408]{1,0:T(8,128)(2,1)S(1)}, bf16[192,1408]{1,0:T(8,128)(2,1)S(1)}, u32[]{:S(2)}, u32[]{:S(2)}) collective-permute-start(bf16[192,1408]{1,0:T(8,128)(2,1)S(1)} %hold.6.refs_2_), channel_id=1, source_target_pairs={{0,8},{4,12},{8,0},{12,4},{16,24},{20,28},{24,16},{28,20},{1,9},{5... | collective-permute-start | bytes 1622024 | tf_op jit(solution)/shard_map/ppermute | solution.py:635
  59.9 21.5 %collective-permute-start.17 = (bf16[192,1472]{1,0:T(8,128)(2,1)S(1)}, bf16[192,1472]{1,0:T(8,128)(2,1)S(1)}, u32[]{:S(2)}, u32[]{:S(2)}) collective-permute-start(bf16[192,1472]{1,0:T(8,128)(2,1)S(1)} %combine.5.refs_6_.refs_10_), channel_id=1, source_target_pairs={{8,16},{12,20},{16,8},{20,12},{9,17},{13,21},{17,9},{21,13},{10,18... | collective-permute-start | bytes 1695752 | tf_op jit(solution)/shard_map/ppermute | solution.py:635
  68.2 32.2 %collective-permute-start.27 = (bf16[192,2880]{1,0:T(8,128)(2,1)S(1)}, bf16[192,2880]{1,0:T(8,128)(2,1)S(1)}, u32[]{:S(2)}, u32[]{:S(2)}) collective-permute-start(bf16[192,2880]{1,0:T(8,128)(2,1)S(1)} %combine.6.refs_2_), channel_id=1, source_target_pairs={{0,8},{4,12},{24,16},{28,20},{1,9},{5,13},{25,17},{29,21},{2,10},{... | collective-permute-start | bytes 3317768 | tf_op jit(solution)/shard_map/ppermute | solution.py:635
  72.2 29.7 %collective-permute-start.15 = (bf16[192,2880]{1,0:T(8,128)(2,1)S(1)}, bf16[192,2880]{1,0:T(8,128)(2,1)S(1)}, u32[]{:S(2)}, u32[]{:S(2)}) collective-permute-start(bf16[192,2880]{1,0:T(8,128)(2,1)S(1)} %collective-permute-done.14.refs_13_), channel_id=1, source_target_pairs={{8,0},{12,4},{16,24},{20,28},{9,1},{13,5},{17,25},{21,29},{10,2},{... | collective-permute-start | bytes 3317768 | tf_op jit(solution)/shard_map/ppermute | solution.py:635
  74.2 20.5 %collective-permute-start.19 = (bf16[192,1408]{1,0:T(8,128)(2,1)S(1)}, bf16[192,1408]{1,0:T(8,128)(2,1)S(1)}, u32[]{:S(2)}, u32[]{:S(2)}) collective-permute-start(bf16[192,1408]{1,0:T(8,128)(2,1)S(1)} %combine.7.refs_14_.refs_15_), channel_id=1, source_target_pairs={{8,16},{12,20},{16,8},{20,12},{9,17},{13,21},{17,9},{21,13},{10,18... | collective-permute-start | bytes 1622024 | tf_op jit(solution)/shard_map/ppermute | solution.py:635
  79.8 7.9 %collective-permute-start.20 = (bf16[192,512]{1,0:T(8,128)(2,1)S(1)}, bf16[192,512]{1,0:T(8,128)(2,1)S(1)}, u32[]{:S(2)}, u32[]{:S(2)}) collective-permute-start(bf16[192,512]{1,0:T(8,128)(2,1)S(1)} %get-tuple-element.32), channel_id=1, source_target_pairs={{0,4},{4,0},{8,12},{12,8},{16,20},{20,16},{24,28},{28,24},{1,5},{5... | collective-permute-start | bytes 589832 | tf_op jit(solution)/shard_map/ppermute | solution.py:623
  81.4 10.5 %collective-permute-start.21 = (bf16[192,512]{1,0:T(8,128)(2,1)S(1)}, bf16[192,512]{1,0:T(8,128)(2,1)S(1)}, u32[]{:S(2)}, u32[]{:S(2)}) collective-permute-start(bf16[192,512]{1,0:T(8,128)(2,1)S(1)} %get-tuple-element.33), channel_id=1, source_target_pairs={{0,4},{4,0},{8,12},{12,8},{16,20},{20,16},{24,28},{28,24},{1,5},{5... | collective-permute-start | bytes 589832 | tf_op jit(solution)/shard_map/ppermute | solution.py:623
  87.7 7.0 %collective-permute-start.22 = (bf16[192,512]{1,0:T(8,128)(2,1)S(1)}, bf16[192,512]{1,0:T(8,128)(2,1)S(1)}, u32[]{:S(2)}, u32[]{:S(2)}) collective-permute-start(bf16[192,512]{1,0:T(8,128)(2,1)S(1)} %get-tuple-element.34), channel_id=1, source_target_pairs={{0,4},{4,0},{8,12},{12,8},{16,20},{20,16},{24,28},{28,24},{1,5},{5... | collective-permute-start | bytes 589832 | tf_op jit(solution)/shard_map/ppermute | solution.py:623
  95.5 29.2 %collective-permute-start.26 = (bf16[192,2880]{1,0:T(8,128)(2,1)S(1)}, bf16[192,2880]{1,0:T(8,128)(2,1)S(1)}, u32[]{:S(2)}, u32[]{:S(2)}) collective-permute-start(bf16[192,2880]{1,0:T(8,128)(2,1)S(1)} %combine.8.refs_15_), channel_id=1, source_target_pairs={{0,8},{4,12},{8,0},{12,4},{16,24},{20,28},{24,16},{28,20},{1,9},{5... | collective-permute-start | bytes 3317768 | tf_op jit(solution)/shard_map/ppermute | solution.py:635
  101.2 19.2 %collective-permute-start.28 = (bf16[192,1472]{1,0:T(8,128)(2,1)S(1)}, bf16[192,1472]{1,0:T(8,128)(2,1)S(1)}, u32[]{:S(2)}, u32[]{:S(2)}) collective-permute-start(bf16[192,1472]{1,0:T(8,128)(2,1)S(1)} %get-tuple-element.43), channel_id=1, source_target_pairs={{8,16},{12,20},{16,8},{20,12},{9,17},{13,21},{17,9},{21,13},{10,18... | collective-permute-start | bytes 1695752 | tf_op jit(solution)/shard_map/ppermute | solution.py:635
  102.0 18.4 %collective-permute-start.29 = (bf16[192,1408]{1,0:T(8,128)(2,1)S(1)}, bf16[192,1408]{1,0:T(8,128)(2,1)S(1)}, u32[]{:S(2)}, u32[]{:S(2)}) collective-permute-start(bf16[192,1408]{1,0:T(8,128)(2,1)S(1)} %hold.7), channel_id=1, source_target_pairs={{8,16},{12,20},{16,8},{20,12},{9,17},{13,21},{17,9},{21,13},{10,18... | collective-permute-start | bytes 1622024 | tf_op jit(solution)/shard_map/ppermute | solution.py:635
  106.9 10.6 %collective-permute-start.24 = (bf16[192,512]{1,0:T(8,128)(2,1)S(1)}, bf16[192,512]{1,0:T(8,128)(2,1)S(1)}, u32[]{:S(2)}, u32[]{:S(2)}) collective-permute-start(bf16[192,512]{1,0:T(8,128)(2,1)S(1)} %get-tuple-element.40), channel_id=1, source_target_pairs={{0,4},{4,0},{8,12},{12,8},{16,20},{20,16},{24,28},{28,24},{1,5},{5... | collective-permute-start | bytes 589832 | tf_op jit(solution)/shard_map/ppermute | solution.py:623
  109.1 8.4 %collective-permute-start.25 = (bf16[192,512]{1,0:T(8,128)(2,1)S(1)}, bf16[192,512]{1,0:T(8,128)(2,1)S(1)}, u32[]{:S(2)}, u32[]{:S(2)}) collective-permute-start(bf16[192,512]{1,0:T(8,128)(2,1)S(1)} %get-tuple-element.42), channel_id=1, source_target_pairs={{0,4},{4,0},{8,12},{12,8},{16,20},{20,16},{24,28},{28,24},{1,5},{5... | collective-permute-start | bytes 589832 | tf_op jit(solution)/shard_map/ppermute | solution.py:623
  (13 other events, 91.5 us)

commit v8 on v7

--- a/solution.py
+++ b/solution.py
@@ -11,6 +11,7 @@
 LANES = 128
 SCALE = 1_000_000
 BEGIN_WEIGHT = 600
+FIRST_WEIGHT = 12_000
 NT = (((1,), (1,)), ((), ()))
 NN = (((1,), (0,)), ((), ()))
 f32 = jnp.float32
@@ -210,7 +211,7 @@
     del refs
 
 
-def hold(values, after):
+def hold(values, after, weight=0):
     return pl.pallas_call(
         hold_kernel,
         out_shape=tuple(jax.ShapeDtypeStruct(value.shape, value.dtype) for value in values),
@@ -218,7 +219,7 @@
         out_specs=(anywhere(),) * len(values),
         input_output_aliases={place: place for place in range(len(values))},
         compiler_params=params(),
-        cost_estimate=taking(0),
+        cost_estimate=taking(weight),
         name="hold",
     )(*values, *after)
 
@@ -266,51 +267,94 @@
     return pl.multiple_of(start, tokens)
 
 
-def products_kernel(table, model, counts, places, shards, skip, where_ref, *refs):
+def scale_rows(table, model, where_ref, rows, gated, scaled):
+    tokens = rows[0].shape[0]
+    me = where_ref[table["me"]]
+    lane = lax.broadcasted_iota(jnp.int32, (tokens, LANES), 1)
+    for place, block in enumerate(rows):
+        here = pl.ds(place_of(place, len(rows) // 2, me, tokens), tokens)
+        tile = gated[place][:, gated[place].shape[1] - LANES :]
+        picked = jnp.where(lane == model % LANES + me, tile.astype(f32), 0.0)
+        gate = jnp.sum(picked, axis=1, keepdims=True)
+        scaled[here, :] = (block[:, : scaled.shape[1]].astype(f32) * gate).astype(bf16)
+
+
+def products_kernel(table, model, counts, places, shards, skip, guard, where_ref, *refs):
     used = sum(counts)
     rows = blocks_of(refs[: counts[0]], places[0])
     gated = blocks_of(refs[counts[0] : used], places[1])
-    number = len(rows)
     own_ref, other_ref = refs[used : used + 2]
     kept_ref, scaled = refs[-2:]
-    tokens = rows[0].shape[0]
     units, slots = own_ref.shape[1:]
-    width = kept_ref.shape[2]
-    me = where_ref[table["me"]]
-    lane = lax.broadcasted_iota(jnp.int32, (tokens, LANES), 1)
-    for place in range(number):
-        here = pl.ds(place_of(place, number // 2, me, tokens), tokens)
-        tile = gated[place][:, gated[place].shape[1] - LANES :]
-        picked = jnp.where(lane == model % LANES + me, tile.astype(f32), 0.0)
-        gate = jnp.sum(picked, axis=1, keepdims=True)
-        scaled[here, :] = (rows[place][:, :width].astype(f32) * gate).astype(bf16)
 
     def stacked(ref, offset):
         parts = [ref[offset + shard] for shard in range(shards)]
         return jnp.concatenate(parts, axis=0) if len(parts) > 1 else parts[0]
 
-    total = dot(stacked(own_ref, skip), scaled[:slots, :], NN)
-    total = total + dot(stacked(other_ref, 0), scaled[slots:, :], NN)
-    for shard in range(shards):
-        kept_ref[shard] = total[shard * units : (shard + 1) * units]
-
-
-def products(table, where, rows, gated, own, other, skip, model, width, name, after):
+    def work():
+        scale_rows(table, model, where_ref, rows, gated, scaled)
+        total = dot(stacked(own_ref, skip), scaled[:slots, :], NN)
+        total = total + dot(stacked(other_ref, 0), scaled[slots:, :], NN)
+        for shard in range(shards):
+            kept_ref[shard] = total[shard * units : (shard + 1) * units]
+
+    if guard:
+        pl.when(where_ref[table["use", 2, "A"]] != 0)(work)
+    else:
+        work()
+
+
+def products(table, where, rows, gated, own, other, skip, model, width, name, after, guard=False):
     arrays, places = zip(rows, gated)
     tokens = arrays[0][0].shape[-2]
     counts = [len(part) for part in arrays]
-    number = 2 * (own.shape[2] // tokens)
     shards, units, slots = other.shape
     return pl.pallas_call(
-        functools.partial(products_kernel, table, model, counts, places, shards, skip),
+        functools.partial(products_kernel, table, model, counts, places, shards, skip, guard),
         out_shape=jax.ShapeDtypeStruct((shards, units, width), f32),
         in_specs=[scalars()] + [whole()] * (sum(counts) + 2) + [anywhere()] * len(after),
         out_specs=whole(),
-        scratch_shapes=[pltpu.VMEM((number * tokens, width), bf16)],
+        scratch_shapes=[pltpu.VMEM((2 * slots, width), bf16)],
         compiler_params=params(),
         cost_estimate=taking(4),
         name=name,
     )(where, *arrays[0], *arrays[1], own, other, *after)
+
+
+def first_kernel(table, model, counts, places, start, where_ref, *refs):
+    used = sum(counts)
+    rows = blocks_of(refs[: counts[0]], places[0])
+    gated = blocks_of(refs[counts[0] : used], places[1])
+    own_ref, other_ref, coming_ref = refs[used : used + 3]
+    out_ref, scaled = refs[-2:]
+    slots = own_ref.shape[2]
+    ends = where_ref[table["use", 2, "A"]] == 0
+
+    @pl.when(ends)
+    def _():
+        scale_rows(table, model, where_ref, rows, gated, scaled)
+        total = dot(own_ref[0], scaled[:slots, :], NN)
+        out_ref[...] = (total + dot(other_ref[0], scaled[slots:, :], NN)).astype(bf16)
+
+    @pl.when(jnp.logical_not(ends))
+    def _():
+        out_ref[...] = coming_ref[:, start : start + out_ref.shape[1]]
+
+
+def first_sums(table, where, rows, gated, own, other, coming, model, start, width, after):
+    arrays, places = zip(rows, gated)
+    counts = [len(part) for part in arrays]
+    units, slots = own.shape[1:]
+    return pl.pallas_call(
+        functools.partial(first_kernel, table, model, counts, places, start),
+        out_shape=jax.ShapeDtypeStruct((units, width), bf16),
+        in_specs=[scalars()] + [whole()] * (sum(counts) + 3) + [anywhere()] * len(after),
+        out_specs=whole(),
+        scratch_shapes=[pltpu.VMEM((2 * slots, width), bf16)],
+        compiler_params=params(),
+        cost_estimate=taking(BEGIN_WEIGHT),
+        name="first_sums",
+    )(where, *arrays[0], *arrays[1], own, other, coming, *after)
 
 
 def rows_of(units):
@@ -378,36 +422,6 @@
     )(where, *coming, *operands, *after)
 
 
-def begin_kernel(table, start, stop, where_ref, coming_ref, kept_ref, *refs):
-    out_ref = refs[-1]
-    flag = where_ref[table["use", 2, "A"]] == 0
-    total = coming_ref[:, start:stop].astype(f32) + jnp.where(flag, kept_ref[0], 0.0)
-    out_ref[...] = total.astype(bf16)
-
-
-def begin(table, where, coming, kept, start, after):
-    units, model = coming.shape
-    width = kept.shape[2]
-    block = rows_of(units)
-    return pl.pallas_call(
-        functools.partial(begin_kernel, table, start, start + width),
-        out_shape=jax.ShapeDtypeStruct((units, width), bf16),
-        grid_spec=pltpu.PrefetchScalarGridSpec(
-            num_scalar_prefetch=1,
-            grid=(units // block,),
-            in_specs=[
-                pl.BlockSpec((block, model), lambda j, s: (j, 0)),
-                pl.BlockSpec((1, block, width), lambda j, s: (0, j, 0)),
-            ]
-            + [anywhere()] * len(after),
-            out_specs=pl.BlockSpec((block, width), lambda j, s: (j, 0)),
-        ),
-        compiler_params=params(),
-        cost_estimate=taking(BEGIN_WEIGHT),
-        name="begin",
-    )(where, coming, kept, *after)
-
-
 def total_kernel(cut, counts, *refs):
     coming = [refs[: counts[0]], refs[counts[0] : sum(counts)]]
     out_ref = refs[-1]
@@ -452,8 +466,7 @@
         weight_refs[key] = refs[used : used + count]
         used += count
     before_ref = refs[used] if summed else None
-    outs = refs[len(refs) - 2 * len(choices) - 1 : -1]
-    sums_ref = refs[-1]
+    outs, sums_ref = refs[-3:-1], refs[-1]
     tokens = late[0].shape[0]
     units = own_ref.shape[1]
     me = where_ref[table["me"]]
@@ -499,7 +512,7 @@
                 total = jnp.zeros((1, tokens), f32)
                 for index, (valid, slot) in enumerate(zip(here_valid, here_slot)):
                     some = slice(index * units, (index + 1) * units)
-                    outs[2 * index + (0 if near else 1)][:, here] = gated[some]
+                    outs[0 if near else 1][index, :, here] = gated[some]
                     if near:
                         hidden = own_ref[slot, :, here].astype(f32)
                     else:
@@ -526,10 +539,10 @@
     keys = [key for choice in choices for key in choice]
     weights = [got[key] for key in keys]
     flat = [part for weight in weights for part in weight]
-    half = jax.ShapeDtypeStruct((units, slots), bf16)
+    half = jax.ShapeDtypeStruct((len(choices), units, slots), bf16)
     summed = before is not None
     operands = [*arrays[0], *arrays[1], own, first, rest, *flat] + ([before] if summed else [])
-    outs = [half] * (2 * len(choices)) + [jax.ShapeDtypeStruct((8, 2 * slots), f32)]
+    outs = [half, half, jax.ShapeDtypeStruct((8, 2 * slots), f32)]
     parts = [len(weight) for weight in weights]
     return pl.pallas_call(
         functools.partial(
@@ -552,8 +565,12 @@
     unit = jnp.where(row == column, 1.0, 0.0).astype(bf16)
     low = where_ref[table["x"]] == 0
     copies = []
-    for place, choice in enumerate(choices):
-        mine, theirs = refs[2 * place][...], refs[2 * place + 1][...]
+    pairs = [
+        (refs[2 * group][place], refs[2 * group + 1][place])
+        for group in range((len(refs) - 3) // 2)
+        for place in range(refs[2 * group].shape[0])
+    ]
+    for place, (choice, (mine, theirs)) in enumerate(zip(choices, pairs)):
         index = where_ref[table[("shard",) + choice[0]]]
         for key in choice[1:]:
             index = jnp.where(index >= 0, index, where_ref[table[("shard",) + key]])
@@ -567,23 +584,21 @@
         pl.when(index >= 0)(copy.wait)
 
 
-def join_hidden(table, where, choices, halves, slots, hidden, before, after):
-    units = halves[0].shape[0]
-    extends = before is not None
+def join_hidden(table, where, choices, halves, slots, hidden):
+    units = halves[0].shape[1]
     return pl.pallas_call(
         functools.partial(join_kernel, table, choices),
         out_shape=jax.ShapeDtypeStruct((slots, hidden), bf16),
-        in_specs=[scalars()] + [whole()] * len(halves) + [anywhere()] * (extends + len(after)),
+        in_specs=[scalars()] + [whole()] * len(halves),
         out_specs=anywhere(),
         scratch_shapes=[
             pltpu.VMEM((len(choices), slots, 2 * units), bf16),
             pltpu.SemaphoreType.DMA((len(choices),)),
         ],
-        input_output_aliases={1 + len(halves): 0} if extends else {},
         compiler_params=params(),
         cost_estimate=taking(2),
         name="join_hidden",
-    )(where, *halves, *([before] if extends else []), *after)
+    )(where, *halves)
 
 
 def logits_kernel(gates_ref, ids_ref, grads_ref, out_ref):
@@ -654,7 +669,7 @@
     late_mine = late_near + [late_x] + [swap(late_x, 0, high) for high in highs]
     (early,) = hold((early,), [late_x, other_first])
     early_x = swap(early, 1, 0)
-    late_rows = sides(pack(late_mine, [got[1, "B"][0], got[1, "A"][0], early_x]))
+    late_rows = sides(pack(late_mine, [early_x]))
     late_rows = (late_rows, [(side, place) for place in range(experts) for side in range(2)])
     early_rows = sides(pack([early, early_x], []))
     places = [(0, 0), (1, 0)]
@@ -667,27 +682,34 @@
     early_rows = (early_rows, places)
     other_rest = swap(other_rest, 1, 0)
 
-    first = [products(table, where, late_rows, late_rows, own, other_first, 0, model, model - cut, "first_late", [])]
-    sent = [begin(table, where, got[1, "B"][0], first[0], cut, [early_rows[0][1]])]
-    got[2, "A"] = [swap_z(sent[0], "A")]
+    for name, value in zip("BA", hold([got[1, "B"][0], got[1, "A"][0]], [], FIRST_WEIGHT)):
+        got[1, name] = [value]
+    chunks = ((late_rows, cut, model - cut), (early_rows, 0, cut))
+    after = [early_rows[0][1]]
+    first = []
+    for rows, start, columns in chunks:
+        value = first_sums(
+            table, where, rows, late_rows, own, other_first, got[1, "B"][0], model, start, columns, after
+        )
+        if first:
+            (value,) = hold([value], [other_rest])
+        got.setdefault((2, "A"), []).append(swap_z(value, "A"))
+        first.append(
+            products(table, where, rows, late_rows, own, other_first, 0, model, columns, "first_kept", [value], True)
+        )
+        after = [got[2, "A"][0], first[0]]
+    marker = value
     got[2, "B"] = [swap_z(got[1, "A"][0], "B")]
-    first.append(
-        products(table, where, early_rows, late_rows, own, other_first, 0, model, cut, "first_early", [])
-    )
-    sent.append(begin(table, where, got[1, "B"][0], first[1], 0, [got[2, "A"][0]]))
-    sent[1:] = hold((sent[1],), [other_rest])
-    got[2, "A"].append(swap_z(sent[1], "A"))
 
     halves, all_choices, weights_of = [], [], {}
     only_first = max(uses[3, "B"]) <= 0
 
     def backprop(choices, before, guard, after):
-        *outs, sums = back_part(
+        mine, theirs, sums = back_part(
             table, where, late_rows, early_rows, own, other_first, other_rest, choices,
             {**got, **weights_of}, before, guard, after, model,
         )
-        for mine, theirs in zip(outs[::2], outs[1::2]):
-            halves.extend([mine, swap(theirs, 1, 0)])
+        halves.extend([mine, swap(theirs, 1, 0)])
         all_choices.extend(choices)
         return sums
 
@@ -714,10 +736,10 @@
         return [[(turn, "A")], [(turn, "B")]] if both else [[(turn, "A"), (turn, "B")]]
 
     rest = []
-    marker = pass_on(3, "B", [sent[1]], 0) if only_first else sent[1]
-    for rows, columns, name in ((late_rows, model - cut, "rest_late"), (early_rows, cut, "rest_early")):
+    marker = pass_on(3, "B", [marker], 0) if only_first else marker
+    for rows, _, columns in chunks:
         rest.append(
-            products(table, where, rows, late_rows, own, other_rest, 1, model, columns, name, [marker])
+            products(table, where, rows, late_rows, own, other_rest, 1, model, columns, "rest_kept", [marker])
         )
     marker = pass_on(3, "A", rest)
     for chunk in range(2)[only_first:]:
@@ -729,14 +751,14 @@
         if turn > 2:
             waited = [array for key in ((turn, "A"), (turn, "B")) for array in weights_of.get(key, [])]
             pass_on(turn + 1, "B", [sums, *sooner], waited=waited)
-            marker = pass_on(turn + 1, "A", [sums, *sooner])
+            marker = pass_on(turn + 1, "A", [sums])
         sums = backprop(choices, sums, len(choices) == 1, [marker])
     slot_grad = sums[0:1, :slots] + swap(sums[0:1, slots:], 1, 0)
     grads = lax.all_to_all(
         slot_grad.reshape(experts, tokens), "exp", split_axis=0, concat_axis=0, tiled=True
     )
     logit_grad = logits_grad(gates, expert_ids.T, grads)
-    hidden_grad = join_hidden(table, where, all_choices, halves, slots, hidden, None, [])
+    hidden_grad = join_hidden(table, where, all_choices, halves, slots, hidden)
     weight_grad = total_grad(got[depth, "A"], got[depth, "B"], rest, cut)
     return (logit_grad.T, hidden_grad[None, None], weight_grad)
 

time: 127 us -> 123 us (0.969)
  waiting for transfers between devices: 37.3 us -> 32.6 us
    ppermute x10 -> x8, waiting for transfers between devices: 22.5 us -> 12.3 us  [swap(): return lax.ppermute(value, 'ctx', [(i, i ^ x) for i in range(groups)])]
    ppermute x12, starting transfers between devices: 23.6 us -> 29.1 us  [swap_z(): return lax.ppermute(value, 'ctx', pairs)]
    ppermute x12, waiting for transfers between devices: 5.35 us -> 9.62 us  [swap_z(): return lax.ppermute(value, 'ctx', pairs)]
    ppermute x10 -> x8, starting transfers between devices: 12 us -> 8.46 us  [swap(): return lax.ppermute(value, 'ctx', [(i, i ^ x) for i in range(groups)])]
    pallas_call x4, Pallas kernels: 11.1 us -> 7.85 us  [products(): pl.pallas_call(functools.partial(products_kernel, table, model, counts, p...]
    pallas_call x2, Pallas kernels: 1.46 us -> 4.32 us  [first_sums(): pl.pallas_call(functools.partial(first_kernel, table, model, counts, plac...]
    ppermute x8, waiting for transfers between devices: 9.37 us -> 10.7 us  [swap(): return lax.ppermute(value, 'exp', [(i, i ^ exp) for i in range(experts)])]
    ppermute x8, starting transfers between devices: 6.02 us -> 4.66 us  [swap(): return lax.ppermute(value, 'exp', [(i, i ^ exp) for i in range(experts)])]
  transfers between devices with their start and end apart: 30 -> 28, of which waited for: 14 -> 11; matrix products, arithmetic and copies ran while one was open for 1% -> 1% of each run, Pallas kernels for 27% -> 27%
where the time goes in v8:
time: 123 us; the launch traced here: 122 us
  starting transfers between devices  42.2 us (34%)
  Pallas kernels  36.5 us (30%)
  waiting for transfers between devices  32.6 us (27%)
  blocking collectives  6.32 us (5%)
  local copies, waits for them, and re-layouts  3.13 us (3%)
    ppermute x12, starting transfers between devices, swap_z(): return lax.ppermute(value, 'ctx', pairs)  29.1 us
    ppermute x8, waiting for transfers between devices, swap(): return lax.ppermute(value, 'ctx', [(i, i ^ x) for i in range(groups)])  12.3 us
    ppermute x8, waiting for transfers between devices, swap(): return lax.ppermute(value, 'exp', [(i, i ^ exp) for i in range(experts)])  10.7 us
    pallas_call x3, Pallas kernels, back_part(): pl.pallas_call(functools.partial(back_kernel, table, model, cut, counts,...  9.96 us
    ppermute x12, waiting for transfers between devices, swap_z(): return lax.ppermute(value, 'ctx', pairs)  9.62 us
    ppermute x8, starting transfers between devices, swap(): return lax.ppermute(value, 'ctx', [(i, i ^ x) for i in range(groups)])  8.46 us
    pallas_call x4, Pallas kernels, products(): pl.pallas_call(functools.partial(products_kernel, table, model, counts, p...  7.85 us
    all_to_all x1, blocking collectives, per_device_full(): lax.all_to_all(slot_grad.reshape(experts, tokens), 'exp', split_axis=0, c...  6.32 us
  transfers between devices with their start and end apart: 28, of which 11 were waited for; matrix products, arithmetic and copies ran while one was open for 1% of the time, Pallas kernels for 27%

profile of v8, /device:TPU:0, one launch (start us, length us, event | category | flops | bytes accessed | tf_op | source)
XLA Modules:
  0.0 121.8 jit_solution(7937137733098041882)
XLA Ops:
  0.6 2.2 %make_rows.1 = (bf16[128,1536]{1,0:T(8,128)(2,1)}, bf16[128,1408]{1,0:T(8,128)(2,1)}, f32[4,128]{1,0:T(4,128)}) custom-call(bf16[2880,128]{1,0:T(8,128)(2,1)} %bitcast.22, f32[4,128]{1,0:T(4,128)} %bitcast.23, s32[4,128]{1,0:T(4,128)} %bitcast.18), custom_call_target="tpu_custom_call" | custom-call | flops 2000000 | bytes 6000000 | tf_op jit(solution)/shard_map/make_rows/pallas_call | solution.py:161
  2.8 3.0 %collective-permute-start.1 = (bf16[128,1536]{1,0:T(8,128)(2,1)}, bf16[128,1536]{1,0:T(8,128)(2,1)S(1)}, u32[]{:S(2)}, u32[]{:S(2)}) collective-permute-start(bf16[128,1536]{1,0:T(8,128)(2,1)} %get-tuple-element.23.refs_0_), channel_id=1, source_target_pairs={{0,4},{4,0},{8,12},{12,8},{16,20},{20,16},{24,28},{28,24},{1,5},{5... | collective-permute-start | bytes 1179656 | tf_op jit(solution)/shard_map/ppermute | solution.py:638
  7.4 1.6 %collective-permute-start.13 = (bf16[192,2880]{1,0:T(8,128)(2,1)}, bf16[192,2880]{1,0:T(8,128)(2,1)S(1)}, u32[]{:S(2)}, u32[]{:S(2)}) collective-permute-start(bf16[192,2880]{1,0:T(8,128)(2,1)} %bitcast.15), channel_id=1, source_target_pairs={{0,8},{4,12},{8,0},{12,4},{16,24},{20,28},{24,16},{28,20},{1,9},{5... | collective-permute-start | bytes 3317768 | tf_op jit(solution)/shard_map/ppermute | solution.py:650
  12.8 2.2 %split_hidden.1 = (bf16[4,192,512]{2,1,0:T(8,128)(2,1)S(1)}, bf16[1,192,512]{2,1,0:T(8,128)(2,1)S(1)}, bf16[3,192,512]{2,1,0:T(8,128)(2,1)S(1)}) custom-call(s32[32]{0:T(128)S(1)} %dynamic-slice_bitcast_fusion.where_ref, bf16[512,1536]{1,0:T(8,128)(2,1)S(1)} %bitcast.14, bf16[128,1536]{1,0:T(8,128)(2,1)S(1)} %copy-done.1), custom_call_target="tpu_custom_call" | custom-call | flops 2000000 | bytes 6000000 | tf_op jit(solution)/shard_map/split_hidden/pallas_call | solution.py:252
  18.1 2.7 %collective-permute-done.3.refs_2_.refs_5_.refs_9_ = bf16[1,192,512]{2,1,0:T(8,128)(2,1)S(1)} collective-permute-done((bf16[1,192,512]{2,1,0:T(8,128)(2,1)S(1)}, bf16[1,192,512]{2,1,0:T(8,128)(2,1)S(1)}, u32[]{:S(2)}, u32[]{:S(2)}) %collective-permute-start.3) | collective-permute-done | bytes 196640 | tf_op jit(solution)/shard_map/ppermute | solution.py:638
  21.4 7.9 %collective-permute-done.4.refs_4_.refs_1_ = bf16[128,1408]{1,0:T(8,128)(2,1)S(1)} collective-permute-done((bf16[128,1408]{1,0:T(8,128)(2,1)S(1)}, bf16[128,1408]{1,0:T(8,128)(2,1)S(1)}, u32[]{:S(2)}, u32[]{:S(2)}) %collective-permute-start.4) | collective-permute-done | bytes 360480 | tf_op jit(solution)/shard_map/ppermute | solution.py:638
  31.5 2.2 %collective-permute-done.13.refs_1_ = bf16[192,2880]{1,0:T(8,128)(2,1)S(1)} collective-permute-done((bf16[192,2880]{1,0:T(8,128)(2,1)}, bf16[192,2880]{1,0:T(8,128)(2,1)S(1)}, u32[]{:S(2)}, u32[]{:S(2)}) %collective-permute-start.13) | collective-permute-done | bytes 1105952 | tf_op jit(solution)/shard_map/ppermute | solution.py:650
  34.6 2.2 %first_sums.2.refs_6_ = bf16[192,1472]{1,0:T(8,128)(2,1)S(1)} custom-call(s32[32]{0:T(128)S(1)} %dynamic-slice_bitcast_fusion.where_ref, bf16[4,128,1536]{2,1,0:T(8,128)(2,1)S(1)} %pack_rows.2.refs_0_.refs_2_.refs_6_, bf16[4,128,1536]{2,1,0:T(8,128)(2,1)S(1)} %collective-permute-done.5.refs_1_.refs_3_.refs_7_, ...), custom_call_target="tpu_custom_call" | custom-call | flops 600000000 | bytes 1800000000 | tf_op jit(solution)/shard_map/first_sums/pallas_call | solution.py:348
  36.8 2.4 %collective-permute-start.16 = (bf16[192,1472]{1,0:T(8,128)(2,1)S(1)}, bf16[192,1472]{1,0:T(8,128)(2,1)S(1)}, u32[]{:S(2)}, u32[]{:S(2)}) collective-permute-start(bf16[192,1472]{1,0:T(8,128)(2,1)S(1)} %first_sums.2.refs_6_), channel_id=1, source_target_pairs={{0,8},{4,12},{8,0},{12,4},{16,24},{20,28},{24,16},{28,20},{1,9},{5... | collective-permute-start | bytes 1695752 | tf_op jit(solution)/shard_map/ppermute | solution.py:650
  41.4 7.3 %collective-permute-done.9.refs_4_.refs_6_ = bf16[128,1408]{1,0:T(8,128)(2,1)S(1)} collective-permute-done((bf16[128,1408]{1,0:T(8,128)(2,1)S(1)}, bf16[128,1408]{1,0:T(8,128)(2,1)S(1)}, u32[]{:S(2)}, u32[]{:S(2)}) %collective-permute-start.9) | collective-permute-done | bytes 360480 | tf_op jit(solution)/shard_map/ppermute | solution.py:640
  50.4 2.5 %collective-permute-done.16.refs_11_.refs_0_ = bf16[192,1472]{1,0:T(8,128)(2,1)S(1)} collective-permute-done((bf16[192,1472]{1,0:T(8,128)(2,1)S(1)}, bf16[192,1472]{1,0:T(8,128)(2,1)S(1)}, u32[]{:S(2)}, u32[]{:S(2)}) %collective-permute-start.16) | collective-permute-done | bytes 565280 | tf_op jit(solution)/shard_map/ppermute | solution.py:650
  52.8 2.1 %first_sums.3.refs_0_ = bf16[192,1408]{1,0:T(8,128)(2,1)S(1)} custom-call(s32[32]{0:T(128)S(1)} %dynamic-slice_bitcast_fusion.where_ref, bf16[2,128,1408]{2,1,0:T(8,128)(2,1)S(1)} %pack_rows.3.refs_0_.refs_2_, bf16[2,128,1408]{2,1,0:T(8,128)(2,1)S(1)} %collective-permute-done.6.refs_7_.refs_1_.refs_3_, ...), custom_call_target="tpu_custom_call" | custom-call | flops 600000000 | bytes 1800000000 | tf_op jit(solution)/shard_map/first_sums/pallas_call | solution.py:348
  56.3 3.4 %rest_kept.3.refs_1_.refs_3_.refs_2_.refs_4_ = f32[3,192,1408]{2,1,0:T(8,128)S(1)} custom-call(s32[32]{0:T(128)S(1)} %dynamic-slice_bitcast_fusion.where_ref, bf16[2,128,1408]{2,1,0:T(8,128)(2,1)S(1)} %pack_rows.3.refs_0_.refs_2_, bf16[2,128,1408]{2,1,0:T(8,128)(2,1)S(1)} %collective-permute-done.6.refs_7_.refs_1_.refs_3_, ...), custom_call_target="tpu_custom_call" | custom-call | flops 4000000 | bytes 12000000 | tf_op jit(solution)/shard_map/rest_kept/pallas_call | solution.py:312
  59.6 3.4 %rest_kept.2.refs_0_.refs_2_.refs_1_.refs_3_ = f32[3,192,1472]{2,1,0:T(8,128)S(1)} custom-call(s32[32]{0:T(128)S(1)} %dynamic-slice_bitcast_fusion.where_ref, bf16[4,128,1536]{2,1,0:T(8,128)(2,1)S(1)} %pack_rows.2.refs_0_.refs_2_.refs_6_, bf16[4,128,1536]{2,1,0:T(8,128)(2,1)S(1)} %collective-permute-done.5.refs_1_.refs_3_.refs_7_, ...), custom_call_target="tpu_custom_call" | custom-call | flops 4000000 | bytes 12000000 | tf_op jit(solution)/shard_map/rest_kept/pallas_call | solution.py:312
  63.9 3.5 %collective-permute-start.25 = (bf16[192,2880]{1,0:T(8,128)(2,1)S(1)}, bf16[192,2880]{1,0:T(8,128)(2,1)S(1)}, u32[]{:S(2)}, u32[]{:S(2)}) collective-permute-start(bf16[192,2880]{1,0:T(8,128)(2,1)S(1)} %combine.6.refs_2_), channel_id=1, source_target_pairs={{0,8},{4,12},{24,16},{28,20},{1,9},{5,13},{25,17},{29,21},{2,10},{... | collective-permute-start | bytes 3317768 | tf_op jit(solution)/shard_map/ppermute | solution.py:650
  71.6 4.7 %back_part.3 = (bf16[3,192,512]{2,1,0:T(8,128)(2,1)S(1)}, bf16[3,192,512]{2,1,0:T(8,128)(2,1)S(1)}, f32[8,1024]{1,0:T(8,128)S(1)}) custom-call(s32[32]{0:T(128)S(1)} %dynamic-slice_bitcast_fusion.where_ref, bf16[4,128,1536]{2,1,0:T(8,128)(2,1)S(1)} %pack_rows.2.refs_0_.refs_2_.refs_6_, ...), custom_call_target="tpu_custom_call" | custom-call | flops 6000000 | bytes 18000000 | tf_op jit(solution)/shard_map/back_part/pallas_call | solution.py:547
  76.9 2.6 %back_part.4 = (bf16[1,192,512]{2,1,0:T(8,128)(2,1)S(1)}, bf16[1,192,512]{2,1,0:T(8,128)(2,1)S(1)}, f32[8,1024]{1,0:T(8,128)S(1)}) custom-call(s32[32]{0:T(128)S(1)} %dynamic-slice_bitcast_fusion.where_ref, bf16[4,128,1536]{2,1,0:T(8,128)(2,1)S(1)} %pack_rows.2.refs_0_.refs_2_.refs_6_, ...), custom_call_target="tpu_custom_call" | custom-call | flops 6000000 | bytes 18000000 | tf_op jit(solution)/shard_map/back_part/pallas_call | solution.py:547
  80.4 15.3 %collective-permute-start.24 = (bf16[192,2880]{1,0:T(8,128)(2,1)S(1)}, bf16[192,2880]{1,0:T(8,128)(2,1)S(1)}, u32[]{:S(2)}, u32[]{:S(2)}) collective-permute-start(bf16[192,2880]{1,0:T(8,128)(2,1)S(1)} %combine.8.refs_15_), channel_id=1, source_target_pairs={{0,8},{4,12},{8,0},{12,4},{16,24},{20,28},{24,16},{28,20},{1,9},{5... | collective-permute-start | bytes 3317768 | tf_op jit(solution)/shard_map/ppermute | solution.py:650
  98.0 2.7 %back_part.5 = (bf16[1,192,512]{2,1,0:T(8,128)(2,1)S(1)}, bf16[1,192,512]{2,1,0:T(8,128)(2,1)S(1)}, f32[8,1024]{1,0:T(8,128)S(1)}) custom-call(s32[32]{0:T(128)S(1)} %dynamic-slice_bitcast_fusion.where_ref, bf16[4,128,1536]{2,1,0:T(8,128)(2,1)S(1)} %pack_rows.2.refs_0_.refs_2_.refs_6_, ...), custom_call_target="tpu_custom_call" | custom-call | flops 6000000 | bytes 18000000 | tf_op jit(solution)/shard_map/back_part/pallas_call | solution.py:547
  102.7 1.6 %collective-permute-done.20 = f32[1,512]{1,0:T(1,128)S(1)} collective-permute-done((f32[1,512]{1,0:T(1,128)S(1)}, f32[1,512]{1,0:T(1,128)S(1)}, u32[]{:S(2)}, u32[]{:S(2)}) %collective-permute-start.20) | collective-permute-done | bytes 2080 | tf_op jit(solution)/shard_map/ppermute | solution.py:638
  105.5 6.3 %all_to_all.11 = f32[4,1,128]{2,1,0:T(1,128)S(1)} all-to-all(f32[4,1,128]{2,1,0:T(1,128)S(1)} %add_bitcast_fusion), channel_id=1, replica_groups=mesh['ctx'=8,'exp'=4] {'exp'}, dimensions={0} | all-to-all | bytes 4096 | tf_op jit(solution)/shard_map/all_to_all | solution.py:757
  112.4 2.9 %join_hidden.1 = bf16[512,1536]{1,0:T(8,128)(2,1)} custom-call(s32[32]{0:T(128)S(1)} %dynamic-slice_bitcast_fusion.where_ref, bf16[3,192,512]{2,1,0:T(8,128)(2,1)S(1)} %get-tuple-element.33.refs_0_, bf16[3,192,512]{2,1,0:T(8,128)(2,1)S(1)} %collective-permute-done.21.refs_1_.refs_4_, bf16[1,192,512]{2,1,0:T(8,128)(2,1)S(1)} %get-tuple-element.35.refs_2_, ...), custom_call_target="tpu_custom_call" | custom-call | flops 2000000 | bytes 6000000 | tf_op jit(solution)/shard_map/join_hidden/pallas_call | solution.py:589
  115.3 5.0 %collective-permute-done.24.refs_0_ = bf16[192,2880]{1,0:T(8,128)(2,1)S(1)} collective-permute-done((bf16[192,2880]{1,0:T(8,128)(2,1)S(1)}, bf16[192,2880]{1,0:T(8,128)(2,1)S(1)}, u32[]{:S(2)}, u32[]{:S(2)}) %collective-permute-start.24) | collective-permute-done | bytes 1105952 | tf_op jit(solution)/shard_map/ppermute | solution.py:650
  120.3 1.5 %total_grad.1 = f32[1,192,2880]{2,1,0:T(8,128)} custom-call(bf16[192,2880]{1,0:T(8,128)(2,1)S(1)} %collective-permute-done.24.refs_0_, bf16[192,1472]{1,0:T(8,128)(2,1)S(1)} %collective-permute-done.26.refs_1_, bf16[192,1408]{1,0:T(8,128)(2,1)S(1)} %collective-permute-done.27.refs_2_, f32[3,192,1472]{2,1,0:T(8,128)S(1)} %rest_kept.2.refs_0_.refs_2_.refs_1_.refs_3_, ...), custom_call_target="tpu_custom_call" | custom-call | flops 2000000 | bytes 6000000 | tf_op jit(solution)/shard_map/total_grad/pallas_call | solution.py:441
  (76 shorter events, 29.7 us)
Async XLA Ops:
  2.8 12.8 %collective-permute-start.1 = (bf16[128,1536]{1,0:T(8,128)(2,1)}, bf16[128,1536]{1,0:T(8,128)(2,1)S(1)}, u32[]{:S(2)}, u32[]{:S(2)}) collective-permute-start(bf16[128,1536]{1,0:T(8,128)(2,1)} %get-tuple-element.23.refs_0_), channel_id=1, source_target_pairs={{0,4},{4,0},{8,12},{12,8},{16,20},{20,16},{24,28},{28,24},{1,5},{5... | collective-permute-start | bytes 1179656 | tf_op jit(solution)/shard_map/ppermute | solution.py:638
  5.8 10.8 %collective-permute-start = (bf16[128,1536]{1,0:T(8,128)(2,1)}, bf16[128,1536]{1,0:T(8,128)(2,1)S(1)}, u32[]{:S(2)}, u32[]{:S(2)}) collective-permute-start(bf16[128,1536]{1,0:T(8,128)(2,1)} %get-tuple-element.23.refs_0_), channel_id=1, source_target_pairs={{0,2},{1,3},{2,0},{3,1},{4,6},{5,7},{6,4},{7,5},{8,10},{9,11},{10,... | collective-permute-start | bytes 1179656 | tf_op jit(solution)/shard_map/ppermute | solution.py:640
  7.4 26.3 %collective-permute-start.13 = (bf16[192,2880]{1,0:T(8,128)(2,1)}, bf16[192,2880]{1,0:T(8,128)(2,1)S(1)}, u32[]{:S(2)}, u32[]{:S(2)}) collective-permute-start(bf16[192,2880]{1,0:T(8,128)(2,1)} %bitcast.15), channel_id=1, source_target_pairs={{0,8},{4,12},{8,0},{12,4},{16,24},{20,28},{24,16},{28,20},{1,9},{5... | collective-permute-start | bytes 3317768 | tf_op jit(solution)/shard_map/ppermute | solution.py:650
  8.9 25.2 %collective-permute-start.12 = (bf16[192,2880]{1,0:T(8,128)(2,1)}, bf16[192,2880]{1,0:T(8,128)(2,1)S(1)}, u32[]{:S(2)}, u32[]{:S(2)}) collective-permute-start(bf16[192,2880]{1,0:T(8,128)(2,1)} %bitcast.16), channel_id=1, source_target_pairs={{8,16},{12,20},{16,8},{20,12},{9,17},{13,21},{17,9},{21,13},{10,18... | collective-permute-start | bytes 3317768 | tf_op jit(solution)/shard_map/ppermute | solution.py:650
  15.0 5.9 %collective-permute-start.3 = (bf16[1,192,512]{2,1,0:T(8,128)(2,1)S(1)}, bf16[1,192,512]{2,1,0:T(8,128)(2,1)S(1)}, u32[]{:S(2)}, u32[]{:S(2)}) collective-permute-start(bf16[1,192,512]{2,1,0:T(8,128)(2,1)S(1)} %get-tuple-element.25), channel_id=1, source_target_pairs={{0,4},{4,0},{8,12},{12,8},{16,20},{20,16},{24,28},{28,24},{1,5},{5... | collective-permute-start | bytes 589832 | tf_op jit(solution)/shard_map/ppermute | solution.py:638
  16.6 12.6 %collective-permute-start.2 = (bf16[128,1536]{1,0:T(8,128)(2,1)S(1)}, bf16[128,1536]{1,0:T(8,128)(2,1)S(1)}, u32[]{:S(2)}, u32[]{:S(2)}) collective-permute-start(bf16[128,1536]{1,0:T(8,128)(2,1)S(1)} %hold.5.refs_1_.refs_2_), channel_id=1, source_target_pairs={{0,2},{1,3},{2,0},{3,1},{4,6},{5,7},{6,4},{7,5},{8,10},{9,11},{10,... | collective-permute-start | bytes 1179656 | tf_op jit(solution)/shard_map/ppermute | solution.py:640
  20.9 8.4 %collective-permute-start.4 = (bf16[128,1408]{1,0:T(8,128)(2,1)S(1)}, bf16[128,1408]{1,0:T(8,128)(2,1)S(1)}, u32[]{:S(2)}, u32[]{:S(2)}) collective-permute-start(bf16[128,1408]{1,0:T(8,128)(2,1)S(1)} %hold.6.refs_0_), channel_id=1, source_target_pairs={{0,4},{4,0},{8,12},{12,8},{16,20},{20,16},{24,28},{28,24},{1,5},{5... | collective-permute-start | bytes 1081352 | tf_op jit(solution)/shard_map/ppermute | solution.py:638
  30.1 11.3 %collective-permute-start.7 = (bf16[128,1408]{1,0:T(8,128)(2,1)S(1)}, bf16[128,1408]{1,0:T(8,128)(2,1)S(1)}, u32[]{:S(2)}, u32[]{:S(2)}) collective-permute-start(bf16[128,1408]{1,0:T(8,128)(2,1)S(1)} %hold.6.refs_0_), channel_id=1, source_target_pairs={{0,2},{1,3},{2,0},{3,1},{4,6},{5,7},{6,4},{7,5},{8,10},{9,11},{10,... | collective-permute-start | bytes 1081352 | tf_op jit(solution)/shard_map/ppermute | solution.py:640
  33.7 15.0 %collective-permute-start.9 = (bf16[128,1408]{1,0:T(8,128)(2,1)S(1)}, bf16[128,1408]{1,0:T(8,128)(2,1)S(1)}, u32[]{:S(2)}, u32[]{:S(2)}) collective-permute-start(bf16[128,1408]{1,0:T(8,128)(2,1)S(1)} %collective-permute-done.4.refs_4_.refs_1_), channel_id=1, source_target_pairs={{0,2},{1,3},{2,0},{3,1},{4,6},{5,7},{6,4},{7,5},{8,10},{9,11},{10,... | collective-permute-start | bytes 1081352 | tf_op jit(solution)/shard_map/ppermute | solution.py:640
  36.8 16.1 %collective-permute-start.16 = (bf16[192,1472]{1,0:T(8,128)(2,1)S(1)}, bf16[192,1472]{1,0:T(8,128)(2,1)S(1)}, u32[]{:S(2)}, u32[]{:S(2)}) collective-permute-start(bf16[192,1472]{1,0:T(8,128)(2,1)S(1)} %first_sums.2.refs_6_), channel_id=1, source_target_pairs={{0,8},{4,12},{8,0},{12,4},{16,24},{20,28},{24,16},{28,20},{1,9},{5... | collective-permute-start | bytes 1695752 | tf_op jit(solution)/shard_map/ppermute | solution.py:650
  39.2 15.8 %collective-permute-start.11 = (bf16[3,192,512]{2,1,0:T(8,128)(2,1)S(1)}, bf16[3,192,512]{2,1,0:T(8,128)(2,1)S(1)}, u32[]{:S(2)}, u32[]{:S(2)}) collective-permute-start(bf16[3,192,512]{2,1,0:T(8,128)(2,1)S(1)} %get-tuple-element.27), channel_id=1, source_target_pairs={{0,4},{4,0},{8,12},{12,8},{16,20},{20,16},{24,28},{28,24},{1,5},{5... | collective-permute-start | bytes 1769480 | tf_op jit(solution)/shard_map/ppermute | solution.py:638
  39.7 28.3 %collective-permute-start.14 = (bf16[192,2880]{1,0:T(8,128)(2,1)S(1)}, bf16[192,2880]{1,0:T(8,128)(2,1)S(1)}, u32[]{:S(2)}, u32[]{:S(2)}) collective-permute-start(bf16[192,2880]{1,0:T(8,128)(2,1)S(1)} %get-tuple-element.28.refs_12_), channel_id=1, source_target_pairs={{8,16},{12,20},{16,8},{20,12},{9,17},{13,21},{17,9},{21,13},{10,18... | collective-permute-start | bytes 3317768 | tf_op jit(solution)/shard_map/ppermute | solution.py:650
  41.4 7.8 %collective-permute-start.8 = (bf16[128,1408]{1,0:T(8,128)(2,1)S(1)}, bf16[128,1408]{1,0:T(8,128)(2,1)S(1)}, u32[]{:S(2)}, u32[]{:S(2)}) collective-permute-start(bf16[128,1408]{1,0:T(8,128)(2,1)S(1)} %collective-permute-done.7.refs_2_.refs_4_), channel_id=1, source_target_pairs={{0,1},{1,0},{2,3},{3,2},{4,5},{5,4},{6,7},{7,6},{8,9},{9,8},{10,11... | collective-permute-start | bytes 1081352 | tf_op jit(solution)/shard_map/ppermute | solution.py:640
  55.0 15.2 %collective-permute-start.18 = (bf16[192,1408]{1,0:T(8,128)(2,1)S(1)}, bf16[192,1408]{1,0:T(8,128)(2,1)S(1)}, u32[]{:S(2)}, u32[]{:S(2)}) collective-permute-start(bf16[192,1408]{1,0:T(8,128)(2,1)S(1)} %hold.8.refs_2_.refs_10_), channel_id=1, source_target_pairs={{0,8},{4,12},{8,0},{12,4},{16,24},{20,28},{24,16},{28,20},{1,9},{5... | collective-permute-start | bytes 1622024 | tf_op jit(solution)/shard_map/ppermute | solution.py:650
  63.9 31.8 %collective-permute-start.25 = (bf16[192,2880]{1,0:T(8,128)(2,1)S(1)}, bf16[192,2880]{1,0:T(8,128)(2,1)S(1)}, u32[]{:S(2)}, u32[]{:S(2)}) collective-permute-start(bf16[192,2880]{1,0:T(8,128)(2,1)S(1)} %combine.6.refs_2_), channel_id=1, source_target_pairs={{0,8},{4,12},{24,16},{28,20},{1,9},{5,13},{25,17},{29,21},{2,10},{... | collective-permute-start | bytes 3317768 | tf_op jit(solution)/shard_map/ppermute | solution.py:650
  67.4 12.1 %collective-permute-start.17 = (bf16[192,1472]{1,0:T(8,128)(2,1)S(1)}, bf16[192,1472]{1,0:T(8,128)(2,1)S(1)}, u32[]{:S(2)}, u32[]{:S(2)}) collective-permute-start(bf16[192,1472]{1,0:T(8,128)(2,1)S(1)} %combine.5.refs_6_.refs_10_), channel_id=1, source_target_pairs={{8,16},{12,20},{16,8},{20,12},{9,17},{13,21},{17,9},{21,13},{10,18... | collective-permute-start | bytes 1695752 | tf_op jit(solution)/shard_map/ppermute | solution.py:650
  68.1 29.1 %collective-permute-start.15 = (bf16[192,2880]{1,0:T(8,128)(2,1)S(1)}, bf16[192,2880]{1,0:T(8,128)(2,1)S(1)}, u32[]{:S(2)}, u32[]{:S(2)}) collective-permute-start(bf16[192,2880]{1,0:T(8,128)(2,1)S(1)} %collective-permute-done.14.refs_13_), channel_id=1, source_target_pairs={{8,0},{12,4},{16,24},{20,28},{9,1},{13,5},{17,25},{21,29},{10,2},{... | collective-permute-start | bytes 3317768 | tf_op jit(solution)/shard_map/ppermute | solution.py:650
  70.9 8.7 %collective-permute-start.19 = (bf16[192,1408]{1,0:T(8,128)(2,1)S(1)}, bf16[192,1408]{1,0:T(8,128)(2,1)S(1)}, u32[]{:S(2)}, u32[]{:S(2)}) collective-permute-start(bf16[192,1408]{1,0:T(8,128)(2,1)S(1)} %combine.7.refs_14_.refs_15_), channel_id=1, source_target_pairs={{8,16},{12,20},{16,8},{20,12},{9,17},{13,21},{17,9},{21,13},{10,18... | collective-permute-start | bytes 1622024 | tf_op jit(solution)/shard_map/ppermute | solution.py:650
  76.3 19.4 %collective-permute-start.21 = (bf16[3,192,512]{2,1,0:T(8,128)(2,1)S(1)}, bf16[3,192,512]{2,1,0:T(8,128)(2,1)S(1)}, u32[]{:S(2)}, u32[]{:S(2)}) collective-permute-start(bf16[3,192,512]{2,1,0:T(8,128)(2,1)S(1)} %get-tuple-element.34), channel_id=1, source_target_pairs={{0,4},{4,0},{8,12},{12,8},{16,20},{20,16},{24,28},{28,24},{1,5},{5... | collective-permute-start | bytes 1769480 | tf_op jit(solution)/shard_map/ppermute | solution.py:638
  80.4 39.9 %collective-permute-start.24 = (bf16[192,2880]{1,0:T(8,128)(2,1)S(1)}, bf16[192,2880]{1,0:T(8,128)(2,1)S(1)}, u32[]{:S(2)}, u32[]{:S(2)}) collective-permute-start(bf16[192,2880]{1,0:T(8,128)(2,1)S(1)} %combine.8.refs_15_), channel_id=1, source_target_pairs={{0,8},{4,12},{8,0},{12,4},{16,24},{20,28},{24,16},{28,20},{1,9},{5... | collective-permute-start | bytes 3317768 | tf_op jit(solution)/shard_map/ppermute | solution.py:650
  96.5 18.8 %collective-permute-start.26 = (bf16[192,1472]{1,0:T(8,128)(2,1)S(1)}, bf16[192,1472]{1,0:T(8,128)(2,1)S(1)}, u32[]{:S(2)}, u32[]{:S(2)}) collective-permute-start(bf16[192,1472]{1,0:T(8,128)(2,1)S(1)} %get-tuple-element.39), channel_id=1, source_target_pairs={{8,16},{12,20},{16,8},{20,12},{9,17},{13,21},{17,9},{21,13},{10,18... | collective-permute-start | bytes 1695752 | tf_op jit(solution)/shard_map/ppermute | solution.py:650
  97.3 18.0 %collective-permute-start.27 = (bf16[192,1408]{1,0:T(8,128)(2,1)S(1)}, bf16[192,1408]{1,0:T(8,128)(2,1)S(1)}, u32[]{:S(2)}, u32[]{:S(2)}) collective-permute-start(bf16[192,1408]{1,0:T(8,128)(2,1)S(1)} %hold.9), channel_id=1, source_target_pairs={{8,16},{12,20},{16,8},{20,12},{9,17},{13,21},{17,9},{21,13},{10,18... | collective-permute-start | bytes 1622024 | tf_op jit(solution)/shard_map/ppermute | solution.py:650
  101.8 10.6 %collective-permute-start.22 = (bf16[1,192,512]{2,1,0:T(8,128)(2,1)S(1)}, bf16[1,192,512]{2,1,0:T(8,128)(2,1)S(1)}, u32[]{:S(2)}, u32[]{:S(2)}) collective-permute-start(bf16[1,192,512]{2,1,0:T(8,128)(2,1)S(1)} %get-tuple-element.36), channel_id=1, source_target_pairs={{0,4},{4,0},{8,12},{12,8},{16,20},{20,16},{24,28},{28,24},{1,5},{5... | collective-permute-start | bytes 589832 | tf_op jit(solution)/shard_map/ppermute | solution.py:638
  104.4 8.0 %collective-permute-start.23 = (bf16[1,192,512]{2,1,0:T(8,128)(2,1)S(1)}, bf16[1,192,512]{2,1,0:T(8,128)(2,1)S(1)}, u32[]{:S(2)}, u32[]{:S(2)}) collective-permute-start(bf16[1,192,512]{2,1,0:T(8,128)(2,1)S(1)} %get-tuple-element.38), channel_id=1, source_target_pairs={{0,4},{4,0},{8,12},{12,8},{16,20},{20,16},{24,28},{28,24},{1,5},{5... | collective-permute-start | bytes 589832 | tf_op jit(solution)/shard_map/ppermute | solution.py:638
  (11 other events, 68.6 us)

commit v9 on v8

--- a/solution.py
+++ b/solution.py
@@ -12,6 +12,7 @@
 SCALE = 1_000_000
 BEGIN_WEIGHT = 600
 FIRST_WEIGHT = 12_000
+LAST_WEIGHT = 90
 NT = (((1,), (1,)), ((), ()))
 NN = (((1,), (0,)), ((), ()))
 f32 = jnp.float32
@@ -352,7 +353,7 @@
         out_specs=whole(),
         scratch_shapes=[pltpu.VMEM((2 * slots, width), bf16)],
         compiler_params=params(),
-        cost_estimate=taking(BEGIN_WEIGHT),
+        cost_estimate=taking(1),
         name="first_sums",
     )(where, *arrays[0], *arrays[1], own, other, coming, *after)
 
@@ -388,7 +389,7 @@
             outs[chunk][...] = total
 
 
-def combine(table, where, coming, first, rest, turn, name, used, cut, after, chunked=False):
+def combine(table, where, coming, first, rest, turn, name, used, cut, after, chunked=False, weight=1):
     units = first[0].shape[1]
     model = sum(part.shape[2] for part in first)
     block = rows_of(units)
@@ -417,7 +418,7 @@
             out_specs=[pl.BlockSpec((block, count), lambda j, s: (j, 0)) for count in widths],
         ),
         compiler_params=params(),
-        cost_estimate=taking(1.5),
+        cost_estimate=taking(weight),
         name="combine",
     )(where, *coming, *operands, *after)
 
@@ -692,12 +693,13 @@
             table, where, rows, late_rows, own, other_first, got[1, "B"][0], model, start, columns, after
         )
         if first:
+            (value,) = hold([value], [got[2, "A"][0]], BEGIN_WEIGHT)
             (value,) = hold([value], [other_rest])
         got.setdefault((2, "A"), []).append(swap_z(value, "A"))
         first.append(
             products(table, where, rows, late_rows, own, other_first, 0, model, columns, "first_kept", [value], True)
         )
-        after = [got[2, "A"][0], first[0]]
+        after = [first[0]]
     marker = value
     got[2, "B"] = [swap_z(got[1, "A"][0], "B")]
 
@@ -725,9 +727,10 @@
             coming = [] if set(senders) <= ends else coming
         if chunk is not None:
             coming, parts, start = [coming[chunk]], (first[chunk:][:1], rest[chunk:][:1]), 0
-        values = list(combine(table, where, coming, *parts, turn, name, used, start, after, chunked))
+        weight = LAST_WEIGHT if (turn, name) == (depth, "A") else 1
+        values = list(combine(table, where, coming, *parts, turn, name, used, start, after, chunked, weight))
         if waited:
-            values[1:] = hold(values[1:], list(waited))
+            values[1:] = hold(values[1:], list(waited), 2 * LAST_WEIGHT)
         got.setdefault((turn, name), []).extend(swap_z(value, name, senders) for value in values)
         return values[-1]
 

time: 123 us -> 125 us (1.016)
    ppermute x12, starting transfers between devices: 29.1 us -> 27.4 us  [swap_z(): return lax.ppermute(value, 'ctx', pairs)]
    ppermute x8, starting transfers between devices: 8.46 us -> 10.1 us  [swap(): return lax.ppermute(value, 'ctx', [(i, i ^ x) for i in range(groups)])]
    ppermute x8, waiting for transfers between devices: 12.3 us -> 13.7 us  [swap(): return lax.ppermute(value, 'ctx', [(i, i ^ x) for i in range(groups)])]
  transfers between devices with their start and end apart: 28 -> 28, of which waited for: 11 -> 13; matrix products, arithmetic and copies ran while one was open for 1% -> 1% of each run, Pallas kernels for 27% -> 27%
where the time goes in v9:
time: 125 us; the launch traced here: 123 us
  starting transfers between devices  42.2 us (34%)
  Pallas kernels  36.6 us (29%)
  waiting for transfers between devices  33.7 us (27%)
  blocking collectives  6.39 us (5%)
  local copies, waits for them, and re-layouts  3.12 us (2%)
    ppermute x12, starting transfers between devices, swap_z(): return lax.ppermute(value, 'ctx', pairs)  27.4 us
    ppermute x8, waiting for transfers between devices, swap(): return lax.ppermute(value, 'ctx', [(i, i ^ x) for i in range(groups)])  13.7 us
    ppermute x8, waiting for transfers between devices, swap(): return lax.ppermute(value, 'exp', [(i, i ^ exp) for i in range(experts)])  10.7 us
    ppermute x8, starting transfers between devices, swap(): return lax.ppermute(value, 'ctx', [(i, i ^ x) for i in range(groups)])  10.1 us
    pallas_call x3, Pallas kernels, back_part(): pl.pallas_call(functools.partial(back_kernel, table, model, cut, counts,...  9.99 us
    ppermute x12, waiting for transfers between devices, swap_z(): return lax.ppermute(value, 'ctx', pairs)  9.26 us
    pallas_call x4, Pallas kernels, products(): pl.pallas_call(functools.partial(products_kernel, table, model, counts, p...  7.85 us
    all_to_all x1, blocking collectives, per_device_full(): lax.all_to_all(slot_grad.reshape(experts, tokens), 'exp', split_axis=0, c...  6.39 us
  transfers between devices with their start and end apart: 28, of which 13 were waited for; matrix products, arithmetic and copies ran while one was open for 1% of the time, Pallas kernels for 27%

profile of v9, /device:TPU:0, one launch (start us, length us, event | category | flops | bytes accessed | tf_op | source)
XLA Modules:
  0.0 123.0 jit_solution(7536598413543278811)
XLA Ops:
  0.6 2.2 %make_rows.1 = (bf16[128,1536]{1,0:T(8,128)(2,1)}, bf16[128,1408]{1,0:T(8,128)(2,1)}, f32[4,128]{1,0:T(4,128)}) custom-call(bf16[2880,128]{1,0:T(8,128)(2,1)} %bitcast.22, f32[4,128]{1,0:T(4,128)} %bitcast.23, s32[4,128]{1,0:T(4,128)} %bitcast.18), custom_call_target="tpu_custom_call" | custom-call | flops 2000000 | bytes 6000000 | tf_op jit(solution)/shard_map/make_rows/pallas_call | solution.py:162
  2.8 3.0 %collective-permute-start.1 = (bf16[128,1536]{1,0:T(8,128)(2,1)}, bf16[128,1536]{1,0:T(8,128)(2,1)S(1)}, u32[]{:S(2)}, u32[]{:S(2)}) collective-permute-start(bf16[128,1536]{1,0:T(8,128)(2,1)} %get-tuple-element.23.refs_0_), channel_id=1, source_target_pairs={{0,4},{4,0},{8,12},{12,8},{16,20},{20,16},{24,28},{28,24},{1,5},{5... | collective-permute-start | bytes 1179656 | tf_op jit(solution)/shard_map/ppermute | solution.py:639
  12.8 2.2 %split_hidden.1 = (bf16[4,192,512]{2,1,0:T(8,128)(2,1)S(1)}, bf16[1,192,512]{2,1,0:T(8,128)(2,1)S(1)}, bf16[3,192,512]{2,1,0:T(8,128)(2,1)S(1)}) custom-call(s32[32]{0:T(128)S(1)} %dynamic-slice_bitcast_fusion.where_ref, bf16[512,1536]{1,0:T(8,128)(2,1)S(1)} %bitcast.14, bf16[128,1536]{1,0:T(8,128)(2,1)S(1)} %copy-done.1), custom_call_target="tpu_custom_call" | custom-call | flops 2000000 | bytes 6000000 | tf_op jit(solution)/shard_map/split_hidden/pallas_call | solution.py:253
  18.1 2.7 %collective-permute-done.3.refs_2_.refs_5_.refs_9_ = bf16[1,192,512]{2,1,0:T(8,128)(2,1)S(1)} collective-permute-done((bf16[1,192,512]{2,1,0:T(8,128)(2,1)S(1)}, bf16[1,192,512]{2,1,0:T(8,128)(2,1)S(1)}, u32[]{:S(2)}, u32[]{:S(2)}) %collective-permute-start.3) | collective-permute-done | bytes 196640 | tf_op jit(solution)/shard_map/ppermute | solution.py:639
  21.4 7.9 %collective-permute-done.4.refs_4_.refs_1_ = bf16[128,1408]{1,0:T(8,128)(2,1)S(1)} collective-permute-done((bf16[128,1408]{1,0:T(8,128)(2,1)S(1)}, bf16[128,1408]{1,0:T(8,128)(2,1)S(1)}, u32[]{:S(2)}, u32[]{:S(2)}) %collective-permute-start.4) | collective-permute-done | bytes 360480 | tf_op jit(solution)/shard_map/ppermute | solution.py:639
  31.5 2.2 %collective-permute-done.13.refs_1_ = bf16[192,2880]{1,0:T(8,128)(2,1)S(1)} collective-permute-done((bf16[192,2880]{1,0:T(8,128)(2,1)}, bf16[192,2880]{1,0:T(8,128)(2,1)S(1)}, u32[]{:S(2)}, u32[]{:S(2)}) %collective-permute-start.13) | collective-permute-done | bytes 1105952 | tf_op jit(solution)/shard_map/ppermute | solution.py:651
  34.6 2.2 %first_sums.2.refs_6_ = bf16[192,1472]{1,0:T(8,128)(2,1)S(1)} custom-call(s32[32]{0:T(128)S(1)} %dynamic-slice_bitcast_fusion.where_ref, bf16[4,128,1536]{2,1,0:T(8,128)(2,1)S(1)} %pack_rows.2.refs_0_.refs_2_.refs_6_, bf16[4,128,1536]{2,1,0:T(8,128)(2,1)S(1)} %collective-permute-done.5.refs_1_.refs_3_.refs_7_, ...), custom_call_target="tpu_custom_call" | custom-call | flops 1000000 | bytes 3000000 | tf_op jit(solution)/shard_map/first_sums/pallas_call | solution.py:349
  36.8 2.4 %collective-permute-start.16 = (bf16[192,1472]{1,0:T(8,128)(2,1)S(1)}, bf16[192,1472]{1,0:T(8,128)(2,1)S(1)}, u32[]{:S(2)}, u32[]{:S(2)}) collective-permute-start(bf16[192,1472]{1,0:T(8,128)(2,1)S(1)} %first_sums.2.refs_6_), channel_id=1, source_target_pairs={{0,8},{4,12},{8,0},{12,4},{16,24},{20,28},{24,16},{28,20},{1,9},{5... | collective-permute-start | bytes 1695752 | tf_op jit(solution)/shard_map/ppermute | solution.py:651
  41.4 7.3 %collective-permute-done.9.refs_4_.refs_6_ = bf16[128,1408]{1,0:T(8,128)(2,1)S(1)} collective-permute-done((bf16[128,1408]{1,0:T(8,128)(2,1)S(1)}, bf16[128,1408]{1,0:T(8,128)(2,1)S(1)}, u32[]{:S(2)}, u32[]{:S(2)}) %collective-permute-start.9) | collective-permute-done | bytes 360480 | tf_op jit(solution)/shard_map/ppermute | solution.py:641
  50.4 2.1 %first_sums.3.refs_0_ = bf16[192,1408]{1,0:T(8,128)(2,1)S(1)} custom-call(s32[32]{0:T(128)S(1)} %dynamic-slice_bitcast_fusion.where_ref, bf16[2,128,1408]{2,1,0:T(8,128)(2,1)S(1)} %pack_rows.3.refs_0_.refs_2_, bf16[2,128,1408]{2,1,0:T(8,128)(2,1)S(1)} %collective-permute-done.6.refs_7_.refs_1_.refs_3_, ...), custom_call_target="tpu_custom_call" | custom-call | flops 1000000 | bytes 3000000 | tf_op jit(solution)/shard_map/first_sums/pallas_call | solution.py:349
  57.0 3.4 %rest_kept.3.refs_1_.refs_3_.refs_2_.refs_4_ = f32[3,192,1408]{2,1,0:T(8,128)S(1)} custom-call(s32[32]{0:T(128)S(1)} %dynamic-slice_bitcast_fusion.where_ref, bf16[2,128,1408]{2,1,0:T(8,128)(2,1)S(1)} %pack_rows.3.refs_0_.refs_2_, bf16[2,128,1408]{2,1,0:T(8,128)(2,1)S(1)} %collective-permute-done.6.refs_7_.refs_1_.refs_3_, ...), custom_call_target="tpu_custom_call" | custom-call | flops 4000000 | bytes 12000000 | tf_op jit(solution)/shard_map/rest_kept/pallas_call | solution.py:313
  60.4 3.4 %rest_kept.2.refs_0_.refs_2_.refs_1_.refs_3_ = f32[3,192,1472]{2,1,0:T(8,128)S(1)} custom-call(s32[32]{0:T(128)S(1)} %dynamic-slice_bitcast_fusion.where_ref, bf16[4,128,1536]{2,1,0:T(8,128)(2,1)S(1)} %pack_rows.2.refs_0_.refs_2_.refs_6_, bf16[4,128,1536]{2,1,0:T(8,128)(2,1)S(1)} %collective-permute-done.5.refs_1_.refs_3_.refs_7_, ...), custom_call_target="tpu_custom_call" | custom-call | flops 4000000 | bytes 12000000 | tf_op jit(solution)/shard_map/rest_kept/pallas_call | solution.py:313
  64.6 4.4 %collective-permute-start.25 = (bf16[192,2880]{1,0:T(8,128)(2,1)S(1)}, bf16[192,2880]{1,0:T(8,128)(2,1)S(1)}, u32[]{:S(2)}, u32[]{:S(2)}) collective-permute-start(bf16[192,2880]{1,0:T(8,128)(2,1)S(1)} %combine.6.refs_2_), channel_id=1, source_target_pairs={{0,8},{4,12},{24,16},{28,20},{1,9},{5,13},{25,17},{29,21},{2,10},{... | collective-permute-start | bytes 3317768 | tf_op jit(solution)/shard_map/ppermute | solution.py:651
  72.5 4.7 %back_part.3 = (bf16[3,192,512]{2,1,0:T(8,128)(2,1)S(1)}, bf16[3,192,512]{2,1,0:T(8,128)(2,1)S(1)}, f32[8,1024]{1,0:T(8,128)S(1)}) custom-call(s32[32]{0:T(128)S(1)} %dynamic-slice_bitcast_fusion.where_ref, bf16[4,128,1536]{2,1,0:T(8,128)(2,1)S(1)} %pack_rows.2.refs_0_.refs_2_.refs_6_, ...), custom_call_target="tpu_custom_call" | custom-call | flops 6000000 | bytes 18000000 | tf_op jit(solution)/shard_map/back_part/pallas_call | solution.py:548
  77.2 1.7 %collective-permute-start.21 = (bf16[3,192,512]{2,1,0:T(8,128)(2,1)S(1)}, bf16[3,192,512]{2,1,0:T(8,128)(2,1)S(1)}, u32[]{:S(2)}, u32[]{:S(2)}) collective-permute-start(bf16[3,192,512]{2,1,0:T(8,128)(2,1)S(1)} %get-tuple-element.34), channel_id=1, source_target_pairs={{0,4},{4,0},{8,12},{12,8},{16,20},{20,16},{24,28},{28,24},{1,5},{5... | collective-permute-start | bytes 1769480 | tf_op jit(solution)/shard_map/ppermute | solution.py:639
  78.9 2.6 %back_part.4 = (bf16[1,192,512]{2,1,0:T(8,128)(2,1)S(1)}, bf16[1,192,512]{2,1,0:T(8,128)(2,1)S(1)}, f32[8,1024]{1,0:T(8,128)S(1)}) custom-call(s32[32]{0:T(128)S(1)} %dynamic-slice_bitcast_fusion.where_ref, bf16[4,128,1536]{2,1,0:T(8,128)(2,1)S(1)} %pack_rows.2.refs_0_.refs_2_.refs_6_, ...), custom_call_target="tpu_custom_call" | custom-call | flops 6000000 | bytes 18000000 | tf_op jit(solution)/shard_map/back_part/pallas_call | solution.py:548
  82.4 11.9 %collective-permute-start.24 = (bf16[192,2880]{1,0:T(8,128)(2,1)S(1)}, bf16[192,2880]{1,0:T(8,128)(2,1)S(1)}, u32[]{:S(2)}, u32[]{:S(2)}) collective-permute-start(bf16[192,2880]{1,0:T(8,128)(2,1)S(1)} %combine.8.refs_15_), channel_id=1, source_target_pairs={{0,8},{4,12},{8,0},{12,4},{16,24},{20,28},{24,16},{28,20},{1,9},{5... | collective-permute-start | bytes 3317768 | tf_op jit(solution)/shard_map/ppermute | solution.py:651
  95.9 3.1 %collective-permute-done.15.refs_11_.refs_1_ = bf16[192,2880]{1,0:T(8,128)(2,1)S(1)} collective-permute-done((bf16[192,2880]{1,0:T(8,128)(2,1)S(1)}, bf16[192,2880]{1,0:T(8,128)(2,1)S(1)}, u32[]{:S(2)}, u32[]{:S(2)}) %collective-permute-start.15) | collective-permute-done | bytes 1105952 | tf_op jit(solution)/shard_map/ppermute | solution.py:651
  99.8 2.7 %back_part.5 = (bf16[1,192,512]{2,1,0:T(8,128)(2,1)S(1)}, bf16[1,192,512]{2,1,0:T(8,128)(2,1)S(1)}, f32[8,1024]{1,0:T(8,128)S(1)}) custom-call(s32[32]{0:T(128)S(1)} %dynamic-slice_bitcast_fusion.where_ref, bf16[4,128,1536]{2,1,0:T(8,128)(2,1)S(1)} %pack_rows.2.refs_0_.refs_2_.refs_6_, ...), custom_call_target="tpu_custom_call" | custom-call | flops 6000000 | bytes 18000000 | tf_op jit(solution)/shard_map/back_part/pallas_call | solution.py:548
  102.4 1.7 %collective-permute-start.20 = (f32[1,512]{1,0:T(1,128)S(1)}, f32[1,512]{1,0:T(1,128)S(1)}, u32[]{:S(2)}, u32[]{:S(2)}) collective-permute-start(f32[1,512]{1,0:T(1,128)S(1)} %slice.7), channel_id=1, source_target_pairs={{0,4},{4,0},{8,12},{12,8},{16,20},{20,16},{24,28},{28,24},{1,5},{5... | collective-permute-start | bytes 6152 | tf_op jit(solution)/shard_map/ppermute | solution.py:639
  106.2 1.6 %collective-permute-start.23 = (bf16[1,192,512]{2,1,0:T(8,128)(2,1)S(1)}, bf16[1,192,512]{2,1,0:T(8,128)(2,1)S(1)}, u32[]{:S(2)}, u32[]{:S(2)}) collective-permute-start(bf16[1,192,512]{2,1,0:T(8,128)(2,1)S(1)} %get-tuple-element.38), channel_id=1, source_target_pairs={{0,4},{4,0},{8,12},{12,8},{16,20},{20,16},{24,28},{28,24},{1,5},{5... | collective-permute-start | bytes 589832 | tf_op jit(solution)/shard_map/ppermute | solution.py:639
  107.8 6.4 %all_to_all.11 = f32[4,1,128]{2,1,0:T(1,128)S(1)} all-to-all(f32[4,1,128]{2,1,0:T(1,128)S(1)} %add_bitcast_fusion), channel_id=1, replica_groups=mesh['ctx'=8,'exp'=4] {'exp'}, dimensions={0} | all-to-all | bytes 4096 | tf_op jit(solution)/shard_map/all_to_all | solution.py:760
  114.8 2.9 %join_hidden.1 = bf16[512,1536]{1,0:T(8,128)(2,1)} custom-call(s32[32]{0:T(128)S(1)} %dynamic-slice_bitcast_fusion.where_ref, bf16[3,192,512]{2,1,0:T(8,128)(2,1)S(1)} %get-tuple-element.33.refs_0_, bf16[3,192,512]{2,1,0:T(8,128)(2,1)S(1)} %collective-permute-done.21.refs_1_.refs_4_, bf16[1,192,512]{2,1,0:T(8,128)(2,1)S(1)} %get-tuple-element.35.refs_2_, ...), custom_call_target="tpu_custom_call" | custom-call | flops 2000000 | bytes 6000000 | tf_op jit(solution)/shard_map/join_hidden/pallas_call | solution.py:590
  117.7 3.7 %collective-permute-done.24.refs_0_ = bf16[192,2880]{1,0:T(8,128)(2,1)S(1)} collective-permute-done((bf16[192,2880]{1,0:T(8,128)(2,1)S(1)}, bf16[192,2880]{1,0:T(8,128)(2,1)S(1)}, u32[]{:S(2)}, u32[]{:S(2)}) %collective-permute-start.24) | collective-permute-done | bytes 1105952 | tf_op jit(solution)/shard_map/ppermute | solution.py:651
  (77 shorter events, 33.6 us)
Async XLA Ops:
  2.8 12.8 %collective-permute-start.1 = (bf16[128,1536]{1,0:T(8,128)(2,1)}, bf16[128,1536]{1,0:T(8,128)(2,1)S(1)}, u32[]{:S(2)}, u32[]{:S(2)}) collective-permute-start(bf16[128,1536]{1,0:T(8,128)(2,1)} %get-tuple-element.23.refs_0_), channel_id=1, source_target_pairs={{0,4},{4,0},{8,12},{12,8},{16,20},{20,16},{24,28},{28,24},{1,5},{5... | collective-permute-start | bytes 1179656 | tf_op jit(solution)/shard_map/ppermute | solution.py:639
  5.8 10.8 %collective-permute-start = (bf16[128,1536]{1,0:T(8,128)(2,1)}, bf16[128,1536]{1,0:T(8,128)(2,1)S(1)}, u32[]{:S(2)}, u32[]{:S(2)}) collective-permute-start(bf16[128,1536]{1,0:T(8,128)(2,1)} %get-tuple-element.23.refs_0_), channel_id=1, source_target_pairs={{0,2},{1,3},{2,0},{3,1},{4,6},{5,7},{6,4},{7,5},{8,10},{9,11},{10,... | collective-permute-start | bytes 1179656 | tf_op jit(solution)/shard_map/ppermute | solution.py:641
  7.4 26.3 %collective-permute-start.13 = (bf16[192,2880]{1,0:T(8,128)(2,1)}, bf16[192,2880]{1,0:T(8,128)(2,1)S(1)}, u32[]{:S(2)}, u32[]{:S(2)}) collective-permute-start(bf16[192,2880]{1,0:T(8,128)(2,1)} %bitcast.15), channel_id=1, source_target_pairs={{0,8},{4,12},{8,0},{12,4},{16,24},{20,28},{24,16},{28,20},{1,9},{5... | collective-permute-start | bytes 3317768 | tf_op jit(solution)/shard_map/ppermute | solution.py:651
  8.9 25.2 %collective-permute-start.12 = (bf16[192,2880]{1,0:T(8,128)(2,1)}, bf16[192,2880]{1,0:T(8,128)(2,1)S(1)}, u32[]{:S(2)}, u32[]{:S(2)}) collective-permute-start(bf16[192,2880]{1,0:T(8,128)(2,1)} %bitcast.16), channel_id=1, source_target_pairs={{8,16},{12,20},{16,8},{20,12},{9,17},{13,21},{17,9},{21,13},{10,18... | collective-permute-start | bytes 3317768 | tf_op jit(solution)/shard_map/ppermute | solution.py:651
  15.0 5.9 %collective-permute-start.3 = (bf16[1,192,512]{2,1,0:T(8,128)(2,1)S(1)}, bf16[1,192,512]{2,1,0:T(8,128)(2,1)S(1)}, u32[]{:S(2)}, u32[]{:S(2)}) collective-permute-start(bf16[1,192,512]{2,1,0:T(8,128)(2,1)S(1)} %get-tuple-element.25), channel_id=1, source_target_pairs={{0,4},{4,0},{8,12},{12,8},{16,20},{20,16},{24,28},{28,24},{1,5},{5... | collective-permute-start | bytes 589832 | tf_op jit(solution)/shard_map/ppermute | solution.py:639
  16.6 12.6 %collective-permute-start.2 = (bf16[128,1536]{1,0:T(8,128)(2,1)S(1)}, bf16[128,1536]{1,0:T(8,128)(2,1)S(1)}, u32[]{:S(2)}, u32[]{:S(2)}) collective-permute-start(bf16[128,1536]{1,0:T(8,128)(2,1)S(1)} %hold.6.refs_1_.refs_2_), channel_id=1, source_target_pairs={{0,2},{1,3},{2,0},{3,1},{4,6},{5,7},{6,4},{7,5},{8,10},{9,11},{10,... | collective-permute-start | bytes 1179656 | tf_op jit(solution)/shard_map/ppermute | solution.py:641
  20.9 8.4 %collective-permute-start.4 = (bf16[128,1408]{1,0:T(8,128)(2,1)S(1)}, bf16[128,1408]{1,0:T(8,128)(2,1)S(1)}, u32[]{:S(2)}, u32[]{:S(2)}) collective-permute-start(bf16[128,1408]{1,0:T(8,128)(2,1)S(1)} %hold.7.refs_0_), channel_id=1, source_target_pairs={{0,4},{4,0},{8,12},{12,8},{16,20},{20,16},{24,28},{28,24},{1,5},{5... | collective-permute-start | bytes 1081352 | tf_op jit(solution)/shard_map/ppermute | solution.py:639
  30.1 11.3 %collective-permute-start.7 = (bf16[128,1408]{1,0:T(8,128)(2,1)S(1)}, bf16[128,1408]{1,0:T(8,128)(2,1)S(1)}, u32[]{:S(2)}, u32[]{:S(2)}) collective-permute-start(bf16[128,1408]{1,0:T(8,128)(2,1)S(1)} %hold.7.refs_0_), channel_id=1, source_target_pairs={{0,2},{1,3},{2,0},{3,1},{4,6},{5,7},{6,4},{7,5},{8,10},{9,11},{10,... | collective-permute-start | bytes 1081352 | tf_op jit(solution)/shard_map/ppermute | solution.py:641
  33.7 15.0 %collective-permute-start.9 = (bf16[128,1408]{1,0:T(8,128)(2,1)S(1)}, bf16[128,1408]{1,0:T(8,128)(2,1)S(1)}, u32[]{:S(2)}, u32[]{:S(2)}) collective-permute-start(bf16[128,1408]{1,0:T(8,128)(2,1)S(1)} %collective-permute-done.4.refs_4_.refs_1_), channel_id=1, source_target_pairs={{0,2},{1,3},{2,0},{3,1},{4,6},{5,7},{6,4},{7,5},{8,10},{9,11},{10,... | collective-permute-start | bytes 1081352 | tf_op jit(solution)/shard_map/ppermute | solution.py:641
  36.8 16.1 %collective-permute-start.16 = (bf16[192,1472]{1,0:T(8,128)(2,1)S(1)}, bf16[192,1472]{1,0:T(8,128)(2,1)S(1)}, u32[]{:S(2)}, u32[]{:S(2)}) collective-permute-start(bf16[192,1472]{1,0:T(8,128)(2,1)S(1)} %first_sums.2.refs_6_), channel_id=1, source_target_pairs={{0,8},{4,12},{8,0},{12,4},{16,24},{20,28},{24,16},{28,20},{1,9},{5... | collective-permute-start | bytes 1695752 | tf_op jit(solution)/shard_map/ppermute | solution.py:651
  39.2 15.1 %collective-permute-start.11 = (bf16[3,192,512]{2,1,0:T(8,128)(2,1)S(1)}, bf16[3,192,512]{2,1,0:T(8,128)(2,1)S(1)}, u32[]{:S(2)}, u32[]{:S(2)}) collective-permute-start(bf16[3,192,512]{2,1,0:T(8,128)(2,1)S(1)} %get-tuple-element.27), channel_id=1, source_target_pairs={{0,4},{4,0},{8,12},{12,8},{16,20},{20,16},{24,28},{28,24},{1,5},{5... | collective-permute-start | bytes 1769480 | tf_op jit(solution)/shard_map/ppermute | solution.py:639
  39.7 29.3 %collective-permute-start.14 = (bf16[192,2880]{1,0:T(8,128)(2,1)S(1)}, bf16[192,2880]{1,0:T(8,128)(2,1)S(1)}, u32[]{:S(2)}, u32[]{:S(2)}) collective-permute-start(bf16[192,2880]{1,0:T(8,128)(2,1)S(1)} %get-tuple-element.28.refs_12_), channel_id=1, source_target_pairs={{8,16},{12,20},{16,8},{20,12},{9,17},{13,21},{17,9},{21,13},{10,18... | collective-permute-start | bytes 3317768 | tf_op jit(solution)/shard_map/ppermute | solution.py:651
  41.4 7.8 %collective-permute-start.8 = (bf16[128,1408]{1,0:T(8,128)(2,1)S(1)}, bf16[128,1408]{1,0:T(8,128)(2,1)S(1)}, u32[]{:S(2)}, u32[]{:S(2)}) collective-permute-start(bf16[128,1408]{1,0:T(8,128)(2,1)S(1)} %collective-permute-done.7.refs_2_.refs_4_), channel_id=1, source_target_pairs={{0,1},{1,0},{2,3},{3,2},{4,5},{5,4},{6,7},{7,6},{8,9},{9,8},{10,11... | collective-permute-start | bytes 1081352 | tf_op jit(solution)/shard_map/ppermute | solution.py:641
  54.3 16.8 %collective-permute-start.18 = (bf16[192,1408]{1,0:T(8,128)(2,1)S(1)}, bf16[192,1408]{1,0:T(8,128)(2,1)S(1)}, u32[]{:S(2)}, u32[]{:S(2)}) collective-permute-start(bf16[192,1408]{1,0:T(8,128)(2,1)S(1)} %hold.10.refs_2_.refs_10_), channel_id=1, source_target_pairs={{0,8},{4,12},{8,0},{12,4},{16,24},{20,28},{24,16},{28,20},{1,9},{5... | collective-permute-start | bytes 1622024 | tf_op jit(solution)/shard_map/ppermute | solution.py:651
  56.3 25.3 %collective-permute-start.17 = (bf16[192,1472]{1,0:T(8,128)(2,1)S(1)}, bf16[192,1472]{1,0:T(8,128)(2,1)S(1)}, u32[]{:S(2)}, u32[]{:S(2)}) collective-permute-start(bf16[192,1472]{1,0:T(8,128)(2,1)S(1)} %combine.5.refs_6_.refs_10_), channel_id=1, source_target_pairs={{8,16},{12,20},{16,8},{20,12},{9,17},{13,21},{17,9},{21,13},{10,18... | collective-permute-start | bytes 1695752 | tf_op jit(solution)/shard_map/ppermute | solution.py:651
  64.6 29.7 %collective-permute-start.25 = (bf16[192,2880]{1,0:T(8,128)(2,1)S(1)}, bf16[192,2880]{1,0:T(8,128)(2,1)S(1)}, u32[]{:S(2)}, u32[]{:S(2)}) collective-permute-start(bf16[192,2880]{1,0:T(8,128)(2,1)S(1)} %combine.6.refs_2_), channel_id=1, source_target_pairs={{0,8},{4,12},{24,16},{28,20},{1,9},{5,13},{25,17},{29,21},{2,10},{... | collective-permute-start | bytes 3317768 | tf_op jit(solution)/shard_map/ppermute | solution.py:651
  69.0 29.9 %collective-permute-start.15 = (bf16[192,2880]{1,0:T(8,128)(2,1)S(1)}, bf16[192,2880]{1,0:T(8,128)(2,1)S(1)}, u32[]{:S(2)}, u32[]{:S(2)}) collective-permute-start(bf16[192,2880]{1,0:T(8,128)(2,1)S(1)} %collective-permute-done.14.refs_13_), channel_id=1, source_target_pairs={{8,0},{12,4},{16,24},{20,28},{9,1},{13,5},{17,25},{21,29},{10,2},{... | collective-permute-start | bytes 3317768 | tf_op jit(solution)/shard_map/ppermute | solution.py:651
  71.8 9.8 %collective-permute-start.19 = (bf16[192,1408]{1,0:T(8,128)(2,1)S(1)}, bf16[192,1408]{1,0:T(8,128)(2,1)S(1)}, u32[]{:S(2)}, u32[]{:S(2)}) collective-permute-start(bf16[192,1408]{1,0:T(8,128)(2,1)S(1)} %combine.7.refs_14_.refs_15_), channel_id=1, source_target_pairs={{8,16},{12,20},{16,8},{20,12},{9,17},{13,21},{17,9},{21,13},{10,18... | collective-permute-start | bytes 1622024 | tf_op jit(solution)/shard_map/ppermute | solution.py:651
  77.2 17.1 %collective-permute-start.21 = (bf16[3,192,512]{2,1,0:T(8,128)(2,1)S(1)}, bf16[3,192,512]{2,1,0:T(8,128)(2,1)S(1)}, u32[]{:S(2)}, u32[]{:S(2)}) collective-permute-start(bf16[3,192,512]{2,1,0:T(8,128)(2,1)S(1)} %get-tuple-element.34), channel_id=1, source_target_pairs={{0,4},{4,0},{8,12},{12,8},{16,20},{20,16},{24,28},{28,24},{1,5},{5... | collective-permute-start | bytes 1769480 | tf_op jit(solution)/shard_map/ppermute | solution.py:639
  82.4 39.0 %collective-permute-start.24 = (bf16[192,2880]{1,0:T(8,128)(2,1)S(1)}, bf16[192,2880]{1,0:T(8,128)(2,1)S(1)}, u32[]{:S(2)}, u32[]{:S(2)}) collective-permute-start(bf16[192,2880]{1,0:T(8,128)(2,1)S(1)} %combine.8.refs_15_), channel_id=1, source_target_pairs={{0,8},{4,12},{8,0},{12,4},{16,24},{20,28},{24,16},{28,20},{1,9},{5... | collective-permute-start | bytes 3317768 | tf_op jit(solution)/shard_map/ppermute | solution.py:651
  95.2 22.6 %collective-permute-start.26 = (bf16[192,1472]{1,0:T(8,128)(2,1)S(1)}, bf16[192,1472]{1,0:T(8,128)(2,1)S(1)}, u32[]{:S(2)}, u32[]{:S(2)}) collective-permute-start(bf16[192,1472]{1,0:T(8,128)(2,1)S(1)} %get-tuple-element.39), channel_id=1, source_target_pairs={{8,16},{12,20},{16,8},{20,12},{9,17},{13,21},{17,9},{21,13},{10,18... | collective-permute-start | bytes 1695752 | tf_op jit(solution)/shard_map/ppermute | solution.py:651
  98.9 18.8 %collective-permute-start.27 = (bf16[192,1408]{1,0:T(8,128)(2,1)S(1)}, bf16[192,1408]{1,0:T(8,128)(2,1)S(1)}, u32[]{:S(2)}, u32[]{:S(2)}) collective-permute-start(bf16[192,1408]{1,0:T(8,128)(2,1)S(1)} %hold.11), channel_id=1, source_target_pairs={{8,16},{12,20},{16,8},{20,12},{9,17},{13,21},{17,9},{21,13},{10,18... | collective-permute-start | bytes 1622024 | tf_op jit(solution)/shard_map/ppermute | solution.py:651
  104.2 10.7 %collective-permute-start.22 = (bf16[1,192,512]{2,1,0:T(8,128)(2,1)S(1)}, bf16[1,192,512]{2,1,0:T(8,128)(2,1)S(1)}, u32[]{:S(2)}, u32[]{:S(2)}) collective-permute-start(bf16[1,192,512]{2,1,0:T(8,128)(2,1)S(1)} %get-tuple-element.36), channel_id=1, source_target_pairs={{0,4},{4,0},{8,12},{12,8},{16,20},{20,16},{24,28},{28,24},{1,5},{5... | collective-permute-start | bytes 589832 | tf_op jit(solution)/shard_map/ppermute | solution.py:639
  106.2 8.7 %collective-permute-start.23 = (bf16[1,192,512]{2,1,0:T(8,128)(2,1)S(1)}, bf16[1,192,512]{2,1,0:T(8,128)(2,1)S(1)}, u32[]{:S(2)}, u32[]{:S(2)}) collective-permute-start(bf16[1,192,512]{2,1,0:T(8,128)(2,1)S(1)} %get-tuple-element.38), channel_id=1, source_target_pairs={{0,4},{4,0},{8,12},{12,8},{16,20},{20,16},{24,28},{28,24},{1,5},{5... | collective-permute-start | bytes 589832 | tf_op jit(solution)/shard_map/ppermute | solution.py:639
  (11 other events, 70.0 us)

commit v10 on v9

--- a/solution.py
+++ b/solution.py
@@ -10,8 +10,10 @@
 
 LANES = 128
 SCALE = 1_000_000
-BEGIN_WEIGHT = 600
 FIRST_WEIGHT = 12_000
+NEXT_WEIGHT = 600
+HIDDEN_WEIGHT = 5_000
+PASS_WEIGHT = 700
 LAST_WEIGHT = 90
 NT = (((1,), (1,)), ((), ()))
 NN = (((1,), (0,)), ((), ()))
@@ -280,46 +282,52 @@
         scaled[here, :] = (block[:, : scaled.shape[1]].astype(f32) * gate).astype(bf16)
 
 
-def products_kernel(table, model, counts, places, shards, skip, guard, where_ref, *refs):
+def products_kernel(table, model, counts, places, shards, skip, ends, where_ref, *refs):
     used = sum(counts)
     rows = blocks_of(refs[: counts[0]], places[0])
     gated = blocks_of(refs[counts[0] : used], places[1])
     own_ref, other_ref = refs[used : used + 2]
-    kept_ref, scaled = refs[-2:]
+    kept_ref, scaled, total_ref, sem = refs[-4:]
     units, slots = own_ref.shape[1:]
 
     def stacked(ref, offset):
         parts = [ref[offset + shard] for shard in range(shards)]
         return jnp.concatenate(parts, axis=0) if len(parts) > 1 else parts[0]
 
-    def work():
+    @pl.when((where_ref[table["use", 2, "A"]] == 0) == ends)
+    def _():
         scale_rows(table, model, where_ref, rows, gated, scaled)
         total = dot(stacked(own_ref, skip), scaled[:slots, :], NN)
         total = total + dot(stacked(other_ref, 0), scaled[slots:, :], NN)
         for shard in range(shards):
-            kept_ref[shard] = total[shard * units : (shard + 1) * units]
-
-    if guard:
-        pl.when(where_ref[table["use", 2, "A"]] != 0)(work)
-    else:
-        work()
-
-
-def products(table, where, rows, gated, own, other, skip, model, width, name, after, guard=False):
+            total_ref[shard] = total[shard * units : (shard + 1) * units]
+        copy = pltpu.make_async_copy(total_ref, kept_ref, sem)
+        copy.start()
+        copy.wait()
+
+
+def products(table, where, rows, gated, own, other, skip, model, width, name, after, ends, before=None):
     arrays, places = zip(rows, gated)
-    tokens = arrays[0][0].shape[-2]
     counts = [len(part) for part in arrays]
     shards, units, slots = other.shape
-    return pl.pallas_call(
-        functools.partial(products_kernel, table, model, counts, places, shards, skip, guard),
-        out_shape=jax.ShapeDtypeStruct((shards, units, width), f32),
-        in_specs=[scalars()] + [whole()] * (sum(counts) + 2) + [anywhere()] * len(after),
-        out_specs=whole(),
-        scratch_shapes=[pltpu.VMEM((2 * slots, width), bf16)],
-        compiler_params=params(),
-        cost_estimate=taking(4),
+    kept = jax.ShapeDtypeStruct((shards, units, width), f32)
+    operands = [*arrays[0], *arrays[1], own, other]
+    extra = ([] if before is None else [before]) + list(after)
+    return pl.pallas_call(
+        functools.partial(products_kernel, table, model, counts, places, shards, skip, ends),
+        out_shape=kept,
+        in_specs=[scalars()] + [whole()] * len(operands) + [anywhere()] * len(extra),
+        out_specs=anywhere(),
+        scratch_shapes=[
+            pltpu.VMEM((2 * slots, width), bf16),
+            pltpu.VMEM(kept.shape, f32),
+            pltpu.SemaphoreType.DMA,
+        ],
+        input_output_aliases={} if before is None else {1 + len(operands): 0},
+        compiler_params=params(),
+        cost_estimate=taking(1),
         name=name,
-    )(where, *arrays[0], *arrays[1], own, other, *after)
+    )(where, *operands, *extra)
 
 
 def first_kernel(table, model, counts, places, start, where_ref, *refs):
@@ -683,8 +691,7 @@
     early_rows = (early_rows, places)
     other_rest = swap(other_rest, 1, 0)
 
-    for name, value in zip("BA", hold([got[1, "B"][0], got[1, "A"][0]], [], FIRST_WEIGHT)):
-        got[1, name] = [value]
+    got[1, "B"] = list(hold(got[1, "B"], got[1, "A"], FIRST_WEIGHT))
     chunks = ((late_rows, cut, model - cut), (early_rows, 0, cut))
     after = [early_rows[0][1]]
     first = []
@@ -693,15 +700,17 @@
             table, where, rows, late_rows, own, other_first, got[1, "B"][0], model, start, columns, after
         )
         if first:
-            (value,) = hold([value], [got[2, "A"][0]], BEGIN_WEIGHT)
-            (value,) = hold([value], [other_rest])
+            (value,) = hold([value], got[2, "A"], NEXT_WEIGHT)
         got.setdefault((2, "A"), []).append(swap_z(value, "A"))
         first.append(
-            products(table, where, rows, late_rows, own, other_first, 0, model, columns, "first_kept", [value], True)
+            products(
+                table, where, rows, late_rows, own, other_first, 0, model, columns, "first_kept", [value], False
+            )
         )
         after = [first[0]]
     marker = value
     got[2, "B"] = [swap_z(got[1, "A"][0], "B")]
+    (other_rest,) = hold([other_rest], [], HIDDEN_WEIGHT)
 
     halves, all_choices, weights_of = [], [], {}
     only_first = max(uses[3, "B"]) <= 0
@@ -722,6 +731,7 @@
         senders = [z for z in range(depth) if used[z] >= 0] if turn == depth - 1 else range(depth)
         others = [z for z in range(depth) if z not in senders]
         if others and chunk is None and len(coming) == 1:
+            coming[:] = hold(coming, [], PASS_WEIGHT)
             weights_of[turn, name] = [swap_z(coming[0], name, others)]
             ends = {0, depth - 1} if name == "A" else set()
             coming = [] if set(senders) <= ends else coming
@@ -742,11 +752,20 @@
     marker = pass_on(3, "B", [marker], 0) if only_first else marker
     for rows, _, columns in chunks:
         rest.append(
-            products(table, where, rows, late_rows, own, other_rest, 1, model, columns, "rest_kept", [marker])
+            products(
+                table, where, rows, late_rows, own, other_rest, 1, model, columns, "rest_kept", [marker], True
+            )
         )
     marker = pass_on(3, "A", rest)
     for chunk in range(2)[only_first:]:
         marker = pass_on(3, "B", [marker], chunk)
+    rest[:] = [
+        products(
+            table, where, rows, late_rows, own, other_rest, 1, model, columns, "rest_kept", [marker], False, before
+        )
+        for (rows, _, columns), before in zip(chunks, rest)
+    ]
+    marker = rest[1]
     sums = backprop([[(0, "own")], [(1, "A")], [(1, "B")]], None, False, [marker])
     sooner = halves[1::2]
     for turn in range(2, depth):

time: 125 us -> 128 us (1.024)
  the two profiles are of different devices: /device:TPU:0 before, /device:TPU:16 now
where the time goes in v10:
time: 128 us; the launch traced here: 127 us
  waiting for transfers between devices  47.2 us (37%)
  Pallas kernels  37 us (29%)
  starting transfers between devices  32.7 us (26%)
  blocking collectives  6.08 us (5%)
  local copies, waits for them, and re-layouts  3.13 us (2%)
    ppermute x12, starting transfers between devices, swap_z(): return lax.ppermute(value, 'ctx', pairs)  22.5 us
    ppermute x8, waiting for transfers between devices, swap(): return lax.ppermute(value, 'ctx', [(i, i ^ x) for i in range(groups)])  20.9 us
    ppermute x12, waiting for transfers between devices, swap_z(): return lax.ppermute(value, 'ctx', pairs)  16.9 us
    pallas_call x6, Pallas kernels, products(): pl.pallas_call(functools.partial(products_kernel, table, model, counts, p...  13.4 us
    ppermute x8, waiting for transfers between devices, swap(): return lax.ppermute(value, 'exp', [(i, i ^ exp) for i in range(experts)])  9.41 us
    pallas_call x3, Pallas kernels, back_part(): pl.pallas_call(functools.partial(back_kernel, table, model, cut, counts,...  8.13 us
    ppermute x8, starting transfers between devices, swap(): return lax.ppermute(value, 'ctx', [(i, i ^ x) for i in range(groups)])  6.66 us
    all_to_all x1, blocking collectives, per_device_full(): lax.all_to_all(slot_grad.reshape(experts, tokens), 'exp', split_axis=0, c...  6.08 us
  transfers between devices with their start and end apart: 28, of which 12 were waited for; matrix products, arithmetic and copies ran while one was open for 1% of the time, Pallas kernels for 26%

profile of v10, /device:TPU:16, one launch (start us, length us, event | category | flops | bytes accessed | tf_op | source)
XLA Modules:
  0.0 127.1 jit_solution(6644772039649393978)
XLA Ops:
  0.6 2.2 %make_rows.1 = (bf16[128,1536]{1,0:T(8,128)(2,1)}, bf16[128,1408]{1,0:T(8,128)(2,1)}, f32[4,128]{1,0:T(4,128)}) custom-call(bf16[2880,128]{1,0:T(8,128)(2,1)} %bitcast.22, f32[4,128]{1,0:T(4,128)} %bitcast.23, s32[4,128]{1,0:T(4,128)} %bitcast.18), custom_call_target="tpu_custom_call" | custom-call | flops 2000000 | bytes 6000000 | tf_op jit(solution)/shard_map/make_rows/pallas_call | solution.py:164
  12.5 2.2 %split_hidden.1 = (bf16[4,192,512]{2,1,0:T(8,128)(2,1)S(1)}, bf16[1,192,512]{2,1,0:T(8,128)(2,1)S(1)}, bf16[3,192,512]{2,1,0:T(8,128)(2,1)S(1)}) custom-call(s32[32]{0:T(128)S(1)} %dynamic-slice_bitcast_fusion.where_ref, bf16[512,1536]{1,0:T(8,128)(2,1)S(1)} %bitcast.14, bf16[128,1536]{1,0:T(8,128)(2,1)S(1)} %copy-done.1), custom_call_target="tpu_custom_call" | custom-call | flops 2000000 | bytes 6000000 | tf_op jit(solution)/shard_map/split_hidden/pallas_call | solution.py:255
  15.9 4.7 %collective-permute-done.3.refs_2_.refs_5_.refs_9_ = bf16[1,192,512]{2,1,0:T(8,128)(2,1)S(1)} collective-permute-done((bf16[1,192,512]{2,1,0:T(8,128)(2,1)S(1)}, bf16[1,192,512]{2,1,0:T(8,128)(2,1)S(1)}, u32[]{:S(2)}, u32[]{:S(2)}) %collective-permute-start.3) | collective-permute-done | bytes 196640 | tf_op jit(solution)/shard_map/ppermute | solution.py:647
  21.1 7.8 %collective-permute-done.4.refs_4_.refs_1_ = bf16[128,1408]{1,0:T(8,128)(2,1)S(1)} collective-permute-done((bf16[128,1408]{1,0:T(8,128)(2,1)S(1)}, bf16[128,1408]{1,0:T(8,128)(2,1)S(1)}, u32[]{:S(2)}, u32[]{:S(2)}) %collective-permute-start.4) | collective-permute-done | bytes 360480 | tf_op jit(solution)/shard_map/ppermute | solution.py:647
  32.7 2.7 %collective-permute-done.15.refs_0_ = bf16[192,2880]{1,0:T(8,128)(2,1)S(1)} collective-permute-done((bf16[192,2880]{1,0:T(8,128)(2,1)}, bf16[192,2880]{1,0:T(8,128)(2,1)S(1)}, u32[]{:S(2)}, u32[]{:S(2)}) %collective-permute-start.15) | collective-permute-done | bytes 1105952 | tf_op jit(solution)/shard_map/ppermute | solution.py:659
  35.4 2.2 %collective-permute-start.13 = (bf16[192,2880]{1,0:T(8,128)(2,1)S(1)}, bf16[192,2880]{1,0:T(8,128)(2,1)S(1)}, u32[]{:S(2)}, u32[]{:S(2)}) collective-permute-start(bf16[192,2880]{1,0:T(8,128)(2,1)S(1)} %collective-permute-done.12.refs_1_.refs_12_), channel_id=1, source_target_pairs={{8,16},{12,20},{16,8},{20,12},{9,17},{13,21},{17,9},{21,13},{10,18... | collective-permute-start | bytes 3317768 | tf_op jit(solution)/shard_map/ppermute | solution.py:659
  39.0 2.1 %collective-permute-done.7.refs_2_.refs_4_ = bf16[128,1408]{1,0:T(8,128)(2,1)S(1)} collective-permute-done((bf16[128,1408]{1,0:T(8,128)(2,1)S(1)}, bf16[128,1408]{1,0:T(8,128)(2,1)S(1)}, u32[]{:S(2)}, u32[]{:S(2)}) %collective-permute-start.7) | collective-permute-done | bytes 360480 | tf_op jit(solution)/shard_map/ppermute | solution.py:649
  41.1 7.3 %collective-permute-done.9.refs_4_.refs_6_ = bf16[128,1408]{1,0:T(8,128)(2,1)S(1)} collective-permute-done((bf16[128,1408]{1,0:T(8,128)(2,1)S(1)}, bf16[128,1408]{1,0:T(8,128)(2,1)S(1)}, u32[]{:S(2)}, u32[]{:S(2)}) %collective-permute-start.9) | collective-permute-done | bytes 360480 | tf_op jit(solution)/shard_map/ppermute | solution.py:649
  48.4 2.4 %first_kept.2.refs_11_.refs_1_ = f32[1,192,1472]{2,1,0:T(8,128)S(1)} custom-call(s32[32]{0:T(128)S(1)} %dynamic-slice_bitcast_fusion.where_ref, bf16[4,128,1536]{2,1,0:T(8,128)(2,1)S(1)} %pack_rows.2.refs_0_.refs_2_.refs_6_, bf16[4,128,1536]{2,1,0:T(8,128)(2,1)S(1)} %collective-permute-done.5.refs_1_.refs_3_.refs_7_, ...), custom_call_target="tpu_custom_call" | custom-call | flops 1000000 | bytes 3000000 | tf_op jit(solution)/shard_map/first_kept/pallas_call | solution.py:316
  54.4 1.9 %collective-permute-start.17 = (bf16[192,1472]{1,0:T(8,128)(2,1)S(1)}, bf16[192,1472]{1,0:T(8,128)(2,1)S(1)}, u32[]{:S(2)}, u32[]{:S(2)}) collective-permute-start(bf16[192,1472]{1,0:T(8,128)(2,1)S(1)} %combine.5.refs_6_.refs_10_), channel_id=1, source_target_pairs={{8,16},{12,20},{16,8},{20,12},{9,17},{13,21},{17,9},{21,13},{10,18... | collective-permute-start | bytes 1695752 | tf_op jit(solution)/shard_map/ppermute | solution.py:659
  59.8 5.3 %collective-permute-done.13.refs_0_ = bf16[192,2880]{1,0:T(8,128)(2,1)S(1)} collective-permute-done((bf16[192,2880]{1,0:T(8,128)(2,1)S(1)}, bf16[192,2880]{1,0:T(8,128)(2,1)S(1)}, u32[]{:S(2)}, u32[]{:S(2)}) %collective-permute-start.13) | collective-permute-done | bytes 1105952 | tf_op jit(solution)/shard_map/ppermute | solution.py:659
  65.1 2.1 %collective-permute-start.14 = (bf16[192,2880]{1,0:T(8,128)(2,1)S(1)}, bf16[192,2880]{1,0:T(8,128)(2,1)S(1)}, u32[]{:S(2)}, u32[]{:S(2)}) collective-permute-start(bf16[192,2880]{1,0:T(8,128)(2,1)S(1)} %hold.10.refs_13_), channel_id=1, source_target_pairs={{8,0},{12,4},{16,24},{20,28},{9,1},{13,5},{17,25},{21,29},{10,2},{... | collective-permute-start | bytes 3317768 | tf_op jit(solution)/shard_map/ppermute | solution.py:659
  67.2 2.3 %first_kept.3.refs_1_ = f32[1,192,1408]{2,1,0:T(8,128)S(1)} custom-call(s32[32]{0:T(128)S(1)} %dynamic-slice_bitcast_fusion.where_ref, bf16[2,128,1408]{2,1,0:T(8,128)(2,1)S(1)} %pack_rows.3.refs_0_.refs_2_, bf16[2,128,1408]{2,1,0:T(8,128)(2,1)S(1)} %collective-permute-done.6.refs_7_.refs_1_.refs_3_, ...), custom_call_target="tpu_custom_call" | custom-call | flops 1000000 | bytes 3000000 | tf_op jit(solution)/shard_map/first_kept/pallas_call | solution.py:316
  70.3 3.5 %collective-permute-start.19 = (bf16[192,1408]{1,0:T(8,128)(2,1)S(1)}, bf16[192,1408]{1,0:T(8,128)(2,1)S(1)}, u32[]{:S(2)}, u32[]{:S(2)}) collective-permute-start(bf16[192,1408]{1,0:T(8,128)(2,1)S(1)} %combine.7.refs_11_.refs_7_), channel_id=1, source_target_pairs={{8,16},{12,20},{16,8},{20,12},{9,17},{13,21},{17,9},{21,13},{10,18... | collective-permute-start | bytes 1622024 | tf_op jit(solution)/shard_map/ppermute | solution.py:659
  73.8 3.7 %rest_kept.6.refs_14_.refs_15_.refs_3_.refs_2_.refs_4_ = f32[3,192,1408]{2,1,0:T(8,128)S(1)} custom-call(s32[32]{0:T(128)S(1)} %dynamic-slice_bitcast_fusion.where_ref, bf16[2,128,1408]{2,1,0:T(8,128)(2,1)S(1)} %pack_rows.3.refs_0_.refs_2_, bf16[2,128,1408]{2,1,0:T(8,128)(2,1)S(1)} %collective-permute-done.6.refs_7_.refs_1_.refs_3_, ...), custom_call_target="tpu_custom_call", output_to_operand_aliasing={{}: (11, {})} | custom-call | flops 1000000 | bytes 3000000 | tf_op jit(solution)/shard_map/rest_kept/pallas_call | solution.py:316
  77.5 4.7 %back_part.3 = (bf16[3,192,512]{2,1,0:T(8,128)(2,1)S(1)}, bf16[3,192,512]{2,1,0:T(8,128)(2,1)S(1)}, f32[8,1024]{1,0:T(8,128)S(1)}) custom-call(s32[32]{0:T(128)S(1)} %dynamic-slice_bitcast_fusion.where_ref, bf16[4,128,1536]{2,1,0:T(8,128)(2,1)S(1)} %pack_rows.2.refs_0_.refs_2_.refs_6_, ...), custom_call_target="tpu_custom_call" | custom-call | flops 6000000 | bytes 18000000 | tf_op jit(solution)/shard_map/back_part/pallas_call | solution.py:556
  82.8 3.9 %rest_kept.7.refs_2_.refs_1_.refs_3_ = f32[3,192,1472]{2,1,0:T(8,128)S(1)} custom-call(s32[32]{0:T(128)S(1)} %dynamic-slice_bitcast_fusion.where_ref, bf16[4,128,1536]{2,1,0:T(8,128)(2,1)S(1)} %pack_rows.2.refs_0_.refs_2_.refs_6_, bf16[4,128,1536]{2,1,0:T(8,128)(2,1)S(1)} %collective-permute-done.5.refs_1_.refs_3_.refs_7_, ...), custom_call_target="tpu_custom_call", output_to_operand_aliasing={{}: (7, {})} | custom-call | flops 1000000 | bytes 3000000 | tf_op jit(solution)/shard_map/rest_kept/pallas_call | solution.py:316
  86.7 2.7 %back_part.4 = (bf16[1,192,512]{2,1,0:T(8,128)(2,1)S(1)}, bf16[1,192,512]{2,1,0:T(8,128)(2,1)S(1)}, f32[8,1024]{1,0:T(8,128)S(1)}) custom-call(s32[32]{0:T(128)S(1)} %dynamic-slice_bitcast_fusion.where_ref, bf16[4,128,1536]{2,1,0:T(8,128)(2,1)S(1)} %pack_rows.2.refs_0_.refs_2_.refs_6_, ...), custom_call_target="tpu_custom_call" | custom-call | flops 6000000 | bytes 18000000 | tf_op jit(solution)/shard_map/back_part/pallas_call | solution.py:556
  90.5 6.7 %collective-permute-done.21.refs_1_.refs_4_ = bf16[3,192,512]{2,1,0:T(8,128)(2,1)S(1)} collective-permute-done((bf16[3,192,512]{2,1,0:T(8,128)(2,1)S(1)}, bf16[3,192,512]{2,1,0:T(8,128)(2,1)S(1)}, u32[]{:S(2)}, u32[]{:S(2)}) %collective-permute-start.21) | collective-permute-done | bytes 589856 | tf_op jit(solution)/shard_map/ppermute | solution.py:647
  98.1 2.3 %collective-permute-start.26 = (bf16[192,1472]{1,0:T(8,128)(2,1)S(1)}, bf16[192,1472]{1,0:T(8,128)(2,1)S(1)}, u32[]{:S(2)}, u32[]{:S(2)}) collective-permute-start(bf16[192,1472]{1,0:T(8,128)(2,1)S(1)} %get-tuple-element.35), channel_id=1, source_target_pairs={{8,16},{12,20},{16,8},{20,12},{9,17},{13,21},{17,9},{21,13},{10,18... | collective-permute-start | bytes 1695752 | tf_op jit(solution)/shard_map/ppermute | solution.py:659
  100.4 3.6 %collective-permute-start.27 = (bf16[192,1408]{1,0:T(8,128)(2,1)S(1)}, bf16[192,1408]{1,0:T(8,128)(2,1)S(1)}, u32[]{:S(2)}, u32[]{:S(2)}) collective-permute-start(bf16[192,1408]{1,0:T(8,128)(2,1)S(1)} %hold.13), channel_id=1, source_target_pairs={{8,16},{12,20},{16,8},{20,12},{9,17},{13,21},{17,9},{21,13},{10,18... | collective-permute-start | bytes 1622024 | tf_op jit(solution)/shard_map/ppermute | solution.py:659
  109.1 6.1 %all_to_all.11 = f32[4,1,128]{2,1,0:T(1,128)S(1)} all-to-all(f32[4,1,128]{2,1,0:T(1,128)S(1)} %add_bitcast_fusion), channel_id=1, replica_groups=mesh['ctx'=8,'exp'=4] {'exp'}, dimensions={0} | all-to-all | bytes 4096 | tf_op jit(solution)/shard_map/all_to_all | solution.py:779
  115.7 2.6 %join_hidden.1 = bf16[512,1536]{1,0:T(8,128)(2,1)} custom-call(s32[32]{0:T(128)S(1)} %dynamic-slice_bitcast_fusion.where_ref, bf16[3,192,512]{2,1,0:T(8,128)(2,1)S(1)} %get-tuple-element.29.refs_0_, bf16[3,192,512]{2,1,0:T(8,128)(2,1)S(1)} %collective-permute-done.21.refs_1_.refs_4_, bf16[1,192,512]{2,1,0:T(8,128)(2,1)S(1)} %get-tuple-element.31.refs_2_, ...), custom_call_target="tpu_custom_call" | custom-call | flops 2000000 | bytes 6000000 | tf_op jit(solution)/shard_map/join_hidden/pallas_call | solution.py:598
  118.4 7.2 %collective-permute-done.27.refs_2_ = bf16[192,1408]{1,0:T(8,128)(2,1)S(1)} collective-permute-done((bf16[192,1408]{1,0:T(8,128)(2,1)S(1)}, bf16[192,1408]{1,0:T(8,128)(2,1)S(1)}, u32[]{:S(2)}, u32[]{:S(2)}) %collective-permute-start.27) | collective-permute-done | bytes 540704 | tf_op jit(solution)/shard_map/ppermute | solution.py:659
  (80 shorter events, 33.9 us)
Async XLA Ops:
  2.8 12.5 %collective-permute-start = (bf16[128,1536]{1,0:T(8,128)(2,1)}, bf16[128,1536]{1,0:T(8,128)(2,1)S(1)}, u32[]{:S(2)}, u32[]{:S(2)}) collective-permute-start(bf16[128,1536]{1,0:T(8,128)(2,1)} %get-tuple-element.21.refs_0_), channel_id=1, source_target_pairs={{0,2},{1,3},{2,0},{3,1},{4,6},{5,7},{6,4},{7,5},{8,10},{9,11},{10,... | collective-permute-start | bytes 1179656 | tf_op jit(solution)/shard_map/ppermute | solution.py:649
  4.4 10.9 %collective-permute-start.1 = (bf16[128,1536]{1,0:T(8,128)(2,1)}, bf16[128,1536]{1,0:T(8,128)(2,1)S(1)}, u32[]{:S(2)}, u32[]{:S(2)}) collective-permute-start(bf16[128,1536]{1,0:T(8,128)(2,1)} %get-tuple-element.21.refs_0_), channel_id=1, source_target_pairs={{0,4},{4,0},{8,12},{12,8},{16,20},{20,16},{24,28},{28,24},{1,5},{5... | collective-permute-start | bytes 1179656 | tf_op jit(solution)/shard_map/ppermute | solution.py:647
  5.9 26.3 %collective-permute-start.12 = (bf16[192,2880]{1,0:T(8,128)(2,1)}, bf16[192,2880]{1,0:T(8,128)(2,1)S(1)}, u32[]{:S(2)}, u32[]{:S(2)}) collective-permute-start(bf16[192,2880]{1,0:T(8,128)(2,1)} %bitcast.15), channel_id=1, source_target_pairs={{0,8},{4,12},{8,0},{12,4},{16,24},{20,28},{24,16},{28,20},{1,9},{5... | collective-permute-start | bytes 3317768 | tf_op jit(solution)/shard_map/ppermute | solution.py:659
  7.5 27.9 %collective-permute-start.15 = (bf16[192,2880]{1,0:T(8,128)(2,1)}, bf16[192,2880]{1,0:T(8,128)(2,1)S(1)}, u32[]{:S(2)}, u32[]{:S(2)}) collective-permute-start(bf16[192,2880]{1,0:T(8,128)(2,1)} %bitcast.16), channel_id=1, source_target_pairs={{8,16},{12,20},{16,8},{20,12},{9,17},{13,21},{17,9},{21,13},{10,18... | collective-permute-start | bytes 3317768 | tf_op jit(solution)/shard_map/ppermute | solution.py:659
  15.3 13.6 %collective-permute-start.2 = (bf16[128,1536]{1,0:T(8,128)(2,1)S(1)}, bf16[128,1536]{1,0:T(8,128)(2,1)S(1)}, u32[]{:S(2)}, u32[]{:S(2)}) collective-permute-start(bf16[128,1536]{1,0:T(8,128)(2,1)S(1)} %hold.7.refs_1_.refs_2_), channel_id=1, source_target_pairs={{0,2},{1,3},{2,0},{3,1},{4,6},{5,7},{6,4},{7,5},{8,10},{9,11},{10,... | collective-permute-start | bytes 1179656 | tf_op jit(solution)/shard_map/ppermute | solution.py:649
  20.6 8.4 %collective-permute-start.4 = (bf16[128,1408]{1,0:T(8,128)(2,1)S(1)}, bf16[128,1408]{1,0:T(8,128)(2,1)S(1)}, u32[]{:S(2)}, u32[]{:S(2)}) collective-permute-start(bf16[128,1408]{1,0:T(8,128)(2,1)S(1)} %hold.8.refs_0_), channel_id=1, source_target_pairs={{0,4},{4,0},{8,12},{12,8},{16,20},{20,16},{24,28},{28,24},{1,5},{5... | collective-permute-start | bytes 1081352 | tf_op jit(solution)/shard_map/ppermute | solution.py:647
  29.8 7.8 %collective-permute-start.5 = (bf16[4,128,1536]{2,1,0:T(8,128)(2,1)S(1)}, bf16[4,128,1536]{2,1,0:T(8,128)(2,1)S(1)}, u32[]{:S(2)}, u32[]{:S(2)}) collective-permute-start(bf16[4,128,1536]{2,1,0:T(8,128)(2,1)S(1)} %pack_rows.2.refs_0_.refs_2_.refs_6_), channel_id=1, source_target_pairs={{0,1},{1,0},{2,3},{3,2},{4,5},{5,4},{6,7},{7,6},{8,9},{9,8},{10,11... | collective-permute-start | bytes 4718600 | tf_op jit(solution)/shard_map/ppermute | solution.py:649
  29.9 11.3 %collective-permute-start.7 = (bf16[128,1408]{1,0:T(8,128)(2,1)S(1)}, bf16[128,1408]{1,0:T(8,128)(2,1)S(1)}, u32[]{:S(2)}, u32[]{:S(2)}) collective-permute-start(bf16[128,1408]{1,0:T(8,128)(2,1)S(1)} %hold.8.refs_0_), channel_id=1, source_target_pairs={{0,2},{1,3},{2,0},{3,1},{4,6},{5,7},{6,4},{7,5},{8,10},{9,11},{10,... | collective-permute-start | bytes 1081352 | tf_op jit(solution)/shard_map/ppermute | solution.py:649
  32.2 16.2 %collective-permute-start.9 = (bf16[128,1408]{1,0:T(8,128)(2,1)S(1)}, bf16[128,1408]{1,0:T(8,128)(2,1)S(1)}, u32[]{:S(2)}, u32[]{:S(2)}) collective-permute-start(bf16[128,1408]{1,0:T(8,128)(2,1)S(1)} %collective-permute-done.4.refs_4_.refs_1_), channel_id=1, source_target_pairs={{0,2},{1,3},{2,0},{3,1},{4,6},{5,7},{6,4},{7,5},{8,10},{9,11},{10,... | collective-permute-start | bytes 1081352 | tf_op jit(solution)/shard_map/ppermute | solution.py:649
  35.4 29.7 %collective-permute-start.13 = (bf16[192,2880]{1,0:T(8,128)(2,1)S(1)}, bf16[192,2880]{1,0:T(8,128)(2,1)S(1)}, u32[]{:S(2)}, u32[]{:S(2)}) collective-permute-start(bf16[192,2880]{1,0:T(8,128)(2,1)S(1)} %collective-permute-done.12.refs_1_.refs_12_), channel_id=1, source_target_pairs={{8,16},{12,20},{16,8},{20,12},{9,17},{13,21},{17,9},{21,13},{10,18... | collective-permute-start | bytes 3317768 | tf_op jit(solution)/shard_map/ppermute | solution.py:659
  38.2 13.6 %collective-permute-start.16 = (bf16[192,1472]{1,0:T(8,128)(2,1)S(1)}, bf16[192,1472]{1,0:T(8,128)(2,1)S(1)}, u32[]{:S(2)}, u32[]{:S(2)}) collective-permute-start(bf16[192,1472]{1,0:T(8,128)(2,1)S(1)} %first_sums.2.refs_6_), channel_id=1, source_target_pairs={{0,8},{4,12},{8,0},{12,4},{16,24},{20,28},{24,16},{28,20},{1,9},{5... | collective-permute-start | bytes 1695752 | tf_op jit(solution)/shard_map/ppermute | solution.py:659
  38.3 15.4 %collective-permute-start.11 = (bf16[3,192,512]{2,1,0:T(8,128)(2,1)S(1)}, bf16[3,192,512]{2,1,0:T(8,128)(2,1)S(1)}, u32[]{:S(2)}, u32[]{:S(2)}) collective-permute-start(bf16[3,192,512]{2,1,0:T(8,128)(2,1)S(1)} %get-tuple-element.25), channel_id=1, source_target_pairs={{0,4},{4,0},{8,12},{12,8},{16,20},{20,16},{24,28},{28,24},{1,5},{5... | collective-permute-start | bytes 1769480 | tf_op jit(solution)/shard_map/ppermute | solution.py:647
  41.1 9.7 %collective-permute-start.8 = (bf16[128,1408]{1,0:T(8,128)(2,1)S(1)}, bf16[128,1408]{1,0:T(8,128)(2,1)S(1)}, u32[]{:S(2)}, u32[]{:S(2)}) collective-permute-start(bf16[128,1408]{1,0:T(8,128)(2,1)S(1)} %collective-permute-done.7.refs_2_.refs_4_), channel_id=1, source_target_pairs={{0,1},{1,0},{2,3},{3,2},{4,5},{5,4},{6,7},{7,6},{8,9},{9,8},{10,11... | collective-permute-start | bytes 1081352 | tf_op jit(solution)/shard_map/ppermute | solution.py:649
  51.8 17.7 %collective-permute-start.18 = (bf16[192,1408]{1,0:T(8,128)(2,1)S(1)}, bf16[192,1408]{1,0:T(8,128)(2,1)S(1)}, u32[]{:S(2)}, u32[]{:S(2)}) collective-permute-start(bf16[192,1408]{1,0:T(8,128)(2,1)S(1)} %hold.12.refs_2_.refs_10_), channel_id=1, source_target_pairs={{0,8},{4,12},{8,0},{12,4},{16,24},{20,28},{24,16},{28,20},{1,9},{5... | collective-permute-start | bytes 1622024 | tf_op jit(solution)/shard_map/ppermute | solution.py:659
  54.4 34.9 %collective-permute-start.17 = (bf16[192,1472]{1,0:T(8,128)(2,1)S(1)}, bf16[192,1472]{1,0:T(8,128)(2,1)S(1)}, u32[]{:S(2)}, u32[]{:S(2)}) collective-permute-start(bf16[192,1472]{1,0:T(8,128)(2,1)S(1)} %combine.5.refs_6_.refs_10_), channel_id=1, source_target_pairs={{8,16},{12,20},{16,8},{20,12},{9,17},{13,21},{17,9},{21,13},{10,18... | collective-permute-start | bytes 1695752 | tf_op jit(solution)/shard_map/ppermute | solution.py:659
  58.3 32.2 %collective-permute-start.25 = (bf16[192,2880]{1,0:T(8,128)(2,1)S(1)}, bf16[192,2880]{1,0:T(8,128)(2,1)S(1)}, u32[]{:S(2)}, u32[]{:S(2)}) collective-permute-start(bf16[192,2880]{1,0:T(8,128)(2,1)S(1)} %combine.6.refs_2_), channel_id=1, source_target_pairs={{0,8},{4,12},{24,16},{28,20},{1,9},{5,13},{25,17},{29,21},{2,10},{... | collective-permute-start | bytes 3317768 | tf_op jit(solution)/shard_map/ppermute | solution.py:659
  65.1 35.2 %collective-permute-start.14 = (bf16[192,2880]{1,0:T(8,128)(2,1)S(1)}, bf16[192,2880]{1,0:T(8,128)(2,1)S(1)}, u32[]{:S(2)}, u32[]{:S(2)}) collective-permute-start(bf16[192,2880]{1,0:T(8,128)(2,1)S(1)} %hold.10.refs_13_), channel_id=1, source_target_pairs={{8,0},{12,4},{16,24},{20,28},{9,1},{13,5},{17,25},{21,29},{10,2},{... | collective-permute-start | bytes 3317768 | tf_op jit(solution)/shard_map/ppermute | solution.py:659
  70.3 19.1 %collective-permute-start.19 = (bf16[192,1408]{1,0:T(8,128)(2,1)S(1)}, bf16[192,1408]{1,0:T(8,128)(2,1)S(1)}, u32[]{:S(2)}, u32[]{:S(2)}) collective-permute-start(bf16[192,1408]{1,0:T(8,128)(2,1)S(1)} %combine.7.refs_11_.refs_7_), channel_id=1, source_target_pairs={{8,16},{12,20},{16,8},{20,12},{9,17},{13,21},{17,9},{21,13},{10,18... | collective-permute-start | bytes 1622024 | tf_op jit(solution)/shard_map/ppermute | solution.py:659
  82.2 15.0 %collective-permute-start.21 = (bf16[3,192,512]{2,1,0:T(8,128)(2,1)S(1)}, bf16[3,192,512]{2,1,0:T(8,128)(2,1)S(1)}, u32[]{:S(2)}, u32[]{:S(2)}) collective-permute-start(bf16[3,192,512]{2,1,0:T(8,128)(2,1)S(1)} %get-tuple-element.30), channel_id=1, source_target_pairs={{0,4},{4,0},{8,12},{12,8},{16,20},{20,16},{24,28},{28,24},{1,5},{5... | collective-permute-start | bytes 1769480 | tf_op jit(solution)/shard_map/ppermute | solution.py:647
  90.2 35.3 %collective-permute-start.24 = (bf16[192,2880]{1,0:T(8,128)(2,1)S(1)}, bf16[192,2880]{1,0:T(8,128)(2,1)S(1)}, u32[]{:S(2)}, u32[]{:S(2)}) collective-permute-start(bf16[192,2880]{1,0:T(8,128)(2,1)S(1)} %combine.8.refs_15_), channel_id=1, source_target_pairs={{0,8},{4,12},{8,0},{12,4},{16,24},{20,28},{24,16},{28,20},{1,9},{5... | collective-permute-start | bytes 3317768 | tf_op jit(solution)/shard_map/ppermute | solution.py:659
  98.1 27.5 %collective-permute-start.26 = (bf16[192,1472]{1,0:T(8,128)(2,1)S(1)}, bf16[192,1472]{1,0:T(8,128)(2,1)S(1)}, u32[]{:S(2)}, u32[]{:S(2)}) collective-permute-start(bf16[192,1472]{1,0:T(8,128)(2,1)S(1)} %get-tuple-element.35), channel_id=1, source_target_pairs={{8,16},{12,20},{16,8},{20,12},{9,17},{13,21},{17,9},{21,13},{10,18... | collective-permute-start | bytes 1695752 | tf_op jit(solution)/shard_map/ppermute | solution.py:659
  100.4 25.1 %collective-permute-start.27 = (bf16[192,1408]{1,0:T(8,128)(2,1)S(1)}, bf16[192,1408]{1,0:T(8,128)(2,1)S(1)}, u32[]{:S(2)}, u32[]{:S(2)}) collective-permute-start(bf16[192,1408]{1,0:T(8,128)(2,1)S(1)} %hold.13), channel_id=1, source_target_pairs={{8,16},{12,20},{16,8},{20,12},{9,17},{13,21},{17,9},{21,13},{10,18... | collective-permute-start | bytes 1622024 | tf_op jit(solution)/shard_map/ppermute | solution.py:659
  105.4 10.4 %collective-permute-start.22 = (bf16[1,192,512]{2,1,0:T(8,128)(2,1)S(1)}, bf16[1,192,512]{2,1,0:T(8,128)(2,1)S(1)}, u32[]{:S(2)}, u32[]{:S(2)}) collective-permute-start(bf16[1,192,512]{2,1,0:T(8,128)(2,1)S(1)} %get-tuple-element.32), channel_id=1, source_target_pairs={{0,4},{4,0},{8,12},{12,8},{16,20},{20,16},{24,28},{28,24},{1,5},{5... | collective-permute-start | bytes 589832 | tf_op jit(solution)/shard_map/ppermute | solution.py:647
  108.4 7.3 %collective-permute-start.23 = (bf16[1,192,512]{2,1,0:T(8,128)(2,1)S(1)}, bf16[1,192,512]{2,1,0:T(8,128)(2,1)S(1)}, u32[]{:S(2)}, u32[]{:S(2)}) collective-permute-start(bf16[1,192,512]{2,1,0:T(8,128)(2,1)S(1)} %get-tuple-element.34), channel_id=1, source_target_pairs={{0,4},{4,0},{8,12},{12,8},{16,20},{20,16},{24,28},{28,24},{1,5},{5... | collective-permute-start | bytes 589832 | tf_op jit(solution)/shard_map/ppermute | solution.py:647
  (11 other events, 80.4 us)

commit v11 on v9

--- a/solution.py
+++ b/solution.py
@@ -10,8 +10,13 @@
 
 LANES = 128
 SCALE = 1_000_000
-BEGIN_WEIGHT = 600
 FIRST_WEIGHT = 12_000
+NEXT_WEIGHT = 600
+HIDDEN_WEIGHT = 5_000
+PASS_WEIGHT = 1
+WAITED_WEIGHT = 210
+ENTER_WEIGHT = 575
+LEAVE_WEIGHT = 5_300
 LAST_WEIGHT = 90
 NT = (((1,), (1,)), ((), ()))
 NN = (((1,), (0,)), ((), ()))
@@ -280,7 +285,7 @@
         scaled[here, :] = (block[:, : scaled.shape[1]].astype(f32) * gate).astype(bf16)
 
 
-def products_kernel(table, model, counts, places, shards, skip, guard, where_ref, *refs):
+def products_kernel(table, model, counts, places, shards, skip, middle, where_ref, *refs):
     used = sum(counts)
     rows = blocks_of(refs[: counts[0]], places[0])
     gated = blocks_of(refs[counts[0] : used], places[1])
@@ -299,27 +304,28 @@
         for shard in range(shards):
             kept_ref[shard] = total[shard * units : (shard + 1) * units]
 
-    if guard:
+    if middle:
         pl.when(where_ref[table["use", 2, "A"]] != 0)(work)
     else:
         work()
 
 
-def products(table, where, rows, gated, own, other, skip, model, width, name, after, guard=False):
+def products(table, where, rows, gated, own, other, skip, model, width, name, after, middle=False):
     arrays, places = zip(rows, gated)
-    tokens = arrays[0][0].shape[-2]
     counts = [len(part) for part in arrays]
     shards, units, slots = other.shape
-    return pl.pallas_call(
-        functools.partial(products_kernel, table, model, counts, places, shards, skip, guard),
-        out_shape=jax.ShapeDtypeStruct((shards, units, width), f32),
-        in_specs=[scalars()] + [whole()] * (sum(counts) + 2) + [anywhere()] * len(after),
+    kept = jax.ShapeDtypeStruct((shards, units, width), f32)
+    operands = [*arrays[0], *arrays[1], own, other]
+    return pl.pallas_call(
+        functools.partial(products_kernel, table, model, counts, places, shards, skip, middle),
+        out_shape=kept,
+        in_specs=[scalars()] + [whole()] * len(operands) + [anywhere()] * len(after),
         out_specs=whole(),
         scratch_shapes=[pltpu.VMEM((2 * slots, width), bf16)],
         compiler_params=params(),
-        cost_estimate=taking(4),
+        cost_estimate=taking(1),
         name=name,
-    )(where, *arrays[0], *arrays[1], own, other, *after)
+    )(where, *operands, *after)
 
 
 def first_kernel(table, model, counts, places, start, where_ref, *refs):
@@ -683,8 +689,7 @@
     early_rows = (early_rows, places)
     other_rest = swap(other_rest, 1, 0)
 
-    for name, value in zip("BA", hold([got[1, "B"][0], got[1, "A"][0]], [], FIRST_WEIGHT)):
-        got[1, name] = [value]
+    got[1, "B"] = list(hold(got[1, "B"], got[1, "A"], FIRST_WEIGHT))
     chunks = ((late_rows, cut, model - cut), (early_rows, 0, cut))
     after = [early_rows[0][1]]
     first = []
@@ -693,15 +698,17 @@
             table, where, rows, late_rows, own, other_first, got[1, "B"][0], model, start, columns, after
         )
         if first:
-            (value,) = hold([value], [got[2, "A"][0]], BEGIN_WEIGHT)
-            (value,) = hold([value], [other_rest])
+            (value,) = hold([value], got[2, "A"], NEXT_WEIGHT)
         got.setdefault((2, "A"), []).append(swap_z(value, "A"))
         first.append(
-            products(table, where, rows, late_rows, own, other_first, 0, model, columns, "first_kept", [value], True)
+            products(
+                table, where, rows, late_rows, own, other_first, 0, model, columns, "first_kept", [value], True
+            )
         )
         after = [first[0]]
     marker = value
     got[2, "B"] = [swap_z(got[1, "A"][0], "B")]
+    (other_rest,) = hold([other_rest], [], HIDDEN_WEIGHT)
 
     halves, all_choices, weights_of = [], [], {}
     only_first = max(uses[3, "B"]) <= 0
@@ -715,22 +722,24 @@
         all_choices.extend(choices)
         return sums
 
-    def pass_on(turn, name, after, chunk=None, waited=()):
+    def pass_on(turn, name, after, chunk=None, waited=(), weight=1):
         coming = got[turn - 1, "B" if name == "A" else "A"]
-        parts, start, chunked = (first, rest), cut, turn == depth and name == "B"
         used = uses[turn, name]
-        senders = [z for z in range(depth) if used[z] >= 0] if turn == depth - 1 else range(depth)
-        others = [z for z in range(depth) if z not in senders]
-        if others and chunk is None and len(coming) == 1:
-            weights_of[turn, name] = [swap_z(coming[0], name, others)]
-            ends = {0, depth - 1} if name == "A" else set()
-            coming = [] if set(senders) <= ends else coming
+        senders = range(depth)
+        if turn == depth - 1 and min(used) < 0 and name == "A" and len(coming) == 1:
+            senders = [z for z in range(depth) if used[z] >= 0]
+            if (turn, name) not in weights_of:
+                coming[:] = hold(coming, [], PASS_WEIGHT)
+                others = [z for z in range(depth) if z not in senders]
+                weights_of[turn, name] = [swap_z(coming[0], name, others)]
+            if set(senders) <= {0, depth - 1}:
+                coming = []
+        parts, start = (first, rest), cut
         if chunk is not None:
-            coming, parts, start = [coming[chunk]], (first[chunk:][:1], rest[chunk:][:1]), 0
-        weight = LAST_WEIGHT if (turn, name) == (depth, "A") else 1
-        values = list(combine(table, where, coming, *parts, turn, name, used, start, after, chunked, weight))
+            coming, parts, start = coming[chunk:][:1], (first[chunk:][:1], rest[chunk:][:1]), 0
+        values = list(combine(table, where, coming, *parts, turn, name, used, start, after, False, weight))
         if waited:
-            values[1:] = hold(values[1:], list(waited), 2 * LAST_WEIGHT)
+            values = list(hold(values, list(waited), WAITED_WEIGHT))
         got.setdefault((turn, name), []).extend(swap_z(value, name, senders) for value in values)
         return values[-1]
 
@@ -739,22 +748,38 @@
         return [[(turn, "A")], [(turn, "B")]] if both else [[(turn, "A"), (turn, "B")]]
 
     rest = []
-    marker = pass_on(3, "B", [marker], 0) if only_first else marker
-    for rows, _, columns in chunks:
+
+    def other_products(chunk, after):
+        rows, _, columns = chunks[chunk]
         rest.append(
-            products(table, where, rows, late_rows, own, other_rest, 1, model, columns, "rest_kept", [marker])
+            products(table, where, rows, late_rows, own, other_rest, 1, model, columns, "rest_kept", after)
         )
-    marker = pass_on(3, "A", rest)
-    for chunk in range(2)[only_first:]:
-        marker = pass_on(3, "B", [marker], chunk)
-    sums = backprop([[(0, "own")], [(1, "A")], [(1, "B")]], None, False, [marker])
+        return rest[chunk]
+
+    apart = max(uses[3, "B"]) <= 0 and depth == 4
+    if apart:
+        for chunk in range(2):
+            marker = pass_on(3, "B", [marker], chunk)
+            marker = other_products(chunk, [marker])
+            marker = pass_on(3, "A", [marker], chunk)
+    else:
+        marker = other_products(1, [other_products(0, [marker])])
+        marker = pass_on(3, "A", [marker])
+        for chunk in range(2):
+            marker = pass_on(3, "B", [marker], chunk)
+    sums = backprop([[(0, "own")], [(1, "A")], [(1, "B")]], None, False, got[2, "A"][:1])
     sooner = halves[1::2]
     for turn in range(2, depth):
         choices = choices_of(turn)
         if turn > 2:
             waited = [array for key in ((turn, "A"), (turn, "B")) for array in weights_of.get(key, [])]
-            pass_on(turn + 1, "B", [sums, *sooner], waited=waited)
-            marker = pass_on(turn + 1, "A", [sums])
+            if apart and turn + 1 == depth:
+                pass_on(depth, "B", [sums], 0, (), ENTER_WEIGHT)
+                pass_on(depth, "B", [sums, *sooner], 1, waited, LEAVE_WEIGHT)
+                marker = pass_on(depth, "A", [sums], weight=LAST_WEIGHT)
+            else:
+                pass_on(turn + 1, "B", [sums, *sooner, *waited])
+                marker = pass_on(turn + 1, "A", [sums])
         sums = backprop(choices, sums, len(choices) == 1, [marker])
     slot_grad = sums[0:1, :slots] + swap(sums[0:1, slots:], 1, 0)
     grads = lax.all_to_all(

time: 125 us -> 124 us (level); the launches traced: 123 us -> 124 us
  waiting for transfers between devices: 33.7 us -> 35.7 us
  starting transfers between devices: 42.2 us -> 40.4 us
    pallas_call x5 -> x7, Pallas kernels: 3.9 us -> 5.09 us  [combine(): pl.pallas_call(functools.partial(combine_kernel, table, ('use', turn, nam...]
    ppermute x12 -> x13, waiting for transfers between devices: 9.26 us -> 9.96 us  [swap_z(): return lax.ppermute(value, 'ctx', pairs)]
    ppermute x12 -> x13, starting transfers between devices: 27.4 us -> 27 us  [swap_z(): return lax.ppermute(value, 'ctx', pairs)]
  transfers between devices with their start and end apart: 28 -> 29, of which waited for: 13 -> 11; matrix products, arithmetic and copies ran while one was open for 1% -> 1% of each run, Pallas kernels for 27% -> 27%
where the time goes in v11:
time: 124 us
  starting transfers between devices  40.4 us (33%)
  Pallas kernels  37.7 us (30%)
  waiting for transfers between devices  35.7 us (29%)
  blocking collectives  6.08 us (5%)
  local copies, waits for them, and re-layouts  3.12 us (3%)
    ppermute x13, starting transfers between devices, swap_z(): return lax.ppermute(value, 'ctx', pairs)  27 us
    ppermute x8, waiting for transfers between devices, swap(): return lax.ppermute(value, 'ctx', [(i, i ^ x) for i in range(groups)])  13.8 us
    ppermute x8, waiting for transfers between devices, swap(): return lax.ppermute(value, 'exp', [(i, i ^ exp) for i in range(experts)])  11.9 us
    pallas_call x3, Pallas kernels, back_part(): pl.pallas_call(functools.partial(back_kernel, table, model, cut, counts,...  9.99 us
    ppermute x13, waiting for transfers between devices, swap_z(): return lax.ppermute(value, 'ctx', pairs)  9.96 us
    ppermute x8, starting transfers between devices, swap(): return lax.ppermute(value, 'ctx', [(i, i ^ x) for i in range(groups)])  8.93 us
    pallas_call x4, Pallas kernels, products(): pl.pallas_call(functools.partial(products_kernel, table, model, counts, p...  7.85 us
    all_to_all x1, blocking collectives, per_device_full(): lax.all_to_all(slot_grad.reshape(experts, tokens), 'exp', split_axis=0, c...  6.08 us
  transfers between devices with their start and end apart: 29, of which 11 were waited for; matrix products, arithmetic and copies ran while one was open for 1% of the time, Pallas kernels for 27%

profile of v11, /device:TPU:0, one launch (start us, length us, event | category | flops | bytes accessed | tf_op | source)
XLA Modules:
  0.0 124.0 jit_solution(18401262720337706537)
XLA Ops:
  0.6 2.2 %make_rows.1 = (bf16[128,1536]{1,0:T(8,128)(2,1)}, bf16[128,1408]{1,0:T(8,128)(2,1)}, f32[4,128]{1,0:T(4,128)}) custom-call(bf16[2880,128]{1,0:T(8,128)(2,1)} %bitcast.22, f32[4,128]{1,0:T(4,128)} %bitcast.23, s32[4,128]{1,0:T(4,128)} %bitcast.18), custom_call_target="tpu_custom_call" | custom-call | flops 2000000 | bytes 6000000 | tf_op jit(solution)/shard_map/make_rows/pallas_call | solution.py:167
  2.8 3.0 %collective-permute-start.1 = (bf16[128,1536]{1,0:T(8,128)(2,1)}, bf16[128,1536]{1,0:T(8,128)(2,1)S(1)}, u32[]{:S(2)}, u32[]{:S(2)}) collective-permute-start(bf16[128,1536]{1,0:T(8,128)(2,1)} %get-tuple-element.19.refs_0_), channel_id=1, source_target_pairs={{0,4},{4,0},{8,12},{12,8},{16,20},{20,16},{24,28},{28,24},{1,5},{5... | collective-permute-start | bytes 1179656 | tf_op jit(solution)/shard_map/ppermute | solution.py:645
  8.1 4.4 %collective-permute-start.12 = (bf16[192,2880]{1,0:T(8,128)(2,1)}, bf16[192,2880]{1,0:T(8,128)(2,1)S(1)}, u32[]{:S(2)}, u32[]{:S(2)}) collective-permute-start(bf16[192,2880]{1,0:T(8,128)(2,1)} %bitcast.16), channel_id=1, source_target_pairs={{0,8},{4,12},{8,0},{12,4},{16,24},{20,28},{24,16},{28,20},{1,9},{5... | collective-permute-start | bytes 3317768 | tf_op jit(solution)/shard_map/ppermute | solution.py:657
  15.6 2.2 %split_hidden.1 = (bf16[4,192,512]{2,1,0:T(8,128)(2,1)S(1)}, bf16[1,192,512]{2,1,0:T(8,128)(2,1)S(1)}, bf16[3,192,512]{2,1,0:T(8,128)(2,1)S(1)}) custom-call(s32[32]{0:T(128)S(1)} %dynamic-slice_bitcast_fusion.where_ref, bf16[512,1536]{1,0:T(8,128)(2,1)S(1)} %bitcast.14, bf16[128,1536]{1,0:T(8,128)(2,1)S(1)} %copy-done.1), custom_call_target="tpu_custom_call" | custom-call | flops 2000000 | bytes 6000000 | tf_op jit(solution)/shard_map/split_hidden/pallas_call | solution.py:258
  18.9 4.6 %collective-permute-done.3.refs_2_.refs_5_.refs_9_ = bf16[1,192,512]{2,1,0:T(8,128)(2,1)S(1)} collective-permute-done((bf16[1,192,512]{2,1,0:T(8,128)(2,1)S(1)}, bf16[1,192,512]{2,1,0:T(8,128)(2,1)S(1)}, u32[]{:S(2)}, u32[]{:S(2)}) %collective-permute-start.3) | collective-permute-done | bytes 196640 | tf_op jit(solution)/shard_map/ppermute | solution.py:645
  24.1 7.6 %collective-permute-done.4.refs_4_.refs_1_ = bf16[128,1408]{1,0:T(8,128)(2,1)S(1)} collective-permute-done((bf16[128,1408]{1,0:T(8,128)(2,1)S(1)}, bf16[128,1408]{1,0:T(8,128)(2,1)S(1)}, u32[]{:S(2)}, u32[]{:S(2)}) %collective-permute-start.4) | collective-permute-done | bytes 360480 | tf_op jit(solution)/shard_map/ppermute | solution.py:645
  37.0 2.2 %first_sums.2.refs_6_ = bf16[192,1472]{1,0:T(8,128)(2,1)S(1)} custom-call(s32[32]{0:T(128)S(1)} %dynamic-slice_bitcast_fusion.where_ref, bf16[4,128,1536]{2,1,0:T(8,128)(2,1)S(1)} %pack_rows.2.refs_0_.refs_2_.refs_6_, bf16[4,128,1536]{2,1,0:T(8,128)(2,1)S(1)} %collective-permute-done.5.refs_1_.refs_3_.refs_7_, ...), custom_call_target="tpu_custom_call" | custom-call | flops 1000000 | bytes 3000000 | tf_op jit(solution)/shard_map/first_sums/pallas_call | solution.py:355
  40.6 3.2 %collective-permute-done.7.refs_2_.refs_4_ = bf16[128,1408]{1,0:T(8,128)(2,1)S(1)} collective-permute-done((bf16[128,1408]{1,0:T(8,128)(2,1)S(1)}, bf16[128,1408]{1,0:T(8,128)(2,1)S(1)}, u32[]{:S(2)}, u32[]{:S(2)}) %collective-permute-start.7) | collective-permute-done | bytes 360480 | tf_op jit(solution)/shard_map/ppermute | solution.py:647
  43.9 7.3 %collective-permute-done.9.refs_4_.refs_6_ = bf16[128,1408]{1,0:T(8,128)(2,1)S(1)} collective-permute-done((bf16[128,1408]{1,0:T(8,128)(2,1)S(1)}, bf16[128,1408]{1,0:T(8,128)(2,1)S(1)}, u32[]{:S(2)}, u32[]{:S(2)}) %collective-permute-start.9) | collective-permute-done | bytes 360480 | tf_op jit(solution)/shard_map/ppermute | solution.py:647
  52.8 2.1 %first_sums.3.refs_0_ = bf16[192,1408]{1,0:T(8,128)(2,1)S(1)} custom-call(s32[32]{0:T(128)S(1)} %dynamic-slice_bitcast_fusion.where_ref, bf16[2,128,1408]{2,1,0:T(8,128)(2,1)S(1)} %pack_rows.3.refs_0_.refs_2_, bf16[2,128,1408]{2,1,0:T(8,128)(2,1)S(1)} %collective-permute-done.6.refs_7_.refs_1_.refs_3_, ...), custom_call_target="tpu_custom_call" | custom-call | flops 1000000 | bytes 3000000 | tf_op jit(solution)/shard_map/first_sums/pallas_call | solution.py:355
  56.5 3.4 %rest_kept.2.refs_0_.refs_1_.refs_2_.refs_3_ = f32[3,192,1472]{2,1,0:T(8,128)S(1)} custom-call(s32[32]{0:T(128)S(1)} %dynamic-slice_bitcast_fusion.where_ref, bf16[4,128,1536]{2,1,0:T(8,128)(2,1)S(1)} %pack_rows.2.refs_0_.refs_2_.refs_6_, bf16[4,128,1536]{2,1,0:T(8,128)(2,1)S(1)} %collective-permute-done.5.refs_1_.refs_3_.refs_7_, ...), custom_call_target="tpu_custom_call" | custom-call | flops 1000000 | bytes 3000000 | tf_op jit(solution)/shard_map/rest_kept/pallas_call | solution.py:319
  60.6 5.6 %collective-permute-start.25 = (bf16[192,1472]{1,0:T(8,128)(2,1)S(1)}, bf16[192,1472]{1,0:T(8,128)(2,1)S(1)}, u32[]{:S(2)}, u32[]{:S(2)}) collective-permute-start(bf16[192,1472]{1,0:T(8,128)(2,1)S(1)} %combine.8.refs_2_), channel_id=1, source_target_pairs={{0,8},{4,12},{24,16},{28,20},{1,9},{5,13},{25,17},{29,21},{2,10},{... | collective-permute-start | bytes 1695752 | tf_op jit(solution)/shard_map/ppermute | solution.py:657
  71.0 4.7 %back_part.3 = (bf16[3,192,512]{2,1,0:T(8,128)(2,1)S(1)}, bf16[3,192,512]{2,1,0:T(8,128)(2,1)S(1)}, f32[8,1024]{1,0:T(8,128)S(1)}) custom-call(s32[32]{0:T(128)S(1)} %dynamic-slice_bitcast_fusion.where_ref, bf16[4,128,1536]{2,1,0:T(8,128)(2,1)S(1)} %pack_rows.2.refs_0_.refs_2_.refs_6_, ...), custom_call_target="tpu_custom_call" | custom-call | flops 6000000 | bytes 18000000 | tf_op jit(solution)/shard_map/back_part/pallas_call | solution.py:554
  76.3 3.3 %rest_kept.3.refs_0_.refs_1_.refs_3_.refs_4_ = f32[3,192,1408]{2,1,0:T(8,128)S(1)} custom-call(s32[32]{0:T(128)S(1)} %dynamic-slice_bitcast_fusion.where_ref, bf16[2,128,1408]{2,1,0:T(8,128)(2,1)S(1)} %pack_rows.3.refs_0_.refs_2_, bf16[2,128,1408]{2,1,0:T(8,128)(2,1)S(1)} %collective-permute-done.6.refs_7_.refs_1_.refs_3_, ...), custom_call_target="tpu_custom_call" | custom-call | flops 1000000 | bytes 3000000 | tf_op jit(solution)/shard_map/rest_kept/pallas_call | solution.py:319
  80.3 8.8 %collective-permute-start.27 = (bf16[192,1408]{1,0:T(8,128)(2,1)S(1)}, bf16[192,1408]{1,0:T(8,128)(2,1)S(1)}, u32[]{:S(2)}, u32[]{:S(2)}) collective-permute-start(bf16[192,1408]{1,0:T(8,128)(2,1)S(1)} %combine.10.refs_15_), channel_id=1, source_target_pairs={{0,8},{4,12},{24,16},{28,20},{1,9},{5,13},{25,17},{29,21},{2,10},{... | collective-permute-start | bytes 1622024 | tf_op jit(solution)/shard_map/ppermute | solution.py:657
  89.1 2.6 %back_part.4 = (bf16[1,192,512]{2,1,0:T(8,128)(2,1)S(1)}, bf16[1,192,512]{2,1,0:T(8,128)(2,1)S(1)}, f32[8,1024]{1,0:T(8,128)S(1)}) custom-call(s32[32]{0:T(128)S(1)} %dynamic-slice_bitcast_fusion.where_ref, bf16[4,128,1536]{2,1,0:T(8,128)(2,1)S(1)} %pack_rows.2.refs_0_.refs_2_.refs_6_, ...), custom_call_target="tpu_custom_call" | custom-call | flops 6000000 | bytes 18000000 | tf_op jit(solution)/shard_map/back_part/pallas_call | solution.py:554
  92.6 2.4 %collective-permute-start.24 = (bf16[192,2880]{1,0:T(8,128)(2,1)S(1)}, bf16[192,2880]{1,0:T(8,128)(2,1)S(1)}, u32[]{:S(2)}, u32[]{:S(2)}) collective-permute-start(bf16[192,2880]{1,0:T(8,128)(2,1)S(1)} %combine.11.refs_15_), channel_id=1, source_target_pairs={{0,8},{4,12},{8,0},{12,4},{16,24},{20,28},{24,16},{28,20},{1,9},{5... | collective-permute-start | bytes 3317768 | tf_op jit(solution)/shard_map/ppermute | solution.py:657
  96.4 5.3 %collective-permute-done.27.refs_0_ = bf16[192,1408]{1,0:T(8,128)(2,1)S(1)} collective-permute-done((bf16[192,1408]{1,0:T(8,128)(2,1)S(1)}, bf16[192,1408]{1,0:T(8,128)(2,1)S(1)}, u32[]{:S(2)}, u32[]{:S(2)}) %collective-permute-start.27) | collective-permute-done | bytes 540704 | tf_op jit(solution)/shard_map/ppermute | solution.py:657
  103.3 2.7 %back_part.5 = (bf16[1,192,512]{2,1,0:T(8,128)(2,1)S(1)}, bf16[1,192,512]{2,1,0:T(8,128)(2,1)S(1)}, f32[8,1024]{1,0:T(8,128)S(1)}) custom-call(s32[32]{0:T(128)S(1)} %dynamic-slice_bitcast_fusion.where_ref, bf16[4,128,1536]{2,1,0:T(8,128)(2,1)S(1)} %pack_rows.2.refs_0_.refs_2_.refs_6_, ...), custom_call_target="tpu_custom_call" | custom-call | flops 6000000 | bytes 18000000 | tf_op jit(solution)/shard_map/back_part/pallas_call | solution.py:554
  105.9 1.6 %collective-permute-start.20 = (f32[1,512]{1,0:T(1,128)S(1)}, f32[1,512]{1,0:T(1,128)S(1)}, u32[]{:S(2)}, u32[]{:S(2)}) collective-permute-start(f32[1,512]{1,0:T(1,128)S(1)} %slice.7), channel_id=1, source_target_pairs={{0,4},{4,0},{8,12},{12,8},{16,20},{20,16},{24,28},{28,24},{1,5},{5... | collective-permute-start | bytes 6152 | tf_op jit(solution)/shard_map/ppermute | solution.py:645
  108.0 1.6 %collective-permute-done.20 = f32[1,512]{1,0:T(1,128)S(1)} collective-permute-done((f32[1,512]{1,0:T(1,128)S(1)}, f32[1,512]{1,0:T(1,128)S(1)}, u32[]{:S(2)}, u32[]{:S(2)}) %collective-permute-start.20) | collective-permute-done | bytes 2080 | tf_op jit(solution)/shard_map/ppermute | solution.py:645
  111.1 6.1 %all_to_all.11 = f32[4,1,128]{2,1,0:T(1,128)S(1)} all-to-all(f32[4,1,128]{2,1,0:T(1,128)S(1)} %add_bitcast_fusion), channel_id=1, replica_groups=mesh['ctx'=8,'exp'=4] {'exp'}, dimensions={0} | all-to-all | bytes 4096 | tf_op jit(solution)/shard_map/all_to_all | solution.py:785
  117.8 2.9 %join_hidden.1 = bf16[512,1536]{1,0:T(8,128)(2,1)} custom-call(s32[32]{0:T(128)S(1)} %dynamic-slice_bitcast_fusion.where_ref, bf16[3,192,512]{2,1,0:T(8,128)(2,1)S(1)} %get-tuple-element.27.refs_0_, bf16[3,192,512]{2,1,0:T(8,128)(2,1)S(1)} %collective-permute-done.21.refs_1_.refs_3_, bf16[1,192,512]{2,1,0:T(8,128)(2,1)S(1)} %get-tuple-element.29.refs_2_, ...), custom_call_target="tpu_custom_call" | custom-call | flops 2000000 | bytes 6000000 | tf_op jit(solution)/shard_map/join_hidden/pallas_call | solution.py:596
  120.7 1.8 %collective-permute-done.24.refs_0_ = bf16[192,2880]{1,0:T(8,128)(2,1)S(1)} collective-permute-done((bf16[192,2880]{1,0:T(8,128)(2,1)S(1)}, bf16[192,2880]{1,0:T(8,128)(2,1)S(1)}, u32[]{:S(2)}, u32[]{:S(2)}) %collective-permute-start.24) | collective-permute-done | bytes 1105952 | tf_op jit(solution)/shard_map/ppermute | solution.py:657
  (82 shorter events, 31.3 us)
Async XLA Ops:
  2.8 15.6 %collective-permute-start.1 = (bf16[128,1536]{1,0:T(8,128)(2,1)}, bf16[128,1536]{1,0:T(8,128)(2,1)S(1)}, u32[]{:S(2)}, u32[]{:S(2)}) collective-permute-start(bf16[128,1536]{1,0:T(8,128)(2,1)} %get-tuple-element.19.refs_0_), channel_id=1, source_target_pairs={{0,4},{4,0},{8,12},{12,8},{16,20},{20,16},{24,28},{28,24},{1,5},{5... | collective-permute-start | bytes 1179656 | tf_op jit(solution)/shard_map/ppermute | solution.py:645
  5.8 12.6 %collective-permute-start = (bf16[128,1536]{1,0:T(8,128)(2,1)}, bf16[128,1536]{1,0:T(8,128)(2,1)S(1)}, u32[]{:S(2)}, u32[]{:S(2)}) collective-permute-start(bf16[128,1536]{1,0:T(8,128)(2,1)} %get-tuple-element.19.refs_0_), channel_id=1, source_target_pairs={{0,2},{1,3},{2,0},{3,1},{4,6},{5,7},{6,4},{7,5},{8,10},{9,11},{10,... | collective-permute-start | bytes 1179656 | tf_op jit(solution)/shard_map/ppermute | solution.py:647
  7.4 26.4 %collective-permute-start.15 = (bf16[192,2880]{1,0:T(8,128)(2,1)}, bf16[192,2880]{1,0:T(8,128)(2,1)S(1)}, u32[]{:S(2)}, u32[]{:S(2)}) collective-permute-start(bf16[192,2880]{1,0:T(8,128)(2,1)} %bitcast.15), channel_id=1, source_target_pairs={{8,16},{12,20},{16,8},{20,12},{9,17},{13,21},{17,9},{21,13},{10,18... | collective-permute-start | bytes 3317768 | tf_op jit(solution)/shard_map/ppermute | solution.py:657
  8.1 28.7 %collective-permute-start.12 = (bf16[192,2880]{1,0:T(8,128)(2,1)}, bf16[192,2880]{1,0:T(8,128)(2,1)S(1)}, u32[]{:S(2)}, u32[]{:S(2)}) collective-permute-start(bf16[192,2880]{1,0:T(8,128)(2,1)} %bitcast.16), channel_id=1, source_target_pairs={{0,8},{4,12},{8,0},{12,4},{16,24},{20,28},{24,16},{28,20},{1,9},{5... | collective-permute-start | bytes 3317768 | tf_op jit(solution)/shard_map/ppermute | solution.py:657
  18.4 13.3 %collective-permute-start.2 = (bf16[128,1536]{1,0:T(8,128)(2,1)S(1)}, bf16[128,1536]{1,0:T(8,128)(2,1)S(1)}, u32[]{:S(2)}, u32[]{:S(2)}) collective-permute-start(bf16[128,1536]{1,0:T(8,128)(2,1)S(1)} %hold.7.refs_1_.refs_2_), channel_id=1, source_target_pairs={{0,2},{1,3},{2,0},{3,1},{4,6},{5,7},{6,4},{7,5},{8,10},{9,11},{10,... | collective-permute-start | bytes 1179656 | tf_op jit(solution)/shard_map/ppermute | solution.py:647
  23.5 8.2 %collective-permute-start.4 = (bf16[128,1408]{1,0:T(8,128)(2,1)S(1)}, bf16[128,1408]{1,0:T(8,128)(2,1)S(1)}, u32[]{:S(2)}, u32[]{:S(2)}) collective-permute-start(bf16[128,1408]{1,0:T(8,128)(2,1)S(1)} %hold.8.refs_0_), channel_id=1, source_target_pairs={{0,4},{4,0},{8,12},{12,8},{16,20},{20,16},{24,28},{28,24},{1,5},{5... | collective-permute-start | bytes 1081352 | tf_op jit(solution)/shard_map/ppermute | solution.py:645
  32.6 11.3 %collective-permute-start.7 = (bf16[128,1408]{1,0:T(8,128)(2,1)S(1)}, bf16[128,1408]{1,0:T(8,128)(2,1)S(1)}, u32[]{:S(2)}, u32[]{:S(2)}) collective-permute-start(bf16[128,1408]{1,0:T(8,128)(2,1)S(1)} %hold.8.refs_0_), channel_id=1, source_target_pairs={{0,2},{1,3},{2,0},{3,1},{4,6},{5,7},{6,4},{7,5},{8,10},{9,11},{10,... | collective-permute-start | bytes 1081352 | tf_op jit(solution)/shard_map/ppermute | solution.py:647
  33.7 17.4 %collective-permute-start.9 = (bf16[128,1408]{1,0:T(8,128)(2,1)S(1)}, bf16[128,1408]{1,0:T(8,128)(2,1)S(1)}, u32[]{:S(2)}, u32[]{:S(2)}) collective-permute-start(bf16[128,1408]{1,0:T(8,128)(2,1)S(1)} %collective-permute-done.4.refs_4_.refs_1_), channel_id=1, source_target_pairs={{0,2},{1,3},{2,0},{3,1},{4,6},{5,7},{6,4},{7,5},{8,10},{9,11},{10,... | collective-permute-start | bytes 1081352 | tf_op jit(solution)/shard_map/ppermute | solution.py:647
  39.2 15.7 %collective-permute-start.16 = (bf16[192,1472]{1,0:T(8,128)(2,1)S(1)}, bf16[192,1472]{1,0:T(8,128)(2,1)S(1)}, u32[]{:S(2)}, u32[]{:S(2)}) collective-permute-start(bf16[192,1472]{1,0:T(8,128)(2,1)S(1)} %first_sums.2.refs_6_), channel_id=1, source_target_pairs={{0,8},{4,12},{8,0},{12,4},{16,24},{20,28},{24,16},{28,20},{1,9},{5... | collective-permute-start | bytes 1695752 | tf_op jit(solution)/shard_map/ppermute | solution.py:657
  39.3 27.0 %collective-permute-start.13 = (bf16[192,2880]{1,0:T(8,128)(2,1)S(1)}, bf16[192,2880]{1,0:T(8,128)(2,1)S(1)}, u32[]{:S(2)}, u32[]{:S(2)}) collective-permute-start(bf16[192,2880]{1,0:T(8,128)(2,1)S(1)} %collective-permute-done.12.refs_1_.refs_12_), channel_id=1, source_target_pairs={{8,16},{12,20},{16,8},{20,12},{9,17},{13,21},{17,9},{21,13},{10,18... | collective-permute-start | bytes 3317768 | tf_op jit(solution)/shard_map/ppermute | solution.py:657
  40.0 16.5 %collective-permute-start.11 = (bf16[3,192,512]{2,1,0:T(8,128)(2,1)S(1)}, bf16[3,192,512]{2,1,0:T(8,128)(2,1)S(1)}, u32[]{:S(2)}, u32[]{:S(2)}) collective-permute-start(bf16[3,192,512]{2,1,0:T(8,128)(2,1)S(1)} %get-tuple-element.23), channel_id=1, source_target_pairs={{0,4},{4,0},{8,12},{12,8},{16,20},{20,16},{24,28},{28,24},{1,5},{5... | collective-permute-start | bytes 1769480 | tf_op jit(solution)/shard_map/ppermute | solution.py:645
  43.9 7.8 %collective-permute-start.8 = (bf16[128,1408]{1,0:T(8,128)(2,1)S(1)}, bf16[128,1408]{1,0:T(8,128)(2,1)S(1)}, u32[]{:S(2)}, u32[]{:S(2)}) collective-permute-start(bf16[128,1408]{1,0:T(8,128)(2,1)S(1)} %collective-permute-done.7.refs_2_.refs_4_), channel_id=1, source_target_pairs={{0,1},{1,0},{2,3},{3,2},{4,5},{5,4},{6,7},{7,6},{8,9},{9,8},{10,11... | collective-permute-start | bytes 1081352 | tf_op jit(solution)/shard_map/ppermute | solution.py:647
  55.0 14.4 %collective-permute-start.18 = (bf16[192,1408]{1,0:T(8,128)(2,1)S(1)}, bf16[192,1408]{1,0:T(8,128)(2,1)S(1)}, u32[]{:S(2)}, u32[]{:S(2)}) collective-permute-start(bf16[192,1408]{1,0:T(8,128)(2,1)S(1)} %hold.12.refs_2_.refs_10_), channel_id=1, source_target_pairs={{0,8},{4,12},{8,0},{12,4},{16,24},{20,28},{24,16},{28,20},{1,9},{5... | collective-permute-start | bytes 1622024 | tf_op jit(solution)/shard_map/ppermute | solution.py:657
  55.8 24.6 %collective-permute-start.17 = (bf16[192,1472]{1,0:T(8,128)(2,1)S(1)}, bf16[192,1472]{1,0:T(8,128)(2,1)S(1)}, u32[]{:S(2)}, u32[]{:S(2)}) collective-permute-start(bf16[192,1472]{1,0:T(8,128)(2,1)S(1)} %combine.7.refs_6_), channel_id=1, source_target_pairs={{8,16},{12,20},{16,8},{20,12},{9,17},{13,21},{17,9},{21,13},{10,18... | collective-permute-start | bytes 1695752 | tf_op jit(solution)/shard_map/ppermute | solution.py:657
  60.6 34.4 %collective-permute-start.25 = (bf16[192,1472]{1,0:T(8,128)(2,1)S(1)}, bf16[192,1472]{1,0:T(8,128)(2,1)S(1)}, u32[]{:S(2)}, u32[]{:S(2)}) collective-permute-start(bf16[192,1472]{1,0:T(8,128)(2,1)S(1)} %combine.8.refs_2_), channel_id=1, source_target_pairs={{0,8},{4,12},{24,16},{28,20},{1,9},{5,13},{25,17},{29,21},{2,10},{... | collective-permute-start | bytes 1695752 | tf_op jit(solution)/shard_map/ppermute | solution.py:657
  66.3 36.2 %collective-permute-start.14 = (bf16[192,2880]{1,0:T(8,128)(2,1)S(1)}, bf16[192,2880]{1,0:T(8,128)(2,1)S(1)}, u32[]{:S(2)}, u32[]{:S(2)}) collective-permute-start(bf16[192,2880]{1,0:T(8,128)(2,1)S(1)} %hold.10.refs_13_), channel_id=1, source_target_pairs={{8,0},{12,4},{16,24},{20,28},{9,1},{13,5},{17,25},{21,29},{10,2},{... | collective-permute-start | bytes 3317768 | tf_op jit(solution)/shard_map/ppermute | solution.py:657
  70.1 21.7 %collective-permute-start.19 = (bf16[192,1408]{1,0:T(8,128)(2,1)S(1)}, bf16[192,1408]{1,0:T(8,128)(2,1)S(1)}, u32[]{:S(2)}, u32[]{:S(2)}) collective-permute-start(bf16[192,1408]{1,0:T(8,128)(2,1)S(1)} %combine.9.refs_10_), channel_id=1, source_target_pairs={{8,16},{12,20},{16,8},{20,12},{9,17},{13,21},{17,9},{21,13},{10,18... | collective-permute-start | bytes 1622024 | tf_op jit(solution)/shard_map/ppermute | solution.py:657
  75.7 20.8 %collective-permute-start.21 = (bf16[3,192,512]{2,1,0:T(8,128)(2,1)S(1)}, bf16[3,192,512]{2,1,0:T(8,128)(2,1)S(1)}, u32[]{:S(2)}, u32[]{:S(2)}) collective-permute-start(bf16[3,192,512]{2,1,0:T(8,128)(2,1)S(1)} %get-tuple-element.28), channel_id=1, source_target_pairs={{0,4},{4,0},{8,12},{12,8},{16,20},{20,16},{24,28},{28,24},{1,5},{5... | collective-permute-start | bytes 1769480 | tf_op jit(solution)/shard_map/ppermute | solution.py:645
  80.3 21.4 %collective-permute-start.27 = (bf16[192,1408]{1,0:T(8,128)(2,1)S(1)}, bf16[192,1408]{1,0:T(8,128)(2,1)S(1)}, u32[]{:S(2)}, u32[]{:S(2)}) collective-permute-start(bf16[192,1408]{1,0:T(8,128)(2,1)S(1)} %combine.10.refs_15_), channel_id=1, source_target_pairs={{0,8},{4,12},{24,16},{28,20},{1,9},{5,13},{25,17},{29,21},{2,10},{... | collective-permute-start | bytes 1622024 | tf_op jit(solution)/shard_map/ppermute | solution.py:657
  92.6 29.9 %collective-permute-start.24 = (bf16[192,2880]{1,0:T(8,128)(2,1)S(1)}, bf16[192,2880]{1,0:T(8,128)(2,1)S(1)}, u32[]{:S(2)}, u32[]{:S(2)}) collective-permute-start(bf16[192,2880]{1,0:T(8,128)(2,1)S(1)} %combine.11.refs_15_), channel_id=1, source_target_pairs={{0,8},{4,12},{8,0},{12,4},{16,24},{20,28},{24,16},{28,20},{1,9},{5... | collective-permute-start | bytes 3317768 | tf_op jit(solution)/shard_map/ppermute | solution.py:657
  95.7 24.9 %collective-permute-start.26 = (bf16[192,1472]{1,0:T(8,128)(2,1)S(1)}, bf16[192,1472]{1,0:T(8,128)(2,1)S(1)}, u32[]{:S(2)}, u32[]{:S(2)}) collective-permute-start(bf16[192,1472]{1,0:T(8,128)(2,1)S(1)} %combine.12), channel_id=1, source_target_pairs={{8,16},{12,20},{16,8},{20,12},{9,17},{13,21},{17,9},{21,13},{10,18... | collective-permute-start | bytes 1695752 | tf_op jit(solution)/shard_map/ppermute | solution.py:657
  102.6 18.1 %collective-permute-start.28 = (bf16[192,1408]{1,0:T(8,128)(2,1)S(1)}, bf16[192,1408]{1,0:T(8,128)(2,1)S(1)}, u32[]{:S(2)}, u32[]{:S(2)}) collective-permute-start(bf16[192,1408]{1,0:T(8,128)(2,1)S(1)} %hold.13), channel_id=1, source_target_pairs={{8,16},{12,20},{16,8},{20,12},{9,17},{13,21},{17,9},{21,13},{10,18... | collective-permute-start | bytes 1622024 | tf_op jit(solution)/shard_map/ppermute | solution.py:657
  107.5 10.3 %collective-permute-start.22 = (bf16[1,192,512]{2,1,0:T(8,128)(2,1)S(1)}, bf16[1,192,512]{2,1,0:T(8,128)(2,1)S(1)}, u32[]{:S(2)}, u32[]{:S(2)}) collective-permute-start(bf16[1,192,512]{2,1,0:T(8,128)(2,1)S(1)} %get-tuple-element.30), channel_id=1, source_target_pairs={{0,4},{4,0},{8,12},{12,8},{16,20},{20,16},{24,28},{28,24},{1,5},{5... | collective-permute-start | bytes 589832 | tf_op jit(solution)/shard_map/ppermute | solution.py:645
  109.6 8.2 %collective-permute-start.23 = (bf16[1,192,512]{2,1,0:T(8,128)(2,1)S(1)}, bf16[1,192,512]{2,1,0:T(8,128)(2,1)S(1)}, u32[]{:S(2)}, u32[]{:S(2)}) collective-permute-start(bf16[1,192,512]{2,1,0:T(8,128)(2,1)S(1)} %get-tuple-element.32), channel_id=1, source_target_pairs={{0,4},{4,0},{8,12},{12,8},{16,20},{20,16},{24,28},{28,24},{1,5},{5... | collective-permute-start | bytes 589832 | tf_op jit(solution)/shard_map/ppermute | solution.py:645
  (12 other events, 75.5 us)

commit v12 on v11

--- a/solution.py
+++ b/solution.py
@@ -16,7 +16,7 @@
 PASS_WEIGHT = 1
 WAITED_WEIGHT = 210
 ENTER_WEIGHT = 575
-LEAVE_WEIGHT = 5_300
+LEAVE_WEIGHT = 5_250
 LAST_WEIGHT = 90
 NT = (((1,), (1,)), ((), ()))
 NN = (((1,), (0,)), ((), ()))
@@ -689,7 +689,8 @@
     early_rows = (early_rows, places)
     other_rest = swap(other_rest, 1, 0)
 
-    got[1, "B"] = list(hold(got[1, "B"], got[1, "A"], FIRST_WEIGHT))
+    for name, value in zip("BA", hold([got[1, "B"][0], got[1, "A"][0]], [], FIRST_WEIGHT)):
+        got[1, name] = [value]
     chunks = ((late_rows, cut, model - cut), (early_rows, 0, cut))
     after = [early_rows[0][1]]
     first = []
@@ -722,16 +723,20 @@
         all_choices.extend(choices)
         return sums
 
+    def forward(turn, name, after):
+        coming = got[turn - 1, "B" if name == "A" else "A"]
+        coming[:] = hold(coming, after, PASS_WEIGHT)
+        others = [z for z in range(depth) if uses[turn, name][z] < 0]
+        weights_of[turn, name] = [swap_z(coming[0], name, others)]
+
     def pass_on(turn, name, after, chunk=None, waited=(), weight=1):
         coming = got[turn - 1, "B" if name == "A" else "A"]
         used = uses[turn, name]
         senders = range(depth)
         if turn == depth - 1 and min(used) < 0 and name == "A" and len(coming) == 1:
             senders = [z for z in range(depth) if used[z] >= 0]
-            if (turn, name) not in weights_of:
-                coming[:] = hold(coming, [], PASS_WEIGHT)
-                others = [z for z in range(depth) if z not in senders]
-                weights_of[turn, name] = [swap_z(coming[0], name, others)]
+            if chunk is None:
+                forward(turn, name, [])
             if set(senders) <= {0, depth - 1}:
                 coming = []
         parts, start = (first, rest), cut
@@ -758,10 +763,12 @@
 
     apart = max(uses[3, "B"]) <= 0 and depth == 4
     if apart:
+        marker = pass_on(3, "B", [marker], 0)
         for chunk in range(2):
-            marker = pass_on(3, "B", [marker], chunk)
             marker = other_products(chunk, [marker])
             marker = pass_on(3, "A", [marker], chunk)
+        forward(3, "A", [marker, first[1]])
+        marker = pass_on(3, "B", [marker], 1)
     else:
         marker = other_products(1, [other_products(0, [marker])])
         marker = pass_on(3, "A", [marker])
@@ -775,7 +782,7 @@
             waited = [array for key in ((turn, "A"), (turn, "B")) for array in weights_of.get(key, [])]
             if apart and turn + 1 == depth:
                 pass_on(depth, "B", [sums], 0, (), ENTER_WEIGHT)
-                pass_on(depth, "B", [sums, *sooner], 1, waited, LEAVE_WEIGHT)
+                pass_on(depth, "B", [sums], 1, [*waited, *sooner], LEAVE_WEIGHT)
                 marker = pass_on(depth, "A", [sums], weight=LAST_WEIGHT)
             else:
                 pass_on(turn + 1, "B", [sums, *sooner, *waited])

time: 124 us -> 125 us (level)
  waiting for transfers between devices: 35.7 us -> 34 us
  starting transfers between devices: 40.4 us -> 41.8 us
    ppermute x13, waiting for transfers between devices: 9.96 us -> 7.35 us  [swap_z(): return lax.ppermute(value, 'ctx', pairs)]
    ppermute x8, waiting for transfers between devices: 13.8 us -> 15.9 us  [swap(): return lax.ppermute(value, 'ctx', [(i, i ^ x) for i in range(groups)])]
  transfers between devices with their start and end apart: 29 -> 29, of which waited for: 11 -> 13; matrix products, arithmetic and copies ran while one was open for 1% -> 1% of each run, Pallas kernels for 27% -> 28%
where the time goes in v12:
time: 125 us; the launch traced here: 124 us
  starting transfers between devices  41.8 us (33%)
  Pallas kernels  37.9 us (30%)
  waiting for transfers between devices  34 us (27%)
  blocking collectives  6.4 us (5%)
  local copies, waits for them, and re-layouts  3.12 us (2%)
    ppermute x13, starting transfers between devices, swap_z(): return lax.ppermute(value, 'ctx', pairs)  27.8 us
    ppermute x8, waiting for transfers between devices, swap(): return lax.ppermute(value, 'ctx', [(i, i ^ x) for i in range(groups)])  15.9 us
    ppermute x8, waiting for transfers between devices, swap(): return lax.ppermute(value, 'exp', [(i, i ^ exp) for i in range(experts)])  10.7 us
    pallas_call x3, Pallas kernels, back_part(): pl.pallas_call(functools.partial(back_kernel, table, model, cut, counts,...  9.96 us
    ppermute x8, starting transfers between devices, swap(): return lax.ppermute(value, 'ctx', [(i, i ^ x) for i in range(groups)])  9.37 us
    pallas_call x4, Pallas kernels, products(): pl.pallas_call(functools.partial(products_kernel, table, model, counts, p...  8.03 us
    ppermute x13, waiting for transfers between devices, swap_z(): return lax.ppermute(value, 'ctx', pairs)  7.35 us
    all_to_all x1, blocking collectives, per_device_full(): lax.all_to_all(slot_grad.reshape(experts, tokens), 'exp', split_axis=0, c...  6.4 us
  transfers between devices with their start and end apart: 29, of which 13 were waited for; matrix products, arithmetic and copies ran while one was open for 1% of the time, Pallas kernels for 28%

profile of v12, /device:TPU:0, one launch (start us, length us, event | category | flops | bytes accessed | tf_op | source)
XLA Modules:
  0.0 124.2 jit_solution(9473829303852546983)
XLA Ops:
  0.6 2.2 %make_rows.1 = (bf16[128,1536]{1,0:T(8,128)(2,1)}, bf16[128,1408]{1,0:T(8,128)(2,1)}, f32[4,128]{1,0:T(4,128)}) custom-call(bf16[2880,128]{1,0:T(8,128)(2,1)} %bitcast.22, f32[4,128]{1,0:T(4,128)} %bitcast.23, s32[4,128]{1,0:T(4,128)} %bitcast.18), custom_call_target="tpu_custom_call" | custom-call | flops 2000000 | bytes 6000000 | tf_op jit(solution)/shard_map/make_rows/pallas_call | solution.py:167
  2.8 3.0 %collective-permute-start.1 = (bf16[128,1536]{1,0:T(8,128)(2,1)}, bf16[128,1536]{1,0:T(8,128)(2,1)S(1)}, u32[]{:S(2)}, u32[]{:S(2)}) collective-permute-start(bf16[128,1536]{1,0:T(8,128)(2,1)} %get-tuple-element.21.refs_0_), channel_id=1, source_target_pairs={{0,4},{4,0},{8,12},{12,8},{16,20},{20,16},{24,28},{28,24},{1,5},{5... | collective-permute-start | bytes 1179656 | tf_op jit(solution)/shard_map/ppermute | solution.py:645
  12.8 2.2 %split_hidden.1 = (bf16[4,192,512]{2,1,0:T(8,128)(2,1)S(1)}, bf16[1,192,512]{2,1,0:T(8,128)(2,1)S(1)}, bf16[3,192,512]{2,1,0:T(8,128)(2,1)S(1)}) custom-call(s32[32]{0:T(128)S(1)} %dynamic-slice_bitcast_fusion.where_ref, bf16[512,1536]{1,0:T(8,128)(2,1)S(1)} %bitcast.14, bf16[128,1536]{1,0:T(8,128)(2,1)S(1)} %copy-done.1), custom_call_target="tpu_custom_call" | custom-call | flops 2000000 | bytes 6000000 | tf_op jit(solution)/shard_map/split_hidden/pallas_call | solution.py:258
  18.1 2.7 %collective-permute-done.3.refs_2_.refs_5_.refs_9_ = bf16[1,192,512]{2,1,0:T(8,128)(2,1)S(1)} collective-permute-done((bf16[1,192,512]{2,1,0:T(8,128)(2,1)S(1)}, bf16[1,192,512]{2,1,0:T(8,128)(2,1)S(1)}, u32[]{:S(2)}, u32[]{:S(2)}) %collective-permute-start.3) | collective-permute-done | bytes 196640 | tf_op jit(solution)/shard_map/ppermute | solution.py:645
  21.4 7.9 %collective-permute-done.4.refs_4_.refs_1_ = bf16[128,1408]{1,0:T(8,128)(2,1)S(1)} collective-permute-done((bf16[128,1408]{1,0:T(8,128)(2,1)S(1)}, bf16[128,1408]{1,0:T(8,128)(2,1)S(1)}, u32[]{:S(2)}, u32[]{:S(2)}) %collective-permute-start.4) | collective-permute-done | bytes 360480 | tf_op jit(solution)/shard_map/ppermute | solution.py:645
  31.5 2.2 %collective-permute-done.13.refs_1_ = bf16[192,2880]{1,0:T(8,128)(2,1)S(1)} collective-permute-done((bf16[192,2880]{1,0:T(8,128)(2,1)}, bf16[192,2880]{1,0:T(8,128)(2,1)S(1)}, u32[]{:S(2)}, u32[]{:S(2)}) %collective-permute-start.13) | collective-permute-done | bytes 1105952 | tf_op jit(solution)/shard_map/ppermute | solution.py:657
  34.6 2.2 %first_sums.2.refs_6_ = bf16[192,1472]{1,0:T(8,128)(2,1)S(1)} custom-call(s32[32]{0:T(128)S(1)} %dynamic-slice_bitcast_fusion.where_ref, bf16[4,128,1536]{2,1,0:T(8,128)(2,1)S(1)} %pack_rows.2.refs_0_.refs_2_.refs_6_, bf16[4,128,1536]{2,1,0:T(8,128)(2,1)S(1)} %collective-permute-done.5.refs_1_.refs_3_.refs_7_, ...), custom_call_target="tpu_custom_call" | custom-call | flops 1000000 | bytes 3000000 | tf_op jit(solution)/shard_map/first_sums/pallas_call | solution.py:355
  36.8 2.4 %collective-permute-start.15 = (bf16[192,1472]{1,0:T(8,128)(2,1)S(1)}, bf16[192,1472]{1,0:T(8,128)(2,1)S(1)}, u32[]{:S(2)}, u32[]{:S(2)}) collective-permute-start(bf16[192,1472]{1,0:T(8,128)(2,1)S(1)} %first_sums.2.refs_6_), channel_id=1, source_target_pairs={{0,8},{4,12},{8,0},{12,4},{16,24},{20,28},{24,16},{28,20},{1,9},{5... | collective-permute-start | bytes 1695752 | tf_op jit(solution)/shard_map/ppermute | solution.py:657
  41.4 7.3 %collective-permute-done.9.refs_4_.refs_6_ = bf16[128,1408]{1,0:T(8,128)(2,1)S(1)} collective-permute-done((bf16[128,1408]{1,0:T(8,128)(2,1)S(1)}, bf16[128,1408]{1,0:T(8,128)(2,1)S(1)}, u32[]{:S(2)}, u32[]{:S(2)}) %collective-permute-start.9) | collective-permute-done | bytes 360480 | tf_op jit(solution)/shard_map/ppermute | solution.py:647
  50.4 2.1 %first_sums.3.refs_0_ = bf16[192,1408]{1,0:T(8,128)(2,1)S(1)} custom-call(s32[32]{0:T(128)S(1)} %dynamic-slice_bitcast_fusion.where_ref, bf16[2,128,1408]{2,1,0:T(8,128)(2,1)S(1)} %pack_rows.3.refs_0_.refs_2_, bf16[2,128,1408]{2,1,0:T(8,128)(2,1)S(1)} %collective-permute-done.6.refs_7_.refs_1_.refs_3_, ...), custom_call_target="tpu_custom_call" | custom-call | flops 1000000 | bytes 3000000 | tf_op jit(solution)/shard_map/first_sums/pallas_call | solution.py:355
  52.8 2.7 %collective-permute-start.18 = (bf16[192,1408]{1,0:T(8,128)(2,1)S(1)}, bf16[192,1408]{1,0:T(8,128)(2,1)S(1)}, u32[]{:S(2)}, u32[]{:S(2)}) collective-permute-start(bf16[192,1408]{1,0:T(8,128)(2,1)S(1)} %hold.11.refs_2_.refs_10_), channel_id=1, source_target_pairs={{0,8},{4,12},{8,0},{12,4},{16,24},{20,28},{24,16},{28,20},{1,9},{5... | collective-permute-start | bytes 1622024 | tf_op jit(solution)/shard_map/ppermute | solution.py:657
  57.0 3.4 %rest_kept.2.refs_0_.refs_1_.refs_2_.refs_3_ = f32[3,192,1472]{2,1,0:T(8,128)S(1)} custom-call(s32[32]{0:T(128)S(1)} %dynamic-slice_bitcast_fusion.where_ref, bf16[4,128,1536]{2,1,0:T(8,128)(2,1)S(1)} %pack_rows.2.refs_0_.refs_2_.refs_6_, bf16[4,128,1536]{2,1,0:T(8,128)(2,1)S(1)} %collective-permute-done.5.refs_1_.refs_3_.refs_7_, ...), custom_call_target="tpu_custom_call" | custom-call | flops 1000000 | bytes 3000000 | tf_op jit(solution)/shard_map/rest_kept/pallas_call | solution.py:319
  61.1 4.4 %collective-permute-start.25 = (bf16[192,1472]{1,0:T(8,128)(2,1)S(1)}, bf16[192,1472]{1,0:T(8,128)(2,1)S(1)}, u32[]{:S(2)}, u32[]{:S(2)}) collective-permute-start(bf16[192,1472]{1,0:T(8,128)(2,1)S(1)} %combine.8.refs_10_), channel_id=1, source_target_pairs={{0,8},{4,12},{24,16},{28,20},{1,9},{5,13},{25,17},{29,21},{2,10},{... | collective-permute-start | bytes 1695752 | tf_op jit(solution)/shard_map/ppermute | solution.py:657
  65.5 3.4 %rest_kept.3.refs_0_.refs_1_.refs_3_.refs_4_ = f32[3,192,1408]{2,1,0:T(8,128)S(1)} custom-call(s32[32]{0:T(128)S(1)} %dynamic-slice_bitcast_fusion.where_ref, bf16[2,128,1408]{2,1,0:T(8,128)(2,1)S(1)} %pack_rows.3.refs_0_.refs_2_, bf16[2,128,1408]{2,1,0:T(8,128)(2,1)S(1)} %collective-permute-done.6.refs_7_.refs_1_.refs_3_, ...), custom_call_target="tpu_custom_call" | custom-call | flops 1000000 | bytes 3000000 | tf_op jit(solution)/shard_map/rest_kept/pallas_call | solution.py:319
  73.2 6.7 %collective-permute-start.27 = (bf16[192,1408]{1,0:T(8,128)(2,1)S(1)}, bf16[192,1408]{1,0:T(8,128)(2,1)S(1)}, u32[]{:S(2)}, u32[]{:S(2)}) collective-permute-start(bf16[192,1408]{1,0:T(8,128)(2,1)S(1)} %combine.9.refs_1_.refs_2_), channel_id=1, source_target_pairs={{0,8},{4,12},{24,16},{28,20},{1,9},{5,13},{25,17},{29,21},{2,10},{... | collective-permute-start | bytes 1622024 | tf_op jit(solution)/shard_map/ppermute | solution.py:657
  79.9 4.7 %back_part.3 = (bf16[3,192,512]{2,1,0:T(8,128)(2,1)S(1)}, bf16[3,192,512]{2,1,0:T(8,128)(2,1)S(1)}, f32[8,1024]{1,0:T(8,128)S(1)}) custom-call(s32[32]{0:T(128)S(1)} %dynamic-slice_bitcast_fusion.where_ref, bf16[4,128,1536]{2,1,0:T(8,128)(2,1)S(1)} %pack_rows.2.refs_0_.refs_2_.refs_6_, ...), custom_call_target="tpu_custom_call" | custom-call | flops 6000000 | bytes 18000000 | tf_op jit(solution)/shard_map/back_part/pallas_call | solution.py:554
  85.5 2.6 %back_part.4 = (bf16[1,192,512]{2,1,0:T(8,128)(2,1)S(1)}, bf16[1,192,512]{2,1,0:T(8,128)(2,1)S(1)}, f32[8,1024]{1,0:T(8,128)S(1)}) custom-call(s32[32]{0:T(128)S(1)} %dynamic-slice_bitcast_fusion.where_ref, bf16[4,128,1536]{2,1,0:T(8,128)(2,1)S(1)} %pack_rows.2.refs_0_.refs_2_.refs_6_, ...), custom_call_target="tpu_custom_call" | custom-call | flops 6000000 | bytes 18000000 | tf_op jit(solution)/shard_map/back_part/pallas_call | solution.py:554
  89.0 4.2 %collective-permute-start.24 = (bf16[192,2880]{1,0:T(8,128)(2,1)S(1)}, bf16[192,2880]{1,0:T(8,128)(2,1)S(1)}, u32[]{:S(2)}, u32[]{:S(2)}) collective-permute-start(bf16[192,2880]{1,0:T(8,128)(2,1)S(1)} %combine.11.refs_15_), channel_id=1, source_target_pairs={{0,8},{4,12},{8,0},{12,4},{16,24},{20,28},{24,16},{28,20},{1,9},{5... | collective-permute-start | bytes 3317768 | tf_op jit(solution)/shard_map/ppermute | solution.py:657
  95.4 3.7 %collective-permute-done.21.refs_1_.refs_2_ = bf16[3,192,512]{2,1,0:T(8,128)(2,1)S(1)} collective-permute-done((bf16[3,192,512]{2,1,0:T(8,128)(2,1)S(1)}, bf16[3,192,512]{2,1,0:T(8,128)(2,1)S(1)}, u32[]{:S(2)}, u32[]{:S(2)}) %collective-permute-start.21) | collective-permute-done | bytes 589856 | tf_op jit(solution)/shard_map/ppermute | solution.py:645
  101.0 2.7 %back_part.5 = (bf16[1,192,512]{2,1,0:T(8,128)(2,1)S(1)}, bf16[1,192,512]{2,1,0:T(8,128)(2,1)S(1)}, f32[8,1024]{1,0:T(8,128)S(1)}) custom-call(s32[32]{0:T(128)S(1)} %dynamic-slice_bitcast_fusion.where_ref, bf16[4,128,1536]{2,1,0:T(8,128)(2,1)S(1)} %pack_rows.2.refs_0_.refs_2_.refs_6_, ...), custom_call_target="tpu_custom_call" | custom-call | flops 6000000 | bytes 18000000 | tf_op jit(solution)/shard_map/back_part/pallas_call | solution.py:554
  103.7 1.7 %collective-permute-start.20 = (f32[1,512]{1,0:T(1,128)S(1)}, f32[1,512]{1,0:T(1,128)S(1)}, u32[]{:S(2)}, u32[]{:S(2)}) collective-permute-start(f32[1,512]{1,0:T(1,128)S(1)} %slice.7), channel_id=1, source_target_pairs={{0,4},{4,0},{8,12},{12,8},{16,20},{20,16},{24,28},{28,24},{1,5},{5... | collective-permute-start | bytes 6152 | tf_op jit(solution)/shard_map/ppermute | solution.py:645
  109.1 6.4 %all_to_all.11 = f32[4,1,128]{2,1,0:T(1,128)S(1)} all-to-all(f32[4,1,128]{2,1,0:T(1,128)S(1)} %add_bitcast_fusion), channel_id=1, replica_groups=mesh['ctx'=8,'exp'=4] {'exp'}, dimensions={0} | all-to-all | bytes 4096 | tf_op jit(solution)/shard_map/all_to_all | solution.py:792
  116.1 2.9 %join_hidden.1 = bf16[512,1536]{1,0:T(8,128)(2,1)} custom-call(s32[32]{0:T(128)S(1)} %dynamic-slice_bitcast_fusion.where_ref, bf16[3,192,512]{2,1,0:T(8,128)(2,1)S(1)} %get-tuple-element.31.refs_0_, bf16[3,192,512]{2,1,0:T(8,128)(2,1)S(1)} %collective-permute-done.21.refs_1_.refs_2_, bf16[1,192,512]{2,1,0:T(8,128)(2,1)S(1)} %get-tuple-element.33.refs_2_, ...), custom_call_target="tpu_custom_call" | custom-call | flops 2000000 | bytes 6000000 | tf_op jit(solution)/shard_map/join_hidden/pallas_call | solution.py:596
  119.0 3.7 %collective-permute-done.24.refs_0_ = bf16[192,2880]{1,0:T(8,128)(2,1)S(1)} collective-permute-done((bf16[192,2880]{1,0:T(8,128)(2,1)S(1)}, bf16[192,2880]{1,0:T(8,128)(2,1)S(1)}, u32[]{:S(2)}, u32[]{:S(2)}) %collective-permute-start.24) | collective-permute-done | bytes 1105952 | tf_op jit(solution)/shard_map/ppermute | solution.py:657
  (82 shorter events, 35.9 us)
Async XLA Ops:
  2.8 12.8 %collective-permute-start.1 = (bf16[128,1536]{1,0:T(8,128)(2,1)}, bf16[128,1536]{1,0:T(8,128)(2,1)S(1)}, u32[]{:S(2)}, u32[]{:S(2)}) collective-permute-start(bf16[128,1536]{1,0:T(8,128)(2,1)} %get-tuple-element.21.refs_0_), channel_id=1, source_target_pairs={{0,4},{4,0},{8,12},{12,8},{16,20},{20,16},{24,28},{28,24},{1,5},{5... | collective-permute-start | bytes 1179656 | tf_op jit(solution)/shard_map/ppermute | solution.py:645
  5.8 10.8 %collective-permute-start = (bf16[128,1536]{1,0:T(8,128)(2,1)}, bf16[128,1536]{1,0:T(8,128)(2,1)S(1)}, u32[]{:S(2)}, u32[]{:S(2)}) collective-permute-start(bf16[128,1536]{1,0:T(8,128)(2,1)} %get-tuple-element.21.refs_0_), channel_id=1, source_target_pairs={{0,2},{1,3},{2,0},{3,1},{4,6},{5,7},{6,4},{7,5},{8,10},{9,11},{10,... | collective-permute-start | bytes 1179656 | tf_op jit(solution)/shard_map/ppermute | solution.py:647
  7.4 26.3 %collective-permute-start.13 = (bf16[192,2880]{1,0:T(8,128)(2,1)}, bf16[192,2880]{1,0:T(8,128)(2,1)S(1)}, u32[]{:S(2)}, u32[]{:S(2)}) collective-permute-start(bf16[192,2880]{1,0:T(8,128)(2,1)} %bitcast.15), channel_id=1, source_target_pairs={{0,8},{4,12},{8,0},{12,4},{16,24},{20,28},{24,16},{28,20},{1,9},{5... | collective-permute-start | bytes 3317768 | tf_op jit(solution)/shard_map/ppermute | solution.py:657
  8.9 25.2 %collective-permute-start.12 = (bf16[192,2880]{1,0:T(8,128)(2,1)}, bf16[192,2880]{1,0:T(8,128)(2,1)S(1)}, u32[]{:S(2)}, u32[]{:S(2)}) collective-permute-start(bf16[192,2880]{1,0:T(8,128)(2,1)} %bitcast.16), channel_id=1, source_target_pairs={{8,16},{12,20},{16,8},{20,12},{9,17},{13,21},{17,9},{21,13},{10,18... | collective-permute-start | bytes 3317768 | tf_op jit(solution)/shard_map/ppermute | solution.py:657
  16.6 12.6 %collective-permute-start.2 = (bf16[128,1536]{1,0:T(8,128)(2,1)S(1)}, bf16[128,1536]{1,0:T(8,128)(2,1)S(1)}, u32[]{:S(2)}, u32[]{:S(2)}) collective-permute-start(bf16[128,1536]{1,0:T(8,128)(2,1)S(1)} %hold.7.refs_1_.refs_2_), channel_id=1, source_target_pairs={{0,2},{1,3},{2,0},{3,1},{4,6},{5,7},{6,4},{7,5},{8,10},{9,11},{10,... | collective-permute-start | bytes 1179656 | tf_op jit(solution)/shard_map/ppermute | solution.py:647
  20.9 8.4 %collective-permute-start.4 = (bf16[128,1408]{1,0:T(8,128)(2,1)S(1)}, bf16[128,1408]{1,0:T(8,128)(2,1)S(1)}, u32[]{:S(2)}, u32[]{:S(2)}) collective-permute-start(bf16[128,1408]{1,0:T(8,128)(2,1)S(1)} %hold.8.refs_0_), channel_id=1, source_target_pairs={{0,4},{4,0},{8,12},{12,8},{16,20},{20,16},{24,28},{28,24},{1,5},{5... | collective-permute-start | bytes 1081352 | tf_op jit(solution)/shard_map/ppermute | solution.py:645
  30.1 11.3 %collective-permute-start.7 = (bf16[128,1408]{1,0:T(8,128)(2,1)S(1)}, bf16[128,1408]{1,0:T(8,128)(2,1)S(1)}, u32[]{:S(2)}, u32[]{:S(2)}) collective-permute-start(bf16[128,1408]{1,0:T(8,128)(2,1)S(1)} %hold.8.refs_0_), channel_id=1, source_target_pairs={{0,2},{1,3},{2,0},{3,1},{4,6},{5,7},{6,4},{7,5},{8,10},{9,11},{10,... | collective-permute-start | bytes 1081352 | tf_op jit(solution)/shard_map/ppermute | solution.py:647
  33.7 15.0 %collective-permute-start.9 = (bf16[128,1408]{1,0:T(8,128)(2,1)S(1)}, bf16[128,1408]{1,0:T(8,128)(2,1)S(1)}, u32[]{:S(2)}, u32[]{:S(2)}) collective-permute-start(bf16[128,1408]{1,0:T(8,128)(2,1)S(1)} %collective-permute-done.4.refs_4_.refs_1_), channel_id=1, source_target_pairs={{0,2},{1,3},{2,0},{3,1},{4,6},{5,7},{6,4},{7,5},{8,10},{9,11},{10,... | collective-permute-start | bytes 1081352 | tf_op jit(solution)/shard_map/ppermute | solution.py:647
  36.8 16.1 %collective-permute-start.15 = (bf16[192,1472]{1,0:T(8,128)(2,1)S(1)}, bf16[192,1472]{1,0:T(8,128)(2,1)S(1)}, u32[]{:S(2)}, u32[]{:S(2)}) collective-permute-start(bf16[192,1472]{1,0:T(8,128)(2,1)S(1)} %first_sums.2.refs_6_), channel_id=1, source_target_pairs={{0,8},{4,12},{8,0},{12,4},{16,24},{20,28},{24,16},{28,20},{1,9},{5... | collective-permute-start | bytes 1695752 | tf_op jit(solution)/shard_map/ppermute | solution.py:657
  39.2 31.1 %collective-permute-start.14 = (bf16[192,2880]{1,0:T(8,128)(2,1)S(1)}, bf16[192,2880]{1,0:T(8,128)(2,1)S(1)}, u32[]{:S(2)}, u32[]{:S(2)}) collective-permute-start(bf16[192,2880]{1,0:T(8,128)(2,1)S(1)} %get-tuple-element.26.refs_12_), channel_id=1, source_target_pairs={{8,16},{12,20},{16,8},{20,12},{9,17},{13,21},{17,9},{21,13},{10,18... | collective-permute-start | bytes 3317768 | tf_op jit(solution)/shard_map/ppermute | solution.py:657
  39.9 17.0 %collective-permute-start.11 = (bf16[3,192,512]{2,1,0:T(8,128)(2,1)S(1)}, bf16[3,192,512]{2,1,0:T(8,128)(2,1)S(1)}, u32[]{:S(2)}, u32[]{:S(2)}) collective-permute-start(bf16[3,192,512]{2,1,0:T(8,128)(2,1)S(1)} %get-tuple-element.25), channel_id=1, source_target_pairs={{0,4},{4,0},{8,12},{12,8},{16,20},{20,16},{24,28},{28,24},{1,5},{5... | collective-permute-start | bytes 1769480 | tf_op jit(solution)/shard_map/ppermute | solution.py:645
  41.4 7.8 %collective-permute-start.8 = (bf16[128,1408]{1,0:T(8,128)(2,1)S(1)}, bf16[128,1408]{1,0:T(8,128)(2,1)S(1)}, u32[]{:S(2)}, u32[]{:S(2)}) collective-permute-start(bf16[128,1408]{1,0:T(8,128)(2,1)S(1)} %collective-permute-done.7.refs_2_.refs_4_), channel_id=1, source_target_pairs={{0,1},{1,0},{2,3},{3,2},{4,5},{5,4},{6,7},{7,6},{8,9},{9,8},{10,11... | collective-permute-start | bytes 1081352 | tf_op jit(solution)/shard_map/ppermute | solution.py:647
  52.8 18.9 %collective-permute-start.18 = (bf16[192,1408]{1,0:T(8,128)(2,1)S(1)}, bf16[192,1408]{1,0:T(8,128)(2,1)S(1)}, u32[]{:S(2)}, u32[]{:S(2)}) collective-permute-start(bf16[192,1408]{1,0:T(8,128)(2,1)S(1)} %hold.11.refs_2_.refs_10_), channel_id=1, source_target_pairs={{0,8},{4,12},{8,0},{12,4},{16,24},{20,28},{24,16},{28,20},{1,9},{5... | collective-permute-start | bytes 1622024 | tf_op jit(solution)/shard_map/ppermute | solution.py:657
  56.3 28.4 %collective-permute-start.17 = (bf16[192,1472]{1,0:T(8,128)(2,1)S(1)}, bf16[192,1472]{1,0:T(8,128)(2,1)S(1)}, u32[]{:S(2)}, u32[]{:S(2)}) collective-permute-start(bf16[192,1472]{1,0:T(8,128)(2,1)S(1)} %combine.7.refs_6_), channel_id=1, source_target_pairs={{8,16},{12,20},{16,8},{20,12},{9,17},{13,21},{17,9},{21,13},{10,18... | collective-permute-start | bytes 1695752 | tf_op jit(solution)/shard_map/ppermute | solution.py:657
  61.1 32.1 %collective-permute-start.25 = (bf16[192,1472]{1,0:T(8,128)(2,1)S(1)}, bf16[192,1472]{1,0:T(8,128)(2,1)S(1)}, u32[]{:S(2)}, u32[]{:S(2)}) collective-permute-start(bf16[192,1472]{1,0:T(8,128)(2,1)S(1)} %combine.8.refs_10_), channel_id=1, source_target_pairs={{0,8},{4,12},{24,16},{28,20},{1,9},{5,13},{25,17},{29,21},{2,10},{... | collective-permute-start | bytes 1695752 | tf_op jit(solution)/shard_map/ppermute | solution.py:657
  70.3 29.9 %collective-permute-start.16 = (bf16[192,2880]{1,0:T(8,128)(2,1)S(1)}, bf16[192,2880]{1,0:T(8,128)(2,1)S(1)}, u32[]{:S(2)}, u32[]{:S(2)}) collective-permute-start(bf16[192,2880]{1,0:T(8,128)(2,1)S(1)} %hold.12.refs_13_), channel_id=1, source_target_pairs={{8,0},{12,4},{16,24},{20,28},{9,1},{13,5},{17,25},{21,29},{10,2},{... | collective-permute-start | bytes 3317768 | tf_op jit(solution)/shard_map/ppermute | solution.py:657
  72.5 15.7 %collective-permute-start.19 = (bf16[192,1408]{1,0:T(8,128)(2,1)S(1)}, bf16[192,1408]{1,0:T(8,128)(2,1)S(1)}, u32[]{:S(2)}, u32[]{:S(2)}) collective-permute-start(bf16[192,1408]{1,0:T(8,128)(2,1)S(1)} %combine.10.refs_15_), channel_id=1, source_target_pairs={{8,16},{12,20},{16,8},{20,12},{9,17},{13,21},{17,9},{21,13},{10,18... | collective-permute-start | bytes 1622024 | tf_op jit(solution)/shard_map/ppermute | solution.py:657
  73.2 21.5 %collective-permute-start.27 = (bf16[192,1408]{1,0:T(8,128)(2,1)S(1)}, bf16[192,1408]{1,0:T(8,128)(2,1)S(1)}, u32[]{:S(2)}, u32[]{:S(2)}) collective-permute-start(bf16[192,1408]{1,0:T(8,128)(2,1)S(1)} %combine.9.refs_1_.refs_2_), channel_id=1, source_target_pairs={{0,8},{4,12},{24,16},{28,20},{1,9},{5,13},{25,17},{29,21},{2,10},{... | collective-permute-start | bytes 1622024 | tf_op jit(solution)/shard_map/ppermute | solution.py:657
  84.6 14.4 %collective-permute-start.21 = (bf16[3,192,512]{2,1,0:T(8,128)(2,1)S(1)}, bf16[3,192,512]{2,1,0:T(8,128)(2,1)S(1)}, u32[]{:S(2)}, u32[]{:S(2)}) collective-permute-start(bf16[3,192,512]{2,1,0:T(8,128)(2,1)S(1)} %get-tuple-element.32), channel_id=1, source_target_pairs={{0,4},{4,0},{8,12},{12,8},{16,20},{20,16},{24,28},{28,24},{1,5},{5... | collective-permute-start | bytes 1769480 | tf_op jit(solution)/shard_map/ppermute | solution.py:645
  89.0 33.7 %collective-permute-start.24 = (bf16[192,2880]{1,0:T(8,128)(2,1)S(1)}, bf16[192,2880]{1,0:T(8,128)(2,1)S(1)}, u32[]{:S(2)}, u32[]{:S(2)}) collective-permute-start(bf16[192,2880]{1,0:T(8,128)(2,1)S(1)} %combine.11.refs_15_), channel_id=1, source_target_pairs={{0,8},{4,12},{8,0},{12,4},{16,24},{20,28},{24,16},{28,20},{1,9},{5... | collective-permute-start | bytes 3317768 | tf_op jit(solution)/shard_map/ppermute | solution.py:657
  93.9 25.1 %collective-permute-start.26 = (bf16[192,1472]{1,0:T(8,128)(2,1)S(1)}, bf16[192,1472]{1,0:T(8,128)(2,1)S(1)}, u32[]{:S(2)}, u32[]{:S(2)}) collective-permute-start(bf16[192,1472]{1,0:T(8,128)(2,1)S(1)} %combine.12), channel_id=1, source_target_pairs={{8,16},{12,20},{16,8},{20,12},{9,17},{13,21},{17,9},{21,13},{10,18... | collective-permute-start | bytes 1695752 | tf_op jit(solution)/shard_map/ppermute | solution.py:657
  100.2 18.8 %collective-permute-start.28 = (bf16[192,1408]{1,0:T(8,128)(2,1)S(1)}, bf16[192,1408]{1,0:T(8,128)(2,1)S(1)}, u32[]{:S(2)}, u32[]{:S(2)}) collective-permute-start(bf16[192,1408]{1,0:T(8,128)(2,1)S(1)} %hold.13), channel_id=1, source_target_pairs={{8,16},{12,20},{16,8},{20,12},{9,17},{13,21},{17,9},{21,13},{10,18... | collective-permute-start | bytes 1622024 | tf_op jit(solution)/shard_map/ppermute | solution.py:657
  105.4 10.7 %collective-permute-start.22 = (bf16[1,192,512]{2,1,0:T(8,128)(2,1)S(1)}, bf16[1,192,512]{2,1,0:T(8,128)(2,1)S(1)}, u32[]{:S(2)}, u32[]{:S(2)}) collective-permute-start(bf16[1,192,512]{2,1,0:T(8,128)(2,1)S(1)} %get-tuple-element.34), channel_id=1, source_target_pairs={{0,4},{4,0},{8,12},{12,8},{16,20},{20,16},{24,28},{28,24},{1,5},{5... | collective-permute-start | bytes 589832 | tf_op jit(solution)/shard_map/ppermute | solution.py:645
  107.4 8.7 %collective-permute-start.23 = (bf16[1,192,512]{2,1,0:T(8,128)(2,1)S(1)}, bf16[1,192,512]{2,1,0:T(8,128)(2,1)S(1)}, u32[]{:S(2)}, u32[]{:S(2)}) collective-permute-start(bf16[1,192,512]{2,1,0:T(8,128)(2,1)S(1)} %get-tuple-element.36), channel_id=1, source_target_pairs={{0,4},{4,0},{8,12},{12,8},{16,20},{20,16},{24,28},{28,24},{1,5},{5... | collective-permute-start | bytes 589832 | tf_op jit(solution)/shard_map/ppermute | solution.py:645
  (12 other events, 84.1 us)

commit v13 on v12

--- a/solution.py
+++ b/solution.py
@@ -10,13 +10,14 @@
 
 LANES = 128
 SCALE = 1_000_000
+ORDER_WEIGHT = 100
 FIRST_WEIGHT = 12_000
 NEXT_WEIGHT = 600
 HIDDEN_WEIGHT = 5_000
 PASS_WEIGHT = 1
 WAITED_WEIGHT = 210
 ENTER_WEIGHT = 575
-LEAVE_WEIGHT = 5_250
+LEAVE_WEIGHT = 5_300
 LAST_WEIGHT = 90
 NT = (((1,), (1,)), ((), ()))
 NN = (((1,), (0,)), ((), ()))
@@ -285,12 +286,12 @@
         scaled[here, :] = (block[:, : scaled.shape[1]].astype(f32) * gate).astype(bf16)
 
 
-def products_kernel(table, model, counts, places, shards, skip, middle, where_ref, *refs):
+def products_kernel(table, model, counts, places, shards, skip, where_it_runs, where_ref, *refs):
     used = sum(counts)
     rows = blocks_of(refs[: counts[0]], places[0])
     gated = blocks_of(refs[counts[0] : used], places[1])
     own_ref, other_ref = refs[used : used + 2]
-    kept_ref, scaled = refs[-2:]
+    kept_ref, scaled, total_ref, sem = refs[-4:]
     units, slots = own_ref.shape[1:]
 
     def stacked(ref, offset):
@@ -302,30 +303,44 @@
         total = dot(stacked(own_ref, skip), scaled[:slots, :], NN)
         total = total + dot(stacked(other_ref, 0), scaled[slots:, :], NN)
         for shard in range(shards):
-            kept_ref[shard] = total[shard * units : (shard + 1) * units]
-
-    if middle:
-        pl.when(where_ref[table["use", 2, "A"]] != 0)(work)
+            total_ref[shard] = total[shard * units : (shard + 1) * units]
+        copy = pltpu.make_async_copy(total_ref, kept_ref, sem)
+        copy.start()
+        copy.wait()
+
+    at_end = where_ref[table["use", 2, "A"]] == 0
+    if where_it_runs == "ends":
+        pl.when(at_end)(work)
+    elif where_it_runs == "middle":
+        pl.when(jnp.logical_not(at_end))(work)
     else:
         work()
 
 
-def products(table, where, rows, gated, own, other, skip, model, width, name, after, middle=False):
+def products(
+    table, where, rows, gated, own, other, skip, model, width, name, after, where_it_runs="all", before=None
+):
     arrays, places = zip(rows, gated)
     counts = [len(part) for part in arrays]
     shards, units, slots = other.shape
     kept = jax.ShapeDtypeStruct((shards, units, width), f32)
     operands = [*arrays[0], *arrays[1], own, other]
-    return pl.pallas_call(
-        functools.partial(products_kernel, table, model, counts, places, shards, skip, middle),
+    extra = ([] if before is None else [before]) + list(after)
+    return pl.pallas_call(
+        functools.partial(products_kernel, table, model, counts, places, shards, skip, where_it_runs),
         out_shape=kept,
-        in_specs=[scalars()] + [whole()] * len(operands) + [anywhere()] * len(after),
-        out_specs=whole(),
-        scratch_shapes=[pltpu.VMEM((2 * slots, width), bf16)],
+        in_specs=[scalars()] + [whole()] * len(operands) + [anywhere()] * len(extra),
+        out_specs=anywhere(),
+        scratch_shapes=[
+            pltpu.VMEM((2 * slots, width), bf16),
+            pltpu.VMEM(kept.shape, f32),
+            pltpu.SemaphoreType.DMA,
+        ],
+        input_output_aliases={} if before is None else {1 + len(operands): 0},
         compiler_params=params(),
         cost_estimate=taking(1),
         name=name,
-    )(where, *operands, *after)
+    )(where, *operands, *extra)
 
 
 def first_kernel(table, model, counts, places, start, where_ref, *refs):
@@ -672,6 +687,7 @@
         table, where, saved_hidden[0, 0], depth, w_down.shape[1], [late]
     )
     other_first = swap(other_first, 1, 0)
+    (late_x,) = hold((late_x,), [], ORDER_WEIGHT)
     (late_x,) = hold((late_x,), late_near[1:])
     late_mine = late_near + [late_x] + [swap(late_x, 0, high) for high in highs]
     (early,) = hold((early,), [late_x, other_first])
@@ -679,35 +695,38 @@
     late_rows = sides(pack(late_mine, [early_x]))
     late_rows = (late_rows, [(side, place) for place in range(experts) for side in range(2)])
     early_rows = sides(pack([early, early_x], []))
-    places = [(0, 0), (1, 0)]
-    for block, base in ((early, 0), (early_x, 1)):
-        if base:
-            places += [(0, 1), (1, 1)]
-        for high in highs:
-            places += [(len(early_rows), None), (len(early_rows) + 1, None)]
-            early_rows += sides(swap(block, 0, high))
-    early_rows = (early_rows, places)
+    early_far = [[swap(block, 0, high) for high in highs] for block in (early, early_x)]
     other_rest = swap(other_rest, 1, 0)
 
-    for name, value in zip("BA", hold([got[1, "B"][0], got[1, "A"][0]], [], FIRST_WEIGHT)):
-        got[1, name] = [value]
-    chunks = ((late_rows, cut, model - cut), (early_rows, 0, cut))
-    after = [early_rows[0][1]]
-    first = []
-    for rows, start, columns in chunks:
+    got[1, "A"] = list(hold(got[1, "A"], [], ORDER_WEIGHT))
+    got[1, "B"] = list(hold(got[1, "B"], got[1, "A"], FIRST_WEIGHT))
+    chunks, first = [], []
+
+    def first_chunk(rows, start, columns, after, before):
+        chunks.append((rows, start, columns))
         value = first_sums(
             table, where, rows, late_rows, own, other_first, got[1, "B"][0], model, start, columns, after
         )
-        if first:
-            (value,) = hold([value], got[2, "A"], NEXT_WEIGHT)
+        if before:
+            (value,) = hold([value], before, NEXT_WEIGHT)
         got.setdefault((2, "A"), []).append(swap_z(value, "A"))
         first.append(
             products(
-                table, where, rows, late_rows, own, other_first, 0, model, columns, "first_kept", [value], True
+                table, where, rows, late_rows, own, other_first, 0, model, columns, "first_kept", [value], "middle"
             )
         )
-        after = [first[0]]
-    marker = value
+        return value
+
+    first_chunk(late_rows, cut, model - cut, [early_rows[1]], [])
+    places = []
+    for base, blocks in enumerate(early_far):
+        places += [(0, base), (1, base)]
+        for block in hold(blocks, first):
+            places += [(len(early_rows), None), (len(early_rows) + 1, None)]
+            mine, theirs = sides(block)
+            early_rows += [mine, theirs if base else hold([theirs], [], ORDER_WEIGHT)[0]]
+    early_rows = (early_rows, places)
+    marker = first_chunk(early_rows, 0, cut, [first[0]], got[2, "A"])
     got[2, "B"] = [swap_z(got[1, "A"][0], "B")]
     (other_rest,) = hold([other_rest], [], HIDDEN_WEIGHT)
 
@@ -754,24 +773,27 @@
 
     rest = []
 
-    def other_products(chunk, after):
+    def other_products(chunk, after, *where_it_runs):
         rows, _, columns = chunks[chunk]
-        rest.append(
-            products(table, where, rows, late_rows, own, other_rest, 1, model, columns, "rest_kept", after)
+        return products(
+            table, where, rows, late_rows, own, other_rest, 1, model, columns, "rest_kept", after, *where_it_runs
         )
-        return rest[chunk]
 
     apart = max(uses[3, "B"]) <= 0 and depth == 4
     if apart:
         marker = pass_on(3, "B", [marker], 0)
-        for chunk in range(2):
-            marker = other_products(chunk, [marker])
-            marker = pass_on(3, "A", [marker], chunk)
-        forward(3, "A", [marker, first[1]])
+        rest.append(other_products(0, [marker]))
+        marker = pass_on(3, "A", rest, 0)
+        forward(3, "A", [marker])
+        rest.append(other_products(1, got[2, "B"], "ends"))
+        marker = pass_on(3, "A", rest, 1)
         marker = pass_on(3, "B", [marker], 1)
+        rest[1] = other_products(1, [marker], "middle", rest[1])
+        marker = rest[1]
     else:
-        marker = other_products(1, [other_products(0, [marker])])
-        marker = pass_on(3, "A", [marker])
+        rest.append(other_products(0, [marker]))
+        rest.append(other_products(1, rest))
+        marker = pass_on(3, "A", rest)
         for chunk in range(2):
             marker = pass_on(3, "B", [marker], chunk)
     sums = backprop([[(0, "own")], [(1, "A")], [(1, "B")]], None, False, got[2, "A"][:1])

time: 125 us -> 121 us (0.968)
  waiting for transfers between devices: 34 us -> 28.7 us
  Pallas kernels: 37.9 us -> 39.5 us
    ppermute x13, waiting for transfers between devices: 7.35 us -> 3.96 us  [swap_z(): return lax.ppermute(value, 'ctx', pairs)]
    ppermute x8, waiting for transfers between devices: 15.9 us -> 14.2 us  [swap(): return lax.ppermute(value, 'ctx', [(i, i ^ x) for i in range(groups)])]
    ppermute x13, starting transfers between devices: 27.8 us -> 26.1 us  [swap_z(): return lax.ppermute(value, 'ctx', pairs)]
    pallas_call x4 -> x5, Pallas kernels: 8.03 us -> 9.45 us  [products(): pl.pallas_call(functools.partial(products_kernel, table, model, counts, p...]
  transfers between devices with their start and end apart: 29 -> 29, of which waited for: 13 -> 12; matrix products, arithmetic and copies ran while one was open for 1% -> 1% of each run, Pallas kernels for 28% -> 30%
where the time goes in v13:
time: 121 us; the launch traced here: 120 us
  starting transfers between devices  40.8 us (34%)
  Pallas kernels  39.5 us (33%)
  waiting for transfers between devices  28.7 us (24%)
  blocking collectives  6.42 us (5%)
  local copies, waits for them, and re-layouts  3.12 us (3%)
    ppermute x13, starting transfers between devices, swap_z(): return lax.ppermute(value, 'ctx', pairs)  26.1 us
    ppermute x8, waiting for transfers between devices, swap(): return lax.ppermute(value, 'ctx', [(i, i ^ x) for i in range(groups)])  14.2 us
    ppermute x8, waiting for transfers between devices, swap(): return lax.ppermute(value, 'exp', [(i, i ^ exp) for i in range(experts)])  10.6 us
    pallas_call x3, Pallas kernels, back_part(): pl.pallas_call(functools.partial(back_kernel, table, model, cut, counts,...  10.2 us
    ppermute x8, starting transfers between devices, swap(): return lax.ppermute(value, 'ctx', [(i, i ^ x) for i in range(groups)])  10.1 us
    pallas_call x5, Pallas kernels, products(): pl.pallas_call(functools.partial(products_kernel, table, model, counts, p...  9.45 us
    all_to_all x1, blocking collectives, per_device_full(): lax.all_to_all(slot_grad.reshape(experts, tokens), 'exp', split_axis=0, c...  6.42 us
    pallas_call x7, Pallas kernels, combine(): pl.pallas_call(functools.partial(combine_kernel, table, ('use', turn, nam...  5.1 us
  transfers between devices with their start and end apart: 29, of which 12 were waited for; matrix products, arithmetic and copies ran while one was open for 1% of the time, Pallas kernels for 30%

profile of v13, /device:TPU:0, one launch (start us, length us, event | category | flops | bytes accessed | tf_op | source)
XLA Modules:
  0.0 119.7 jit_solution(16948691257208526704)
XLA Ops:
  0.6 2.2 %make_rows.1 = (bf16[128,1536]{1,0:T(8,128)(2,1)}, bf16[128,1408]{1,0:T(8,128)(2,1)}, f32[4,128]{1,0:T(4,128)}) custom-call(bf16[2880,128]{1,0:T(8,128)(2,1)} %bitcast.22, f32[4,128]{1,0:T(4,128)} %bitcast.23, s32[4,128]{1,0:T(4,128)} %bitcast.18), custom_call_target="tpu_custom_call" | custom-call | flops 2000000 | bytes 6000000 | tf_op jit(solution)/shard_map/make_rows/pallas_call | solution.py:168
  2.8 3.0 %collective-permute-start.1 = (bf16[128,1536]{1,0:T(8,128)(2,1)}, bf16[128,1536]{1,0:T(8,128)(2,1)S(1)}, u32[]{:S(2)}, u32[]{:S(2)}) collective-permute-start(bf16[128,1536]{1,0:T(8,128)(2,1)} %get-tuple-element.19.refs_0_), channel_id=1, source_target_pairs={{0,4},{4,0},{8,12},{12,8},{16,20},{20,16},{24,28},{28,24},{1,5},{5... | collective-permute-start | bytes 1179656 | tf_op jit(solution)/shard_map/ppermute | solution.py:660
  12.8 2.2 %split_hidden.1 = (bf16[4,192,512]{2,1,0:T(8,128)(2,1)S(1)}, bf16[1,192,512]{2,1,0:T(8,128)(2,1)S(1)}, bf16[3,192,512]{2,1,0:T(8,128)(2,1)S(1)}) custom-call(s32[32]{0:T(128)S(1)} %dynamic-slice_bitcast_fusion.where_ref, bf16[512,1536]{1,0:T(8,128)(2,1)S(1)} %bitcast.14, bf16[128,1536]{1,0:T(8,128)(2,1)S(1)} %copy-done.1), custom_call_target="tpu_custom_call" | custom-call | flops 2000000 | bytes 6000000 | tf_op jit(solution)/shard_map/split_hidden/pallas_call | solution.py:259
  18.1 2.7 %collective-permute-done.3.refs_2_.refs_5_.refs_9_ = bf16[1,192,512]{2,1,0:T(8,128)(2,1)S(1)} collective-permute-done((bf16[1,192,512]{2,1,0:T(8,128)(2,1)S(1)}, bf16[1,192,512]{2,1,0:T(8,128)(2,1)S(1)}, u32[]{:S(2)}, u32[]{:S(2)}) %collective-permute-start.3) | collective-permute-done | bytes 196640 | tf_op jit(solution)/shard_map/ppermute | solution.py:660
  21.4 7.8 %collective-permute-done.4.refs_4_.refs_1_ = bf16[128,1408]{1,0:T(8,128)(2,1)S(1)} collective-permute-done((bf16[128,1408]{1,0:T(8,128)(2,1)S(1)}, bf16[128,1408]{1,0:T(8,128)(2,1)S(1)}, u32[]{:S(2)}, u32[]{:S(2)}) %collective-permute-start.4) | collective-permute-done | bytes 360480 | tf_op jit(solution)/shard_map/ppermute | solution.py:660
  31.5 2.2 %collective-permute-done.9.refs_0_ = bf16[192,2880]{1,0:T(8,128)(2,1)S(1)} collective-permute-done((bf16[192,2880]{1,0:T(8,128)(2,1)}, bf16[192,2880]{1,0:T(8,128)(2,1)S(1)}, u32[]{:S(2)}, u32[]{:S(2)}) %collective-permute-start.9) | collective-permute-done | bytes 1105952 | tf_op jit(solution)/shard_map/ppermute | solution.py:672
  34.5 2.2 %first_sums.2.refs_6_ = bf16[192,1472]{1,0:T(8,128)(2,1)S(1)} custom-call(s32[32]{0:T(128)S(1)} %dynamic-slice_bitcast_fusion.where_ref, bf16[4,128,1536]{2,1,0:T(8,128)(2,1)S(1)} %pack_rows.2.refs_0_.refs_2_.refs_6_, bf16[4,128,1536]{2,1,0:T(8,128)(2,1)S(1)} %collective-permute-done.5.refs_1_.refs_3_.refs_7_, ...), custom_call_target="tpu_custom_call" | custom-call | flops 1000000 | bytes 3000000 | tf_op jit(solution)/shard_map/first_sums/pallas_call | solution.py:370
  36.7 2.5 %collective-permute-start.15 = (bf16[192,1472]{1,0:T(8,128)(2,1)S(1)}, bf16[192,1472]{1,0:T(8,128)(2,1)S(1)}, u32[]{:S(2)}, u32[]{:S(2)}) collective-permute-start(bf16[192,1472]{1,0:T(8,128)(2,1)S(1)} %first_sums.2.refs_6_), channel_id=1, source_target_pairs={{0,8},{4,12},{8,0},{12,4},{16,24},{20,28},{24,16},{28,20},{1,9},{5... | collective-permute-start | bytes 1695752 | tf_op jit(solution)/shard_map/ppermute | solution.py:672
  41.4 7.3 %collective-permute-done.11.refs_0_ = bf16[128,1408]{1,0:T(8,128)(2,1)S(1)} collective-permute-done((bf16[128,1408]{1,0:T(8,128)(2,1)S(1)}, bf16[128,1408]{1,0:T(8,128)(2,1)S(1)}, u32[]{:S(2)}, u32[]{:S(2)}) %collective-permute-start.11) | collective-permute-done | bytes 360480 | tf_op jit(solution)/shard_map/ppermute | solution.py:662
  50.3 2.1 %first_sums.3.refs_0_ = bf16[192,1408]{1,0:T(8,128)(2,1)S(1)} custom-call(s32[32]{0:T(128)S(1)} %dynamic-slice_bitcast_fusion.where_ref, bf16[2,128,1408]{2,1,0:T(8,128)(2,1)S(1)} %pack_rows.3.refs_0_.refs_2_, bf16[2,128,1408]{2,1,0:T(8,128)(2,1)S(1)} %collective-permute-done.6.refs_7_.refs_1_.refs_3_, bf16[128,1408]{1,0:T(8,128)(2,1)S(1)} %hold.17.refs_2_.refs_4_, ...), custom_call_target="tpu_custom_call" | custom-call | flops 1000000 | bytes 3000000 | tf_op jit(solution)/shard_map/first_sums/pallas_call | solution.py:370
  52.8 2.2 %collective-permute-start.18 = (bf16[192,1408]{1,0:T(8,128)(2,1)S(1)}, bf16[192,1408]{1,0:T(8,128)(2,1)S(1)}, u32[]{:S(2)}, u32[]{:S(2)}) collective-permute-start(bf16[192,1408]{1,0:T(8,128)(2,1)S(1)} %hold.21.refs_2_.refs_10_), channel_id=1, source_target_pairs={{0,8},{4,12},{8,0},{12,4},{16,24},{20,28},{24,16},{28,20},{1,9},{5... | collective-permute-start | bytes 1622024 | tf_op jit(solution)/shard_map/ppermute | solution.py:672
  56.5 3.9 %rest_kept.3.refs_0_.refs_1_.refs_2_.refs_3_ = f32[3,192,1472]{2,1,0:T(8,128)S(1)} custom-call(s32[32]{0:T(128)S(1)} %dynamic-slice_bitcast_fusion.where_ref, bf16[4,128,1536]{2,1,0:T(8,128)(2,1)S(1)} %pack_rows.2.refs_0_.refs_2_.refs_6_, bf16[4,128,1536]{2,1,0:T(8,128)(2,1)S(1)} %collective-permute-done.5.refs_1_.refs_3_.refs_7_, ...), custom_call_target="tpu_custom_call" | custom-call | flops 1000000 | bytes 3000000 | tf_op jit(solution)/shard_map/rest_kept/pallas_call | solution.py:329
  61.1 4.9 %collective-permute-start.25 = (bf16[192,1472]{1,0:T(8,128)(2,1)S(1)}, bf16[192,1472]{1,0:T(8,128)(2,1)S(1)}, u32[]{:S(2)}, u32[]{:S(2)}) collective-permute-start(bf16[192,1472]{1,0:T(8,128)(2,1)S(1)} %combine.8.refs_1_), channel_id=1, source_target_pairs={{0,8},{4,12},{24,16},{28,20},{1,9},{5,13},{25,17},{29,21},{2,10},{... | collective-permute-start | bytes 1695752 | tf_op jit(solution)/shard_map/ppermute | solution.py:672
  67.2 3.9 %rest_kept.4.refs_0_.refs_2_.refs_10_ = f32[3,192,1408]{2,1,0:T(8,128)S(1)} custom-call(s32[32]{0:T(128)S(1)} %dynamic-slice_bitcast_fusion.where_ref, bf16[2,128,1408]{2,1,0:T(8,128)(2,1)S(1)} %pack_rows.3.refs_0_.refs_2_, bf16[2,128,1408]{2,1,0:T(8,128)(2,1)S(1)} %collective-permute-done.6.refs_7_.refs_1_.refs_3_, ...), custom_call_target="tpu_custom_call" | custom-call | flops 1000000 | bytes 3000000 | tf_op jit(solution)/shard_map/rest_kept/pallas_call | solution.py:329
  73.9 6.7 %collective-permute-start.27 = (bf16[192,1408]{1,0:T(8,128)(2,1)S(1)}, bf16[192,1408]{1,0:T(8,128)(2,1)S(1)}, u32[]{:S(2)}, u32[]{:S(2)}) collective-permute-start(bf16[192,1408]{1,0:T(8,128)(2,1)S(1)} %combine.9.refs_2_), channel_id=1, source_target_pairs={{0,8},{4,12},{24,16},{28,20},{1,9},{5,13},{25,17},{29,21},{2,10},{... | collective-permute-start | bytes 1622024 | tf_op jit(solution)/shard_map/ppermute | solution.py:672
  80.6 4.7 %back_part.3 = (bf16[3,192,512]{2,1,0:T(8,128)(2,1)S(1)}, bf16[3,192,512]{2,1,0:T(8,128)(2,1)S(1)}, f32[8,1024]{1,0:T(8,128)S(1)}) custom-call(s32[32]{0:T(128)S(1)} %dynamic-slice_bitcast_fusion.where_ref, bf16[4,128,1536]{2,1,0:T(8,128)(2,1)S(1)} %pack_rows.2.refs_0_.refs_2_.refs_6_, ...), custom_call_target="tpu_custom_call" | custom-call | flops 6000000 | bytes 18000000 | tf_op jit(solution)/shard_map/back_part/pallas_call | solution.py:569
  87.4 2.6 %back_part.4 = (bf16[1,192,512]{2,1,0:T(8,128)(2,1)S(1)}, bf16[1,192,512]{2,1,0:T(8,128)(2,1)S(1)}, f32[8,1024]{1,0:T(8,128)S(1)}) custom-call(s32[32]{0:T(128)S(1)} %dynamic-slice_bitcast_fusion.where_ref, bf16[4,128,1536]{2,1,0:T(8,128)(2,1)S(1)} %pack_rows.2.refs_0_.refs_2_.refs_6_, ...), custom_call_target="tpu_custom_call" | custom-call | flops 6000000 | bytes 18000000 | tf_op jit(solution)/shard_map/back_part/pallas_call | solution.py:569
  90.9 2.6 %collective-permute-start.24 = (bf16[192,2880]{1,0:T(8,128)(2,1)S(1)}, bf16[192,2880]{1,0:T(8,128)(2,1)S(1)}, u32[]{:S(2)}, u32[]{:S(2)}) collective-permute-start(bf16[192,2880]{1,0:T(8,128)(2,1)S(1)} %combine.11.refs_15_), channel_id=1, source_target_pairs={{0,8},{4,12},{8,0},{12,4},{16,24},{20,28},{24,16},{28,20},{1,9},{5... | collective-permute-start | bytes 3317768 | tf_op jit(solution)/shard_map/ppermute | solution.py:672
  95.6 2.0 %collective-permute-done.21.refs_1_.refs_2_ = bf16[3,192,512]{2,1,0:T(8,128)(2,1)S(1)} collective-permute-done((bf16[3,192,512]{2,1,0:T(8,128)(2,1)S(1)}, bf16[3,192,512]{2,1,0:T(8,128)(2,1)S(1)}, u32[]{:S(2)}, u32[]{:S(2)}) %collective-permute-start.21) | collective-permute-done | bytes 589856 | tf_op jit(solution)/shard_map/ppermute | solution.py:660
  98.5 2.9 %back_part.5 = (bf16[1,192,512]{2,1,0:T(8,128)(2,1)S(1)}, bf16[1,192,512]{2,1,0:T(8,128)(2,1)S(1)}, f32[8,1024]{1,0:T(8,128)S(1)}) custom-call(s32[32]{0:T(128)S(1)} %dynamic-slice_bitcast_fusion.where_ref, bf16[4,128,1536]{2,1,0:T(8,128)(2,1)S(1)} %pack_rows.2.refs_0_.refs_2_.refs_6_, ...), custom_call_target="tpu_custom_call" | custom-call | flops 6000000 | bytes 18000000 | tf_op jit(solution)/shard_map/back_part/pallas_call | solution.py:569
  101.3 1.8 %collective-permute-start.20 = (f32[1,512]{1,0:T(1,128)S(1)}, f32[1,512]{1,0:T(1,128)S(1)}, u32[]{:S(2)}, u32[]{:S(2)}) collective-permute-start(f32[1,512]{1,0:T(1,128)S(1)} %slice.7), channel_id=1, source_target_pairs={{0,4},{4,0},{8,12},{12,8},{16,20},{20,16},{24,28},{28,24},{1,5},{5... | collective-permute-start | bytes 6152 | tf_op jit(solution)/shard_map/ppermute | solution.py:660
  105.1 1.7 %collective-permute-start.23 = (bf16[1,192,512]{2,1,0:T(8,128)(2,1)S(1)}, bf16[1,192,512]{2,1,0:T(8,128)(2,1)S(1)}, u32[]{:S(2)}, u32[]{:S(2)}) collective-permute-start(bf16[1,192,512]{2,1,0:T(8,128)(2,1)S(1)} %get-tuple-element.32), channel_id=1, source_target_pairs={{0,4},{4,0},{8,12},{12,8},{16,20},{20,16},{24,28},{28,24},{1,5},{5... | collective-permute-start | bytes 589832 | tf_op jit(solution)/shard_map/ppermute | solution.py:660
  106.8 6.4 %all_to_all.11 = f32[4,1,128]{2,1,0:T(1,128)S(1)} all-to-all(f32[4,1,128]{2,1,0:T(1,128)S(1)} %add_bitcast_fusion), channel_id=1, replica_groups=mesh['ctx'=8,'exp'=4] {'exp'}, dimensions={0} | all-to-all | bytes 4096 | tf_op jit(solution)/shard_map/all_to_all | solution.py:814
  113.8 2.9 %join_hidden.1 = bf16[512,1536]{1,0:T(8,128)(2,1)} custom-call(s32[32]{0:T(128)S(1)} %dynamic-slice_bitcast_fusion.where_ref, bf16[3,192,512]{2,1,0:T(8,128)(2,1)S(1)} %get-tuple-element.27.refs_0_, bf16[3,192,512]{2,1,0:T(8,128)(2,1)S(1)} %collective-permute-done.21.refs_1_.refs_2_, bf16[1,192,512]{2,1,0:T(8,128)(2,1)S(1)} %get-tuple-element.29.refs_2_, ...), custom_call_target="tpu_custom_call" | custom-call | flops 2000000 | bytes 6000000 | tf_op jit(solution)/shard_map/join_hidden/pallas_call | solution.py:611
  (88 shorter events, 35.4 us)
Async XLA Ops:
  2.8 12.8 %collective-permute-start.1 = (bf16[128,1536]{1,0:T(8,128)(2,1)}, bf16[128,1536]{1,0:T(8,128)(2,1)S(1)}, u32[]{:S(2)}, u32[]{:S(2)}) collective-permute-start(bf16[128,1536]{1,0:T(8,128)(2,1)} %get-tuple-element.19.refs_0_), channel_id=1, source_target_pairs={{0,4},{4,0},{8,12},{12,8},{16,20},{20,16},{24,28},{28,24},{1,5},{5... | collective-permute-start | bytes 1179656 | tf_op jit(solution)/shard_map/ppermute | solution.py:660
  5.8 10.8 %collective-permute-start = (bf16[128,1536]{1,0:T(8,128)(2,1)}, bf16[128,1536]{1,0:T(8,128)(2,1)S(1)}, u32[]{:S(2)}, u32[]{:S(2)}) collective-permute-start(bf16[128,1536]{1,0:T(8,128)(2,1)} %get-tuple-element.19.refs_0_), channel_id=1, source_target_pairs={{0,2},{1,3},{2,0},{3,1},{4,6},{5,7},{6,4},{7,5},{8,10},{9,11},{10,... | collective-permute-start | bytes 1179656 | tf_op jit(solution)/shard_map/ppermute | solution.py:662
  7.4 26.3 %collective-permute-start.9 = (bf16[192,2880]{1,0:T(8,128)(2,1)}, bf16[192,2880]{1,0:T(8,128)(2,1)S(1)}, u32[]{:S(2)}, u32[]{:S(2)}) collective-permute-start(bf16[192,2880]{1,0:T(8,128)(2,1)} %bitcast.15), channel_id=1, source_target_pairs={{0,8},{4,12},{8,0},{12,4},{16,24},{20,28},{24,16},{28,20},{1,9},{5... | collective-permute-start | bytes 3317768 | tf_op jit(solution)/shard_map/ppermute | solution.py:672
  8.9 25.2 %collective-permute-start.8 = (bf16[192,2880]{1,0:T(8,128)(2,1)}, bf16[192,2880]{1,0:T(8,128)(2,1)S(1)}, u32[]{:S(2)}, u32[]{:S(2)}) collective-permute-start(bf16[192,2880]{1,0:T(8,128)(2,1)} %bitcast.16), channel_id=1, source_target_pairs={{8,16},{12,20},{16,8},{20,12},{9,17},{13,21},{17,9},{21,13},{10,18... | collective-permute-start | bytes 3317768 | tf_op jit(solution)/shard_map/ppermute | solution.py:672
  16.6 12.6 %collective-permute-start.2 = (bf16[128,1536]{1,0:T(8,128)(2,1)S(1)}, bf16[128,1536]{1,0:T(8,128)(2,1)S(1)}, u32[]{:S(2)}, u32[]{:S(2)}) collective-permute-start(bf16[128,1536]{1,0:T(8,128)(2,1)S(1)} %hold.13.refs_1_.refs_2_), channel_id=1, source_target_pairs={{0,2},{1,3},{2,0},{3,1},{4,6},{5,7},{6,4},{7,5},{8,10},{9,11},{10,... | collective-permute-start | bytes 1179656 | tf_op jit(solution)/shard_map/ppermute | solution.py:662
  20.9 8.4 %collective-permute-start.4 = (bf16[128,1408]{1,0:T(8,128)(2,1)S(1)}, bf16[128,1408]{1,0:T(8,128)(2,1)S(1)}, u32[]{:S(2)}, u32[]{:S(2)}) collective-permute-start(bf16[128,1408]{1,0:T(8,128)(2,1)S(1)} %hold.14.refs_0_), channel_id=1, source_target_pairs={{0,4},{4,0},{8,12},{12,8},{16,20},{20,16},{24,28},{28,24},{1,5},{5... | collective-permute-start | bytes 1081352 | tf_op jit(solution)/shard_map/ppermute | solution.py:660
  30.1 11.3 %collective-permute-start.7 = (bf16[128,1408]{1,0:T(8,128)(2,1)S(1)}, bf16[128,1408]{1,0:T(8,128)(2,1)S(1)}, u32[]{:S(2)}, u32[]{:S(2)}) collective-permute-start(bf16[128,1408]{1,0:T(8,128)(2,1)S(1)} %hold.14.refs_0_), channel_id=1, source_target_pairs={{0,2},{1,3},{2,0},{3,1},{4,6},{5,7},{6,4},{7,5},{8,10},{9,11},{10,... | collective-permute-start | bytes 1081352 | tf_op jit(solution)/shard_map/ppermute | solution.py:662
  33.7 15.0 %collective-permute-start.11 = (bf16[128,1408]{1,0:T(8,128)(2,1)S(1)}, bf16[128,1408]{1,0:T(8,128)(2,1)S(1)}, u32[]{:S(2)}, u32[]{:S(2)}) collective-permute-start(bf16[128,1408]{1,0:T(8,128)(2,1)S(1)} %collective-permute-done.4.refs_4_.refs_1_), channel_id=1, source_target_pairs={{0,2},{1,3},{2,0},{3,1},{4,6},{5,7},{6,4},{7,5},{8,10},{9,11},{10,... | collective-permute-start | bytes 1081352 | tf_op jit(solution)/shard_map/ppermute | solution.py:662
  36.7 16.1 %collective-permute-start.15 = (bf16[192,1472]{1,0:T(8,128)(2,1)S(1)}, bf16[192,1472]{1,0:T(8,128)(2,1)S(1)}, u32[]{:S(2)}, u32[]{:S(2)}) collective-permute-start(bf16[192,1472]{1,0:T(8,128)(2,1)S(1)} %first_sums.2.refs_6_), channel_id=1, source_target_pairs={{0,8},{4,12},{8,0},{12,4},{16,24},{20,28},{24,16},{28,20},{1,9},{5... | collective-permute-start | bytes 1695752 | tf_op jit(solution)/shard_map/ppermute | solution.py:672
  39.2 26.7 %collective-permute-start.14 = (bf16[192,2880]{1,0:T(8,128)(2,1)S(1)}, bf16[192,2880]{1,0:T(8,128)(2,1)S(1)}, u32[]{:S(2)}, u32[]{:S(2)}) collective-permute-start(bf16[192,2880]{1,0:T(8,128)(2,1)S(1)} %hold.15.refs_1_.refs_12_), channel_id=1, source_target_pairs={{8,16},{12,20},{16,8},{20,12},{9,17},{13,21},{17,9},{21,13},{10,18... | collective-permute-start | bytes 3317768 | tf_op jit(solution)/shard_map/ppermute | solution.py:672
  39.9 16.5 %collective-permute-start.13 = (bf16[3,192,512]{2,1,0:T(8,128)(2,1)S(1)}, bf16[3,192,512]{2,1,0:T(8,128)(2,1)S(1)}, u32[]{:S(2)}, u32[]{:S(2)}) collective-permute-start(bf16[3,192,512]{2,1,0:T(8,128)(2,1)S(1)} %get-tuple-element.23), channel_id=1, source_target_pairs={{0,4},{4,0},{8,12},{12,8},{16,20},{20,16},{24,28},{28,24},{1,5},{5... | collective-permute-start | bytes 1769480 | tf_op jit(solution)/shard_map/ppermute | solution.py:660
  41.4 7.3 %collective-permute-start.10 = (bf16[128,1408]{1,0:T(8,128)(2,1)S(1)}, bf16[128,1408]{1,0:T(8,128)(2,1)S(1)}, u32[]{:S(2)}, u32[]{:S(2)}) collective-permute-start(bf16[128,1408]{1,0:T(8,128)(2,1)S(1)} %hold.17.refs_2_.refs_4_), channel_id=1, source_target_pairs={{0,1},{1,0},{2,3},{3,2},{4,5},{5,4},{6,7},{7,6},{8,9},{9,8},{10,11... | collective-permute-start | bytes 1081352 | tf_op jit(solution)/shard_map/ppermute | solution.py:662
  52.8 19.6 %collective-permute-start.18 = (bf16[192,1408]{1,0:T(8,128)(2,1)S(1)}, bf16[192,1408]{1,0:T(8,128)(2,1)S(1)}, u32[]{:S(2)}, u32[]{:S(2)}) collective-permute-start(bf16[192,1408]{1,0:T(8,128)(2,1)S(1)} %hold.21.refs_2_.refs_10_), channel_id=1, source_target_pairs={{0,8},{4,12},{8,0},{12,4},{16,24},{20,28},{24,16},{28,20},{1,9},{5... | collective-permute-start | bytes 1622024 | tf_op jit(solution)/shard_map/ppermute | solution.py:672
  55.7 29.6 %collective-permute-start.17 = (bf16[192,1472]{1,0:T(8,128)(2,1)S(1)}, bf16[192,1472]{1,0:T(8,128)(2,1)S(1)}, u32[]{:S(2)}, u32[]{:S(2)}) collective-permute-start(bf16[192,1472]{1,0:T(8,128)(2,1)S(1)} %combine.7.refs_6_), channel_id=1, source_target_pairs={{8,16},{12,20},{16,8},{20,12},{9,17},{13,21},{17,9},{21,13},{10,18... | collective-permute-start | bytes 1695752 | tf_op jit(solution)/shard_map/ppermute | solution.py:672
  61.1 32.4 %collective-permute-start.25 = (bf16[192,1472]{1,0:T(8,128)(2,1)S(1)}, bf16[192,1472]{1,0:T(8,128)(2,1)S(1)}, u32[]{:S(2)}, u32[]{:S(2)}) collective-permute-start(bf16[192,1472]{1,0:T(8,128)(2,1)S(1)} %combine.8.refs_1_), channel_id=1, source_target_pairs={{0,8},{4,12},{24,16},{28,20},{1,9},{5,13},{25,17},{29,21},{2,10},{... | collective-permute-start | bytes 1695752 | tf_op jit(solution)/shard_map/ppermute | solution.py:672
  65.9 31.7 %collective-permute-start.16 = (bf16[192,2880]{1,0:T(8,128)(2,1)S(1)}, bf16[192,2880]{1,0:T(8,128)(2,1)S(1)}, u32[]{:S(2)}, u32[]{:S(2)}) collective-permute-start(bf16[192,2880]{1,0:T(8,128)(2,1)S(1)} %hold.22.refs_10_.refs_13_), channel_id=1, source_target_pairs={{8,0},{12,4},{16,24},{20,28},{9,1},{13,5},{17,25},{21,29},{10,2},{... | collective-permute-start | bytes 3317768 | tf_op jit(solution)/shard_map/ppermute | solution.py:672
  73.2 16.8 %collective-permute-start.19 = (bf16[192,1408]{1,0:T(8,128)(2,1)S(1)}, bf16[192,1408]{1,0:T(8,128)(2,1)S(1)}, u32[]{:S(2)}, u32[]{:S(2)}) collective-permute-start(bf16[192,1408]{1,0:T(8,128)(2,1)S(1)} %combine.10.refs_11_), channel_id=1, source_target_pairs={{8,16},{12,20},{16,8},{20,12},{9,17},{13,21},{17,9},{21,13},{10,18... | collective-permute-start | bytes 1622024 | tf_op jit(solution)/shard_map/ppermute | solution.py:672
  73.9 21.0 %collective-permute-start.27 = (bf16[192,1408]{1,0:T(8,128)(2,1)S(1)}, bf16[192,1408]{1,0:T(8,128)(2,1)S(1)}, u32[]{:S(2)}, u32[]{:S(2)}) collective-permute-start(bf16[192,1408]{1,0:T(8,128)(2,1)S(1)} %combine.9.refs_2_), channel_id=1, source_target_pairs={{0,8},{4,12},{24,16},{28,20},{1,9},{5,13},{25,17},{29,21},{2,10},{... | collective-permute-start | bytes 1622024 | tf_op jit(solution)/shard_map/ppermute | solution.py:672
  85.3 12.3 %collective-permute-start.21 = (bf16[3,192,512]{2,1,0:T(8,128)(2,1)S(1)}, bf16[3,192,512]{2,1,0:T(8,128)(2,1)S(1)}, u32[]{:S(2)}, u32[]{:S(2)}) collective-permute-start(bf16[3,192,512]{2,1,0:T(8,128)(2,1)S(1)} %get-tuple-element.28), channel_id=1, source_target_pairs={{0,4},{4,0},{8,12},{12,8},{16,20},{20,16},{24,28},{28,24},{1,5},{5... | collective-permute-start | bytes 1769480 | tf_op jit(solution)/shard_map/ppermute | solution.py:660
  90.9 27.3 %collective-permute-start.24 = (bf16[192,2880]{1,0:T(8,128)(2,1)S(1)}, bf16[192,2880]{1,0:T(8,128)(2,1)S(1)}, u32[]{:S(2)}, u32[]{:S(2)}) collective-permute-start(bf16[192,2880]{1,0:T(8,128)(2,1)S(1)} %combine.11.refs_15_), channel_id=1, source_target_pairs={{0,8},{4,12},{8,0},{12,4},{16,24},{20,28},{24,16},{28,20},{1,9},{5... | collective-permute-start | bytes 3317768 | tf_op jit(solution)/shard_map/ppermute | solution.py:672
  94.2 22.5 %collective-permute-start.26 = (bf16[192,1472]{1,0:T(8,128)(2,1)S(1)}, bf16[192,1472]{1,0:T(8,128)(2,1)S(1)}, u32[]{:S(2)}, u32[]{:S(2)}) collective-permute-start(bf16[192,1472]{1,0:T(8,128)(2,1)S(1)} %combine.12), channel_id=1, source_target_pairs={{8,16},{12,20},{16,8},{20,12},{9,17},{13,21},{17,9},{21,13},{10,18... | collective-permute-start | bytes 1695752 | tf_op jit(solution)/shard_map/ppermute | solution.py:672
  97.6 19.1 %collective-permute-start.28 = (bf16[192,1408]{1,0:T(8,128)(2,1)S(1)}, bf16[192,1408]{1,0:T(8,128)(2,1)S(1)}, u32[]{:S(2)}, u32[]{:S(2)}) collective-permute-start(bf16[192,1408]{1,0:T(8,128)(2,1)S(1)} %hold.23), channel_id=1, source_target_pairs={{8,16},{12,20},{16,8},{20,12},{9,17},{13,21},{17,9},{21,13},{10,18... | collective-permute-start | bytes 1622024 | tf_op jit(solution)/shard_map/ppermute | solution.py:672
  103.2 10.7 %collective-permute-start.22 = (bf16[1,192,512]{2,1,0:T(8,128)(2,1)S(1)}, bf16[1,192,512]{2,1,0:T(8,128)(2,1)S(1)}, u32[]{:S(2)}, u32[]{:S(2)}) collective-permute-start(bf16[1,192,512]{2,1,0:T(8,128)(2,1)S(1)} %get-tuple-element.30), channel_id=1, source_target_pairs={{0,4},{4,0},{8,12},{12,8},{16,20},{20,16},{24,28},{28,24},{1,5},{5... | collective-permute-start | bytes 589832 | tf_op jit(solution)/shard_map/ppermute | solution.py:660
  105.1 8.8 %collective-permute-start.23 = (bf16[1,192,512]{2,1,0:T(8,128)(2,1)S(1)}, bf16[1,192,512]{2,1,0:T(8,128)(2,1)S(1)}, u32[]{:S(2)}, u32[]{:S(2)}) collective-permute-start(bf16[1,192,512]{2,1,0:T(8,128)(2,1)S(1)} %get-tuple-element.32), channel_id=1, source_target_pairs={{0,4},{4,0},{8,12},{12,8},{16,20},{20,16},{24,28},{28,24},{1,5},{5... | collective-permute-start | bytes 589832 | tf_op jit(solution)/shard_map/ppermute | solution.py:660
  (12 other events, 80.4 us)

commit v14 on v13

--- a/solution.py
+++ b/solution.py
@@ -784,7 +784,7 @@
         marker = pass_on(3, "B", [marker], 0)
         rest.append(other_products(0, [marker]))
         marker = pass_on(3, "A", rest, 0)
-        forward(3, "A", [marker])
+        forward(3, "A", [marker, first[1]])
         rest.append(other_products(1, got[2, "B"], "ends"))
         marker = pass_on(3, "A", rest, 1)
         marker = pass_on(3, "B", [marker], 1)

time: 121 us -> 121 us (level)
    ppermute x13, waiting for transfers between devices: 3.96 us -> 6.64 us  [swap_z(): return lax.ppermute(value, 'ctx', pairs)]
    ppermute x8, waiting for transfers between devices: 14.2 us -> 12.5 us  [swap(): return lax.ppermute(value, 'ctx', [(i, i ^ x) for i in range(groups)])]
where the time goes in v14:
time: 121 us; the launch traced here: 120 us
  starting transfers between devices  40.6 us (34%)
  Pallas kernels  39.3 us (32%)
  waiting for transfers between devices  29.7 us (25%)
  blocking collectives  6.41 us (5%)
  local copies, waits for them, and re-layouts  3.12 us (3%)
    ppermute x13, starting transfers between devices, swap_z(): return lax.ppermute(value, 'ctx', pairs)  25.8 us
    ppermute x8, waiting for transfers between devices, swap(): return lax.ppermute(value, 'ctx', [(i, i ^ x) for i in range(groups)])  12.5 us
    ppermute x8, waiting for transfers between devices, swap(): return lax.ppermute(value, 'exp', [(i, i ^ exp) for i in range(experts)])  10.6 us
    ppermute x8, starting transfers between devices, swap(): return lax.ppermute(value, 'ctx', [(i, i ^ x) for i in range(groups)])  10.2 us
    pallas_call x3, Pallas kernels, back_part(): pl.pallas_call(functools.partial(back_kernel, table, model, cut, counts,...  9.98 us
    pallas_call x5, Pallas kernels, products(): pl.pallas_call(functools.partial(products_kernel, table, model, counts, p...  9.45 us
    ppermute x13, waiting for transfers between devices, swap_z(): return lax.ppermute(value, 'ctx', pairs)  6.64 us
    all_to_all x1, blocking collectives, per_device_full(): lax.all_to_all(slot_grad.reshape(experts, tokens), 'exp', split_axis=0, c...  6.41 us
  transfers between devices with their start and end apart: 29, of which 12 were waited for; matrix products, arithmetic and copies ran while one was open for 1% of the time, Pallas kernels for 30%

profile of v14, /device:TPU:0, one launch (start us, length us, event | category | flops | bytes accessed | tf_op | source)
XLA Modules:
  0.0 120.3 jit_solution(6048694146036012941)
XLA Ops:
  0.6 2.2 %make_rows.1 = (bf16[128,1536]{1,0:T(8,128)(2,1)}, bf16[128,1408]{1,0:T(8,128)(2,1)}, f32[4,128]{1,0:T(4,128)}) custom-call(bf16[2880,128]{1,0:T(8,128)(2,1)} %bitcast.22, f32[4,128]{1,0:T(4,128)} %bitcast.23, s32[4,128]{1,0:T(4,128)} %bitcast.18), custom_call_target="tpu_custom_call" | custom-call | flops 2000000 | bytes 6000000 | tf_op jit(solution)/shard_map/make_rows/pallas_call | solution.py:168
  2.8 3.0 %collective-permute-start.1 = (bf16[128,1536]{1,0:T(8,128)(2,1)}, bf16[128,1536]{1,0:T(8,128)(2,1)S(1)}, u32[]{:S(2)}, u32[]{:S(2)}) collective-permute-start(bf16[128,1536]{1,0:T(8,128)(2,1)} %get-tuple-element.19.refs_0_), channel_id=1, source_target_pairs={{0,4},{4,0},{8,12},{12,8},{16,20},{20,16},{24,28},{28,24},{1,5},{5... | collective-permute-start | bytes 1179656 | tf_op jit(solution)/shard_map/ppermute | solution.py:660
  12.8 2.2 %split_hidden.1 = (bf16[4,192,512]{2,1,0:T(8,128)(2,1)S(1)}, bf16[1,192,512]{2,1,0:T(8,128)(2,1)S(1)}, bf16[3,192,512]{2,1,0:T(8,128)(2,1)S(1)}) custom-call(s32[32]{0:T(128)S(1)} %dynamic-slice_bitcast_fusion.where_ref, bf16[512,1536]{1,0:T(8,128)(2,1)S(1)} %bitcast.14, bf16[128,1536]{1,0:T(8,128)(2,1)S(1)} %copy-done.1), custom_call_target="tpu_custom_call" | custom-call | flops 2000000 | bytes 6000000 | tf_op jit(solution)/shard_map/split_hidden/pallas_call | solution.py:259
  18.1 2.7 %collective-permute-done.3.refs_2_.refs_5_.refs_9_ = bf16[1,192,512]{2,1,0:T(8,128)(2,1)S(1)} collective-permute-done((bf16[1,192,512]{2,1,0:T(8,128)(2,1)S(1)}, bf16[1,192,512]{2,1,0:T(8,128)(2,1)S(1)}, u32[]{:S(2)}, u32[]{:S(2)}) %collective-permute-start.3) | collective-permute-done | bytes 196640 | tf_op jit(solution)/shard_map/ppermute | solution.py:660
  21.4 7.8 %collective-permute-done.4.refs_4_.refs_1_ = bf16[128,1408]{1,0:T(8,128)(2,1)S(1)} collective-permute-done((bf16[128,1408]{1,0:T(8,128)(2,1)S(1)}, bf16[128,1408]{1,0:T(8,128)(2,1)S(1)}, u32[]{:S(2)}, u32[]{:S(2)}) %collective-permute-start.4) | collective-permute-done | bytes 360480 | tf_op jit(solution)/shard_map/ppermute | solution.py:660
  31.5 2.2 %collective-permute-done.9.refs_0_ = bf16[192,2880]{1,0:T(8,128)(2,1)S(1)} collective-permute-done((bf16[192,2880]{1,0:T(8,128)(2,1)}, bf16[192,2880]{1,0:T(8,128)(2,1)S(1)}, u32[]{:S(2)}, u32[]{:S(2)}) %collective-permute-start.9) | collective-permute-done | bytes 1105952 | tf_op jit(solution)/shard_map/ppermute | solution.py:672
  34.5 2.2 %first_sums.2.refs_6_ = bf16[192,1472]{1,0:T(8,128)(2,1)S(1)} custom-call(s32[32]{0:T(128)S(1)} %dynamic-slice_bitcast_fusion.where_ref, bf16[4,128,1536]{2,1,0:T(8,128)(2,1)S(1)} %pack_rows.2.refs_0_.refs_2_.refs_6_, bf16[4,128,1536]{2,1,0:T(8,128)(2,1)S(1)} %collective-permute-done.5.refs_1_.refs_3_.refs_7_, ...), custom_call_target="tpu_custom_call" | custom-call | flops 1000000 | bytes 3000000 | tf_op jit(solution)/shard_map/first_sums/pallas_call | solution.py:370
  36.7 2.5 %collective-permute-start.15 = (bf16[192,1472]{1,0:T(8,128)(2,1)S(1)}, bf16[192,1472]{1,0:T(8,128)(2,1)S(1)}, u32[]{:S(2)}, u32[]{:S(2)}) collective-permute-start(bf16[192,1472]{1,0:T(8,128)(2,1)S(1)} %first_sums.2.refs_6_), channel_id=1, source_target_pairs={{0,8},{4,12},{8,0},{12,4},{16,24},{20,28},{24,16},{28,20},{1,9},{5... | collective-permute-start | bytes 1695752 | tf_op jit(solution)/shard_map/ppermute | solution.py:672
  41.4 7.3 %collective-permute-done.11.refs_0_ = bf16[128,1408]{1,0:T(8,128)(2,1)S(1)} collective-permute-done((bf16[128,1408]{1,0:T(8,128)(2,1)S(1)}, bf16[128,1408]{1,0:T(8,128)(2,1)S(1)}, u32[]{:S(2)}, u32[]{:S(2)}) %collective-permute-start.11) | collective-permute-done | bytes 360480 | tf_op jit(solution)/shard_map/ppermute | solution.py:662
  50.3 2.1 %first_sums.3.refs_0_ = bf16[192,1408]{1,0:T(8,128)(2,1)S(1)} custom-call(s32[32]{0:T(128)S(1)} %dynamic-slice_bitcast_fusion.where_ref, bf16[2,128,1408]{2,1,0:T(8,128)(2,1)S(1)} %pack_rows.3.refs_0_.refs_2_, bf16[2,128,1408]{2,1,0:T(8,128)(2,1)S(1)} %collective-permute-done.6.refs_7_.refs_1_.refs_3_, bf16[128,1408]{1,0:T(8,128)(2,1)S(1)} %hold.17.refs_2_.refs_4_, ...), custom_call_target="tpu_custom_call" | custom-call | flops 1000000 | bytes 3000000 | tf_op jit(solution)/shard_map/first_sums/pallas_call | solution.py:370
  52.8 2.2 %collective-permute-start.18 = (bf16[192,1408]{1,0:T(8,128)(2,1)S(1)}, bf16[192,1408]{1,0:T(8,128)(2,1)S(1)}, u32[]{:S(2)}, u32[]{:S(2)}) collective-permute-start(bf16[192,1408]{1,0:T(8,128)(2,1)S(1)} %hold.21.refs_2_.refs_10_), channel_id=1, source_target_pairs={{0,8},{4,12},{8,0},{12,4},{16,24},{20,28},{24,16},{28,20},{1,9},{5... | collective-permute-start | bytes 1622024 | tf_op jit(solution)/shard_map/ppermute | solution.py:672
  56.5 3.9 %rest_kept.3.refs_0_.refs_1_.refs_2_.refs_3_ = f32[3,192,1472]{2,1,0:T(8,128)S(1)} custom-call(s32[32]{0:T(128)S(1)} %dynamic-slice_bitcast_fusion.where_ref, bf16[4,128,1536]{2,1,0:T(8,128)(2,1)S(1)} %pack_rows.2.refs_0_.refs_2_.refs_6_, bf16[4,128,1536]{2,1,0:T(8,128)(2,1)S(1)} %collective-permute-done.5.refs_1_.refs_3_.refs_7_, ...), custom_call_target="tpu_custom_call" | custom-call | flops 1000000 | bytes 3000000 | tf_op jit(solution)/shard_map/rest_kept/pallas_call | solution.py:329
  61.1 4.9 %collective-permute-start.25 = (bf16[192,1472]{1,0:T(8,128)(2,1)S(1)}, bf16[192,1472]{1,0:T(8,128)(2,1)S(1)}, u32[]{:S(2)}, u32[]{:S(2)}) collective-permute-start(bf16[192,1472]{1,0:T(8,128)(2,1)S(1)} %combine.8.refs_1_), channel_id=1, source_target_pairs={{0,8},{4,12},{24,16},{28,20},{1,9},{5,13},{25,17},{29,21},{2,10},{... | collective-permute-start | bytes 1695752 | tf_op jit(solution)/shard_map/ppermute | solution.py:672
  67.8 3.9 %rest_kept.4.refs_0_.refs_2_.refs_10_ = f32[3,192,1408]{2,1,0:T(8,128)S(1)} custom-call(s32[32]{0:T(128)S(1)} %dynamic-slice_bitcast_fusion.where_ref, bf16[2,128,1408]{2,1,0:T(8,128)(2,1)S(1)} %pack_rows.3.refs_0_.refs_2_, bf16[2,128,1408]{2,1,0:T(8,128)(2,1)S(1)} %collective-permute-done.6.refs_7_.refs_1_.refs_3_, ...), custom_call_target="tpu_custom_call" | custom-call | flops 1000000 | bytes 3000000 | tf_op jit(solution)/shard_map/rest_kept/pallas_call | solution.py:329
  73.9 4.4 %collective-permute-start.27 = (bf16[192,1408]{1,0:T(8,128)(2,1)S(1)}, bf16[192,1408]{1,0:T(8,128)(2,1)S(1)}, u32[]{:S(2)}, u32[]{:S(2)}) collective-permute-start(bf16[192,1408]{1,0:T(8,128)(2,1)S(1)} %combine.9.refs_2_), channel_id=1, source_target_pairs={{0,8},{4,12},{24,16},{28,20},{1,9},{5,13},{25,17},{29,21},{2,10},{... | collective-permute-start | bytes 1622024 | tf_op jit(solution)/shard_map/ppermute | solution.py:672
  78.3 4.7 %back_part.3 = (bf16[3,192,512]{2,1,0:T(8,128)(2,1)S(1)}, bf16[3,192,512]{2,1,0:T(8,128)(2,1)S(1)}, f32[8,1024]{1,0:T(8,128)S(1)}) custom-call(s32[32]{0:T(128)S(1)} %dynamic-slice_bitcast_fusion.where_ref, bf16[4,128,1536]{2,1,0:T(8,128)(2,1)S(1)} %pack_rows.2.refs_0_.refs_2_.refs_6_, ...), custom_call_target="tpu_custom_call" | custom-call | flops 6000000 | bytes 18000000 | tf_op jit(solution)/shard_map/back_part/pallas_call | solution.py:569
  85.1 2.6 %back_part.4 = (bf16[1,192,512]{2,1,0:T(8,128)(2,1)S(1)}, bf16[1,192,512]{2,1,0:T(8,128)(2,1)S(1)}, f32[8,1024]{1,0:T(8,128)S(1)}) custom-call(s32[32]{0:T(128)S(1)} %dynamic-slice_bitcast_fusion.where_ref, bf16[4,128,1536]{2,1,0:T(8,128)(2,1)S(1)} %pack_rows.2.refs_0_.refs_2_.refs_6_, ...), custom_call_target="tpu_custom_call" | custom-call | flops 6000000 | bytes 18000000 | tf_op jit(solution)/shard_map/back_part/pallas_call | solution.py:569
  88.6 4.6 %collective-permute-start.24 = (bf16[192,2880]{1,0:T(8,128)(2,1)S(1)}, bf16[192,2880]{1,0:T(8,128)(2,1)S(1)}, u32[]{:S(2)}, u32[]{:S(2)}) collective-permute-start(bf16[192,2880]{1,0:T(8,128)(2,1)S(1)} %combine.11.refs_15_), channel_id=1, source_target_pairs={{0,8},{4,12},{8,0},{12,4},{16,24},{20,28},{24,16},{28,20},{1,9},{5... | collective-permute-start | bytes 3317768 | tf_op jit(solution)/shard_map/ppermute | solution.py:672
  96.5 2.7 %back_part.5 = (bf16[1,192,512]{2,1,0:T(8,128)(2,1)S(1)}, bf16[1,192,512]{2,1,0:T(8,128)(2,1)S(1)}, f32[8,1024]{1,0:T(8,128)S(1)}) custom-call(s32[32]{0:T(128)S(1)} %dynamic-slice_bitcast_fusion.where_ref, bf16[4,128,1536]{2,1,0:T(8,128)(2,1)S(1)} %pack_rows.2.refs_0_.refs_2_.refs_6_, ...), custom_call_target="tpu_custom_call" | custom-call | flops 6000000 | bytes 18000000 | tf_op jit(solution)/shard_map/back_part/pallas_call | solution.py:569
  99.2 1.9 %collective-permute-start.20 = (f32[1,512]{1,0:T(1,128)S(1)}, f32[1,512]{1,0:T(1,128)S(1)}, u32[]{:S(2)}, u32[]{:S(2)}) collective-permute-start(f32[1,512]{1,0:T(1,128)S(1)} %slice.7), channel_id=1, source_target_pairs={{0,4},{4,0},{8,12},{12,8},{16,20},{20,16},{24,28},{28,24},{1,5},{5... | collective-permute-start | bytes 6152 | tf_op jit(solution)/shard_map/ppermute | solution.py:660
  102.9 1.8 %collective-permute-start.23 = (bf16[1,192,512]{2,1,0:T(8,128)(2,1)S(1)}, bf16[1,192,512]{2,1,0:T(8,128)(2,1)S(1)}, u32[]{:S(2)}, u32[]{:S(2)}) collective-permute-start(bf16[1,192,512]{2,1,0:T(8,128)(2,1)S(1)} %get-tuple-element.32), channel_id=1, source_target_pairs={{0,4},{4,0},{8,12},{12,8},{16,20},{20,16},{24,28},{28,24},{1,5},{5... | collective-permute-start | bytes 589832 | tf_op jit(solution)/shard_map/ppermute | solution.py:660
  104.7 6.4 %all_to_all.11 = f32[4,1,128]{2,1,0:T(1,128)S(1)} all-to-all(f32[4,1,128]{2,1,0:T(1,128)S(1)} %add_bitcast_fusion), channel_id=1, replica_groups=mesh['ctx'=8,'exp'=4] {'exp'}, dimensions={0} | all-to-all | bytes 4096 | tf_op jit(solution)/shard_map/all_to_all | solution.py:814
  111.7 2.9 %join_hidden.1 = bf16[512,1536]{1,0:T(8,128)(2,1)} custom-call(s32[32]{0:T(128)S(1)} %dynamic-slice_bitcast_fusion.where_ref, bf16[3,192,512]{2,1,0:T(8,128)(2,1)S(1)} %get-tuple-element.27.refs_0_, bf16[3,192,512]{2,1,0:T(8,128)(2,1)S(1)} %collective-permute-done.21.refs_1_.refs_2_, bf16[1,192,512]{2,1,0:T(8,128)(2,1)S(1)} %get-tuple-element.29.refs_2_, ...), custom_call_target="tpu_custom_call" | custom-call | flops 2000000 | bytes 6000000 | tf_op jit(solution)/shard_map/join_hidden/pallas_call | solution.py:611
  114.6 4.1 %collective-permute-done.24.refs_0_ = bf16[192,2880]{1,0:T(8,128)(2,1)S(1)} collective-permute-done((bf16[192,2880]{1,0:T(8,128)(2,1)S(1)}, bf16[192,2880]{1,0:T(8,128)(2,1)S(1)}, u32[]{:S(2)}, u32[]{:S(2)}) %collective-permute-start.24) | collective-permute-done | bytes 1105952 | tf_op jit(solution)/shard_map/ppermute | solution.py:672
  (88 shorter events, 34.1 us)
Async XLA Ops:
  2.8 12.8 %collective-permute-start.1 = (bf16[128,1536]{1,0:T(8,128)(2,1)}, bf16[128,1536]{1,0:T(8,128)(2,1)S(1)}, u32[]{:S(2)}, u32[]{:S(2)}) collective-permute-start(bf16[128,1536]{1,0:T(8,128)(2,1)} %get-tuple-element.19.refs_0_), channel_id=1, source_target_pairs={{0,4},{4,0},{8,12},{12,8},{16,20},{20,16},{24,28},{28,24},{1,5},{5... | collective-permute-start | bytes 1179656 | tf_op jit(solution)/shard_map/ppermute | solution.py:660
  5.8 10.8 %collective-permute-start = (bf16[128,1536]{1,0:T(8,128)(2,1)}, bf16[128,1536]{1,0:T(8,128)(2,1)S(1)}, u32[]{:S(2)}, u32[]{:S(2)}) collective-permute-start(bf16[128,1536]{1,0:T(8,128)(2,1)} %get-tuple-element.19.refs_0_), channel_id=1, source_target_pairs={{0,2},{1,3},{2,0},{3,1},{4,6},{5,7},{6,4},{7,5},{8,10},{9,11},{10,... | collective-permute-start | bytes 1179656 | tf_op jit(solution)/shard_map/ppermute | solution.py:662
  7.4 26.3 %collective-permute-start.9 = (bf16[192,2880]{1,0:T(8,128)(2,1)}, bf16[192,2880]{1,0:T(8,128)(2,1)S(1)}, u32[]{:S(2)}, u32[]{:S(2)}) collective-permute-start(bf16[192,2880]{1,0:T(8,128)(2,1)} %bitcast.15), channel_id=1, source_target_pairs={{0,8},{4,12},{8,0},{12,4},{16,24},{20,28},{24,16},{28,20},{1,9},{5... | collective-permute-start | bytes 3317768 | tf_op jit(solution)/shard_map/ppermute | solution.py:672
  8.9 25.2 %collective-permute-start.8 = (bf16[192,2880]{1,0:T(8,128)(2,1)}, bf16[192,2880]{1,0:T(8,128)(2,1)S(1)}, u32[]{:S(2)}, u32[]{:S(2)}) collective-permute-start(bf16[192,2880]{1,0:T(8,128)(2,1)} %bitcast.16), channel_id=1, source_target_pairs={{8,16},{12,20},{16,8},{20,12},{9,17},{13,21},{17,9},{21,13},{10,18... | collective-permute-start | bytes 3317768 | tf_op jit(solution)/shard_map/ppermute | solution.py:672
  16.6 12.6 %collective-permute-start.2 = (bf16[128,1536]{1,0:T(8,128)(2,1)S(1)}, bf16[128,1536]{1,0:T(8,128)(2,1)S(1)}, u32[]{:S(2)}, u32[]{:S(2)}) collective-permute-start(bf16[128,1536]{1,0:T(8,128)(2,1)S(1)} %hold.13.refs_1_.refs_2_), channel_id=1, source_target_pairs={{0,2},{1,3},{2,0},{3,1},{4,6},{5,7},{6,4},{7,5},{8,10},{9,11},{10,... | collective-permute-start | bytes 1179656 | tf_op jit(solution)/shard_map/ppermute | solution.py:662
  20.9 8.4 %collective-permute-start.4 = (bf16[128,1408]{1,0:T(8,128)(2,1)S(1)}, bf16[128,1408]{1,0:T(8,128)(2,1)S(1)}, u32[]{:S(2)}, u32[]{:S(2)}) collective-permute-start(bf16[128,1408]{1,0:T(8,128)(2,1)S(1)} %hold.14.refs_0_), channel_id=1, source_target_pairs={{0,4},{4,0},{8,12},{12,8},{16,20},{20,16},{24,28},{28,24},{1,5},{5... | collective-permute-start | bytes 1081352 | tf_op jit(solution)/shard_map/ppermute | solution.py:660
  30.1 11.3 %collective-permute-start.7 = (bf16[128,1408]{1,0:T(8,128)(2,1)S(1)}, bf16[128,1408]{1,0:T(8,128)(2,1)S(1)}, u32[]{:S(2)}, u32[]{:S(2)}) collective-permute-start(bf16[128,1408]{1,0:T(8,128)(2,1)S(1)} %hold.14.refs_0_), channel_id=1, source_target_pairs={{0,2},{1,3},{2,0},{3,1},{4,6},{5,7},{6,4},{7,5},{8,10},{9,11},{10,... | collective-permute-start | bytes 1081352 | tf_op jit(solution)/shard_map/ppermute | solution.py:662
  33.7 15.0 %collective-permute-start.11 = (bf16[128,1408]{1,0:T(8,128)(2,1)S(1)}, bf16[128,1408]{1,0:T(8,128)(2,1)S(1)}, u32[]{:S(2)}, u32[]{:S(2)}) collective-permute-start(bf16[128,1408]{1,0:T(8,128)(2,1)S(1)} %collective-permute-done.4.refs_4_.refs_1_), channel_id=1, source_target_pairs={{0,2},{1,3},{2,0},{3,1},{4,6},{5,7},{6,4},{7,5},{8,10},{9,11},{10,... | collective-permute-start | bytes 1081352 | tf_op jit(solution)/shard_map/ppermute | solution.py:662
  36.7 16.1 %collective-permute-start.15 = (bf16[192,1472]{1,0:T(8,128)(2,1)S(1)}, bf16[192,1472]{1,0:T(8,128)(2,1)S(1)}, u32[]{:S(2)}, u32[]{:S(2)}) collective-permute-start(bf16[192,1472]{1,0:T(8,128)(2,1)S(1)} %first_sums.2.refs_6_), channel_id=1, source_target_pairs={{0,8},{4,12},{8,0},{12,4},{16,24},{20,28},{24,16},{28,20},{1,9},{5... | collective-permute-start | bytes 1695752 | tf_op jit(solution)/shard_map/ppermute | solution.py:672
  39.2 27.3 %collective-permute-start.14 = (bf16[192,2880]{1,0:T(8,128)(2,1)S(1)}, bf16[192,2880]{1,0:T(8,128)(2,1)S(1)}, u32[]{:S(2)}, u32[]{:S(2)}) collective-permute-start(bf16[192,2880]{1,0:T(8,128)(2,1)S(1)} %hold.15.refs_1_.refs_12_), channel_id=1, source_target_pairs={{8,16},{12,20},{16,8},{20,12},{9,17},{13,21},{17,9},{21,13},{10,18... | collective-permute-start | bytes 3317768 | tf_op jit(solution)/shard_map/ppermute | solution.py:672
  39.9 16.5 %collective-permute-start.13 = (bf16[3,192,512]{2,1,0:T(8,128)(2,1)S(1)}, bf16[3,192,512]{2,1,0:T(8,128)(2,1)S(1)}, u32[]{:S(2)}, u32[]{:S(2)}) collective-permute-start(bf16[3,192,512]{2,1,0:T(8,128)(2,1)S(1)} %get-tuple-element.23), channel_id=1, source_target_pairs={{0,4},{4,0},{8,12},{12,8},{16,20},{20,16},{24,28},{28,24},{1,5},{5... | collective-permute-start | bytes 1769480 | tf_op jit(solution)/shard_map/ppermute | solution.py:660
  41.4 7.3 %collective-permute-start.10 = (bf16[128,1408]{1,0:T(8,128)(2,1)S(1)}, bf16[128,1408]{1,0:T(8,128)(2,1)S(1)}, u32[]{:S(2)}, u32[]{:S(2)}) collective-permute-start(bf16[128,1408]{1,0:T(8,128)(2,1)S(1)} %hold.17.refs_2_.refs_4_), channel_id=1, source_target_pairs={{0,1},{1,0},{2,3},{3,2},{4,5},{5,4},{6,7},{7,6},{8,9},{9,8},{10,11... | collective-permute-start | bytes 1081352 | tf_op jit(solution)/shard_map/ppermute | solution.py:662
  52.8 19.6 %collective-permute-start.18 = (bf16[192,1408]{1,0:T(8,128)(2,1)S(1)}, bf16[192,1408]{1,0:T(8,128)(2,1)S(1)}, u32[]{:S(2)}, u32[]{:S(2)}) collective-permute-start(bf16[192,1408]{1,0:T(8,128)(2,1)S(1)} %hold.21.refs_2_.refs_10_), channel_id=1, source_target_pairs={{0,8},{4,12},{8,0},{12,4},{16,24},{20,28},{24,16},{28,20},{1,9},{5... | collective-permute-start | bytes 1622024 | tf_op jit(solution)/shard_map/ppermute | solution.py:672
  55.7 27.3 %collective-permute-start.17 = (bf16[192,1472]{1,0:T(8,128)(2,1)S(1)}, bf16[192,1472]{1,0:T(8,128)(2,1)S(1)}, u32[]{:S(2)}, u32[]{:S(2)}) collective-permute-start(bf16[192,1472]{1,0:T(8,128)(2,1)S(1)} %combine.7.refs_6_), channel_id=1, source_target_pairs={{8,16},{12,20},{16,8},{20,12},{9,17},{13,21},{17,9},{21,13},{10,18... | collective-permute-start | bytes 1695752 | tf_op jit(solution)/shard_map/ppermute | solution.py:672
  61.1 32.2 %collective-permute-start.25 = (bf16[192,1472]{1,0:T(8,128)(2,1)S(1)}, bf16[192,1472]{1,0:T(8,128)(2,1)S(1)}, u32[]{:S(2)}, u32[]{:S(2)}) collective-permute-start(bf16[192,1472]{1,0:T(8,128)(2,1)S(1)} %combine.8.refs_1_), channel_id=1, source_target_pairs={{0,8},{4,12},{24,16},{28,20},{1,9},{5,13},{25,17},{29,21},{2,10},{... | collective-permute-start | bytes 1695752 | tf_op jit(solution)/shard_map/ppermute | solution.py:672
  66.5 29.2 %collective-permute-start.16 = (bf16[192,2880]{1,0:T(8,128)(2,1)S(1)}, bf16[192,2880]{1,0:T(8,128)(2,1)S(1)}, u32[]{:S(2)}, u32[]{:S(2)}) collective-permute-start(bf16[192,2880]{1,0:T(8,128)(2,1)S(1)} %hold.22.refs_10_.refs_13_), channel_id=1, source_target_pairs={{8,0},{12,4},{16,24},{20,28},{9,1},{13,5},{17,25},{21,29},{10,2},{... | collective-permute-start | bytes 3317768 | tf_op jit(solution)/shard_map/ppermute | solution.py:672
  73.2 14.5 %collective-permute-start.19 = (bf16[192,1408]{1,0:T(8,128)(2,1)S(1)}, bf16[192,1408]{1,0:T(8,128)(2,1)S(1)}, u32[]{:S(2)}, u32[]{:S(2)}) collective-permute-start(bf16[192,1408]{1,0:T(8,128)(2,1)S(1)} %combine.10.refs_11_), channel_id=1, source_target_pairs={{8,16},{12,20},{16,8},{20,12},{9,17},{13,21},{17,9},{21,13},{10,18... | collective-permute-start | bytes 1622024 | tf_op jit(solution)/shard_map/ppermute | solution.py:672
  73.9 20.8 %collective-permute-start.27 = (bf16[192,1408]{1,0:T(8,128)(2,1)S(1)}, bf16[192,1408]{1,0:T(8,128)(2,1)S(1)}, u32[]{:S(2)}, u32[]{:S(2)}) collective-permute-start(bf16[192,1408]{1,0:T(8,128)(2,1)S(1)} %combine.9.refs_2_), channel_id=1, source_target_pairs={{0,8},{4,12},{24,16},{28,20},{1,9},{5,13},{25,17},{29,21},{2,10},{... | collective-permute-start | bytes 1622024 | tf_op jit(solution)/shard_map/ppermute | solution.py:672
  83.0 12.6 %collective-permute-start.21 = (bf16[3,192,512]{2,1,0:T(8,128)(2,1)S(1)}, bf16[3,192,512]{2,1,0:T(8,128)(2,1)S(1)}, u32[]{:S(2)}, u32[]{:S(2)}) collective-permute-start(bf16[3,192,512]{2,1,0:T(8,128)(2,1)S(1)} %get-tuple-element.28), channel_id=1, source_target_pairs={{0,4},{4,0},{8,12},{12,8},{16,20},{20,16},{24,28},{28,24},{1,5},{5... | collective-permute-start | bytes 1769480 | tf_op jit(solution)/shard_map/ppermute | solution.py:660
  88.6 30.2 %collective-permute-start.24 = (bf16[192,2880]{1,0:T(8,128)(2,1)S(1)}, bf16[192,2880]{1,0:T(8,128)(2,1)S(1)}, u32[]{:S(2)}, u32[]{:S(2)}) collective-permute-start(bf16[192,2880]{1,0:T(8,128)(2,1)S(1)} %combine.11.refs_15_), channel_id=1, source_target_pairs={{0,8},{4,12},{8,0},{12,4},{16,24},{20,28},{24,16},{28,20},{1,9},{5... | collective-permute-start | bytes 3317768 | tf_op jit(solution)/shard_map/ppermute | solution.py:672
  93.9 20.7 %collective-permute-start.26 = (bf16[192,1472]{1,0:T(8,128)(2,1)S(1)}, bf16[192,1472]{1,0:T(8,128)(2,1)S(1)}, u32[]{:S(2)}, u32[]{:S(2)}) collective-permute-start(bf16[192,1472]{1,0:T(8,128)(2,1)S(1)} %combine.12), channel_id=1, source_target_pairs={{8,16},{12,20},{16,8},{20,12},{9,17},{13,21},{17,9},{21,13},{10,18... | collective-permute-start | bytes 1695752 | tf_op jit(solution)/shard_map/ppermute | solution.py:672
  95.7 18.9 %collective-permute-start.28 = (bf16[192,1408]{1,0:T(8,128)(2,1)S(1)}, bf16[192,1408]{1,0:T(8,128)(2,1)S(1)}, u32[]{:S(2)}, u32[]{:S(2)}) collective-permute-start(bf16[192,1408]{1,0:T(8,128)(2,1)S(1)} %hold.23), channel_id=1, source_target_pairs={{8,16},{12,20},{16,8},{20,12},{9,17},{13,21},{17,9},{21,13},{10,18... | collective-permute-start | bytes 1622024 | tf_op jit(solution)/shard_map/ppermute | solution.py:672
  101.1 10.6 %collective-permute-start.22 = (bf16[1,192,512]{2,1,0:T(8,128)(2,1)S(1)}, bf16[1,192,512]{2,1,0:T(8,128)(2,1)S(1)}, u32[]{:S(2)}, u32[]{:S(2)}) collective-permute-start(bf16[1,192,512]{2,1,0:T(8,128)(2,1)S(1)} %get-tuple-element.30), channel_id=1, source_target_pairs={{0,4},{4,0},{8,12},{12,8},{16,20},{20,16},{24,28},{28,24},{1,5},{5... | collective-permute-start | bytes 589832 | tf_op jit(solution)/shard_map/ppermute | solution.py:660
  102.9 8.8 %collective-permute-start.23 = (bf16[1,192,512]{2,1,0:T(8,128)(2,1)S(1)}, bf16[1,192,512]{2,1,0:T(8,128)(2,1)S(1)}, u32[]{:S(2)}, u32[]{:S(2)}) collective-permute-start(bf16[1,192,512]{2,1,0:T(8,128)(2,1)S(1)} %get-tuple-element.32), channel_id=1, source_target_pairs={{0,4},{4,0},{8,12},{12,8},{16,20},{20,16},{24,28},{28,24},{1,5},{5... | collective-permute-start | bytes 589832 | tf_op jit(solution)/shard_map/ppermute | solution.py:660
  (12 other events, 77.7 us)

commit v15 on v14

--- a/solution.py
+++ b/solution.py
@@ -13,12 +13,13 @@
 ORDER_WEIGHT = 100
 FIRST_WEIGHT = 12_000
 NEXT_WEIGHT = 600
-HIDDEN_WEIGHT = 5_000
+HIDDEN_WEIGHT = 4_600
 PASS_WEIGHT = 1
-WAITED_WEIGHT = 210
-ENTER_WEIGHT = 575
-LEAVE_WEIGHT = 5_300
-LAST_WEIGHT = 90
+WAITED_WEIGHT = 1
+ENTER_WEIGHT = 3_000
+CLOSE_WEIGHT = 3_450
+LEAVE_WEIGHT = 2_650
+LAST_WEIGHT = 2_800
 NT = (((1,), (1,)), ((), ()))
 NN = (((1,), (0,)), ((), ()))
 f32 = jnp.float32
@@ -803,19 +804,24 @@
         if turn > 2:
             waited = [array for key in ((turn, "A"), (turn, "B")) for array in weights_of.get(key, [])]
             if apart and turn + 1 == depth:
-                pass_on(depth, "B", [sums], 0, (), ENTER_WEIGHT)
-                pass_on(depth, "B", [sums], 1, [*waited, *sooner], LEAVE_WEIGHT)
+                pass_on(depth, "B", [], 0)
+                pass_on(depth, "B", [], 1, sooner, LEAVE_WEIGHT)
                 marker = pass_on(depth, "A", [sums], weight=LAST_WEIGHT)
+                sums = backprop(choices_of(turn - 1), sums, True, [marker])
             else:
                 pass_on(turn + 1, "B", [sums, *sooner, *waited])
                 marker = pass_on(turn + 1, "A", [sums])
-        sums = backprop(choices, sums, len(choices) == 1, [marker])
+        if not apart or turn > 2:
+            sums = backprop(choices, sums, len(choices) == 1, [marker])
     slot_grad = sums[0:1, :slots] + swap(sums[0:1, slots:], 1, 0)
     grads = lax.all_to_all(
         slot_grad.reshape(experts, tokens), "exp", split_axis=0, concat_axis=0, tiled=True
     )
     logit_grad = logits_grad(gates, expert_ids.T, grads)
     hidden_grad = join_hidden(table, where, all_choices, halves, slots, hidden)
+    if apart:
+        entered = list(hold(got[depth, "B"][:1], [hidden_grad], ENTER_WEIGHT))
+        got[depth, "B"] = entered + list(hold(got[depth, "B"][1:], entered, CLOSE_WEIGHT))
     weight_grad = total_grad(got[depth, "A"], got[depth, "B"], rest, cut)
     return (logit_grad.T, hidden_grad[None, None], weight_grad)
 

time: 121 us -> 121 us (level)
  waiting for transfers between devices: 29.7 us -> 25.7 us
  starting transfers between devices: 40.6 us -> 43.1 us
  local copies, waits for them, and re-layouts: 3.12 us -> 4.53 us
    ppermute x13, waiting for transfers between devices: 6.64 us -> 2.54 us  [swap_z(): return lax.ppermute(value, 'ctx', pairs)]
    ppermute x13, starting transfers between devices: 25.8 us -> 28.1 us  [swap_z(): return lax.ppermute(value, 'ctx', pairs)]
    unnamed x14 -> x16, local copies, waits for them, and re-layouts: 2.43 us -> 3.83 us
where the time goes in v15:
time: 121 us; the launch traced here: 120 us
  starting transfers between devices  43.1 us (36%)
  Pallas kernels  39.4 us (33%)
  waiting for transfers between devices  25.7 us (21%)
  blocking collectives  6.45 us (5%)
  local copies, waits for them, and re-layouts  4.53 us (4%)
    ppermute x13, starting transfers between devices, swap_z(): return lax.ppermute(value, 'ctx', pairs)  28.1 us
    ppermute x8, waiting for transfers between devices, swap(): return lax.ppermute(value, 'ctx', [(i, i ^ x) for i in range(groups)])  12.5 us
    ppermute x8, waiting for transfers between devices, swap(): return lax.ppermute(value, 'exp', [(i, i ^ exp) for i in range(experts)])  10.6 us
    ppermute x8, starting transfers between devices, swap(): return lax.ppermute(value, 'ctx', [(i, i ^ x) for i in range(groups)])  10.4 us
    pallas_call x3, Pallas kernels, back_part(): pl.pallas_call(functools.partial(back_kernel, table, model, cut, counts,...  9.98 us
    pallas_call x5, Pallas kernels, products(): pl.pallas_call(functools.partial(products_kernel, table, model, counts, p...  9.45 us
    all_to_all x1, blocking collectives, per_device_full(): lax.all_to_all(slot_grad.reshape(experts, tokens), 'exp', split_axis=0, c...  6.45 us
    pallas_call x7, Pallas kernels, combine(): pl.pallas_call(functools.partial(combine_kernel, table, ('use', turn, nam...  5.11 us
  transfers between devices with their start and end apart: 29, of which 12 were waited for; matrix products, arithmetic and copies ran while one was open for 1% of the time, Pallas kernels for 30%

profile of v15, /device:TPU:0, one launch (start us, length us, event | category | flops | bytes accessed | tf_op | source)
XLA Modules:
  0.0 120.2 jit_solution(11349102122837925801)
XLA Ops:
  0.6 2.2 %make_rows.1 = (bf16[128,1536]{1,0:T(8,128)(2,1)}, bf16[128,1408]{1,0:T(8,128)(2,1)}, f32[4,128]{1,0:T(4,128)}) custom-call(bf16[2880,128]{1,0:T(8,128)(2,1)} %bitcast.22, f32[4,128]{1,0:T(4,128)} %bitcast.23, s32[4,128]{1,0:T(4,128)} %bitcast.19), custom_call_target="tpu_custom_call" | custom-call | flops 2000000 | bytes 6000000 | tf_op jit(solution)/shard_map/make_rows/pallas_call | solution.py:169
  2.8 3.0 %collective-permute-start.1 = (bf16[128,1536]{1,0:T(8,128)(2,1)}, bf16[128,1536]{1,0:T(8,128)(2,1)S(1)}, u32[]{:S(2)}, u32[]{:S(2)}) collective-permute-start(bf16[128,1536]{1,0:T(8,128)(2,1)} %get-tuple-element.19.refs_0_), channel_id=1, source_target_pairs={{0,4},{4,0},{8,12},{12,8},{16,20},{20,16},{24,28},{28,24},{1,5},{5... | collective-permute-start | bytes 1179656 | tf_op jit(solution)/shard_map/ppermute | solution.py:661
  12.8 2.2 %split_hidden.1 = (bf16[4,192,512]{2,1,0:T(8,128)(2,1)S(1)}, bf16[1,192,512]{2,1,0:T(8,128)(2,1)S(1)}, bf16[3,192,512]{2,1,0:T(8,128)(2,1)S(1)}) custom-call(s32[32]{0:T(128)S(1)} %dynamic-slice_bitcast_fusion.where_ref, bf16[512,1536]{1,0:T(8,128)(2,1)S(1)} %bitcast.14, bf16[128,1536]{1,0:T(8,128)(2,1)S(1)} %copy-done.2), custom_call_target="tpu_custom_call" | custom-call | flops 2000000 | bytes 6000000 | tf_op jit(solution)/shard_map/split_hidden/pallas_call | solution.py:260
  18.1 2.7 %collective-permute-done.3.refs_2_.refs_5_.refs_9_ = bf16[1,192,512]{2,1,0:T(8,128)(2,1)S(1)} collective-permute-done((bf16[1,192,512]{2,1,0:T(8,128)(2,1)S(1)}, bf16[1,192,512]{2,1,0:T(8,128)(2,1)S(1)}, u32[]{:S(2)}, u32[]{:S(2)}) %collective-permute-start.3) | collective-permute-done | bytes 196640 | tf_op jit(solution)/shard_map/ppermute | solution.py:661
  21.4 7.8 %collective-permute-done.4.refs_4_.refs_1_ = bf16[128,1408]{1,0:T(8,128)(2,1)S(1)} collective-permute-done((bf16[128,1408]{1,0:T(8,128)(2,1)S(1)}, bf16[128,1408]{1,0:T(8,128)(2,1)S(1)}, u32[]{:S(2)}, u32[]{:S(2)}) %collective-permute-start.4) | collective-permute-done | bytes 360480 | tf_op jit(solution)/shard_map/ppermute | solution.py:661
  31.5 2.2 %collective-permute-done.9.refs_0_ = bf16[192,2880]{1,0:T(8,128)(2,1)S(1)} collective-permute-done((bf16[192,2880]{1,0:T(8,128)(2,1)}, bf16[192,2880]{1,0:T(8,128)(2,1)S(1)}, u32[]{:S(2)}, u32[]{:S(2)}) %collective-permute-start.9) | collective-permute-done | bytes 1105952 | tf_op jit(solution)/shard_map/ppermute | solution.py:673
  34.5 2.2 %first_sums.2.refs_6_ = bf16[192,1472]{1,0:T(8,128)(2,1)S(1)} custom-call(s32[32]{0:T(128)S(1)} %dynamic-slice_bitcast_fusion.where_ref, bf16[4,128,1536]{2,1,0:T(8,128)(2,1)S(1)} %pack_rows.2.refs_0_.refs_2_.refs_6_, bf16[4,128,1536]{2,1,0:T(8,128)(2,1)S(1)} %collective-permute-done.5.refs_1_.refs_3_.refs_7_, ...), custom_call_target="tpu_custom_call" | custom-call | flops 1000000 | bytes 3000000 | tf_op jit(solution)/shard_map/first_sums/pallas_call | solution.py:371
  36.7 2.5 %collective-permute-start.15 = (bf16[192,1472]{1,0:T(8,128)(2,1)S(1)}, bf16[192,1472]{1,0:T(8,128)(2,1)S(1)}, u32[]{:S(2)}, u32[]{:S(2)}) collective-permute-start(bf16[192,1472]{1,0:T(8,128)(2,1)S(1)} %first_sums.2.refs_6_), channel_id=1, source_target_pairs={{0,8},{4,12},{8,0},{12,4},{16,24},{20,28},{24,16},{28,20},{1,9},{5... | collective-permute-start | bytes 1695752 | tf_op jit(solution)/shard_map/ppermute | solution.py:673
  41.4 7.3 %collective-permute-done.11.refs_0_ = bf16[128,1408]{1,0:T(8,128)(2,1)S(1)} collective-permute-done((bf16[128,1408]{1,0:T(8,128)(2,1)S(1)}, bf16[128,1408]{1,0:T(8,128)(2,1)S(1)}, u32[]{:S(2)}, u32[]{:S(2)}) %collective-permute-start.11) | collective-permute-done | bytes 360480 | tf_op jit(solution)/shard_map/ppermute | solution.py:663
  50.3 2.1 %first_sums.3.refs_0_ = bf16[192,1408]{1,0:T(8,128)(2,1)S(1)} custom-call(s32[32]{0:T(128)S(1)} %dynamic-slice_bitcast_fusion.where_ref, bf16[2,128,1408]{2,1,0:T(8,128)(2,1)S(1)} %pack_rows.3.refs_0_.refs_2_, bf16[2,128,1408]{2,1,0:T(8,128)(2,1)S(1)} %collective-permute-done.6.refs_7_.refs_1_.refs_3_, bf16[128,1408]{1,0:T(8,128)(2,1)S(1)} %hold.19.refs_2_.refs_4_, ...), custom_call_target="tpu_custom_call" | custom-call | flops 1000000 | bytes 3000000 | tf_op jit(solution)/shard_map/first_sums/pallas_call | solution.py:371
  52.8 2.2 %collective-permute-start.18 = (bf16[192,1408]{1,0:T(8,128)(2,1)S(1)}, bf16[192,1408]{1,0:T(8,128)(2,1)S(1)}, u32[]{:S(2)}, u32[]{:S(2)}) collective-permute-start(bf16[192,1408]{1,0:T(8,128)(2,1)S(1)} %hold.23.refs_2_.refs_10_), channel_id=1, source_target_pairs={{0,8},{4,12},{8,0},{12,4},{16,24},{20,28},{24,16},{28,20},{1,9},{5... | collective-permute-start | bytes 1622024 | tf_op jit(solution)/shard_map/ppermute | solution.py:673
  55.8 3.9 %rest_kept.3.refs_0_.refs_1_.refs_2_.refs_3_ = f32[3,192,1472]{2,1,0:T(8,128)S(1)} custom-call(s32[32]{0:T(128)S(1)} %dynamic-slice_bitcast_fusion.where_ref, bf16[4,128,1536]{2,1,0:T(8,128)(2,1)S(1)} %pack_rows.2.refs_0_.refs_2_.refs_6_, bf16[4,128,1536]{2,1,0:T(8,128)(2,1)S(1)} %collective-permute-done.5.refs_1_.refs_3_.refs_7_, ...), custom_call_target="tpu_custom_call" | custom-call | flops 1000000 | bytes 3000000 | tf_op jit(solution)/shard_map/rest_kept/pallas_call | solution.py:330
  60.4 4.6 %collective-permute-start.25 = (bf16[192,1472]{1,0:T(8,128)(2,1)S(1)}, bf16[192,1472]{1,0:T(8,128)(2,1)S(1)}, u32[]{:S(2)}, u32[]{:S(2)}) collective-permute-start(bf16[192,1472]{1,0:T(8,128)(2,1)S(1)} %combine.8.refs_1_), channel_id=1, source_target_pairs={{0,8},{4,12},{24,16},{28,20},{1,9},{5,13},{25,17},{29,21},{2,10},{... | collective-permute-start | bytes 1695752 | tf_op jit(solution)/shard_map/ppermute | solution.py:673
  67.6 3.9 %rest_kept.4.refs_0_.refs_2_.refs_10_ = f32[3,192,1408]{2,1,0:T(8,128)S(1)} custom-call(s32[32]{0:T(128)S(1)} %dynamic-slice_bitcast_fusion.where_ref, bf16[2,128,1408]{2,1,0:T(8,128)(2,1)S(1)} %pack_rows.3.refs_0_.refs_2_, bf16[2,128,1408]{2,1,0:T(8,128)(2,1)S(1)} %collective-permute-done.6.refs_7_.refs_1_.refs_3_, ...), custom_call_target="tpu_custom_call" | custom-call | flops 1000000 | bytes 3000000 | tf_op jit(solution)/shard_map/rest_kept/pallas_call | solution.py:330
  73.7 4.3 %collective-permute-start.27 = (bf16[192,1408]{1,0:T(8,128)(2,1)S(1)}, bf16[192,1408]{1,0:T(8,128)(2,1)S(1)}, u32[]{:S(2)}, u32[]{:S(2)}) collective-permute-start(bf16[192,1408]{1,0:T(8,128)(2,1)S(1)} %combine.9.refs_2_), channel_id=1, source_target_pairs={{0,8},{4,12},{24,16},{28,20},{1,9},{5,13},{25,17},{29,21},{2,10},{... | collective-permute-start | bytes 1622024 | tf_op jit(solution)/shard_map/ppermute | solution.py:673
  78.0 4.7 %back_part.3 = (bf16[3,192,512]{2,1,0:T(8,128)(2,1)S(1)}, bf16[3,192,512]{2,1,0:T(8,128)(2,1)S(1)}, f32[8,1024]{1,0:T(8,128)S(1)}) custom-call(s32[32]{0:T(128)S(1)} %dynamic-slice_bitcast_fusion.where_ref, bf16[4,128,1536]{2,1,0:T(8,128)(2,1)S(1)} %pack_rows.2.refs_0_.refs_2_.refs_6_, ...), custom_call_target="tpu_custom_call" | custom-call | flops 6000000 | bytes 18000000 | tf_op jit(solution)/shard_map/back_part/pallas_call | solution.py:570
  82.7 1.8 %collective-permute-start.21 = (bf16[3,192,512]{2,1,0:T(8,128)(2,1)S(1)}, bf16[3,192,512]{2,1,0:T(8,128)(2,1)S(1)}, u32[]{:S(2)}, u32[]{:S(2)}) collective-permute-start(bf16[3,192,512]{2,1,0:T(8,128)(2,1)S(1)} %get-tuple-element.28), channel_id=1, source_target_pairs={{0,4},{4,0},{8,12},{12,8},{16,20},{20,16},{24,28},{28,24},{1,5},{5... | collective-permute-start | bytes 1769480 | tf_op jit(solution)/shard_map/ppermute | solution.py:661
  87.4 7.4 %collective-permute-start.24 = (bf16[192,2880]{1,0:T(8,128)(2,1)S(1)}, bf16[192,2880]{1,0:T(8,128)(2,1)S(1)}, u32[]{:S(2)}, u32[]{:S(2)}) collective-permute-start(bf16[192,2880]{1,0:T(8,128)(2,1)S(1)} %combine.11.refs_15_), channel_id=1, source_target_pairs={{0,8},{4,12},{8,0},{12,4},{16,24},{20,28},{24,16},{28,20},{1,9},{5... | collective-permute-start | bytes 3317768 | tf_op jit(solution)/shard_map/ppermute | solution.py:673
  96.5 2.6 %back_part.4 = (bf16[1,192,512]{2,1,0:T(8,128)(2,1)S(1)}, bf16[1,192,512]{2,1,0:T(8,128)(2,1)S(1)}, f32[8,1024]{1,0:T(8,128)S(1)}) custom-call(s32[32]{0:T(128)S(1)} %dynamic-slice_bitcast_fusion.where_ref, bf16[4,128,1536]{2,1,0:T(8,128)(2,1)S(1)} %pack_rows.2.refs_0_.refs_2_.refs_6_, ...), custom_call_target="tpu_custom_call" | custom-call | flops 6000000 | bytes 18000000 | tf_op jit(solution)/shard_map/back_part/pallas_call | solution.py:570
  99.2 2.7 %back_part.5 = (bf16[1,192,512]{2,1,0:T(8,128)(2,1)S(1)}, bf16[1,192,512]{2,1,0:T(8,128)(2,1)S(1)}, f32[8,1024]{1,0:T(8,128)S(1)}) custom-call(s32[32]{0:T(128)S(1)} %dynamic-slice_bitcast_fusion.where_ref, bf16[4,128,1536]{2,1,0:T(8,128)(2,1)S(1)} %pack_rows.2.refs_0_.refs_2_.refs_6_, ...), custom_call_target="tpu_custom_call" | custom-call | flops 6000000 | bytes 18000000 | tf_op jit(solution)/shard_map/back_part/pallas_call | solution.py:570
  101.8 1.8 %collective-permute-start.20 = (f32[1,512]{1,0:T(1,128)S(1)}, f32[1,512]{1,0:T(1,128)S(1)}, u32[]{:S(2)}, u32[]{:S(2)}) collective-permute-start(f32[1,512]{1,0:T(1,128)S(1)} %slice.7), channel_id=1, source_target_pairs={{0,4},{4,0},{8,12},{12,8},{16,20},{20,16},{24,28},{28,24},{1,5},{5... | collective-permute-start | bytes 6152 | tf_op jit(solution)/shard_map/ppermute | solution.py:661
  105.6 1.7 %collective-permute-start.23 = (bf16[1,192,512]{2,1,0:T(8,128)(2,1)S(1)}, bf16[1,192,512]{2,1,0:T(8,128)(2,1)S(1)}, u32[]{:S(2)}, u32[]{:S(2)}) collective-permute-start(bf16[1,192,512]{2,1,0:T(8,128)(2,1)S(1)} %get-tuple-element.32), channel_id=1, source_target_pairs={{0,4},{4,0},{8,12},{12,8},{16,20},{20,16},{24,28},{28,24},{1,5},{5... | collective-permute-start | bytes 589832 | tf_op jit(solution)/shard_map/ppermute | solution.py:661
  107.3 6.5 %all_to_all.11 = f32[4,1,128]{2,1,0:T(1,128)S(1)} all-to-all(f32[4,1,128]{2,1,0:T(1,128)S(1)} %add_bitcast_fusion), channel_id=1, replica_groups=mesh['ctx'=8,'exp'=4] {'exp'}, dimensions={0} | all-to-all | bytes 4096 | tf_op jit(solution)/shard_map/all_to_all | solution.py:817
  114.3 2.9 %join_hidden.1.refs_1_ = bf16[512,1536]{1,0:T(8,128)(2,1)} custom-call(s32[32]{0:T(128)S(1)} %dynamic-slice_bitcast_fusion.where_ref, bf16[3,192,512]{2,1,0:T(8,128)(2,1)S(1)} %get-tuple-element.27.refs_0_, bf16[3,192,512]{2,1,0:T(8,128)(2,1)S(1)} %collective-permute-done.21.refs_1_, bf16[1,192,512]{2,1,0:T(8,128)(2,1)S(1)} %get-tuple-element.29.refs_2_, ...), custom_call_target="tpu_custom_call" | custom-call | flops 2000000 | bytes 6000000 | tf_op jit(solution)/shard_map/join_hidden/pallas_call | solution.py:612
  (92 shorter events, 34.1 us)
Async XLA Ops:
  2.8 12.8 %collective-permute-start.1 = (bf16[128,1536]{1,0:T(8,128)(2,1)}, bf16[128,1536]{1,0:T(8,128)(2,1)S(1)}, u32[]{:S(2)}, u32[]{:S(2)}) collective-permute-start(bf16[128,1536]{1,0:T(8,128)(2,1)} %get-tuple-element.19.refs_0_), channel_id=1, source_target_pairs={{0,4},{4,0},{8,12},{12,8},{16,20},{20,16},{24,28},{28,24},{1,5},{5... | collective-permute-start | bytes 1179656 | tf_op jit(solution)/shard_map/ppermute | solution.py:661
  5.8 10.8 %collective-permute-start = (bf16[128,1536]{1,0:T(8,128)(2,1)}, bf16[128,1536]{1,0:T(8,128)(2,1)S(1)}, u32[]{:S(2)}, u32[]{:S(2)}) collective-permute-start(bf16[128,1536]{1,0:T(8,128)(2,1)} %get-tuple-element.19.refs_0_), channel_id=1, source_target_pairs={{0,2},{1,3},{2,0},{3,1},{4,6},{5,7},{6,4},{7,5},{8,10},{9,11},{10,... | collective-permute-start | bytes 1179656 | tf_op jit(solution)/shard_map/ppermute | solution.py:663
  7.4 26.3 %collective-permute-start.9 = (bf16[192,2880]{1,0:T(8,128)(2,1)}, bf16[192,2880]{1,0:T(8,128)(2,1)S(1)}, u32[]{:S(2)}, u32[]{:S(2)}) collective-permute-start(bf16[192,2880]{1,0:T(8,128)(2,1)} %bitcast.16), channel_id=1, source_target_pairs={{0,8},{4,12},{8,0},{12,4},{16,24},{20,28},{24,16},{28,20},{1,9},{5... | collective-permute-start | bytes 3317768 | tf_op jit(solution)/shard_map/ppermute | solution.py:673
  8.9 25.2 %collective-permute-start.8 = (bf16[192,2880]{1,0:T(8,128)(2,1)}, bf16[192,2880]{1,0:T(8,128)(2,1)S(1)}, u32[]{:S(2)}, u32[]{:S(2)}) collective-permute-start(bf16[192,2880]{1,0:T(8,128)(2,1)} %bitcast.17), channel_id=1, source_target_pairs={{8,16},{12,20},{16,8},{20,12},{9,17},{13,21},{17,9},{21,13},{10,18... | collective-permute-start | bytes 3317768 | tf_op jit(solution)/shard_map/ppermute | solution.py:673
  16.6 12.6 %collective-permute-start.2 = (bf16[128,1536]{1,0:T(8,128)(2,1)S(1)}, bf16[128,1536]{1,0:T(8,128)(2,1)S(1)}, u32[]{:S(2)}, u32[]{:S(2)}) collective-permute-start(bf16[128,1536]{1,0:T(8,128)(2,1)S(1)} %hold.15.refs_1_.refs_2_), channel_id=1, source_target_pairs={{0,2},{1,3},{2,0},{3,1},{4,6},{5,7},{6,4},{7,5},{8,10},{9,11},{10,... | collective-permute-start | bytes 1179656 | tf_op jit(solution)/shard_map/ppermute | solution.py:663
  20.9 8.4 %collective-permute-start.4 = (bf16[128,1408]{1,0:T(8,128)(2,1)S(1)}, bf16[128,1408]{1,0:T(8,128)(2,1)S(1)}, u32[]{:S(2)}, u32[]{:S(2)}) collective-permute-start(bf16[128,1408]{1,0:T(8,128)(2,1)S(1)} %hold.16.refs_0_), channel_id=1, source_target_pairs={{0,4},{4,0},{8,12},{12,8},{16,20},{20,16},{24,28},{28,24},{1,5},{5... | collective-permute-start | bytes 1081352 | tf_op jit(solution)/shard_map/ppermute | solution.py:661
  30.1 11.3 %collective-permute-start.7 = (bf16[128,1408]{1,0:T(8,128)(2,1)S(1)}, bf16[128,1408]{1,0:T(8,128)(2,1)S(1)}, u32[]{:S(2)}, u32[]{:S(2)}) collective-permute-start(bf16[128,1408]{1,0:T(8,128)(2,1)S(1)} %hold.16.refs_0_), channel_id=1, source_target_pairs={{0,2},{1,3},{2,0},{3,1},{4,6},{5,7},{6,4},{7,5},{8,10},{9,11},{10,... | collective-permute-start | bytes 1081352 | tf_op jit(solution)/shard_map/ppermute | solution.py:663
  33.7 15.0 %collective-permute-start.11 = (bf16[128,1408]{1,0:T(8,128)(2,1)S(1)}, bf16[128,1408]{1,0:T(8,128)(2,1)S(1)}, u32[]{:S(2)}, u32[]{:S(2)}) collective-permute-start(bf16[128,1408]{1,0:T(8,128)(2,1)S(1)} %collective-permute-done.4.refs_4_.refs_1_), channel_id=1, source_target_pairs={{0,2},{1,3},{2,0},{3,1},{4,6},{5,7},{6,4},{7,5},{8,10},{9,11},{10,... | collective-permute-start | bytes 1081352 | tf_op jit(solution)/shard_map/ppermute | solution.py:663
  36.7 16.1 %collective-permute-start.15 = (bf16[192,1472]{1,0:T(8,128)(2,1)S(1)}, bf16[192,1472]{1,0:T(8,128)(2,1)S(1)}, u32[]{:S(2)}, u32[]{:S(2)}) collective-permute-start(bf16[192,1472]{1,0:T(8,128)(2,1)S(1)} %first_sums.2.refs_6_), channel_id=1, source_target_pairs={{0,8},{4,12},{8,0},{12,4},{16,24},{20,28},{24,16},{28,20},{1,9},{5... | collective-permute-start | bytes 1695752 | tf_op jit(solution)/shard_map/ppermute | solution.py:673
  39.2 27.1 %collective-permute-start.14 = (bf16[192,2880]{1,0:T(8,128)(2,1)S(1)}, bf16[192,2880]{1,0:T(8,128)(2,1)S(1)}, u32[]{:S(2)}, u32[]{:S(2)}) collective-permute-start(bf16[192,2880]{1,0:T(8,128)(2,1)S(1)} %hold.17.refs_1_.refs_12_), channel_id=1, source_target_pairs={{8,16},{12,20},{16,8},{20,12},{9,17},{13,21},{17,9},{21,13},{10,18... | collective-permute-start | bytes 3317768 | tf_op jit(solution)/shard_map/ppermute | solution.py:673
  39.9 15.2 %collective-permute-start.13 = (bf16[3,192,512]{2,1,0:T(8,128)(2,1)S(1)}, bf16[3,192,512]{2,1,0:T(8,128)(2,1)S(1)}, u32[]{:S(2)}, u32[]{:S(2)}) collective-permute-start(bf16[3,192,512]{2,1,0:T(8,128)(2,1)S(1)} %get-tuple-element.23), channel_id=1, source_target_pairs={{0,4},{4,0},{8,12},{12,8},{16,20},{20,16},{24,28},{28,24},{1,5},{5... | collective-permute-start | bytes 1769480 | tf_op jit(solution)/shard_map/ppermute | solution.py:661
  41.4 7.3 %collective-permute-start.10 = (bf16[128,1408]{1,0:T(8,128)(2,1)S(1)}, bf16[128,1408]{1,0:T(8,128)(2,1)S(1)}, u32[]{:S(2)}, u32[]{:S(2)}) collective-permute-start(bf16[128,1408]{1,0:T(8,128)(2,1)S(1)} %hold.19.refs_2_.refs_4_), channel_id=1, source_target_pairs={{0,1},{1,0},{2,3},{3,2},{4,5},{5,4},{6,7},{7,6},{8,9},{9,8},{10,11... | collective-permute-start | bytes 1081352 | tf_op jit(solution)/shard_map/ppermute | solution.py:663
  52.8 19.4 %collective-permute-start.18 = (bf16[192,1408]{1,0:T(8,128)(2,1)S(1)}, bf16[192,1408]{1,0:T(8,128)(2,1)S(1)}, u32[]{:S(2)}, u32[]{:S(2)}) collective-permute-start(bf16[192,1408]{1,0:T(8,128)(2,1)S(1)} %hold.23.refs_2_.refs_10_), channel_id=1, source_target_pairs={{0,8},{4,12},{8,0},{12,4},{16,24},{20,28},{24,16},{28,20},{1,9},{5... | collective-permute-start | bytes 1622024 | tf_op jit(solution)/shard_map/ppermute | solution.py:673
  60.4 22.3 %collective-permute-start.25 = (bf16[192,1472]{1,0:T(8,128)(2,1)S(1)}, bf16[192,1472]{1,0:T(8,128)(2,1)S(1)}, u32[]{:S(2)}, u32[]{:S(2)}) collective-permute-start(bf16[192,1472]{1,0:T(8,128)(2,1)S(1)} %combine.8.refs_1_), channel_id=1, source_target_pairs={{0,8},{4,12},{24,16},{28,20},{1,9},{5,13},{25,17},{29,21},{2,10},{... | collective-permute-start | bytes 1695752 | tf_op jit(solution)/shard_map/ppermute | solution.py:673
  65.0 20.8 %collective-permute-start.17 = (bf16[192,1472]{1,0:T(8,128)(2,1)S(1)}, bf16[192,1472]{1,0:T(8,128)(2,1)S(1)}, u32[]{:S(2)}, u32[]{:S(2)}) collective-permute-start(bf16[192,1472]{1,0:T(8,128)(2,1)S(1)} %combine.7.refs_6_), channel_id=1, source_target_pairs={{8,16},{12,20},{16,8},{20,12},{9,17},{13,21},{17,9},{21,13},{10,18... | collective-permute-start | bytes 1695752 | tf_op jit(solution)/shard_map/ppermute | solution.py:673
  66.3 32.8 %collective-permute-start.16 = (bf16[192,2880]{1,0:T(8,128)(2,1)S(1)}, bf16[192,2880]{1,0:T(8,128)(2,1)S(1)}, u32[]{:S(2)}, u32[]{:S(2)}) collective-permute-start(bf16[192,2880]{1,0:T(8,128)(2,1)S(1)} %hold.24.refs_10_.refs_13_), channel_id=1, source_target_pairs={{8,0},{12,4},{16,24},{20,28},{9,1},{13,5},{17,25},{21,29},{10,2},{... | collective-permute-start | bytes 3317768 | tf_op jit(solution)/shard_map/ppermute | solution.py:673
  73.0 13.6 %collective-permute-start.19 = (bf16[192,1408]{1,0:T(8,128)(2,1)S(1)}, bf16[192,1408]{1,0:T(8,128)(2,1)S(1)}, u32[]{:S(2)}, u32[]{:S(2)}) collective-permute-start(bf16[192,1408]{1,0:T(8,128)(2,1)S(1)} %combine.10.refs_11_), channel_id=1, source_target_pairs={{8,16},{12,20},{16,8},{20,12},{9,17},{13,21},{17,9},{21,13},{10,18... | collective-permute-start | bytes 1622024 | tf_op jit(solution)/shard_map/ppermute | solution.py:673
  73.7 21.2 %collective-permute-start.27 = (bf16[192,1408]{1,0:T(8,128)(2,1)S(1)}, bf16[192,1408]{1,0:T(8,128)(2,1)S(1)}, u32[]{:S(2)}, u32[]{:S(2)}) collective-permute-start(bf16[192,1408]{1,0:T(8,128)(2,1)S(1)} %combine.9.refs_2_), channel_id=1, source_target_pairs={{0,8},{4,12},{24,16},{28,20},{1,9},{5,13},{25,17},{29,21},{2,10},{... | collective-permute-start | bytes 1622024 | tf_op jit(solution)/shard_map/ppermute | solution.py:673
  82.7 13.1 %collective-permute-start.21 = (bf16[3,192,512]{2,1,0:T(8,128)(2,1)S(1)}, bf16[3,192,512]{2,1,0:T(8,128)(2,1)S(1)}, u32[]{:S(2)}, u32[]{:S(2)}) collective-permute-start(bf16[3,192,512]{2,1,0:T(8,128)(2,1)S(1)} %get-tuple-element.28), channel_id=1, source_target_pairs={{0,4},{4,0},{8,12},{12,8},{16,20},{20,16},{24,28},{28,24},{1,5},{5... | collective-permute-start | bytes 1769480 | tf_op jit(solution)/shard_map/ppermute | solution.py:661
  85.8 31.4 %collective-permute-start.26 = (bf16[192,1472]{1,0:T(8,128)(2,1)S(1)}, bf16[192,1472]{1,0:T(8,128)(2,1)S(1)}, u32[]{:S(2)}, u32[]{:S(2)}) collective-permute-start(bf16[192,1472]{1,0:T(8,128)(2,1)S(1)} %combine.12), channel_id=1, source_target_pairs={{8,16},{12,20},{16,8},{20,12},{9,17},{13,21},{17,9},{21,13},{10,18... | collective-permute-start | bytes 1695752 | tf_op jit(solution)/shard_map/ppermute | solution.py:673
  87.4 31.2 %collective-permute-start.24 = (bf16[192,2880]{1,0:T(8,128)(2,1)S(1)}, bf16[192,2880]{1,0:T(8,128)(2,1)S(1)}, u32[]{:S(2)}, u32[]{:S(2)}) collective-permute-start(bf16[192,2880]{1,0:T(8,128)(2,1)S(1)} %combine.11.refs_15_), channel_id=1, source_target_pairs={{0,8},{4,12},{8,0},{12,4},{16,24},{20,28},{24,16},{28,20},{1,9},{5... | collective-permute-start | bytes 3317768 | tf_op jit(solution)/shard_map/ppermute | solution.py:673
  95.8 22.9 %collective-permute-start.28 = (bf16[192,1408]{1,0:T(8,128)(2,1)S(1)}, bf16[192,1408]{1,0:T(8,128)(2,1)S(1)}, u32[]{:S(2)}, u32[]{:S(2)}) collective-permute-start(bf16[192,1408]{1,0:T(8,128)(2,1)S(1)} %hold.26), channel_id=1, source_target_pairs={{8,16},{12,20},{16,8},{20,12},{9,17},{13,21},{17,9},{21,13},{10,18... | collective-permute-start | bytes 1622024 | tf_op jit(solution)/shard_map/ppermute | solution.py:673
  103.6 10.7 %collective-permute-start.22 = (bf16[1,192,512]{2,1,0:T(8,128)(2,1)S(1)}, bf16[1,192,512]{2,1,0:T(8,128)(2,1)S(1)}, u32[]{:S(2)}, u32[]{:S(2)}) collective-permute-start(bf16[1,192,512]{2,1,0:T(8,128)(2,1)S(1)} %get-tuple-element.30), channel_id=1, source_target_pairs={{0,4},{4,0},{8,12},{12,8},{16,20},{20,16},{24,28},{28,24},{1,5},{5... | collective-permute-start | bytes 589832 | tf_op jit(solution)/shard_map/ppermute | solution.py:661
  105.6 8.8 %collective-permute-start.23 = (bf16[1,192,512]{2,1,0:T(8,128)(2,1)S(1)}, bf16[1,192,512]{2,1,0:T(8,128)(2,1)S(1)}, u32[]{:S(2)}, u32[]{:S(2)}) collective-permute-start(bf16[1,192,512]{2,1,0:T(8,128)(2,1)S(1)} %get-tuple-element.32), channel_id=1, source_target_pairs={{0,4},{4,0},{8,12},{12,8},{16,20},{20,16},{24,28},{28,24},{1,5},{5... | collective-permute-start | bytes 589832 | tf_op jit(solution)/shard_map/ppermute | solution.py:661
  (13 other events, 77.4 us)

commit v16 on v15

--- a/solution.py
+++ b/solution.py
@@ -581,7 +581,8 @@
 
 
 def join_kernel(table, choices, where_ref, *refs):
-    out_ref, turned, sem = refs[-3:]
+    out_ref, done_ref, turned, sem = refs[-4:]
+    done_ref[...] = jnp.zeros(done_ref.shape, f32)
     slots, width = turned.shape[1:]
     row = lax.broadcasted_iota(jnp.int32, (slots, slots), 0)
     column = lax.broadcasted_iota(jnp.int32, (slots, slots), 1)
@@ -590,7 +591,7 @@
     copies = []
     pairs = [
         (refs[2 * group][place], refs[2 * group + 1][place])
-        for group in range((len(refs) - 3) // 2)
+        for group in range((len(refs) - 4) // 2)
         for place in range(refs[2 * group].shape[0])
     ]
     for place, (choice, (mine, theirs)) in enumerate(zip(choices, pairs)):
@@ -611,9 +612,12 @@
     units = halves[0].shape[1]
     return pl.pallas_call(
         functools.partial(join_kernel, table, choices),
-        out_shape=jax.ShapeDtypeStruct((slots, hidden), bf16),
+        out_shape=(
+            jax.ShapeDtypeStruct((slots, hidden), bf16),
+            jax.ShapeDtypeStruct((8, LANES), f32),
+        ),
         in_specs=[scalars()] + [whole()] * len(halves),
-        out_specs=anywhere(),
+        out_specs=(anywhere(), whole()),
         scratch_shapes=[
             pltpu.VMEM((len(choices), slots, 2 * units), bf16),
             pltpu.SemaphoreType.DMA((len(choices),)),
@@ -818,9 +822,9 @@
         slot_grad.reshape(experts, tokens), "exp", split_axis=0, concat_axis=0, tiled=True
     )
     logit_grad = logits_grad(gates, expert_ids.T, grads)
-    hidden_grad = join_hidden(table, where, all_choices, halves, slots, hidden)
+    hidden_grad, joined = join_hidden(table, where, all_choices, halves, slots, hidden)
     if apart:
-        entered = list(hold(got[depth, "B"][:1], [hidden_grad], ENTER_WEIGHT))
+        entered = list(hold(got[depth, "B"][:1], [joined], ENTER_WEIGHT))
         got[depth, "B"] = entered + list(hold(got[depth, "B"][1:], entered, CLOSE_WEIGHT))
     weight_grad = total_grad(got[depth, "A"], got[depth, "B"], rest, cut)
     return (logit_grad.T, hidden_grad[None, None], weight_grad)

time: 121 us -> 120 us (level)
  local copies, waits for them, and re-layouts: 4.53 us -> 3.13 us
    unnamed x16 -> x14, local copies, waits for them, and re-layouts: 3.83 us -> 2.43 us
  transfers between devices with their start and end apart: 29 -> 29, of which waited for: 12 -> 13; matrix products, arithmetic and copies ran while one was open for 1% -> 1% of each run, Pallas kernels for 30% -> 30%
where the time goes in v16:
time: 120 us
  starting transfers between devices  43.2 us (36%)
  Pallas kernels  39.3 us (33%)
  waiting for transfers between devices  26.8 us (22%)
  blocking collectives  6.41 us (5%)
  local copies, waits for them, and re-layouts  3.13 us (3%)
    ppermute x13, starting transfers between devices, swap_z(): return lax.ppermute(value, 'ctx', pairs)  28.1 us
    ppermute x8, waiting for transfers between devices, swap(): return lax.ppermute(value, 'ctx', [(i, i ^ x) for i in range(groups)])  12.5 us
    ppermute x8, waiting for transfers between devices, swap(): return lax.ppermute(value, 'exp', [(i, i ^ exp) for i in range(experts)])  10.6 us
    ppermute x8, starting transfers between devices, swap(): return lax.ppermute(value, 'ctx', [(i, i ^ x) for i in range(groups)])  10.4 us
    pallas_call x3, Pallas kernels, back_part(): pl.pallas_call(functools.partial(back_kernel, table, model, cut, counts,...  9.98 us
    pallas_call x5, Pallas kernels, products(): pl.pallas_call(functools.partial(products_kernel, table, model, counts, p...  9.45 us
    all_to_all x1, blocking collectives, per_device_full(): lax.all_to_all(slot_grad.reshape(experts, tokens), 'exp', split_axis=0, c...  6.41 us
    pallas_call x7, Pallas kernels, combine(): pl.pallas_call(functools.partial(combine_kernel, table, ('use', turn, nam...  5.11 us
  transfers between devices with their start and end apart: 29, of which 13 were waited for; matrix products, arithmetic and copies ran while one was open for 1% of the time, Pallas kernels for 30%

profile of v16, /device:TPU:0, one launch (start us, length us, event | category | flops | bytes accessed | tf_op | source)
XLA Modules:
  0.0 119.9 jit_solution(2926067736492027106)
XLA Ops:
  0.6 2.2 %make_rows.1 = (bf16[128,1536]{1,0:T(8,128)(2,1)}, bf16[128,1408]{1,0:T(8,128)(2,1)}, f32[4,128]{1,0:T(4,128)}) custom-call(bf16[2880,128]{1,0:T(8,128)(2,1)} %bitcast.21, f32[4,128]{1,0:T(4,128)} %bitcast.22, s32[4,128]{1,0:T(4,128)} %bitcast.18), custom_call_target="tpu_custom_call" | custom-call | flops 2000000 | bytes 6000000 | tf_op jit(solution)/shard_map/make_rows/pallas_call | solution.py:169
  2.8 3.0 %collective-permute-start.1 = (bf16[128,1536]{1,0:T(8,128)(2,1)}, bf16[128,1536]{1,0:T(8,128)(2,1)S(1)}, u32[]{:S(2)}, u32[]{:S(2)}) collective-permute-start(bf16[128,1536]{1,0:T(8,128)(2,1)} %get-tuple-element.21.refs_0_), channel_id=1, source_target_pairs={{0,4},{4,0},{8,12},{12,8},{16,20},{20,16},{24,28},{28,24},{1,5},{5... | collective-permute-start | bytes 1179656 | tf_op jit(solution)/shard_map/ppermute | solution.py:665
  12.8 2.2 %split_hidden.1 = (bf16[4,192,512]{2,1,0:T(8,128)(2,1)S(1)}, bf16[1,192,512]{2,1,0:T(8,128)(2,1)S(1)}, bf16[3,192,512]{2,1,0:T(8,128)(2,1)S(1)}) custom-call(s32[32]{0:T(128)S(1)} %dynamic-slice_bitcast_fusion.where_ref, bf16[512,1536]{1,0:T(8,128)(2,1)S(1)} %bitcast.14, bf16[128,1536]{1,0:T(8,128)(2,1)S(1)} %copy-done.1), custom_call_target="tpu_custom_call" | custom-call | flops 2000000 | bytes 6000000 | tf_op jit(solution)/shard_map/split_hidden/pallas_call | solution.py:260
  18.1 2.7 %collective-permute-done.3.refs_2_.refs_5_.refs_9_ = bf16[1,192,512]{2,1,0:T(8,128)(2,1)S(1)} collective-permute-done((bf16[1,192,512]{2,1,0:T(8,128)(2,1)S(1)}, bf16[1,192,512]{2,1,0:T(8,128)(2,1)S(1)}, u32[]{:S(2)}, u32[]{:S(2)}) %collective-permute-start.3) | collective-permute-done | bytes 196640 | tf_op jit(solution)/shard_map/ppermute | solution.py:665
  21.4 7.8 %collective-permute-done.4.refs_4_.refs_1_ = bf16[128,1408]{1,0:T(8,128)(2,1)S(1)} collective-permute-done((bf16[128,1408]{1,0:T(8,128)(2,1)S(1)}, bf16[128,1408]{1,0:T(8,128)(2,1)S(1)}, u32[]{:S(2)}, u32[]{:S(2)}) %collective-permute-start.4) | collective-permute-done | bytes 360480 | tf_op jit(solution)/shard_map/ppermute | solution.py:665
  31.5 2.2 %collective-permute-done.9.refs_0_ = bf16[192,2880]{1,0:T(8,128)(2,1)S(1)} collective-permute-done((bf16[192,2880]{1,0:T(8,128)(2,1)}, bf16[192,2880]{1,0:T(8,128)(2,1)S(1)}, u32[]{:S(2)}, u32[]{:S(2)}) %collective-permute-start.9) | collective-permute-done | bytes 1105952 | tf_op jit(solution)/shard_map/ppermute | solution.py:677
  34.5 2.2 %first_sums.2.refs_6_ = bf16[192,1472]{1,0:T(8,128)(2,1)S(1)} custom-call(s32[32]{0:T(128)S(1)} %dynamic-slice_bitcast_fusion.where_ref, bf16[4,128,1536]{2,1,0:T(8,128)(2,1)S(1)} %pack_rows.2.refs_0_.refs_2_.refs_6_, bf16[4,128,1536]{2,1,0:T(8,128)(2,1)S(1)} %collective-permute-done.5.refs_1_.refs_3_.refs_7_, ...), custom_call_target="tpu_custom_call" | custom-call | flops 1000000 | bytes 3000000 | tf_op jit(solution)/shard_map/first_sums/pallas_call | solution.py:371
  36.7 2.5 %collective-permute-start.15 = (bf16[192,1472]{1,0:T(8,128)(2,1)S(1)}, bf16[192,1472]{1,0:T(8,128)(2,1)S(1)}, u32[]{:S(2)}, u32[]{:S(2)}) collective-permute-start(bf16[192,1472]{1,0:T(8,128)(2,1)S(1)} %first_sums.2.refs_6_), channel_id=1, source_target_pairs={{0,8},{4,12},{8,0},{12,4},{16,24},{20,28},{24,16},{28,20},{1,9},{5... | collective-permute-start | bytes 1695752 | tf_op jit(solution)/shard_map/ppermute | solution.py:677
  41.4 7.3 %collective-permute-done.11.refs_0_ = bf16[128,1408]{1,0:T(8,128)(2,1)S(1)} collective-permute-done((bf16[128,1408]{1,0:T(8,128)(2,1)S(1)}, bf16[128,1408]{1,0:T(8,128)(2,1)S(1)}, u32[]{:S(2)}, u32[]{:S(2)}) %collective-permute-start.11) | collective-permute-done | bytes 360480 | tf_op jit(solution)/shard_map/ppermute | solution.py:667
  50.3 2.1 %first_sums.3.refs_0_ = bf16[192,1408]{1,0:T(8,128)(2,1)S(1)} custom-call(s32[32]{0:T(128)S(1)} %dynamic-slice_bitcast_fusion.where_ref, bf16[2,128,1408]{2,1,0:T(8,128)(2,1)S(1)} %pack_rows.3.refs_0_.refs_2_, bf16[2,128,1408]{2,1,0:T(8,128)(2,1)S(1)} %collective-permute-done.6.refs_7_.refs_1_.refs_3_, bf16[128,1408]{1,0:T(8,128)(2,1)S(1)} %hold.19.refs_2_.refs_4_, ...), custom_call_target="tpu_custom_call" | custom-call | flops 1000000 | bytes 3000000 | tf_op jit(solution)/shard_map/first_sums/pallas_call | solution.py:371
  52.8 2.2 %collective-permute-start.18 = (bf16[192,1408]{1,0:T(8,128)(2,1)S(1)}, bf16[192,1408]{1,0:T(8,128)(2,1)S(1)}, u32[]{:S(2)}, u32[]{:S(2)}) collective-permute-start(bf16[192,1408]{1,0:T(8,128)(2,1)S(1)} %hold.23.refs_2_.refs_10_), channel_id=1, source_target_pairs={{0,8},{4,12},{8,0},{12,4},{16,24},{20,28},{24,16},{28,20},{1,9},{5... | collective-permute-start | bytes 1622024 | tf_op jit(solution)/shard_map/ppermute | solution.py:677
  55.8 3.9 %rest_kept.3.refs_0_.refs_1_.refs_2_.refs_3_ = f32[3,192,1472]{2,1,0:T(8,128)S(1)} custom-call(s32[32]{0:T(128)S(1)} %dynamic-slice_bitcast_fusion.where_ref, bf16[4,128,1536]{2,1,0:T(8,128)(2,1)S(1)} %pack_rows.2.refs_0_.refs_2_.refs_6_, bf16[4,128,1536]{2,1,0:T(8,128)(2,1)S(1)} %collective-permute-done.5.refs_1_.refs_3_.refs_7_, ...), custom_call_target="tpu_custom_call" | custom-call | flops 1000000 | bytes 3000000 | tf_op jit(solution)/shard_map/rest_kept/pallas_call | solution.py:330
  60.4 4.6 %collective-permute-start.25 = (bf16[192,1472]{1,0:T(8,128)(2,1)S(1)}, bf16[192,1472]{1,0:T(8,128)(2,1)S(1)}, u32[]{:S(2)}, u32[]{:S(2)}) collective-permute-start(bf16[192,1472]{1,0:T(8,128)(2,1)S(1)} %combine.8.refs_1_), channel_id=1, source_target_pairs={{0,8},{4,12},{24,16},{28,20},{1,9},{5,13},{25,17},{29,21},{2,10},{... | collective-permute-start | bytes 1695752 | tf_op jit(solution)/shard_map/ppermute | solution.py:677
  67.6 3.9 %rest_kept.4.refs_0_.refs_2_.refs_10_ = f32[3,192,1408]{2,1,0:T(8,128)S(1)} custom-call(s32[32]{0:T(128)S(1)} %dynamic-slice_bitcast_fusion.where_ref, bf16[2,128,1408]{2,1,0:T(8,128)(2,1)S(1)} %pack_rows.3.refs_0_.refs_2_, bf16[2,128,1408]{2,1,0:T(8,128)(2,1)S(1)} %collective-permute-done.6.refs_7_.refs_1_.refs_3_, ...), custom_call_target="tpu_custom_call" | custom-call | flops 1000000 | bytes 3000000 | tf_op jit(solution)/shard_map/rest_kept/pallas_call | solution.py:330
  73.7 4.3 %collective-permute-start.27 = (bf16[192,1408]{1,0:T(8,128)(2,1)S(1)}, bf16[192,1408]{1,0:T(8,128)(2,1)S(1)}, u32[]{:S(2)}, u32[]{:S(2)}) collective-permute-start(bf16[192,1408]{1,0:T(8,128)(2,1)S(1)} %combine.9.refs_2_), channel_id=1, source_target_pairs={{0,8},{4,12},{24,16},{28,20},{1,9},{5,13},{25,17},{29,21},{2,10},{... | collective-permute-start | bytes 1622024 | tf_op jit(solution)/shard_map/ppermute | solution.py:677
  78.0 4.7 %back_part.3 = (bf16[3,192,512]{2,1,0:T(8,128)(2,1)S(1)}, bf16[3,192,512]{2,1,0:T(8,128)(2,1)S(1)}, f32[8,1024]{1,0:T(8,128)S(1)}) custom-call(s32[32]{0:T(128)S(1)} %dynamic-slice_bitcast_fusion.where_ref, bf16[4,128,1536]{2,1,0:T(8,128)(2,1)S(1)} %pack_rows.2.refs_0_.refs_2_.refs_6_, ...), custom_call_target="tpu_custom_call" | custom-call | flops 6000000 | bytes 18000000 | tf_op jit(solution)/shard_map/back_part/pallas_call | solution.py:570
  82.7 1.8 %collective-permute-start.21 = (bf16[3,192,512]{2,1,0:T(8,128)(2,1)S(1)}, bf16[3,192,512]{2,1,0:T(8,128)(2,1)S(1)}, u32[]{:S(2)}, u32[]{:S(2)}) collective-permute-start(bf16[3,192,512]{2,1,0:T(8,128)(2,1)S(1)} %get-tuple-element.30), channel_id=1, source_target_pairs={{0,4},{4,0},{8,12},{12,8},{16,20},{20,16},{24,28},{28,24},{1,5},{5... | collective-permute-start | bytes 1769480 | tf_op jit(solution)/shard_map/ppermute | solution.py:665
  87.4 7.4 %collective-permute-start.24 = (bf16[192,2880]{1,0:T(8,128)(2,1)S(1)}, bf16[192,2880]{1,0:T(8,128)(2,1)S(1)}, u32[]{:S(2)}, u32[]{:S(2)}) collective-permute-start(bf16[192,2880]{1,0:T(8,128)(2,1)S(1)} %combine.11.refs_15_), channel_id=1, source_target_pairs={{0,8},{4,12},{8,0},{12,4},{16,24},{20,28},{24,16},{28,20},{1,9},{5... | collective-permute-start | bytes 3317768 | tf_op jit(solution)/shard_map/ppermute | solution.py:677
  96.5 2.6 %back_part.4 = (bf16[1,192,512]{2,1,0:T(8,128)(2,1)S(1)}, bf16[1,192,512]{2,1,0:T(8,128)(2,1)S(1)}, f32[8,1024]{1,0:T(8,128)S(1)}) custom-call(s32[32]{0:T(128)S(1)} %dynamic-slice_bitcast_fusion.where_ref, bf16[4,128,1536]{2,1,0:T(8,128)(2,1)S(1)} %pack_rows.2.refs_0_.refs_2_.refs_6_, ...), custom_call_target="tpu_custom_call" | custom-call | flops 6000000 | bytes 18000000 | tf_op jit(solution)/shard_map/back_part/pallas_call | solution.py:570
  99.2 2.7 %back_part.5 = (bf16[1,192,512]{2,1,0:T(8,128)(2,1)S(1)}, bf16[1,192,512]{2,1,0:T(8,128)(2,1)S(1)}, f32[8,1024]{1,0:T(8,128)S(1)}) custom-call(s32[32]{0:T(128)S(1)} %dynamic-slice_bitcast_fusion.where_ref, bf16[4,128,1536]{2,1,0:T(8,128)(2,1)S(1)} %pack_rows.2.refs_0_.refs_2_.refs_6_, ...), custom_call_target="tpu_custom_call" | custom-call | flops 6000000 | bytes 18000000 | tf_op jit(solution)/shard_map/back_part/pallas_call | solution.py:570
  101.8 1.8 %collective-permute-start.20 = (f32[1,512]{1,0:T(1,128)S(1)}, f32[1,512]{1,0:T(1,128)S(1)}, u32[]{:S(2)}, u32[]{:S(2)}) collective-permute-start(f32[1,512]{1,0:T(1,128)S(1)} %slice.7), channel_id=1, source_target_pairs={{0,4},{4,0},{8,12},{12,8},{16,20},{20,16},{24,28},{28,24},{1,5},{5... | collective-permute-start | bytes 6152 | tf_op jit(solution)/shard_map/ppermute | solution.py:665
  105.6 1.7 %collective-permute-start.23 = (bf16[1,192,512]{2,1,0:T(8,128)(2,1)S(1)}, bf16[1,192,512]{2,1,0:T(8,128)(2,1)S(1)}, u32[]{:S(2)}, u32[]{:S(2)}) collective-permute-start(bf16[1,192,512]{2,1,0:T(8,128)(2,1)S(1)} %get-tuple-element.34), channel_id=1, source_target_pairs={{0,4},{4,0},{8,12},{12,8},{16,20},{20,16},{24,28},{28,24},{1,5},{5... | collective-permute-start | bytes 589832 | tf_op jit(solution)/shard_map/ppermute | solution.py:665
  107.3 6.4 %all_to_all.11 = f32[4,1,128]{2,1,0:T(1,128)S(1)} all-to-all(f32[4,1,128]{2,1,0:T(1,128)S(1)} %add_bitcast_fusion), channel_id=1, replica_groups=mesh['ctx'=8,'exp'=4] {'exp'}, dimensions={0} | all-to-all | bytes 4096 | tf_op jit(solution)/shard_map/all_to_all | solution.py:821
  114.3 2.9 %join_hidden.1 = (bf16[512,1536]{1,0:T(8,128)(2,1)}, f32[8,128]{1,0:T(8,128)S(1)}) custom-call(s32[32]{0:T(128)S(1)} %dynamic-slice_bitcast_fusion.where_ref, bf16[3,192,512]{2,1,0:T(8,128)(2,1)S(1)} %get-tuple-element.29.refs_0_, bf16[3,192,512]{2,1,0:T(8,128)(2,1)S(1)} %collective-permute-done.21.refs_1_, ...), custom_call_target="tpu_custom_call" | custom-call | flops 2000000 | bytes 6000000 | tf_op jit(solution)/shard_map/join_hidden/pallas_call | solution.py:613
  (90 shorter events, 33.8 us)
Async XLA Ops:
  2.8 12.8 %collective-permute-start.1 = (bf16[128,1536]{1,0:T(8,128)(2,1)}, bf16[128,1536]{1,0:T(8,128)(2,1)S(1)}, u32[]{:S(2)}, u32[]{:S(2)}) collective-permute-start(bf16[128,1536]{1,0:T(8,128)(2,1)} %get-tuple-element.21.refs_0_), channel_id=1, source_target_pairs={{0,4},{4,0},{8,12},{12,8},{16,20},{20,16},{24,28},{28,24},{1,5},{5... | collective-permute-start | bytes 1179656 | tf_op jit(solution)/shard_map/ppermute | solution.py:665
  5.8 10.8 %collective-permute-start = (bf16[128,1536]{1,0:T(8,128)(2,1)}, bf16[128,1536]{1,0:T(8,128)(2,1)S(1)}, u32[]{:S(2)}, u32[]{:S(2)}) collective-permute-start(bf16[128,1536]{1,0:T(8,128)(2,1)} %get-tuple-element.21.refs_0_), channel_id=1, source_target_pairs={{0,2},{1,3},{2,0},{3,1},{4,6},{5,7},{6,4},{7,5},{8,10},{9,11},{10,... | collective-permute-start | bytes 1179656 | tf_op jit(solution)/shard_map/ppermute | solution.py:667
  7.4 26.3 %collective-permute-start.9 = (bf16[192,2880]{1,0:T(8,128)(2,1)}, bf16[192,2880]{1,0:T(8,128)(2,1)S(1)}, u32[]{:S(2)}, u32[]{:S(2)}) collective-permute-start(bf16[192,2880]{1,0:T(8,128)(2,1)} %bitcast.15), channel_id=1, source_target_pairs={{0,8},{4,12},{8,0},{12,4},{16,24},{20,28},{24,16},{28,20},{1,9},{5... | collective-permute-start | bytes 3317768 | tf_op jit(solution)/shard_map/ppermute | solution.py:677
  8.9 25.2 %collective-permute-start.8 = (bf16[192,2880]{1,0:T(8,128)(2,1)}, bf16[192,2880]{1,0:T(8,128)(2,1)S(1)}, u32[]{:S(2)}, u32[]{:S(2)}) collective-permute-start(bf16[192,2880]{1,0:T(8,128)(2,1)} %bitcast.16), channel_id=1, source_target_pairs={{8,16},{12,20},{16,8},{20,12},{9,17},{13,21},{17,9},{21,13},{10,18... | collective-permute-start | bytes 3317768 | tf_op jit(solution)/shard_map/ppermute | solution.py:677
  16.6 12.6 %collective-permute-start.2 = (bf16[128,1536]{1,0:T(8,128)(2,1)S(1)}, bf16[128,1536]{1,0:T(8,128)(2,1)S(1)}, u32[]{:S(2)}, u32[]{:S(2)}) collective-permute-start(bf16[128,1536]{1,0:T(8,128)(2,1)S(1)} %hold.15.refs_1_.refs_2_), channel_id=1, source_target_pairs={{0,2},{1,3},{2,0},{3,1},{4,6},{5,7},{6,4},{7,5},{8,10},{9,11},{10,... | collective-permute-start | bytes 1179656 | tf_op jit(solution)/shard_map/ppermute | solution.py:667
  20.9 8.4 %collective-permute-start.4 = (bf16[128,1408]{1,0:T(8,128)(2,1)S(1)}, bf16[128,1408]{1,0:T(8,128)(2,1)S(1)}, u32[]{:S(2)}, u32[]{:S(2)}) collective-permute-start(bf16[128,1408]{1,0:T(8,128)(2,1)S(1)} %hold.16.refs_0_), channel_id=1, source_target_pairs={{0,4},{4,0},{8,12},{12,8},{16,20},{20,16},{24,28},{28,24},{1,5},{5... | collective-permute-start | bytes 1081352 | tf_op jit(solution)/shard_map/ppermute | solution.py:665
  30.1 11.3 %collective-permute-start.7 = (bf16[128,1408]{1,0:T(8,128)(2,1)S(1)}, bf16[128,1408]{1,0:T(8,128)(2,1)S(1)}, u32[]{:S(2)}, u32[]{:S(2)}) collective-permute-start(bf16[128,1408]{1,0:T(8,128)(2,1)S(1)} %hold.16.refs_0_), channel_id=1, source_target_pairs={{0,2},{1,3},{2,0},{3,1},{4,6},{5,7},{6,4},{7,5},{8,10},{9,11},{10,... | collective-permute-start | bytes 1081352 | tf_op jit(solution)/shard_map/ppermute | solution.py:667
  33.7 15.0 %collective-permute-start.11 = (bf16[128,1408]{1,0:T(8,128)(2,1)S(1)}, bf16[128,1408]{1,0:T(8,128)(2,1)S(1)}, u32[]{:S(2)}, u32[]{:S(2)}) collective-permute-start(bf16[128,1408]{1,0:T(8,128)(2,1)S(1)} %collective-permute-done.4.refs_4_.refs_1_), channel_id=1, source_target_pairs={{0,2},{1,3},{2,0},{3,1},{4,6},{5,7},{6,4},{7,5},{8,10},{9,11},{10,... | collective-permute-start | bytes 1081352 | tf_op jit(solution)/shard_map/ppermute | solution.py:667
  36.7 16.1 %collective-permute-start.15 = (bf16[192,1472]{1,0:T(8,128)(2,1)S(1)}, bf16[192,1472]{1,0:T(8,128)(2,1)S(1)}, u32[]{:S(2)}, u32[]{:S(2)}) collective-permute-start(bf16[192,1472]{1,0:T(8,128)(2,1)S(1)} %first_sums.2.refs_6_), channel_id=1, source_target_pairs={{0,8},{4,12},{8,0},{12,4},{16,24},{20,28},{24,16},{28,20},{1,9},{5... | collective-permute-start | bytes 1695752 | tf_op jit(solution)/shard_map/ppermute | solution.py:677
  39.2 27.1 %collective-permute-start.14 = (bf16[192,2880]{1,0:T(8,128)(2,1)S(1)}, bf16[192,2880]{1,0:T(8,128)(2,1)S(1)}, u32[]{:S(2)}, u32[]{:S(2)}) collective-permute-start(bf16[192,2880]{1,0:T(8,128)(2,1)S(1)} %hold.17.refs_1_.refs_12_), channel_id=1, source_target_pairs={{8,16},{12,20},{16,8},{20,12},{9,17},{13,21},{17,9},{21,13},{10,18... | collective-permute-start | bytes 3317768 | tf_op jit(solution)/shard_map/ppermute | solution.py:677
  39.9 15.2 %collective-permute-start.13 = (bf16[3,192,512]{2,1,0:T(8,128)(2,1)S(1)}, bf16[3,192,512]{2,1,0:T(8,128)(2,1)S(1)}, u32[]{:S(2)}, u32[]{:S(2)}) collective-permute-start(bf16[3,192,512]{2,1,0:T(8,128)(2,1)S(1)} %get-tuple-element.25), channel_id=1, source_target_pairs={{0,4},{4,0},{8,12},{12,8},{16,20},{20,16},{24,28},{28,24},{1,5},{5... | collective-permute-start | bytes 1769480 | tf_op jit(solution)/shard_map/ppermute | solution.py:665
  41.4 7.3 %collective-permute-start.10 = (bf16[128,1408]{1,0:T(8,128)(2,1)S(1)}, bf16[128,1408]{1,0:T(8,128)(2,1)S(1)}, u32[]{:S(2)}, u32[]{:S(2)}) collective-permute-start(bf16[128,1408]{1,0:T(8,128)(2,1)S(1)} %hold.19.refs_2_.refs_4_), channel_id=1, source_target_pairs={{0,1},{1,0},{2,3},{3,2},{4,5},{5,4},{6,7},{7,6},{8,9},{9,8},{10,11... | collective-permute-start | bytes 1081352 | tf_op jit(solution)/shard_map/ppermute | solution.py:667
  52.8 19.4 %collective-permute-start.18 = (bf16[192,1408]{1,0:T(8,128)(2,1)S(1)}, bf16[192,1408]{1,0:T(8,128)(2,1)S(1)}, u32[]{:S(2)}, u32[]{:S(2)}) collective-permute-start(bf16[192,1408]{1,0:T(8,128)(2,1)S(1)} %hold.23.refs_2_.refs_10_), channel_id=1, source_target_pairs={{0,8},{4,12},{8,0},{12,4},{16,24},{20,28},{24,16},{28,20},{1,9},{5... | collective-permute-start | bytes 1622024 | tf_op jit(solution)/shard_map/ppermute | solution.py:677
  60.4 22.3 %collective-permute-start.25 = (bf16[192,1472]{1,0:T(8,128)(2,1)S(1)}, bf16[192,1472]{1,0:T(8,128)(2,1)S(1)}, u32[]{:S(2)}, u32[]{:S(2)}) collective-permute-start(bf16[192,1472]{1,0:T(8,128)(2,1)S(1)} %combine.8.refs_1_), channel_id=1, source_target_pairs={{0,8},{4,12},{24,16},{28,20},{1,9},{5,13},{25,17},{29,21},{2,10},{... | collective-permute-start | bytes 1695752 | tf_op jit(solution)/shard_map/ppermute | solution.py:677
  65.0 20.8 %collective-permute-start.17 = (bf16[192,1472]{1,0:T(8,128)(2,1)S(1)}, bf16[192,1472]{1,0:T(8,128)(2,1)S(1)}, u32[]{:S(2)}, u32[]{:S(2)}) collective-permute-start(bf16[192,1472]{1,0:T(8,128)(2,1)S(1)} %combine.7.refs_6_), channel_id=1, source_target_pairs={{8,16},{12,20},{16,8},{20,12},{9,17},{13,21},{17,9},{21,13},{10,18... | collective-permute-start | bytes 1695752 | tf_op jit(solution)/shard_map/ppermute | solution.py:677
  66.3 32.8 %collective-permute-start.16 = (bf16[192,2880]{1,0:T(8,128)(2,1)S(1)}, bf16[192,2880]{1,0:T(8,128)(2,1)S(1)}, u32[]{:S(2)}, u32[]{:S(2)}) collective-permute-start(bf16[192,2880]{1,0:T(8,128)(2,1)S(1)} %hold.24.refs_10_.refs_13_), channel_id=1, source_target_pairs={{8,0},{12,4},{16,24},{20,28},{9,1},{13,5},{17,25},{21,29},{10,2},{... | collective-permute-start | bytes 3317768 | tf_op jit(solution)/shard_map/ppermute | solution.py:677
  73.0 13.6 %collective-permute-start.19 = (bf16[192,1408]{1,0:T(8,128)(2,1)S(1)}, bf16[192,1408]{1,0:T(8,128)(2,1)S(1)}, u32[]{:S(2)}, u32[]{:S(2)}) collective-permute-start(bf16[192,1408]{1,0:T(8,128)(2,1)S(1)} %combine.10.refs_11_), channel_id=1, source_target_pairs={{8,16},{12,20},{16,8},{20,12},{9,17},{13,21},{17,9},{21,13},{10,18... | collective-permute-start | bytes 1622024 | tf_op jit(solution)/shard_map/ppermute | solution.py:677
  73.7 21.2 %collective-permute-start.27 = (bf16[192,1408]{1,0:T(8,128)(2,1)S(1)}, bf16[192,1408]{1,0:T(8,128)(2,1)S(1)}, u32[]{:S(2)}, u32[]{:S(2)}) collective-permute-start(bf16[192,1408]{1,0:T(8,128)(2,1)S(1)} %combine.9.refs_2_), channel_id=1, source_target_pairs={{0,8},{4,12},{24,16},{28,20},{1,9},{5,13},{25,17},{29,21},{2,10},{... | collective-permute-start | bytes 1622024 | tf_op jit(solution)/shard_map/ppermute | solution.py:677
  82.7 13.1 %collective-permute-start.21 = (bf16[3,192,512]{2,1,0:T(8,128)(2,1)S(1)}, bf16[3,192,512]{2,1,0:T(8,128)(2,1)S(1)}, u32[]{:S(2)}, u32[]{:S(2)}) collective-permute-start(bf16[3,192,512]{2,1,0:T(8,128)(2,1)S(1)} %get-tuple-element.30), channel_id=1, source_target_pairs={{0,4},{4,0},{8,12},{12,8},{16,20},{20,16},{24,28},{28,24},{1,5},{5... | collective-permute-start | bytes 1769480 | tf_op jit(solution)/shard_map/ppermute | solution.py:665
  85.8 31.4 %collective-permute-start.26 = (bf16[192,1472]{1,0:T(8,128)(2,1)S(1)}, bf16[192,1472]{1,0:T(8,128)(2,1)S(1)}, u32[]{:S(2)}, u32[]{:S(2)}) collective-permute-start(bf16[192,1472]{1,0:T(8,128)(2,1)S(1)} %combine.12), channel_id=1, source_target_pairs={{8,16},{12,20},{16,8},{20,12},{9,17},{13,21},{17,9},{21,13},{10,18... | collective-permute-start | bytes 1695752 | tf_op jit(solution)/shard_map/ppermute | solution.py:677
  87.4 31.0 %collective-permute-start.24 = (bf16[192,2880]{1,0:T(8,128)(2,1)S(1)}, bf16[192,2880]{1,0:T(8,128)(2,1)S(1)}, u32[]{:S(2)}, u32[]{:S(2)}) collective-permute-start(bf16[192,2880]{1,0:T(8,128)(2,1)S(1)} %combine.11.refs_15_), channel_id=1, source_target_pairs={{0,8},{4,12},{8,0},{12,4},{16,24},{20,28},{24,16},{28,20},{1,9},{5... | collective-permute-start | bytes 3317768 | tf_op jit(solution)/shard_map/ppermute | solution.py:677
  95.8 21.4 %collective-permute-start.28 = (bf16[192,1408]{1,0:T(8,128)(2,1)S(1)}, bf16[192,1408]{1,0:T(8,128)(2,1)S(1)}, u32[]{:S(2)}, u32[]{:S(2)}) collective-permute-start(bf16[192,1408]{1,0:T(8,128)(2,1)S(1)} %hold.26), channel_id=1, source_target_pairs={{8,16},{12,20},{16,8},{20,12},{9,17},{13,21},{17,9},{21,13},{10,18... | collective-permute-start | bytes 1622024 | tf_op jit(solution)/shard_map/ppermute | solution.py:677
  103.7 10.7 %collective-permute-start.22 = (bf16[1,192,512]{2,1,0:T(8,128)(2,1)S(1)}, bf16[1,192,512]{2,1,0:T(8,128)(2,1)S(1)}, u32[]{:S(2)}, u32[]{:S(2)}) collective-permute-start(bf16[1,192,512]{2,1,0:T(8,128)(2,1)S(1)} %get-tuple-element.32), channel_id=1, source_target_pairs={{0,4},{4,0},{8,12},{12,8},{16,20},{20,16},{24,28},{28,24},{1,5},{5... | collective-permute-start | bytes 589832 | tf_op jit(solution)/shard_map/ppermute | solution.py:665
  105.6 8.8 %collective-permute-start.23 = (bf16[1,192,512]{2,1,0:T(8,128)(2,1)S(1)}, bf16[1,192,512]{2,1,0:T(8,128)(2,1)S(1)}, u32[]{:S(2)}, u32[]{:S(2)}) collective-permute-start(bf16[1,192,512]{2,1,0:T(8,128)(2,1)S(1)} %get-tuple-element.34), channel_id=1, source_target_pairs={{0,4},{4,0},{8,12},{12,8},{16,20},{20,16},{24,28},{28,24},{1,5},{5... | collective-permute-start | bytes 589832 | tf_op jit(solution)/shard_map/ppermute | solution.py:665
  (12 other events, 76.0 us)

commit v17 on v16

--- a/solution.py
+++ b/solution.py
@@ -10,6 +10,7 @@
 
 LANES = 128
 SCALE = 1_000_000
+SPLIT_MIB = 52
 ORDER_WEIGHT = 100
 FIRST_WEIGHT = 12_000
 NEXT_WEIGHT = 600
@@ -123,13 +124,16 @@
 def rows_kernel(cut, grad_hbm, logits_hbm, ids_hbm, late_ref, early_ref, gates_ref, *scratch):
     grad_ref, logits_ref, ids_ref, sems = scratch
     model, tokens = grad_ref.shape
+    bounds = list(range(cut, model, 4 * LANES)) + list(range(0, cut, 4 * LANES))
     copies = [
         pltpu.make_async_copy(source, target, sems.at[place])
-        for place, (source, target) in enumerate(
-            ((grad_hbm, grad_ref), (logits_hbm, logits_ref), (ids_hbm, ids_ref))
-        )
+        for place, (source, target) in enumerate(((logits_hbm, logits_ref), (ids_hbm, ids_ref)))
     ]
-    for copy in copies:
+    pieces = {}
+    for place, start in enumerate(bounds):
+        here = slice(start, min(start + 4 * LANES, model if start >= cut else cut))
+        pieces[start] = pltpu.make_async_copy(grad_hbm.at[here, :], grad_ref.at[here, :], sems.at[2 + place])
+    for copy in [*pieces.values(), *copies]:
         copy.start()
     for copy in copies:
         copy.wait()
@@ -146,8 +150,10 @@
     for expert in range(count):
         chosen = jnp.sum(jnp.where(ids == expert, sent, 0.0), axis=0, keepdims=True)
         extra = extra + jnp.where(row == expert, chosen, 0.0)
-    for start in range(0, width, LANES):
+    for start in [*range(cut, width, LANES), *range(0, cut, LANES)]:
         stop = start + LANES
+        if start in pieces:
+            pieces[start].wait()
         if stop <= model:
             block = grad_ref[start:stop, :].astype(f32)
         elif start >= model:
@@ -179,7 +185,7 @@
             pltpu.VMEM((model, tokens), bf16),
             pltpu.VMEM((count, tokens), f32),
             pltpu.VMEM((count, tokens), jnp.int32),
-            pltpu.SemaphoreType.DMA((3,)),
+            pltpu.SemaphoreType.DMA((2 + pl.cdiv(cut, 4 * LANES) + pl.cdiv(model - cut, 4 * LANES),)),
         ],
         compiler_params=params(58),
         cost_estimate=taking(2),
@@ -233,14 +239,20 @@
 
 
 def split_kernel(table, where_ref, hidden_ref, *refs):
-    own_ref, first_ref, rest_ref = refs[-3:]
+    own_ref, first_ref, rest_ref, held, sems = refs[-5:]
     parts, units, _ = own_ref.shape
+    copies = []
+    for part in range(parts):
+        here = slice(part * 2 * units, (part + 1) * 2 * units)
+        copies.append(pltpu.make_async_copy(hidden_ref.at[:, here], held.at[:, here], sems.at[part]))
+        copies[-1].start()
     row = lax.broadcasted_iota(jnp.int32, (2 * units, 2 * units), 0)
     column = lax.broadcasted_iota(jnp.int32, (2 * units, 2 * units), 1)
     unit = jnp.where(row == column, 1.0, 0.0).astype(bf16)
     low = where_ref[table["x"]] == 0
     for part in range(parts):
-        block = hidden_ref[:, part * 2 * units : (part + 1) * 2 * units]
+        copies[part].wait()
+        block = held[:, part * 2 * units : (part + 1) * 2 * units]
         turned = dot(unit, block, NT).astype(bf16)
         slot = where_ref[table["slot of", part]]
         other = jnp.where(low, turned[units:], turned[:units])
@@ -262,9 +274,10 @@
         out_shape=tuple(
             jax.ShapeDtypeStruct((count, units, slots), bf16) for count in (parts, 1, parts - 1)
         ),
-        in_specs=[scalars(), whole()] + [anywhere()] * len(after),
+        in_specs=[scalars()] + [anywhere()] * (1 + len(after)),
         out_specs=(whole(),) * 3,
-        compiler_params=params(),
+        scratch_shapes=[pltpu.VMEM(hidden.shape, bf16), pltpu.SemaphoreType.DMA((parts,))],
+        compiler_params=params(SPLIT_MIB),
         cost_estimate=taking(2),
         name="split_hidden",
     )(where, hidden, *after)

time: 120 us -> 120 us (level)
  Pallas kernels: 39.3 us -> 40.8 us
  local copies, waits for them, and re-layouts: 3.13 us -> 1.72 us
    unnamed x14 -> x10, local copies, waits for them, and re-layouts: 2.43 us -> 1.02 us
  transfers between devices with their start and end apart: 29 -> 29, of which waited for: 13 -> 12; matrix products, arithmetic and copies ran while one was open for 1% -> 1% of each run, Pallas kernels for 30% -> 31%
where the time goes in v17:
time: 120 us
  starting transfers between devices  43.6 us (36%)
  Pallas kernels  40.8 us (34%)
  waiting for transfers between devices  26.2 us (22%)
  blocking collectives  6.36 us (5%)
  local copies, waits for them, and re-layouts  1.72 us (1%)
    ppermute x13, starting transfers between devices, swap_z(): return lax.ppermute(value, 'ctx', pairs)  28.1 us
    ppermute x8, waiting for transfers between devices, swap(): return lax.ppermute(value, 'ctx', [(i, i ^ x) for i in range(groups)])  12.8 us
    ppermute x8, waiting for transfers between devices, swap(): return lax.ppermute(value, 'exp', [(i, i ^ exp) for i in range(experts)])  10.6 us
    ppermute x8, starting transfers between devices, swap(): return lax.ppermute(value, 'ctx', [(i, i ^ x) for i in range(groups)])  10.2 us
    pallas_call x3, Pallas kernels, back_part(): pl.pallas_call(functools.partial(back_kernel, table, model, cut, counts,...  9.99 us
    pallas_call x5, Pallas kernels, products(): pl.pallas_call(functools.partial(products_kernel, table, model, counts, p...  9.45 us
    all_to_all x1, blocking collectives, per_device_full(): lax.all_to_all(slot_grad.reshape(experts, tokens), 'exp', split_axis=0, c...  6.36 us
    ppermute x8, starting transfers between devices, swap(): return lax.ppermute(value, 'exp', [(i, i ^ exp) for i in range(experts)])  5.3 us
  transfers between devices with their start and end apart: 29, of which 12 were waited for; matrix products, arithmetic and copies ran while one was open for 1% of the time, Pallas kernels for 31%

profile of v17, /device:TPU:0, one launch (start us, length us, event | category | flops | bytes accessed | tf_op | source)
XLA Modules:
  0.0 119.8 jit_solution(7218992182257048355)
XLA Ops:
  0.6 2.6 %make_rows.1 = (bf16[128,1536]{1,0:T(8,128)(2,1)}, bf16[128,1408]{1,0:T(8,128)(2,1)}, f32[4,128]{1,0:T(4,128)}) custom-call(bf16[2880,128]{1,0:T(8,128)(2,1)} %bitcast.21, f32[4,128]{1,0:T(4,128)} %bitcast.22, s32[4,128]{1,0:T(4,128)} %bitcast.17), custom_call_target="tpu_custom_call" | custom-call | flops 2000000 | bytes 6000000 | tf_op jit(solution)/shard_map/make_rows/pallas_call | solution.py:175
  3.2 3.0 %collective-permute-start.1 = (bf16[128,1536]{1,0:T(8,128)(2,1)}, bf16[128,1536]{1,0:T(8,128)(2,1)S(1)}, u32[]{:S(2)}, u32[]{:S(2)}) collective-permute-start(bf16[128,1536]{1,0:T(8,128)(2,1)} %get-tuple-element.21.refs_0_), channel_id=1, source_target_pairs={{0,4},{4,0},{8,12},{12,8},{16,20},{20,16},{24,28},{28,24},{1,5},{5... | collective-permute-start | bytes 1179656 | tf_op jit(solution)/shard_map/ppermute | solution.py:678
  11.7 3.2 %split_hidden.1 = (bf16[4,192,512]{2,1,0:T(8,128)(2,1)S(1)}, bf16[1,192,512]{2,1,0:T(8,128)(2,1)S(1)}, bf16[3,192,512]{2,1,0:T(8,128)(2,1)S(1)}) custom-call(s32[32]{0:T(128)S(1)} %dynamic-slice_bitcast_fusion.where_ref, bf16[512,1536]{1,0:T(8,128)(2,1)} %bitcast.20, bf16[128,1536]{1,0:T(8,128)(2,1)S(1)} %copy-done), custom_call_target="tpu_custom_call" | custom-call | flops 2000000 | bytes 6000000 | tf_op jit(solution)/shard_map/split_hidden/pallas_call | solution.py:272
  18.5 2.4 %collective-permute-done.3.refs_2_.refs_5_.refs_9_ = bf16[1,192,512]{2,1,0:T(8,128)(2,1)S(1)} collective-permute-done((bf16[1,192,512]{2,1,0:T(8,128)(2,1)S(1)}, bf16[1,192,512]{2,1,0:T(8,128)(2,1)S(1)}, u32[]{:S(2)}, u32[]{:S(2)}) %collective-permute-start.3) | collective-permute-done | bytes 196640 | tf_op jit(solution)/shard_map/ppermute | solution.py:678
  21.5 7.8 %collective-permute-done.4.refs_4_.refs_1_ = bf16[128,1408]{1,0:T(8,128)(2,1)S(1)} collective-permute-done((bf16[128,1408]{1,0:T(8,128)(2,1)S(1)}, bf16[128,1408]{1,0:T(8,128)(2,1)S(1)}, u32[]{:S(2)}, u32[]{:S(2)}) %collective-permute-start.4) | collective-permute-done | bytes 360480 | tf_op jit(solution)/shard_map/ppermute | solution.py:678
  32.1 1.9 %collective-permute-done.9.refs_0_ = bf16[192,2880]{1,0:T(8,128)(2,1)S(1)} collective-permute-done((bf16[192,2880]{1,0:T(8,128)(2,1)}, bf16[192,2880]{1,0:T(8,128)(2,1)S(1)}, u32[]{:S(2)}, u32[]{:S(2)}) %collective-permute-start.9) | collective-permute-done | bytes 1105952 | tf_op jit(solution)/shard_map/ppermute | solution.py:690
  34.6 2.2 %first_sums.2.refs_6_ = bf16[192,1472]{1,0:T(8,128)(2,1)S(1)} custom-call(s32[32]{0:T(128)S(1)} %dynamic-slice_bitcast_fusion.where_ref, bf16[4,128,1536]{2,1,0:T(8,128)(2,1)S(1)} %pack_rows.2.refs_0_.refs_2_.refs_6_, bf16[4,128,1536]{2,1,0:T(8,128)(2,1)S(1)} %collective-permute-done.5.refs_1_.refs_3_.refs_7_, ...), custom_call_target="tpu_custom_call" | custom-call | flops 1000000 | bytes 3000000 | tf_op jit(solution)/shard_map/first_sums/pallas_call | solution.py:384
  36.8 2.5 %collective-permute-start.15 = (bf16[192,1472]{1,0:T(8,128)(2,1)S(1)}, bf16[192,1472]{1,0:T(8,128)(2,1)S(1)}, u32[]{:S(2)}, u32[]{:S(2)}) collective-permute-start(bf16[192,1472]{1,0:T(8,128)(2,1)S(1)} %first_sums.2.refs_6_), channel_id=1, source_target_pairs={{0,8},{4,12},{8,0},{12,4},{16,24},{20,28},{24,16},{28,20},{1,9},{5... | collective-permute-start | bytes 1695752 | tf_op jit(solution)/shard_map/ppermute | solution.py:690
  41.4 7.3 %collective-permute-done.11.refs_0_ = bf16[128,1408]{1,0:T(8,128)(2,1)S(1)} collective-permute-done((bf16[128,1408]{1,0:T(8,128)(2,1)S(1)}, bf16[128,1408]{1,0:T(8,128)(2,1)S(1)}, u32[]{:S(2)}, u32[]{:S(2)}) %collective-permute-start.11) | collective-permute-done | bytes 360480 | tf_op jit(solution)/shard_map/ppermute | solution.py:680
  48.7 1.7 %collective-permute-done.12.refs_5_.refs_7_ = bf16[128,1408]{1,0:T(8,128)(2,1)S(1)} collective-permute-done((bf16[128,1408]{1,0:T(8,128)(2,1)S(1)}, bf16[128,1408]{1,0:T(8,128)(2,1)S(1)}, u32[]{:S(2)}, u32[]{:S(2)}) %collective-permute-start.12) | collective-permute-done | bytes 360480 | tf_op jit(solution)/shard_map/ppermute | solution.py:680
  50.4 2.1 %first_sums.3.refs_0_ = bf16[192,1408]{1,0:T(8,128)(2,1)S(1)} custom-call(s32[32]{0:T(128)S(1)} %dynamic-slice_bitcast_fusion.where_ref, bf16[2,128,1408]{2,1,0:T(8,128)(2,1)S(1)} %pack_rows.3.refs_0_.refs_2_, bf16[2,128,1408]{2,1,0:T(8,128)(2,1)S(1)} %collective-permute-done.6.refs_7_.refs_1_.refs_3_, bf16[128,1408]{1,0:T(8,128)(2,1)S(1)} %hold.19.refs_2_.refs_4_, ...), custom_call_target="tpu_custom_call" | custom-call | flops 1000000 | bytes 3000000 | tf_op jit(solution)/shard_map/first_sums/pallas_call | solution.py:384
  52.8 2.2 %collective-permute-start.18 = (bf16[192,1408]{1,0:T(8,128)(2,1)S(1)}, bf16[192,1408]{1,0:T(8,128)(2,1)S(1)}, u32[]{:S(2)}, u32[]{:S(2)}) collective-permute-start(bf16[192,1408]{1,0:T(8,128)(2,1)S(1)} %hold.23.refs_2_.refs_10_), channel_id=1, source_target_pairs={{0,8},{4,12},{8,0},{12,4},{16,24},{20,28},{24,16},{28,20},{1,9},{5... | collective-permute-start | bytes 1622024 | tf_op jit(solution)/shard_map/ppermute | solution.py:690
  55.8 3.9 %rest_kept.3.refs_0_.refs_1_.refs_2_.refs_3_ = f32[3,192,1472]{2,1,0:T(8,128)S(1)} custom-call(s32[32]{0:T(128)S(1)} %dynamic-slice_bitcast_fusion.where_ref, bf16[4,128,1536]{2,1,0:T(8,128)(2,1)S(1)} %pack_rows.2.refs_0_.refs_2_.refs_6_, bf16[4,128,1536]{2,1,0:T(8,128)(2,1)S(1)} %collective-permute-done.5.refs_1_.refs_3_.refs_7_, ...), custom_call_target="tpu_custom_call" | custom-call | flops 1000000 | bytes 3000000 | tf_op jit(solution)/shard_map/rest_kept/pallas_call | solution.py:343
  60.4 5.0 %collective-permute-start.25 = (bf16[192,1472]{1,0:T(8,128)(2,1)S(1)}, bf16[192,1472]{1,0:T(8,128)(2,1)S(1)}, u32[]{:S(2)}, u32[]{:S(2)}) collective-permute-start(bf16[192,1472]{1,0:T(8,128)(2,1)S(1)} %combine.8.refs_1_), channel_id=1, source_target_pairs={{0,8},{4,12},{24,16},{28,20},{1,9},{5,13},{25,17},{29,21},{2,10},{... | collective-permute-start | bytes 1695752 | tf_op jit(solution)/shard_map/ppermute | solution.py:690
  68.0 3.9 %rest_kept.4.refs_0_.refs_2_.refs_10_ = f32[3,192,1408]{2,1,0:T(8,128)S(1)} custom-call(s32[32]{0:T(128)S(1)} %dynamic-slice_bitcast_fusion.where_ref, bf16[2,128,1408]{2,1,0:T(8,128)(2,1)S(1)} %pack_rows.3.refs_0_.refs_2_, bf16[2,128,1408]{2,1,0:T(8,128)(2,1)S(1)} %collective-permute-done.6.refs_7_.refs_1_.refs_3_, ...), custom_call_target="tpu_custom_call" | custom-call | flops 1000000 | bytes 3000000 | tf_op jit(solution)/shard_map/rest_kept/pallas_call | solution.py:343
  74.0 4.7 %collective-permute-start.27 = (bf16[192,1408]{1,0:T(8,128)(2,1)S(1)}, bf16[192,1408]{1,0:T(8,128)(2,1)S(1)}, u32[]{:S(2)}, u32[]{:S(2)}) collective-permute-start(bf16[192,1408]{1,0:T(8,128)(2,1)S(1)} %combine.9.refs_2_), channel_id=1, source_target_pairs={{0,8},{4,12},{24,16},{28,20},{1,9},{5,13},{25,17},{29,21},{2,10},{... | collective-permute-start | bytes 1622024 | tf_op jit(solution)/shard_map/ppermute | solution.py:690
  78.7 4.7 %back_part.3 = (bf16[3,192,512]{2,1,0:T(8,128)(2,1)S(1)}, bf16[3,192,512]{2,1,0:T(8,128)(2,1)S(1)}, f32[8,1024]{1,0:T(8,128)S(1)}) custom-call(s32[32]{0:T(128)S(1)} %dynamic-slice_bitcast_fusion.where_ref, bf16[4,128,1536]{2,1,0:T(8,128)(2,1)S(1)} %pack_rows.2.refs_0_.refs_2_.refs_6_, ...), custom_call_target="tpu_custom_call" | custom-call | flops 6000000 | bytes 18000000 | tf_op jit(solution)/shard_map/back_part/pallas_call | solution.py:583
  87.9 6.7 %collective-permute-start.24 = (bf16[192,2880]{1,0:T(8,128)(2,1)S(1)}, bf16[192,2880]{1,0:T(8,128)(2,1)S(1)}, u32[]{:S(2)}, u32[]{:S(2)}) collective-permute-start(bf16[192,2880]{1,0:T(8,128)(2,1)S(1)} %combine.11.refs_15_), channel_id=1, source_target_pairs={{0,8},{4,12},{8,0},{12,4},{16,24},{20,28},{24,16},{28,20},{1,9},{5... | collective-permute-start | bytes 3317768 | tf_op jit(solution)/shard_map/ppermute | solution.py:690
  96.9 2.6 %back_part.4 = (bf16[1,192,512]{2,1,0:T(8,128)(2,1)S(1)}, bf16[1,192,512]{2,1,0:T(8,128)(2,1)S(1)}, f32[8,1024]{1,0:T(8,128)S(1)}) custom-call(s32[32]{0:T(128)S(1)} %dynamic-slice_bitcast_fusion.where_ref, bf16[4,128,1536]{2,1,0:T(8,128)(2,1)S(1)} %pack_rows.2.refs_0_.refs_2_.refs_6_, ...), custom_call_target="tpu_custom_call" | custom-call | flops 6000000 | bytes 18000000 | tf_op jit(solution)/shard_map/back_part/pallas_call | solution.py:583
  99.6 2.7 %back_part.5 = (bf16[1,192,512]{2,1,0:T(8,128)(2,1)S(1)}, bf16[1,192,512]{2,1,0:T(8,128)(2,1)S(1)}, f32[8,1024]{1,0:T(8,128)S(1)}) custom-call(s32[32]{0:T(128)S(1)} %dynamic-slice_bitcast_fusion.where_ref, bf16[4,128,1536]{2,1,0:T(8,128)(2,1)S(1)} %pack_rows.2.refs_0_.refs_2_.refs_6_, ...), custom_call_target="tpu_custom_call" | custom-call | flops 6000000 | bytes 18000000 | tf_op jit(solution)/shard_map/back_part/pallas_call | solution.py:583
  102.3 1.8 %collective-permute-start.20 = (f32[1,512]{1,0:T(1,128)S(1)}, f32[1,512]{1,0:T(1,128)S(1)}, u32[]{:S(2)}, u32[]{:S(2)}) collective-permute-start(f32[1,512]{1,0:T(1,128)S(1)} %slice.7), channel_id=1, source_target_pairs={{0,4},{4,0},{8,12},{12,8},{16,20},{20,16},{24,28},{28,24},{1,5},{5... | collective-permute-start | bytes 6152 | tf_op jit(solution)/shard_map/ppermute | solution.py:678
  106.0 1.7 %collective-permute-start.23 = (bf16[1,192,512]{2,1,0:T(8,128)(2,1)S(1)}, bf16[1,192,512]{2,1,0:T(8,128)(2,1)S(1)}, u32[]{:S(2)}, u32[]{:S(2)}) collective-permute-start(bf16[1,192,512]{2,1,0:T(8,128)(2,1)S(1)} %get-tuple-element.34), channel_id=1, source_target_pairs={{0,4},{4,0},{8,12},{12,8},{16,20},{20,16},{24,28},{28,24},{1,5},{5... | collective-permute-start | bytes 589832 | tf_op jit(solution)/shard_map/ppermute | solution.py:678
  107.7 6.4 %all_to_all.11 = f32[4,1,128]{2,1,0:T(1,128)S(1)} all-to-all(f32[4,1,128]{2,1,0:T(1,128)S(1)} %add_bitcast_fusion), channel_id=1, replica_groups=mesh['ctx'=8,'exp'=4] {'exp'}, dimensions={0} | all-to-all | bytes 4096 | tf_op jit(solution)/shard_map/all_to_all | solution.py:834
  114.7 2.9 %join_hidden.1 = (bf16[512,1536]{1,0:T(8,128)(2,1)}, f32[8,128]{1,0:T(8,128)S(1)}) custom-call(s32[32]{0:T(128)S(1)} %dynamic-slice_bitcast_fusion.where_ref, bf16[3,192,512]{2,1,0:T(8,128)(2,1)S(1)} %get-tuple-element.29.refs_0_, bf16[3,192,512]{2,1,0:T(8,128)(2,1)S(1)} %collective-permute-done.21.refs_1_, ...), custom_call_target="tpu_custom_call" | custom-call | flops 2000000 | bytes 6000000 | tf_op jit(solution)/shard_map/join_hidden/pallas_call | solution.py:626
  (86 shorter events, 33.0 us)
Async XLA Ops:
  3.2 12.4 %collective-permute-start.1 = (bf16[128,1536]{1,0:T(8,128)(2,1)}, bf16[128,1536]{1,0:T(8,128)(2,1)S(1)}, u32[]{:S(2)}, u32[]{:S(2)}) collective-permute-start(bf16[128,1536]{1,0:T(8,128)(2,1)} %get-tuple-element.21.refs_0_), channel_id=1, source_target_pairs={{0,4},{4,0},{8,12},{12,8},{16,20},{20,16},{24,28},{28,24},{1,5},{5... | collective-permute-start | bytes 1179656 | tf_op jit(solution)/shard_map/ppermute | solution.py:678
  6.2 10.8 %collective-permute-start = (bf16[128,1536]{1,0:T(8,128)(2,1)}, bf16[128,1536]{1,0:T(8,128)(2,1)S(1)}, u32[]{:S(2)}, u32[]{:S(2)}) collective-permute-start(bf16[128,1536]{1,0:T(8,128)(2,1)} %get-tuple-element.21.refs_0_), channel_id=1, source_target_pairs={{0,2},{1,3},{2,0},{3,1},{4,6},{5,7},{6,4},{7,5},{8,10},{9,11},{10,... | collective-permute-start | bytes 1179656 | tf_op jit(solution)/shard_map/ppermute | solution.py:680
  7.7 26.3 %collective-permute-start.9 = (bf16[192,2880]{1,0:T(8,128)(2,1)}, bf16[192,2880]{1,0:T(8,128)(2,1)S(1)}, u32[]{:S(2)}, u32[]{:S(2)}) collective-permute-start(bf16[192,2880]{1,0:T(8,128)(2,1)} %bitcast.14), channel_id=1, source_target_pairs={{0,8},{4,12},{8,0},{12,4},{16,24},{20,28},{24,16},{28,20},{1,9},{5... | collective-permute-start | bytes 3317768 | tf_op jit(solution)/shard_map/ppermute | solution.py:690
  9.3 25.2 %collective-permute-start.8 = (bf16[192,2880]{1,0:T(8,128)(2,1)}, bf16[192,2880]{1,0:T(8,128)(2,1)S(1)}, u32[]{:S(2)}, u32[]{:S(2)}) collective-permute-start(bf16[192,2880]{1,0:T(8,128)(2,1)} %bitcast.15), channel_id=1, source_target_pairs={{8,16},{12,20},{16,8},{20,12},{9,17},{13,21},{17,9},{21,13},{10,18... | collective-permute-start | bytes 3317768 | tf_op jit(solution)/shard_map/ppermute | solution.py:690
  17.0 12.3 %collective-permute-start.2 = (bf16[128,1536]{1,0:T(8,128)(2,1)S(1)}, bf16[128,1536]{1,0:T(8,128)(2,1)S(1)}, u32[]{:S(2)}, u32[]{:S(2)}) collective-permute-start(bf16[128,1536]{1,0:T(8,128)(2,1)S(1)} %hold.15.refs_1_.refs_2_), channel_id=1, source_target_pairs={{0,2},{1,3},{2,0},{3,1},{4,6},{5,7},{6,4},{7,5},{8,10},{9,11},{10,... | collective-permute-start | bytes 1179656 | tf_op jit(solution)/shard_map/ppermute | solution.py:680
  20.9 8.4 %collective-permute-start.4 = (bf16[128,1408]{1,0:T(8,128)(2,1)S(1)}, bf16[128,1408]{1,0:T(8,128)(2,1)S(1)}, u32[]{:S(2)}, u32[]{:S(2)}) collective-permute-start(bf16[128,1408]{1,0:T(8,128)(2,1)S(1)} %hold.16.refs_0_), channel_id=1, source_target_pairs={{0,4},{4,0},{8,12},{12,8},{16,20},{20,16},{24,28},{28,24},{1,5},{5... | collective-permute-start | bytes 1081352 | tf_op jit(solution)/shard_map/ppermute | solution.py:678
  30.1 11.3 %collective-permute-start.7 = (bf16[128,1408]{1,0:T(8,128)(2,1)S(1)}, bf16[128,1408]{1,0:T(8,128)(2,1)S(1)}, u32[]{:S(2)}, u32[]{:S(2)}) collective-permute-start(bf16[128,1408]{1,0:T(8,128)(2,1)S(1)} %hold.16.refs_0_), channel_id=1, source_target_pairs={{0,2},{1,3},{2,0},{3,1},{4,6},{5,7},{6,4},{7,5},{8,10},{9,11},{10,... | collective-permute-start | bytes 1081352 | tf_op jit(solution)/shard_map/ppermute | solution.py:680
  34.0 14.7 %collective-permute-start.11 = (bf16[128,1408]{1,0:T(8,128)(2,1)S(1)}, bf16[128,1408]{1,0:T(8,128)(2,1)S(1)}, u32[]{:S(2)}, u32[]{:S(2)}) collective-permute-start(bf16[128,1408]{1,0:T(8,128)(2,1)S(1)} %collective-permute-done.4.refs_4_.refs_1_), channel_id=1, source_target_pairs={{0,2},{1,3},{2,0},{3,1},{4,6},{5,7},{6,4},{7,5},{8,10},{9,11},{10,... | collective-permute-start | bytes 1081352 | tf_op jit(solution)/shard_map/ppermute | solution.py:680
  36.8 16.1 %collective-permute-start.15 = (bf16[192,1472]{1,0:T(8,128)(2,1)S(1)}, bf16[192,1472]{1,0:T(8,128)(2,1)S(1)}, u32[]{:S(2)}, u32[]{:S(2)}) collective-permute-start(bf16[192,1472]{1,0:T(8,128)(2,1)S(1)} %first_sums.2.refs_6_), channel_id=1, source_target_pairs={{0,8},{4,12},{8,0},{12,4},{16,24},{20,28},{24,16},{28,20},{1,9},{5... | collective-permute-start | bytes 1695752 | tf_op jit(solution)/shard_map/ppermute | solution.py:690
  39.3 27.3 %collective-permute-start.14 = (bf16[192,2880]{1,0:T(8,128)(2,1)S(1)}, bf16[192,2880]{1,0:T(8,128)(2,1)S(1)}, u32[]{:S(2)}, u32[]{:S(2)}) collective-permute-start(bf16[192,2880]{1,0:T(8,128)(2,1)S(1)} %hold.17.refs_1_.refs_12_), channel_id=1, source_target_pairs={{8,16},{12,20},{16,8},{20,12},{9,17},{13,21},{17,9},{21,13},{10,18... | collective-permute-start | bytes 3317768 | tf_op jit(solution)/shard_map/ppermute | solution.py:690
  40.0 15.1 %collective-permute-start.13 = (bf16[3,192,512]{2,1,0:T(8,128)(2,1)S(1)}, bf16[3,192,512]{2,1,0:T(8,128)(2,1)S(1)}, u32[]{:S(2)}, u32[]{:S(2)}) collective-permute-start(bf16[3,192,512]{2,1,0:T(8,128)(2,1)S(1)} %get-tuple-element.25), channel_id=1, source_target_pairs={{0,4},{4,0},{8,12},{12,8},{16,20},{20,16},{24,28},{28,24},{1,5},{5... | collective-permute-start | bytes 1769480 | tf_op jit(solution)/shard_map/ppermute | solution.py:678
  41.4 7.3 %collective-permute-start.10 = (bf16[128,1408]{1,0:T(8,128)(2,1)S(1)}, bf16[128,1408]{1,0:T(8,128)(2,1)S(1)}, u32[]{:S(2)}, u32[]{:S(2)}) collective-permute-start(bf16[128,1408]{1,0:T(8,128)(2,1)S(1)} %hold.19.refs_2_.refs_4_), channel_id=1, source_target_pairs={{0,1},{1,0},{2,3},{3,2},{4,5},{5,4},{6,7},{7,6},{8,9},{9,8},{10,11... | collective-permute-start | bytes 1081352 | tf_op jit(solution)/shard_map/ppermute | solution.py:680
  52.8 19.8 %collective-permute-start.18 = (bf16[192,1408]{1,0:T(8,128)(2,1)S(1)}, bf16[192,1408]{1,0:T(8,128)(2,1)S(1)}, u32[]{:S(2)}, u32[]{:S(2)}) collective-permute-start(bf16[192,1408]{1,0:T(8,128)(2,1)S(1)} %hold.23.refs_2_.refs_10_), channel_id=1, source_target_pairs={{0,8},{4,12},{8,0},{12,4},{16,24},{20,28},{24,16},{28,20},{1,9},{5... | collective-permute-start | bytes 1622024 | tf_op jit(solution)/shard_map/ppermute | solution.py:690
  60.4 23.0 %collective-permute-start.25 = (bf16[192,1472]{1,0:T(8,128)(2,1)S(1)}, bf16[192,1472]{1,0:T(8,128)(2,1)S(1)}, u32[]{:S(2)}, u32[]{:S(2)}) collective-permute-start(bf16[192,1472]{1,0:T(8,128)(2,1)S(1)} %combine.8.refs_1_), channel_id=1, source_target_pairs={{0,8},{4,12},{24,16},{28,20},{1,9},{5,13},{25,17},{29,21},{2,10},{... | collective-permute-start | bytes 1695752 | tf_op jit(solution)/shard_map/ppermute | solution.py:690
  65.4 20.9 %collective-permute-start.17 = (bf16[192,1472]{1,0:T(8,128)(2,1)S(1)}, bf16[192,1472]{1,0:T(8,128)(2,1)S(1)}, u32[]{:S(2)}, u32[]{:S(2)}) collective-permute-start(bf16[192,1472]{1,0:T(8,128)(2,1)S(1)} %combine.7.refs_6_), channel_id=1, source_target_pairs={{8,16},{12,20},{16,8},{20,12},{9,17},{13,21},{17,9},{21,13},{10,18... | collective-permute-start | bytes 1695752 | tf_op jit(solution)/shard_map/ppermute | solution.py:690
  66.7 32.9 %collective-permute-start.16 = (bf16[192,2880]{1,0:T(8,128)(2,1)S(1)}, bf16[192,2880]{1,0:T(8,128)(2,1)S(1)}, u32[]{:S(2)}, u32[]{:S(2)}) collective-permute-start(bf16[192,2880]{1,0:T(8,128)(2,1)S(1)} %hold.24.refs_10_.refs_13_), channel_id=1, source_target_pairs={{8,0},{12,4},{16,24},{20,28},{9,1},{13,5},{17,25},{21,29},{10,2},{... | collective-permute-start | bytes 3317768 | tf_op jit(solution)/shard_map/ppermute | solution.py:690
  73.3 13.7 %collective-permute-start.19 = (bf16[192,1408]{1,0:T(8,128)(2,1)S(1)}, bf16[192,1408]{1,0:T(8,128)(2,1)S(1)}, u32[]{:S(2)}, u32[]{:S(2)}) collective-permute-start(bf16[192,1408]{1,0:T(8,128)(2,1)S(1)} %combine.10.refs_11_), channel_id=1, source_target_pairs={{8,16},{12,20},{16,8},{20,12},{9,17},{13,21},{17,9},{21,13},{10,18... | collective-permute-start | bytes 1622024 | tf_op jit(solution)/shard_map/ppermute | solution.py:690
  74.0 20.5 %collective-permute-start.27 = (bf16[192,1408]{1,0:T(8,128)(2,1)S(1)}, bf16[192,1408]{1,0:T(8,128)(2,1)S(1)}, u32[]{:S(2)}, u32[]{:S(2)}) collective-permute-start(bf16[192,1408]{1,0:T(8,128)(2,1)S(1)} %combine.9.refs_2_), channel_id=1, source_target_pairs={{0,8},{4,12},{24,16},{28,20},{1,9},{5,13},{25,17},{29,21},{2,10},{... | collective-permute-start | bytes 1622024 | tf_op jit(solution)/shard_map/ppermute | solution.py:690
  83.4 12.8 %collective-permute-start.21 = (bf16[3,192,512]{2,1,0:T(8,128)(2,1)S(1)}, bf16[3,192,512]{2,1,0:T(8,128)(2,1)S(1)}, u32[]{:S(2)}, u32[]{:S(2)}) collective-permute-start(bf16[3,192,512]{2,1,0:T(8,128)(2,1)S(1)} %get-tuple-element.30), channel_id=1, source_target_pairs={{0,4},{4,0},{8,12},{12,8},{16,20},{20,16},{24,28},{28,24},{1,5},{5... | collective-permute-start | bytes 1769480 | tf_op jit(solution)/shard_map/ppermute | solution.py:678
  86.3 31.3 %collective-permute-start.26 = (bf16[192,1472]{1,0:T(8,128)(2,1)S(1)}, bf16[192,1472]{1,0:T(8,128)(2,1)S(1)}, u32[]{:S(2)}, u32[]{:S(2)}) collective-permute-start(bf16[192,1472]{1,0:T(8,128)(2,1)S(1)} %combine.12), channel_id=1, source_target_pairs={{8,16},{12,20},{16,8},{20,12},{9,17},{13,21},{17,9},{21,13},{10,18... | collective-permute-start | bytes 1695752 | tf_op jit(solution)/shard_map/ppermute | solution.py:690
  87.9 30.4 %collective-permute-start.24 = (bf16[192,2880]{1,0:T(8,128)(2,1)S(1)}, bf16[192,2880]{1,0:T(8,128)(2,1)S(1)}, u32[]{:S(2)}, u32[]{:S(2)}) collective-permute-start(bf16[192,2880]{1,0:T(8,128)(2,1)S(1)} %combine.11.refs_15_), channel_id=1, source_target_pairs={{0,8},{4,12},{8,0},{12,4},{16,24},{20,28},{24,16},{28,20},{1,9},{5... | collective-permute-start | bytes 3317768 | tf_op jit(solution)/shard_map/ppermute | solution.py:690
  96.2 21.4 %collective-permute-start.28 = (bf16[192,1408]{1,0:T(8,128)(2,1)S(1)}, bf16[192,1408]{1,0:T(8,128)(2,1)S(1)}, u32[]{:S(2)}, u32[]{:S(2)}) collective-permute-start(bf16[192,1408]{1,0:T(8,128)(2,1)S(1)} %hold.26), channel_id=1, source_target_pairs={{8,16},{12,20},{16,8},{20,12},{9,17},{13,21},{17,9},{21,13},{10,18... | collective-permute-start | bytes 1622024 | tf_op jit(solution)/shard_map/ppermute | solution.py:690
  104.1 10.6 %collective-permute-start.22 = (bf16[1,192,512]{2,1,0:T(8,128)(2,1)S(1)}, bf16[1,192,512]{2,1,0:T(8,128)(2,1)S(1)}, u32[]{:S(2)}, u32[]{:S(2)}) collective-permute-start(bf16[1,192,512]{2,1,0:T(8,128)(2,1)S(1)} %get-tuple-element.32), channel_id=1, source_target_pairs={{0,4},{4,0},{8,12},{12,8},{16,20},{20,16},{24,28},{28,24},{1,5},{5... | collective-permute-start | bytes 589832 | tf_op jit(solution)/shard_map/ppermute | solution.py:678
  106.0 8.7 %collective-permute-start.23 = (bf16[1,192,512]{2,1,0:T(8,128)(2,1)S(1)}, bf16[1,192,512]{2,1,0:T(8,128)(2,1)S(1)}, u32[]{:S(2)}, u32[]{:S(2)}) collective-permute-start(bf16[1,192,512]{2,1,0:T(8,128)(2,1)S(1)} %get-tuple-element.34), channel_id=1, source_target_pairs={{0,4},{4,0},{8,12},{12,8},{16,20},{20,16},{24,28},{28,24},{1,5},{5... | collective-permute-start | bytes 589832 | tf_op jit(solution)/shard_map/ppermute | solution.py:678
  (10 other events, 60.4 us)

commit v18 on v16

--- a/solution.py
+++ b/solution.py
@@ -733,7 +733,7 @@
     early_rows = (early_rows, places)
     marker = first_chunk(early_rows, 0, cut, [first[0]], got[2, "A"])
     got[2, "B"] = [swap_z(got[1, "A"][0], "B")]
-    (other_rest,) = hold([other_rest], [], HIDDEN_WEIGHT)
+    (other_rest,) = hold([other_rest], first[1:], HIDDEN_WEIGHT)
 
     halves, all_choices, weights_of = [], [], {}
     only_first = max(uses[3, "B"]) <= 0

time: 120 us -> 120 us (level)
  transfers between devices with their start and end apart: 29 -> 29, of which waited for: 13 -> 12; matrix products, arithmetic and copies ran while one was open for 1% -> 1% of each run, Pallas kernels for 30% -> 30%
where the time goes in v18:
time: 120 us
  starting transfers between devices  42.8 us (36%)
  Pallas kernels  39.3 us (33%)
  waiting for transfers between devices  26.9 us (22%)
  blocking collectives  6.42 us (5%)
  local copies, waits for them, and re-layouts  3.13 us (3%)
    ppermute x13, starting transfers between devices, swap_z(): return lax.ppermute(value, 'ctx', pairs)  27.9 us
    ppermute x8, waiting for transfers between devices, swap(): return lax.ppermute(value, 'ctx', [(i, i ^ x) for i in range(groups)])  12.8 us
    ppermute x8, waiting for transfers between devices, swap(): return lax.ppermute(value, 'exp', [(i, i ^ exp) for i in range(experts)])  10.6 us
    ppermute x8, starting transfers between devices, swap(): return lax.ppermute(value, 'ctx', [(i, i ^ x) for i in range(groups)])  10.2 us
    pallas_call x3, Pallas kernels, back_part(): pl.pallas_call(functools.partial(back_kernel, table, model, cut, counts,...  9.98 us
    pallas_call x5, Pallas kernels, products(): pl.pallas_call(functools.partial(products_kernel, table, model, counts, p...  9.45 us
    all_to_all x1, blocking collectives, per_device_full(): lax.all_to_all(slot_grad.reshape(experts, tokens), 'exp', split_axis=0, c...  6.42 us
    pallas_call x7, Pallas kernels, combine(): pl.pallas_call(functools.partial(combine_kernel, table, ('use', turn, nam...  5.1 us
  transfers between devices with their start and end apart: 29, of which 12 were waited for; matrix products, arithmetic and copies ran while one was open for 1% of the time, Pallas kernels for 30%

profile of v18, /device:TPU:0, one launch (start us, length us, event | category | flops | bytes accessed | tf_op | source)
XLA Modules:
  0.0 119.6 jit_solution(12010738106743637814)
XLA Ops:
  0.6 2.2 %make_rows.1 = (bf16[128,1536]{1,0:T(8,128)(2,1)}, bf16[128,1408]{1,0:T(8,128)(2,1)}, f32[4,128]{1,0:T(4,128)}) custom-call(bf16[2880,128]{1,0:T(8,128)(2,1)} %bitcast.21, f32[4,128]{1,0:T(4,128)} %bitcast.22, s32[4,128]{1,0:T(4,128)} %bitcast.18), custom_call_target="tpu_custom_call" | custom-call | flops 2000000 | bytes 6000000 | tf_op jit(solution)/shard_map/make_rows/pallas_call | solution.py:169
  2.8 3.0 %collective-permute-start.1 = (bf16[128,1536]{1,0:T(8,128)(2,1)}, bf16[128,1536]{1,0:T(8,128)(2,1)S(1)}, u32[]{:S(2)}, u32[]{:S(2)}) collective-permute-start(bf16[128,1536]{1,0:T(8,128)(2,1)} %get-tuple-element.21.refs_0_), channel_id=1, source_target_pairs={{0,4},{4,0},{8,12},{12,8},{16,20},{20,16},{24,28},{28,24},{1,5},{5... | collective-permute-start | bytes 1179656 | tf_op jit(solution)/shard_map/ppermute | solution.py:665
  12.8 2.2 %split_hidden.1 = (bf16[4,192,512]{2,1,0:T(8,128)(2,1)S(1)}, bf16[1,192,512]{2,1,0:T(8,128)(2,1)S(1)}, bf16[3,192,512]{2,1,0:T(8,128)(2,1)S(1)}) custom-call(s32[32]{0:T(128)S(1)} %dynamic-slice_bitcast_fusion.where_ref, bf16[512,1536]{1,0:T(8,128)(2,1)S(1)} %bitcast.14, bf16[128,1536]{1,0:T(8,128)(2,1)S(1)} %copy-done.1), custom_call_target="tpu_custom_call" | custom-call | flops 2000000 | bytes 6000000 | tf_op jit(solution)/shard_map/split_hidden/pallas_call | solution.py:260
  18.1 2.7 %collective-permute-done.3.refs_2_.refs_5_.refs_9_ = bf16[1,192,512]{2,1,0:T(8,128)(2,1)S(1)} collective-permute-done((bf16[1,192,512]{2,1,0:T(8,128)(2,1)S(1)}, bf16[1,192,512]{2,1,0:T(8,128)(2,1)S(1)}, u32[]{:S(2)}, u32[]{:S(2)}) %collective-permute-start.3) | collective-permute-done | bytes 196640 | tf_op jit(solution)/shard_map/ppermute | solution.py:665
  21.4 7.8 %collective-permute-done.4.refs_4_.refs_1_ = bf16[128,1408]{1,0:T(8,128)(2,1)S(1)} collective-permute-done((bf16[128,1408]{1,0:T(8,128)(2,1)S(1)}, bf16[128,1408]{1,0:T(8,128)(2,1)S(1)}, u32[]{:S(2)}, u32[]{:S(2)}) %collective-permute-start.4) | collective-permute-done | bytes 360480 | tf_op jit(solution)/shard_map/ppermute | solution.py:665
  31.5 2.2 %collective-permute-done.9.refs_0_ = bf16[192,2880]{1,0:T(8,128)(2,1)S(1)} collective-permute-done((bf16[192,2880]{1,0:T(8,128)(2,1)}, bf16[192,2880]{1,0:T(8,128)(2,1)S(1)}, u32[]{:S(2)}, u32[]{:S(2)}) %collective-permute-start.9) | collective-permute-done | bytes 1105952 | tf_op jit(solution)/shard_map/ppermute | solution.py:677
  34.5 2.2 %first_sums.2.refs_6_ = bf16[192,1472]{1,0:T(8,128)(2,1)S(1)} custom-call(s32[32]{0:T(128)S(1)} %dynamic-slice_bitcast_fusion.where_ref, bf16[4,128,1536]{2,1,0:T(8,128)(2,1)S(1)} %pack_rows.2.refs_0_.refs_2_.refs_6_, bf16[4,128,1536]{2,1,0:T(8,128)(2,1)S(1)} %collective-permute-done.5.refs_1_.refs_3_.refs_7_, ...), custom_call_target="tpu_custom_call" | custom-call | flops 1000000 | bytes 3000000 | tf_op jit(solution)/shard_map/first_sums/pallas_call | solution.py:371
  36.7 2.5 %collective-permute-start.14 = (bf16[192,1472]{1,0:T(8,128)(2,1)S(1)}, bf16[192,1472]{1,0:T(8,128)(2,1)S(1)}, u32[]{:S(2)}, u32[]{:S(2)}) collective-permute-start(bf16[192,1472]{1,0:T(8,128)(2,1)S(1)} %first_sums.2.refs_6_), channel_id=1, source_target_pairs={{0,8},{4,12},{8,0},{12,4},{16,24},{20,28},{24,16},{28,20},{1,9},{5... | collective-permute-start | bytes 1695752 | tf_op jit(solution)/shard_map/ppermute | solution.py:677
  41.4 7.3 %collective-permute-done.11.refs_0_ = bf16[128,1408]{1,0:T(8,128)(2,1)S(1)} collective-permute-done((bf16[128,1408]{1,0:T(8,128)(2,1)S(1)}, bf16[128,1408]{1,0:T(8,128)(2,1)S(1)}, u32[]{:S(2)}, u32[]{:S(2)}) %collective-permute-start.11) | collective-permute-done | bytes 360480 | tf_op jit(solution)/shard_map/ppermute | solution.py:667
  48.7 1.7 %collective-permute-done.12.refs_5_.refs_7_ = bf16[128,1408]{1,0:T(8,128)(2,1)S(1)} collective-permute-done((bf16[128,1408]{1,0:T(8,128)(2,1)S(1)}, bf16[128,1408]{1,0:T(8,128)(2,1)S(1)}, u32[]{:S(2)}, u32[]{:S(2)}) %collective-permute-start.12) | collective-permute-done | bytes 360480 | tf_op jit(solution)/shard_map/ppermute | solution.py:667
  50.3 2.1 %first_sums.3.refs_0_ = bf16[192,1408]{1,0:T(8,128)(2,1)S(1)} custom-call(s32[32]{0:T(128)S(1)} %dynamic-slice_bitcast_fusion.where_ref, bf16[2,128,1408]{2,1,0:T(8,128)(2,1)S(1)} %pack_rows.3.refs_0_.refs_2_, bf16[2,128,1408]{2,1,0:T(8,128)(2,1)S(1)} %collective-permute-done.6.refs_7_.refs_1_.refs_3_, bf16[128,1408]{1,0:T(8,128)(2,1)S(1)} %hold.19.refs_2_.refs_4_, ...), custom_call_target="tpu_custom_call" | custom-call | flops 1000000 | bytes 3000000 | tf_op jit(solution)/shard_map/first_sums/pallas_call | solution.py:371
  52.8 2.2 %collective-permute-start.18 = (bf16[192,1408]{1,0:T(8,128)(2,1)S(1)}, bf16[192,1408]{1,0:T(8,128)(2,1)S(1)}, u32[]{:S(2)}, u32[]{:S(2)}) collective-permute-start(bf16[192,1408]{1,0:T(8,128)(2,1)S(1)} %hold.22.refs_10_.refs_2_), channel_id=1, source_target_pairs={{0,8},{4,12},{8,0},{12,4},{16,24},{20,28},{24,16},{28,20},{1,9},{5... | collective-permute-start | bytes 1622024 | tf_op jit(solution)/shard_map/ppermute | solution.py:677
  56.3 3.9 %rest_kept.3.refs_0_.refs_1_.refs_2_.refs_3_ = f32[3,192,1472]{2,1,0:T(8,128)S(1)} custom-call(s32[32]{0:T(128)S(1)} %dynamic-slice_bitcast_fusion.where_ref, bf16[4,128,1536]{2,1,0:T(8,128)(2,1)S(1)} %pack_rows.2.refs_0_.refs_2_.refs_6_, bf16[4,128,1536]{2,1,0:T(8,128)(2,1)S(1)} %collective-permute-done.5.refs_1_.refs_3_.refs_7_, ...), custom_call_target="tpu_custom_call" | custom-call | flops 1000000 | bytes 3000000 | tf_op jit(solution)/shard_map/rest_kept/pallas_call | solution.py:330
  60.9 3.7 %collective-permute-start.25 = (bf16[192,1472]{1,0:T(8,128)(2,1)S(1)}, bf16[192,1472]{1,0:T(8,128)(2,1)S(1)}, u32[]{:S(2)}, u32[]{:S(2)}) collective-permute-start(bf16[192,1472]{1,0:T(8,128)(2,1)S(1)} %combine.8.refs_1_), channel_id=1, source_target_pairs={{0,8},{4,12},{24,16},{28,20},{1,9},{5,13},{25,17},{29,21},{2,10},{... | collective-permute-start | bytes 1695752 | tf_op jit(solution)/shard_map/ppermute | solution.py:677
  66.6 3.9 %rest_kept.4.refs_0_.refs_2_.refs_10_ = f32[3,192,1408]{2,1,0:T(8,128)S(1)} custom-call(s32[32]{0:T(128)S(1)} %dynamic-slice_bitcast_fusion.where_ref, bf16[2,128,1408]{2,1,0:T(8,128)(2,1)S(1)} %pack_rows.3.refs_0_.refs_2_, bf16[2,128,1408]{2,1,0:T(8,128)(2,1)S(1)} %collective-permute-done.6.refs_7_.refs_1_.refs_3_, ...), custom_call_target="tpu_custom_call" | custom-call | flops 1000000 | bytes 3000000 | tf_op jit(solution)/shard_map/rest_kept/pallas_call | solution.py:330
  72.7 4.4 %collective-permute-start.27 = (bf16[192,1408]{1,0:T(8,128)(2,1)S(1)}, bf16[192,1408]{1,0:T(8,128)(2,1)S(1)}, u32[]{:S(2)}, u32[]{:S(2)}) collective-permute-start(bf16[192,1408]{1,0:T(8,128)(2,1)S(1)} %combine.9.refs_2_), channel_id=1, source_target_pairs={{0,8},{4,12},{24,16},{28,20},{1,9},{5,13},{25,17},{29,21},{2,10},{... | collective-permute-start | bytes 1622024 | tf_op jit(solution)/shard_map/ppermute | solution.py:677
  77.1 4.7 %back_part.3 = (bf16[3,192,512]{2,1,0:T(8,128)(2,1)S(1)}, bf16[3,192,512]{2,1,0:T(8,128)(2,1)S(1)}, f32[8,1024]{1,0:T(8,128)S(1)}) custom-call(s32[32]{0:T(128)S(1)} %dynamic-slice_bitcast_fusion.where_ref, bf16[4,128,1536]{2,1,0:T(8,128)(2,1)S(1)} %pack_rows.2.refs_0_.refs_2_.refs_6_, ...), custom_call_target="tpu_custom_call" | custom-call | flops 6000000 | bytes 18000000 | tf_op jit(solution)/shard_map/back_part/pallas_call | solution.py:570
  81.8 1.7 %collective-permute-start.21 = (bf16[3,192,512]{2,1,0:T(8,128)(2,1)S(1)}, bf16[3,192,512]{2,1,0:T(8,128)(2,1)S(1)}, u32[]{:S(2)}, u32[]{:S(2)}) collective-permute-start(bf16[3,192,512]{2,1,0:T(8,128)(2,1)S(1)} %get-tuple-element.30), channel_id=1, source_target_pairs={{0,4},{4,0},{8,12},{12,8},{16,20},{20,16},{24,28},{28,24},{1,5},{5... | collective-permute-start | bytes 1769480 | tf_op jit(solution)/shard_map/ppermute | solution.py:665
  86.4 8.1 %collective-permute-start.24 = (bf16[192,2880]{1,0:T(8,128)(2,1)S(1)}, bf16[192,2880]{1,0:T(8,128)(2,1)S(1)}, u32[]{:S(2)}, u32[]{:S(2)}) collective-permute-start(bf16[192,2880]{1,0:T(8,128)(2,1)S(1)} %combine.11.refs_15_), channel_id=1, source_target_pairs={{0,8},{4,12},{8,0},{12,4},{16,24},{20,28},{24,16},{28,20},{1,9},{5... | collective-permute-start | bytes 3317768 | tf_op jit(solution)/shard_map/ppermute | solution.py:677
  96.5 2.6 %back_part.4 = (bf16[1,192,512]{2,1,0:T(8,128)(2,1)S(1)}, bf16[1,192,512]{2,1,0:T(8,128)(2,1)S(1)}, f32[8,1024]{1,0:T(8,128)S(1)}) custom-call(s32[32]{0:T(128)S(1)} %dynamic-slice_bitcast_fusion.where_ref, bf16[4,128,1536]{2,1,0:T(8,128)(2,1)S(1)} %pack_rows.2.refs_0_.refs_2_.refs_6_, ...), custom_call_target="tpu_custom_call" | custom-call | flops 6000000 | bytes 18000000 | tf_op jit(solution)/shard_map/back_part/pallas_call | solution.py:570
  99.2 2.7 %back_part.5 = (bf16[1,192,512]{2,1,0:T(8,128)(2,1)S(1)}, bf16[1,192,512]{2,1,0:T(8,128)(2,1)S(1)}, f32[8,1024]{1,0:T(8,128)S(1)}) custom-call(s32[32]{0:T(128)S(1)} %dynamic-slice_bitcast_fusion.where_ref, bf16[4,128,1536]{2,1,0:T(8,128)(2,1)S(1)} %pack_rows.2.refs_0_.refs_2_.refs_6_, ...), custom_call_target="tpu_custom_call" | custom-call | flops 6000000 | bytes 18000000 | tf_op jit(solution)/shard_map/back_part/pallas_call | solution.py:570
  101.9 1.7 %collective-permute-start.20 = (f32[1,512]{1,0:T(1,128)S(1)}, f32[1,512]{1,0:T(1,128)S(1)}, u32[]{:S(2)}, u32[]{:S(2)}) collective-permute-start(f32[1,512]{1,0:T(1,128)S(1)} %slice.7), channel_id=1, source_target_pairs={{0,4},{4,0},{8,12},{12,8},{16,20},{20,16},{24,28},{28,24},{1,5},{5... | collective-permute-start | bytes 6152 | tf_op jit(solution)/shard_map/ppermute | solution.py:665
  107.2 6.4 %all_to_all.11 = f32[4,1,128]{2,1,0:T(1,128)S(1)} all-to-all(f32[4,1,128]{2,1,0:T(1,128)S(1)} %add_bitcast_fusion), channel_id=1, replica_groups=mesh['ctx'=8,'exp'=4] {'exp'}, dimensions={0} | all-to-all | bytes 4096 | tf_op jit(solution)/shard_map/all_to_all | solution.py:821
  114.2 2.9 %join_hidden.1 = (bf16[512,1536]{1,0:T(8,128)(2,1)}, f32[8,128]{1,0:T(8,128)S(1)}) custom-call(s32[32]{0:T(128)S(1)} %dynamic-slice_bitcast_fusion.where_ref, bf16[3,192,512]{2,1,0:T(8,128)(2,1)S(1)} %get-tuple-element.29.refs_0_, bf16[3,192,512]{2,1,0:T(8,128)(2,1)S(1)} %collective-permute-done.21.refs_1_, ...), custom_call_target="tpu_custom_call" | custom-call | flops 2000000 | bytes 6000000 | tf_op jit(solution)/shard_map/join_hidden/pallas_call | solution.py:613
  (90 shorter events, 33.9 us)
Async XLA Ops:
  2.8 12.8 %collective-permute-start.1 = (bf16[128,1536]{1,0:T(8,128)(2,1)}, bf16[128,1536]{1,0:T(8,128)(2,1)S(1)}, u32[]{:S(2)}, u32[]{:S(2)}) collective-permute-start(bf16[128,1536]{1,0:T(8,128)(2,1)} %get-tuple-element.21.refs_0_), channel_id=1, source_target_pairs={{0,4},{4,0},{8,12},{12,8},{16,20},{20,16},{24,28},{28,24},{1,5},{5... | collective-permute-start | bytes 1179656 | tf_op jit(solution)/shard_map/ppermute | solution.py:665
  5.8 10.8 %collective-permute-start = (bf16[128,1536]{1,0:T(8,128)(2,1)}, bf16[128,1536]{1,0:T(8,128)(2,1)S(1)}, u32[]{:S(2)}, u32[]{:S(2)}) collective-permute-start(bf16[128,1536]{1,0:T(8,128)(2,1)} %get-tuple-element.21.refs_0_), channel_id=1, source_target_pairs={{0,2},{1,3},{2,0},{3,1},{4,6},{5,7},{6,4},{7,5},{8,10},{9,11},{10,... | collective-permute-start | bytes 1179656 | tf_op jit(solution)/shard_map/ppermute | solution.py:667
  7.4 26.3 %collective-permute-start.9 = (bf16[192,2880]{1,0:T(8,128)(2,1)}, bf16[192,2880]{1,0:T(8,128)(2,1)S(1)}, u32[]{:S(2)}, u32[]{:S(2)}) collective-permute-start(bf16[192,2880]{1,0:T(8,128)(2,1)} %bitcast.15), channel_id=1, source_target_pairs={{0,8},{4,12},{8,0},{12,4},{16,24},{20,28},{24,16},{28,20},{1,9},{5... | collective-permute-start | bytes 3317768 | tf_op jit(solution)/shard_map/ppermute | solution.py:677
  8.9 25.2 %collective-permute-start.8 = (bf16[192,2880]{1,0:T(8,128)(2,1)}, bf16[192,2880]{1,0:T(8,128)(2,1)S(1)}, u32[]{:S(2)}, u32[]{:S(2)}) collective-permute-start(bf16[192,2880]{1,0:T(8,128)(2,1)} %bitcast.16), channel_id=1, source_target_pairs={{8,16},{12,20},{16,8},{20,12},{9,17},{13,21},{17,9},{21,13},{10,18... | collective-permute-start | bytes 3317768 | tf_op jit(solution)/shard_map/ppermute | solution.py:677
  16.6 12.6 %collective-permute-start.2 = (bf16[128,1536]{1,0:T(8,128)(2,1)S(1)}, bf16[128,1536]{1,0:T(8,128)(2,1)S(1)}, u32[]{:S(2)}, u32[]{:S(2)}) collective-permute-start(bf16[128,1536]{1,0:T(8,128)(2,1)S(1)} %hold.15.refs_1_.refs_2_), channel_id=1, source_target_pairs={{0,2},{1,3},{2,0},{3,1},{4,6},{5,7},{6,4},{7,5},{8,10},{9,11},{10,... | collective-permute-start | bytes 1179656 | tf_op jit(solution)/shard_map/ppermute | solution.py:667
  20.9 8.4 %collective-permute-start.4 = (bf16[128,1408]{1,0:T(8,128)(2,1)S(1)}, bf16[128,1408]{1,0:T(8,128)(2,1)S(1)}, u32[]{:S(2)}, u32[]{:S(2)}) collective-permute-start(bf16[128,1408]{1,0:T(8,128)(2,1)S(1)} %hold.16.refs_0_), channel_id=1, source_target_pairs={{0,4},{4,0},{8,12},{12,8},{16,20},{20,16},{24,28},{28,24},{1,5},{5... | collective-permute-start | bytes 1081352 | tf_op jit(solution)/shard_map/ppermute | solution.py:665
  30.1 11.3 %collective-permute-start.7 = (bf16[128,1408]{1,0:T(8,128)(2,1)S(1)}, bf16[128,1408]{1,0:T(8,128)(2,1)S(1)}, u32[]{:S(2)}, u32[]{:S(2)}) collective-permute-start(bf16[128,1408]{1,0:T(8,128)(2,1)S(1)} %hold.16.refs_0_), channel_id=1, source_target_pairs={{0,2},{1,3},{2,0},{3,1},{4,6},{5,7},{6,4},{7,5},{8,10},{9,11},{10,... | collective-permute-start | bytes 1081352 | tf_op jit(solution)/shard_map/ppermute | solution.py:667
  33.7 15.0 %collective-permute-start.11 = (bf16[128,1408]{1,0:T(8,128)(2,1)S(1)}, bf16[128,1408]{1,0:T(8,128)(2,1)S(1)}, u32[]{:S(2)}, u32[]{:S(2)}) collective-permute-start(bf16[128,1408]{1,0:T(8,128)(2,1)S(1)} %collective-permute-done.4.refs_4_.refs_1_), channel_id=1, source_target_pairs={{0,2},{1,3},{2,0},{3,1},{4,6},{5,7},{6,4},{7,5},{8,10},{9,11},{10,... | collective-permute-start | bytes 1081352 | tf_op jit(solution)/shard_map/ppermute | solution.py:667
  36.7 16.1 %collective-permute-start.14 = (bf16[192,1472]{1,0:T(8,128)(2,1)S(1)}, bf16[192,1472]{1,0:T(8,128)(2,1)S(1)}, u32[]{:S(2)}, u32[]{:S(2)}) collective-permute-start(bf16[192,1472]{1,0:T(8,128)(2,1)S(1)} %first_sums.2.refs_6_), channel_id=1, source_target_pairs={{0,8},{4,12},{8,0},{12,4},{16,24},{20,28},{24,16},{28,20},{1,9},{5... | collective-permute-start | bytes 1695752 | tf_op jit(solution)/shard_map/ppermute | solution.py:677
  39.2 26.1 %collective-permute-start.15 = (bf16[192,2880]{1,0:T(8,128)(2,1)S(1)}, bf16[192,2880]{1,0:T(8,128)(2,1)S(1)}, u32[]{:S(2)}, u32[]{:S(2)}) collective-permute-start(bf16[192,2880]{1,0:T(8,128)(2,1)S(1)} %hold.17.refs_1_.refs_12_), channel_id=1, source_target_pairs={{8,16},{12,20},{16,8},{20,12},{9,17},{13,21},{17,9},{21,13},{10,18... | collective-permute-start | bytes 3317768 | tf_op jit(solution)/shard_map/ppermute | solution.py:677
  39.9 16.4 %collective-permute-start.13 = (bf16[3,192,512]{2,1,0:T(8,128)(2,1)S(1)}, bf16[3,192,512]{2,1,0:T(8,128)(2,1)S(1)}, u32[]{:S(2)}, u32[]{:S(2)}) collective-permute-start(bf16[3,192,512]{2,1,0:T(8,128)(2,1)S(1)} %get-tuple-element.25), channel_id=1, source_target_pairs={{0,4},{4,0},{8,12},{12,8},{16,20},{20,16},{24,28},{28,24},{1,5},{5... | collective-permute-start | bytes 1769480 | tf_op jit(solution)/shard_map/ppermute | solution.py:665
  41.4 7.3 %collective-permute-start.10 = (bf16[128,1408]{1,0:T(8,128)(2,1)S(1)}, bf16[128,1408]{1,0:T(8,128)(2,1)S(1)}, u32[]{:S(2)}, u32[]{:S(2)}) collective-permute-start(bf16[128,1408]{1,0:T(8,128)(2,1)S(1)} %hold.19.refs_2_.refs_4_), channel_id=1, source_target_pairs={{0,1},{1,0},{2,3},{3,2},{4,5},{5,4},{6,7},{7,6},{8,9},{9,8},{10,11... | collective-permute-start | bytes 1081352 | tf_op jit(solution)/shard_map/ppermute | solution.py:667
  52.8 18.4 %collective-permute-start.18 = (bf16[192,1408]{1,0:T(8,128)(2,1)S(1)}, bf16[192,1408]{1,0:T(8,128)(2,1)S(1)}, u32[]{:S(2)}, u32[]{:S(2)}) collective-permute-start(bf16[192,1408]{1,0:T(8,128)(2,1)S(1)} %hold.22.refs_10_.refs_2_), channel_id=1, source_target_pairs={{0,8},{4,12},{8,0},{12,4},{16,24},{20,28},{24,16},{28,20},{1,9},{5... | collective-permute-start | bytes 1622024 | tf_op jit(solution)/shard_map/ppermute | solution.py:677
  60.9 20.9 %collective-permute-start.25 = (bf16[192,1472]{1,0:T(8,128)(2,1)S(1)}, bf16[192,1472]{1,0:T(8,128)(2,1)S(1)}, u32[]{:S(2)}, u32[]{:S(2)}) collective-permute-start(bf16[192,1472]{1,0:T(8,128)(2,1)S(1)} %combine.8.refs_1_), channel_id=1, source_target_pairs={{0,8},{4,12},{24,16},{28,20},{1,9},{5,13},{25,17},{29,21},{2,10},{... | collective-permute-start | bytes 1695752 | tf_op jit(solution)/shard_map/ppermute | solution.py:677
  64.6 20.2 %collective-permute-start.17 = (bf16[192,1472]{1,0:T(8,128)(2,1)S(1)}, bf16[192,1472]{1,0:T(8,128)(2,1)S(1)}, u32[]{:S(2)}, u32[]{:S(2)}) collective-permute-start(bf16[192,1472]{1,0:T(8,128)(2,1)S(1)} %combine.7.refs_6_), channel_id=1, source_target_pairs={{8,16},{12,20},{16,8},{20,12},{9,17},{13,21},{17,9},{21,13},{10,18... | collective-permute-start | bytes 1695752 | tf_op jit(solution)/shard_map/ppermute | solution.py:677
  65.3 33.8 %collective-permute-start.16 = (bf16[192,2880]{1,0:T(8,128)(2,1)S(1)}, bf16[192,2880]{1,0:T(8,128)(2,1)S(1)}, u32[]{:S(2)}, u32[]{:S(2)}) collective-permute-start(bf16[192,2880]{1,0:T(8,128)(2,1)S(1)} %hold.24.refs_10_.refs_13_), channel_id=1, source_target_pairs={{8,0},{12,4},{16,24},{20,28},{9,1},{13,5},{17,25},{21,29},{10,2},{... | collective-permute-start | bytes 3317768 | tf_op jit(solution)/shard_map/ppermute | solution.py:677
  72.0 13.6 %collective-permute-start.19 = (bf16[192,1408]{1,0:T(8,128)(2,1)S(1)}, bf16[192,1408]{1,0:T(8,128)(2,1)S(1)}, u32[]{:S(2)}, u32[]{:S(2)}) collective-permute-start(bf16[192,1408]{1,0:T(8,128)(2,1)S(1)} %combine.10.refs_11_), channel_id=1, source_target_pairs={{8,16},{12,20},{16,8},{20,12},{9,17},{13,21},{17,9},{21,13},{10,18... | collective-permute-start | bytes 1622024 | tf_op jit(solution)/shard_map/ppermute | solution.py:677
  72.7 21.8 %collective-permute-start.27 = (bf16[192,1408]{1,0:T(8,128)(2,1)S(1)}, bf16[192,1408]{1,0:T(8,128)(2,1)S(1)}, u32[]{:S(2)}, u32[]{:S(2)}) collective-permute-start(bf16[192,1408]{1,0:T(8,128)(2,1)S(1)} %combine.9.refs_2_), channel_id=1, source_target_pairs={{0,8},{4,12},{24,16},{28,20},{1,9},{5,13},{25,17},{29,21},{2,10},{... | collective-permute-start | bytes 1622024 | tf_op jit(solution)/shard_map/ppermute | solution.py:677
  81.8 14.0 %collective-permute-start.21 = (bf16[3,192,512]{2,1,0:T(8,128)(2,1)S(1)}, bf16[3,192,512]{2,1,0:T(8,128)(2,1)S(1)}, u32[]{:S(2)}, u32[]{:S(2)}) collective-permute-start(bf16[3,192,512]{2,1,0:T(8,128)(2,1)S(1)} %get-tuple-element.30), channel_id=1, source_target_pairs={{0,4},{4,0},{8,12},{12,8},{16,20},{20,16},{24,28},{28,24},{1,5},{5... | collective-permute-start | bytes 1769480 | tf_op jit(solution)/shard_map/ppermute | solution.py:665
  84.9 32.3 %collective-permute-start.26 = (bf16[192,1472]{1,0:T(8,128)(2,1)S(1)}, bf16[192,1472]{1,0:T(8,128)(2,1)S(1)}, u32[]{:S(2)}, u32[]{:S(2)}) collective-permute-start(bf16[192,1472]{1,0:T(8,128)(2,1)S(1)} %combine.12), channel_id=1, source_target_pairs={{8,16},{12,20},{16,8},{20,12},{9,17},{13,21},{17,9},{21,13},{10,18... | collective-permute-start | bytes 1695752 | tf_op jit(solution)/shard_map/ppermute | solution.py:677
  86.4 31.7 %collective-permute-start.24 = (bf16[192,2880]{1,0:T(8,128)(2,1)S(1)}, bf16[192,2880]{1,0:T(8,128)(2,1)S(1)}, u32[]{:S(2)}, u32[]{:S(2)}) collective-permute-start(bf16[192,2880]{1,0:T(8,128)(2,1)S(1)} %combine.11.refs_15_), channel_id=1, source_target_pairs={{0,8},{4,12},{8,0},{12,4},{16,24},{20,28},{24,16},{28,20},{1,9},{5... | collective-permute-start | bytes 3317768 | tf_op jit(solution)/shard_map/ppermute | solution.py:677
  95.8 21.3 %collective-permute-start.28 = (bf16[192,1408]{1,0:T(8,128)(2,1)S(1)}, bf16[192,1408]{1,0:T(8,128)(2,1)S(1)}, u32[]{:S(2)}, u32[]{:S(2)}) collective-permute-start(bf16[192,1408]{1,0:T(8,128)(2,1)S(1)} %hold.26), channel_id=1, source_target_pairs={{8,16},{12,20},{16,8},{20,12},{9,17},{13,21},{17,9},{21,13},{10,18... | collective-permute-start | bytes 1622024 | tf_op jit(solution)/shard_map/ppermute | solution.py:677
  103.6 10.6 %collective-permute-start.22 = (bf16[1,192,512]{2,1,0:T(8,128)(2,1)S(1)}, bf16[1,192,512]{2,1,0:T(8,128)(2,1)S(1)}, u32[]{:S(2)}, u32[]{:S(2)}) collective-permute-start(bf16[1,192,512]{2,1,0:T(8,128)(2,1)S(1)} %get-tuple-element.32), channel_id=1, source_target_pairs={{0,4},{4,0},{8,12},{12,8},{16,20},{20,16},{24,28},{28,24},{1,5},{5... | collective-permute-start | bytes 589832 | tf_op jit(solution)/shard_map/ppermute | solution.py:665
  105.6 8.6 %collective-permute-start.23 = (bf16[1,192,512]{2,1,0:T(8,128)(2,1)S(1)}, bf16[1,192,512]{2,1,0:T(8,128)(2,1)S(1)}, u32[]{:S(2)}, u32[]{:S(2)}) collective-permute-start(bf16[1,192,512]{2,1,0:T(8,128)(2,1)S(1)} %get-tuple-element.34), channel_id=1, source_target_pairs={{0,4},{4,0},{8,12},{12,8},{16,20},{20,16},{24,28},{28,24},{1,5},{5... | collective-permute-start | bytes 589832 | tf_op jit(solution)/shard_map/ppermute | solution.py:665
  (12 other events, 75.7 us)

commit v19 on v18

--- a/solution.py
+++ b/solution.py
@@ -233,14 +233,20 @@
 
 
 def split_kernel(table, where_ref, hidden_ref, *refs):
-    own_ref, first_ref, rest_ref = refs[-3:]
+    own_ref, first_ref, rest_ref, held, sems = refs[-5:]
     parts, units, _ = own_ref.shape
+    copies = []
+    for part in range(parts):
+        here = slice(part * 2 * units, (part + 1) * 2 * units)
+        copies.append(pltpu.make_async_copy(hidden_ref.at[:, here], held.at[:, here], sems.at[part]))
+        copies[-1].start()
     row = lax.broadcasted_iota(jnp.int32, (2 * units, 2 * units), 0)
     column = lax.broadcasted_iota(jnp.int32, (2 * units, 2 * units), 1)
     unit = jnp.where(row == column, 1.0, 0.0).astype(bf16)
     low = where_ref[table["x"]] == 0
     for part in range(parts):
-        block = hidden_ref[:, part * 2 * units : (part + 1) * 2 * units]
+        copies[part].wait()
+        block = held[:, part * 2 * units : (part + 1) * 2 * units]
         turned = dot(unit, block, NT).astype(bf16)
         slot = where_ref[table["slot of", part]]
         other = jnp.where(low, turned[units:], turned[:units])
@@ -262,9 +268,10 @@
         out_shape=tuple(
             jax.ShapeDtypeStruct((count, units, slots), bf16) for count in (parts, 1, parts - 1)
         ),
-        in_specs=[scalars(), whole()] + [anywhere()] * len(after),
+        in_specs=[scalars()] + [anywhere()] * (1 + len(after)),
         out_specs=(whole(),) * 3,
-        compiler_params=params(),
+        scratch_shapes=[pltpu.VMEM(hidden.shape, bf16), pltpu.SemaphoreType.DMA((parts,))],
+        compiler_params=params(52),
         cost_estimate=taking(2),
         name="split_hidden",
     )(where, hidden, *after)

time: 120 us -> 120 us (level)
  local copies, waits for them, and re-layouts: 3.13 us -> 1.72 us
    unnamed x14 -> x10, local copies, waits for them, and re-layouts: 2.43 us -> 1.02 us
  transfers between devices with their start and end apart: 29 -> 29, of which waited for: 12 -> 11; matrix products, arithmetic and copies ran while one was open for 1% -> 1% of each run, Pallas kernels for 30% -> 31%
where the time goes in v19:
time: 120 us; the launch traced here: 119 us
  starting transfers between devices  43.6 us (36%)
  Pallas kernels  40.4 us (34%)
  waiting for transfers between devices  26.1 us (22%)
  blocking collectives  6.36 us (5%)
  local copies, waits for them, and re-layouts  1.72 us (1%)
    ppermute x13, starting transfers between devices, swap_z(): return lax.ppermute(value, 'ctx', pairs)  28 us
    ppermute x8, waiting for transfers between devices, swap(): return lax.ppermute(value, 'ctx', [(i, i ^ x) for i in range(groups)])  12.7 us
    ppermute x8, waiting for transfers between devices, swap(): return lax.ppermute(value, 'exp', [(i, i ^ exp) for i in range(experts)])  10.6 us
    ppermute x8, starting transfers between devices, swap(): return lax.ppermute(value, 'ctx', [(i, i ^ x) for i in range(groups)])  10.3 us
    pallas_call x3, Pallas kernels, back_part(): pl.pallas_call(functools.partial(back_kernel, table, model, cut, counts,...  9.99 us
    pallas_call x5, Pallas kernels, products(): pl.pallas_call(functools.partial(products_kernel, table, model, counts, p...  9.45 us
    all_to_all x1, blocking collectives, per_device_full(): lax.all_to_all(slot_grad.reshape(experts, tokens), 'exp', split_axis=0, c...  6.36 us
    ppermute x8, starting transfers between devices, swap(): return lax.ppermute(value, 'exp', [(i, i ^ exp) for i in range(experts)])  5.3 us
  transfers between devices with their start and end apart: 29, of which 11 were waited for; matrix products, arithmetic and copies ran while one was open for 1% of the time, Pallas kernels for 31%

profile of v19, /device:TPU:0, one launch (start us, length us, event | category | flops | bytes accessed | tf_op | source)
XLA Modules:
  0.0 119.3 jit_solution(17188807657093034361)
XLA Ops:
  0.6 2.2 %make_rows.1 = (bf16[128,1536]{1,0:T(8,128)(2,1)}, bf16[128,1408]{1,0:T(8,128)(2,1)}, f32[4,128]{1,0:T(4,128)}) custom-call(bf16[2880,128]{1,0:T(8,128)(2,1)} %bitcast.21, f32[4,128]{1,0:T(4,128)} %bitcast.22, s32[4,128]{1,0:T(4,128)} %bitcast.17), custom_call_target="tpu_custom_call" | custom-call | flops 2000000 | bytes 6000000 | tf_op jit(solution)/shard_map/make_rows/pallas_call | solution.py:169
  2.8 3.0 %collective-permute-start.1 = (bf16[128,1536]{1,0:T(8,128)(2,1)}, bf16[128,1536]{1,0:T(8,128)(2,1)S(1)}, u32[]{:S(2)}, u32[]{:S(2)}) collective-permute-start(bf16[128,1536]{1,0:T(8,128)(2,1)} %get-tuple-element.21.refs_0_), channel_id=1, source_target_pairs={{0,4},{4,0},{8,12},{12,8},{16,20},{20,16},{24,28},{28,24},{1,5},{5... | collective-permute-start | bytes 1179656 | tf_op jit(solution)/shard_map/ppermute | solution.py:672
  11.4 3.2 %split_hidden.1 = (bf16[4,192,512]{2,1,0:T(8,128)(2,1)S(1)}, bf16[1,192,512]{2,1,0:T(8,128)(2,1)S(1)}, bf16[3,192,512]{2,1,0:T(8,128)(2,1)S(1)}) custom-call(s32[32]{0:T(128)S(1)} %dynamic-slice_bitcast_fusion.where_ref, bf16[512,1536]{1,0:T(8,128)(2,1)} %bitcast.20, bf16[128,1536]{1,0:T(8,128)(2,1)S(1)} %copy-done), custom_call_target="tpu_custom_call" | custom-call | flops 2000000 | bytes 6000000 | tf_op jit(solution)/shard_map/split_hidden/pallas_call | solution.py:266
  18.1 2.4 %collective-permute-done.3.refs_2_.refs_5_.refs_9_ = bf16[1,192,512]{2,1,0:T(8,128)(2,1)S(1)} collective-permute-done((bf16[1,192,512]{2,1,0:T(8,128)(2,1)S(1)}, bf16[1,192,512]{2,1,0:T(8,128)(2,1)S(1)}, u32[]{:S(2)}, u32[]{:S(2)}) %collective-permute-start.3) | collective-permute-done | bytes 196640 | tf_op jit(solution)/shard_map/ppermute | solution.py:672
  21.1 7.8 %collective-permute-done.4.refs_4_.refs_1_ = bf16[128,1408]{1,0:T(8,128)(2,1)S(1)} collective-permute-done((bf16[128,1408]{1,0:T(8,128)(2,1)S(1)}, bf16[128,1408]{1,0:T(8,128)(2,1)S(1)}, u32[]{:S(2)}, u32[]{:S(2)}) %collective-permute-start.4) | collective-permute-done | bytes 360480 | tf_op jit(solution)/shard_map/ppermute | solution.py:672
  31.7 1.9 %collective-permute-done.9.refs_0_ = bf16[192,2880]{1,0:T(8,128)(2,1)S(1)} collective-permute-done((bf16[192,2880]{1,0:T(8,128)(2,1)}, bf16[192,2880]{1,0:T(8,128)(2,1)S(1)}, u32[]{:S(2)}, u32[]{:S(2)}) %collective-permute-start.9) | collective-permute-done | bytes 1105952 | tf_op jit(solution)/shard_map/ppermute | solution.py:684
  34.2 2.2 %first_sums.2.refs_6_ = bf16[192,1472]{1,0:T(8,128)(2,1)S(1)} custom-call(s32[32]{0:T(128)S(1)} %dynamic-slice_bitcast_fusion.where_ref, bf16[4,128,1536]{2,1,0:T(8,128)(2,1)S(1)} %pack_rows.2.refs_0_.refs_2_.refs_6_, bf16[4,128,1536]{2,1,0:T(8,128)(2,1)S(1)} %collective-permute-done.5.refs_1_.refs_3_.refs_7_, ...), custom_call_target="tpu_custom_call" | custom-call | flops 1000000 | bytes 3000000 | tf_op jit(solution)/shard_map/first_sums/pallas_call | solution.py:378
  36.4 2.5 %collective-permute-start.14 = (bf16[192,1472]{1,0:T(8,128)(2,1)S(1)}, bf16[192,1472]{1,0:T(8,128)(2,1)S(1)}, u32[]{:S(2)}, u32[]{:S(2)}) collective-permute-start(bf16[192,1472]{1,0:T(8,128)(2,1)S(1)} %first_sums.2.refs_6_), channel_id=1, source_target_pairs={{0,8},{4,12},{8,0},{12,4},{16,24},{20,28},{24,16},{28,20},{1,9},{5... | collective-permute-start | bytes 1695752 | tf_op jit(solution)/shard_map/ppermute | solution.py:684
  41.0 7.3 %collective-permute-done.11.refs_0_ = bf16[128,1408]{1,0:T(8,128)(2,1)S(1)} collective-permute-done((bf16[128,1408]{1,0:T(8,128)(2,1)S(1)}, bf16[128,1408]{1,0:T(8,128)(2,1)S(1)}, u32[]{:S(2)}, u32[]{:S(2)}) %collective-permute-start.11) | collective-permute-done | bytes 360480 | tf_op jit(solution)/shard_map/ppermute | solution.py:674
  48.3 1.7 %collective-permute-done.12.refs_5_.refs_7_ = bf16[128,1408]{1,0:T(8,128)(2,1)S(1)} collective-permute-done((bf16[128,1408]{1,0:T(8,128)(2,1)S(1)}, bf16[128,1408]{1,0:T(8,128)(2,1)S(1)}, u32[]{:S(2)}, u32[]{:S(2)}) %collective-permute-start.12) | collective-permute-done | bytes 360480 | tf_op jit(solution)/shard_map/ppermute | solution.py:674
  50.0 2.1 %first_sums.3.refs_0_ = bf16[192,1408]{1,0:T(8,128)(2,1)S(1)} custom-call(s32[32]{0:T(128)S(1)} %dynamic-slice_bitcast_fusion.where_ref, bf16[2,128,1408]{2,1,0:T(8,128)(2,1)S(1)} %pack_rows.3.refs_0_.refs_2_, bf16[2,128,1408]{2,1,0:T(8,128)(2,1)S(1)} %collective-permute-done.6.refs_7_.refs_1_.refs_3_, bf16[128,1408]{1,0:T(8,128)(2,1)S(1)} %hold.19.refs_2_.refs_4_, ...), custom_call_target="tpu_custom_call" | custom-call | flops 1000000 | bytes 3000000 | tf_op jit(solution)/shard_map/first_sums/pallas_call | solution.py:378
  52.5 2.2 %collective-permute-start.18 = (bf16[192,1408]{1,0:T(8,128)(2,1)S(1)}, bf16[192,1408]{1,0:T(8,128)(2,1)S(1)}, u32[]{:S(2)}, u32[]{:S(2)}) collective-permute-start(bf16[192,1408]{1,0:T(8,128)(2,1)S(1)} %hold.22.refs_10_.refs_2_), channel_id=1, source_target_pairs={{0,8},{4,12},{8,0},{12,4},{16,24},{20,28},{24,16},{28,20},{1,9},{5... | collective-permute-start | bytes 1622024 | tf_op jit(solution)/shard_map/ppermute | solution.py:684
  56.0 3.9 %rest_kept.3.refs_0_.refs_1_.refs_2_.refs_3_ = f32[3,192,1472]{2,1,0:T(8,128)S(1)} custom-call(s32[32]{0:T(128)S(1)} %dynamic-slice_bitcast_fusion.where_ref, bf16[4,128,1536]{2,1,0:T(8,128)(2,1)S(1)} %pack_rows.2.refs_0_.refs_2_.refs_6_, bf16[4,128,1536]{2,1,0:T(8,128)(2,1)S(1)} %collective-permute-done.5.refs_1_.refs_3_.refs_7_, ...), custom_call_target="tpu_custom_call" | custom-call | flops 1000000 | bytes 3000000 | tf_op jit(solution)/shard_map/rest_kept/pallas_call | solution.py:337
  60.5 3.7 %collective-permute-start.25 = (bf16[192,1472]{1,0:T(8,128)(2,1)S(1)}, bf16[192,1472]{1,0:T(8,128)(2,1)S(1)}, u32[]{:S(2)}, u32[]{:S(2)}) collective-permute-start(bf16[192,1472]{1,0:T(8,128)(2,1)S(1)} %combine.8.refs_1_), channel_id=1, source_target_pairs={{0,8},{4,12},{24,16},{28,20},{1,9},{5,13},{25,17},{29,21},{2,10},{... | collective-permute-start | bytes 1695752 | tf_op jit(solution)/shard_map/ppermute | solution.py:684
  66.3 3.9 %rest_kept.4.refs_0_.refs_2_.refs_10_ = f32[3,192,1408]{2,1,0:T(8,128)S(1)} custom-call(s32[32]{0:T(128)S(1)} %dynamic-slice_bitcast_fusion.where_ref, bf16[2,128,1408]{2,1,0:T(8,128)(2,1)S(1)} %pack_rows.3.refs_0_.refs_2_, bf16[2,128,1408]{2,1,0:T(8,128)(2,1)S(1)} %collective-permute-done.6.refs_7_.refs_1_.refs_3_, ...), custom_call_target="tpu_custom_call" | custom-call | flops 1000000 | bytes 3000000 | tf_op jit(solution)/shard_map/rest_kept/pallas_call | solution.py:337
  72.4 4.7 %collective-permute-start.27 = (bf16[192,1408]{1,0:T(8,128)(2,1)S(1)}, bf16[192,1408]{1,0:T(8,128)(2,1)S(1)}, u32[]{:S(2)}, u32[]{:S(2)}) collective-permute-start(bf16[192,1408]{1,0:T(8,128)(2,1)S(1)} %combine.9.refs_2_), channel_id=1, source_target_pairs={{0,8},{4,12},{24,16},{28,20},{1,9},{5,13},{25,17},{29,21},{2,10},{... | collective-permute-start | bytes 1622024 | tf_op jit(solution)/shard_map/ppermute | solution.py:684
  77.1 4.7 %back_part.3 = (bf16[3,192,512]{2,1,0:T(8,128)(2,1)S(1)}, bf16[3,192,512]{2,1,0:T(8,128)(2,1)S(1)}, f32[8,1024]{1,0:T(8,128)S(1)}) custom-call(s32[32]{0:T(128)S(1)} %dynamic-slice_bitcast_fusion.where_ref, bf16[4,128,1536]{2,1,0:T(8,128)(2,1)S(1)} %pack_rows.2.refs_0_.refs_2_.refs_6_, ...), custom_call_target="tpu_custom_call" | custom-call | flops 6000000 | bytes 18000000 | tf_op jit(solution)/shard_map/back_part/pallas_call | solution.py:577
  81.8 1.8 %collective-permute-start.21 = (bf16[3,192,512]{2,1,0:T(8,128)(2,1)S(1)}, bf16[3,192,512]{2,1,0:T(8,128)(2,1)S(1)}, u32[]{:S(2)}, u32[]{:S(2)}) collective-permute-start(bf16[3,192,512]{2,1,0:T(8,128)(2,1)S(1)} %get-tuple-element.30), channel_id=1, source_target_pairs={{0,4},{4,0},{8,12},{12,8},{16,20},{20,16},{24,28},{28,24},{1,5},{5... | collective-permute-start | bytes 1769480 | tf_op jit(solution)/shard_map/ppermute | solution.py:672
  86.5 7.7 %collective-permute-start.24 = (bf16[192,2880]{1,0:T(8,128)(2,1)S(1)}, bf16[192,2880]{1,0:T(8,128)(2,1)S(1)}, u32[]{:S(2)}, u32[]{:S(2)}) collective-permute-start(bf16[192,2880]{1,0:T(8,128)(2,1)S(1)} %combine.11.refs_15_), channel_id=1, source_target_pairs={{0,8},{4,12},{8,0},{12,4},{16,24},{20,28},{24,16},{28,20},{1,9},{5... | collective-permute-start | bytes 3317768 | tf_op jit(solution)/shard_map/ppermute | solution.py:684
  96.5 2.6 %back_part.4 = (bf16[1,192,512]{2,1,0:T(8,128)(2,1)S(1)}, bf16[1,192,512]{2,1,0:T(8,128)(2,1)S(1)}, f32[8,1024]{1,0:T(8,128)S(1)}) custom-call(s32[32]{0:T(128)S(1)} %dynamic-slice_bitcast_fusion.where_ref, bf16[4,128,1536]{2,1,0:T(8,128)(2,1)S(1)} %pack_rows.2.refs_0_.refs_2_.refs_6_, ...), custom_call_target="tpu_custom_call" | custom-call | flops 6000000 | bytes 18000000 | tf_op jit(solution)/shard_map/back_part/pallas_call | solution.py:577
  99.2 2.7 %back_part.5 = (bf16[1,192,512]{2,1,0:T(8,128)(2,1)S(1)}, bf16[1,192,512]{2,1,0:T(8,128)(2,1)S(1)}, f32[8,1024]{1,0:T(8,128)S(1)}) custom-call(s32[32]{0:T(128)S(1)} %dynamic-slice_bitcast_fusion.where_ref, bf16[4,128,1536]{2,1,0:T(8,128)(2,1)S(1)} %pack_rows.2.refs_0_.refs_2_.refs_6_, ...), custom_call_target="tpu_custom_call" | custom-call | flops 6000000 | bytes 18000000 | tf_op jit(solution)/shard_map/back_part/pallas_call | solution.py:577
  101.9 1.8 %collective-permute-start.20 = (f32[1,512]{1,0:T(1,128)S(1)}, f32[1,512]{1,0:T(1,128)S(1)}, u32[]{:S(2)}, u32[]{:S(2)}) collective-permute-start(f32[1,512]{1,0:T(1,128)S(1)} %slice.7), channel_id=1, source_target_pairs={{0,4},{4,0},{8,12},{12,8},{16,20},{20,16},{24,28},{28,24},{1,5},{5... | collective-permute-start | bytes 6152 | tf_op jit(solution)/shard_map/ppermute | solution.py:672
  107.3 6.4 %all_to_all.11 = f32[4,1,128]{2,1,0:T(1,128)S(1)} all-to-all(f32[4,1,128]{2,1,0:T(1,128)S(1)} %add_bitcast_fusion), channel_id=1, replica_groups=mesh['ctx'=8,'exp'=4] {'exp'}, dimensions={0} | all-to-all | bytes 4096 | tf_op jit(solution)/shard_map/all_to_all | solution.py:828
  114.2 2.9 %join_hidden.1 = (bf16[512,1536]{1,0:T(8,128)(2,1)}, f32[8,128]{1,0:T(8,128)S(1)}) custom-call(s32[32]{0:T(128)S(1)} %dynamic-slice_bitcast_fusion.where_ref, bf16[3,192,512]{2,1,0:T(8,128)(2,1)S(1)} %get-tuple-element.29.refs_0_, bf16[3,192,512]{2,1,0:T(8,128)(2,1)S(1)} %collective-permute-done.21.refs_1_, ...), custom_call_target="tpu_custom_call" | custom-call | flops 2000000 | bytes 6000000 | tf_op jit(solution)/shard_map/join_hidden/pallas_call | solution.py:620
  (86 shorter events, 33.0 us)
Async XLA Ops:
  2.8 12.4 %collective-permute-start.1 = (bf16[128,1536]{1,0:T(8,128)(2,1)}, bf16[128,1536]{1,0:T(8,128)(2,1)S(1)}, u32[]{:S(2)}, u32[]{:S(2)}) collective-permute-start(bf16[128,1536]{1,0:T(8,128)(2,1)} %get-tuple-element.21.refs_0_), channel_id=1, source_target_pairs={{0,4},{4,0},{8,12},{12,8},{16,20},{20,16},{24,28},{28,24},{1,5},{5... | collective-permute-start | bytes 1179656 | tf_op jit(solution)/shard_map/ppermute | solution.py:672
  5.8 10.8 %collective-permute-start = (bf16[128,1536]{1,0:T(8,128)(2,1)}, bf16[128,1536]{1,0:T(8,128)(2,1)S(1)}, u32[]{:S(2)}, u32[]{:S(2)}) collective-permute-start(bf16[128,1536]{1,0:T(8,128)(2,1)} %get-tuple-element.21.refs_0_), channel_id=1, source_target_pairs={{0,2},{1,3},{2,0},{3,1},{4,6},{5,7},{6,4},{7,5},{8,10},{9,11},{10,... | collective-permute-start | bytes 1179656 | tf_op jit(solution)/shard_map/ppermute | solution.py:674
  7.4 26.3 %collective-permute-start.9 = (bf16[192,2880]{1,0:T(8,128)(2,1)}, bf16[192,2880]{1,0:T(8,128)(2,1)S(1)}, u32[]{:S(2)}, u32[]{:S(2)}) collective-permute-start(bf16[192,2880]{1,0:T(8,128)(2,1)} %bitcast.14), channel_id=1, source_target_pairs={{0,8},{4,12},{8,0},{12,4},{16,24},{20,28},{24,16},{28,20},{1,9},{5... | collective-permute-start | bytes 3317768 | tf_op jit(solution)/shard_map/ppermute | solution.py:684
  8.9 25.2 %collective-permute-start.8 = (bf16[192,2880]{1,0:T(8,128)(2,1)}, bf16[192,2880]{1,0:T(8,128)(2,1)S(1)}, u32[]{:S(2)}, u32[]{:S(2)}) collective-permute-start(bf16[192,2880]{1,0:T(8,128)(2,1)} %bitcast.15), channel_id=1, source_target_pairs={{8,16},{12,20},{16,8},{20,12},{9,17},{13,21},{17,9},{21,13},{10,18... | collective-permute-start | bytes 3317768 | tf_op jit(solution)/shard_map/ppermute | solution.py:684
  16.6 12.3 %collective-permute-start.2 = (bf16[128,1536]{1,0:T(8,128)(2,1)S(1)}, bf16[128,1536]{1,0:T(8,128)(2,1)S(1)}, u32[]{:S(2)}, u32[]{:S(2)}) collective-permute-start(bf16[128,1536]{1,0:T(8,128)(2,1)S(1)} %hold.15.refs_1_.refs_2_), channel_id=1, source_target_pairs={{0,2},{1,3},{2,0},{3,1},{4,6},{5,7},{6,4},{7,5},{8,10},{9,11},{10,... | collective-permute-start | bytes 1179656 | tf_op jit(solution)/shard_map/ppermute | solution.py:674
  20.5 8.4 %collective-permute-start.4 = (bf16[128,1408]{1,0:T(8,128)(2,1)S(1)}, bf16[128,1408]{1,0:T(8,128)(2,1)S(1)}, u32[]{:S(2)}, u32[]{:S(2)}) collective-permute-start(bf16[128,1408]{1,0:T(8,128)(2,1)S(1)} %hold.16.refs_0_), channel_id=1, source_target_pairs={{0,4},{4,0},{8,12},{12,8},{16,20},{20,16},{24,28},{28,24},{1,5},{5... | collective-permute-start | bytes 1081352 | tf_op jit(solution)/shard_map/ppermute | solution.py:672
  29.8 11.3 %collective-permute-start.7 = (bf16[128,1408]{1,0:T(8,128)(2,1)S(1)}, bf16[128,1408]{1,0:T(8,128)(2,1)S(1)}, u32[]{:S(2)}, u32[]{:S(2)}) collective-permute-start(bf16[128,1408]{1,0:T(8,128)(2,1)S(1)} %hold.16.refs_0_), channel_id=1, source_target_pairs={{0,2},{1,3},{2,0},{3,1},{4,6},{5,7},{6,4},{7,5},{8,10},{9,11},{10,... | collective-permute-start | bytes 1081352 | tf_op jit(solution)/shard_map/ppermute | solution.py:674
  33.7 14.7 %collective-permute-start.11 = (bf16[128,1408]{1,0:T(8,128)(2,1)S(1)}, bf16[128,1408]{1,0:T(8,128)(2,1)S(1)}, u32[]{:S(2)}, u32[]{:S(2)}) collective-permute-start(bf16[128,1408]{1,0:T(8,128)(2,1)S(1)} %collective-permute-done.4.refs_4_.refs_1_), channel_id=1, source_target_pairs={{0,2},{1,3},{2,0},{3,1},{4,6},{5,7},{6,4},{7,5},{8,10},{9,11},{10,... | collective-permute-start | bytes 1081352 | tf_op jit(solution)/shard_map/ppermute | solution.py:674
  36.4 16.1 %collective-permute-start.14 = (bf16[192,1472]{1,0:T(8,128)(2,1)S(1)}, bf16[192,1472]{1,0:T(8,128)(2,1)S(1)}, u32[]{:S(2)}, u32[]{:S(2)}) collective-permute-start(bf16[192,1472]{1,0:T(8,128)(2,1)S(1)} %first_sums.2.refs_6_), channel_id=1, source_target_pairs={{0,8},{4,12},{8,0},{12,4},{16,24},{20,28},{24,16},{28,20},{1,9},{5... | collective-permute-start | bytes 1695752 | tf_op jit(solution)/shard_map/ppermute | solution.py:684
  38.9 26.0 %collective-permute-start.15 = (bf16[192,2880]{1,0:T(8,128)(2,1)S(1)}, bf16[192,2880]{1,0:T(8,128)(2,1)S(1)}, u32[]{:S(2)}, u32[]{:S(2)}) collective-permute-start(bf16[192,2880]{1,0:T(8,128)(2,1)S(1)} %hold.17.refs_1_.refs_12_), channel_id=1, source_target_pairs={{8,16},{12,20},{16,8},{20,12},{9,17},{13,21},{17,9},{21,13},{10,18... | collective-permute-start | bytes 3317768 | tf_op jit(solution)/shard_map/ppermute | solution.py:684
  39.7 16.3 %collective-permute-start.13 = (bf16[3,192,512]{2,1,0:T(8,128)(2,1)S(1)}, bf16[3,192,512]{2,1,0:T(8,128)(2,1)S(1)}, u32[]{:S(2)}, u32[]{:S(2)}) collective-permute-start(bf16[3,192,512]{2,1,0:T(8,128)(2,1)S(1)} %get-tuple-element.25), channel_id=1, source_target_pairs={{0,4},{4,0},{8,12},{12,8},{16,20},{20,16},{24,28},{28,24},{1,5},{5... | collective-permute-start | bytes 1769480 | tf_op jit(solution)/shard_map/ppermute | solution.py:672
  41.0 7.3 %collective-permute-start.10 = (bf16[128,1408]{1,0:T(8,128)(2,1)S(1)}, bf16[128,1408]{1,0:T(8,128)(2,1)S(1)}, u32[]{:S(2)}, u32[]{:S(2)}) collective-permute-start(bf16[128,1408]{1,0:T(8,128)(2,1)S(1)} %hold.19.refs_2_.refs_4_), channel_id=1, source_target_pairs={{0,1},{1,0},{2,3},{3,2},{4,5},{5,4},{6,7},{7,6},{8,9},{9,8},{10,11... | collective-permute-start | bytes 1081352 | tf_op jit(solution)/shard_map/ppermute | solution.py:674
  52.5 18.5 %collective-permute-start.18 = (bf16[192,1408]{1,0:T(8,128)(2,1)S(1)}, bf16[192,1408]{1,0:T(8,128)(2,1)S(1)}, u32[]{:S(2)}, u32[]{:S(2)}) collective-permute-start(bf16[192,1408]{1,0:T(8,128)(2,1)S(1)} %hold.22.refs_10_.refs_2_), channel_id=1, source_target_pairs={{0,8},{4,12},{8,0},{12,4},{16,24},{20,28},{24,16},{28,20},{1,9},{5... | collective-permute-start | bytes 1622024 | tf_op jit(solution)/shard_map/ppermute | solution.py:684
  60.5 21.3 %collective-permute-start.25 = (bf16[192,1472]{1,0:T(8,128)(2,1)S(1)}, bf16[192,1472]{1,0:T(8,128)(2,1)S(1)}, u32[]{:S(2)}, u32[]{:S(2)}) collective-permute-start(bf16[192,1472]{1,0:T(8,128)(2,1)S(1)} %combine.8.refs_1_), channel_id=1, source_target_pairs={{0,8},{4,12},{24,16},{28,20},{1,9},{5,13},{25,17},{29,21},{2,10},{... | collective-permute-start | bytes 1695752 | tf_op jit(solution)/shard_map/ppermute | solution.py:684
  64.3 20.6 %collective-permute-start.17 = (bf16[192,1472]{1,0:T(8,128)(2,1)S(1)}, bf16[192,1472]{1,0:T(8,128)(2,1)S(1)}, u32[]{:S(2)}, u32[]{:S(2)}) collective-permute-start(bf16[192,1472]{1,0:T(8,128)(2,1)S(1)} %combine.7.refs_6_), channel_id=1, source_target_pairs={{8,16},{12,20},{16,8},{20,12},{9,17},{13,21},{17,9},{21,13},{10,18... | collective-permute-start | bytes 1695752 | tf_op jit(solution)/shard_map/ppermute | solution.py:684
  65.0 34.2 %collective-permute-start.16 = (bf16[192,2880]{1,0:T(8,128)(2,1)S(1)}, bf16[192,2880]{1,0:T(8,128)(2,1)S(1)}, u32[]{:S(2)}, u32[]{:S(2)}) collective-permute-start(bf16[192,2880]{1,0:T(8,128)(2,1)S(1)} %hold.24.refs_10_.refs_13_), channel_id=1, source_target_pairs={{8,0},{12,4},{16,24},{20,28},{9,1},{13,5},{17,25},{21,29},{10,2},{... | collective-permute-start | bytes 3317768 | tf_op jit(solution)/shard_map/ppermute | solution.py:684
  71.7 13.9 %collective-permute-start.19 = (bf16[192,1408]{1,0:T(8,128)(2,1)S(1)}, bf16[192,1408]{1,0:T(8,128)(2,1)S(1)}, u32[]{:S(2)}, u32[]{:S(2)}) collective-permute-start(bf16[192,1408]{1,0:T(8,128)(2,1)S(1)} %combine.10.refs_11_), channel_id=1, source_target_pairs={{8,16},{12,20},{16,8},{20,12},{9,17},{13,21},{17,9},{21,13},{10,18... | collective-permute-start | bytes 1622024 | tf_op jit(solution)/shard_map/ppermute | solution.py:684
  72.4 21.8 %collective-permute-start.27 = (bf16[192,1408]{1,0:T(8,128)(2,1)S(1)}, bf16[192,1408]{1,0:T(8,128)(2,1)S(1)}, u32[]{:S(2)}, u32[]{:S(2)}) collective-permute-start(bf16[192,1408]{1,0:T(8,128)(2,1)S(1)} %combine.9.refs_2_), channel_id=1, source_target_pairs={{0,8},{4,12},{24,16},{28,20},{1,9},{5,13},{25,17},{29,21},{2,10},{... | collective-permute-start | bytes 1622024 | tf_op jit(solution)/shard_map/ppermute | solution.py:684
  81.8 14.0 %collective-permute-start.21 = (bf16[3,192,512]{2,1,0:T(8,128)(2,1)S(1)}, bf16[3,192,512]{2,1,0:T(8,128)(2,1)S(1)}, u32[]{:S(2)}, u32[]{:S(2)}) collective-permute-start(bf16[3,192,512]{2,1,0:T(8,128)(2,1)S(1)} %get-tuple-element.30), channel_id=1, source_target_pairs={{0,4},{4,0},{8,12},{12,8},{16,20},{20,16},{24,28},{28,24},{1,5},{5... | collective-permute-start | bytes 1769480 | tf_op jit(solution)/shard_map/ppermute | solution.py:672
  84.9 32.2 %collective-permute-start.26 = (bf16[192,1472]{1,0:T(8,128)(2,1)S(1)}, bf16[192,1472]{1,0:T(8,128)(2,1)S(1)}, u32[]{:S(2)}, u32[]{:S(2)}) collective-permute-start(bf16[192,1472]{1,0:T(8,128)(2,1)S(1)} %combine.12), channel_id=1, source_target_pairs={{8,16},{12,20},{16,8},{20,12},{9,17},{13,21},{17,9},{21,13},{10,18... | collective-permute-start | bytes 1695752 | tf_op jit(solution)/shard_map/ppermute | solution.py:684
  86.5 31.3 %collective-permute-start.24 = (bf16[192,2880]{1,0:T(8,128)(2,1)S(1)}, bf16[192,2880]{1,0:T(8,128)(2,1)S(1)}, u32[]{:S(2)}, u32[]{:S(2)}) collective-permute-start(bf16[192,2880]{1,0:T(8,128)(2,1)S(1)} %combine.11.refs_15_), channel_id=1, source_target_pairs={{0,8},{4,12},{8,0},{12,4},{16,24},{20,28},{24,16},{28,20},{1,9},{5... | collective-permute-start | bytes 3317768 | tf_op jit(solution)/shard_map/ppermute | solution.py:684
  95.8 21.3 %collective-permute-start.28 = (bf16[192,1408]{1,0:T(8,128)(2,1)S(1)}, bf16[192,1408]{1,0:T(8,128)(2,1)S(1)}, u32[]{:S(2)}, u32[]{:S(2)}) collective-permute-start(bf16[192,1408]{1,0:T(8,128)(2,1)S(1)} %hold.26), channel_id=1, source_target_pairs={{8,16},{12,20},{16,8},{20,12},{9,17},{13,21},{17,9},{21,13},{10,18... | collective-permute-start | bytes 1622024 | tf_op jit(solution)/shard_map/ppermute | solution.py:684
  103.7 10.6 %collective-permute-start.22 = (bf16[1,192,512]{2,1,0:T(8,128)(2,1)S(1)}, bf16[1,192,512]{2,1,0:T(8,128)(2,1)S(1)}, u32[]{:S(2)}, u32[]{:S(2)}) collective-permute-start(bf16[1,192,512]{2,1,0:T(8,128)(2,1)S(1)} %get-tuple-element.32), channel_id=1, source_target_pairs={{0,4},{4,0},{8,12},{12,8},{16,20},{20,16},{24,28},{28,24},{1,5},{5... | collective-permute-start | bytes 589832 | tf_op jit(solution)/shard_map/ppermute | solution.py:672
  105.6 8.6 %collective-permute-start.23 = (bf16[1,192,512]{2,1,0:T(8,128)(2,1)S(1)}, bf16[1,192,512]{2,1,0:T(8,128)(2,1)S(1)}, u32[]{:S(2)}, u32[]{:S(2)}) collective-permute-start(bf16[1,192,512]{2,1,0:T(8,128)(2,1)S(1)} %get-tuple-element.34), channel_id=1, source_target_pairs={{0,4},{4,0},{8,12},{12,8},{16,20},{20,16},{24,28},{28,24},{1,5},{5... | collective-permute-start | bytes 589832 | tf_op jit(solution)/shard_map/ppermute | solution.py:672
  (10 other events, 60.4 us)
